TPU v7x, 32 devices: a whole 2x2x4 slice. The times are simulated.
32 devices in a mesh: groups: 2 (over y), dp: 4 (over z), mp: 4 (over x, core).
Axes of the slice: x: 2, y: 2, z: 4, core: 2. Of those that a mesh axis runs over, the one named last changes fastest.
Arguments:
- hidden_states: bfloat16 [1024, 2048], P(('groups', 'dp'), 'mp'), parts along dimension 0, may hold values from -6 to 6
- norm_gain: float32 [2048], replicated, may hold values from 0.1 to 1.9
- gate_up_weight: bfloat16 [2, 98304, 2048], P(None, ('dp', 'mp')), may hold values from -0.125 to 0.125
- down_weight: bfloat16 [98304, 2048], P(('dp', 'mp')), may hold values from -0.21875 to 0.21875
- routes: int32 [1024, 8], P(('groups', 'dp')), parts along dimension 0, may hold values from 0 to 127, all different within a row; in each aligned block of 128 rows (0 to 127, 128 to 255, ...) at most 16 rows name the same one
- gates: float32 [1024, 8], P(('groups', 'dp')), parts along dimension 0, may hold values from 0.02 to 0.5
- kv_rows: bfloat16 [1024, 1024], P(('groups', 'dp'), 'mp'), parts along dimension 0, may hold values from -6 to 6
- lengths: int32 [8, 4], P('groups'), parts along dimension 0, may hold values from 1 to 40, 128 in all within a row
- owners: int32 [8, 4], P('groups'), parts along dimension 0, may hold values from 0 to 3, as said below
Outputs:
- mixed_out: bfloat16 [1024, 2048], P(('groups', 'dp'), 'mp'), parts along dimension 0
- kv_cache: bfloat16 [1280, 1024], P(('groups', 'dp'), 'mp'), parts along dimension 0
There are 2 independent parts, one for each index of `groups`. A program takes and returns all parts, laid end to end along the dimension named above; an argument that names none is the same for every part. Nothing has to cross between parts.
Inputs may be any that keep to these rules, and one draw needn't show every extreme that they name: `routes`: each row names 8 different experts; among the 128 rows of one index of dp (aligned blocks) no expert is named by more than 16 rows, and in some block one expert is named by exactly 16. Each row holds the 4 segment lengths of one index of dp, summing to 128; the largest of a row is exactly 40. The 4 owners of one row are distinct, and every owner is named by exactly 4 segments.
All inputs are finite; a program needn't handle non-finite values.
Results may differ from a plain program's by a relative error of at most 0.0048.
Values may be sent and summed in bfloat16 or wider, within the bound.
No kernel may reach another device: no remote copies, remote signals or barrier semaphores. Data moves between devices by JAX's collectives and lax.ppermute only.
A program may use at most 192 MiB of HBM per device.

v0:
```python
import jax
import jax.numpy as jnp
from jax import lax
from jax.sharding import PartitionSpec as P

FF = 768
EXPERTS = 128
TOPK = 8
CAP = 16
SEND_CAP = 40


epsilon = 1e-06


def node_slots(routes_node, experts, capacity):
    pair_list = routes_node.reshape(-1)
    onehot = (pair_list[:, None] == jnp.arange(experts, dtype=jnp.int32)[None, :]).astype(jnp.int32)
    before = jnp.cumsum(onehot, axis=0) - onehot
    slot_index = jnp.sum(before * onehot, axis=1)
    token_of = jnp.arange(pair_list.shape[0], dtype=jnp.int32) // routes_node.shape[1]
    filler = (
        jnp.full((experts * capacity,), routes_node.shape[0], jnp.int32)
        .at[pair_list * capacity + slot_index]
        .set(token_of)
    )
    return (slot_index.reshape(routes_node.shape), filler.reshape(experts, capacity))


def sources_for(owners, owner_number, seg_count):
    has_seg = jnp.any(owners == owner_number, axis=1)
    has_int = has_seg.astype(jnp.int32)
    seg_rank = jnp.cumsum(has_int) - has_int
    node_ids = jnp.arange(owners.shape[0], dtype=jnp.int32)
    seg_numbers = jnp.arange(seg_count, dtype=jnp.int32)
    return jnp.sum(
        jnp.where(
            has_seg[None, :] & (seg_rank[None, :] == seg_numbers[:, None]), node_ids[None, :], 0
        ),
        axis=1,
    )


def local(
    hidden_states, norm_gain, gate_up_weight, down_weight, routes, gates, kv_rows, lengths, owners
):
    node_count = lax.axis_size("dp")
    column_count = lax.axis_size("mp")
    node_index = lax.axis_index("dp")
    column_index = lax.axis_index("mp")
    tok_node = hidden_states.shape[0]
    model_width = hidden_states.shape[1] * column_count
    ff_dev = down_weight.shape[0]
    ff_part = min(FF, ff_dev)
    held_count = ff_dev // ff_part
    capacity = CAP
    seg_count = owners.shape[1]
    whole_rows = lax.all_gather(hidden_states, "mp", axis=1, tiled=True)
    wide_rows = whole_rows.astype(jnp.float32)
    inv_scale = lax.rsqrt(jnp.mean(wide_rows * wide_rows, axis=1, keepdims=True) + epsilon)
    normed = (wide_rows * inv_scale * norm_gain[None, :]).astype(jnp.bfloat16)
    padded = jnp.concatenate([normed, jnp.zeros((1, model_width), jnp.bfloat16)], axis=0)
    slot_index, filler = node_slots(routes, EXPERTS, capacity)
    destination = jnp.arange(node_count, dtype=jnp.int32)
    first_unit = (destination * column_count + column_index) * ff_dev
    held_experts = first_unit[:, None] // FF + jnp.arange(held_count, dtype=jnp.int32)[None, :]
    send_rows = filler[held_experts]
    weights_gate_up = gate_up_weight.reshape(2, held_count, ff_part, model_width)
    weights_down = down_weight.reshape(held_count, ff_part, model_width)
    outgoing = padded[send_rows]
    gate_up = jnp.einsum(
        "jhcd,ghfd->gjhcf",
        lax.all_to_all(outgoing, "dp", split_axis=0, concat_axis=0, tiled=True),
        weights_gate_up,
        preferred_element_type=jnp.float32,
    )
    activated = (jax.nn.silu(gate_up[0]) * gate_up[1]).astype(jnp.bfloat16)
    served = jnp.einsum(
        "jhcf,hfd->jhcd", activated, weights_down, preferred_element_type=jnp.float32
    )
    returned = lax.all_to_all(served, "dp", split_axis=0, concat_axis=0, tiled=True)
    owner_node = routes // (EXPERTS // node_count)
    base_expert = (owner_node * column_count + column_index) * ff_dev // FF
    offset = routes - base_expert
    usable = (offset >= 0) & (offset < held_count) & (slot_index >= 0) & (slot_index < capacity)
    position = (
        owner_node * held_count + jnp.clip(offset, 0, held_count - 1)
    ) * capacity + jnp.clip(slot_index, 0, capacity - 1)
    flat_rows = returned.reshape(-1, model_width)
    weight = jnp.where(usable, gates, 0.0)
    term_sum = jnp.zeros((tok_node, model_width), jnp.float32)
    for choice_number in range(TOPK):
        picked = flat_rows[position[:, choice_number]]
        term_sum = term_sum + weight[:, choice_number][:, None] * picked
    moe_share = lax.psum_scatter(term_sum, "mp", scatter_dimension=1, tiled=True)
    mixed_out = (hidden_states.astype(jnp.float32) + moe_share).astype(jnp.bfloat16)
    kv_width = kv_rows.shape[1]
    starts = jnp.cumsum(lengths, axis=1) - lengths
    page_slot = jnp.arange(SEND_CAP, dtype=jnp.int32)
    source_of = sources_for(owners, node_index, seg_count)
    all_rows = lax.all_gather(kv_rows, "dp", axis=0, tiled=True)
    owner_match = owners == node_index
    seg_len = jnp.sum(jnp.where(owner_match, lengths, 0), axis=1)
    seg_start = jnp.sum(jnp.where(owner_match, starts, 0), axis=1) + destination * tok_node
    row_index = jnp.where(
        page_slot[None, :] < seg_len[:, None],
        seg_start[:, None] + page_slot[None, :],
        node_count * tok_node,
    )
    padded_all = jnp.concatenate([all_rows, jnp.zeros((1, kv_width), jnp.bfloat16)], axis=0)
    cache_rows = padded_all[row_index[source_of]].reshape(-1, kv_width)
    return (mixed_out, cache_rows)


def solution(mesh):
    in_specs = (
        P(("groups", "dp"), "mp"),
        P(),
        P(None, ("dp", "mp"), None),
        P(("dp", "mp"), None),
        P(("groups", "dp"), None),
        P(("groups", "dp"), None),
        P(("groups", "dp"), "mp"),
        P("groups", None),
        P("groups", None),
    )
    out_specs = (P(("groups", "dp"), "mp"), P(("groups", "dp"), "mp"))
    return jax.shard_map(local, mesh=mesh, in_specs=in_specs, out_specs=out_specs, check_vma=False)
```

profile of v0, /device:TPU:0, one launch (start us, length us, event | category | flops | bytes accessed | tf_op | source)
XLA Modules:
  0.0 285.0 jit_solution(2932074452341663129)
XLA Ops:
  7.2 0.8 copy.47
  8.3 0.2 fusion.17
  8.7 0.4 fusion.16
  9.4 4.3 %scatter_custom_fusion = s32[2048]{0:T(1024)S(1)} fusion(s32[1024]{0:T(1024)S(1)} %bitcast.68, s32[1024]{0:T(1024)S(1)} %add_select_fusion.2, s32[]{:T(128)} %constant.98.clone.1), kind=kCustom, calls=%fused_computation.102 | custom fusion | bytes 8196 | tf_op jit(solution)/shard_map/scatter | solution.py:25
  14.0 0.6 gather_fusion
  14.7 8.6 %all_gather.6 = bf16[128,2048]{1,0:T(8,128)(2,1)S(1)} all-gather(bf16[128,512]{1,0:T(8,128)(2,1)S(1)} %copy-done), channel_id=1, replica_groups=mesh['groups'=2,'dp'=4,'mp'=4] {'mp'}, dimensions={1}, use_global_device_ids=true | all-gather | bytes 655360 | tf_op jit(solution)/shard_map/all_gather | solution.py:58
  23.3 0.2 fusion.10
  23.5 0.2 fusion.12
  23.8 2.5 gather_fusion.1
  26.2 53.5 %all_to_all.10 = bf16[4,8,16,2048]{3,2,1,0:T(8,128)(2,1)} all-to-all(bf16[4,8,16,2048]{3,2,1,0:T(8,128)(2,1)S(1)} %bitcast.66), channel_id=1, replica_groups=mesh['groups'=2,'dp'=4,'mp'=4] {'dp'}, dimensions={0} | all-to-all | bytes 4194304 | tf_op jit(solution)/shard_map/all_to_all | solution.py:73
  79.7 23.3 %fusion.3 = f32[2,4,8,16,768]{4,3,0,1,2:T(8,128)} fusion(bf16[2,8,768,2048,1]{3,2,1,0,4:T(8,128)(2,1)} %bitcast.69, bf16[4,8,16,2048]{3,2,1,0:T(8,128)(2,1)} %all_to_all.10), kind=kOutput, calls=%fused_computation.17 | convolution fusion | flops 3221225472 | bytes 55574528 | tf_op jit(solution)/shard_map/jhcd,ghfd->gjhcf/dot_general | solution.py:71
  103.0 11.4 %convolution_bitcast_fusion = f32[4,8,16,2048]{3,2,0,1:T(8,128)S(1)} fusion(bf16[8,768,2048,1]{2,1,3,0:T(8,128)(2,1)} %bitcast.65, f32[2,4,8,16,768]{4,3,0,1,2:T(8,128)} %fusion.3), kind=kOutput, calls=%fused_computation.15 | convolution fusion | flops 1612972032 | bytes 32505856 | tf_op jit(solution)/shard_map/jhcf,hfd->jhcd/dot_general | solution.py:78
  114.4 2.2 copy.57
  116.7 5.0 %all-to-all-start.1 = ((f32[4,8,16,2048]{3,2,1,0:T(8,128)}), f32[4,8,16,2048]{3,2,1,0:T(8,128)}, u32[]{:S(2)}, u32[]{:S(2)}) async-start(f32[4,8,16,2048]{3,2,1,0:T(8,128)} %copy.57), calls=%async_computation.1 | async-start | bytes 8388608 | tf_op jit(solution)/shard_map/all_to_all | solution.py:81
  121.7 0.2 reduce-scatter.2.cloned.1.call-start
  122.2 0.4 fusion.22
  122.8 0.4 slice_reduce_fusion.7
  123.1 91.4 %all-to-all-done.1 = f32[4,8,16,2048]{3,2,1,0:T(8,128)} async-done(((f32[4,8,16,2048]{3,2,1,0:T(8,128)}), f32[4,8,16,2048]{3,2,1,0:T(8,128)}, u32[]{:S(2)}, u32[]{:S(2)}) %all-to-all-start.1) | async-done | bytes 4194336 | tf_op jit(solution)/shard_map/all_to_all | solution.py:81
  214.5 3.6 %gather_fusion.2 = f32[128,2048]{1,0:T(8,128)S(1)} fusion(f32[512,2048]{1,0:T(8,128)} %bitcast.17, s32[1024]{0:T(1024)S(1)} %get-tuple-element.33), kind=kCustom, calls=%fused_computation.2 | custom fusion | bytes 2097664 | tf_op jit(solution)/shard_map/gather | solution.py:93
  218.2 3.6 %gather_fusion.3 = f32[128,2048]{1,0:T(8,128)S(1)} fusion(f32[512,2048]{1,0:T(8,128)} %bitcast.17, s32[1024]{0:T(1024)S(1)} %get-tuple-element.32), kind=kCustom, calls=%fused_computation.3 | custom fusion | bytes 2097664 | tf_op jit(solution)/shard_map/gather | solution.py:93
  221.8 3.6 %gather_fusion.4 = f32[128,2048]{1,0:T(8,128)S(1)} fusion(f32[512,2048]{1,0:T(8,128)} %bitcast.17, s32[1024]{0:T(1024)S(1)} %get-tuple-element.31), kind=kCustom, calls=%fused_computation.4 | custom fusion | bytes 2097664 | tf_op jit(solution)/shard_map/gather | solution.py:93
  225.5 4.6 %gather_fusion.5 = f32[128,2048]{1,0:T(8,128)} fusion(f32[512,2048]{1,0:T(8,128)} %bitcast.17, s32[1024]{0:T(1024)S(1)} %get-tuple-element.30), kind=kCustom, calls=%fused_computation.5 | custom fusion | bytes 2097664 | tf_op jit(solution)/shard_map/gather | solution.py:93
  230.1 4.6 %gather_fusion.6 = f32[128,2048]{1,0:T(8,128)} fusion(f32[512,2048]{1,0:T(8,128)} %bitcast.17, s32[1024]{0:T(1024)S(1)} %get-tuple-element.29), kind=kCustom, calls=%fused_computation.6 | custom fusion | bytes 2097664 | tf_op jit(solution)/shard_map/gather | solution.py:93
  234.7 4.6 %gather_fusion.7 = f32[128,2048]{1,0:T(8,128)} fusion(f32[512,2048]{1,0:T(8,128)} %bitcast.17, s32[1024]{0:T(1024)S(1)} %get-tuple-element.28), kind=kCustom, calls=%fused_computation.7 | custom fusion | bytes 2097664 | tf_op jit(solution)/shard_map/gather | solution.py:93
  239.3 4.6 %gather_fusion.8 = f32[128,2048]{1,0:T(8,128)} fusion(f32[512,2048]{1,0:T(8,128)} %bitcast.17, s32[1024]{0:T(1024)S(1)} %get-tuple-element.27), kind=kCustom, calls=%fused_computation.8 | custom fusion | bytes 2097664 | tf_op jit(solution)/shard_map/gather | solution.py:93
  243.8 4.7 %gather_fusion.9 = f32[128,2048]{1,0:T(8,128)} fusion(f32[512,2048]{1,0:T(8,128)} %bitcast.17, s32[1024]{0:T(1024)S(1)} %get-tuple-element.26), kind=kCustom, calls=%fused_computation.9 | custom fusion | bytes 2097664 | tf_op jit(solution)/shard_map/gather | solution.py:93
  248.5 4.2 %multiply_add_fusion = f32[128,2048]{1,0:T(8,128)} fusion(f32[128,2048]{1,0:T(8,128)} %gather_fusion.9, f32[128,2048]{1,0:T(8,128)} %gather_fusion.8, f32[128,2048]{1,0:T(8,128)} %gather_fusion.7, f32[128,2048]{1,0:T(8,128)} %gather_fusion.6, f32[128,2048]{1,0:T(8,128)} %gather_fusion.5, f32[128,2048]{1,0:T(8,128)S(1)} %gather_fusion.4, ...), kind=kLoop, calls=%fused_computation.27 | loop fusion | flops 3932160 | bytes 9441280 | tf_op jit(solution)/shard_map/add | solution.py:94
  253.5 0.6 gather_fusion.10
  254.2 14.2 %all_gather.7 = bf16[512,256]{1,0:T(8,128)(2,1)S(1)} all-gather(bf16[128,256]{1,0:T(8,128)(2,1)S(1)} %copy-done.1), channel_id=1, replica_groups=mesh['groups'=2,'dp'=4,'mp'=4] {'dp'}, dimensions={0}, use_global_device_ids=true | all-gather | bytes 327680 | tf_op jit(solution)/shard_map/all_gather | solution.py:101
  268.4 1.6 gather_fusion.11
  270.0 6.5 %reduce-scatter.2.cloned.1.call-done = f32[128,512]{1,0:T(8,128)} async-done(((f32[128,2048]{1,0:T(8,128)}), f32[128,512]{1,0:T(8,128)}) %reduce-scatter.2.cloned.1.call-update) | async-done | bytes 262160 | tf_op jit(solution)/shard_map/reduce_scatter | solution.py:95
  276.5 1.6 add_convert_fusion
  (60 shorter events, 2.5 us)
Async XLA Ops:
  7.2 7.5 %copy-start = (bf16[128,512]{1,0:T(8,128)(2,1)S(1)}, bf16[128,512]{1,0:T(8,128)(2,1)}, u32[]{:S(2)}) copy-start(bf16[128,512]{1,0:T(8,128)(2,1)} %param.9) | copy-start | bytes 393220
  7.2 16.3 %copy-start.2 = (f32[2048]{0:T(1024)S(1)}, f32[2048]{0:T(1024)}, u32[]{:S(2)}) copy-start(f32[2048]{0:T(1024)} %param.10) | copy-start | bytes 24580
  116.7 5.4 %copy-start.4 = (f32[128,8]{0,1:T(8,128)S(1)}, f32[128,8]{0,1:T(8,128)}, u32[]{:S(2)}) copy-start(f32[128,8]{0,1:T(8,128)} %param.14) | copy-start | bytes 12292
  116.7 97.9 %all-to-all-start.1 = ((f32[4,8,16,2048]{3,2,1,0:T(8,128)}), f32[4,8,16,2048]{3,2,1,0:T(8,128)}, u32[]{:S(2)}, u32[]{:S(2)}) async-start(f32[4,8,16,2048]{3,2,1,0:T(8,128)} %copy.57), calls=%async_computation.1 | async-start | bytes 8388608 | tf_op jit(solution)/shard_map/all_to_all | solution.py:81
  121.7 154.9 %reduce-scatter.2.cloned.1.call-start = ((), (), s32[]{:S(2)}) async-start(), calls=%async_computation.3 | async-start | bytes 1310720 | tf_op jit(solution)/shard_map/reduce_scatter | solution.py:95
  248.5 4.3 %copy-start.5 = (s32[4,4]{1,0:T(4,128)S(1)}, s32[4,4]{1,0:T(4,128)}, u32[]{:S(2)}) copy-start(s32[4,4]{1,0:T(4,128)} %param.17) | copy-start | bytes 196
  248.5 4.6 %copy-start.3 = (s32[4,4]{1,0:T(4,128)S(1)}, s32[4,4]{1,0:T(4,128)}, u32[]{:S(2)}) copy-start(s32[4,4]{1,0:T(4,128)} %param.16) | copy-start | bytes 196
  248.5 5.7 %copy-start.1 = (bf16[128,256]{1,0:T(8,128)(2,1)S(1)}, bf16[128,256]{1,0:T(8,128)(2,1)}, u32[]{:S(2)}) copy-start(bf16[128,256]{1,0:T(8,128)(2,1)} %param.15) | copy-start | bytes 196612
Sparse Core Ops, SparseCore 0:
  252.9 23.6 reduce-scatter.1
where the time goes:
time: 286 us; the launch traced here: 285 us
  waiting for transfers between devices  98 us (34%)
  blocking collectives  76.3 us (27%)
  local copies, waits for them, and re-layouts  48.1 us (17%)
  matrix products  34.7 us (12%)
  between operations  14.3 us (5%)
  other arithmetic  8.37 us (3%)
  starting transfers between devices  5.21 us (2%)
    all_to_all x1, waiting for transfers between devices, local(): lax.all_to_all(served, 'dp', split_axis=0, concat_axis=0, tiled=True)  91.4 us
    all_to_all x1, blocking collectives, local(): lax.all_to_all(outgoing, 'dp', split_axis=0, concat_axis=0, tiled=True)  53.5 us
    gather x8, local copies, waits for them, and re-layouts, local(): picked = flat_rows[position[:, choice_number]]  33.9 us
    dot_general x1, matrix products, local(): jnp.einsum('jhcd,ghfd->gjhcf', lax.all_to_all(outgoing, 'dp', split_axis=...  23.3 us
    all_gather x1, blocking collectives, local(): all_rows = lax.all_gather(kv_rows, 'dp', axis=0, tiled=True)  14.2 us
    dot_general x1, matrix products, local(): jnp.einsum('jhcf,hfd->jhcd', activated, weights_down, preferred_element_t...  11.4 us
    all_gather x1, blocking collectives, local(): whole_rows = lax.all_gather(hidden_states, 'mp', axis=1, tiled=True)  8.62 us
    reduce_scatter x1, waiting for transfers between devices, local(): lax.psum_scatter(term_sum, 'mp', scatter_dimension=1, tiled=True)  6.55 us
  transfers between devices with their start and end apart: 2, of which 2 were waited for; matrix products, arithmetic and copies ran while one was open for 1% of the time, Pallas kernels for 0%

commit v1 on v0

v1 whole, which is shorter than its diff:
```python
import functools

import jax
import jax.numpy as jnp
from jax import lax
from jax.experimental import pallas as pl
from jax.experimental.pallas import tpu as pltpu
from jax.sharding import PartitionSpec as P

FF = 768
EXPERTS = 128
TOPK = 8
CAP = 16
SEND_CAP = 40


epsilon = 1e-06


def sources_for(owners, owner_number, seg_count):
    has_seg = jnp.any(owners == owner_number, axis=1)
    has_int = has_seg.astype(jnp.int32)
    seg_rank = jnp.cumsum(has_int) - has_int
    node_ids = jnp.arange(owners.shape[0], dtype=jnp.int32)
    seg_numbers = jnp.arange(seg_count, dtype=jnp.int32)
    return jnp.sum(
        jnp.where(
            has_seg[None, :] & (seg_rank[None, :] == seg_numbers[:, None]), node_ids[None, :], 0
        ),
        axis=1,
    )


def expert_kernel(
    first_expert_ref, rows_ref, gain_ref, routes_ref, gates_ref, gate_up_ref, down_ref, out_ref,
    normed_ref, pick_ref, picked_ref, slot_gate_ref, served_ref, gu_buf, down_buf, gu_sem, down_sem,
    *, held, capacity, pieces, slots,
):
    nodes, columns, tok_node, width = rows_ref.shape
    tokens = nodes * tok_node
    model_width = columns * width
    ff_part = down_ref.shape[0] // held
    ff_piece = ff_part // pieces
    steps = held * pieces

    def fetch(step, slot):
        at = pl.multiple_of(step * ff_piece, ff_piece)
        return (
            pltpu.make_async_copy(
                gate_up_ref.at[:, pl.ds(at, ff_piece), :], gu_buf.at[slot], gu_sem.at[slot]
            ),
            pltpu.make_async_copy(
                down_ref.at[pl.ds(at, ff_piece), :], down_buf.at[slot], down_sem.at[slot]
            ),
        )

    for step in range(min(slots, steps)):
        for copy in fetch(step, step):
            copy.start()

    for node in range(nodes):
        at = node * tok_node
        total = jnp.zeros((tok_node, 1), jnp.float32)
        for column in range(columns):
            wide = rows_ref[node, column].astype(jnp.float32)
            total = total + jnp.sum(wide * wide, axis=1, keepdims=True)
        inv_scale = lax.rsqrt(total / model_width + epsilon)
        for column in range(columns):
            wide = rows_ref[node, column].astype(jnp.float32)
            part = pl.ds(column * width, width)
            normed_ref[pl.ds(at, tok_node), part] = (
                wide * inv_scale * gain_ref[:, part]
            ).astype(jnp.bfloat16)

    expert = first_expert_ref[0] + lax.broadcasted_iota(jnp.int32, (held, 1), 0)
    named = jnp.zeros((held, tokens), jnp.float32)
    gate = jnp.zeros((held, tokens), jnp.float32)
    for choice in range(routes_ref.shape[0]):
        match = routes_ref[choice : choice + 1, :] == expert
        named = named + jnp.where(match, 1.0, 0.0)
        gate = gate + jnp.where(match, gates_ref[choice : choice + 1, :], 0.0)
    earlier = (
        lax.broadcasted_iota(jnp.int32, (tokens, tokens), 0)
        < lax.broadcasted_iota(jnp.int32, (tokens, tokens), 1)
    )
    rank = jnp.dot(
        named.astype(jnp.bfloat16),
        jnp.where(earlier, 1.0, 0.0).astype(jnp.bfloat16),
        preferred_element_type=jnp.float32,
    )
    rank = jnp.where(named > 0.0, rank, -1.0).astype(jnp.int32)
    slot_number = lax.broadcasted_iota(jnp.int32, (capacity, tokens), 0)
    for h in range(held):
        here = rank[h : h + 1, :] == slot_number
        at = pl.ds(h * capacity, capacity)
        pick_ref[at, :] = jnp.where(here, 1.0, 0.0).astype(jnp.bfloat16)
        slot_gate_ref[at, :] = jnp.sum(
            jnp.where(here, gate[h : h + 1, :], 0.0), axis=1, keepdims=True
        )
    picked_ref[...] = jnp.dot(
        pick_ref[...], normed_ref[...], preferred_element_type=jnp.float32
    ).astype(jnp.bfloat16)

    def one_expert(h, carry):
        at = pl.ds(pl.multiple_of(h * capacity, capacity), capacity)
        rows = picked_ref[at, :]
        served = jnp.zeros((capacity, model_width), jnp.float32)
        for piece in range(pieces):
            step = h * pieces + piece
            slot = lax.rem(step, slots)
            for copy in fetch(step, slot):
                copy.wait()
            along = (((1,), (1,)), ((), ()))
            gate_part = lax.dot_general(
                rows, gu_buf[slot, 0], along, preferred_element_type=jnp.float32
            )
            up_part = lax.dot_general(
                rows, gu_buf[slot, 1], along, preferred_element_type=jnp.float32
            )
            activated = (jax.nn.silu(gate_part) * up_part).astype(jnp.bfloat16)
            served = served + jnp.dot(
                activated, down_buf[slot], preferred_element_type=jnp.float32
            )

            @pl.when(step + slots < steps)
            def _():
                for copy in fetch(step + slots, slot):
                    copy.start()

        served_ref[at, :] = (served * slot_gate_ref[at, :]).astype(jnp.bfloat16)
        return carry

    lax.fori_loop(0, held, one_expert, 0)

    for node in range(nodes):
        back = pick_ref[:, pl.ds(node * tok_node, tok_node)]
        summed = lax.dot_general(
            back, served_ref[...], (((0,), (0,)), ((), ())), preferred_element_type=jnp.float32
        ).astype(jnp.bfloat16)
        for column in range(columns):
            out_ref[node, column] = summed[:, column * width : (column + 1) * width]


def expert_sums(first_expert, rows, gain, routes, gates, gate_up_weight, down_weight):
    nodes, columns, tok_node, width = rows.shape
    tokens = nodes * tok_node
    model_width = columns * width
    ff_dev = down_weight.shape[0]
    held = max(1, ff_dev // FF)
    capacity = CAP * nodes
    pieces = 2 if ff_dev >= FF else 1
    ff_piece = ff_dev // held // pieces
    slots = min(6, held * pieces)
    all_slots = held * capacity
    vmem = pl.BlockSpec(memory_space=pltpu.VMEM)
    return pl.pallas_call(
        functools.partial(
            expert_kernel, held=held, capacity=capacity, pieces=pieces, slots=slots
        ),
        out_shape=jax.ShapeDtypeStruct(rows.shape, jnp.bfloat16),
        in_specs=[
            pl.BlockSpec(memory_space=pltpu.SMEM),
            vmem, vmem, vmem, vmem,
            pl.BlockSpec(memory_space=pl.ANY),
            pl.BlockSpec(memory_space=pl.ANY),
        ],
        out_specs=vmem,
        scratch_shapes=[
            pltpu.VMEM((tokens, model_width), jnp.bfloat16),
            pltpu.VMEM((all_slots, tokens), jnp.bfloat16),
            pltpu.VMEM((all_slots, model_width), jnp.bfloat16),
            pltpu.VMEM((all_slots, 1), jnp.float32),
            pltpu.VMEM((all_slots, model_width), jnp.bfloat16),
            pltpu.VMEM((slots, 2, ff_piece, model_width), jnp.bfloat16),
            pltpu.VMEM((slots, ff_piece, model_width), jnp.bfloat16),
            pltpu.SemaphoreType.DMA((slots,)),
            pltpu.SemaphoreType.DMA((slots,)),
        ],
        compiler_params=pltpu.CompilerParams(vmem_limit_bytes=60 * 1024 * 1024),
        cost_estimate=pl.CostEstimate(
            flops=6 * all_slots * (ff_dev // held) * model_width,
            bytes_accessed=6 * ff_dev * model_width,
            transcendentals=0,
        ),
    )(first_expert, rows, gain, routes, gates, gate_up_weight, down_weight)


def local(
    hidden_states, norm_gain, gate_up_weight, down_weight, routes, gates, kv_rows, lengths, owners
):
    node_count = lax.axis_size("dp")
    column_count = lax.axis_size("mp")
    node_index = lax.axis_index("dp")
    column_index = lax.axis_index("mp")
    tok_node, width = hidden_states.shape
    ff_dev = down_weight.shape[0]
    seg_count = owners.shape[1]
    rows = lax.all_gather(hidden_states, ("dp", "mp"), axis=0, tiled=False)
    rows = rows.reshape(node_count, column_count, tok_node, width)
    choices = jnp.concatenate([routes.astype(jnp.float32), gates], axis=1)
    choices = lax.all_gather(choices, "dp", axis=0, tiled=True)
    all_routes = choices[:, :TOPK].astype(jnp.int32).T
    all_gates = choices[:, TOPK:].T
    first_expert = ((node_index * column_count + column_index) * ff_dev // FF).reshape(1)
    partial_sums = expert_sums(
        first_expert, rows, norm_gain[None, :], all_routes, all_gates, gate_up_weight, down_weight
    )
    moe_share = lax.psum_scatter(
        partial_sums.reshape(node_count * column_count, tok_node, width),
        ("dp", "mp"), scatter_dimension=0, tiled=False,
    )
    mixed_out = (
        hidden_states.astype(jnp.float32) + moe_share.astype(jnp.float32)
    ).astype(jnp.bfloat16)
    kv_width = kv_rows.shape[1]
    starts = jnp.cumsum(lengths, axis=1) - lengths
    page_slot = jnp.arange(SEND_CAP, dtype=jnp.int32)
    destination = jnp.arange(node_count, dtype=jnp.int32)
    source_of = sources_for(owners, node_index, seg_count)
    all_rows = lax.all_gather(kv_rows, "dp", axis=0, tiled=True)
    owner_match = owners == node_index
    seg_len = jnp.sum(jnp.where(owner_match, lengths, 0), axis=1)
    seg_start = jnp.sum(jnp.where(owner_match, starts, 0), axis=1) + destination * tok_node
    row_index = jnp.where(
        page_slot[None, :] < seg_len[:, None],
        seg_start[:, None] + page_slot[None, :],
        node_count * tok_node,
    )
    padded_all = jnp.concatenate([all_rows, jnp.zeros((1, kv_width), jnp.bfloat16)], axis=0)
    cache_rows = padded_all[row_index[source_of]].reshape(-1, kv_width)
    return (mixed_out, cache_rows)


def solution(mesh):
    in_specs = (
        P(("groups", "dp"), "mp"),
        P(),
        P(None, ("dp", "mp"), None),
        P(("dp", "mp"), None),
        P(("groups", "dp"), None),
        P(("groups", "dp"), None),
        P(("groups", "dp"), "mp"),
        P("groups", None),
        P("groups", None),
    )
    out_specs = (P(("groups", "dp"), "mp"), P(("groups", "dp"), "mp"))
    return jax.shard_map(local, mesh=mesh, in_specs=in_specs, out_specs=out_specs, check_vma=False)
```

time: 286 us -> 153 us (0.53)
  blocking collectives: 76.3 us -> 28.6 us
  local copies, waits for them, and re-layouts: 48.1 us -> 2.24 us
  matrix products: 34.7 us -> 0 us
  Pallas kernels: 0 us -> 29.8 us
  waiting for transfers between devices: 98 us -> 74 us
  starting transfers between devices: 5.21 us -> 0.08 us
  other arithmetic: 8.37 us -> 4.32 us
    all_to_all x1 -> x0, waiting for transfers between devices: 91.4 us -> none  [local(): lax.all_to_all(served, 'dp', split_axis=0, concat_axis=0, tiled=True)]
    all_to_all x1 -> x0, blocking collectives: 53.5 us -> none  [local(): lax.all_to_all(outgoing, 'dp', split_axis=0, concat_axis=0, tiled=True)]
    reduce_scatter x1, waiting for transfers between devices: 6.55 us -> 43.7 us  [local(): lax.psum_scatter(partial_sums.reshape(node_count * column_count, tok_node...]
    gather x10 -> x0, local copies, waits for them, and re-layouts: 37 us -> none  [the longest x8 33.9 us: local(): picked = flat_rows[position[:, choice_number]]]
    dot_general x2 -> x0, matrix products: 34.7 us -> none  [the longest x1 23.3 us: local(): jnp.einsum('jhcd,ghfd->gjhcf', lax.all_to_all(outgoing, 'dp', split_axis=...]
    pallas_call x0 -> x1, Pallas kernels: none -> 29.8 us  [expert_sums(): pl.pallas_call(functools.partial(expert_kernel, held=held, capacity=capac...]
    all_gather x0 -> x1, waiting for transfers between devices: none -> 29.5 us  [local(): rows = lax.all_gather(hidden_states, ('dp', 'mp'), axis=0, tiled=False)]
    all_gather x1, blocking collectives: 8.62 us -> 14.8 us  [local(): choices = lax.all_gather(choices, 'dp', axis=0, tiled=True)]
  transfers between devices with their start and end apart: 2 -> 2, of which waited for: 2 -> 2; matrix products, arithmetic and copies ran while one was open for 1% -> 3% of each run, Pallas kernels for 0% -> 0%
where the time goes in v1:
time: 153 us
  waiting for transfers between devices  74 us (48%)
  Pallas kernels  29.8 us (19%)
  blocking collectives  28.6 us (19%)
  between operations  14.1 us (9%)
  other arithmetic  4.32 us (3%)
  local copies, waits for them, and re-layouts  2.24 us (1%)
    reduce_scatter x1, waiting for transfers between devices, local(): lax.psum_scatter(partial_sums.reshape(node_count * column_count, tok_node...  43.7 us
    pallas_call x1, Pallas kernels, expert_sums(): pl.pallas_call(functools.partial(expert_kernel, held=held, capacity=capac...  29.8 us
    all_gather x1, waiting for transfers between devices, local(): rows = lax.all_gather(hidden_states, ('dp', 'mp'), axis=0, tiled=False)  29.5 us
    all_gather x1, blocking collectives, local(): choices = lax.all_gather(choices, 'dp', axis=0, tiled=True)  14.8 us
    all_gather x1, blocking collectives, local(): all_rows = lax.all_gather(kv_rows, 'dp', axis=0, tiled=True)  13.8 us
  transfers between devices with their start and end apart: 2, of which 2 were waited for; matrix products, arithmetic and copies ran while one was open for 3% of the time, Pallas kernels for 0%

profile of v1, /device:TPU:0, one launch (start us, length us, event | category | flops | bytes accessed | tf_op | source)
XLA Modules:
  0.0 153.1 jit_solution(4302310484626580403)
XLA Ops:
  7.2 0.0 all-gather.3.cloned.1.call-start
  7.2 0.7 all-gather.3.cloned.1.call-update
  7.9 0.0 reduce-scatter.2.cloned.1.call-start
  8.0 0.7 convert_element_type.40
  8.7 0.7 pad_maximum_fusion
  9.3 14.8 %all_gather.14 = f32[512,16]{0,1:T(8,128)S(1)} all-gather(f32[128,16]{0,1:T(8,128)S(1)} %pad_maximum_fusion), channel_id=1, replica_groups=mesh['groups'=2,'dp'=4,'mp'=4] {'dp'}, dimensions={0}, use_global_device_ids=true | all-gather | bytes 40960 | tf_op jit(solution)/shard_map/all_gather | solution.py:201
  24.1 0.6 slice_bitcast_fusion
  24.8 29.5 %all-gather.3.cloned.1.call-done = bf16[2048,512]{1,0:T(8,128)(2,1)} async-done(((bf16[128,512]{1,0:T(8,128)(2,1)}), bf16[2048,512]{1,0:T(8,128)(2,1)}) %all-gather.3.cloned.1.call-update) | async-done | bytes 2097168 | tf_op jit(solution)/shard_map/all_gather | solution.py:198
  54.3 0.0 copy-start.2
  54.3 0.0 copy-start.3
  54.3 0.0 copy-start.1
  54.3 0.0 copy-start
  54.3 29.8 %shard_map.104 = bf16[4,4,128,512]{3,2,1,0:T(8,128)(2,1)} custom-call(s32[1]{0:T(128)} %bitcast.first_expert_ref, bf16[4,4,128,512]{3,2,1,0:T(8,128)(2,1)} %bitcast.24, f32[1,2048]{1,0:T(1,128)} %bitcast.25, s32[8,512]{1,0:T(8,128)} %get-tuple-element.7.routes_ref, f32[8,512]{1,0:T(8,128)} %get-tuple-element.6.gates_ref, bf16[2,6144,2048]{2,1,0:T(8,128)(2,1)} %gate_up_ref.1, ...), custom_call_target="tpu_custom_call" | custom-call | flops 4831838208 | bytes 75497472 | tf_op jit(solution)/shard_map/pallas_call | solution.py:156
  84.1 0.0 reduce-scatter.2.cloned.1.call-update
  84.2 0.0 copy-done.2
  84.2 0.2 reduce_window_sum.18
  84.3 0.0 copy-done.3
  84.3 0.1 fusion.4
  84.5 0.2 reduce-window.8
  84.7 0.2 select_reduce_fusion.2
  84.8 0.1 add_select_fusion
  84.9 0.6 gather_fusion
  85.5 0.1 reshape.105
  85.6 0.0 copy-done.1
  85.6 13.8 %all_gather.15 = bf16[512,256]{1,0:T(8,128)(2,1)S(1)} all-gather(bf16[128,256]{1,0:T(8,128)(2,1)S(1)} %copy-done.1), channel_id=1, replica_groups=mesh['groups'=2,'dp'=4,'mp'=4] {'dp'}, dimensions={0}, use_global_device_ids=true | all-gather | bytes 327680 | tf_op jit(solution)/shard_map/all_gather | solution.py:220
  99.4 1.6 %gather_fusion.1 = bf16[160,256]{1,0:T(8,128)(2,1)} fusion(bf16[513,256]{1,0:T(8,128)(2,1)S(1)} %concatenate.7, s32[1024]{0:T(1024)S(1)} %pad_clamp_fusion), kind=kCustom, calls=%fused_computation.1 | custom fusion | bytes 164480 | tf_op jit(solution)/shard_map/gather | solution.py:230
  101.0 43.7 %reduce-scatter.2.cloned.1.call-done = bf16[1,128,512]{2,1,0:T(8,128)(2,1)} async-done(((bf16[16,128,512]{2,1,0:T(8,128)(2,1)}), bf16[1,128,512]{2,1,0:T(8,128)(2,1)}) %reduce-scatter.2.cloned.1.call-update) | async-done | bytes 131088 | tf_op jit(solution)/shard_map/reduce_scatter | solution.py:208
  144.7 0.0 copy-done
  144.7 1.6 %fusion = bf16[128,512]{1,0:T(8,128)(2,1)} fusion(bf16[128,512]{1,0:T(8,128)(2,1)S(1)} %copy-done, bf16[1,128,512]{2,1,0:T(8,128)(2,1)} %reduce-scatter.2.cloned.1.call-done), kind=kLoop, calls=%fused_computation.3 | loop fusion | flops 262144 | bytes 393216 | tf_op jit(solution)/shard_map/convert_element_type | solution.py:214
  (8 shorter events, 0.1 us)
Async XLA Ops:
  7.2 47.1 %all-gather.3.cloned.1.call-start = ((), (), s32[]{:S(2)}) async-start(), calls=%async_computation.2 | async-start | bytes 2228224 | tf_op jit(solution)/shard_map/all_gather | solution.py:198
  7.9 136.8 %reduce-scatter.2.cloned.1.call-start = ((), (), s32[]{:S(2)}) async-start(), calls=%async_computation.1 | async-start | bytes 2228224 | tf_op jit(solution)/shard_map/reduce_scatter | solution.py:208
  54.3 29.9 %copy-start.2 = (s32[4,4]{1,0:T(4,128)S(1)}, s32[4,4]{1,0:T(4,128)}, u32[]{:S(2)}) copy-start(s32[4,4]{1,0:T(4,128)} %param.16) | copy-start | bytes 196
  54.3 30.0 %copy-start.3 = (s32[4,4]{1,0:T(4,128)S(1)}, s32[4,4]{1,0:T(4,128)}, u32[]{:S(2)}) copy-start(s32[4,4]{1,0:T(4,128)} %param.17) | copy-start | bytes 196
  54.3 31.3 %copy-start.1 = (bf16[128,256]{1,0:T(8,128)(2,1)S(1)}, bf16[128,256]{1,0:T(8,128)(2,1)}, u32[]{:S(2)}) copy-start(bf16[128,256]{1,0:T(8,128)(2,1)} %param.15) | copy-start | bytes 196612
  54.3 90.4 %copy-start = (bf16[128,512]{1,0:T(8,128)(2,1)S(1)}, bf16[128,512]{1,0:T(8,128)(2,1)}, u32[]{:S(2)}) copy-start(bf16[128,512]{1,0:T(8,128)(2,1)} %param.9) | copy-start | bytes 393220
Sparse Core Ops, SparseCore 0:
  10.2 44.0 all-gather.2
  84.3 60.3 reduce-scatter.1

commit v2 on v0

--- a/solution.py
+++ b/solution.py
@@ -1,6 +1,10 @@
+import functools
+
 import jax
 import jax.numpy as jnp
 from jax import lax
+from jax.experimental import pallas as pl
+from jax.experimental.pallas import tpu as pltpu
 from jax.sharding import PartitionSpec as P
 
 FF = 768
@@ -8,7 +12,9 @@
 TOPK = 8
 CAP = 16
 SEND_CAP = 40
-
+META_ROWS = 8
+CORES = 2
+MOST_SHIFTS = 4
 
 epsilon = 1e-06
 
@@ -41,7 +47,238 @@
     )
 
 
-def local(
+def shift_dp(value, shift):
+    count = lax.axis_size("dp")
+    return lax.ppermute(value, "dp", [(i, (i + shift) % count) for i in range(count)])
+
+
+def shift_x(value, shift):
+    count = lax.axis_size("mp")
+    return lax.ppermute(value, "mp", [(i, (i + CORES * shift) % count) for i in range(count)])
+
+
+def other_core(value):
+    count = lax.axis_size("mp")
+    return lax.ppermute(value, "mp", [(i, i ^ 1) for i in range(count)])
+
+
+def expert_kernel(
+    place_ref, gain_ref, gate_up_ref, down_ref, *refs, held, capacity, pieces, slots, parts, chips,
+):
+    block_refs, out_refs = refs[: parts * chips * CORES], refs[parts * chips * CORES :]
+    out_refs, scratch = out_refs[: parts * CORES], out_refs[parts * CORES :]
+    (
+        normed_ref, pick_ref, picked_ref, slot_gate_ref, served_ref, gu_buf, down_buf, gu_sem,
+        down_sem,
+    ) = scratch
+    each, block_rows, width = block_refs[0].shape
+    tok_node = block_rows - META_ROWS
+    tokens, model_width = normed_ref.shape
+    ff_part = down_ref.shape[0] // held
+    ff_piece = ff_part // pieces
+    steps = held * pieces
+
+    def fetch(step, slot):
+        at = pl.multiple_of(step * ff_piece, ff_piece)
+        return (
+            pltpu.make_async_copy(
+                gate_up_ref.at[:, pl.ds(at, ff_piece), :], gu_buf.at[slot], gu_sem.at[slot]
+            ),
+            pltpu.make_async_copy(
+                down_ref.at[pl.ds(at, ff_piece), :], down_buf.at[slot], down_sem.at[slot]
+            ),
+        )
+
+    for step in range(min(slots, steps)):
+        for copy in fetch(step, step):
+            copy.start()
+
+    blocks = [
+        [[block_refs[(z * chips + x) * CORES + c] for c in range(CORES)] for x in range(chips)]
+        for z in range(parts)
+    ]
+    features = [
+        [
+            pl.ds(
+                pl.multiple_of(
+                    (lax.rem(place_ref[1] + chips - x, chips) * CORES + (place_ref[2] ^ c)) * width,
+                    width,
+                ),
+                width,
+            )
+            for c in range(CORES)
+        ]
+        for x in range(chips)
+    ]
+
+    expert = place_ref[0] + lax.broadcasted_iota(jnp.int32, (held, 1), 0)
+    named, gate = [], []
+    for z in range(parts):
+        for node in range(each):
+            total = jnp.zeros((tok_node, 1), jnp.float32)
+            for x in range(chips):
+                for c in range(CORES):
+                    wide = blocks[z][x][c][node, :tok_node, :].astype(jnp.float32)
+                    total = total + jnp.sum(wide * wide, axis=1, keepdims=True)
+            inv_scale = lax.rsqrt(total / model_width + epsilon)
+            at = pl.ds((z * each + node) * tok_node, tok_node)
+            node_named = jnp.zeros((held, tok_node), jnp.float32)
+            node_gate = jnp.zeros((held, tok_node), jnp.float32)
+            for x in range(chips):
+                for c in range(CORES):
+                    block = blocks[z][x][c]
+                    wide = block[node, :tok_node, :].astype(jnp.float32)
+                    normed_ref[at, features[x][c]] = (
+                        wide * inv_scale * gain_ref[:, features[x][c]]
+                    ).astype(jnp.bfloat16)
+                    meta = block[node, tok_node:, :].astype(jnp.float32)
+                    choices = width // (2 * tok_node)
+                    for choice in range(choices):
+                        lead = slice(choice * tok_node, (choice + 1) * tok_node)
+                        tail = slice(
+                            (choices + choice) * tok_node, (choices + choice + 1) * tok_node
+                        )
+                        match = meta[0:1, lead].astype(jnp.int32) == expert
+                        value = meta[0:1, tail] + meta[1:2, lead] + meta[1:2, tail]
+                        node_named = node_named + jnp.where(match, 1.0, 0.0)
+                        node_gate = node_gate + jnp.where(match, value, 0.0)
+            named.append(node_named)
+            gate.append(node_gate)
+
+    named = jnp.concatenate(named, axis=1)
+    gate = jnp.concatenate(gate, axis=1)
+    earlier = (
+        lax.broadcasted_iota(jnp.int32, (tokens, tokens), 0)
+        < lax.broadcasted_iota(jnp.int32, (tokens, tokens), 1)
+    )
+    rank = jnp.dot(
+        named.astype(jnp.bfloat16),
+        jnp.where(earlier, 1.0, 0.0).astype(jnp.bfloat16),
+        preferred_element_type=jnp.float32,
+    )
+    rank = jnp.where(named > 0.0, rank, -1.0).astype(jnp.int32)
+    slot_number = lax.broadcasted_iota(jnp.int32, (capacity, tokens), 0)
+    for h in range(held):
+        here = rank[h : h + 1, :] == slot_number
+        at = pl.ds(h * capacity, capacity)
+        pick_ref[at, :] = jnp.where(here, 1.0, 0.0).astype(jnp.bfloat16)
+        slot_gate_ref[at, :] = jnp.sum(
+            jnp.where(here, gate[h : h + 1, :], 0.0), axis=1, keepdims=True
+        )
+    picked_ref[...] = jnp.dot(
+        pick_ref[...], normed_ref[...], preferred_element_type=jnp.float32
+    ).astype(jnp.bfloat16)
+
+    def one_expert(h, carry):
+        at = pl.ds(pl.multiple_of(h * capacity, capacity), capacity)
+        rows = picked_ref[at, :]
+        served = jnp.zeros((capacity, model_width), jnp.float32)
+        for piece in range(pieces):
+            step = h * pieces + piece
+            slot = lax.rem(step, slots)
+            for copy in fetch(step, slot):
+                copy.wait()
+            along = (((1,), (1,)), ((), ()))
+            gate_part = lax.dot_general(
+                rows, gu_buf[slot, 0], along, preferred_element_type=jnp.float32
+            )
+            up_part = lax.dot_general(
+                rows, gu_buf[slot, 1], along, preferred_element_type=jnp.float32
+            )
+            activated = (jax.nn.silu(gate_part) * up_part).astype(jnp.bfloat16)
+            served = served + jnp.dot(
+                activated, down_buf[slot], preferred_element_type=jnp.float32
+            )
+
+            @pl.when(step + slots < steps)
+            def _():
+                for copy in fetch(step + slots, slot):
+                    copy.start()
+
+        served_ref[at, :] = (served * slot_gate_ref[at, :]).astype(jnp.bfloat16)
+        return carry
+
+    lax.fori_loop(0, held, one_expert, 0)
+
+    for z in range(parts):
+        for node in range(each):
+            back = pick_ref[:, pl.ds((z * each + node) * tok_node, tok_node)]
+            for x in range(chips):
+                for c in range(CORES):
+                    out_refs[z * CORES + c][x, node] = lax.dot_general(
+                        back, served_ref[:, features[x][c]], (((0,), (0,)), ((), ())),
+                        preferred_element_type=jnp.float32,
+                    ).astype(jnp.bfloat16)
+
+
+def expert_sums(place, gain, gate_up_weight, down_weight, blocks):
+    parts, chips = len(blocks), len(blocks[0])
+    each, block_rows, width = blocks[0][0][0].shape
+    tok_node = block_rows - META_ROWS
+    tokens = parts * each * tok_node
+    model_width = chips * CORES * width
+    ff_dev = down_weight.shape[0]
+    held = max(1, ff_dev // FF)
+    capacity = CAP * parts * each
+    pieces = 2 if ff_dev >= FF else 1
+    ff_piece = ff_dev // held // pieces
+    slots = min(6, held * pieces)
+    all_slots = held * capacity
+    vmem = pl.BlockSpec(memory_space=pltpu.VMEM)
+    flat = [blocks[z][x][c] for z in range(parts) for x in range(chips) for c in range(CORES)]
+    sums = pl.pallas_call(
+        functools.partial(
+            expert_kernel, held=held, capacity=capacity, pieces=pieces, slots=slots, parts=parts,
+            chips=chips,
+        ),
+        out_shape=[jax.ShapeDtypeStruct((chips, each, tok_node, width), jnp.bfloat16)]
+        * (parts * CORES),
+        in_specs=[
+            pl.BlockSpec(memory_space=pltpu.SMEM),
+            vmem,
+            pl.BlockSpec(memory_space=pl.ANY),
+            pl.BlockSpec(memory_space=pl.ANY),
+        ]
+        + [vmem] * len(flat),
+        out_specs=[vmem] * (parts * CORES),
+        scratch_shapes=[
+            pltpu.VMEM((tokens, model_width), jnp.bfloat16),
+            pltpu.VMEM((all_slots, tokens), jnp.bfloat16),
+            pltpu.VMEM((all_slots, model_width), jnp.bfloat16),
+            pltpu.VMEM((all_slots, 1), jnp.float32),
+            pltpu.VMEM((all_slots, model_width), jnp.bfloat16),
+            pltpu.VMEM((slots, 2, ff_piece, model_width), jnp.bfloat16),
+            pltpu.VMEM((slots, ff_piece, model_width), jnp.bfloat16),
+            pltpu.SemaphoreType.DMA((slots,)),
+            pltpu.SemaphoreType.DMA((slots,)),
+        ],
+        compiler_params=pltpu.CompilerParams(vmem_limit_bytes=46 * 1024 * 1024),
+        cost_estimate=pl.CostEstimate(
+            flops=6 * all_slots * (ff_dev // held) * model_width,
+            bytes_accessed=6 * ff_dev * model_width,
+            transcendentals=0,
+        ),
+    )(place, gain, gate_up_weight, down_weight, *flat)
+    return [sums[z * CORES : (z + 1) * CORES] for z in range(parts)]
+
+
+def packed_choices(routes, gates, column_index, column_count, width):
+    mine = TOPK // column_count
+    share_routes = lax.dynamic_slice_in_dim(routes, column_index * mine, mine, 1).T
+    share_gates = lax.dynamic_slice_in_dim(gates, column_index * mine, mine, 1).T
+    first = lax.reduce_precision(share_gates, 8, 7)
+    rest = share_gates - first
+    second = lax.reduce_precision(rest, 8, 7)
+    values = jnp.stack([share_routes.astype(jnp.float32), first, second, rest - second])
+    rows = values.astype(jnp.bfloat16).reshape(-1, width)
+    return jnp.pad(rows, ((0, META_ROWS - rows.shape[0]), (0, 0)))
+
+
+def added(*values):
+    return sum(value.astype(jnp.float32) for value in values).astype(jnp.bfloat16)
+
+
+def plain_local(
     hidden_states, norm_gain, gate_up_weight, down_weight, routes, gates, kv_rows, lengths, owners
 ):
     node_count = lax.axis_size("dp")
@@ -112,6 +349,69 @@
     return (mixed_out, cache_rows)
 
 
+def local(
+    hidden_states, norm_gain, gate_up_weight, down_weight, routes, gates, kv_rows, lengths, owners
+):
+    node_count = lax.axis_size("dp")
+    column_count = lax.axis_size("mp")
+    chips = column_count // CORES
+    node_index = lax.axis_index("dp")
+    column_index = lax.axis_index("mp")
+    tok_node, width = hidden_states.shape
+    ff_dev = down_weight.shape[0]
+    seg_count = owners.shape[1]
+    block = jnp.concatenate(
+        [hidden_states, packed_choices(routes, gates, column_index, column_count, width)], axis=0
+    )[None]
+    parts = [block] + [shift_dp(block, s) for s in range(1, node_count)]
+    blocks = []
+    for part in parts:
+        row = [part] + [shift_x(part, s) for s in range(1, chips)]
+        blocks.append([[value, other_core(value)] for value in row])
+
+    place = jnp.stack(
+        [
+            (node_index * column_count + column_index) * ff_dev // FF,
+            column_index // CORES,
+            column_index % CORES,
+        ]
+    )
+    sums = expert_sums(place, norm_gain[None, :], gate_up_weight, down_weight, blocks)
+
+    shares = []
+    for keep, send in sums:
+        chip_sum = added(keep, other_core(send))
+        shares.append(
+            added(chip_sum[0], *[shift_x(chip_sum[s], -s) for s in range(1, chips)])
+        )
+    moe_share = sum(
+        (shares[s] if s == 0 else shift_dp(shares[s], -s)).astype(jnp.float32)
+        for s in range(node_count)
+    )[0]
+    mixed_out = (hidden_states.astype(jnp.float32) + moe_share).astype(jnp.bfloat16)
+
+    kv_width = kv_rows.shape[1]
+    starts = jnp.cumsum(lengths, axis=1) - lengths
+    page_slot = jnp.arange(SEND_CAP, dtype=jnp.int32)
+    source = jnp.arange(node_count, dtype=jnp.int32)
+    source_of = sources_for(owners, node_index, seg_count)
+    all_rows = jnp.concatenate(
+        [kv_rows] + [shift_dp(kv_rows, s) for s in range(1, node_count)], axis=0
+    )
+    source = (node_index - source) % node_count
+    owner_match = owners == node_index
+    seg_len = jnp.sum(jnp.where(owner_match, lengths, 0), axis=1)
+    seg_start = jnp.sum(jnp.where(owner_match, starts, 0), axis=1) + source * tok_node
+    row_index = jnp.where(
+        page_slot[None, :] < seg_len[:, None],
+        seg_start[:, None] + page_slot[None, :],
+        node_count * tok_node,
+    )
+    padded_all = jnp.concatenate([all_rows, jnp.zeros((1, kv_width), jnp.bfloat16)], axis=0)
+    cache_rows = padded_all[row_index[source_of]].reshape(-1, kv_width)
+    return (mixed_out, cache_rows)
+
+
 def solution(mesh):
     in_specs = (
         P(("groups", "dp"), "mp"),
@@ -125,4 +425,5 @@
         P("groups", None),
     )
     out_specs = (P(("groups", "dp"), "mp"), P(("groups", "dp"), "mp"))
-    return jax.shard_map(local, mesh=mesh, in_specs=in_specs, out_specs=out_specs, check_vma=False)
+    body = local if mesh.shape["dp"] <= MOST_SHIFTS else plain_local
+    return jax.shard_map(body, mesh=mesh, in_specs=in_specs, out_specs=out_specs, check_vma=False)

time: 286 us -> 90.1 us (0.32)
  blocking collectives: 76.3 us -> 0 us
  waiting for transfers between devices: 98 us -> 22 us
  local copies, waits for them, and re-layouts: 48.1 us -> 3.84 us
  matrix products: 34.7 us -> 0 us
  Pallas kernels: 0 us -> 28.4 us
  starting transfers between devices: 5.21 us -> 28.3 us
  between operations: 14.3 us -> 0.83 us
    all_to_all x1 -> x0, waiting for transfers between devices: 91.4 us -> none  [local(): lax.all_to_all(served, 'dp', split_axis=0, concat_axis=0, tiled=True)]
    all_to_all x1 -> x0, blocking collectives: 53.5 us -> none  [local(): lax.all_to_all(outgoing, 'dp', split_axis=0, concat_axis=0, tiled=True)]
    gather x10 -> x0, local copies, waits for them, and re-layouts: 37 us -> none  [the longest x8 33.9 us: local(): picked = flat_rows[position[:, choice_number]]]
    dot_general x2 -> x0, matrix products: 34.7 us -> none  [the longest x1 23.3 us: local(): jnp.einsum('jhcd,ghfd->gjhcf', lax.all_to_all(outgoing, 'dp', split_axis=...]
    pallas_call x0 -> x1, Pallas kernels: none -> 28.4 us  [expert_sums(): pl.pallas_call(functools.partial(expert_kernel, held=held, capacity=capac...]
    ppermute x0 -> x29, starting transfers between devices: none -> 28.3 us  [the longest x9 16.7 us: shift_dp(): lax.ppermute(value, 'dp', [(i, (i + shift) % count) for i in range(count)])]
    all_gather x2 -> x0, blocking collectives: 22.8 us -> none  [the longest x1 14.2 us: local(): all_rows = lax.all_gather(kv_rows, 'dp', axis=0, tiled=True)]
    ppermute x0 -> x29, waiting for transfers between devices: none -> 22 us  [the longest x8 13.2 us: shift_x(): lax.ppermute(value, 'mp', [(i, (i + CORES * shift) % count) for i in rang...]
  transfers between devices with their start and end apart: 2 -> 29, of which waited for: 2 -> 8; matrix products, arithmetic and copies ran while one was open for 1% -> 7% of each run, Pallas kernels for 0% -> 32%
where the time goes in v2:
time: 90.1 us; the launch traced here: 89.8 us
  Pallas kernels  28.4 us (32%)
  starting transfers between devices  28.3 us (31%)
  waiting for transfers between devices  22 us (24%)
  other arithmetic  6.35 us (7%)
  local copies, waits for them, and re-layouts  3.84 us (4%)
    pallas_call x1, Pallas kernels, expert_sums(): pl.pallas_call(functools.partial(expert_kernel, held=held, capacity=capac...  28.4 us
    ppermute x9, starting transfers between devices, shift_dp(): lax.ppermute(value, 'dp', [(i, (i + shift) % count) for i in range(count)])  16.7 us
    ppermute x8, waiting for transfers between devices, shift_x(): lax.ppermute(value, 'mp', [(i, (i + CORES * shift) % count) for i in rang...  13.2 us
    ppermute x8, starting transfers between devices, shift_x(): lax.ppermute(value, 'mp', [(i, (i + CORES * shift) % count) for i in rang...  9.39 us
    ppermute x9, waiting for transfers between devices, shift_dp(): lax.ppermute(value, 'dp', [(i, (i + shift) % count) for i in range(count)])  8.43 us
    ppermute x12, starting transfers between devices, other_core(): return lax.ppermute(value, 'mp', [(i, i ^ 1) for i in range(count)])  2.23 us
    gather x2, local copies, waits for them, and re-layouts, local(): cache_rows = padded_all[row_index[source_of]].reshape(-1, kv_width)  2.12 us
  transfers between devices with their start and end apart: 29, of which 8 were waited for; matrix products, arithmetic and copies ran while one was open for 7% of the time, Pallas kernels for 32%

profile of v2, /device:TPU:0, one launch (start us, length us, event | category | flops | bytes accessed | tf_op | source)
XLA Modules:
  0.0 89.8 jit_solution(10041643244812626706)
XLA Ops:
  0.6 0.7 fusion.11
  1.4 0.7 fusion.10
  2.1 0.9 %fusion.7.refs_0_ = bf16[1,136,512]{2,1,0:T(8,128)(2,1)S(1)} fusion(bf16[2,512]{1,0:T(2,128)(2,1)S(1)} %convert_element_type.171, bf16[128,512]{1,0:T(8,128)(2,1)} %param.9), kind=kLoop, calls=%fused_computation.19 | loop fusion | flops 417792 | bytes 272384 | tf_op jit(solution)/shard_map/broadcast_in_dim | solution.py:363
  3.0 4.1 %collective-permute-start.7 = (bf16[1,136,512]{2,1,0:T(8,128)(2,1)S(1)}, bf16[1,136,512]{2,1,0:T(8,128)(2,1)S(1)}, u32[]{:S(2)}, u32[]{:S(2)}) collective-permute-start(bf16[1,136,512]{2,1,0:T(8,128)(2,1)S(1)} %fusion.7.refs_0_), channel_id=1, source_target_pairs={{0,8},{4,12},{8,0},{12,4},{1,9},{5,13},{9,1},{13,5},{2,10},{6,14},... | collective-permute-start | bytes 417800 | tf_op jit(solution)/shard_map/ppermute | solution.py:52
  7.1 1.3 %collective-permute-start.11 = (bf16[1,136,512]{2,1,0:T(8,128)(2,1)S(1)}, bf16[1,136,512]{2,1,0:T(8,128)(2,1)S(1)}, u32[]{:S(2)}, u32[]{:S(2)}) collective-permute-start(bf16[1,136,512]{2,1,0:T(8,128)(2,1)S(1)} %fusion.7.refs_0_), channel_id=1, source_target_pairs={{0,12},{4,0},{8,4},{12,8},{1,13},{5,1},{9,5},{13,9},{2,14},{6,2},{... | collective-permute-start | bytes 417800 | tf_op jit(solution)/shard_map/ppermute | solution.py:52
  8.5 0.7 collective-permute-start.3
  9.2 1.5 %collective-permute-start.1 = (bf16[1,136,512]{2,1,0:T(8,128)(2,1)S(1)}, bf16[1,136,512]{2,1,0:T(8,128)(2,1)S(1)}, u32[]{:S(2)}, u32[]{:S(2)}) collective-permute-start(bf16[1,136,512]{2,1,0:T(8,128)(2,1)S(1)} %fusion.7.refs_0_), channel_id=1, source_target_pairs={{0,2},{1,3},{2,0},{3,1},{4,6},{5,7},{6,4},{7,5},{8,10},{9,11},{10,... | collective-permute-start | bytes 417800 | tf_op jit(solution)/shard_map/ppermute | solution.py:57
  10.6 0.8 fusion.18
  11.6 0.9 reduce_window_sum.18
  12.5 0.8 select_reduce_fusion.2
  13.4 0.6 gather_fusion
  14.2 1.5 %collective-permute-start.13 = (bf16[1,136,512]{2,1,0:T(8,128)(2,1)S(1)}, bf16[1,136,512]{2,1,0:T(8,128)(2,1)S(1)}, u32[]{:S(2)}, u32[]{:S(2)}) collective-permute-start(bf16[1,136,512]{2,1,0:T(8,128)(2,1)S(1)} %collective-permute-done.11.refs_12_), channel_id=1, source_target_pairs={{0,2},{1,3},{2,0},{3,1},{4,6},{5,7},{6,4},{7,5},{8,10},{9,11},{10,... | collective-permute-start | bytes 417800 | tf_op jit(solution)/shard_map/ppermute | solution.py:57
  15.7 2.2 %collective-permute-done.3.refs_4_ = bf16[1,136,512]{2,1,0:T(8,128)(2,1)S(1)} collective-permute-done((bf16[1,136,512]{2,1,0:T(8,128)(2,1)S(1)}, bf16[1,136,512]{2,1,0:T(8,128)(2,1)S(1)}, u32[]{:S(2)}, u32[]{:S(2)}) %collective-permute-start.3) | collective-permute-done | bytes 139296 | tf_op jit(solution)/shard_map/ppermute | solution.py:52
  18.0 1.5 %collective-permute-start.5 = (bf16[1,136,512]{2,1,0:T(8,128)(2,1)S(1)}, bf16[1,136,512]{2,1,0:T(8,128)(2,1)S(1)}, u32[]{:S(2)}, u32[]{:S(2)}) collective-permute-start(bf16[1,136,512]{2,1,0:T(8,128)(2,1)S(1)} %collective-permute-done.3.refs_4_), channel_id=1, source_target_pairs={{0,2},{1,3},{2,0},{3,1},{4,6},{5,7},{6,4},{7,5},{8,10},{9,11},{10,... | collective-permute-start | bytes 417800 | tf_op jit(solution)/shard_map/ppermute | solution.py:57
  19.5 0.6 collective-permute-start.9
  20.1 6.0 %collective-permute-done.9.refs_10_ = bf16[1,136,512]{2,1,0:T(8,128)(2,1)S(1)} collective-permute-done((bf16[1,136,512]{2,1,0:T(8,128)(2,1)S(1)}, bf16[1,136,512]{2,1,0:T(8,128)(2,1)S(1)}, u32[]{:S(2)}, u32[]{:S(2)}) %collective-permute-start.9) | collective-permute-done | bytes 139296 | tf_op jit(solution)/shard_map/ppermute | solution.py:57
  27.4 0.8 constant_dynamic-update-slice_fusion.4
  28.2 5.2 %collective-permute-start.26 = (bf16[128,256]{1,0:T(8,128)(2,1)}, bf16[128,256]{1,0:T(8,128)(2,1)S(1)}, u32[]{:S(2)}, u32[]{:S(2)}) collective-permute-start(bf16[128,256]{1,0:T(8,128)(2,1)} %param.15), channel_id=1, source_target_pairs={{0,4},{4,8},{8,12},{12,0},{1,5},{5,9},{9,13},{13,1},{2,6},{6,10},{... | collective-permute-start | bytes 196616 | tf_op jit(solution)/shard_map/ppermute | solution.py:52
  33.5 2.6 %collective-permute-start.28 = (bf16[128,256]{1,0:T(8,128)(2,1)}, bf16[128,256]{1,0:T(8,128)(2,1)S(1)}, u32[]{:S(2)}, u32[]{:S(2)}) collective-permute-start(bf16[128,256]{1,0:T(8,128)(2,1)} %param.15), channel_id=1, source_target_pairs={{0,12},{4,0},{8,4},{12,8},{1,13},{5,1},{9,5},{13,9},{2,14},{6,2},{... | collective-permute-start | bytes 196616 | tf_op jit(solution)/shard_map/ppermute | solution.py:52
  36.1 0.7 copy-done
  36.8 28.4 %shard_map.104 = (bf16[2,1,128,512]{3,2,1,0:T(8,128)(2,1)S(1)}, bf16[2,1,128,512]{3,2,1,0:T(8,128)(2,1)S(1)}, bf16[2,1,128,512]{3,2,1,0:T(8,128)(2,1)S(1)}, bf16...) custom-call(s32[3]{0:T(128)S(1)} %pad_add_fusion.place_ref, ...), custom_call_target="tpu_custom_call" | custom-call | flops 4831838208 | bytes 75497472 | tf_op jit(solution)/shard_map/pallas_call | solution.py:229
  66.9 1.6 %collective-permute-start.16 = (bf16[1,128,512]{2,1,0:T(8,128)(2,1)S(1)}, bf16[1,128,512]{2,1,0:T(8,128)(2,1)S(1)}, u32[]{:S(2)}, u32[]{:S(2)}) collective-permute-start(bf16[1,128,512]{2,1,0:T(8,128)(2,1)S(1)} %slice_bitcast_fusion.6), channel_id=1, source_target_pairs={{0,2},{1,3},{2,0},{3,1},{4,6},{5,7},{6,4},{7,5},{8,10},{9,11},{10,... | collective-permute-start | bytes 393224 | tf_op jit(solution)/shard_map/ppermute | solution.py:57
  68.5 0.6 collective-permute-start.18
  69.2 1.6 %collective-permute-start.21 = (bf16[1,128,512]{2,1,0:T(8,128)(2,1)S(1)}, bf16[1,128,512]{2,1,0:T(8,128)(2,1)S(1)}, u32[]{:S(2)}, u32[]{:S(2)}) collective-permute-start(bf16[1,128,512]{2,1,0:T(8,128)(2,1)S(1)} %slice_bitcast_fusion.2), channel_id=1, source_target_pairs={{0,2},{1,3},{2,0},{3,1},{4,6},{5,7},{6,4},{7,5},{8,10},{9,11},{10,... | collective-permute-start | bytes 393224 | tf_op jit(solution)/shard_map/ppermute | solution.py:57
  70.9 0.6 collective-permute-start.24
  71.5 4.6 %collective-permute-done.18 = bf16[1,128,512]{2,1,0:T(8,128)(2,1)S(1)} collective-permute-done((bf16[1,128,512]{2,1,0:T(8,128)(2,1)S(1)}, bf16[1,128,512]{2,1,0:T(8,128)(2,1)S(1)}, u32[]{:S(2)}, u32[]{:S(2)}) %collective-permute-start.18) | collective-permute-done | bytes 131104 | tf_op jit(solution)/shard_map/ppermute | solution.py:57
  76.2 1.8 %collective-permute-start.19 = (bf16[1,128,512]{2,1,0:T(8,128)(2,1)S(1)}, bf16[1,128,512]{2,1,0:T(8,128)(2,1)S(1)}, u32[]{:S(2)}, u32[]{:S(2)}) collective-permute-start(bf16[1,128,512]{2,1,0:T(8,128)(2,1)S(1)} %fusion.3), channel_id=1, source_target_pairs={{0,12},{4,0},{8,4},{12,8},{1,13},{5,1},{9,5},{13,9},{2,14},{6,2},{... | collective-permute-start | bytes 393224 | tf_op jit(solution)/shard_map/ppermute | solution.py:52
  78.0 0.9 %collective-permute-done.21 = bf16[1,128,512]{2,1,0:T(8,128)(2,1)S(1)} collective-permute-done((bf16[1,128,512]{2,1,0:T(8,128)(2,1)S(1)}, bf16[1,128,512]{2,1,0:T(8,128)(2,1)S(1)}, u32[]{:S(2)}, u32[]{:S(2)}) %collective-permute-start.21) | collective-permute-done | bytes 131104 | tf_op jit(solution)/shard_map/ppermute | solution.py:57
  79.4 1.6 %collective-permute-done.24 = bf16[1,128,512]{2,1,0:T(8,128)(2,1)S(1)} collective-permute-done((bf16[1,128,512]{2,1,0:T(8,128)(2,1)S(1)}, bf16[1,128,512]{2,1,0:T(8,128)(2,1)S(1)}, u32[]{:S(2)}, u32[]{:S(2)}) %collective-permute-start.24) | collective-permute-done | bytes 131104 | tf_op jit(solution)/shard_map/ppermute | solution.py:57
  81.5 1.6 %gather_fusion.1 = bf16[160,256]{1,0:T(8,128)(2,1)} fusion(bf16[513,256]{1,0:T(8,128)(2,1)S(1)} %constant_dynamic-update-slice_fusion, s32[1024]{0:T(1024)S(1)} %pad_clamp_fusion), kind=kCustom, calls=%fused_computation.1 | custom fusion | bytes 164480 | tf_op jit(solution)/shard_map/gather | solution.py:411
  83.1 5.9 %collective-permute-done.22 = bf16[1,128,512]{2,1,0:T(8,128)(2,1)S(1)} collective-permute-done((bf16[1,128,512]{2,1,0:T(8,128)(2,1)S(1)}, bf16[1,128,512]{2,1,0:T(8,128)(2,1)S(1)}, u32[]{:S(2)}, u32[]{:S(2)}) %collective-permute-start.22) | collective-permute-done | bytes 131104 | tf_op jit(solution)/shard_map/ppermute | solution.py:52
  89.0 0.8 fusion.5
  (69 shorter events, 4.7 us)
Async XLA Ops:
  0.6 88.4 %copy-start.1 = (bf16[128,512]{1,0:T(8,128)(2,1)S(1)}, bf16[128,512]{1,0:T(8,128)(2,1)}, u32[]{:S(2)}) copy-start(bf16[128,512]{1,0:T(8,128)(2,1)} %param.9) | copy-start | bytes 393220
  3.0 12.7 %collective-permute-start.7 = (bf16[1,136,512]{2,1,0:T(8,128)(2,1)S(1)}, bf16[1,136,512]{2,1,0:T(8,128)(2,1)S(1)}, u32[]{:S(2)}, u32[]{:S(2)}) collective-permute-start(bf16[1,136,512]{2,1,0:T(8,128)(2,1)S(1)} %fusion.7.refs_0_), channel_id=1, source_target_pairs={{0,8},{4,12},{8,0},{12,4},{1,9},{5,13},{9,1},{13,5},{2,10},{6,14},... | collective-permute-start | bytes 417800 | tf_op jit(solution)/shard_map/ppermute | solution.py:52
  7.1 7.1 %collective-permute-start.11 = (bf16[1,136,512]{2,1,0:T(8,128)(2,1)S(1)}, bf16[1,136,512]{2,1,0:T(8,128)(2,1)S(1)}, u32[]{:S(2)}, u32[]{:S(2)}) collective-permute-start(bf16[1,136,512]{2,1,0:T(8,128)(2,1)S(1)} %fusion.7.refs_0_), channel_id=1, source_target_pairs={{0,12},{4,0},{8,4},{12,8},{1,13},{5,1},{9,5},{13,9},{2,14},{6,2},{... | collective-permute-start | bytes 417800 | tf_op jit(solution)/shard_map/ppermute | solution.py:52
  8.5 9.5 %collective-permute-start.3 = (bf16[1,136,512]{2,1,0:T(8,128)(2,1)S(1)}, bf16[1,136,512]{2,1,0:T(8,128)(2,1)S(1)}, u32[]{:S(2)}, u32[]{:S(2)}) collective-permute-start(bf16[1,136,512]{2,1,0:T(8,128)(2,1)S(1)} %fusion.7.refs_0_), channel_id=1, source_target_pairs={{0,4},{4,8},{8,12},{12,0},{1,5},{5,9},{9,13},{13,1},{2,6},{6,10},{... | collective-permute-start | bytes 417800 | tf_op jit(solution)/shard_map/ppermute | solution.py:52
  9.2 10.3 %collective-permute-start.1 = (bf16[1,136,512]{2,1,0:T(8,128)(2,1)S(1)}, bf16[1,136,512]{2,1,0:T(8,128)(2,1)S(1)}, u32[]{:S(2)}, u32[]{:S(2)}) collective-permute-start(bf16[1,136,512]{2,1,0:T(8,128)(2,1)S(1)} %fusion.7.refs_0_), channel_id=1, source_target_pairs={{0,2},{1,3},{2,0},{3,1},{4,6},{5,7},{6,4},{7,5},{8,10},{9,11},{10,... | collective-permute-start | bytes 417800 | tf_op jit(solution)/shard_map/ppermute | solution.py:57
  10.6 8.8 %collective-permute-start = (bf16[1,136,512]{2,1,0:T(8,128)(2,1)S(1)}, bf16[1,136,512]{2,1,0:T(8,128)(2,1)S(1)}, u32[]{:S(2)}, u32[]{:S(2)}) collective-permute-start(bf16[1,136,512]{2,1,0:T(8,128)(2,1)S(1)} %fusion.7.refs_0_), channel_id=1, source_target_pairs={{0,1},{1,0},{2,3},{3,2},{4,5},{5,4},{6,7},{7,6},{8,9},{9,8},{10,11... | collective-permute-start | bytes 417800 | tf_op jit(solution)/shard_map/ppermute | solution.py:62
  14.2 11.9 %collective-permute-start.13 = (bf16[1,136,512]{2,1,0:T(8,128)(2,1)S(1)}, bf16[1,136,512]{2,1,0:T(8,128)(2,1)S(1)}, u32[]{:S(2)}, u32[]{:S(2)}) collective-permute-start(bf16[1,136,512]{2,1,0:T(8,128)(2,1)S(1)} %collective-permute-done.11.refs_12_), channel_id=1, source_target_pairs={{0,2},{1,3},{2,0},{3,1},{4,6},{5,7},{6,4},{7,5},{8,10},{9,11},{10,... | collective-permute-start | bytes 417800 | tf_op jit(solution)/shard_map/ppermute | solution.py:57
  15.7 11.0 %collective-permute-start.12 = (bf16[1,136,512]{2,1,0:T(8,128)(2,1)S(1)}, bf16[1,136,512]{2,1,0:T(8,128)(2,1)S(1)}, u32[]{:S(2)}, u32[]{:S(2)}) collective-permute-start(bf16[1,136,512]{2,1,0:T(8,128)(2,1)S(1)} %collective-permute-done.11.refs_12_), channel_id=1, source_target_pairs={{0,1},{1,0},{2,3},{3,2},{4,5},{5,4},{6,7},{7,6},{8,9},{9,8},{10,11... | collective-permute-start | bytes 417800 | tf_op jit(solution)/shard_map/ppermute | solution.py:62
  18.0 8.7 %collective-permute-start.5 = (bf16[1,136,512]{2,1,0:T(8,128)(2,1)S(1)}, bf16[1,136,512]{2,1,0:T(8,128)(2,1)S(1)}, u32[]{:S(2)}, u32[]{:S(2)}) collective-permute-start(bf16[1,136,512]{2,1,0:T(8,128)(2,1)S(1)} %collective-permute-done.3.refs_4_), channel_id=1, source_target_pairs={{0,2},{1,3},{2,0},{3,1},{4,6},{5,7},{6,4},{7,5},{8,10},{9,11},{10,... | collective-permute-start | bytes 417800 | tf_op jit(solution)/shard_map/ppermute | solution.py:57
  19.5 7.7 %collective-permute-start.4 = (bf16[1,136,512]{2,1,0:T(8,128)(2,1)S(1)}, bf16[1,136,512]{2,1,0:T(8,128)(2,1)S(1)}, u32[]{:S(2)}, u32[]{:S(2)}) collective-permute-start(bf16[1,136,512]{2,1,0:T(8,128)(2,1)S(1)} %collective-permute-done.3.refs_4_), channel_id=1, source_target_pairs={{0,1},{1,0},{2,3},{3,2},{4,5},{5,4},{6,7},{7,6},{8,9},{9,8},{10,11... | collective-permute-start | bytes 417800 | tf_op jit(solution)/shard_map/ppermute | solution.py:62
  19.5 6.6 %collective-permute-start.9 = (bf16[1,136,512]{2,1,0:T(8,128)(2,1)S(1)}, bf16[1,136,512]{2,1,0:T(8,128)(2,1)S(1)}, u32[]{:S(2)}, u32[]{:S(2)}) collective-permute-start(bf16[1,136,512]{2,1,0:T(8,128)(2,1)S(1)} %collective-permute-done.7.refs_8_), channel_id=1, source_target_pairs={{0,2},{1,3},{2,0},{3,1},{4,6},{5,7},{6,4},{7,5},{8,10},{9,11},{10,... | collective-permute-start | bytes 417800 | tf_op jit(solution)/shard_map/ppermute | solution.py:57
  26.1 2.1 %collective-permute-start.8 = (bf16[1,136,512]{2,1,0:T(8,128)(2,1)S(1)}, bf16[1,136,512]{2,1,0:T(8,128)(2,1)S(1)}, u32[]{:S(2)}, u32[]{:S(2)}) collective-permute-start(bf16[1,136,512]{2,1,0:T(8,128)(2,1)S(1)} %collective-permute-done.7.refs_8_), channel_id=1, source_target_pairs={{0,1},{1,0},{2,3},{3,2},{4,5},{5,4},{6,7},{7,6},{8,9},{9,8},{10,11... | collective-permute-start | bytes 417800 | tf_op jit(solution)/shard_map/ppermute | solution.py:62
  26.1 7.3 %collective-permute-start.2 = (bf16[1,136,512]{2,1,0:T(8,128)(2,1)S(1)}, bf16[1,136,512]{2,1,0:T(8,128)(2,1)S(1)}, u32[]{:S(2)}, u32[]{:S(2)}) collective-permute-start(bf16[1,136,512]{2,1,0:T(8,128)(2,1)S(1)} %collective-permute-done.1.refs_2_), channel_id=1, source_target_pairs={{0,1},{1,0},{2,3},{3,2},{4,5},{5,4},{6,7},{7,6},{8,9},{9,8},{10,11... | collective-permute-start | bytes 417800 | tf_op jit(solution)/shard_map/ppermute | solution.py:62
  26.6 6.8 %collective-permute-start.10 = (bf16[1,136,512]{2,1,0:T(8,128)(2,1)S(1)}, bf16[1,136,512]{2,1,0:T(8,128)(2,1)S(1)}, u32[]{:S(2)}, u32[]{:S(2)}) collective-permute-start(bf16[1,136,512]{2,1,0:T(8,128)(2,1)S(1)} %collective-permute-done.9.refs_10_), channel_id=1, source_target_pairs={{0,1},{1,0},{2,3},{3,2},{4,5},{5,4},{6,7},{7,6},{8,9},{9,8},{10,11... | collective-permute-start | bytes 417800 | tf_op jit(solution)/shard_map/ppermute | solution.py:62
  26.7 9.3 %collective-permute-start.14 = (bf16[1,136,512]{2,1,0:T(8,128)(2,1)S(1)}, bf16[1,136,512]{2,1,0:T(8,128)(2,1)S(1)}, u32[]{:S(2)}, u32[]{:S(2)}) collective-permute-start(bf16[1,136,512]{2,1,0:T(8,128)(2,1)S(1)} %collective-permute-done.13.refs_14_), channel_id=1, source_target_pairs={{0,1},{1,0},{2,3},{3,2},{4,5},{5,4},{6,7},{7,6},{8,9},{9,8},{10,11... | collective-permute-start | bytes 417800 | tf_op jit(solution)/shard_map/ppermute | solution.py:62
  27.2 8.9 %collective-permute-start.6 = (bf16[1,136,512]{2,1,0:T(8,128)(2,1)S(1)}, bf16[1,136,512]{2,1,0:T(8,128)(2,1)S(1)}, u32[]{:S(2)}, u32[]{:S(2)}) collective-permute-start(bf16[1,136,512]{2,1,0:T(8,128)(2,1)S(1)} %collective-permute-done.5.refs_6_), channel_id=1, source_target_pairs={{0,1},{1,0},{2,3},{3,2},{4,5},{5,4},{6,7},{7,6},{8,9},{9,8},{10,11... | collective-permute-start | bytes 417800 | tf_op jit(solution)/shard_map/ppermute | solution.py:62
  28.2 37.1 %collective-permute-start.26 = (bf16[128,256]{1,0:T(8,128)(2,1)}, bf16[128,256]{1,0:T(8,128)(2,1)S(1)}, u32[]{:S(2)}, u32[]{:S(2)}) collective-permute-start(bf16[128,256]{1,0:T(8,128)(2,1)} %param.15), channel_id=1, source_target_pairs={{0,4},{4,8},{8,12},{12,0},{1,5},{5,9},{9,13},{13,1},{2,6},{6,10},{... | collective-permute-start | bytes 196616 | tf_op jit(solution)/shard_map/ppermute | solution.py:52
  33.5 31.9 %collective-permute-start.27 = (bf16[128,256]{1,0:T(8,128)(2,1)}, bf16[128,256]{1,0:T(8,128)(2,1)S(1)}, u32[]{:S(2)}, u32[]{:S(2)}) collective-permute-start(bf16[128,256]{1,0:T(8,128)(2,1)} %param.15), channel_id=1, source_target_pairs={{0,8},{4,12},{8,0},{12,4},{1,9},{5,13},{9,1},{13,5},{2,10},{6,14},... | collective-permute-start | bytes 196616 | tf_op jit(solution)/shard_map/ppermute | solution.py:52
  33.5 48.0 %collective-permute-start.28 = (bf16[128,256]{1,0:T(8,128)(2,1)}, bf16[128,256]{1,0:T(8,128)(2,1)S(1)}, u32[]{:S(2)}, u32[]{:S(2)}) collective-permute-start(bf16[128,256]{1,0:T(8,128)(2,1)} %param.15), channel_id=1, source_target_pairs={{0,12},{4,0},{8,4},{12,8},{1,13},{5,1},{9,5},{13,9},{2,14},{6,2},{... | collective-permute-start | bytes 196616 | tf_op jit(solution)/shard_map/ppermute | solution.py:52
  36.1 0.7 copy-start
  65.2 1.6 %collective-permute-start.15 = (bf16[2,1,128,512]{3,2,1,0:T(8,128)(2,1)S(1)}, bf16[2,1,128,512]{3,2,1,0:T(8,128)(2,1)S(1)}, u32[]{:S(2)}, u32[]{:S(2)}) collective-permute-start(bf16[2,1,128,512]{3,2,1,0:T(8,128)(2,1)S(1)} %get-tuple-element.11), channel_id=1, source_target_pairs={{0,1},{1,0},{2,3},{3,2},{4,5},{5,4},{6,7},{7,6},{8,9},{9,8},{10,11... | collective-permute-start | bytes 786440 | tf_op jit(solution)/shard_map/ppermute | solution.py:62
  65.4 3.1 %collective-permute-start.17 = (bf16[2,1,128,512]{3,2,1,0:T(8,128)(2,1)S(1)}, bf16[2,1,128,512]{3,2,1,0:T(8,128)(2,1)S(1)}, u32[]{:S(2)}, u32[]{:S(2)}) collective-permute-start(bf16[2,1,128,512]{3,2,1,0:T(8,128)(2,1)S(1)} %get-tuple-element.13), channel_id=1, source_target_pairs={{0,1},{1,0},{2,3},{3,2},{4,5},{5,4},{6,7},{7,6},{8,9},{9,8},{10,11... | collective-permute-start | bytes 786440 | tf_op jit(solution)/shard_map/ppermute | solution.py:62
  65.9 3.2 %collective-permute-start.20 = (bf16[2,1,128,512]{3,2,1,0:T(8,128)(2,1)S(1)}, bf16[2,1,128,512]{3,2,1,0:T(8,128)(2,1)S(1)}, u32[]{:S(2)}, u32[]{:S(2)}) collective-permute-start(bf16[2,1,128,512]{3,2,1,0:T(8,128)(2,1)S(1)} %get-tuple-element.15), channel_id=1, source_target_pairs={{0,1},{1,0},{2,3},{3,2},{4,5},{5,4},{6,7},{7,6},{8,9},{9,8},{10,11... | collective-permute-start | bytes 786440 | tf_op jit(solution)/shard_map/ppermute | solution.py:62
  66.0 4.8 %collective-permute-start.23 = (bf16[2,1,128,512]{3,2,1,0:T(8,128)(2,1)S(1)}, bf16[2,1,128,512]{3,2,1,0:T(8,128)(2,1)S(1)}, u32[]{:S(2)}, u32[]{:S(2)}) collective-permute-start(bf16[2,1,128,512]{3,2,1,0:T(8,128)(2,1)S(1)} %get-tuple-element.17), channel_id=1, source_target_pairs={{0,1},{1,0},{2,3},{3,2},{4,5},{5,4},{6,7},{7,6},{8,9},{9,8},{10,11... | collective-permute-start | bytes 786440 | tf_op jit(solution)/shard_map/ppermute | solution.py:62
  66.9 16.2 %collective-permute-start.16 = (bf16[1,128,512]{2,1,0:T(8,128)(2,1)S(1)}, bf16[1,128,512]{2,1,0:T(8,128)(2,1)S(1)}, u32[]{:S(2)}, u32[]{:S(2)}) collective-permute-start(bf16[1,128,512]{2,1,0:T(8,128)(2,1)S(1)} %slice_bitcast_fusion.6), channel_id=1, source_target_pairs={{0,2},{1,3},{2,0},{3,1},{4,6},{5,7},{6,4},{7,5},{8,10},{9,11},{10,... | collective-permute-start | bytes 393224 | tf_op jit(solution)/shard_map/ppermute | solution.py:57
  68.5 7.6 %collective-permute-start.18 = (bf16[1,128,512]{2,1,0:T(8,128)(2,1)S(1)}, bf16[1,128,512]{2,1,0:T(8,128)(2,1)S(1)}, u32[]{:S(2)}, u32[]{:S(2)}) collective-permute-start(bf16[1,128,512]{2,1,0:T(8,128)(2,1)S(1)} %slice_bitcast_fusion.4), channel_id=1, source_target_pairs={{0,2},{1,3},{2,0},{3,1},{4,6},{5,7},{6,4},{7,5},{8,10},{9,11},{10,... | collective-permute-start | bytes 393224 | tf_op jit(solution)/shard_map/ppermute | solution.py:57
  69.2 9.7 %collective-permute-start.21 = (bf16[1,128,512]{2,1,0:T(8,128)(2,1)S(1)}, bf16[1,128,512]{2,1,0:T(8,128)(2,1)S(1)}, u32[]{:S(2)}, u32[]{:S(2)}) collective-permute-start(bf16[1,128,512]{2,1,0:T(8,128)(2,1)S(1)} %slice_bitcast_fusion.2), channel_id=1, source_target_pairs={{0,2},{1,3},{2,0},{3,1},{4,6},{5,7},{6,4},{7,5},{8,10},{9,11},{10,... | collective-permute-start | bytes 393224 | tf_op jit(solution)/shard_map/ppermute | solution.py:57
  70.9 10.0 %collective-permute-start.24 = (bf16[1,128,512]{2,1,0:T(8,128)(2,1)S(1)}, bf16[1,128,512]{2,1,0:T(8,128)(2,1)S(1)}, u32[]{:S(2)}, u32[]{:S(2)}) collective-permute-start(bf16[1,128,512]{2,1,0:T(8,128)(2,1)S(1)} %slice_bitcast_fusion), channel_id=1, source_target_pairs={{0,2},{1,3},{2,0},{3,1},{4,6},{5,7},{6,4},{7,5},{8,10},{9,11},{10,... | collective-permute-start | bytes 393224 | tf_op jit(solution)/shard_map/ppermute | solution.py:57
  76.2 6.9 %collective-permute-start.19 = (bf16[1,128,512]{2,1,0:T(8,128)(2,1)S(1)}, bf16[1,128,512]{2,1,0:T(8,128)(2,1)S(1)}, u32[]{:S(2)}, u32[]{:S(2)}) collective-permute-start(bf16[1,128,512]{2,1,0:T(8,128)(2,1)S(1)} %fusion.3), channel_id=1, source_target_pairs={{0,12},{4,0},{8,4},{12,8},{1,13},{5,1},{9,5},{13,9},{2,14},{6,2},{... | collective-permute-start | bytes 393224 | tf_op jit(solution)/shard_map/ppermute | solution.py:52
  79.0 10.0 %collective-permute-start.22 = (bf16[1,128,512]{2,1,0:T(8,128)(2,1)S(1)}, bf16[1,128,512]{2,1,0:T(8,128)(2,1)S(1)}, u32[]{:S(2)}, u32[]{:S(2)}) collective-permute-start(bf16[1,128,512]{2,1,0:T(8,128)(2,1)S(1)} %fusion.2), channel_id=1, source_target_pairs={{0,8},{4,12},{8,0},{12,4},{1,9},{5,13},{9,1},{13,5},{2,10},{6,14},... | collective-permute-start | bytes 393224 | tf_op jit(solution)/shard_map/ppermute | solution.py:52
  81.0 8.0 %collective-permute-start.25 = (bf16[1,128,512]{2,1,0:T(8,128)(2,1)S(1)}, bf16[1,128,512]{2,1,0:T(8,128)(2,1)S(1)}, u32[]{:S(2)}, u32[]{:S(2)}) collective-permute-start(bf16[1,128,512]{2,1,0:T(8,128)(2,1)S(1)} %fusion.1), channel_id=1, source_target_pairs={{0,4},{4,8},{8,12},{12,0},{1,5},{5,9},{9,13},{13,1},{2,6},{6,10},{... | collective-permute-start | bytes 393224 | tf_op jit(solution)/shard_map/ppermute | solution.py:52

commit v3 on v2

--- a/solution.py
+++ b/solution.py
@@ -12,9 +12,12 @@
 TOPK = 8
 CAP = 16
 SEND_CAP = 40
-META_ROWS = 8
 CORES = 2
 MOST_SHIFTS = 4
+STEP_ROWS = 384
+STREAM_SLOTS = 3
+FILLS = (3, 3)
+EXPERT_VMEM = 24 * 1024 * 1024
 
 epsilon = 1e-06
 
@@ -62,35 +65,93 @@
     return lax.ppermute(value, "mp", [(i, i ^ 1) for i in range(count)])
 
 
+def pack_kernel(hidden_ref, routes_ref, gates_ref, out_ref):
+    tok_node = hidden_ref.shape[0]
+    out_ref[0, :tok_node, :] = hidden_ref[...]
+    gate = gates_ref[...].T
+    first = gate.astype(jnp.bfloat16)
+    rest = gate - first.astype(jnp.float32)
+    second = rest.astype(jnp.bfloat16)
+    third = (rest - second.astype(jnp.float32)).astype(jnp.bfloat16)
+    route = routes_ref[...].astype(jnp.float32).T.astype(jnp.bfloat16)
+    out_ref[0, tok_node:, :] = jnp.concatenate([route, first, second, third], axis=1)
+
+
+def packed(hidden_states, routes, gates):
+    tok_node, width = hidden_states.shape
+    vmem = pl.BlockSpec(memory_space=pltpu.VMEM)
+    return pl.pallas_call(
+        pack_kernel,
+        out_shape=jax.ShapeDtypeStruct((1, tok_node + TOPK, width), jnp.bfloat16),
+        in_specs=[vmem] * 3,
+        out_specs=vmem,
+    )(hidden_states, routes, gates)
+
+
+def weight_copies(gate_up_ref, down_ref, step, rows, into, sems):
+    at = pl.multiple_of(step * rows, rows)
+    return (
+        pltpu.make_async_copy(
+            gate_up_ref.at[:, pl.ds(at, rows), :], into.at[pl.ds(0, 2)], sems.at[0]
+        ),
+        pltpu.make_async_copy(down_ref.at[pl.ds(at, rows), :], into.at[2], sems.at[1]),
+    )
+
+
+def fill_kernel(gate_up_ref, down_ref, after_ref, *refs, first):
+    held_refs, sems = refs[:-1], refs[-1]
+    copies = []
+    for i, held_ref in enumerate(held_refs):
+        copies += weight_copies(
+            gate_up_ref, down_ref, first + i, held_ref.shape[1], held_ref, sems.at[i]
+        )
+    for copy in copies:
+        copy.start()
+    for copy in copies:
+        copy.wait()
+
+
+def filled(gate_up_weight, down_weight, first, count, rows, after):
+    width = down_weight.shape[1]
+    return pl.pallas_call(
+        functools.partial(fill_kernel, first=first),
+        out_shape=[pltpu.VMEM((3, rows, width), down_weight.dtype)] * count,
+        in_specs=[
+            pl.BlockSpec(memory_space=pltpu.HBM),
+            pl.BlockSpec(memory_space=pltpu.HBM),
+            pl.BlockSpec(memory_space=pl.ANY),
+        ],
+        out_specs=[pl.BlockSpec(memory_space=pltpu.VMEM)] * count,
+        scratch_shapes=[pltpu.SemaphoreType.DMA((count, 2))],
+        compiler_params=pltpu.CompilerParams(vmem_limit_bytes=1024 * 1024),
+        cost_estimate=pl.CostEstimate(
+            flops=0, bytes_accessed=2 * count * 3 * rows * width, transcendentals=0
+        ),
+    )(gate_up_weight, down_weight, after)
+
+
 def expert_kernel(
-    place_ref, gain_ref, gate_up_ref, down_ref, *refs, held, capacity, pieces, slots, parts, chips,
+    place_ref, gain_ref, gate_up_ref, down_ref, *refs, held, capacity, slots, parts, chips, fills,
 ):
+    held_refs, refs = refs[:fills], refs[fills:]
     block_refs, out_refs = refs[: parts * chips * CORES], refs[parts * chips * CORES :]
     out_refs, scratch = out_refs[: parts * CORES], out_refs[parts * CORES :]
-    (
-        normed_ref, pick_ref, picked_ref, slot_gate_ref, served_ref, gu_buf, down_buf, gu_sem,
-        down_sem,
-    ) = scratch
-    each, block_rows, width = block_refs[0].shape
-    tok_node = block_rows - META_ROWS
+    normed_ref, pick_ref, slot_gate_ref, served_ref, buf_ref, sems = scratch
+    _, block_rows, width = block_refs[0].shape
+    tok_node = block_rows - TOPK
     tokens, model_width = normed_ref.shape
-    ff_part = down_ref.shape[0] // held
-    ff_piece = ff_part // pieces
-    steps = held * pieces
+    rows = buf_ref.shape[2]
+    steps = down_ref.shape[0] // rows
+    pieces = steps // held
+    streamed_from = fills
 
     def fetch(step, slot):
-        at = pl.multiple_of(step * ff_piece, ff_piece)
-        return (
-            pltpu.make_async_copy(
-                gate_up_ref.at[:, pl.ds(at, ff_piece), :], gu_buf.at[slot], gu_sem.at[slot]
-            ),
-            pltpu.make_async_copy(
-                down_ref.at[pl.ds(at, ff_piece), :], down_buf.at[slot], down_sem.at[slot]
-            ),
+        return weight_copies(
+            gate_up_ref, down_ref, step, rows, buf_ref.at[slot], sems.at[slot]
         )
 
-    for step in range(min(slots, steps)):
-        for copy in fetch(step, step):
+    for slot in range(min(slots, steps - streamed_from)):
+        for copy in fetch(streamed_from + slot, slot):
             copy.start()
 
     blocks = [
@@ -114,36 +175,34 @@
     expert = place_ref[0] + lax.broadcasted_iota(jnp.int32, (held, 1), 0)
     named, gate = [], []
     for z in range(parts):
-        for node in range(each):
-            total = jnp.zeros((tok_node, 1), jnp.float32)
-            for x in range(chips):
-                for c in range(CORES):
-                    wide = blocks[z][x][c][node, :tok_node, :].astype(jnp.float32)
-                    total = total + jnp.sum(wide * wide, axis=1, keepdims=True)
-            inv_scale = lax.rsqrt(total / model_width + epsilon)
-            at = pl.ds((z * each + node) * tok_node, tok_node)
-            node_named = jnp.zeros((held, tok_node), jnp.float32)
-            node_gate = jnp.zeros((held, tok_node), jnp.float32)
-            for x in range(chips):
-                for c in range(CORES):
-                    block = blocks[z][x][c]
-                    wide = block[node, :tok_node, :].astype(jnp.float32)
-                    normed_ref[at, features[x][c]] = (
-                        wide * inv_scale * gain_ref[:, features[x][c]]
-                    ).astype(jnp.bfloat16)
-                    meta = block[node, tok_node:, :].astype(jnp.float32)
-                    choices = width // (2 * tok_node)
-                    for choice in range(choices):
-                        lead = slice(choice * tok_node, (choice + 1) * tok_node)
-                        tail = slice(
-                            (choices + choice) * tok_node, (choices + choice + 1) * tok_node
-                        )
-                        match = meta[0:1, lead].astype(jnp.int32) == expert
-                        value = meta[0:1, tail] + meta[1:2, lead] + meta[1:2, tail]
-                        node_named = node_named + jnp.where(match, 1.0, 0.0)
-                        node_gate = node_gate + jnp.where(match, value, 0.0)
-            named.append(node_named)
-            gate.append(node_gate)
+        total = jnp.zeros((tok_node, 1), jnp.float32)
+        for x in range(chips):
+            for c in range(CORES):
+                wide = blocks[z][x][c][0, :tok_node, :].astype(jnp.float32)
+                total = total + jnp.sum(wide * wide, axis=1, keepdims=True)
+        inv_scale = lax.rsqrt(total / model_width + epsilon)
+        at = pl.ds(z * tok_node, tok_node)
+        for x in range(chips):
+            for c in range(CORES):
+                wide = blocks[z][x][c][0, :tok_node, :].astype(jnp.float32)
+                normed_ref[at, features[x][c]] = (
+                    wide * inv_scale * gain_ref[:, features[x][c]]
+                ).astype(jnp.bfloat16)
+        choices = blocks[z][0][0][0, tok_node:, :].astype(jnp.float32)
+        number = choices[:, :tok_node].astype(jnp.int32)
+        value = (
+            choices[:, tok_node : 2 * tok_node]
+            + choices[:, 2 * tok_node : 3 * tok_node]
+            + choices[:, 3 * tok_node :]
+        )
+        node_named = jnp.zeros((held, tok_node), jnp.float32)
+        node_gate = jnp.zeros((held, tok_node), jnp.float32)
+        for choice in range(TOPK):
+            match = number[choice : choice + 1, :] == expert
+            node_named = node_named + jnp.where(match, 1.0, 0.0)
+            node_gate = node_gate + jnp.where(match, value[choice : choice + 1, :], 0.0)
+        named.append(node_named)
+        gate.append(node_gate)
 
     named = jnp.concatenate(named, axis=1)
     gate = jnp.concatenate(gate, axis=1)
@@ -165,113 +224,110 @@
         slot_gate_ref[at, :] = jnp.sum(
             jnp.where(here, gate[h : h + 1, :], 0.0), axis=1, keepdims=True
         )
-    picked_ref[...] = jnp.dot(
-        pick_ref[...], normed_ref[...], preferred_element_type=jnp.float32
-    ).astype(jnp.bfloat16)
-
-    def one_expert(h, carry):
-        at = pl.ds(pl.multiple_of(h * capacity, capacity), capacity)
-        rows = picked_ref[at, :]
-        served = jnp.zeros((capacity, model_width), jnp.float32)
+    def one_expert(h, weights_of):
+        at = pl.ds(h * capacity, capacity)
+        if not isinstance(h, int):
+            at = pl.ds(pl.multiple_of(h * capacity, capacity), capacity)
+        picked = jnp.dot(
+            pick_ref[at, :], normed_ref[...], preferred_element_type=jnp.float32
+        ).astype(jnp.bfloat16)
+        served = None
         for piece in range(pieces):
-            step = h * pieces + piece
-            slot = lax.rem(step, slots)
-            for copy in fetch(step, slot):
-                copy.wait()
+            weights, release = weights_of(h * pieces + piece)
             along = (((1,), (1,)), ((), ()))
             gate_part = lax.dot_general(
-                rows, gu_buf[slot, 0], along, preferred_element_type=jnp.float32
+                picked, weights[0], along, preferred_element_type=jnp.float32
             )
             up_part = lax.dot_general(
-                rows, gu_buf[slot, 1], along, preferred_element_type=jnp.float32
+                picked, weights[1], along, preferred_element_type=jnp.float32
             )
             activated = (jax.nn.silu(gate_part) * up_part).astype(jnp.bfloat16)
-            served = served + jnp.dot(
-                activated, down_buf[slot], preferred_element_type=jnp.float32
-            )
-
+            term = jnp.dot(activated, weights[2], preferred_element_type=jnp.float32)
+            served = term if served is None else served + term
+            release()
+        served_ref[at, :] = (served * slot_gate_ref[at, :]).astype(jnp.bfloat16)
+
+    def streamed(step):
+        slot = lax.rem(step - streamed_from, slots)
+        for copy in fetch(step, slot):
+            copy.wait()
+
+        def release():
             @pl.when(step + slots < steps)
             def _():
                 for copy in fetch(step + slots, slot):
                     copy.start()
 
-        served_ref[at, :] = (served * slot_gate_ref[at, :]).astype(jnp.bfloat16)
+        return buf_ref.at[slot], release
+
+    def either(step):
+        return (held_refs[step], lambda: None) if step < streamed_from else streamed(step)
+
+    static = -(-streamed_from // pieces)
+    for h in range(static):
+        one_expert(h, either)
+
+    def rest(h, carry):
+        one_expert(h, streamed)
         return carry
 
-    lax.fori_loop(0, held, one_expert, 0)
+    lax.fori_loop(static, held, rest, 0)
 
     for z in range(parts):
-        for node in range(each):
-            back = pick_ref[:, pl.ds((z * each + node) * tok_node, tok_node)]
-            for x in range(chips):
-                for c in range(CORES):
-                    out_refs[z * CORES + c][x, node] = lax.dot_general(
-                        back, served_ref[:, features[x][c]], (((0,), (0,)), ((), ())),
-                        preferred_element_type=jnp.float32,
-                    ).astype(jnp.bfloat16)
-
-
-def expert_sums(place, gain, gate_up_weight, down_weight, blocks):
+        back = pick_ref[:, pl.ds(z * tok_node, tok_node)]
+        for x in range(chips):
+            for c in range(CORES):
+                out_refs[z * CORES + c][x, 0] = lax.dot_general(
+                    back, served_ref[:, features[x][c]], (((0,), (0,)), ((), ())),
+                    preferred_element_type=jnp.float32,
+                ).astype(jnp.bfloat16)
+
+
+def expert_sums(place, gain, gate_up_weight, down_weight, held_weights, rows, blocks):
     parts, chips = len(blocks), len(blocks[0])
-    each, block_rows, width = blocks[0][0][0].shape
-    tok_node = block_rows - META_ROWS
-    tokens = parts * each * tok_node
+    _, block_rows, width = blocks[0][0][0].shape
+    tok_node = block_rows - TOPK
+    tokens = parts * tok_node
     model_width = chips * CORES * width
     ff_dev = down_weight.shape[0]
     held = max(1, ff_dev // FF)
-    capacity = CAP * parts * each
-    pieces = 2 if ff_dev >= FF else 1
-    ff_piece = ff_dev // held // pieces
-    slots = min(6, held * pieces)
+    capacity = CAP * parts
+    slots = STREAM_SLOTS
     all_slots = held * capacity
     vmem = pl.BlockSpec(memory_space=pltpu.VMEM)
+    hbm = pl.BlockSpec(memory_space=pltpu.HBM)
     flat = [blocks[z][x][c] for z in range(parts) for x in range(chips) for c in range(CORES)]
+    held_weights = [pltpu.with_memory_space_constraint(w, pltpu.VMEM) for w in held_weights]
     sums = pl.pallas_call(
         functools.partial(
-            expert_kernel, held=held, capacity=capacity, pieces=pieces, slots=slots, parts=parts,
-            chips=chips,
+            expert_kernel, held=held, capacity=capacity, slots=slots, parts=parts, chips=chips,
+            fills=len(held_weights),
         ),
-        out_shape=[jax.ShapeDtypeStruct((chips, each, tok_node, width), jnp.bfloat16)]
+        out_shape=[jax.ShapeDtypeStruct((chips, 1, tok_node, width), jnp.bfloat16)]
         * (parts * CORES),
-        in_specs=[
-            pl.BlockSpec(memory_space=pltpu.SMEM),
-            vmem,
-            pl.BlockSpec(memory_space=pl.ANY),
-            pl.BlockSpec(memory_space=pl.ANY),
-        ]
-        + [vmem] * len(flat),
+        in_specs=[pl.BlockSpec(memory_space=pltpu.SMEM), vmem, hbm, hbm]
+        + [vmem] * (len(held_weights) + len(flat)),
         out_specs=[vmem] * (parts * CORES),
         scratch_shapes=[
             pltpu.VMEM((tokens, model_width), jnp.bfloat16),
             pltpu.VMEM((all_slots, tokens), jnp.bfloat16),
-            pltpu.VMEM((all_slots, model_width), jnp.bfloat16),
             pltpu.VMEM((all_slots, 1), jnp.float32),
             pltpu.VMEM((all_slots, model_width), jnp.bfloat16),
-            pltpu.VMEM((slots, 2, ff_piece, model_width), jnp.bfloat16),
-            pltpu.VMEM((slots, ff_piece, model_width), jnp.bfloat16),
-            pltpu.SemaphoreType.DMA((slots,)),
-            pltpu.SemaphoreType.DMA((slots,)),
+            pltpu.VMEM((slots, 3, rows, model_width), jnp.bfloat16),
+            pltpu.SemaphoreType.DMA((slots, 2)),
         ],
-        compiler_params=pltpu.CompilerParams(vmem_limit_bytes=46 * 1024 * 1024),
+        compiler_params=pltpu.CompilerParams(vmem_limit_bytes=EXPERT_VMEM),
         cost_estimate=pl.CostEstimate(
             flops=6 * all_slots * (ff_dev // held) * model_width,
             bytes_accessed=6 * ff_dev * model_width,
             transcendentals=0,
         ),
-    )(place, gain, gate_up_weight, down_weight, *flat)
+    )(place, gain, gate_up_weight, down_weight, *held_weights, *flat)
     return [sums[z * CORES : (z + 1) * CORES] for z in range(parts)]
 
 
-def packed_choices(routes, gates, column_index, column_count, width):
-    mine = TOPK // column_count
-    share_routes = lax.dynamic_slice_in_dim(routes, column_index * mine, mine, 1).T
-    share_gates = lax.dynamic_slice_in_dim(gates, column_index * mine, mine, 1).T
-    first = lax.reduce_precision(share_gates, 8, 7)
-    rest = share_gates - first
-    second = lax.reduce_precision(rest, 8, 7)
-    values = jnp.stack([share_routes.astype(jnp.float32), first, second, rest - second])
-    rows = values.astype(jnp.bfloat16).reshape(-1, width)
-    return jnp.pad(rows, ((0, META_ROWS - rows.shape[0]), (0, 0)))
+def farthest_first(node_count):
+    return sorted(range(node_count), key=lambda z: (-min(z, node_count - z), z))
 
 
 def added(*values):
@@ -360,14 +416,30 @@
     tok_node, width = hidden_states.shape
     ff_dev = down_weight.shape[0]
     seg_count = owners.shape[1]
-    block = jnp.concatenate(
-        [hidden_states, packed_choices(routes, gates, column_index, column_count, width)], axis=0
-    )[None]
-    parts = [block] + [shift_dp(block, s) for s in range(1, node_count)]
-    blocks = []
-    for part in parts:
-        row = [part] + [shift_x(part, s) for s in range(1, chips)]
-        blocks.append([[value, other_core(value)] for value in row])
+    rows = STEP_ROWS
+    gate_up_weight = pltpu.with_memory_space_constraint(gate_up_weight, pltpu.HBM)
+    down_weight = pltpu.with_memory_space_constraint(down_weight, pltpu.HBM)
+    block = packed(hidden_states, routes, gates)
+
+    far = farthest_first(node_count)[:-1]
+    own_x = [shift_x(block, s) for s in range(1, chips)]
+    by_z = {z: shift_dp(block, z) for z in far}
+    fill_a = filled(gate_up_weight, down_weight, 0, FILLS[0], rows, block)
+    own_x, by_z, fill_a, kv_sent = lax.optimization_barrier((own_x, by_z, fill_a, kv_rows))
+
+    by_z[0] = block
+    chip_rows = {z: [by_z[z]] for z in by_z}
+    chip_rows[0] += own_x
+    for z in far:
+        chip_rows[z] += [shift_x(by_z[z], s) for s in range(1, chips)]
+    core_rows = {z: [other_core(by_z[z])] for z in by_z}
+    core_rows[0] += [other_core(value) for value in own_x]
+    kv_parts = [kv_sent] + [shift_dp(kv_sent, s) for s in range(1, node_count)]
+    fill_b = filled(gate_up_weight, down_weight, FILLS[0], FILLS[1], rows, by_z[far[-1]])
+    chip_rows, fill_b = lax.optimization_barrier((chip_rows, fill_b))
+    for z in far:
+        core_rows[z] += [other_core(value) for value in chip_rows[z][1:]]
+    blocks = [list(zip(chip_rows[z], core_rows[z])) for z in range(node_count)]
 
     place = jnp.stack(
         [
@@ -376,14 +448,15 @@
             column_index % CORES,
         ]
     )
-    sums = expert_sums(place, norm_gain[None, :], gate_up_weight, down_weight, blocks)
-
-    shares = []
-    for keep, send in sums:
+    sums = expert_sums(
+        place, norm_gain[None, :], gate_up_weight, down_weight, fill_a + fill_b, rows, blocks
+    )
+
+    shares = [None] * node_count
+    for z in farthest_first(node_count):
+        keep, send = sums[z]
         chip_sum = added(keep, other_core(send))
-        shares.append(
-            added(chip_sum[0], *[shift_x(chip_sum[s], -s) for s in range(1, chips)])
-        )
+        shares[z] = added(chip_sum[0], *[shift_x(chip_sum[s], -s) for s in range(1, chips)])
     moe_share = sum(
         (shares[s] if s == 0 else shift_dp(shares[s], -s)).astype(jnp.float32)
         for s in range(node_count)
@@ -395,9 +468,7 @@
     page_slot = jnp.arange(SEND_CAP, dtype=jnp.int32)
     source = jnp.arange(node_count, dtype=jnp.int32)
     source_of = sources_for(owners, node_index, seg_count)
-    all_rows = jnp.concatenate(
-        [kv_rows] + [shift_dp(kv_rows, s) for s in range(1, node_count)], axis=0
-    )
+    all_rows = jnp.concatenate(kv_parts, axis=0)
     source = (node_index - source) % node_count
     owner_match = owners == node_index
     seg_len = jnp.sum(jnp.where(owner_match, lengths, 0), axis=1)

time: 90.1 us -> 123 us (1.37)
  local copies, waits for them, and re-layouts: 3.84 us -> 33.1 us
  Pallas kernels: 28.4 us -> 41 us
  waiting for transfers between devices: 22 us -> 16.4 us
  starting transfers between devices: 28.3 us -> 25.1 us
    unnamed x8 -> x40, local copies, waits for them, and re-layouts: 1.57 us -> 30.8 us
    pallas_call x0 -> x3, Pallas kernels: none -> 12 us  [the longest x2 10.3 us: filled(): pl.pallas_call(functools.partial(fill_kernel, first=first), out_shape=[pl...]
    ppermute x8, waiting for transfers between devices: 13.2 us -> 8.85 us  [shift_x(): lax.ppermute(value, 'mp', [(i, (i + CORES * shift) % count) for i in rang...]
    ppermute x9, starting transfers between devices: 16.7 us -> 12.5 us  [shift_dp(): lax.ppermute(value, 'dp', [(i, (i + shift) % count) for i in range(count)])]
    convert_element_type x7, other arithmetic: 0.37 us -> 2.26 us  [added(): sum((value.astype(jnp.float32) for value in values)).astype(jnp.bfloat16)]
    another operation x4 -> x1, other arithmetic: 1.62 us -> 0.18 us  [the longest x3 1.44 us: packed_choices(): jnp.stack([share_routes.astype(jnp.float32), first, second, rest - second])]
  transfers between devices with their start and end apart: 29 -> 29, of which waited for: 8 -> 8; matrix products, arithmetic and copies ran while one was open for 7% -> 6% of each run, Pallas kernels for 32% -> 32%
where the time goes in v3:
time: 123 us; the launch traced here: 122 us
  Pallas kernels  41 us (33%)
  local copies, waits for them, and re-layouts  33.1 us (27%)
  starting transfers between devices  25.1 us (20%)
  waiting for transfers between devices  16.4 us (13%)
  other arithmetic  5.88 us (5%)
    unnamed x40, local copies, waits for them, and re-layouts  30.8 us
    pallas_call x1, Pallas kernels, expert_sums(): pl.pallas_call(functools.partial(expert_kernel, held=held, capacity=capac...  29.1 us
    ppermute x9, starting transfers between devices, shift_dp(): lax.ppermute(value, 'dp', [(i, (i + shift) % count) for i in range(count)])  12.5 us
    pallas_call x2, Pallas kernels, filled(): pl.pallas_call(functools.partial(fill_kernel, first=first), out_shape=[pl...  10.3 us
    ppermute x8, starting transfers between devices, shift_x(): lax.ppermute(value, 'mp', [(i, (i + CORES * shift) % count) for i in rang...  9.88 us
    ppermute x8, waiting for transfers between devices, shift_x(): lax.ppermute(value, 'mp', [(i, (i + CORES * shift) % count) for i in rang...  8.85 us
    ppermute x9, waiting for transfers between devices, shift_dp(): lax.ppermute(value, 'dp', [(i, (i + shift) % count) for i in range(count)])  7.44 us
    ppermute x12, starting transfers between devices, other_core(): return lax.ppermute(value, 'mp', [(i, i ^ 1) for i in range(count)])  2.77 us
  transfers between devices with their start and end apart: 29, of which 8 were waited for; matrix products, arithmetic and copies ran while one was open for 6% of the time, Pallas kernels for 32%

profile of v3, /device:TPU:0, one launch (start us, length us, event | category | flops | bytes accessed | tf_op | source)
XLA Modules:
  0.0 122.4 jit_solution(10629271218730362964)
XLA Ops:
  0.6 1.4 %copy.11.routes_ref = s32[128,8]{1,0:T(8,128)} copy(s32[128,8]{0,1:T(8,128)} %param.13) | data formatting | bytes 8192 | tf_op args[4]
  2.0 1.4 %copy.12.gates_ref = f32[128,8]{1,0:T(8,128)} copy(f32[128,8]{0,1:T(8,128)} %param.14) | data formatting | bytes 8192 | tf_op args[5]
  3.5 1.7 %shard_map.104.after_ref.refs_6_ = bf16[1,136,512]{2,1,0:T(8,128)(2,1)} custom-call(bf16[128,512]{1,0:T(8,128)(2,1)} %hidden_ref.1, s32[128,8]{1,0:T(8,128)} %copy.11.routes_ref, f32[128,8]{1,0:T(8,128)} %copy.12.gates_ref), custom_call_target="tpu_custom_call" | custom-call | tf_op jit(solution)/shard_map/pallas_call | solution.py:83
  5.1 2.9 %collective-permute-start = (bf16[1,136,512]{2,1,0:T(8,128)(2,1)}, bf16[1,136,512]{2,1,0:T(8,128)(2,1)S(1)}, u32[]{:S(2)}, u32[]{:S(2)}) collective-permute-start(bf16[1,136,512]{2,1,0:T(8,128)(2,1)} %shard_map.104.after_ref.refs_6_), channel_id=1, source_target_pairs={{0,2},{1,3},{2,0},{3,1},{4,6},{5,7},{6,4},{7,5},{8,10},{9,11},{10,... | collective-permute-start | bytes 417800 | tf_op jit(solution)/shard_map/ppermute | solution.py:60
  8.1 1.6 %collective-permute-start.1 = (bf16[1,136,512]{2,1,0:T(8,128)(2,1)}, bf16[1,136,512]{2,1,0:T(8,128)(2,1)S(1)}, u32[]{:S(2)}, u32[]{:S(2)}) collective-permute-start(bf16[1,136,512]{2,1,0:T(8,128)(2,1)} %shard_map.104.after_ref.refs_6_), channel_id=1, source_target_pairs={{0,4},{4,8},{8,12},{12,0},{1,5},{5,9},{9,13},{13,1},{2,6},{6,10},{... | collective-permute-start | bytes 417800 | tf_op jit(solution)/shard_map/ppermute | solution.py:55
  9.7 2.6 %collective-permute-start.2 = (bf16[1,136,512]{2,1,0:T(8,128)(2,1)}, bf16[1,136,512]{2,1,0:T(8,128)(2,1)S(1)}, u32[]{:S(2)}, u32[]{:S(2)}) collective-permute-start(bf16[1,136,512]{2,1,0:T(8,128)(2,1)} %shard_map.104.after_ref.refs_6_), channel_id=1, source_target_pairs={{0,8},{4,12},{8,0},{12,4},{1,9},{5,13},{9,1},{13,5},{2,10},{6,14},... | collective-permute-start | bytes 417800 | tf_op jit(solution)/shard_map/ppermute | solution.py:55
  17.2 5.1 %shard_map.105 = (bf16[3,384,2048]{2,1,0:T(8,128)(2,1)S(1)}, bf16[3,384,2048]{2,1,0:T(8,128)(2,1)S(1)}, bf16[3,384,2048]{2,1,0:T(8,128)(2,1)S(1)}) custom-call(bf16[2,6144,2048]{2,1,0:T(8,128)(2,1)} %gate_up_ref.5, bf16[6144,2048]{1,0:T(8,128)(2,1)} %down_ref.5, bf16[1,136,512]{2,1,0:T(8,128)(2,1)S(1)} %copy-done.12), custom_call_target="tpu_custom_call" | custom-call | bytes 14155776 | tf_op jit(solution)/shard_map/pallas_call | solution.py:116
  22.3 2.1 %copy-done = bf16[3,384,2048]{2,1,0:T(8,128)(2,1)} copy-done((bf16[3,384,2048]{2,1,0:T(8,128)(2,1)}, bf16[3,384,2048]{2,1,0:T(8,128)(2,1)S(1)}, u32[]{:S(2)}) %copy-start) | copy-done | bytes 4718616
  24.5 2.2 %copy-done.2 = bf16[3,384,2048]{2,1,0:T(8,128)(2,1)} copy-done((bf16[3,384,2048]{2,1,0:T(8,128)(2,1)}, bf16[3,384,2048]{2,1,0:T(8,128)(2,1)S(1)}, u32[]{:S(2)}) %copy-start.2) | copy-done | bytes 4718616
  26.7 2.2 %copy-done.4 = bf16[3,384,2048]{2,1,0:T(8,128)(2,1)} copy-done((bf16[3,384,2048]{2,1,0:T(8,128)(2,1)}, bf16[3,384,2048]{2,1,0:T(8,128)(2,1)S(1)}, u32[]{:S(2)}) %copy-start.4) | copy-done | bytes 4718616
  30.4 1.5 %collective-permute-start.5 = (bf16[1,136,512]{2,1,0:T(8,128)(2,1)S(1)}, bf16[1,136,512]{2,1,0:T(8,128)(2,1)S(1)}, u32[]{:S(2)}, u32[]{:S(2)}) collective-permute-start(bf16[1,136,512]{2,1,0:T(8,128)(2,1)S(1)} %collective-permute-done.2.refs_14_), channel_id=1, source_target_pairs={{0,2},{1,3},{2,0},{3,1},{4,6},{5,7},{6,4},{7,5},{8,10},{9,11},{10,... | collective-permute-start | bytes 417800 | tf_op jit(solution)/shard_map/ppermute | solution.py:60
  32.5 3.0 %collective-permute-done.4.refs_12_ = bf16[1,136,512]{2,1,0:T(8,128)(2,1)S(1)} collective-permute-done((bf16[1,136,512]{2,1,0:T(8,128)(2,1)S(1)}, bf16[1,136,512]{2,1,0:T(8,128)(2,1)S(1)}, u32[]{:S(2)}, u32[]{:S(2)}) %collective-permute-start.4) | collective-permute-done | bytes 139296 | tf_op jit(solution)/shard_map/ppermute | solution.py:60
  35.6 5.2 %shard_map.106 = (bf16[3,384,2048]{2,1,0:T(8,128)(2,1)S(1)}, bf16[3,384,2048]{2,1,0:T(8,128)(2,1)S(1)}, bf16[3,384,2048]{2,1,0:T(8,128)(2,1)S(1)}) custom-call(bf16[2,6144,2048]{2,1,0:T(8,128)(2,1)} %gate_up_ref.5, bf16[6144,2048]{1,0:T(8,128)(2,1)} %down_ref.5, bf16[1,136,512]{2,1,0:T(8,128)(2,1)S(1)} %collective-permute-done.3.after_ref.refs_18_), custom_call_target="tpu_custom_call" | custom-call | bytes 14155776 | tf_op jit(solution)/shard_map/pallas_call | solution.py:116
  40.7 2.1 %copy-done.6 = bf16[3,384,2048]{2,1,0:T(8,128)(2,1)} copy-done((bf16[3,384,2048]{2,1,0:T(8,128)(2,1)}, bf16[3,384,2048]{2,1,0:T(8,128)(2,1)S(1)}, u32[]{:S(2)}) %copy-start.6) | copy-done | bytes 4718616
  42.9 2.2 %copy-done.8 = bf16[3,384,2048]{2,1,0:T(8,128)(2,1)} copy-done((bf16[3,384,2048]{2,1,0:T(8,128)(2,1)}, bf16[3,384,2048]{2,1,0:T(8,128)(2,1)S(1)}, u32[]{:S(2)}) %copy-start.8) | copy-done | bytes 4718616
  45.0 2.2 %copy-done.10 = bf16[3,384,2048]{2,1,0:T(8,128)(2,1)} copy-done((bf16[3,384,2048]{2,1,0:T(8,128)(2,1)}, bf16[3,384,2048]{2,1,0:T(8,128)(2,1)S(1)}, u32[]{:S(2)}) %copy-start.10) | copy-done | bytes 4718616
  49.8 2.3 %copy-done.1 = bf16[3,384,2048]{2,1,0:T(8,128)(2,1)S(1)} copy-done((bf16[3,384,2048]{2,1,0:T(8,128)(2,1)S(1)}, bf16[3,384,2048]{2,1,0:T(8,128)(2,1)}, u32[]{:S(2)}) %copy-start.1) | copy-done | bytes 4718616
  52.1 2.3 %copy-done.3 = bf16[3,384,2048]{2,1,0:T(8,128)(2,1)S(1)} copy-done((bf16[3,384,2048]{2,1,0:T(8,128)(2,1)S(1)}, bf16[3,384,2048]{2,1,0:T(8,128)(2,1)}, u32[]{:S(2)}) %copy-start.3) | copy-done | bytes 4718616
  54.5 2.3 %copy-done.5 = bf16[3,384,2048]{2,1,0:T(8,128)(2,1)S(1)} copy-done((bf16[3,384,2048]{2,1,0:T(8,128)(2,1)S(1)}, bf16[3,384,2048]{2,1,0:T(8,128)(2,1)}, u32[]{:S(2)}) %copy-start.5) | copy-done | bytes 4718616
  56.8 2.3 %copy-done.7 = bf16[3,384,2048]{2,1,0:T(8,128)(2,1)S(1)} copy-done((bf16[3,384,2048]{2,1,0:T(8,128)(2,1)S(1)}, bf16[3,384,2048]{2,1,0:T(8,128)(2,1)}, u32[]{:S(2)}) %copy-start.7) | copy-done | bytes 4718616
  59.2 2.3 %copy-done.9 = bf16[3,384,2048]{2,1,0:T(8,128)(2,1)S(1)} copy-done((bf16[3,384,2048]{2,1,0:T(8,128)(2,1)S(1)}, bf16[3,384,2048]{2,1,0:T(8,128)(2,1)}, u32[]{:S(2)}) %copy-start.9) | copy-done | bytes 4718616
  61.5 2.3 %copy-done.11 = bf16[3,384,2048]{2,1,0:T(8,128)(2,1)S(1)} copy-done((bf16[3,384,2048]{2,1,0:T(8,128)(2,1)S(1)}, bf16[3,384,2048]{2,1,0:T(8,128)(2,1)}, u32[]{:S(2)}) %copy-start.11) | copy-done | bytes 4718616
  63.8 29.1 %shard_map.107 = (bf16[2,1,128,512]{3,2,1,0:T(8,128)(2,1)S(1)}, bf16[2,1,128,512]{3,2,1,0:T(8,128)(2,1)S(1)}, bf16[2,1,128,512]{3,2,1,0:T(8,128)(2,1)S(1)}, bf16...) custom-call(s32[3]{0:T(128)S(1)} %pad_add_fusion.place_ref, ...), custom_call_target="tpu_custom_call" | custom-call | flops 4831838208 | bytes 75497472 | tf_op jit(solution)/shard_map/pallas_call | solution.py:301
  93.6 2.7 %collective-permute-start.28 = (bf16[128,256]{1,0:T(8,128)(2,1)S(1)}, bf16[128,256]{1,0:T(8,128)(2,1)S(1)}, u32[]{:S(2)}, u32[]{:S(2)}) collective-permute-start(bf16[128,256]{1,0:T(8,128)(2,1)S(1)} %copy-done.16), channel_id=1, source_target_pairs={{0,12},{4,0},{8,4},{12,8},{1,13},{5,1},{9,5},{13,9},{2,14},{6,2},{... | collective-permute-start | bytes 196616 | tf_op jit(solution)/shard_map/ppermute | solution.py:55
  96.3 3.9 %collective-permute-done.27 = bf16[128,256]{1,0:T(8,128)(2,1)S(1)} collective-permute-done((bf16[128,256]{1,0:T(8,128)(2,1)S(1)}, bf16[128,256]{1,0:T(8,128)(2,1)S(1)}, u32[]{:S(2)}, u32[]{:S(2)}) %collective-permute-start.27) | collective-permute-done | bytes 65568 | tf_op jit(solution)/shard_map/ppermute | solution.py:55
  103.5 1.6 %collective-permute-start.21 = (bf16[1,128,512]{2,1,0:T(8,128)(2,1)S(1)}, bf16[1,128,512]{2,1,0:T(8,128)(2,1)S(1)}, u32[]{:S(2)}, u32[]{:S(2)}) collective-permute-start(bf16[1,128,512]{2,1,0:T(8,128)(2,1)S(1)} %slice_bitcast_fusion.2), channel_id=1, source_target_pairs={{0,2},{1,3},{2,0},{3,1},{4,6},{5,7},{6,4},{7,5},{8,10},{9,11},{10,... | collective-permute-start | bytes 393224 | tf_op jit(solution)/shard_map/ppermute | solution.py:60
  105.9 1.6 %collective-permute-start.16 = (bf16[1,128,512]{2,1,0:T(8,128)(2,1)S(1)}, bf16[1,128,512]{2,1,0:T(8,128)(2,1)S(1)}, u32[]{:S(2)}, u32[]{:S(2)}) collective-permute-start(bf16[1,128,512]{2,1,0:T(8,128)(2,1)S(1)} %slice_bitcast_fusion.6), channel_id=1, source_target_pairs={{0,2},{1,3},{2,0},{3,1},{4,6},{5,7},{6,4},{7,5},{8,10},{9,11},{10,... | collective-permute-start | bytes 393224 | tf_op jit(solution)/shard_map/ppermute | solution.py:60
  108.4 2.7 %collective-permute-done.21 = bf16[1,128,512]{2,1,0:T(8,128)(2,1)S(1)} collective-permute-done((bf16[1,128,512]{2,1,0:T(8,128)(2,1)S(1)}, bf16[1,128,512]{2,1,0:T(8,128)(2,1)S(1)}, u32[]{:S(2)}, u32[]{:S(2)}) %collective-permute-start.21) | collective-permute-done | bytes 131104 | tf_op jit(solution)/shard_map/ppermute | solution.py:60
  111.6 2.3 %collective-permute-done.18 = bf16[1,128,512]{2,1,0:T(8,128)(2,1)S(1)} collective-permute-done((bf16[1,128,512]{2,1,0:T(8,128)(2,1)S(1)}, bf16[1,128,512]{2,1,0:T(8,128)(2,1)S(1)}, u32[]{:S(2)}, u32[]{:S(2)}) %collective-permute-start.18) | collective-permute-done | bytes 131104 | tf_op jit(solution)/shard_map/ppermute | solution.py:60
  113.9 2.6 %collective-permute-start.19 = (bf16[1,128,512]{2,1,0:T(8,128)(2,1)S(1)}, bf16[1,128,512]{2,1,0:T(8,128)(2,1)S(1)}, u32[]{:S(2)}, u32[]{:S(2)}) collective-permute-start(bf16[1,128,512]{2,1,0:T(8,128)(2,1)S(1)} %fusion.2), channel_id=1, source_target_pairs={{0,12},{4,0},{8,4},{12,8},{1,13},{5,1},{9,5},{13,9},{2,14},{6,2},{... | collective-permute-start | bytes 393224 | tf_op jit(solution)/shard_map/ppermute | solution.py:55
  116.6 1.6 %gather_fusion.1 = bf16[160,256]{1,0:T(8,128)(2,1)} fusion(bf16[513,256]{1,0:T(8,128)(2,1)S(1)} %constant_dynamic-update-slice_fusion, s32[1024]{0:T(1024)S(1)} %pad_clamp_fusion), kind=kCustom, calls=%fused_computation.1 | custom fusion | bytes 164480 | tf_op jit(solution)/shard_map/gather | solution.py:482
  118.2 2.7 %collective-permute-done.22 = bf16[1,128,512]{2,1,0:T(8,128)(2,1)S(1)} collective-permute-done((bf16[1,128,512]{2,1,0:T(8,128)(2,1)S(1)}, bf16[1,128,512]{2,1,0:T(8,128)(2,1)S(1)}, u32[]{:S(2)}, u32[]{:S(2)}) %collective-permute-start.22) | collective-permute-done | bytes 131104 | tf_op jit(solution)/shard_map/ppermute | solution.py:55
  (99 shorter events, 17.4 us)
Async XLA Ops:
  5.1 23.8 %collective-permute-start = (bf16[1,136,512]{2,1,0:T(8,128)(2,1)}, bf16[1,136,512]{2,1,0:T(8,128)(2,1)S(1)}, u32[]{:S(2)}, u32[]{:S(2)}) collective-permute-start(bf16[1,136,512]{2,1,0:T(8,128)(2,1)} %shard_map.104.after_ref.refs_6_), channel_id=1, source_target_pairs={{0,2},{1,3},{2,0},{3,1},{4,6},{5,7},{6,4},{7,5},{8,10},{9,11},{10,... | collective-permute-start | bytes 417800 | tf_op jit(solution)/shard_map/ppermute | solution.py:60
  8.1 20.9 %collective-permute-start.1 = (bf16[1,136,512]{2,1,0:T(8,128)(2,1)}, bf16[1,136,512]{2,1,0:T(8,128)(2,1)S(1)}, u32[]{:S(2)}, u32[]{:S(2)}) collective-permute-start(bf16[1,136,512]{2,1,0:T(8,128)(2,1)} %shard_map.104.after_ref.refs_6_), channel_id=1, source_target_pairs={{0,4},{4,8},{8,12},{12,0},{1,5},{5,9},{9,13},{13,1},{2,6},{6,10},{... | collective-permute-start | bytes 417800 | tf_op jit(solution)/shard_map/ppermute | solution.py:55
  9.7 19.3 %collective-permute-start.2 = (bf16[1,136,512]{2,1,0:T(8,128)(2,1)}, bf16[1,136,512]{2,1,0:T(8,128)(2,1)S(1)}, u32[]{:S(2)}, u32[]{:S(2)}) collective-permute-start(bf16[1,136,512]{2,1,0:T(8,128)(2,1)} %shard_map.104.after_ref.refs_6_), channel_id=1, source_target_pairs={{0,8},{4,12},{8,0},{12,4},{1,9},{5,13},{9,1},{13,5},{2,10},{6,14},... | collective-permute-start | bytes 417800 | tf_op jit(solution)/shard_map/ppermute | solution.py:55
  12.2 16.7 %collective-permute-start.3 = (bf16[1,136,512]{2,1,0:T(8,128)(2,1)}, bf16[1,136,512]{2,1,0:T(8,128)(2,1)S(1)}, u32[]{:S(2)}, u32[]{:S(2)}) collective-permute-start(bf16[1,136,512]{2,1,0:T(8,128)(2,1)} %shard_map.104.after_ref.refs_6_), channel_id=1, source_target_pairs={{0,12},{4,0},{8,4},{12,8},{1,13},{5,1},{9,5},{13,9},{2,14},{6,2},{... | collective-permute-start | bytes 417800 | tf_op jit(solution)/shard_map/ppermute | solution.py:55
  13.6 34.2 %collective-permute-start.7 = (bf16[1,136,512]{2,1,0:T(8,128)(2,1)}, bf16[1,136,512]{2,1,0:T(8,128)(2,1)S(1)}, u32[]{:S(2)}, u32[]{:S(2)}) collective-permute-start(bf16[1,136,512]{2,1,0:T(8,128)(2,1)} %shard_map.104.after_ref.refs_6_), channel_id=1, source_target_pairs={{0,1},{1,0},{2,3},{3,2},{4,5},{5,4},{6,7},{7,6},{8,9},{9,8},{10,11... | collective-permute-start | bytes 417800 | tf_op jit(solution)/shard_map/ppermute | solution.py:65
  29.0 6.5 %collective-permute-start.4 = (bf16[1,136,512]{2,1,0:T(8,128)(2,1)S(1)}, bf16[1,136,512]{2,1,0:T(8,128)(2,1)S(1)}, u32[]{:S(2)}, u32[]{:S(2)}) collective-permute-start(bf16[1,136,512]{2,1,0:T(8,128)(2,1)S(1)} %collective-permute-done.1.refs_10_), channel_id=1, source_target_pairs={{0,2},{1,3},{2,0},{3,1},{4,6},{5,7},{6,4},{7,5},{8,10},{9,11},{10,... | collective-permute-start | bytes 417800 | tf_op jit(solution)/shard_map/ppermute | solution.py:60
  30.2 18.2 %collective-permute-start.9 = (bf16[1,136,512]{2,1,0:T(8,128)(2,1)S(1)}, bf16[1,136,512]{2,1,0:T(8,128)(2,1)S(1)}, u32[]{:S(2)}, u32[]{:S(2)}) collective-permute-start(bf16[1,136,512]{2,1,0:T(8,128)(2,1)S(1)} %collective-permute-done.1.refs_10_), channel_id=1, source_target_pairs={{0,1},{1,0},{2,3},{3,2},{4,5},{5,4},{6,7},{7,6},{8,9},{9,8},{10,11... | collective-permute-start | bytes 417800 | tf_op jit(solution)/shard_map/ppermute | solution.py:65
  30.4 16.8 %collective-permute-start.5 = (bf16[1,136,512]{2,1,0:T(8,128)(2,1)S(1)}, bf16[1,136,512]{2,1,0:T(8,128)(2,1)S(1)}, u32[]{:S(2)}, u32[]{:S(2)}) collective-permute-start(bf16[1,136,512]{2,1,0:T(8,128)(2,1)S(1)} %collective-permute-done.2.refs_14_), channel_id=1, source_target_pairs={{0,2},{1,3},{2,0},{3,1},{4,6},{5,7},{6,4},{7,5},{8,10},{9,11},{10,... | collective-permute-start | bytes 417800 | tf_op jit(solution)/shard_map/ppermute | solution.py:60
  31.9 15.8 %collective-permute-start.6 = (bf16[1,136,512]{2,1,0:T(8,128)(2,1)S(1)}, bf16[1,136,512]{2,1,0:T(8,128)(2,1)S(1)}, u32[]{:S(2)}, u32[]{:S(2)}) collective-permute-start(bf16[1,136,512]{2,1,0:T(8,128)(2,1)S(1)} %collective-permute-done.3.after_ref.refs_18_), channel_id=1, source_target_pairs={{0,2},{1,3},{2,0},{3,1},{4,6},{5,7},{6,4},{7,5},{8,10},{9,11},{10,... | collective-permute-start | bytes 417800 | tf_op jit(solution)/shard_map/ppermute | solution.py:60
  35.5 12.7 %collective-permute-start.8 = (bf16[1,136,512]{2,1,0:T(8,128)(2,1)S(1)}, bf16[1,136,512]{2,1,0:T(8,128)(2,1)S(1)}, u32[]{:S(2)}, u32[]{:S(2)}) collective-permute-start(bf16[1,136,512]{2,1,0:T(8,128)(2,1)S(1)} %collective-permute-done.refs_8_), channel_id=1, source_target_pairs={{0,1},{1,0},{2,3},{3,2},{4,5},{5,4},{6,7},{7,6},{8,9},{9,8},{10,11... | collective-permute-start | bytes 417800 | tf_op jit(solution)/shard_map/ppermute | solution.py:65
  35.5 14.3 %copy-start.13 = (bf16[1,136,512]{2,1,0:T(8,128)(2,1)S(1)}, bf16[1,136,512]{2,1,0:T(8,128)(2,1)}, u32[]{:S(2)}) copy-start(bf16[1,136,512]{2,1,0:T(8,128)(2,1)} %shard_map.104.after_ref.refs_6_) | copy-start | bytes 417796
  35.5 14.3 %copy-start.14 = (f32[2048]{0:T(1024)S(1)}, f32[2048]{0:T(1024)}, u32[]{:S(2)}) copy-start(f32[2048]{0:T(1024)} %param.10) | copy-start | bytes 24580
  47.2 1.7 %collective-permute-start.11 = (bf16[1,136,512]{2,1,0:T(8,128)(2,1)S(1)}, bf16[1,136,512]{2,1,0:T(8,128)(2,1)S(1)}, u32[]{:S(2)}, u32[]{:S(2)}) collective-permute-start(bf16[1,136,512]{2,1,0:T(8,128)(2,1)S(1)} %collective-permute-done.2.refs_14_), channel_id=1, source_target_pairs={{0,1},{1,0},{2,3},{3,2},{4,5},{5,4},{6,7},{7,6},{8,9},{9,8},{10,11... | collective-permute-start | bytes 417800 | tf_op jit(solution)/shard_map/ppermute | solution.py:65
  47.7 2.0 %collective-permute-start.13 = (bf16[1,136,512]{2,1,0:T(8,128)(2,1)S(1)}, bf16[1,136,512]{2,1,0:T(8,128)(2,1)S(1)}, u32[]{:S(2)}, u32[]{:S(2)}) collective-permute-start(bf16[1,136,512]{2,1,0:T(8,128)(2,1)S(1)} %collective-permute-done.3.after_ref.refs_18_), channel_id=1, source_target_pairs={{0,1},{1,0},{2,3},{3,2},{4,5},{5,4},{6,7},{7,6},{8,9},{9,8},{10,11... | collective-permute-start | bytes 417800 | tf_op jit(solution)/shard_map/ppermute | solution.py:65
  47.8 1.9 %collective-permute-start.10 = (bf16[1,136,512]{2,1,0:T(8,128)(2,1)S(1)}, bf16[1,136,512]{2,1,0:T(8,128)(2,1)S(1)}, u32[]{:S(2)}, u32[]{:S(2)}) collective-permute-start(bf16[1,136,512]{2,1,0:T(8,128)(2,1)S(1)} %collective-permute-done.4.refs_12_), channel_id=1, source_target_pairs={{0,1},{1,0},{2,3},{3,2},{4,5},{5,4},{6,7},{7,6},{8,9},{9,8},{10,11... | collective-permute-start | bytes 417800 | tf_op jit(solution)/shard_map/ppermute | solution.py:65
  48.2 1.4 %collective-permute-start.12 = (bf16[1,136,512]{2,1,0:T(8,128)(2,1)S(1)}, bf16[1,136,512]{2,1,0:T(8,128)(2,1)S(1)}, u32[]{:S(2)}, u32[]{:S(2)}) collective-permute-start(bf16[1,136,512]{2,1,0:T(8,128)(2,1)S(1)} %collective-permute-done.5.refs_16_), channel_id=1, source_target_pairs={{0,1},{1,0},{2,3},{3,2},{4,5},{5,4},{6,7},{7,6},{8,9},{9,8},{10,11... | collective-permute-start | bytes 417800 | tf_op jit(solution)/shard_map/ppermute | solution.py:65
  48.3 1.5 %collective-permute-start.14 = (bf16[1,136,512]{2,1,0:T(8,128)(2,1)S(1)}, bf16[1,136,512]{2,1,0:T(8,128)(2,1)S(1)}, u32[]{:S(2)}, u32[]{:S(2)}) collective-permute-start(bf16[1,136,512]{2,1,0:T(8,128)(2,1)S(1)} %collective-permute-done.6.refs_20_), channel_id=1, source_target_pairs={{0,1},{1,0},{2,3},{3,2},{4,5},{5,4},{6,7},{7,6},{8,9},{9,8},{10,11... | collective-permute-start | bytes 417800 | tf_op jit(solution)/shard_map/ppermute | solution.py:65
  48.9 47.4 %collective-permute-start.26 = (bf16[128,256]{1,0:T(8,128)(2,1)S(1)}, bf16[128,256]{1,0:T(8,128)(2,1)S(1)}, u32[]{:S(2)}, u32[]{:S(2)}) collective-permute-start(bf16[128,256]{1,0:T(8,128)(2,1)S(1)} %copy-done.16), channel_id=1, source_target_pairs={{0,4},{4,8},{8,12},{12,0},{1,5},{5,9},{9,13},{13,1},{2,6},{6,10},{... | collective-permute-start | bytes 196616 | tf_op jit(solution)/shard_map/ppermute | solution.py:55
  92.9 28.8 %copy-start.15 = (bf16[128,512]{1,0:T(8,128)(2,1)S(1)}, bf16[128,512]{1,0:T(8,128)(2,1)}, u32[]{:S(2)}) copy-start(bf16[128,512]{1,0:T(8,128)(2,1)} %hidden_ref.1) | copy-start | bytes 393220
  92.9 8.0 %collective-permute-start.23 = (bf16[2,1,128,512]{3,2,1,0:T(8,128)(2,1)}, bf16[2,1,128,512]{3,2,1,0:T(8,128)(2,1)S(1)}, u32[]{:S(2)}, u32[]{:S(2)}) collective-permute-start(bf16[2,1,128,512]{3,2,1,0:T(8,128)(2,1)} %get-tuple-element.66), channel_id=1, source_target_pairs={{0,1},{1,0},{2,3},{3,2},{4,5},{5,4},{6,7},{7,6},{8,9},{9,8},{10,11... | collective-permute-start | bytes 786440 | tf_op jit(solution)/shard_map/ppermute | solution.py:65
  93.3 7.0 %collective-permute-start.27 = (bf16[128,256]{1,0:T(8,128)(2,1)S(1)}, bf16[128,256]{1,0:T(8,128)(2,1)S(1)}, u32[]{:S(2)}, u32[]{:S(2)}) collective-permute-start(bf16[128,256]{1,0:T(8,128)(2,1)S(1)} %copy-done.16), channel_id=1, source_target_pairs={{0,8},{4,12},{8,0},{12,4},{1,9},{5,13},{9,1},{13,5},{2,10},{6,14},... | collective-permute-start | bytes 196616 | tf_op jit(solution)/shard_map/ppermute | solution.py:55
  93.6 22.9 %collective-permute-start.28 = (bf16[128,256]{1,0:T(8,128)(2,1)S(1)}, bf16[128,256]{1,0:T(8,128)(2,1)S(1)}, u32[]{:S(2)}, u32[]{:S(2)}) collective-permute-start(bf16[128,256]{1,0:T(8,128)(2,1)S(1)} %copy-done.16), channel_id=1, source_target_pairs={{0,12},{4,0},{8,4},{12,8},{1,13},{5,1},{9,5},{13,9},{2,14},{6,2},{... | collective-permute-start | bytes 196616 | tf_op jit(solution)/shard_map/ppermute | solution.py:55
  100.3 2.2 %collective-permute-start.20 = (bf16[2,1,128,512]{3,2,1,0:T(8,128)(2,1)}, bf16[2,1,128,512]{3,2,1,0:T(8,128)(2,1)S(1)}, u32[]{:S(2)}, u32[]{:S(2)}) collective-permute-start(bf16[2,1,128,512]{3,2,1,0:T(8,128)(2,1)} %get-tuple-element.64), channel_id=1, source_target_pairs={{0,1},{1,0},{2,3},{3,2},{4,5},{5,4},{6,7},{7,6},{8,9},{9,8},{10,11... | collective-permute-start | bytes 786440 | tf_op jit(solution)/shard_map/ppermute | solution.py:65
  100.3 4.8 %collective-permute-start.17 = (bf16[2,1,128,512]{3,2,1,0:T(8,128)(2,1)}, bf16[2,1,128,512]{3,2,1,0:T(8,128)(2,1)S(1)}, u32[]{:S(2)}, u32[]{:S(2)}) collective-permute-start(bf16[2,1,128,512]{3,2,1,0:T(8,128)(2,1)} %get-tuple-element.62), channel_id=1, source_target_pairs={{0,1},{1,0},{2,3},{3,2},{4,5},{5,4},{6,7},{7,6},{8,9},{9,8},{10,11... | collective-permute-start | bytes 786440 | tf_op jit(solution)/shard_map/ppermute | solution.py:65
  100.8 5.0 %collective-permute-start.15 = (bf16[2,1,128,512]{3,2,1,0:T(8,128)(2,1)S(1)}, bf16[2,1,128,512]{3,2,1,0:T(8,128)(2,1)S(1)}, u32[]{:S(2)}, u32[]{:S(2)}) collective-permute-start(bf16[2,1,128,512]{3,2,1,0:T(8,128)(2,1)S(1)} %get-tuple-element.60), channel_id=1, source_target_pairs={{0,1},{1,0},{2,3},{3,2},{4,5},{5,4},{6,7},{7,6},{8,9},{9,8},{10,11... | collective-permute-start | bytes 786440 | tf_op jit(solution)/shard_map/ppermute | solution.py:65
  101.9 6.4 %collective-permute-start.24 = (bf16[1,128,512]{2,1,0:T(8,128)(2,1)S(1)}, bf16[1,128,512]{2,1,0:T(8,128)(2,1)S(1)}, u32[]{:S(2)}, u32[]{:S(2)}) collective-permute-start(bf16[1,128,512]{2,1,0:T(8,128)(2,1)S(1)} %slice_bitcast_fusion), channel_id=1, source_target_pairs={{0,2},{1,3},{2,0},{3,1},{4,6},{5,7},{6,4},{7,5},{8,10},{9,11},{10,... | collective-permute-start | bytes 393224 | tf_op jit(solution)/shard_map/ppermute | solution.py:60
  103.5 7.5 %collective-permute-start.21 = (bf16[1,128,512]{2,1,0:T(8,128)(2,1)S(1)}, bf16[1,128,512]{2,1,0:T(8,128)(2,1)S(1)}, u32[]{:S(2)}, u32[]{:S(2)}) collective-permute-start(bf16[1,128,512]{2,1,0:T(8,128)(2,1)S(1)} %slice_bitcast_fusion.2), channel_id=1, source_target_pairs={{0,2},{1,3},{2,0},{3,1},{4,6},{5,7},{6,4},{7,5},{8,10},{9,11},{10,... | collective-permute-start | bytes 393224 | tf_op jit(solution)/shard_map/ppermute | solution.py:60
  105.2 8.7 %collective-permute-start.18 = (bf16[1,128,512]{2,1,0:T(8,128)(2,1)S(1)}, bf16[1,128,512]{2,1,0:T(8,128)(2,1)S(1)}, u32[]{:S(2)}, u32[]{:S(2)}) collective-permute-start(bf16[1,128,512]{2,1,0:T(8,128)(2,1)S(1)} %slice_bitcast_fusion.4), channel_id=1, source_target_pairs={{0,2},{1,3},{2,0},{3,1},{4,6},{5,7},{6,4},{7,5},{8,10},{9,11},{10,... | collective-permute-start | bytes 393224 | tf_op jit(solution)/shard_map/ppermute | solution.py:60
  105.9 12.3 %collective-permute-start.16 = (bf16[1,128,512]{2,1,0:T(8,128)(2,1)S(1)}, bf16[1,128,512]{2,1,0:T(8,128)(2,1)S(1)}, u32[]{:S(2)}, u32[]{:S(2)}) collective-permute-start(bf16[1,128,512]{2,1,0:T(8,128)(2,1)S(1)} %slice_bitcast_fusion.6), channel_id=1, source_target_pairs={{0,2},{1,3},{2,0},{3,1},{4,6},{5,7},{6,4},{7,5},{8,10},{9,11},{10,... | collective-permute-start | bytes 393224 | tf_op jit(solution)/shard_map/ppermute | solution.py:60
  108.3 9.9 %collective-permute-start.25 = (bf16[1,128,512]{2,1,0:T(8,128)(2,1)S(1)}, bf16[1,128,512]{2,1,0:T(8,128)(2,1)S(1)}, u32[]{:S(2)}, u32[]{:S(2)}) collective-permute-start(bf16[1,128,512]{2,1,0:T(8,128)(2,1)S(1)} %fusion), channel_id=1, source_target_pairs={{0,4},{4,8},{8,12},{12,0},{1,5},{5,9},{9,13},{13,1},{2,6},{6,10},{... | collective-permute-start | bytes 393224 | tf_op jit(solution)/shard_map/ppermute | solution.py:55
  111.1 9.8 %collective-permute-start.22 = (bf16[1,128,512]{2,1,0:T(8,128)(2,1)S(1)}, bf16[1,128,512]{2,1,0:T(8,128)(2,1)S(1)}, u32[]{:S(2)}, u32[]{:S(2)}) collective-permute-start(bf16[1,128,512]{2,1,0:T(8,128)(2,1)S(1)} %fusion.1), channel_id=1, source_target_pairs={{0,8},{4,12},{8,0},{12,4},{1,9},{5,13},{9,1},{13,5},{2,10},{6,14},... | collective-permute-start | bytes 393224 | tf_op jit(solution)/shard_map/ppermute | solution.py:55
  113.9 7.7 %collective-permute-start.19 = (bf16[1,128,512]{2,1,0:T(8,128)(2,1)S(1)}, bf16[1,128,512]{2,1,0:T(8,128)(2,1)S(1)}, u32[]{:S(2)}, u32[]{:S(2)}) collective-permute-start(bf16[1,128,512]{2,1,0:T(8,128)(2,1)S(1)} %fusion.2), channel_id=1, source_target_pairs={{0,12},{4,0},{8,4},{12,8},{1,13},{5,1},{9,5},{13,9},{2,14},{6,2},{... | collective-permute-start | bytes 393224 | tf_op jit(solution)/shard_map/ppermute | solution.py:55
  (14 other events, 41.4 us)

commit v4 on v3

--- a/solution.py
+++ b/solution.py
@@ -14,10 +14,8 @@
 SEND_CAP = 40
 CORES = 2
 MOST_SHIFTS = 4
-STEP_ROWS = 384
-STREAM_SLOTS = 3
-FILLS = (3, 3)
-EXPERT_VMEM = 24 * 1024 * 1024
+WEIGHT_SLOTS = 3
+EXPERT_VMEM = 44 * 1024 * 1024
 
 epsilon = 1e-06
 
@@ -68,12 +66,12 @@
 def pack_kernel(hidden_ref, routes_ref, gates_ref, out_ref):
     tok_node = hidden_ref.shape[0]
     out_ref[0, :tok_node, :] = hidden_ref[...]
-    gate = gates_ref[...].T
+    gate = gates_ref[...]
     first = gate.astype(jnp.bfloat16)
     rest = gate - first.astype(jnp.float32)
     second = rest.astype(jnp.bfloat16)
     third = (rest - second.astype(jnp.float32)).astype(jnp.bfloat16)
-    route = routes_ref[...].astype(jnp.float32).T.astype(jnp.bfloat16)
+    route = routes_ref[...].astype(jnp.float32).astype(jnp.bfloat16)
     out_ref[0, tok_node:, :] = jnp.concatenate([route, first, second, third], axis=1)
 
 
@@ -85,73 +83,30 @@
         out_shape=jax.ShapeDtypeStruct((1, tok_node + TOPK, width), jnp.bfloat16),
         in_specs=[vmem] * 3,
         out_specs=vmem,
-    )(hidden_states, routes, gates)
-
-
-def weight_copies(gate_up_ref, down_ref, step, rows, into, sems):
-    at = pl.multiple_of(step * rows, rows)
-    return (
-        pltpu.make_async_copy(
-            gate_up_ref.at[:, pl.ds(at, rows), :], into.at[pl.ds(0, 2)], sems.at[0]
-        ),
-        pltpu.make_async_copy(down_ref.at[pl.ds(at, rows), :], into.at[2], sems.at[1]),
-    )
-
-
-def fill_kernel(gate_up_ref, down_ref, after_ref, *refs, first):
-    held_refs, sems = refs[:-1], refs[-1]
-    copies = []
-    for i, held_ref in enumerate(held_refs):
-        copies += weight_copies(
-            gate_up_ref, down_ref, first + i, held_ref.shape[1], held_ref, sems.at[i]
-        )
-    for copy in copies:
-        copy.start()
-    for copy in copies:
-        copy.wait()
-
-
-def filled(gate_up_weight, down_weight, first, count, rows, after):
-    width = down_weight.shape[1]
-    return pl.pallas_call(
-        functools.partial(fill_kernel, first=first),
-        out_shape=[pltpu.VMEM((3, rows, width), down_weight.dtype)] * count,
-        in_specs=[
-            pl.BlockSpec(memory_space=pltpu.HBM),
-            pl.BlockSpec(memory_space=pltpu.HBM),
-            pl.BlockSpec(memory_space=pl.ANY),
-        ],
-        out_specs=[pl.BlockSpec(memory_space=pltpu.VMEM)] * count,
-        scratch_shapes=[pltpu.SemaphoreType.DMA((count, 2))],
-        compiler_params=pltpu.CompilerParams(vmem_limit_bytes=1024 * 1024),
-        cost_estimate=pl.CostEstimate(
-            flops=0, bytes_accessed=2 * count * 3 * rows * width, transcendentals=0
-        ),
-    )(gate_up_weight, down_weight, after)
+    )(hidden_states, routes.T, gates.T)
 
 
 def expert_kernel(
-    place_ref, gain_ref, gate_up_ref, down_ref, *refs, held, capacity, slots, parts, chips, fills,
+    place_ref, gain_ref, gate_up_ref, down_ref, *refs, held, capacity, parts, chips,
 ):
-    held_refs, refs = refs[:fills], refs[fills:]
     block_refs, out_refs = refs[: parts * chips * CORES], refs[parts * chips * CORES :]
     out_refs, scratch = out_refs[: parts * CORES], out_refs[parts * CORES :]
-    normed_ref, pick_ref, slot_gate_ref, served_ref, buf_ref, sems = scratch
+    normed_ref, pick_ref, picked_ref, slot_gate_ref, served_ref, gu_buf, down_buf, sems = scratch
     _, block_rows, width = block_refs[0].shape
     tok_node = block_rows - TOPK
     tokens, model_width = normed_ref.shape
-    rows = buf_ref.shape[2]
-    steps = down_ref.shape[0] // rows
-    pieces = steps // held
-    streamed_from = fills
-
-    def fetch(step, slot):
-        return weight_copies(
-            gate_up_ref, down_ref, step, rows, buf_ref.at[slot], sems.at[slot]
+    slots, ff_part, _ = down_buf.shape
+
+    def fetch(h, slot):
+        at = pl.ds(pl.multiple_of(h * ff_part, ff_part), ff_part)
+        return (
+            pltpu.make_async_copy(gate_up_ref.at[0, at, :], gu_buf.at[slot, 0], sems.at[slot, 0]),
+            pltpu.make_async_copy(gate_up_ref.at[1, at, :], gu_buf.at[slot, 1], sems.at[slot, 1]),
+            pltpu.make_async_copy(down_ref.at[at, :], down_buf.at[slot], sems.at[slot, 2]),
         )
 
-    for slot in range(min(slots, steps - streamed_from)):
-        for copy in fetch(streamed_from + slot, slot):
+    for h in range(min(slots, held)):
+        for copy in fetch(h, h):
             copy.start()
 
     blocks = [
@@ -224,66 +179,49 @@
         slot_gate_ref[at, :] = jnp.sum(
             jnp.where(here, gate[h : h + 1, :], 0.0), axis=1, keepdims=True
         )
-    def one_expert(h, weights_of):
-        at = pl.ds(h * capacity, capacity)
-        if not isinstance(h, int):
-            at = pl.ds(pl.multiple_of(h * capacity, capacity), capacity)
-        picked = jnp.dot(
-            pick_ref[at, :], normed_ref[...], preferred_element_type=jnp.float32
+    for first in range(0, model_width, width):
+        part = slice(first, first + width)
+        picked_ref[:, part] = jnp.dot(
+            pick_ref[...], normed_ref[:, part], preferred_element_type=jnp.float32
         ).astype(jnp.bfloat16)
-        served = None
-        for piece in range(pieces):
-            weights, release = weights_of(h * pieces + piece)
-            along = (((1,), (1,)), ((), ()))
-            gate_part = lax.dot_general(
-                picked, weights[0], along, preferred_element_type=jnp.float32
-            )
-            up_part = lax.dot_general(
-                picked, weights[1], along, preferred_element_type=jnp.float32
-            )
-            activated = (jax.nn.silu(gate_part) * up_part).astype(jnp.bfloat16)
-            term = jnp.dot(activated, weights[2], preferred_element_type=jnp.float32)
-            served = term if served is None else served + term
-            release()
+
+    def one_expert(h, carry):
+        slot = lax.rem(h, slots)
+        at = pl.ds(pl.multiple_of(h * capacity, capacity), capacity)
+        for copy in fetch(h, slot):
+            copy.wait()
+        picked = picked_ref[at, :]
+        along = (((1,), (1,)), ((), ()))
+        gate_part = lax.dot_general(
+            picked, gu_buf[slot, 0], along, preferred_element_type=jnp.float32
+        )
+        up_part = lax.dot_general(
+            picked, gu_buf[slot, 1], along, preferred_element_type=jnp.float32
+        )
+        activated = (jax.nn.silu(gate_part) * up_part).astype(jnp.bfloat16)
+        served = jnp.dot(activated, down_buf[slot], preferred_element_type=jnp.float32)
         served_ref[at, :] = (served * slot_gate_ref[at, :]).astype(jnp.bfloat16)
 
-    def streamed(step):
-        slot = lax.rem(step - streamed_from, slots)
-        for copy in fetch(step, slot):
-            copy.wait()
-
-        def release():
-            @pl.when(step + slots < steps)
-            def _():
-                for copy in fetch(step + slots, slot):
-                    copy.start()
-
-        return buf_ref.at[slot], release
-
-    def either(step):
-        return (held_refs[step], lambda: None) if step < streamed_from else streamed(step)
-
-    static = -(-streamed_from // pieces)
-    for h in range(static):
-        one_expert(h, either)
-
-    def rest(h, carry):
-        one_expert(h, streamed)
+        @pl.when(h + slots < held)
+        def _():
+            for copy in fetch(h + slots, slot):
+                copy.start()
+
         return carry
 
-    lax.fori_loop(static, held, rest, 0)
-
-    for z in range(parts):
-        back = pick_ref[:, pl.ds(z * tok_node, tok_node)]
-        for x in range(chips):
-            for c in range(CORES):
-                out_refs[z * CORES + c][x, 0] = lax.dot_general(
-                    back, served_ref[:, features[x][c]], (((0,), (0,)), ((), ())),
-                    preferred_element_type=jnp.float32,
-                ).astype(jnp.bfloat16)
-
-
-def expert_sums(place, gain, gate_up_weight, down_weight, held_weights, rows, blocks):
+    lax.fori_loop(0, held, one_expert, 0)
+
+    back = pick_ref[...].T
+    for x in range(chips):
+        for c in range(CORES):
+            summed = jnp.dot(
+                back, served_ref[:, features[x][c]], preferred_element_type=jnp.float32
+            ).astype(jnp.bfloat16)
+            for z in range(parts):
+                out_refs[z * CORES + c][x, 0] = summed[z * tok_node : (z + 1) * tok_node, :]
+
+
+def expert_sums(place, gain, gate_up_weight, down_weight, blocks):
     parts, chips = len(blocks), len(blocks[0])
     _, block_rows, width = blocks[0][0][0].shape
     tok_node = block_rows - TOPK
@@ -292,29 +230,29 @@
     ff_dev = down_weight.shape[0]
     held = max(1, ff_dev // FF)
     capacity = CAP * parts
-    slots = STREAM_SLOTS
+    ff_part = ff_dev // held
     all_slots = held * capacity
     vmem = pl.BlockSpec(memory_space=pltpu.VMEM)
     hbm = pl.BlockSpec(memory_space=pltpu.HBM)
     flat = [blocks[z][x][c] for z in range(parts) for x in range(chips) for c in range(CORES)]
-    held_weights = [pltpu.with_memory_space_constraint(w, pltpu.VMEM) for w in held_weights]
     sums = pl.pallas_call(
         functools.partial(
-            expert_kernel, held=held, capacity=capacity, slots=slots, parts=parts, chips=chips,
-            fills=len(held_weights),
+            expert_kernel, held=held, capacity=capacity, parts=parts, chips=chips
         ),
         out_shape=[jax.ShapeDtypeStruct((chips, 1, tok_node, width), jnp.bfloat16)]
         * (parts * CORES),
         in_specs=[pl.BlockSpec(memory_space=pltpu.SMEM), vmem, hbm, hbm]
-        + [vmem] * (len(held_weights) + len(flat)),
+        + [vmem] * len(flat),
         out_specs=[vmem] * (parts * CORES),
         scratch_shapes=[
             pltpu.VMEM((tokens, model_width), jnp.bfloat16),
             pltpu.VMEM((all_slots, tokens), jnp.bfloat16),
+            pltpu.VMEM((all_slots, model_width), jnp.bfloat16),
             pltpu.VMEM((all_slots, 1), jnp.float32),
             pltpu.VMEM((all_slots, model_width), jnp.bfloat16),
-            pltpu.VMEM((slots, 3, rows, model_width), jnp.bfloat16),
-            pltpu.SemaphoreType.DMA((slots, 2)),
+            pltpu.VMEM((WEIGHT_SLOTS, 2, ff_part, model_width), jnp.bfloat16),
+            pltpu.VMEM((WEIGHT_SLOTS, ff_part, model_width), jnp.bfloat16),
+            pltpu.SemaphoreType.DMA((WEIGHT_SLOTS, 3)),
         ],
         compiler_params=pltpu.CompilerParams(vmem_limit_bytes=EXPERT_VMEM),
         cost_estimate=pl.CostEstimate(
@@ -322,7 +260,7 @@
             bytes_accessed=6 * ff_dev * model_width,
             transcendentals=0,
         ),
-    )(place, gain, gate_up_weight, down_weight, *held_weights, *flat)
+    )(place, gain, gate_up_weight, down_weight, *flat)
     return [sums[z * CORES : (z + 1) * CORES] for z in range(parts)]
 
 
@@ -416,30 +354,20 @@
     tok_node, width = hidden_states.shape
     ff_dev = down_weight.shape[0]
     seg_count = owners.shape[1]
-    rows = STEP_ROWS
     gate_up_weight = pltpu.with_memory_space_constraint(gate_up_weight, pltpu.HBM)
     down_weight = pltpu.with_memory_space_constraint(down_weight, pltpu.HBM)
     block = packed(hidden_states, routes, gates)
 
     far = farthest_first(node_count)[:-1]
-    own_x = [shift_x(block, s) for s in range(1, chips)]
     by_z = {z: shift_dp(block, z) for z in far}
-    fill_a = filled(gate_up_weight, down_weight, 0, FILLS[0], rows, block)
-    own_x, by_z, fill_a, kv_sent = lax.optimization_barrier((own_x, by_z, fill_a, kv_rows))
-
     by_z[0] = block
-    chip_rows = {z: [by_z[z]] for z in by_z}
-    chip_rows[0] += own_x
-    for z in far:
-        chip_rows[z] += [shift_x(by_z[z], s) for s in range(1, chips)]
-    core_rows = {z: [other_core(by_z[z])] for z in by_z}
-    core_rows[0] += [other_core(value) for value in own_x]
-    kv_parts = [kv_sent] + [shift_dp(kv_sent, s) for s in range(1, node_count)]
-    fill_b = filled(gate_up_weight, down_weight, FILLS[0], FILLS[1], rows, by_z[far[-1]])
-    chip_rows, fill_b = lax.optimization_barrier((chip_rows, fill_b))
-    for z in far:
-        core_rows[z] += [other_core(value) for value in chip_rows[z][1:]]
-    blocks = [list(zip(chip_rows[z], core_rows[z])) for z in range(node_count)]
+    chip_rows = {z: [by_z[z]] + [shift_x(by_z[z], s) for s in range(1, chips)] for z in by_z}
+    kv_sent, chip_rows[far[0]][-1] = lax.optimization_barrier((kv_rows, chip_rows[far[0]][-1]))
+    blocks = [
+        [(value, other_core(value)) for value in chip_rows[z]] for z in range(node_count)
+    ]
+    kv_parts = [kv_rows] + [shift_dp(kv_sent, s) for s in range(1, node_count)]
+    blocks, kv_parts = lax.optimization_barrier((blocks, kv_parts))
 
     place = jnp.stack(
         [
@@ -449,7 +377,7 @@
         ]
     )
     sums = expert_sums(
-        place, norm_gain[None, :], gate_up_weight, down_weight, fill_a + fill_b, rows, blocks
+        place, norm_gain[None, :], gate_up_weight, down_weight, blocks
     )
 
     shares = [None] * node_count

time: 123 us -> 94.5 us (0.77)
  local copies, waits for them, and re-layouts: 33.1 us -> 3.89 us
  Pallas kernels: 41 us -> 30.1 us
  starting transfers between devices: 25.1 us -> 32.5 us
  waiting for transfers between devices: 16.4 us -> 22.9 us
  other arithmetic: 5.88 us -> 3.98 us
    unnamed x40 -> x12, local copies, waits for them, and re-layouts: 30.8 us -> 1.63 us
    pallas_call x2 -> x0, Pallas kernels: 10.3 us -> none  [filled(): pl.pallas_call(functools.partial(fill_kernel, first=first), out_shape=[pl...]
    ppermute x9, starting transfers between devices: 12.5 us -> 20.4 us  [shift_dp(): lax.ppermute(value, 'dp', [(i, (i + shift) % count) for i in range(count)])]
    ppermute x9, waiting for transfers between devices: 7.44 us -> 11.7 us  [shift_dp(): lax.ppermute(value, 'dp', [(i, (i + shift) % count) for i in range(count)])]
    convert_element_type x7, other arithmetic: 2.26 us -> 0.36 us  [added(): sum((value.astype(jnp.float32) for value in values)).astype(jnp.bfloat16)]
    ppermute x8, waiting for transfers between devices: 8.85 us -> 10.8 us  [shift_x(): lax.ppermute(value, 'mp', [(i, (i + CORES * shift) % count) for i in rang...]
  transfers between devices with their start and end apart: 29 -> 29, of which waited for: 8 -> 11; matrix products, arithmetic and copies ran while one was open for 6% -> 6% of each run, Pallas kernels for 32% -> 0%
where the time goes in v4:
time: 94.5 us; the launch traced here: 94.2 us
  starting transfers between devices  32.5 us (34%)
  Pallas kernels  30.1 us (32%)
  waiting for transfers between devices  22.9 us (24%)
  other arithmetic  3.98 us (4%)
  local copies, waits for them, and re-layouts  3.89 us (4%)
    pallas_call x1, Pallas kernels, expert_sums(): pl.pallas_call(functools.partial(expert_kernel, held=held, capacity=capac...  28.5 us
    ppermute x9, starting transfers between devices, shift_dp(): lax.ppermute(value, 'dp', [(i, (i + shift) % count) for i in range(count)])  20.4 us
    ppermute x9, waiting for transfers between devices, shift_dp(): lax.ppermute(value, 'dp', [(i, (i + shift) % count) for i in range(count)])  11.7 us
    ppermute x8, waiting for transfers between devices, shift_x(): lax.ppermute(value, 'mp', [(i, (i + CORES * shift) % count) for i in rang...  10.8 us
    ppermute x8, starting transfers between devices, shift_x(): lax.ppermute(value, 'mp', [(i, (i + CORES * shift) % count) for i in rang...  10 us
    gather x2, local copies, waits for them, and re-layouts, local(): cache_rows = padded_all[row_index[source_of]].reshape(-1, kv_width)  2.12 us
    ppermute x12, starting transfers between devices, other_core(): return lax.ppermute(value, 'mp', [(i, i ^ 1) for i in range(count)])  1.99 us
  transfers between devices with their start and end apart: 29, of which 11 were waited for; matrix products, arithmetic and copies ran while one was open for 6% of the time, Pallas kernels for 0%

profile of v4, /device:TPU:0, one launch (start us, length us, event | category | flops | bytes accessed | tf_op | source)
XLA Modules:
  0.0 94.2 jit_solution(15467701666744718663)
XLA Ops:
  0.7 1.7 %shard_map.104.refs_0_ = bf16[1,136,512]{2,1,0:T(8,128)(2,1)} custom-call(bf16[128,512]{1,0:T(8,128)(2,1)} %hidden_ref.1, s32[8,128]{1,0:T(8,128)} %bitcast.51, f32[8,128]{1,0:T(8,128)} %bitcast.52), custom_call_target="tpu_custom_call" | custom-call | tf_op jit(solution)/shard_map/pallas_call | solution.py:81
  2.3 4.0 %collective-permute-start.7 = (bf16[1,136,512]{2,1,0:T(8,128)(2,1)}, bf16[1,136,512]{2,1,0:T(8,128)(2,1)S(1)}, u32[]{:S(2)}, u32[]{:S(2)}) collective-permute-start(bf16[1,136,512]{2,1,0:T(8,128)(2,1)} %shard_map.104.refs_0_), channel_id=1, source_target_pairs={{0,8},{4,12},{8,0},{12,4},{1,9},{5,13},{9,1},{13,5},{2,10},{6,14},... | collective-permute-start | bytes 417800 | tf_op jit(solution)/shard_map/ppermute | solution.py:53
  6.4 1.3 %collective-permute-start.11 = (bf16[1,136,512]{2,1,0:T(8,128)(2,1)}, bf16[1,136,512]{2,1,0:T(8,128)(2,1)S(1)}, u32[]{:S(2)}, u32[]{:S(2)}) collective-permute-start(bf16[1,136,512]{2,1,0:T(8,128)(2,1)} %shard_map.104.refs_0_), channel_id=1, source_target_pairs={{0,12},{4,0},{8,4},{12,8},{1,13},{5,1},{9,5},{13,9},{2,14},{6,2},{... | collective-permute-start | bytes 417800 | tf_op jit(solution)/shard_map/ppermute | solution.py:53
  7.7 0.7 collective-permute-start.3
  8.4 1.5 %collective-permute-start.1 = (bf16[1,136,512]{2,1,0:T(8,128)(2,1)}, bf16[1,136,512]{2,1,0:T(8,128)(2,1)S(1)}, u32[]{:S(2)}, u32[]{:S(2)}) collective-permute-start(bf16[1,136,512]{2,1,0:T(8,128)(2,1)} %shard_map.104.refs_0_), channel_id=1, source_target_pairs={{0,2},{1,3},{2,0},{3,1},{4,6},{5,7},{6,4},{7,5},{8,10},{9,11},{10,... | collective-permute-start | bytes 417800 | tf_op jit(solution)/shard_map/ppermute | solution.py:58
  9.9 0.8 fusion.10
  10.9 0.9 reduce_window_sum.18
  11.7 0.8 select_reduce_fusion.2
  12.6 2.2 %collective-permute-done.7.refs_8_ = bf16[1,136,512]{2,1,0:T(8,128)(2,1)S(1)} collective-permute-done((bf16[1,136,512]{2,1,0:T(8,128)(2,1)}, bf16[1,136,512]{2,1,0:T(8,128)(2,1)S(1)}, u32[]{:S(2)}, u32[]{:S(2)}) %collective-permute-start.7) | collective-permute-done | bytes 139296 | tf_op jit(solution)/shard_map/ppermute | solution.py:53
  14.9 2.1 %collective-permute-start.9 = (bf16[1,136,512]{2,1,0:T(8,128)(2,1)S(1)}, bf16[1,136,512]{2,1,0:T(8,128)(2,1)S(1)}, u32[]{:S(2)}, u32[]{:S(2)}) collective-permute-start(bf16[1,136,512]{2,1,0:T(8,128)(2,1)S(1)} %collective-permute-done.7.refs_8_), channel_id=1, source_target_pairs={{0,2},{1,3},{2,0},{3,1},{4,6},{5,7},{6,4},{7,5},{8,10},{9,11},{10,... | collective-permute-start | bytes 417800 | tf_op jit(solution)/shard_map/ppermute | solution.py:58
  17.7 2.1 %collective-permute-start.5 = (bf16[1,136,512]{2,1,0:T(8,128)(2,1)S(1)}, bf16[1,136,512]{2,1,0:T(8,128)(2,1)S(1)}, u32[]{:S(2)}, u32[]{:S(2)}) collective-permute-start(bf16[1,136,512]{2,1,0:T(8,128)(2,1)S(1)} %collective-permute-done.3.refs_4_), channel_id=1, source_target_pairs={{0,2},{1,3},{2,0},{3,1},{4,6},{5,7},{6,4},{7,5},{8,10},{9,11},{10,... | collective-permute-start | bytes 417800 | tf_op jit(solution)/shard_map/ppermute | solution.py:58
  20.3 2.9 %collective-permute-done.13.refs_14_ = bf16[1,136,512]{2,1,0:T(8,128)(2,1)S(1)} collective-permute-done((bf16[1,136,512]{2,1,0:T(8,128)(2,1)S(1)}, bf16[1,136,512]{2,1,0:T(8,128)(2,1)S(1)}, u32[]{:S(2)}, u32[]{:S(2)}) %collective-permute-start.13) | collective-permute-done | bytes 139296 | tf_op jit(solution)/shard_map/ppermute | solution.py:58
  23.2 1.8 %collective-permute-done.5.refs_6_ = bf16[1,136,512]{2,1,0:T(8,128)(2,1)S(1)} collective-permute-done((bf16[1,136,512]{2,1,0:T(8,128)(2,1)S(1)}, bf16[1,136,512]{2,1,0:T(8,128)(2,1)S(1)}, u32[]{:S(2)}, u32[]{:S(2)}) %collective-permute-start.5) | collective-permute-done | bytes 139296 | tf_op jit(solution)/shard_map/ppermute | solution.py:58
  25.0 3.6 %collective-permute-start.15 = (bf16[128,256]{1,0:T(8,128)(2,1)}, bf16[128,256]{1,0:T(8,128)(2,1)S(1)}, u32[]{:S(2)}, u32[]{:S(2)}) collective-permute-start(bf16[128,256]{1,0:T(8,128)(2,1)} %param.15), channel_id=1, source_target_pairs={{0,4},{4,8},{8,12},{12,0},{1,5},{5,9},{9,13},{13,1},{2,6},{6,10},{... | collective-permute-start | bytes 196616 | tf_op jit(solution)/shard_map/ppermute | solution.py:53
  29.2 3.3 %collective-permute-start.16 = (bf16[128,256]{1,0:T(8,128)(2,1)}, bf16[128,256]{1,0:T(8,128)(2,1)S(1)}, u32[]{:S(2)}, u32[]{:S(2)}) collective-permute-start(bf16[128,256]{1,0:T(8,128)(2,1)} %param.15), channel_id=1, source_target_pairs={{0,8},{4,12},{8,0},{12,4},{1,9},{5,13},{9,1},{13,5},{2,10},{6,14},... | collective-permute-start | bytes 196616 | tf_op jit(solution)/shard_map/ppermute | solution.py:53
  32.6 1.6 %collective-permute-done.15 = bf16[128,256]{1,0:T(8,128)(2,1)S(1)} collective-permute-done((bf16[128,256]{1,0:T(8,128)(2,1)}, bf16[128,256]{1,0:T(8,128)(2,1)S(1)}, u32[]{:S(2)}, u32[]{:S(2)}) %collective-permute-start.15) | collective-permute-done | bytes 65568 | tf_op jit(solution)/shard_map/ppermute | solution.py:53
  34.2 1.7 %collective-permute-start.17 = (bf16[128,256]{1,0:T(8,128)(2,1)}, bf16[128,256]{1,0:T(8,128)(2,1)S(1)}, u32[]{:S(2)}, u32[]{:S(2)}) collective-permute-start(bf16[128,256]{1,0:T(8,128)(2,1)} %param.15), channel_id=1, source_target_pairs={{0,12},{4,0},{8,4},{12,8},{1,13},{5,1},{9,5},{13,9},{2,14},{6,2},{... | collective-permute-start | bytes 196616 | tf_op jit(solution)/shard_map/ppermute | solution.py:53
  35.9 0.8 collective-permute-done.16
  36.7 1.9 %collective-permute-done.17 = bf16[128,256]{1,0:T(8,128)(2,1)S(1)} collective-permute-done((bf16[128,256]{1,0:T(8,128)(2,1)}, bf16[128,256]{1,0:T(8,128)(2,1)S(1)}, u32[]{:S(2)}, u32[]{:S(2)}) %collective-permute-start.17) | collective-permute-done | bytes 65568 | tf_op jit(solution)/shard_map/ppermute | solution.py:53
  38.7 0.9 copy-done
  39.6 0.7 copy-done.1
  40.3 28.5 %shard_map.105 = (bf16[2,1,128,512]{3,2,1,0:T(8,128)(2,1)S(1)}, bf16[2,1,128,512]{3,2,1,0:T(8,128)(2,1)S(1)}, bf16[2,1,128,512]{3,2,1,0:T(8,128)(2,1)S(1)}, bf16...) custom-call(s32[3]{0:T(128)S(1)} %pad_add_fusion.place_ref, ...), custom_call_target="tpu_custom_call" | custom-call | flops 4831838208 | bytes 75497472 | tf_op jit(solution)/shard_map/pallas_call | solution.py:238
  70.4 1.6 %collective-permute-start.19 = (bf16[1,128,512]{2,1,0:T(8,128)(2,1)S(1)}, bf16[1,128,512]{2,1,0:T(8,128)(2,1)S(1)}, u32[]{:S(2)}, u32[]{:S(2)}) collective-permute-start(bf16[1,128,512]{2,1,0:T(8,128)(2,1)S(1)} %slice_bitcast_fusion.6), channel_id=1, source_target_pairs={{0,2},{1,3},{2,0},{3,1},{4,6},{5,7},{6,4},{7,5},{8,10},{9,11},{10,... | collective-permute-start | bytes 393224 | tf_op jit(solution)/shard_map/ppermute | solution.py:58
  72.8 1.6 %collective-permute-start.24 = (bf16[1,128,512]{2,1,0:T(8,128)(2,1)S(1)}, bf16[1,128,512]{2,1,0:T(8,128)(2,1)S(1)}, u32[]{:S(2)}, u32[]{:S(2)}) collective-permute-start(bf16[1,128,512]{2,1,0:T(8,128)(2,1)S(1)} %slice_bitcast_fusion.2), channel_id=1, source_target_pairs={{0,2},{1,3},{2,0},{3,1},{4,6},{5,7},{6,4},{7,5},{8,10},{9,11},{10,... | collective-permute-start | bytes 393224 | tf_op jit(solution)/shard_map/ppermute | solution.py:58
  74.4 0.6 collective-permute-start.27
  75.0 4.6 %collective-permute-done.21 = bf16[1,128,512]{2,1,0:T(8,128)(2,1)S(1)} collective-permute-done((bf16[1,128,512]{2,1,0:T(8,128)(2,1)S(1)}, bf16[1,128,512]{2,1,0:T(8,128)(2,1)S(1)}, u32[]{:S(2)}, u32[]{:S(2)}) %collective-permute-start.21) | collective-permute-done | bytes 131104 | tf_op jit(solution)/shard_map/ppermute | solution.py:58
  79.7 3.5 %collective-permute-start.22 = (bf16[1,128,512]{2,1,0:T(8,128)(2,1)S(1)}, bf16[1,128,512]{2,1,0:T(8,128)(2,1)S(1)}, u32[]{:S(2)}, u32[]{:S(2)}) collective-permute-start(bf16[1,128,512]{2,1,0:T(8,128)(2,1)S(1)} %fusion.2), channel_id=1, source_target_pairs={{0,12},{4,0},{8,4},{12,8},{1,13},{5,1},{9,5},{13,9},{2,14},{6,2},{... | collective-permute-start | bytes 393224 | tf_op jit(solution)/shard_map/ppermute | solution.py:53
  83.3 1.1 %collective-permute-done.27 = bf16[1,128,512]{2,1,0:T(8,128)(2,1)S(1)} collective-permute-done((bf16[1,128,512]{2,1,0:T(8,128)(2,1)S(1)}, bf16[1,128,512]{2,1,0:T(8,128)(2,1)S(1)}, u32[]{:S(2)}, u32[]{:S(2)}) %collective-permute-start.27) | collective-permute-done | bytes 131104 | tf_op jit(solution)/shard_map/ppermute | solution.py:58
  84.5 2.2 %collective-permute-start.28 = (bf16[1,128,512]{2,1,0:T(8,128)(2,1)S(1)}, bf16[1,128,512]{2,1,0:T(8,128)(2,1)S(1)}, u32[]{:S(2)}, u32[]{:S(2)}) collective-permute-start(bf16[1,128,512]{2,1,0:T(8,128)(2,1)S(1)} %fusion), channel_id=1, source_target_pairs={{0,4},{4,8},{8,12},{12,0},{1,5},{5,9},{9,13},{13,1},{2,6},{6,10},{... | collective-permute-start | bytes 393224 | tf_op jit(solution)/shard_map/ppermute | solution.py:53
  86.7 1.6 %gather_fusion.1 = bf16[160,256]{1,0:T(8,128)(2,1)} fusion(bf16[513,256]{1,0:T(8,128)(2,1)S(1)} %constant_dynamic-update-slice_fusion, s32[1024]{0:T(1024)S(1)} %pad_clamp_fusion), kind=kCustom, calls=%fused_computation.1 | custom fusion | bytes 164480 | tf_op jit(solution)/shard_map/gather | solution.py:410
  88.3 5.2 %collective-permute-done.25 = bf16[1,128,512]{2,1,0:T(8,128)(2,1)S(1)} collective-permute-done((bf16[1,128,512]{2,1,0:T(8,128)(2,1)S(1)}, bf16[1,128,512]{2,1,0:T(8,128)(2,1)S(1)}, u32[]{:S(2)}, u32[]{:S(2)}) %collective-permute-start.25) | collective-permute-done | bytes 131104 | tf_op jit(solution)/shard_map/ppermute | solution.py:53
  93.5 0.8 fusion.4
  (69 shorter events, 4.9 us)
Async XLA Ops:
  0.6 92.8 %copy-start.2 = (bf16[128,512]{1,0:T(8,128)(2,1)S(1)}, bf16[128,512]{1,0:T(8,128)(2,1)}, u32[]{:S(2)}) copy-start(bf16[128,512]{1,0:T(8,128)(2,1)} %hidden_ref.1) | copy-start | bytes 393220
  0.6 68.2 %copy-start.3 = (bf16[128,256]{1,0:T(8,128)(2,1)S(1)}, bf16[128,256]{1,0:T(8,128)(2,1)}, u32[]{:S(2)}) copy-start(bf16[128,256]{1,0:T(8,128)(2,1)} %param.15) | copy-start | bytes 196612
  2.3 12.5 %collective-permute-start.7 = (bf16[1,136,512]{2,1,0:T(8,128)(2,1)}, bf16[1,136,512]{2,1,0:T(8,128)(2,1)S(1)}, u32[]{:S(2)}, u32[]{:S(2)}) collective-permute-start(bf16[1,136,512]{2,1,0:T(8,128)(2,1)} %shard_map.104.refs_0_), channel_id=1, source_target_pairs={{0,8},{4,12},{8,0},{12,4},{1,9},{5,13},{9,1},{13,5},{2,10},{6,14},... | collective-permute-start | bytes 417800 | tf_op jit(solution)/shard_map/ppermute | solution.py:53
  6.4 10.7 %collective-permute-start.11 = (bf16[1,136,512]{2,1,0:T(8,128)(2,1)}, bf16[1,136,512]{2,1,0:T(8,128)(2,1)S(1)}, u32[]{:S(2)}, u32[]{:S(2)}) collective-permute-start(bf16[1,136,512]{2,1,0:T(8,128)(2,1)} %shard_map.104.refs_0_), channel_id=1, source_target_pairs={{0,12},{4,0},{8,4},{12,8},{1,13},{5,1},{9,5},{13,9},{2,14},{6,2},{... | collective-permute-start | bytes 417800 | tf_op jit(solution)/shard_map/ppermute | solution.py:53
  7.7 9.9 %collective-permute-start.3 = (bf16[1,136,512]{2,1,0:T(8,128)(2,1)}, bf16[1,136,512]{2,1,0:T(8,128)(2,1)S(1)}, u32[]{:S(2)}, u32[]{:S(2)}) collective-permute-start(bf16[1,136,512]{2,1,0:T(8,128)(2,1)} %shard_map.104.refs_0_), channel_id=1, source_target_pairs={{0,4},{4,8},{8,12},{12,0},{1,5},{5,9},{9,13},{13,1},{2,6},{6,10},{... | collective-permute-start | bytes 417800 | tf_op jit(solution)/shard_map/ppermute | solution.py:53
  8.4 9.3 %collective-permute-start.1 = (bf16[1,136,512]{2,1,0:T(8,128)(2,1)}, bf16[1,136,512]{2,1,0:T(8,128)(2,1)S(1)}, u32[]{:S(2)}, u32[]{:S(2)}) collective-permute-start(bf16[1,136,512]{2,1,0:T(8,128)(2,1)} %shard_map.104.refs_0_), channel_id=1, source_target_pairs={{0,2},{1,3},{2,0},{3,1},{4,6},{5,7},{6,4},{7,5},{8,10},{9,11},{10,... | collective-permute-start | bytes 417800 | tf_op jit(solution)/shard_map/ppermute | solution.py:58
  9.9 9.9 %collective-permute-start = (bf16[1,136,512]{2,1,0:T(8,128)(2,1)}, bf16[1,136,512]{2,1,0:T(8,128)(2,1)S(1)}, u32[]{:S(2)}, u32[]{:S(2)}) collective-permute-start(bf16[1,136,512]{2,1,0:T(8,128)(2,1)} %shard_map.104.refs_0_), channel_id=1, source_target_pairs={{0,1},{1,0},{2,3},{3,2},{4,5},{5,4},{6,7},{7,6},{8,9},{9,8},{10,11... | collective-permute-start | bytes 417800 | tf_op jit(solution)/shard_map/ppermute | solution.py:63
  14.9 5.4 %collective-permute-start.9 = (bf16[1,136,512]{2,1,0:T(8,128)(2,1)S(1)}, bf16[1,136,512]{2,1,0:T(8,128)(2,1)S(1)}, u32[]{:S(2)}, u32[]{:S(2)}) collective-permute-start(bf16[1,136,512]{2,1,0:T(8,128)(2,1)S(1)} %collective-permute-done.7.refs_8_), channel_id=1, source_target_pairs={{0,2},{1,3},{2,0},{3,1},{4,6},{5,7},{6,4},{7,5},{8,10},{9,11},{10,... | collective-permute-start | bytes 417800 | tf_op jit(solution)/shard_map/ppermute | solution.py:58
  17.0 6.1 %collective-permute-start.13 = (bf16[1,136,512]{2,1,0:T(8,128)(2,1)S(1)}, bf16[1,136,512]{2,1,0:T(8,128)(2,1)S(1)}, u32[]{:S(2)}, u32[]{:S(2)}) collective-permute-start(bf16[1,136,512]{2,1,0:T(8,128)(2,1)S(1)} %collective-permute-done.11.refs_12_), channel_id=1, source_target_pairs={{0,2},{1,3},{2,0},{3,1},{4,6},{5,7},{6,4},{7,5},{8,10},{9,11},{10,... | collective-permute-start | bytes 417800 | tf_op jit(solution)/shard_map/ppermute | solution.py:58
  17.6 11.0 %collective-permute-start.12 = (bf16[1,136,512]{2,1,0:T(8,128)(2,1)S(1)}, bf16[1,136,512]{2,1,0:T(8,128)(2,1)S(1)}, u32[]{:S(2)}, u32[]{:S(2)}) collective-permute-start(bf16[1,136,512]{2,1,0:T(8,128)(2,1)S(1)} %collective-permute-done.11.refs_12_), channel_id=1, source_target_pairs={{0,1},{1,0},{2,3},{3,2},{4,5},{5,4},{6,7},{7,6},{8,9},{9,8},{10,11... | collective-permute-start | bytes 417800 | tf_op jit(solution)/shard_map/ppermute | solution.py:63
  17.7 7.3 %collective-permute-start.5 = (bf16[1,136,512]{2,1,0:T(8,128)(2,1)S(1)}, bf16[1,136,512]{2,1,0:T(8,128)(2,1)S(1)}, u32[]{:S(2)}, u32[]{:S(2)}) collective-permute-start(bf16[1,136,512]{2,1,0:T(8,128)(2,1)S(1)} %collective-permute-done.3.refs_4_), channel_id=1, source_target_pairs={{0,2},{1,3},{2,0},{3,1},{4,6},{5,7},{6,4},{7,5},{8,10},{9,11},{10,... | collective-permute-start | bytes 417800 | tf_op jit(solution)/shard_map/ppermute | solution.py:58
  19.8 8.9 %collective-permute-start.4 = (bf16[1,136,512]{2,1,0:T(8,128)(2,1)S(1)}, bf16[1,136,512]{2,1,0:T(8,128)(2,1)S(1)}, u32[]{:S(2)}, u32[]{:S(2)}) collective-permute-start(bf16[1,136,512]{2,1,0:T(8,128)(2,1)S(1)} %collective-permute-done.3.refs_4_), channel_id=1, source_target_pairs={{0,1},{1,0},{2,3},{3,2},{4,5},{5,4},{6,7},{7,6},{8,9},{9,8},{10,11... | collective-permute-start | bytes 417800 | tf_op jit(solution)/shard_map/ppermute | solution.py:63
  20.2 8.9 %collective-permute-start.8 = (bf16[1,136,512]{2,1,0:T(8,128)(2,1)S(1)}, bf16[1,136,512]{2,1,0:T(8,128)(2,1)S(1)}, u32[]{:S(2)}, u32[]{:S(2)}) collective-permute-start(bf16[1,136,512]{2,1,0:T(8,128)(2,1)S(1)} %collective-permute-done.7.refs_8_), channel_id=1, source_target_pairs={{0,1},{1,0},{2,3},{3,2},{4,5},{5,4},{6,7},{7,6},{8,9},{9,8},{10,11... | collective-permute-start | bytes 417800 | tf_op jit(solution)/shard_map/ppermute | solution.py:63
  23.1 6.1 %collective-permute-start.2 = (bf16[1,136,512]{2,1,0:T(8,128)(2,1)S(1)}, bf16[1,136,512]{2,1,0:T(8,128)(2,1)S(1)}, u32[]{:S(2)}, u32[]{:S(2)}) collective-permute-start(bf16[1,136,512]{2,1,0:T(8,128)(2,1)S(1)} %collective-permute-done.1.refs_2_), channel_id=1, source_target_pairs={{0,1},{1,0},{2,3},{3,2},{4,5},{5,4},{6,7},{7,6},{8,9},{9,8},{10,11... | collective-permute-start | bytes 417800 | tf_op jit(solution)/shard_map/ppermute | solution.py:63
  25.0 9.1 %collective-permute-start.15 = (bf16[128,256]{1,0:T(8,128)(2,1)}, bf16[128,256]{1,0:T(8,128)(2,1)S(1)}, u32[]{:S(2)}, u32[]{:S(2)}) collective-permute-start(bf16[128,256]{1,0:T(8,128)(2,1)} %param.15), channel_id=1, source_target_pairs={{0,4},{4,8},{8,12},{12,0},{1,5},{5,9},{9,13},{13,1},{2,6},{6,10},{... | collective-permute-start | bytes 196616 | tf_op jit(solution)/shard_map/ppermute | solution.py:53
  28.6 10.0 %collective-permute-start.10 = (bf16[1,136,512]{2,1,0:T(8,128)(2,1)S(1)}, bf16[1,136,512]{2,1,0:T(8,128)(2,1)S(1)}, u32[]{:S(2)}, u32[]{:S(2)}) collective-permute-start(bf16[1,136,512]{2,1,0:T(8,128)(2,1)S(1)} %collective-permute-done.9.refs_10_), channel_id=1, source_target_pairs={{0,1},{1,0},{2,3},{3,2},{4,5},{5,4},{6,7},{7,6},{8,9},{9,8},{10,11... | collective-permute-start | bytes 417800 | tf_op jit(solution)/shard_map/ppermute | solution.py:63
  28.7 10.0 %collective-permute-start.14 = (bf16[1,136,512]{2,1,0:T(8,128)(2,1)S(1)}, bf16[1,136,512]{2,1,0:T(8,128)(2,1)S(1)}, u32[]{:S(2)}, u32[]{:S(2)}) collective-permute-start(bf16[1,136,512]{2,1,0:T(8,128)(2,1)S(1)} %collective-permute-done.13.refs_14_), channel_id=1, source_target_pairs={{0,1},{1,0},{2,3},{3,2},{4,5},{5,4},{6,7},{7,6},{8,9},{9,8},{10,11... | collective-permute-start | bytes 417800 | tf_op jit(solution)/shard_map/ppermute | solution.py:63
  29.2 9.5 %collective-permute-start.6 = (bf16[1,136,512]{2,1,0:T(8,128)(2,1)S(1)}, bf16[1,136,512]{2,1,0:T(8,128)(2,1)S(1)}, u32[]{:S(2)}, u32[]{:S(2)}) collective-permute-start(bf16[1,136,512]{2,1,0:T(8,128)(2,1)S(1)} %collective-permute-done.5.refs_6_), channel_id=1, source_target_pairs={{0,1},{1,0},{2,3},{3,2},{4,5},{5,4},{6,7},{7,6},{8,9},{9,8},{10,11... | collective-permute-start | bytes 417800 | tf_op jit(solution)/shard_map/ppermute | solution.py:63
  29.2 7.5 %collective-permute-start.16 = (bf16[128,256]{1,0:T(8,128)(2,1)}, bf16[128,256]{1,0:T(8,128)(2,1)S(1)}, u32[]{:S(2)}, u32[]{:S(2)}) collective-permute-start(bf16[128,256]{1,0:T(8,128)(2,1)} %param.15), channel_id=1, source_target_pairs={{0,8},{4,12},{8,0},{12,4},{1,9},{5,13},{9,1},{13,5},{2,10},{6,14},... | collective-permute-start | bytes 196616 | tf_op jit(solution)/shard_map/ppermute | solution.py:53
  34.2 4.5 %collective-permute-start.17 = (bf16[128,256]{1,0:T(8,128)(2,1)}, bf16[128,256]{1,0:T(8,128)(2,1)S(1)}, u32[]{:S(2)}, u32[]{:S(2)}) collective-permute-start(bf16[128,256]{1,0:T(8,128)(2,1)} %param.15), channel_id=1, source_target_pairs={{0,12},{4,0},{8,4},{12,8},{1,13},{5,1},{9,5},{13,9},{2,14},{6,2},{... | collective-permute-start | bytes 196616 | tf_op jit(solution)/shard_map/ppermute | solution.py:53
  38.7 0.9 copy-start
  68.7 1.6 %collective-permute-start.18 = (bf16[2,1,128,512]{3,2,1,0:T(8,128)(2,1)S(1)}, bf16[2,1,128,512]{3,2,1,0:T(8,128)(2,1)S(1)}, u32[]{:S(2)}, u32[]{:S(2)}) collective-permute-start(bf16[2,1,128,512]{3,2,1,0:T(8,128)(2,1)S(1)} %get-tuple-element.51), channel_id=1, source_target_pairs={{0,1},{1,0},{2,3},{3,2},{4,5},{5,4},{6,7},{7,6},{8,9},{9,8},{10,11... | collective-permute-start | bytes 786440 | tf_op jit(solution)/shard_map/ppermute | solution.py:63
  68.9 3.1 %collective-permute-start.20 = (bf16[2,1,128,512]{3,2,1,0:T(8,128)(2,1)S(1)}, bf16[2,1,128,512]{3,2,1,0:T(8,128)(2,1)S(1)}, u32[]{:S(2)}, u32[]{:S(2)}) collective-permute-start(bf16[2,1,128,512]{3,2,1,0:T(8,128)(2,1)S(1)} %get-tuple-element.53), channel_id=1, source_target_pairs={{0,1},{1,0},{2,3},{3,2},{4,5},{5,4},{6,7},{7,6},{8,9},{9,8},{10,11... | collective-permute-start | bytes 786440 | tf_op jit(solution)/shard_map/ppermute | solution.py:63
  69.4 3.3 %collective-permute-start.23 = (bf16[2,1,128,512]{3,2,1,0:T(8,128)(2,1)S(1)}, bf16[2,1,128,512]{3,2,1,0:T(8,128)(2,1)S(1)}, u32[]{:S(2)}, u32[]{:S(2)}) collective-permute-start(bf16[2,1,128,512]{3,2,1,0:T(8,128)(2,1)S(1)} %get-tuple-element.55), channel_id=1, source_target_pairs={{0,1},{1,0},{2,3},{3,2},{4,5},{5,4},{6,7},{7,6},{8,9},{9,8},{10,11... | collective-permute-start | bytes 786440 | tf_op jit(solution)/shard_map/ppermute | solution.py:63
  69.5 4.9 %collective-permute-start.26 = (bf16[2,1,128,512]{3,2,1,0:T(8,128)(2,1)S(1)}, bf16[2,1,128,512]{3,2,1,0:T(8,128)(2,1)S(1)}, u32[]{:S(2)}, u32[]{:S(2)}) collective-permute-start(bf16[2,1,128,512]{3,2,1,0:T(8,128)(2,1)S(1)} %get-tuple-element.57), channel_id=1, source_target_pairs={{0,1},{1,0},{2,3},{3,2},{4,5},{5,4},{6,7},{7,6},{8,9},{9,8},{10,11... | collective-permute-start | bytes 786440 | tf_op jit(solution)/shard_map/ppermute | solution.py:63
  70.4 17.8 %collective-permute-start.19 = (bf16[1,128,512]{2,1,0:T(8,128)(2,1)S(1)}, bf16[1,128,512]{2,1,0:T(8,128)(2,1)S(1)}, u32[]{:S(2)}, u32[]{:S(2)}) collective-permute-start(bf16[1,128,512]{2,1,0:T(8,128)(2,1)S(1)} %slice_bitcast_fusion.6), channel_id=1, source_target_pairs={{0,2},{1,3},{2,0},{3,1},{4,6},{5,7},{6,4},{7,5},{8,10},{9,11},{10,... | collective-permute-start | bytes 393224 | tf_op jit(solution)/shard_map/ppermute | solution.py:58
  72.1 7.6 %collective-permute-start.21 = (bf16[1,128,512]{2,1,0:T(8,128)(2,1)S(1)}, bf16[1,128,512]{2,1,0:T(8,128)(2,1)S(1)}, u32[]{:S(2)}, u32[]{:S(2)}) collective-permute-start(bf16[1,128,512]{2,1,0:T(8,128)(2,1)S(1)} %slice_bitcast_fusion.4), channel_id=1, source_target_pairs={{0,2},{1,3},{2,0},{3,1},{4,6},{5,7},{6,4},{7,5},{8,10},{9,11},{10,... | collective-permute-start | bytes 393224 | tf_op jit(solution)/shard_map/ppermute | solution.py:58
  72.8 10.4 %collective-permute-start.24 = (bf16[1,128,512]{2,1,0:T(8,128)(2,1)S(1)}, bf16[1,128,512]{2,1,0:T(8,128)(2,1)S(1)}, u32[]{:S(2)}, u32[]{:S(2)}) collective-permute-start(bf16[1,128,512]{2,1,0:T(8,128)(2,1)S(1)} %slice_bitcast_fusion.2), channel_id=1, source_target_pairs={{0,2},{1,3},{2,0},{3,1},{4,6},{5,7},{6,4},{7,5},{8,10},{9,11},{10,... | collective-permute-start | bytes 393224 | tf_op jit(solution)/shard_map/ppermute | solution.py:58
  74.4 10.0 %collective-permute-start.27 = (bf16[1,128,512]{2,1,0:T(8,128)(2,1)S(1)}, bf16[1,128,512]{2,1,0:T(8,128)(2,1)S(1)}, u32[]{:S(2)}, u32[]{:S(2)}) collective-permute-start(bf16[1,128,512]{2,1,0:T(8,128)(2,1)S(1)} %slice_bitcast_fusion), channel_id=1, source_target_pairs={{0,2},{1,3},{2,0},{3,1},{4,6},{5,7},{6,4},{7,5},{8,10},{9,11},{10,... | collective-permute-start | bytes 393224 | tf_op jit(solution)/shard_map/ppermute | solution.py:58
  79.7 8.6 %collective-permute-start.22 = (bf16[1,128,512]{2,1,0:T(8,128)(2,1)S(1)}, bf16[1,128,512]{2,1,0:T(8,128)(2,1)S(1)}, u32[]{:S(2)}, u32[]{:S(2)}) collective-permute-start(bf16[1,128,512]{2,1,0:T(8,128)(2,1)S(1)} %fusion.2), channel_id=1, source_target_pairs={{0,12},{4,0},{8,4},{12,8},{1,13},{5,1},{9,5},{13,9},{2,14},{6,2},{... | collective-permute-start | bytes 393224 | tf_op jit(solution)/shard_map/ppermute | solution.py:53
  83.2 10.2 %collective-permute-start.25 = (bf16[1,128,512]{2,1,0:T(8,128)(2,1)S(1)}, bf16[1,128,512]{2,1,0:T(8,128)(2,1)S(1)}, u32[]{:S(2)}, u32[]{:S(2)}) collective-permute-start(bf16[1,128,512]{2,1,0:T(8,128)(2,1)S(1)} %fusion.1), channel_id=1, source_target_pairs={{0,8},{4,12},{8,0},{12,4},{1,9},{5,13},{9,1},{13,5},{2,10},{6,14},... | collective-permute-start | bytes 393224 | tf_op jit(solution)/shard_map/ppermute | solution.py:53
  84.5 9.0 %collective-permute-start.28 = (bf16[1,128,512]{2,1,0:T(8,128)(2,1)S(1)}, bf16[1,128,512]{2,1,0:T(8,128)(2,1)S(1)}, u32[]{:S(2)}, u32[]{:S(2)}) collective-permute-start(bf16[1,128,512]{2,1,0:T(8,128)(2,1)S(1)} %fusion), channel_id=1, source_target_pairs={{0,4},{4,8},{8,12},{12,0},{1,5},{5,9},{9,13},{13,1},{2,6},{6,10},{... | collective-permute-start | bytes 393224 | tf_op jit(solution)/shard_map/ppermute | solution.py:53
  (1 other events, 0.7 us)

commit v5 on v4

--- a/solution.py
+++ b/solution.py
@@ -13,7 +13,9 @@
 CAP = 16
 SEND_CAP = 40
 CORES = 2
-MOST_SHIFTS = 4
+HOP_NODES = 4
+PAGE_FOLD = 24
+SMALL_VMEM = 4 * 1024 * 1024
 WEIGHT_SLOTS = 3
 EXPERT_VMEM = 44 * 1024 * 1024
 
@@ -83,11 +85,86 @@
         out_shape=jax.ShapeDtypeStruct((1, tok_node + TOPK, width), jnp.bfloat16),
         in_specs=[vmem] * 3,
         out_specs=vmem,
+        compiler_params=pltpu.CompilerParams(vmem_limit_bytes=SMALL_VMEM),
     )(hidden_states, routes.T, gates.T)
 
 
+def page_kernel(lengths_ref, owners_ref, kv_ref, out_ref):
+    nodes, _, width = out_ref.shape
+    tok_node, kv_width = kv_ref.shape
+    me = lax.axis_index("dp")
+    token = lax.broadcasted_iota(jnp.int32, (PAGE_FOLD, tok_node), 1)
+    row = lax.broadcasted_iota(jnp.int32, (PAGE_FOLD, tok_node), 0)
+    for s in range(nodes):
+        owner = lax.rem(me + nodes - s, nodes)
+        start, first, length = jnp.int32(0), jnp.int32(0), jnp.int32(0)
+        for segment in range(owners_ref.shape[1]):
+            size = lengths_ref[me, segment]
+            mine = owners_ref[me, segment] == owner
+            first = jnp.where(mine, start, first)
+            length = jnp.where(mine, size, length)
+            start = start + size
+        for half in range(2):
+            at = row + half * PAGE_FOLD
+            pick = jnp.where((at < length) & (token == first + at), 1.0, 0.0)
+            out_ref[s, :, half * kv_width : (half + 1) * kv_width] = jnp.dot(
+                pick.astype(jnp.bfloat16), kv_ref[...], preferred_element_type=jnp.float32
+            ).astype(jnp.bfloat16)
+
+
+def kv_pages(kv_rows, lengths, owners, node_count):
+    vmem = pl.BlockSpec(memory_space=pltpu.VMEM)
+    smem = pl.BlockSpec(memory_space=pltpu.SMEM)
+    return pl.pallas_call(
+        page_kernel,
+        out_shape=jax.ShapeDtypeStruct(
+            (node_count, PAGE_FOLD, 2 * kv_rows.shape[1]), jnp.bfloat16
+        ),
+        in_specs=[smem, smem, vmem],
+        out_specs=vmem,
+        compiler_params=pltpu.CompilerParams(vmem_limit_bytes=SMALL_VMEM),
+    )(lengths, owners, kv_rows)
+
+
+def final_kernel(hidden_ref, own_ref, down_ref, up_ref, pages_ref, mixed_ref, cache_ref):
+    tok_node = hidden_ref.shape[0]
+    nodes = pages_ref.shape[0]
+    kv_width = cache_ref.shape[1]
+    total = hidden_ref[...].astype(jnp.float32)
+    for ref in (own_ref, down_ref, up_ref):
+        total = total + ref[:tok_node, :].astype(jnp.float32)
+    mixed_ref[...] = total.astype(jnp.bfloat16)
+    came = [pages_ref[0], down_ref[tok_node : tok_node + PAGE_FOLD, :]]
+    came += [down_ref[tok_node + PAGE_FOLD :, :], up_ref[tok_node:, :]]
+    came = [page.astype(jnp.float32) for page in came]
+    me = lax.axis_index("dp")
+    rows = []
+    for source in range(nodes):
+        away = lax.rem(source + nodes - me, nodes)
+        page = came[0]
+        for s in range(1, nodes):
+            page = jnp.where(away == s, came[s], page)
+        rows += [page[:, :kv_width], page[: SEND_CAP - PAGE_FOLD, kv_width:]]
+    cache_ref[...] = jnp.concatenate(rows, axis=0).astype(jnp.bfloat16)
+
+
+def finished(hidden_states, own, down, up, pages):
+    vmem = pl.BlockSpec(memory_space=pltpu.VMEM)
+    nodes, _, width = pages.shape
+    return pl.pallas_call(
+        final_kernel,
+        out_shape=[
+            jax.ShapeDtypeStruct(hidden_states.shape, jnp.bfloat16),
+            jax.ShapeDtypeStruct((nodes * SEND_CAP, width // 2), jnp.bfloat16),
+        ],
+        in_specs=[vmem] * 5,
+        out_specs=[vmem] * 2,
+        compiler_params=pltpu.CompilerParams(vmem_limit_bytes=SMALL_VMEM),
+    )(hidden_states, own, down, up, pages)
+
+
 def expert_kernel(
-    place_ref, gain_ref, gate_up_ref, down_ref, *refs, held, capacity, parts, chips,
+    gain_ref, gate_up_ref, down_ref, pages_ref, *refs, held, capacity, parts, chips,
 ):
     block_refs, out_refs = refs[: parts * chips * CORES], refs[parts * chips * CORES :]
     out_refs, scratch = out_refs[: parts * CORES], out_refs[parts * CORES :]
@@ -109,6 +186,9 @@
         for copy in fetch(h, h):
             copy.start()
 
+    column = lax.axis_index("mp")
+    my_x, my_core = lax.div(column, CORES), lax.rem(column, CORES)
+    first_expert = (lax.axis_index("dp") * lax.axis_size("mp") + column) * held
     blocks = [
         [[block_refs[(z * chips + x) * CORES + c] for c in range(CORES)] for x in range(chips)]
         for z in range(parts)
@@ -117,7 +197,7 @@
         [
             pl.ds(
                 pl.multiple_of(
-                    (lax.rem(place_ref[1] + chips - x, chips) * CORES + (place_ref[2] ^ c)) * width,
+                    (lax.rem(my_x + chips - x, chips) * CORES + (my_core ^ c)) * width,
                     width,
                 ),
                 width,
@@ -127,7 +207,7 @@
         for x in range(chips)
     ]
 
-    expert = place_ref[0] + lax.broadcasted_iota(jnp.int32, (held, 1), 0)
+    expert = first_expert + lax.broadcasted_iota(jnp.int32, (held, 1), 0)
     named, gate = [], []
     for z in range(parts):
         total = jnp.zeros((tok_node, 1), jnp.float32)
@@ -221,7 +301,7 @@
                 out_refs[z * CORES + c][x, 0] = summed[z * tok_node : (z + 1) * tok_node, :]
 
 
-def expert_sums(place, gain, gate_up_weight, down_weight, blocks):
+def expert_sums(gain, gate_up_weight, down_weight, pages, blocks):
     parts, chips = len(blocks), len(blocks[0])
     _, block_rows, width = blocks[0][0][0].shape
     tok_node = block_rows - TOPK
@@ -241,8 +321,7 @@
         ),
         out_shape=[jax.ShapeDtypeStruct((chips, 1, tok_node, width), jnp.bfloat16)]
         * (parts * CORES),
-        in_specs=[pl.BlockSpec(memory_space=pltpu.SMEM), vmem, hbm, hbm]
-        + [vmem] * len(flat),
+        in_specs=[vmem, hbm, hbm, pl.BlockSpec(memory_space=pl.ANY)] + [vmem] * len(flat),
         out_specs=[vmem] * (parts * CORES),
         scratch_shapes=[
             pltpu.VMEM((tokens, model_width), jnp.bfloat16),
@@ -260,12 +339,8 @@
             bytes_accessed=6 * ff_dev * model_width,
             transcendentals=0,
         ),
-    )(place, gain, gate_up_weight, down_weight, *flat)
+    )(gain, gate_up_weight, down_weight, pages, *flat)
     return [sums[z * CORES : (z + 1) * CORES] for z in range(parts)]
-
-
-def farthest_first(node_count):
-    return sorted(range(node_count), key=lambda z: (-min(z, node_count - z), z))
 
 
 def added(*values):
@@ -349,66 +424,34 @@
     node_count = lax.axis_size("dp")
     column_count = lax.axis_size("mp")
     chips = column_count // CORES
-    node_index = lax.axis_index("dp")
-    column_index = lax.axis_index("mp")
-    tok_node, width = hidden_states.shape
-    ff_dev = down_weight.shape[0]
-    seg_count = owners.shape[1]
     gate_up_weight = pltpu.with_memory_space_constraint(gate_up_weight, pltpu.HBM)
     down_weight = pltpu.with_memory_space_constraint(down_weight, pltpu.HBM)
     block = packed(hidden_states, routes, gates)
 
-    far = farthest_first(node_count)[:-1]
-    by_z = {z: shift_dp(block, z) for z in far}
-    by_z[0] = block
+    by_z = {0: block, 1: shift_dp(block, 1), 3: shift_dp(block, -1)}
+    by_z[2] = shift_dp(by_z[1], 1)
     chip_rows = {z: [by_z[z]] + [shift_x(by_z[z], s) for s in range(1, chips)] for z in by_z}
-    kv_sent, chip_rows[far[0]][-1] = lax.optimization_barrier((kv_rows, chip_rows[far[0]][-1]))
     blocks = [
         [(value, other_core(value)) for value in chip_rows[z]] for z in range(node_count)
     ]
-    kv_parts = [kv_rows] + [shift_dp(kv_sent, s) for s in range(1, node_count)]
-    blocks, kv_parts = lax.optimization_barrier((blocks, kv_parts))
-
-    place = jnp.stack(
-        [
-            (node_index * column_count + column_index) * ff_dev // FF,
-            column_index // CORES,
-            column_index % CORES,
-        ]
-    )
-    sums = expert_sums(
-        place, norm_gain[None, :], gate_up_weight, down_weight, blocks
-    )
-
-    shares = [None] * node_count
-    for z in farthest_first(node_count):
+    kv_rows, _ = lax.optimization_barrier((kv_rows, by_z[1]))
+    pages = kv_pages(kv_rows, lengths, owners, node_count)
+    sums = expert_sums(norm_gain[None, :], gate_up_weight, down_weight, pages, blocks)
+
+    shares = {}
+    for z in (2, 1, 3, 0):
         keep, send = sums[z]
         chip_sum = added(keep, other_core(send))
-        shares[z] = added(chip_sum[0], *[shift_x(chip_sum[s], -s) for s in range(1, chips)])
-    moe_share = sum(
-        (shares[s] if s == 0 else shift_dp(shares[s], -s)).astype(jnp.float32)
-        for s in range(node_count)
-    )[0]
-    mixed_out = (hidden_states.astype(jnp.float32) + moe_share).astype(jnp.bfloat16)
-
-    kv_width = kv_rows.shape[1]
-    starts = jnp.cumsum(lengths, axis=1) - lengths
-    page_slot = jnp.arange(SEND_CAP, dtype=jnp.int32)
-    source = jnp.arange(node_count, dtype=jnp.int32)
-    source_of = sources_for(owners, node_index, seg_count)
-    all_rows = jnp.concatenate(kv_parts, axis=0)
-    source = (node_index - source) % node_count
-    owner_match = owners == node_index
-    seg_len = jnp.sum(jnp.where(owner_match, lengths, 0), axis=1)
-    seg_start = jnp.sum(jnp.where(owner_match, starts, 0), axis=1) + source * tok_node
-    row_index = jnp.where(
-        page_slot[None, :] < seg_len[:, None],
-        seg_start[:, None] + page_slot[None, :],
-        node_count * tok_node,
-    )
-    padded_all = jnp.concatenate([all_rows, jnp.zeros((1, kv_width), jnp.bfloat16)], axis=0)
-    cache_rows = padded_all[row_index[source_of]].reshape(-1, kv_width)
-    return (mixed_out, cache_rows)
+        shares[z] = added(chip_sum[0], *[shift_x(chip_sum[s], -s) for s in range(1, chips)])[0]
+    passed = shift_dp(jnp.concatenate([shares[2], pages[2]], axis=0), -1)
+    tok_node = hidden_states.shape[0]
+    down = jnp.concatenate(
+        [added(shares[1], passed[:tok_node]), pages[1], passed[tok_node:]], axis=0
+    )
+    up = jnp.concatenate([shares[3], pages[3]], axis=0)
+    return finished(
+        hidden_states, shares[0], shift_dp(down, -1), shift_dp(up, 1), pages
+    )
 
 
 def solution(mesh):
@@ -424,5 +467,5 @@
         P("groups", None),
     )
     out_specs = (P(("groups", "dp"), "mp"), P(("groups", "dp"), "mp"))
-    body = local if mesh.shape["dp"] <= MOST_SHIFTS else plain_local
+    body = local if mesh.shape["dp"] == HOP_NODES else plain_local
     return jax.shard_map(body, mesh=mesh, in_specs=in_specs, out_specs=out_specs, check_vma=False)

time: 94.5 us -> 85.8 us (0.908)
  starting transfers between devices: 32.5 us -> 25.7 us
  other arithmetic: 3.98 us -> 0.51 us
  local copies, waits for them, and re-layouts: 3.89 us -> 5.22 us
    ppermute x9 -> x6, starting transfers between devices: 20.4 us -> 12.6 us  [shift_dp(): lax.ppermute(value, 'dp', [(i, (i + shift) % count) for i in range(count)])]
    unnamed x12 -> x16, local copies, waits for them, and re-layouts: 1.63 us -> 5.17 us
    gather x2 -> x0, local copies, waits for them, and re-layouts: 2.12 us -> none  [local(): cache_rows = padded_all[row_index[source_of]].reshape(-1, kv_width)]
    pallas_call x1, Pallas kernels: 1.66 us -> 0.02 us  [packed(): pl.pallas_call(pack_kernel, out_shape=jax.ShapeDtypeStruct((1, tok_node +...]
    ppermute x9 -> x6, waiting for transfers between devices: 11.7 us -> 13.4 us  [shift_dp(): lax.ppermute(value, 'dp', [(i, (i + shift) % count) for i in range(count)])]
    pallas_call x0 -> x2, Pallas kernels: none -> 1.54 us  [the longest x1 0.79 us: kv_pages(): pl.pallas_call(page_kernel, out_shape=jax.ShapeDtypeStruct((node_count, P...]
    another operation x3 -> x0, other arithmetic: 1.11 us -> none  [the longest x1 0.85 us: local(): starts = jnp.cumsum(lengths, axis=1) - lengths]
    ppermute x8, waiting for transfers between devices: 10.8 us -> 9.7 us  [shift_x(): lax.ppermute(value, 'mp', [(i, (i + CORES * shift) % count) for i in rang...]
  transfers between devices with their start and end apart: 29 -> 26, of which waited for: 11 -> 8; matrix products, arithmetic and copies ran while one was open for 6% -> 1% of each run, Pallas kernels for 0% -> 1%
where the time goes in v5:
time: 85.8 us; the launch traced here: 85.5 us
  Pallas kernels  29.5 us (34%)
  starting transfers between devices  25.7 us (30%)
  waiting for transfers between devices  23.7 us (28%)
  local copies, waits for them, and re-layouts  5.22 us (6%)
    pallas_call x1, Pallas kernels, expert_sums(): pl.pallas_call(functools.partial(expert_kernel, held=held, capacity=capac...  27.9 us
    ppermute x6, waiting for transfers between devices, shift_dp(): lax.ppermute(value, 'dp', [(i, (i + shift) % count) for i in range(count)])  13.4 us
    ppermute x6, starting transfers between devices, shift_dp(): lax.ppermute(value, 'dp', [(i, (i + shift) % count) for i in range(count)])  12.6 us
    ppermute x8, starting transfers between devices, shift_x(): lax.ppermute(value, 'mp', [(i, (i + CORES * shift) % count) for i in rang...  10.7 us
    ppermute x8, waiting for transfers between devices, shift_x(): lax.ppermute(value, 'mp', [(i, (i + CORES * shift) % count) for i in rang...  9.7 us
    unnamed x16, local copies, waits for them, and re-layouts  5.17 us
    ppermute x12, starting transfers between devices, other_core(): return lax.ppermute(value, 'mp', [(i, i ^ 1) for i in range(count)])  2.42 us
  transfers between devices with their start and end apart: 26, of which 8 were waited for; matrix products, arithmetic and copies ran while one was open for 1% of the time, Pallas kernels for 1%

profile of v5, /device:TPU:0, one launch (start us, length us, event | category | flops | bytes accessed | tf_op | source)
XLA Modules:
  0.0 85.5 jit_solution(12356098948842077537)
XLA Ops:
  0.6 0.9 %copy-done = bf16[128,512]{1,0:T(8,128)(2,1)S(1)} copy-done((bf16[128,512]{1,0:T(8,128)(2,1)S(1)}, bf16[128,512]{1,0:T(8,128)(2,1)}, u32[]{:S(2)}) %copy-start) | copy-done | bytes 131096
  1.5 0.7 copy-done.4
  2.2 0.7 copy-done.5
  2.9 3.1 %collective-permute-start = (bf16[1,136,512]{2,1,0:T(8,128)(2,1)S(1)}, bf16[1,136,512]{2,1,0:T(8,128)(2,1)S(1)}, u32[]{:S(2)}, u32[]{:S(2)}) collective-permute-start(bf16[1,136,512]{2,1,0:T(8,128)(2,1)S(1)} %shard_map.104.refs_0_), channel_id=1, source_target_pairs={{0,4},{4,8},{8,12},{12,0},{1,5},{5,9},{9,13},{13,1},{2,6},{6,10},{... | collective-permute-start | bytes 417800 | tf_op jit(solution)/shard_map/ppermute | solution.py:55
  6.0 2.1 %collective-permute-start.11 = (bf16[1,136,512]{2,1,0:T(8,128)(2,1)S(1)}, bf16[1,136,512]{2,1,0:T(8,128)(2,1)S(1)}, u32[]{:S(2)}, u32[]{:S(2)}) collective-permute-start(bf16[1,136,512]{2,1,0:T(8,128)(2,1)S(1)} %shard_map.104.refs_0_), channel_id=1, source_target_pairs={{0,12},{4,0},{8,4},{12,8},{1,13},{5,1},{9,5},{13,9},{2,14},{6,2},{... | collective-permute-start | bytes 417800 | tf_op jit(solution)/shard_map/ppermute | solution.py:55
  8.1 1.6 %collective-permute-start.2 = (bf16[1,136,512]{2,1,0:T(8,128)(2,1)S(1)}, bf16[1,136,512]{2,1,0:T(8,128)(2,1)S(1)}, u32[]{:S(2)}, u32[]{:S(2)}) collective-permute-start(bf16[1,136,512]{2,1,0:T(8,128)(2,1)S(1)} %shard_map.104.refs_0_), channel_id=1, source_target_pairs={{0,2},{1,3},{2,0},{3,1},{4,6},{5,7},{6,4},{7,5},{8,10},{9,11},{10,... | collective-permute-start | bytes 417800 | tf_op jit(solution)/shard_map/ppermute | solution.py:60
  9.7 2.8 %collective-permute-done.refs_4_ = bf16[1,136,512]{2,1,0:T(8,128)(2,1)S(1)} collective-permute-done((bf16[1,136,512]{2,1,0:T(8,128)(2,1)S(1)}, bf16[1,136,512]{2,1,0:T(8,128)(2,1)S(1)}, u32[]{:S(2)}, u32[]{:S(2)}) %collective-permute-start) | collective-permute-done | bytes 139296 | tf_op jit(solution)/shard_map/ppermute | solution.py:55
  12.6 1.7 %collective-permute-start.5 = (bf16[1,136,512]{2,1,0:T(8,128)(2,1)S(1)}, bf16[1,136,512]{2,1,0:T(8,128)(2,1)S(1)}, u32[]{:S(2)}, u32[]{:S(2)}) collective-permute-start(bf16[1,136,512]{2,1,0:T(8,128)(2,1)S(1)} %collective-permute-done.refs_4_), channel_id=1, source_target_pairs={{0,2},{1,3},{2,0},{3,1},{4,6},{5,7},{6,4},{7,5},{8,10},{9,11},{10,... | collective-permute-start | bytes 417800 | tf_op jit(solution)/shard_map/ppermute | solution.py:60
  14.3 1.3 %collective-permute-start.13 = (bf16[1,136,512]{2,1,0:T(8,128)(2,1)S(1)}, bf16[1,136,512]{2,1,0:T(8,128)(2,1)S(1)}, u32[]{:S(2)}, u32[]{:S(2)}) collective-permute-start(bf16[1,136,512]{2,1,0:T(8,128)(2,1)S(1)} %collective-permute-done.11.refs_12_), channel_id=1, source_target_pairs={{0,2},{1,3},{2,0},{3,1},{4,6},{5,7},{6,4},{7,5},{8,10},{9,11},{10,... | collective-permute-start | bytes 417800 | tf_op jit(solution)/shard_map/ppermute | solution.py:60
  15.9 3.6 %collective-permute-done.7.refs_8_ = bf16[1,136,512]{2,1,0:T(8,128)(2,1)S(1)} collective-permute-done((bf16[1,136,512]{2,1,0:T(8,128)(2,1)S(1)}, bf16[1,136,512]{2,1,0:T(8,128)(2,1)S(1)}, u32[]{:S(2)}, u32[]{:S(2)}) %collective-permute-start.7) | collective-permute-done | bytes 139296 | tf_op jit(solution)/shard_map/ppermute | solution.py:55
  19.4 1.7 %collective-permute-start.9 = (bf16[1,136,512]{2,1,0:T(8,128)(2,1)S(1)}, bf16[1,136,512]{2,1,0:T(8,128)(2,1)S(1)}, u32[]{:S(2)}, u32[]{:S(2)}) collective-permute-start(bf16[1,136,512]{2,1,0:T(8,128)(2,1)S(1)} %collective-permute-done.7.refs_8_), channel_id=1, source_target_pairs={{0,2},{1,3},{2,0},{3,1},{4,6},{5,7},{6,4},{7,5},{8,10},{9,11},{10,... | collective-permute-start | bytes 417800 | tf_op jit(solution)/shard_map/ppermute | solution.py:60
  21.1 0.5 collective-permute-start.8
  21.7 0.4 collective-permute-start.14
  22.2 2.3 %collective-permute-done.9.refs_10_ = bf16[1,136,512]{2,1,0:T(8,128)(2,1)S(1)} collective-permute-done((bf16[1,136,512]{2,1,0:T(8,128)(2,1)S(1)}, bf16[1,136,512]{2,1,0:T(8,128)(2,1)S(1)}, u32[]{:S(2)}, u32[]{:S(2)}) %collective-permute-start.9) | collective-permute-done | bytes 139296 | tf_op jit(solution)/shard_map/ppermute | solution.py:60
  24.5 0.8 copy-done.2
  25.3 0.7 copy-done.6
  26.0 0.7 copy-done.7
  26.7 0.8 shard_map.105.pages_ref
  27.5 0.7 copy-done.3
  28.2 27.9 %shard_map.106 = (bf16[2,1,128,512]{3,2,1,0:T(8,128)(2,1)S(1)}, bf16[2,1,128,512]{3,2,1,0:T(8,128)(2,1)S(1)}, bf16[2,1,128,512]{3,2,1,0:T(8,128)(2,1)S(1)}, bf16...) custom-call(f32[1,2048]{1,0:T(1,128)S(1)} %bitcast.48, ...), custom_call_target="tpu_custom_call" | custom-call | flops 4831838208 | bytes 75497472 | tf_op jit(solution)/shard_map/pallas_call | solution.py:318
  56.2 0.6 collective-permute-start.23
  56.8 0.4 collective-permute-start.19
  57.4 0.6 collective-permute-done.23
  58.0 1.8 %collective-permute-start.24 = (bf16[1,128,512]{2,1,0:T(8,128)(2,1)S(1)}, bf16[1,128,512]{2,1,0:T(8,128)(2,1)S(1)}, u32[]{:S(2)}, u32[]{:S(2)}) collective-permute-start(bf16[1,128,512]{2,1,0:T(8,128)(2,1)S(1)} %slice_bitcast_fusion), channel_id=1, source_target_pairs={{0,2},{1,3},{2,0},{3,1},{4,6},{5,7},{6,4},{7,5},{8,10},{9,11},{10,... | collective-permute-start | bytes 393224 | tf_op jit(solution)/shard_map/ppermute | solution.py:60
  60.4 1.8 %collective-permute-start.20 = (bf16[1,128,512]{2,1,0:T(8,128)(2,1)S(1)}, bf16[1,128,512]{2,1,0:T(8,128)(2,1)S(1)}, u32[]{:S(2)}, u32[]{:S(2)}) collective-permute-start(bf16[1,128,512]{2,1,0:T(8,128)(2,1)S(1)} %slice_bitcast_fusion.2), channel_id=1, source_target_pairs={{0,2},{1,3},{2,0},{3,1},{4,6},{5,7},{6,4},{7,5},{8,10},{9,11},{10,... | collective-permute-start | bytes 393224 | tf_op jit(solution)/shard_map/ppermute | solution.py:60
  62.7 7.4 %collective-permute-done.20 = bf16[1,128,512]{2,1,0:T(8,128)(2,1)S(1)} collective-permute-done((bf16[1,128,512]{2,1,0:T(8,128)(2,1)S(1)}, bf16[1,128,512]{2,1,0:T(8,128)(2,1)S(1)}, u32[]{:S(2)}, u32[]{:S(2)}) %collective-permute-start.20) | collective-permute-done | bytes 131104 | tf_op jit(solution)/shard_map/ppermute | solution.py:60
  70.1 3.0 %collective-permute-start.21 = (bf16[152,512]{1,0:T(8,128)(2,1)S(1)}, bf16[152,512]{1,0:T(8,128)(2,1)S(1)}, u32[]{:S(2)}, u32[]{:S(2)}) collective-permute-start(bf16[152,512]{1,0:T(8,128)(2,1)S(1)} %pad_maximum_fusion.1), channel_id=1, source_target_pairs={{0,12},{4,0},{8,4},{12,8},{1,13},{5,1},{9,5},{13,9},{2,14},{6,2},{... | collective-permute-start | bytes 466952 | tf_op jit(solution)/shard_map/ppermute | solution.py:55
  73.2 4.0 %collective-permute-done.21 = bf16[152,512]{1,0:T(8,128)(2,1)S(1)} collective-permute-done((bf16[152,512]{1,0:T(8,128)(2,1)S(1)}, bf16[152,512]{1,0:T(8,128)(2,1)S(1)}, u32[]{:S(2)}, u32[]{:S(2)}) %collective-permute-start.21) | collective-permute-done | bytes 155680 | tf_op jit(solution)/shard_map/ppermute | solution.py:55
  77.3 4.4 %collective-permute-start.22 = (bf16[176,512]{1,0:T(8,128)(2,1)S(1)}, bf16[176,512]{1,0:T(8,128)(2,1)S(1)}, u32[]{:S(2)}, u32[]{:S(2)}) collective-permute-start(bf16[176,512]{1,0:T(8,128)(2,1)S(1)} %pad_maximum_fusion), channel_id=1, source_target_pairs={{0,12},{4,0},{8,4},{12,8},{1,13},{5,1},{9,5},{13,9},{2,14},{6,2},{... | collective-permute-start | bytes 540680 | tf_op jit(solution)/shard_map/ppermute | solution.py:55
  81.7 1.6 %collective-permute-done.25.up_ref = bf16[152,512]{1,0:T(8,128)(2,1)S(1)} collective-permute-done((bf16[152,512]{1,0:T(8,128)(2,1)S(1)}, bf16[152,512]{1,0:T(8,128)(2,1)S(1)}, u32[]{:S(2)}, u32[]{:S(2)}) %collective-permute-start.25) | collective-permute-done | bytes 155680 | tf_op jit(solution)/shard_map/ppermute | solution.py:55
  83.3 1.4 %collective-permute-done.22.down_ref = bf16[176,512]{1,0:T(8,128)(2,1)S(1)} collective-permute-done((bf16[176,512]{1,0:T(8,128)(2,1)S(1)}, bf16[176,512]{1,0:T(8,128)(2,1)S(1)}, u32[]{:S(2)}, u32[]{:S(2)}) %collective-permute-start.22) | collective-permute-done | bytes 180256 | tf_op jit(solution)/shard_map/ppermute | solution.py:55
  84.7 0.8 shard_map.107
  (57 shorter events, 2.0 us)
Async XLA Ops:
  0.6 0.9 %copy-start = (bf16[128,512]{1,0:T(8,128)(2,1)S(1)}, bf16[128,512]{1,0:T(8,128)(2,1)}, u32[]{:S(2)}) copy-start(bf16[128,512]{1,0:T(8,128)(2,1)} %hidden_ref.3) | copy-start | bytes 393220
  1.5 0.7 copy-start.4
  2.2 0.7 copy-start.5
  2.9 81.8 %copy-start.1 = (bf16[128,512]{1,0:T(8,128)(2,1)S(1)}, bf16[128,512]{1,0:T(8,128)(2,1)}, u32[]{:S(2)}) copy-start(bf16[128,512]{1,0:T(8,128)(2,1)} %hidden_ref.3) | copy-start | bytes 393220
  2.9 9.6 %collective-permute-start = (bf16[1,136,512]{2,1,0:T(8,128)(2,1)S(1)}, bf16[1,136,512]{2,1,0:T(8,128)(2,1)S(1)}, u32[]{:S(2)}, u32[]{:S(2)}) collective-permute-start(bf16[1,136,512]{2,1,0:T(8,128)(2,1)S(1)} %shard_map.104.refs_0_), channel_id=1, source_target_pairs={{0,4},{4,8},{8,12},{12,0},{1,5},{5,9},{9,13},{13,1},{2,6},{6,10},{... | collective-permute-start | bytes 417800 | tf_op jit(solution)/shard_map/ppermute | solution.py:55
  6.0 8.3 %collective-permute-start.11 = (bf16[1,136,512]{2,1,0:T(8,128)(2,1)S(1)}, bf16[1,136,512]{2,1,0:T(8,128)(2,1)S(1)}, u32[]{:S(2)}, u32[]{:S(2)}) collective-permute-start(bf16[1,136,512]{2,1,0:T(8,128)(2,1)S(1)} %shard_map.104.refs_0_), channel_id=1, source_target_pairs={{0,12},{4,0},{8,4},{12,8},{1,13},{5,1},{9,5},{13,9},{2,14},{6,2},{... | collective-permute-start | bytes 417800 | tf_op jit(solution)/shard_map/ppermute | solution.py:55
  8.1 6.2 %collective-permute-start.2 = (bf16[1,136,512]{2,1,0:T(8,128)(2,1)S(1)}, bf16[1,136,512]{2,1,0:T(8,128)(2,1)S(1)}, u32[]{:S(2)}, u32[]{:S(2)}) collective-permute-start(bf16[1,136,512]{2,1,0:T(8,128)(2,1)S(1)} %shard_map.104.refs_0_), channel_id=1, source_target_pairs={{0,2},{1,3},{2,0},{3,1},{4,6},{5,7},{6,4},{7,5},{8,10},{9,11},{10,... | collective-permute-start | bytes 417800 | tf_op jit(solution)/shard_map/ppermute | solution.py:60
  9.7 5.9 %collective-permute-start.1 = (bf16[1,136,512]{2,1,0:T(8,128)(2,1)S(1)}, bf16[1,136,512]{2,1,0:T(8,128)(2,1)S(1)}, u32[]{:S(2)}, u32[]{:S(2)}) collective-permute-start(bf16[1,136,512]{2,1,0:T(8,128)(2,1)S(1)} %shard_map.104.refs_0_), channel_id=1, source_target_pairs={{0,1},{1,0},{2,3},{3,2},{4,5},{5,4},{6,7},{7,6},{8,9},{9,8},{10,11... | collective-permute-start | bytes 417800 | tf_op jit(solution)/shard_map/ppermute | solution.py:65
  12.6 6.9 %collective-permute-start.7 = (bf16[1,136,512]{2,1,0:T(8,128)(2,1)S(1)}, bf16[1,136,512]{2,1,0:T(8,128)(2,1)S(1)}, u32[]{:S(2)}, u32[]{:S(2)}) collective-permute-start(bf16[1,136,512]{2,1,0:T(8,128)(2,1)S(1)} %collective-permute-done.refs_4_), channel_id=1, source_target_pairs={{0,4},{4,8},{8,12},{12,0},{1,5},{5,9},{9,13},{13,1},{2,6},{6,10},{... | collective-permute-start | bytes 417800 | tf_op jit(solution)/shard_map/ppermute | solution.py:55
  12.6 8.6 %collective-permute-start.5 = (bf16[1,136,512]{2,1,0:T(8,128)(2,1)S(1)}, bf16[1,136,512]{2,1,0:T(8,128)(2,1)S(1)}, u32[]{:S(2)}, u32[]{:S(2)}) collective-permute-start(bf16[1,136,512]{2,1,0:T(8,128)(2,1)S(1)} %collective-permute-done.refs_4_), channel_id=1, source_target_pairs={{0,2},{1,3},{2,0},{3,1},{4,6},{5,7},{6,4},{7,5},{8,10},{9,11},{10,... | collective-permute-start | bytes 417800 | tf_op jit(solution)/shard_map/ppermute | solution.py:60
  14.3 6.9 %collective-permute-start.4 = (bf16[1,136,512]{2,1,0:T(8,128)(2,1)S(1)}, bf16[1,136,512]{2,1,0:T(8,128)(2,1)S(1)}, u32[]{:S(2)}, u32[]{:S(2)}) collective-permute-start(bf16[1,136,512]{2,1,0:T(8,128)(2,1)S(1)} %collective-permute-done.refs_4_), channel_id=1, source_target_pairs={{0,1},{1,0},{2,3},{3,2},{4,5},{5,4},{6,7},{7,6},{8,9},{9,8},{10,11... | collective-permute-start | bytes 417800 | tf_op jit(solution)/shard_map/ppermute | solution.py:65
  14.3 7.4 %collective-permute-start.13 = (bf16[1,136,512]{2,1,0:T(8,128)(2,1)S(1)}, bf16[1,136,512]{2,1,0:T(8,128)(2,1)S(1)}, u32[]{:S(2)}, u32[]{:S(2)}) collective-permute-start(bf16[1,136,512]{2,1,0:T(8,128)(2,1)S(1)} %collective-permute-done.11.refs_12_), channel_id=1, source_target_pairs={{0,2},{1,3},{2,0},{3,1},{4,6},{5,7},{6,4},{7,5},{8,10},{9,11},{10,... | collective-permute-start | bytes 417800 | tf_op jit(solution)/shard_map/ppermute | solution.py:60
  15.6 6.1 %collective-permute-start.12 = (bf16[1,136,512]{2,1,0:T(8,128)(2,1)S(1)}, bf16[1,136,512]{2,1,0:T(8,128)(2,1)S(1)}, u32[]{:S(2)}, u32[]{:S(2)}) collective-permute-start(bf16[1,136,512]{2,1,0:T(8,128)(2,1)S(1)} %collective-permute-done.11.refs_12_), channel_id=1, source_target_pairs={{0,1},{1,0},{2,3},{3,2},{4,5},{5,4},{6,7},{7,6},{8,9},{9,8},{10,11... | collective-permute-start | bytes 417800 | tf_op jit(solution)/shard_map/ppermute | solution.py:65
  19.4 5.1 %collective-permute-start.9 = (bf16[1,136,512]{2,1,0:T(8,128)(2,1)S(1)}, bf16[1,136,512]{2,1,0:T(8,128)(2,1)S(1)}, u32[]{:S(2)}, u32[]{:S(2)}) collective-permute-start(bf16[1,136,512]{2,1,0:T(8,128)(2,1)S(1)} %collective-permute-done.7.refs_8_), channel_id=1, source_target_pairs={{0,2},{1,3},{2,0},{3,1},{4,6},{5,7},{6,4},{7,5},{8,10},{9,11},{10,... | collective-permute-start | bytes 417800 | tf_op jit(solution)/shard_map/ppermute | solution.py:60
  21.1 6.4 %collective-permute-start.3 = (bf16[1,136,512]{2,1,0:T(8,128)(2,1)S(1)}, bf16[1,136,512]{2,1,0:T(8,128)(2,1)S(1)}, u32[]{:S(2)}, u32[]{:S(2)}) collective-permute-start(bf16[1,136,512]{2,1,0:T(8,128)(2,1)S(1)} %collective-permute-done.2.refs_2_), channel_id=1, source_target_pairs={{0,1},{1,0},{2,3},{3,2},{4,5},{5,4},{6,7},{7,6},{8,9},{9,8},{10,11... | collective-permute-start | bytes 417800 | tf_op jit(solution)/shard_map/ppermute | solution.py:65
  21.1 6.4 %collective-permute-start.8 = (bf16[1,136,512]{2,1,0:T(8,128)(2,1)S(1)}, bf16[1,136,512]{2,1,0:T(8,128)(2,1)S(1)}, u32[]{:S(2)}, u32[]{:S(2)}) collective-permute-start(bf16[1,136,512]{2,1,0:T(8,128)(2,1)S(1)} %collective-permute-done.7.refs_8_), channel_id=1, source_target_pairs={{0,1},{1,0},{2,3},{3,2},{4,5},{5,4},{6,7},{7,6},{8,9},{9,8},{10,11... | collective-permute-start | bytes 417800 | tf_op jit(solution)/shard_map/ppermute | solution.py:65
  21.6 5.9 %collective-permute-start.6 = (bf16[1,136,512]{2,1,0:T(8,128)(2,1)S(1)}, bf16[1,136,512]{2,1,0:T(8,128)(2,1)S(1)}, u32[]{:S(2)}, u32[]{:S(2)}) collective-permute-start(bf16[1,136,512]{2,1,0:T(8,128)(2,1)S(1)} %collective-permute-done.5.refs_6_), channel_id=1, source_target_pairs={{0,1},{1,0},{2,3},{3,2},{4,5},{5,4},{6,7},{7,6},{8,9},{9,8},{10,11... | collective-permute-start | bytes 417800 | tf_op jit(solution)/shard_map/ppermute | solution.py:65
  21.7 5.8 %collective-permute-start.14 = (bf16[1,136,512]{2,1,0:T(8,128)(2,1)S(1)}, bf16[1,136,512]{2,1,0:T(8,128)(2,1)S(1)}, u32[]{:S(2)}, u32[]{:S(2)}) collective-permute-start(bf16[1,136,512]{2,1,0:T(8,128)(2,1)S(1)} %collective-permute-done.13.refs_14_), channel_id=1, source_target_pairs={{0,1},{1,0},{2,3},{3,2},{4,5},{5,4},{6,7},{7,6},{8,9},{9,8},{10,11... | collective-permute-start | bytes 417800 | tf_op jit(solution)/shard_map/ppermute | solution.py:65
  24.5 3.1 %collective-permute-start.10 = (bf16[1,136,512]{2,1,0:T(8,128)(2,1)S(1)}, bf16[1,136,512]{2,1,0:T(8,128)(2,1)S(1)}, u32[]{:S(2)}, u32[]{:S(2)}) collective-permute-start(bf16[1,136,512]{2,1,0:T(8,128)(2,1)S(1)} %collective-permute-done.9.refs_10_), channel_id=1, source_target_pairs={{0,1},{1,0},{2,3},{3,2},{4,5},{5,4},{6,7},{7,6},{8,9},{9,8},{10,11... | collective-permute-start | bytes 417800 | tf_op jit(solution)/shard_map/ppermute | solution.py:65
  24.5 0.8 copy-start.2
  27.5 0.7 copy-start.3
  56.2 1.7 %collective-permute-start.23 = (bf16[2,1,128,512]{3,2,1,0:T(8,128)(2,1)S(1)}, bf16[2,1,128,512]{3,2,1,0:T(8,128)(2,1)S(1)}, u32[]{:S(2)}, u32[]{:S(2)}) collective-permute-start(bf16[2,1,128,512]{3,2,1,0:T(8,128)(2,1)S(1)} %get-tuple-element.19), channel_id=1, source_target_pairs={{0,1},{1,0},{2,3},{3,2},{4,5},{5,4},{6,7},{7,6},{8,9},{9,8},{10,11... | collective-permute-start | bytes 786440 | tf_op jit(solution)/shard_map/ppermute | solution.py:65
  56.8 3.0 %collective-permute-start.17 = (bf16[2,1,128,512]{3,2,1,0:T(8,128)(2,1)S(1)}, bf16[2,1,128,512]{3,2,1,0:T(8,128)(2,1)S(1)}, u32[]{:S(2)}, u32[]{:S(2)}) collective-permute-start(bf16[2,1,128,512]{3,2,1,0:T(8,128)(2,1)S(1)} %get-tuple-element.15), channel_id=1, source_target_pairs={{0,1},{1,0},{2,3},{3,2},{4,5},{5,4},{6,7},{7,6},{8,9},{9,8},{10,11... | collective-permute-start | bytes 786440 | tf_op jit(solution)/shard_map/ppermute | solution.py:65
  56.8 3.4 %collective-permute-start.19 = (bf16[2,1,128,512]{3,2,1,0:T(8,128)(2,1)S(1)}, bf16[2,1,128,512]{3,2,1,0:T(8,128)(2,1)S(1)}, u32[]{:S(2)}, u32[]{:S(2)}) collective-permute-start(bf16[2,1,128,512]{3,2,1,0:T(8,128)(2,1)S(1)} %get-tuple-element.17), channel_id=1, source_target_pairs={{0,1},{1,0},{2,3},{3,2},{4,5},{5,4},{6,7},{7,6},{8,9},{9,8},{10,11... | collective-permute-start | bytes 786440 | tf_op jit(solution)/shard_map/ppermute | solution.py:65
  57.3 4.9 %collective-permute-start.15 = (bf16[2,1,128,512]{3,2,1,0:T(8,128)(2,1)S(1)}, bf16[2,1,128,512]{3,2,1,0:T(8,128)(2,1)S(1)}, u32[]{:S(2)}, u32[]{:S(2)}) collective-permute-start(bf16[2,1,128,512]{3,2,1,0:T(8,128)(2,1)S(1)} %get-tuple-element.13), channel_id=1, source_target_pairs={{0,1},{1,0},{2,3},{3,2},{4,5},{5,4},{6,7},{7,6},{8,9},{9,8},{10,11... | collective-permute-start | bytes 786440 | tf_op jit(solution)/shard_map/ppermute | solution.py:65
  58.0 15.1 %collective-permute-start.24 = (bf16[1,128,512]{2,1,0:T(8,128)(2,1)S(1)}, bf16[1,128,512]{2,1,0:T(8,128)(2,1)S(1)}, u32[]{:S(2)}, u32[]{:S(2)}) collective-permute-start(bf16[1,128,512]{2,1,0:T(8,128)(2,1)S(1)} %slice_bitcast_fusion), channel_id=1, source_target_pairs={{0,2},{1,3},{2,0},{3,1},{4,6},{5,7},{6,4},{7,5},{8,10},{9,11},{10,... | collective-permute-start | bytes 393224 | tf_op jit(solution)/shard_map/ppermute | solution.py:60
  59.9 13.3 %collective-permute-start.18 = (bf16[1,128,512]{2,1,0:T(8,128)(2,1)S(1)}, bf16[1,128,512]{2,1,0:T(8,128)(2,1)S(1)}, u32[]{:S(2)}, u32[]{:S(2)}) collective-permute-start(bf16[1,128,512]{2,1,0:T(8,128)(2,1)S(1)} %slice_bitcast_fusion.4), channel_id=1, source_target_pairs={{0,2},{1,3},{2,0},{3,1},{4,6},{5,7},{6,4},{7,5},{8,10},{9,11},{10,... | collective-permute-start | bytes 393224 | tf_op jit(solution)/shard_map/ppermute | solution.py:60
  60.4 9.6 %collective-permute-start.20 = (bf16[1,128,512]{2,1,0:T(8,128)(2,1)S(1)}, bf16[1,128,512]{2,1,0:T(8,128)(2,1)S(1)}, u32[]{:S(2)}, u32[]{:S(2)}) collective-permute-start(bf16[1,128,512]{2,1,0:T(8,128)(2,1)S(1)} %slice_bitcast_fusion.2), channel_id=1, source_target_pairs={{0,2},{1,3},{2,0},{3,1},{4,6},{5,7},{6,4},{7,5},{8,10},{9,11},{10,... | collective-permute-start | bytes 393224 | tf_op jit(solution)/shard_map/ppermute | solution.py:60
  62.3 19.4 %collective-permute-start.16 = (bf16[1,128,512]{2,1,0:T(8,128)(2,1)S(1)}, bf16[1,128,512]{2,1,0:T(8,128)(2,1)S(1)}, u32[]{:S(2)}, u32[]{:S(2)}) collective-permute-start(bf16[1,128,512]{2,1,0:T(8,128)(2,1)S(1)} %slice_bitcast_fusion.6), channel_id=1, source_target_pairs={{0,2},{1,3},{2,0},{3,1},{4,6},{5,7},{6,4},{7,5},{8,10},{9,11},{10,... | collective-permute-start | bytes 393224 | tf_op jit(solution)/shard_map/ppermute | solution.py:60
  70.1 7.2 %collective-permute-start.21 = (bf16[152,512]{1,0:T(8,128)(2,1)S(1)}, bf16[152,512]{1,0:T(8,128)(2,1)S(1)}, u32[]{:S(2)}, u32[]{:S(2)}) collective-permute-start(bf16[152,512]{1,0:T(8,128)(2,1)S(1)} %pad_maximum_fusion.1), channel_id=1, source_target_pairs={{0,12},{4,0},{8,4},{12,8},{1,13},{5,1},{9,5},{13,9},{2,14},{6,2},{... | collective-permute-start | bytes 466952 | tf_op jit(solution)/shard_map/ppermute | solution.py:55
  73.1 10.2 %collective-permute-start.25 = (bf16[152,512]{1,0:T(8,128)(2,1)S(1)}, bf16[152,512]{1,0:T(8,128)(2,1)S(1)}, u32[]{:S(2)}, u32[]{:S(2)}) collective-permute-start(bf16[152,512]{1,0:T(8,128)(2,1)S(1)} %pad_maximum_fusion.2), channel_id=1, source_target_pairs={{0,4},{4,8},{8,12},{12,0},{1,5},{5,9},{9,13},{13,1},{2,6},{6,10},{... | collective-permute-start | bytes 466952 | tf_op jit(solution)/shard_map/ppermute | solution.py:55
  77.3 7.4 %collective-permute-start.22 = (bf16[176,512]{1,0:T(8,128)(2,1)S(1)}, bf16[176,512]{1,0:T(8,128)(2,1)S(1)}, u32[]{:S(2)}, u32[]{:S(2)}) collective-permute-start(bf16[176,512]{1,0:T(8,128)(2,1)S(1)} %pad_maximum_fusion), channel_id=1, source_target_pairs={{0,12},{4,0},{8,4},{12,8},{1,13},{5,1},{9,5},{13,9},{2,14},{6,2},{... | collective-permute-start | bytes 540680 | tf_op jit(solution)/shard_map/ppermute | solution.py:55
  (2 other events, 1.4 us)

commit v6 on v5

--- a/solution.py
+++ b/solution.py
@@ -14,10 +14,12 @@
 SEND_CAP = 40
 CORES = 2
 HOP_NODES = 4
+RETURNS = ((2,), (1, 3), (0,))
+HOP_CHIPS = 2
 PAGE_FOLD = 24
 SMALL_VMEM = 4 * 1024 * 1024
-WEIGHT_SLOTS = 3
-EXPERT_VMEM = 44 * 1024 * 1024
+WEIGHT_SLOTS = 2
+EXPERT_VMEM = 32 * 1024 * 1024
 
 epsilon = 1e-06
 
@@ -65,31 +67,49 @@
     return lax.ppermute(value, "mp", [(i, i ^ 1) for i in range(count)])
 
 
-def pack_kernel(hidden_ref, routes_ref, gates_ref, out_ref):
+def pack_kernel(hidden_ref, routes_ref, gates_ref, out_ref, route_buf, gate_buf, sems):
     tok_node = hidden_ref.shape[0]
-    out_ref[0, :tok_node, :] = hidden_ref[...]
-    gate = gates_ref[...]
+    copies = [
+        pltpu.make_async_copy(routes_ref, route_buf, sems.at[0]),
+        pltpu.make_async_copy(gates_ref, gate_buf, sems.at[1]),
+        pltpu.make_async_copy(hidden_ref, out_ref.at[0, pl.ds(0, tok_node), :], sems.at[2]),
+    ]
+    for copy in copies:
+        copy.start()
+    copies[0].wait()
+    copies[1].wait()
+    gate = gate_buf[...]
     first = gate.astype(jnp.bfloat16)
     rest = gate - first.astype(jnp.float32)
     second = rest.astype(jnp.bfloat16)
     third = (rest - second.astype(jnp.float32)).astype(jnp.bfloat16)
-    route = routes_ref[...].astype(jnp.float32).astype(jnp.bfloat16)
+    route = route_buf[...].astype(jnp.float32).astype(jnp.bfloat16)
     out_ref[0, tok_node:, :] = jnp.concatenate([route, first, second, third], axis=1)
+    copies[2].wait()
+
+
+def in_hbm(*arrays):
+    return [pltpu.with_memory_space_constraint(array, pltpu.HBM) for array in arrays]
 
 
 def packed(hidden_states, routes, gates):
     tok_node, width = hidden_states.shape
-    vmem = pl.BlockSpec(memory_space=pltpu.VMEM)
+    hbm = pl.BlockSpec(memory_space=pltpu.HBM)
     return pl.pallas_call(
         pack_kernel,
         out_shape=jax.ShapeDtypeStruct((1, tok_node + TOPK, width), jnp.bfloat16),
-        in_specs=[vmem] * 3,
-        out_specs=vmem,
+        in_specs=[hbm] * 3,
+        out_specs=pl.BlockSpec(memory_space=pltpu.VMEM),
+        scratch_shapes=[
+            pltpu.VMEM((TOPK, tok_node), jnp.int32),
+            pltpu.VMEM((TOPK, tok_node), jnp.float32),
+            pltpu.SemaphoreType.DMA((3,)),
+        ],
         compiler_params=pltpu.CompilerParams(vmem_limit_bytes=SMALL_VMEM),
-    )(hidden_states, routes.T, gates.T)
-
-
-def page_kernel(lengths_ref, owners_ref, kv_ref, out_ref):
+    )(*in_hbm(hidden_states, routes.T, gates.T))
+
+
+def write_pages(lengths_ref, owners_ref, kv_ref, out_ref):
     nodes, _, width = out_ref.shape
     tok_node, kv_width = kv_ref.shape
     me = lax.axis_index("dp")
@@ -112,18 +132,82 @@
             ).astype(jnp.bfloat16)
 
 
-def kv_pages(kv_rows, lengths, owners, node_count):
+def expert_copies(gate_up_ref, down_ref, h, gate_up_into, down_into, sems):
+    ff_part = down_into.shape[0]
+    at = pl.ds(pl.multiple_of(h * ff_part, ff_part), ff_part)
+    return (
+        pltpu.make_async_copy(gate_up_ref.at[0, at, :], gate_up_into.at[0], sems.at[0]),
+        pltpu.make_async_copy(gate_up_ref.at[1, at, :], gate_up_into.at[1], sems.at[1]),
+        pltpu.make_async_copy(down_ref.at[at, :], down_into, sems.at[2]),
+    )
+
+
+def fill_kernel(gate_up_ref, down_ref, after_ref, gate_up_out, down_out, sems, *, expert):
+    copies = expert_copies(gate_up_ref, down_ref, expert, gate_up_out, down_out, sems)
+    for copy in copies:
+        copy.start()
+    for copy in copies:
+        copy.wait()
+
+
+def page_fill_kernel(
+    gate_up_ref, down_ref, after_ref, kv_ref, lengths_ref, owners_ref,
+    gate_up_out, down_out, pages_ref,
+    sems, kv_buf, lengths_buf, owners_buf, page_sems, *, expert,
+):
+    small = (
+        pltpu.make_async_copy(kv_ref, kv_buf, page_sems.at[0]),
+        pltpu.make_async_copy(lengths_ref, lengths_buf, page_sems.at[1]),
+        pltpu.make_async_copy(owners_ref, owners_buf, page_sems.at[2]),
+    )
+    copies = expert_copies(gate_up_ref, down_ref, expert, gate_up_out, down_out, sems)
+    for copy in small + copies:
+        copy.start()
+    for copy in small:
+        copy.wait()
+    write_pages(lengths_buf, owners_buf, kv_buf, pages_ref)
+    for copy in copies:
+        copy.wait()
+
+
+def filled(gate_up_weight, down_weight, expert, after, paged=None):
+    width = down_weight.shape[1]
+    ff_part = min(FF, down_weight.shape[0])
+    hbm = pl.BlockSpec(memory_space=pltpu.HBM)
     vmem = pl.BlockSpec(memory_space=pltpu.VMEM)
-    smem = pl.BlockSpec(memory_space=pltpu.SMEM)
+    out_shape = [
+        pltpu.VMEM((2, ff_part, width), down_weight.dtype),
+        pltpu.VMEM((ff_part, width), down_weight.dtype),
+    ]
+    scratch = [pltpu.SemaphoreType.DMA((3,))]
+    operands = [gate_up_weight, down_weight, after]
+    kernel = fill_kernel
+    if paged is not None:
+        kv_rows, lengths, owners = paged
+        kernel = page_fill_kernel
+        operands += in_hbm(kv_rows, lengths, owners)
+        out_shape.append(
+            jax.ShapeDtypeStruct(
+                (lengths.shape[0], PAGE_FOLD, 2 * kv_rows.shape[1]), jnp.bfloat16
+            )
+        )
+        scratch += [
+            pltpu.VMEM(kv_rows.shape, kv_rows.dtype),
+            pltpu.SMEM(lengths.shape, jnp.int32),
+            pltpu.SMEM(owners.shape, jnp.int32),
+            pltpu.SemaphoreType.DMA((3,)),
+        ]
     return pl.pallas_call(
-        page_kernel,
-        out_shape=jax.ShapeDtypeStruct(
-            (node_count, PAGE_FOLD, 2 * kv_rows.shape[1]), jnp.bfloat16
+        functools.partial(kernel, expert=expert),
+        out_shape=out_shape,
+        in_specs=[hbm, hbm, pl.BlockSpec(memory_space=pl.ANY)] + [hbm] * (len(operands) - 3),
+        out_specs=[vmem] * len(out_shape),
+        scratch_shapes=scratch,
+        compiler_params=pltpu.CompilerParams(vmem_limit_bytes=SMALL_VMEM),
+        cost_estimate=pl.CostEstimate(
+            flops=0, bytes_accessed=6 * ff_part * width, transcendentals=0
         ),
-        in_specs=[smem, smem, vmem],
-        out_specs=vmem,
-        compiler_params=pltpu.CompilerParams(vmem_limit_bytes=SMALL_VMEM),
-    )(lengths, owners, kv_rows)
+    )(*operands)
 
 
 def final_kernel(hidden_ref, own_ref, down_ref, up_ref, pages_ref, mixed_ref, cache_ref):
@@ -164,26 +248,29 @@
 
 
 def expert_kernel(
-    gain_ref, gate_up_ref, down_ref, pages_ref, *refs, held, capacity, parts, chips,
+    gain_ref, gate_up_ref, down_ref, *refs, held, capacity, parts, chips, fills,
 ):
+    held_refs, refs = refs[: 2 * fills], refs[2 * fills :]
     block_refs, out_refs = refs[: parts * chips * CORES], refs[parts * chips * CORES :]
-    out_refs, scratch = out_refs[: parts * CORES], out_refs[parts * CORES :]
-    normed_ref, pick_ref, picked_ref, slot_gate_ref, served_ref, gu_buf, down_buf, sems = scratch
+    out_refs, scratch = out_refs[: len(RETURNS) * CORES], out_refs[len(RETURNS) * CORES :]
+    (
+        normed_ref, pick_ref, picked_ref, slot_gate_ref, served_ref, gain_buf, gu_buf, down_buf,
+        sems, gain_sem,
+    ) = scratch
     _, block_rows, width = block_refs[0].shape
     tok_node = block_rows - TOPK
     tokens, model_width = normed_ref.shape
-    slots, ff_part, _ = down_buf.shape
+    slots = down_buf.shape[0]
 
     def fetch(h, slot):
-        at = pl.ds(pl.multiple_of(h * ff_part, ff_part), ff_part)
-        return (
-            pltpu.make_async_copy(gate_up_ref.at[0, at, :], gu_buf.at[slot, 0], sems.at[slot, 0]),
-            pltpu.make_async_copy(gate_up_ref.at[1, at, :], gu_buf.at[slot, 1], sems.at[slot, 1]),
-            pltpu.make_async_copy(down_ref.at[at, :], down_buf.at[slot], sems.at[slot, 2]),
+        return expert_copies(
+            gate_up_ref, down_ref, h, gu_buf.at[slot], down_buf.at[slot], sems.at[slot]
         )
 
-    for h in range(min(slots, held)):
-        for copy in fetch(h, h):
+    gain_copy = pltpu.make_async_copy(gain_ref, gain_buf, gain_sem)
+    gain_copy.start()
+    for slot in range(min(slots, held - fills)):
+        for copy in fetch(fills + slot, slot):
             copy.start()
 
     column = lax.axis_index("mp")
@@ -207,6 +294,7 @@
         for x in range(chips)
     ]
 
+    gain_copy.wait()
     expert = first_expert + lax.broadcasted_iota(jnp.int32, (held, 1), 0)
     named, gate = [], []
     for z in range(parts):
@@ -221,7 +309,7 @@
             for c in range(CORES):
                 wide = blocks[z][x][c][0, :tok_node, :].astype(jnp.float32)
                 normed_ref[at, features[x][c]] = (
-                    wide * inv_scale * gain_ref[:, features[x][c]]
+                    wide * inv_scale * gain_buf[:, features[x][c]]
                 ).astype(jnp.bfloat16)
         choices = blocks[z][0][0][0, tok_node:, :].astype(jnp.float32)
         number = choices[:, :tok_node].astype(jnp.int32)
@@ -265,22 +353,28 @@
             pick_ref[...], normed_ref[:, part], preferred_element_type=jnp.float32
         ).astype(jnp.bfloat16)
 
-    def one_expert(h, carry):
-        slot = lax.rem(h, slots)
-        at = pl.ds(pl.multiple_of(h * capacity, capacity), capacity)
-        for copy in fetch(h, slot):
-            copy.wait()
+    def one_expert(at, gate_up, down):
         picked = picked_ref[at, :]
         along = (((1,), (1,)), ((), ()))
         gate_part = lax.dot_general(
-            picked, gu_buf[slot, 0], along, preferred_element_type=jnp.float32
+            picked, gate_up[0], along, preferred_element_type=jnp.float32
         )
         up_part = lax.dot_general(
-            picked, gu_buf[slot, 1], along, preferred_element_type=jnp.float32
+            picked, gate_up[1], along, preferred_element_type=jnp.float32
         )
         activated = (jax.nn.silu(gate_part) * up_part).astype(jnp.bfloat16)
-        served = jnp.dot(activated, down_buf[slot], preferred_element_type=jnp.float32)
+        served = jnp.dot(activated, down[...], preferred_element_type=jnp.float32)
         served_ref[at, :] = (served * slot_gate_ref[at, :]).astype(jnp.bfloat16)
+
+    for h in range(fills):
+        one_expert(pl.ds(h * capacity, capacity), held_refs[2 * h], held_refs[2 * h + 1])
+
+    def streamed(h, carry):
+        slot = lax.rem(h - fills, slots)
+        for copy in fetch(h, slot):
+            copy.wait()
+        at = pl.ds(pl.multiple_of(h * capacity, capacity), capacity)
+        one_expert(at, gu_buf.at[slot], down_buf.at[slot])
 
         @pl.when(h + slots < held)
         def _():
@@ -289,7 +383,7 @@
 
         return carry
 
-    lax.fori_loop(0, held, one_expert, 0)
+    lax.fori_loop(fills, held, streamed, 0)
 
     back = pick_ref[...].T
     for x in range(chips):
@@ -297,11 +391,14 @@
             summed = jnp.dot(
                 back, served_ref[:, features[x][c]], preferred_element_type=jnp.float32
             ).astype(jnp.bfloat16)
-            for z in range(parts):
-                out_refs[z * CORES + c][x, 0] = summed[z * tok_node : (z + 1) * tok_node, :]
-
-
-def expert_sums(gain, gate_up_weight, down_weight, pages, blocks):
+            for group, members in enumerate(RETURNS):
+                for i, z in enumerate(members):
+                    out_refs[group * CORES + c][x, i] = summed[
+                        z * tok_node : (z + 1) * tok_node, :
+                    ]
+
+
+def expert_sums(gain, gate_up_weight, down_weight, held_weights, blocks):
     parts, chips = len(blocks), len(blocks[0])
     _, block_rows, width = blocks[0][0][0].shape
     tok_node = block_rows - TOPK
@@ -314,24 +411,31 @@
     all_slots = held * capacity
     vmem = pl.BlockSpec(memory_space=pltpu.VMEM)
     hbm = pl.BlockSpec(memory_space=pltpu.HBM)
+    held_weights = [pltpu.with_memory_space_constraint(w, pltpu.VMEM) for w in held_weights]
     flat = [blocks[z][x][c] for z in range(parts) for x in range(chips) for c in range(CORES)]
     sums = pl.pallas_call(
         functools.partial(
-            expert_kernel, held=held, capacity=capacity, parts=parts, chips=chips
+            expert_kernel, held=held, capacity=capacity, parts=parts, chips=chips,
+            fills=len(held_weights) // 2,
         ),
-        out_shape=[jax.ShapeDtypeStruct((chips, 1, tok_node, width), jnp.bfloat16)]
-        * (parts * CORES),
-        in_specs=[vmem, hbm, hbm, pl.BlockSpec(memory_space=pl.ANY)] + [vmem] * len(flat),
-        out_specs=[vmem] * (parts * CORES),
+        out_shape=[
+            jax.ShapeDtypeStruct((chips, len(members), tok_node, width), jnp.bfloat16)
+            for members in RETURNS
+            for _ in range(CORES)
+        ],
+        in_specs=[hbm] * 3 + [vmem] * (len(held_weights) + len(flat)),
+        out_specs=[vmem] * (len(RETURNS) * CORES),
         scratch_shapes=[
             pltpu.VMEM((tokens, model_width), jnp.bfloat16),
             pltpu.VMEM((all_slots, tokens), jnp.bfloat16),
             pltpu.VMEM((all_slots, model_width), jnp.bfloat16),
             pltpu.VMEM((all_slots, 1), jnp.float32),
             pltpu.VMEM((all_slots, model_width), jnp.bfloat16),
+            pltpu.VMEM((1, model_width), jnp.float32),
             pltpu.VMEM((WEIGHT_SLOTS, 2, ff_part, model_width), jnp.bfloat16),
             pltpu.VMEM((WEIGHT_SLOTS, ff_part, model_width), jnp.bfloat16),
             pltpu.SemaphoreType.DMA((WEIGHT_SLOTS, 3)),
+            pltpu.SemaphoreType.DMA(()),
         ],
         compiler_params=pltpu.CompilerParams(vmem_limit_bytes=EXPERT_VMEM),
         cost_estimate=pl.CostEstimate(
@@ -339,8 +443,8 @@
             bytes_accessed=6 * ff_dev * model_width,
             transcendentals=0,
         ),
-    )(gain, gate_up_weight, down_weight, pages, *flat)
-    return [sums[z * CORES : (z + 1) * CORES] for z in range(parts)]
+    )(*in_hbm(gain), gate_up_weight, down_weight, *held_weights, *flat)
+    return [sums[g * CORES : (g + 1) * CORES] for g in range(len(RETURNS))]
 
 
 def added(*values):
@@ -424,25 +528,39 @@
     node_count = lax.axis_size("dp")
     column_count = lax.axis_size("mp")
     chips = column_count // CORES
-    gate_up_weight = pltpu.with_memory_space_constraint(gate_up_weight, pltpu.HBM)
-    down_weight = pltpu.with_memory_space_constraint(down_weight, pltpu.HBM)
+    gate_up_weight, down_weight = in_hbm(gate_up_weight, down_weight)
     block = packed(hidden_states, routes, gates)
 
     by_z = {0: block, 1: shift_dp(block, 1), 3: shift_dp(block, -1)}
+    own_x = [shift_x(block, s) for s in range(1, chips)]
+    *held_a, pages = filled(gate_up_weight, down_weight, 0, block, (kv_rows, lengths, owners))
+    own_core = [other_core(block)]
+    by_z, own_x, own_core, held_a = lax.optimization_barrier((by_z, own_x, own_core, held_a))
     by_z[2] = shift_dp(by_z[1], 1)
-    chip_rows = {z: [by_z[z]] + [shift_x(by_z[z], s) for s in range(1, chips)] for z in by_z}
-    blocks = [
-        [(value, other_core(value)) for value in chip_rows[z]] for z in range(node_count)
+    chip_rows = {z: [by_z[z]] + [shift_x(by_z[z], s) for s in range(1, chips)] for z in (1, 3)}
+    held_b = filled(gate_up_weight, down_weight, 1, by_z[3])
+    by_z[2], chip_rows, held_b = lax.optimization_barrier((by_z[2], chip_rows, held_b))
+    chip_rows[0] = [block] + own_x
+    chip_rows[2] = [by_z[2]] + [shift_x(by_z[2], s) for s in range(1, chips)]
+    own_core += [other_core(value) for value in own_x]
+    blocks = [list(zip(chip_rows[0], own_core))]
+    blocks += [
+        [(value, other_core(value)) for value in chip_rows[z]] for z in range(1, node_count)
     ]
-    kv_rows, _ = lax.optimization_barrier((kv_rows, by_z[1]))
-    pages = kv_pages(kv_rows, lengths, owners, node_count)
-    sums = expert_sums(norm_gain[None, :], gate_up_weight, down_weight, pages, blocks)
-
+    sums = expert_sums(
+        norm_gain[None, :], gate_up_weight, down_weight, [*held_a, *held_b], blocks
+    )
+
+    over = [other_core(send) for _, send in sums]
+    chip_sums = [added(keep, came) for (keep, _), came in zip(sums, over)]
+    came = [shift_x(chip_sum[1], -1) for chip_sum in chip_sums[:2]]
+    first, _ = lax.optimization_barrier((came[0], chip_sums[1]))
+    last, _ = lax.optimization_barrier((chip_sums[2][1], came[1]))
+    came = [first, came[1], shift_x(last, -1)]
     shares = {}
-    for z in (2, 1, 3, 0):
-        keep, send = sums[z]
-        chip_sum = added(keep, other_core(send))
-        shares[z] = added(chip_sum[0], *[shift_x(chip_sum[s], -s) for s in range(1, chips)])[0]
+    for members, chip_sum, extra in zip(RETURNS, chip_sums, came):
+        share = added(chip_sum[0], extra)
+        shares |= {z: share[i] for i, z in enumerate(members)}
     passed = shift_dp(jnp.concatenate([shares[2], pages[2]], axis=0), -1)
     tok_node = hidden_states.shape[0]
     down = jnp.concatenate(
@@ -467,5 +585,6 @@
         P("groups", None),
     )
     out_specs = (P(("groups", "dp"), "mp"), P(("groups", "dp"), "mp"))
-    body = local if mesh.shape["dp"] == HOP_NODES else plain_local
+    hops = mesh.shape["dp"] == HOP_NODES and mesh.shape["mp"] == HOP_CHIPS * CORES
+    body = local if hops else plain_local
     return jax.shard_map(body, mesh=mesh, in_specs=in_specs, out_specs=out_specs, check_vma=False)

time: 85.8 us -> 86.4 us (level)
  Pallas kernels: 29.5 us -> 41.9 us
  local copies, waits for them, and re-layouts: 5.22 us -> 0.06 us
  waiting for transfers between devices: 23.7 us -> 18.7 us
  starting transfers between devices: 25.7 us -> 24.2 us
    pallas_call x1 -> x2, Pallas kernels: 0.79 us -> 7.62 us  [filled(): pl.pallas_call(functools.partial(kernel, expert=expert), out_shape=out_sh...]
    unnamed x16 -> x2, local copies, waits for them, and re-layouts: 5.17 us -> 0.01 us
    pallas_call x1, Pallas kernels: 27.9 us -> 32.6 us  [expert_sums(): pl.pallas_call(functools.partial(expert_kernel, held=held, capacity=capac...]
    ppermute x6, waiting for transfers between devices: 13.4 us -> 8.69 us  [shift_dp(): lax.ppermute(value, 'dp', [(i, (i + shift) % count) for i in range(count)])]
    ppermute x8 -> x7, starting transfers between devices: 10.7 us -> 8.88 us  [shift_x(): lax.ppermute(value, 'mp', [(i, (i + CORES * shift) % count) for i in rang...]
    ppermute x8 -> x7, waiting for transfers between devices: 9.7 us -> 8.22 us  [shift_x(): lax.ppermute(value, 'mp', [(i, (i + CORES * shift) % count) for i in rang...]
    ppermute x12 -> x11, waiting for transfers between devices: 0.59 us -> 1.76 us  [other_core(): return lax.ppermute(value, 'mp', [(i, i ^ 1) for i in range(count)])]
    pallas_call x1, Pallas kernels: 0.02 us -> 0.96 us  [packed(): pl.pallas_call(pack_kernel, out_shape=jax.ShapeDtypeStruct((1, tok_node +...]
  transfers between devices with their start and end apart: 26 -> 24, of which waited for: 8 -> 13; matrix products, arithmetic and copies ran while one was open for 1% -> 1% of each run, Pallas kernels for 1% -> 9%
where the time goes in v6:
time: 86.4 us; the launch traced here: 86.2 us
  Pallas kernels  41.9 us (48%)
  starting transfers between devices  24.2 us (28%)
  waiting for transfers between devices  18.7 us (22%)
    pallas_call x1, Pallas kernels, expert_sums(): pl.pallas_call(functools.partial(expert_kernel, held=held, capacity=capac...  32.6 us
    ppermute x6, starting transfers between devices, shift_dp(): lax.ppermute(value, 'dp', [(i, (i + shift) % count) for i in range(count)])  12.8 us
    ppermute x7, starting transfers between devices, shift_x(): lax.ppermute(value, 'mp', [(i, (i + CORES * shift) % count) for i in rang...  8.88 us
    ppermute x6, waiting for transfers between devices, shift_dp(): lax.ppermute(value, 'dp', [(i, (i + shift) % count) for i in range(count)])  8.69 us
    ppermute x7, waiting for transfers between devices, shift_x(): lax.ppermute(value, 'mp', [(i, (i + CORES * shift) % count) for i in rang...  8.22 us
    pallas_call x2, Pallas kernels, filled(): pl.pallas_call(functools.partial(kernel, expert=expert), out_shape=out_sh...  7.62 us
    ppermute x11, starting transfers between devices, other_core(): return lax.ppermute(value, 'mp', [(i, i ^ 1) for i in range(count)])  2.49 us
    ppermute x11, waiting for transfers between devices, other_core(): return lax.ppermute(value, 'mp', [(i, i ^ 1) for i in range(count)])  1.76 us
  transfers between devices with their start and end apart: 24, of which 13 were waited for; matrix products, arithmetic and copies ran while one was open for 1% of the time, Pallas kernels for 9%

profile of v6, /device:TPU:0, one launch (start us, length us, event | category | flops | bytes accessed | tf_op | source)
XLA Modules:
  0.0 86.2 jit_solution(5801490469304550059)
XLA Ops:
  0.6 1.0 %shard_map.104.after_ref.refs_4_ = bf16[1,136,512]{2,1,0:T(8,128)(2,1)S(1)} custom-call(bf16[128,512]{1,0:T(8,128)(2,1)} %hidden_ref.3, s32[8,128]{1,0:T(8,128)} %bitcast.42, f32[8,128]{1,0:T(8,128)} %bitcast.43), custom_call_target="tpu_custom_call" | custom-call | tf_op jit(solution)/shard_map/pallas_call | solution.py:98
  1.6 3.1 %collective-permute-start = (bf16[1,136,512]{2,1,0:T(8,128)(2,1)S(1)}, bf16[1,136,512]{2,1,0:T(8,128)(2,1)S(1)}, u32[]{:S(2)}, u32[]{:S(2)}) collective-permute-start(bf16[1,136,512]{2,1,0:T(8,128)(2,1)S(1)} %shard_map.104.after_ref.refs_4_), channel_id=1, source_target_pairs={{0,4},{4,8},{8,12},{12,0},{1,5},{5,9},{9,13},{13,1},{2,6},{6,10},{... | collective-permute-start | bytes 417800 | tf_op jit(solution)/shard_map/ppermute | solution.py:57
  4.7 2.1 %collective-permute-start.1 = (bf16[1,136,512]{2,1,0:T(8,128)(2,1)S(1)}, bf16[1,136,512]{2,1,0:T(8,128)(2,1)S(1)}, u32[]{:S(2)}, u32[]{:S(2)}) collective-permute-start(bf16[1,136,512]{2,1,0:T(8,128)(2,1)S(1)} %shard_map.104.after_ref.refs_4_), channel_id=1, source_target_pairs={{0,12},{4,0},{8,4},{12,8},{1,13},{5,1},{9,5},{13,9},{2,14},{6,2},{... | collective-permute-start | bytes 417800 | tf_op jit(solution)/shard_map/ppermute | solution.py:57
  6.8 1.6 %collective-permute-start.2 = (bf16[1,136,512]{2,1,0:T(8,128)(2,1)S(1)}, bf16[1,136,512]{2,1,0:T(8,128)(2,1)S(1)}, u32[]{:S(2)}, u32[]{:S(2)}) collective-permute-start(bf16[1,136,512]{2,1,0:T(8,128)(2,1)S(1)} %shard_map.104.after_ref.refs_4_), channel_id=1, source_target_pairs={{0,2},{1,3},{2,0},{3,1},{4,6},{5,7},{6,4},{7,5},{8,10},{9,11},{10,... | collective-permute-start | bytes 417800 | tf_op jit(solution)/shard_map/ppermute | solution.py:62
  8.4 3.8 %shard_map.105 = (bf16[2,768,2048]{2,1,0:T(8,128)(2,1)S(1)}, bf16[768,2048]{1,0:T(8,128)(2,1)S(1)}, bf16[4,24,512]{2,1,0:T(8,128)(2,1)S(1)}) custom-call(bf16[2,6144,2048]{2,1,0:T(8,128)(2,1)} %gate_up_ref.5, bf16[6144,2048]{1,0:T(8,128)(2,1)} %down_ref.5, bf16[1,136,512]{2,1,0:T(8,128)(2,1)S(1)} %shard_map.104.after_ref.refs_4_, bf16[128,256]{1,0:T(8,128)(2,1)} %kv_ref.1, ...), custom_call_target="tpu_custom_call" | custom-call | bytes 9437184 | tf_op jit(solution)/shard_map/pallas_call | solution.py:200
  12.3 0.5 collective-permute-done.1.after_ref.refs_16_
  12.8 1.1 %collective-permute-start.4 = (bf16[1,136,512]{2,1,0:T(8,128)(2,1)S(1)}, bf16[1,136,512]{2,1,0:T(8,128)(2,1)S(1)}, u32[]{:S(2)}, u32[]{:S(2)}) collective-permute-start(bf16[1,136,512]{2,1,0:T(8,128)(2,1)S(1)} %collective-permute-done.refs_8_), channel_id=1, source_target_pairs={{0,4},{4,8},{8,12},{12,0},{1,5},{5,9},{9,13},{13,1},{2,6},{6,10},{... | collective-permute-start | bytes 417800 | tf_op jit(solution)/shard_map/ppermute | solution.py:57
  13.9 1.5 %collective-permute-start.5 = (bf16[1,136,512]{2,1,0:T(8,128)(2,1)S(1)}, bf16[1,136,512]{2,1,0:T(8,128)(2,1)S(1)}, u32[]{:S(2)}, u32[]{:S(2)}) collective-permute-start(bf16[1,136,512]{2,1,0:T(8,128)(2,1)S(1)} %collective-permute-done.refs_8_), channel_id=1, source_target_pairs={{0,2},{1,3},{2,0},{3,1},{4,6},{5,7},{6,4},{7,5},{8,10},{9,11},{10,... | collective-permute-start | bytes 417800 | tf_op jit(solution)/shard_map/ppermute | solution.py:62
  15.4 0.5 collective-permute-start.6
  16.0 3.8 %shard_map.106 = (bf16[2,768,2048]{2,1,0:T(8,128)(2,1)S(1)}, bf16[768,2048]{1,0:T(8,128)(2,1)S(1)}) custom-call(bf16[2,6144,2048]{2,1,0:T(8,128)(2,1)} %gate_up_ref.5, bf16[6144,2048]{1,0:T(8,128)(2,1)} %down_ref.5, bf16[1,136,512]{2,1,0:T(8,128)(2,1)S(1)} %collective-permute-done.1.after_ref.refs_16_), custom_call_target="tpu_custom_call" | custom-call | bytes 9437184 | tf_op jit(solution)/shard_map/pallas_call | solution.py:200
  19.8 0.4 collective-permute-done.4.refs_12_
  20.5 1.7 %collective-permute-done.6.refs_18_ = bf16[1,136,512]{2,1,0:T(8,128)(2,1)S(1)} collective-permute-done((bf16[1,136,512]{2,1,0:T(8,128)(2,1)S(1)}, bf16[1,136,512]{2,1,0:T(8,128)(2,1)S(1)}, u32[]{:S(2)}, u32[]{:S(2)}) %collective-permute-start.6) | collective-permute-done | bytes 139296 | tf_op jit(solution)/shard_map/ppermute | solution.py:62
  22.2 1.5 %collective-permute-start.11 = (bf16[1,136,512]{2,1,0:T(8,128)(2,1)S(1)}, bf16[1,136,512]{2,1,0:T(8,128)(2,1)S(1)}, u32[]{:S(2)}, u32[]{:S(2)}) collective-permute-start(bf16[1,136,512]{2,1,0:T(8,128)(2,1)S(1)} %collective-permute-done.4.refs_12_), channel_id=1, source_target_pairs={{0,2},{1,3},{2,0},{3,1},{4,6},{5,7},{6,4},{7,5},{8,10},{9,11},{10,... | collective-permute-start | bytes 417800 | tf_op jit(solution)/shard_map/ppermute | solution.py:62
  23.7 0.5 collective-permute-start.13
  24.2 0.5 collective-permute-start.8
  24.7 2.5 %collective-permute-done.11.refs_14_ = bf16[1,136,512]{2,1,0:T(8,128)(2,1)S(1)} collective-permute-done((bf16[1,136,512]{2,1,0:T(8,128)(2,1)S(1)}, bf16[1,136,512]{2,1,0:T(8,128)(2,1)S(1)}, u32[]{:S(2)}, u32[]{:S(2)}) %collective-permute-start.11) | collective-permute-done | bytes 139296 | tf_op jit(solution)/shard_map/ppermute | solution.py:62
  27.3 0.5 collective-permute-start.12
  27.8 0.8 collective-permute-done.9.refs_11_
  28.8 32.6 %shard_map.107 = (bf16[2,1,128,512]{3,2,1,0:T(8,128)(2,1)S(1)}, bf16[2,1,128,512]{3,2,1,0:T(8,128)(2,1)S(1)}, bf16[2,2,128,512]{3,2,1,0:T(8,128)(2,1)S(1)}, bf16...) custom-call(f32[1,2048]{1,0:T(1,128)} %bitcast.41, ...), custom_call_target="tpu_custom_call" | custom-call | flops 4831838208 | bytes 75497472 | tf_op jit(solution)/shard_map/pallas_call | solution.py:416
  61.5 0.4 collective-permute-start.19
  62.1 0.3 collective-permute-start.15
  62.4 0.7 collective-permute-done.19
  63.2 1.6 %collective-permute-start.20 = (bf16[1,128,512]{2,1,0:T(8,128)(2,1)S(1)}, bf16[1,128,512]{2,1,0:T(8,128)(2,1)S(1)}, u32[]{:S(2)}, u32[]{:S(2)}) collective-permute-start(bf16[1,128,512]{2,1,0:T(8,128)(2,1)S(1)} %slice_bitcast_fusion.3), channel_id=1, source_target_pairs={{0,2},{1,3},{2,0},{3,1},{4,6},{5,7},{6,4},{7,5},{8,10},{9,11},{10,... | collective-permute-start | bytes 393224 | tf_op jit(solution)/shard_map/ppermute | solution.py:62
  65.0 1.0 %collective-permute-start.17 = (bf16[2,128,512]{2,1,0:T(8,128)(2,1)S(1)}, bf16[2,128,512]{2,1,0:T(8,128)(2,1)S(1)}, u32[]{:S(2)}, u32[]{:S(2)}) collective-permute-start(bf16[2,128,512]{2,1,0:T(8,128)(2,1)S(1)} %slice_bitcast_fusion.1), channel_id=1, source_target_pairs={{0,2},{1,3},{2,0},{3,1},{4,6},{5,7},{6,4},{7,5},{8,10},{9,11},{10,... | collective-permute-start | bytes 786440 | tf_op jit(solution)/shard_map/ppermute | solution.py:62
  66.0 3.5 %collective-permute-done.20 = bf16[1,128,512]{2,1,0:T(8,128)(2,1)S(1)} collective-permute-done((bf16[1,128,512]{2,1,0:T(8,128)(2,1)S(1)}, bf16[1,128,512]{2,1,0:T(8,128)(2,1)S(1)}, u32[]{:S(2)}, u32[]{:S(2)}) %collective-permute-start.20) | collective-permute-done | bytes 131104 | tf_op jit(solution)/shard_map/ppermute | solution.py:62
  69.6 2.8 %collective-permute-start.21 = (bf16[152,512]{1,0:T(8,128)(2,1)S(1)}, bf16[152,512]{1,0:T(8,128)(2,1)S(1)}, u32[]{:S(2)}, u32[]{:S(2)}) collective-permute-start(bf16[152,512]{1,0:T(8,128)(2,1)S(1)} %pad_maximum_fusion.1), channel_id=1, source_target_pairs={{0,12},{4,0},{8,4},{12,8},{1,13},{5,1},{9,5},{13,9},{2,14},{6,2},{... | collective-permute-start | bytes 466952 | tf_op jit(solution)/shard_map/ppermute | solution.py:57
  72.4 3.2 %collective-permute-done.21 = bf16[152,512]{1,0:T(8,128)(2,1)S(1)} collective-permute-done((bf16[152,512]{1,0:T(8,128)(2,1)S(1)}, bf16[152,512]{1,0:T(8,128)(2,1)S(1)}, u32[]{:S(2)}, u32[]{:S(2)}) %collective-permute-start.21) | collective-permute-done | bytes 155680 | tf_op jit(solution)/shard_map/ppermute | solution.py:57
  75.8 1.1 %collective-permute-start.18 = (bf16[1,128,512]{2,1,0:T(8,128)(2,1)S(1)}, bf16[1,128,512]{2,1,0:T(8,128)(2,1)S(1)}, u32[]{:S(2)}, u32[]{:S(2)}) collective-permute-start(bf16[1,128,512]{2,1,0:T(8,128)(2,1)S(1)} %slice_bitcast_fusion.6), channel_id=1, source_target_pairs={{0,2},{1,3},{2,0},{3,1},{4,6},{5,7},{6,4},{7,5},{8,10},{9,11},{10,... | collective-permute-start | bytes 393224 | tf_op jit(solution)/shard_map/ppermute | solution.py:62
  77.0 3.7 %collective-permute-start.22 = (bf16[176,512]{1,0:T(8,128)(2,1)S(1)}, bf16[176,512]{1,0:T(8,128)(2,1)S(1)}, u32[]{:S(2)}, u32[]{:S(2)}) collective-permute-start(bf16[176,512]{1,0:T(8,128)(2,1)S(1)} %pad_maximum_fusion), channel_id=1, source_target_pairs={{0,12},{4,0},{8,4},{12,8},{1,13},{5,1},{9,5},{13,9},{2,14},{6,2},{... | collective-permute-start | bytes 540680 | tf_op jit(solution)/shard_map/ppermute | solution.py:57
  80.9 3.2 %collective-permute-done.23.up_ref = bf16[152,512]{1,0:T(8,128)(2,1)S(1)} collective-permute-done((bf16[152,512]{1,0:T(8,128)(2,1)S(1)}, bf16[152,512]{1,0:T(8,128)(2,1)S(1)}, u32[]{:S(2)}, u32[]{:S(2)}) %collective-permute-start.23) | collective-permute-done | bytes 155680 | tf_op jit(solution)/shard_map/ppermute | solution.py:57
  84.1 1.3 %collective-permute-done.22.down_ref = bf16[176,512]{1,0:T(8,128)(2,1)S(1)} collective-permute-done((bf16[176,512]{1,0:T(8,128)(2,1)S(1)}, bf16[176,512]{1,0:T(8,128)(2,1)S(1)}, u32[]{:S(2)}, u32[]{:S(2)}) %collective-permute-start.22) | collective-permute-done | bytes 180256 | tf_op jit(solution)/shard_map/ppermute | solution.py:57
  85.5 0.8 shard_map.108
  (39 shorter events, 1.5 us)
Async XLA Ops:
  1.6 10.7 %collective-permute-start = (bf16[1,136,512]{2,1,0:T(8,128)(2,1)S(1)}, bf16[1,136,512]{2,1,0:T(8,128)(2,1)S(1)}, u32[]{:S(2)}, u32[]{:S(2)}) collective-permute-start(bf16[1,136,512]{2,1,0:T(8,128)(2,1)S(1)} %shard_map.104.after_ref.refs_4_), channel_id=1, source_target_pairs={{0,4},{4,8},{8,12},{12,0},{1,5},{5,9},{9,13},{13,1},{2,6},{6,10},{... | collective-permute-start | bytes 417800 | tf_op jit(solution)/shard_map/ppermute | solution.py:57
  4.7 8.1 %collective-permute-start.1 = (bf16[1,136,512]{2,1,0:T(8,128)(2,1)S(1)}, bf16[1,136,512]{2,1,0:T(8,128)(2,1)S(1)}, u32[]{:S(2)}, u32[]{:S(2)}) collective-permute-start(bf16[1,136,512]{2,1,0:T(8,128)(2,1)S(1)} %shard_map.104.after_ref.refs_4_), channel_id=1, source_target_pairs={{0,12},{4,0},{8,4},{12,8},{1,13},{5,1},{9,5},{13,9},{2,14},{6,2},{... | collective-permute-start | bytes 417800 | tf_op jit(solution)/shard_map/ppermute | solution.py:57
  6.8 6.0 %collective-permute-start.2 = (bf16[1,136,512]{2,1,0:T(8,128)(2,1)S(1)}, bf16[1,136,512]{2,1,0:T(8,128)(2,1)S(1)}, u32[]{:S(2)}, u32[]{:S(2)}) collective-permute-start(bf16[1,136,512]{2,1,0:T(8,128)(2,1)S(1)} %shard_map.104.after_ref.refs_4_), channel_id=1, source_target_pairs={{0,2},{1,3},{2,0},{3,1},{4,6},{5,7},{6,4},{7,5},{8,10},{9,11},{10,... | collective-permute-start | bytes 417800 | tf_op jit(solution)/shard_map/ppermute | solution.py:62
  8.4 4.4 %collective-permute-start.3 = (bf16[1,136,512]{2,1,0:T(8,128)(2,1)S(1)}, bf16[1,136,512]{2,1,0:T(8,128)(2,1)S(1)}, u32[]{:S(2)}, u32[]{:S(2)}) collective-permute-start(bf16[1,136,512]{2,1,0:T(8,128)(2,1)S(1)} %shard_map.104.after_ref.refs_4_), channel_id=1, source_target_pairs={{0,1},{1,0},{2,3},{3,2},{4,5},{5,4},{6,7},{7,6},{8,9},{9,8},{10,11... | collective-permute-start | bytes 417800 | tf_op jit(solution)/shard_map/ppermute | solution.py:67
  12.8 7.4 %collective-permute-start.4 = (bf16[1,136,512]{2,1,0:T(8,128)(2,1)S(1)}, bf16[1,136,512]{2,1,0:T(8,128)(2,1)S(1)}, u32[]{:S(2)}, u32[]{:S(2)}) collective-permute-start(bf16[1,136,512]{2,1,0:T(8,128)(2,1)S(1)} %collective-permute-done.refs_8_), channel_id=1, source_target_pairs={{0,4},{4,8},{8,12},{12,0},{1,5},{5,9},{9,13},{13,1},{2,6},{6,10},{... | collective-permute-start | bytes 417800 | tf_op jit(solution)/shard_map/ppermute | solution.py:57
  13.9 6.6 %collective-permute-start.5 = (bf16[1,136,512]{2,1,0:T(8,128)(2,1)S(1)}, bf16[1,136,512]{2,1,0:T(8,128)(2,1)S(1)}, u32[]{:S(2)}, u32[]{:S(2)}) collective-permute-start(bf16[1,136,512]{2,1,0:T(8,128)(2,1)S(1)} %collective-permute-done.refs_8_), channel_id=1, source_target_pairs={{0,2},{1,3},{2,0},{3,1},{4,6},{5,7},{6,4},{7,5},{8,10},{9,11},{10,... | collective-permute-start | bytes 417800 | tf_op jit(solution)/shard_map/ppermute | solution.py:62
  15.4 6.8 %collective-permute-start.6 = (bf16[1,136,512]{2,1,0:T(8,128)(2,1)S(1)}, bf16[1,136,512]{2,1,0:T(8,128)(2,1)S(1)}, u32[]{:S(2)}, u32[]{:S(2)}) collective-permute-start(bf16[1,136,512]{2,1,0:T(8,128)(2,1)S(1)} %collective-permute-done.1.after_ref.refs_16_), channel_id=1, source_target_pairs={{0,2},{1,3},{2,0},{3,1},{4,6},{5,7},{6,4},{7,5},{8,10},{9,11},{10,... | collective-permute-start | bytes 417800 | tf_op jit(solution)/shard_map/ppermute | solution.py:62
  19.7 4.5 %collective-permute-start.7 = (bf16[1,136,512]{2,1,0:T(8,128)(2,1)S(1)}, bf16[1,136,512]{2,1,0:T(8,128)(2,1)S(1)}, u32[]{:S(2)}, u32[]{:S(2)}) collective-permute-start(bf16[1,136,512]{2,1,0:T(8,128)(2,1)S(1)} %collective-permute-done.2.refs_6_), channel_id=1, source_target_pairs={{0,1},{1,0},{2,3},{3,2},{4,5},{5,4},{6,7},{7,6},{8,9},{9,8},{10,11... | collective-permute-start | bytes 417800 | tf_op jit(solution)/shard_map/ppermute | solution.py:67
  22.2 5.1 %collective-permute-start.11 = (bf16[1,136,512]{2,1,0:T(8,128)(2,1)S(1)}, bf16[1,136,512]{2,1,0:T(8,128)(2,1)S(1)}, u32[]{:S(2)}, u32[]{:S(2)}) collective-permute-start(bf16[1,136,512]{2,1,0:T(8,128)(2,1)S(1)} %collective-permute-done.4.refs_12_), channel_id=1, source_target_pairs={{0,2},{1,3},{2,0},{3,1},{4,6},{5,7},{6,4},{7,5},{8,10},{9,11},{10,... | collective-permute-start | bytes 417800 | tf_op jit(solution)/shard_map/ppermute | solution.py:62
  23.7 3.6 %collective-permute-start.10 = (bf16[1,136,512]{2,1,0:T(8,128)(2,1)S(1)}, bf16[1,136,512]{2,1,0:T(8,128)(2,1)S(1)}, u32[]{:S(2)}, u32[]{:S(2)}) collective-permute-start(bf16[1,136,512]{2,1,0:T(8,128)(2,1)S(1)} %collective-permute-done.4.refs_12_), channel_id=1, source_target_pairs={{0,1},{1,0},{2,3},{3,2},{4,5},{5,4},{6,7},{7,6},{8,9},{9,8},{10,11... | collective-permute-start | bytes 417800 | tf_op jit(solution)/shard_map/ppermute | solution.py:67
  23.7 4.1 %collective-permute-start.13 = (bf16[1,136,512]{2,1,0:T(8,128)(2,1)S(1)}, bf16[1,136,512]{2,1,0:T(8,128)(2,1)S(1)}, u32[]{:S(2)}, u32[]{:S(2)}) collective-permute-start(bf16[1,136,512]{2,1,0:T(8,128)(2,1)S(1)} %collective-permute-done.1.after_ref.refs_16_), channel_id=1, source_target_pairs={{0,1},{1,0},{2,3},{3,2},{4,5},{5,4},{6,7},{7,6},{8,9},{9,8},{10,11... | collective-permute-start | bytes 417800 | tf_op jit(solution)/shard_map/ppermute | solution.py:67
  24.2 3.6 %collective-permute-start.14 = (bf16[1,136,512]{2,1,0:T(8,128)(2,1)S(1)}, bf16[1,136,512]{2,1,0:T(8,128)(2,1)S(1)}, u32[]{:S(2)}, u32[]{:S(2)}) collective-permute-start(bf16[1,136,512]{2,1,0:T(8,128)(2,1)S(1)} %collective-permute-done.6.refs_18_), channel_id=1, source_target_pairs={{0,1},{1,0},{2,3},{3,2},{4,5},{5,4},{6,7},{7,6},{8,9},{9,8},{10,11... | collective-permute-start | bytes 417800 | tf_op jit(solution)/shard_map/ppermute | solution.py:67
  24.2 3.6 %collective-permute-start.8 = (bf16[1,136,512]{2,1,0:T(8,128)(2,1)S(1)}, bf16[1,136,512]{2,1,0:T(8,128)(2,1)S(1)}, u32[]{:S(2)}, u32[]{:S(2)}) collective-permute-start(bf16[1,136,512]{2,1,0:T(8,128)(2,1)S(1)} %collective-permute-done.refs_8_), channel_id=1, source_target_pairs={{0,1},{1,0},{2,3},{3,2},{4,5},{5,4},{6,7},{7,6},{8,9},{9,8},{10,11... | collective-permute-start | bytes 417800 | tf_op jit(solution)/shard_map/ppermute | solution.py:67
  27.3 1.4 %collective-permute-start.9 = (bf16[1,136,512]{2,1,0:T(8,128)(2,1)S(1)}, bf16[1,136,512]{2,1,0:T(8,128)(2,1)S(1)}, u32[]{:S(2)}, u32[]{:S(2)}) collective-permute-start(bf16[1,136,512]{2,1,0:T(8,128)(2,1)S(1)} %collective-permute-done.5.refs_10_), channel_id=1, source_target_pairs={{0,1},{1,0},{2,3},{3,2},{4,5},{5,4},{6,7},{7,6},{8,9},{9,8},{10,11... | collective-permute-start | bytes 417800 | tf_op jit(solution)/shard_map/ppermute | solution.py:67
  27.3 1.6 %collective-permute-start.12 = (bf16[1,136,512]{2,1,0:T(8,128)(2,1)S(1)}, bf16[1,136,512]{2,1,0:T(8,128)(2,1)S(1)}, u32[]{:S(2)}, u32[]{:S(2)}) collective-permute-start(bf16[1,136,512]{2,1,0:T(8,128)(2,1)S(1)} %collective-permute-done.11.refs_14_), channel_id=1, source_target_pairs={{0,1},{1,0},{2,3},{3,2},{4,5},{5,4},{6,7},{7,6},{8,9},{9,8},{10,11... | collective-permute-start | bytes 417800 | tf_op jit(solution)/shard_map/ppermute | solution.py:67
  61.5 24.0 %copy-start = (bf16[128,512]{1,0:T(8,128)(2,1)S(1)}, bf16[128,512]{1,0:T(8,128)(2,1)}, u32[]{:S(2)}) copy-start(bf16[128,512]{1,0:T(8,128)(2,1)} %hidden_ref.3) | copy-start | bytes 393220
  61.5 1.6 %collective-permute-start.19 = (bf16[2,1,128,512]{3,2,1,0:T(8,128)(2,1)S(1)}, bf16[2,1,128,512]{3,2,1,0:T(8,128)(2,1)S(1)}, u32[]{:S(2)}, u32[]{:S(2)}) collective-permute-start(bf16[2,1,128,512]{3,2,1,0:T(8,128)(2,1)S(1)} %get-tuple-element.51), channel_id=1, source_target_pairs={{0,1},{1,0},{2,3},{3,2},{4,5},{5,4},{6,7},{7,6},{8,9},{9,8},{10,11... | collective-permute-start | bytes 786440 | tf_op jit(solution)/shard_map/ppermute | solution.py:67
  61.9 3.0 %collective-permute-start.16 = (bf16[2,2,128,512]{3,2,1,0:T(8,128)(2,1)}, bf16[2,2,128,512]{3,2,1,0:T(8,128)(2,1)S(1)}, u32[]{:S(2)}, u32[]{:S(2)}) collective-permute-start(bf16[2,2,128,512]{3,2,1,0:T(8,128)(2,1)} %get-tuple-element.48), channel_id=1, source_target_pairs={{0,1},{1,0},{2,3},{3,2},{4,5},{5,4},{6,7},{7,6},{8,9},{9,8},{10,11... | collective-permute-start | bytes 1572872 | tf_op jit(solution)/shard_map/ppermute | solution.py:67
  62.1 2.7 %collective-permute-start.15 = (bf16[2,1,128,512]{3,2,1,0:T(8,128)(2,1)S(1)}, bf16[2,1,128,512]{3,2,1,0:T(8,128)(2,1)S(1)}, u32[]{:S(2)}, u32[]{:S(2)}) collective-permute-start(bf16[2,1,128,512]{3,2,1,0:T(8,128)(2,1)S(1)} %get-tuple-element.46), channel_id=1, source_target_pairs={{0,1},{1,0},{2,3},{3,2},{4,5},{5,4},{6,7},{7,6},{8,9},{9,8},{10,11... | collective-permute-start | bytes 786440 | tf_op jit(solution)/shard_map/ppermute | solution.py:67
  63.2 6.4 %collective-permute-start.20 = (bf16[1,128,512]{2,1,0:T(8,128)(2,1)S(1)}, bf16[1,128,512]{2,1,0:T(8,128)(2,1)S(1)}, u32[]{:S(2)}, u32[]{:S(2)}) collective-permute-start(bf16[1,128,512]{2,1,0:T(8,128)(2,1)S(1)} %slice_bitcast_fusion.3), channel_id=1, source_target_pairs={{0,2},{1,3},{2,0},{3,1},{4,6},{5,7},{6,4},{7,5},{8,10},{9,11},{10,... | collective-permute-start | bytes 393224 | tf_op jit(solution)/shard_map/ppermute | solution.py:62
  65.0 10.6 %collective-permute-start.17 = (bf16[2,128,512]{2,1,0:T(8,128)(2,1)S(1)}, bf16[2,128,512]{2,1,0:T(8,128)(2,1)S(1)}, u32[]{:S(2)}, u32[]{:S(2)}) collective-permute-start(bf16[2,128,512]{2,1,0:T(8,128)(2,1)S(1)} %slice_bitcast_fusion.1), channel_id=1, source_target_pairs={{0,2},{1,3},{2,0},{3,1},{4,6},{5,7},{6,4},{7,5},{8,10},{9,11},{10,... | collective-permute-start | bytes 786440 | tf_op jit(solution)/shard_map/ppermute | solution.py:62
  69.6 6.0 %collective-permute-start.21 = (bf16[152,512]{1,0:T(8,128)(2,1)S(1)}, bf16[152,512]{1,0:T(8,128)(2,1)S(1)}, u32[]{:S(2)}, u32[]{:S(2)}) collective-permute-start(bf16[152,512]{1,0:T(8,128)(2,1)S(1)} %pad_maximum_fusion.1), channel_id=1, source_target_pairs={{0,12},{4,0},{8,4},{12,8},{1,13},{5,1},{9,5},{13,9},{2,14},{6,2},{... | collective-permute-start | bytes 466952 | tf_op jit(solution)/shard_map/ppermute | solution.py:57
  75.7 8.4 %collective-permute-start.23 = (bf16[152,512]{1,0:T(8,128)(2,1)S(1)}, bf16[152,512]{1,0:T(8,128)(2,1)S(1)}, u32[]{:S(2)}, u32[]{:S(2)}) collective-permute-start(bf16[152,512]{1,0:T(8,128)(2,1)S(1)} %pad_maximum_fusion.2), channel_id=1, source_target_pairs={{0,4},{4,8},{8,12},{12,0},{1,5},{5,9},{9,13},{13,1},{2,6},{6,10},{... | collective-permute-start | bytes 466952 | tf_op jit(solution)/shard_map/ppermute | solution.py:57
  75.8 5.0 %collective-permute-start.18 = (bf16[1,128,512]{2,1,0:T(8,128)(2,1)S(1)}, bf16[1,128,512]{2,1,0:T(8,128)(2,1)S(1)}, u32[]{:S(2)}, u32[]{:S(2)}) collective-permute-start(bf16[1,128,512]{2,1,0:T(8,128)(2,1)S(1)} %slice_bitcast_fusion.6), channel_id=1, source_target_pairs={{0,2},{1,3},{2,0},{3,1},{4,6},{5,7},{6,4},{7,5},{8,10},{9,11},{10,... | collective-permute-start | bytes 393224 | tf_op jit(solution)/shard_map/ppermute | solution.py:62
  77.0 8.5 %collective-permute-start.22 = (bf16[176,512]{1,0:T(8,128)(2,1)S(1)}, bf16[176,512]{1,0:T(8,128)(2,1)S(1)}, u32[]{:S(2)}, u32[]{:S(2)}) collective-permute-start(bf16[176,512]{1,0:T(8,128)(2,1)S(1)} %pad_maximum_fusion), channel_id=1, source_target_pairs={{0,12},{4,0},{8,4},{12,8},{1,13},{5,1},{9,5},{13,9},{2,14},{6,2},{... | collective-permute-start | bytes 540680 | tf_op jit(solution)/shard_map/ppermute | solution.py:57

commit v7 on v6

--- a/solution.py
+++ b/solution.py
@@ -357,13 +357,15 @@
         picked = picked_ref[at, :]
         along = (((1,), (1,)), ((), ()))
         gate_part = lax.dot_general(
-            picked, gate_up[0], along, preferred_element_type=jnp.float32
+            gate_up[0], picked, along, preferred_element_type=jnp.float32
         )
         up_part = lax.dot_general(
-            picked, gate_up[1], along, preferred_element_type=jnp.float32
+            gate_up[1], picked, along, preferred_element_type=jnp.float32
         )
         activated = (jax.nn.silu(gate_part) * up_part).astype(jnp.bfloat16)
-        served = jnp.dot(activated, down[...], preferred_element_type=jnp.float32)
+        served = lax.dot_general(
+            activated, down[...], (((0,), (0,)), ((), ())), preferred_element_type=jnp.float32
+        )
         served_ref[at, :] = (served * slot_gate_ref[at, :]).astype(jnp.bfloat16)
 
     for h in range(fills):

time: 86.4 us -> 85.4 us (0.988)
  Pallas kernels: 41.9 us -> 40.9 us
    pallas_call x1, Pallas kernels: 32.6 us -> 31.5 us  [expert_sums(): pl.pallas_call(functools.partial(expert_kernel, held=held, capacity=capac...]
where the time goes in v7:
time: 85.4 us; the launch traced here: 85.1 us
  Pallas kernels  40.9 us (48%)
  starting transfers between devices  24.2 us (28%)
  waiting for transfers between devices  18.7 us (22%)
    pallas_call x1, Pallas kernels, expert_sums(): pl.pallas_call(functools.partial(expert_kernel, held=held, capacity=capac...  31.5 us
    ppermute x6, starting transfers between devices, shift_dp(): lax.ppermute(value, 'dp', [(i, (i + shift) % count) for i in range(count)])  12.9 us
    ppermute x7, starting transfers between devices, shift_x(): lax.ppermute(value, 'mp', [(i, (i + CORES * shift) % count) for i in rang...  8.88 us
    ppermute x6, waiting for transfers between devices, shift_dp(): lax.ppermute(value, 'dp', [(i, (i + shift) % count) for i in range(count)])  8.68 us
    ppermute x7, waiting for transfers between devices, shift_x(): lax.ppermute(value, 'mp', [(i, (i + CORES * shift) % count) for i in rang...  8.22 us
    pallas_call x2, Pallas kernels, filled(): pl.pallas_call(functools.partial(kernel, expert=expert), out_shape=out_sh...  7.62 us
    ppermute x11, starting transfers between devices, other_core(): return lax.ppermute(value, 'mp', [(i, i ^ 1) for i in range(count)])  2.5 us
    ppermute x11, waiting for transfers between devices, other_core(): return lax.ppermute(value, 'mp', [(i, i ^ 1) for i in range(count)])  1.75 us
  transfers between devices with their start and end apart: 24, of which 13 were waited for; matrix products, arithmetic and copies ran while one was open for 1% of the time, Pallas kernels for 9%

profile of v7, /device:TPU:0, one launch (start us, length us, event | category | flops | bytes accessed | tf_op | source)
XLA Modules:
  0.0 85.1 jit_solution(7320017346145079143)
XLA Ops:
  0.6 1.0 %shard_map.104.after_ref.refs_4_ = bf16[1,136,512]{2,1,0:T(8,128)(2,1)S(1)} custom-call(bf16[128,512]{1,0:T(8,128)(2,1)} %hidden_ref.3, s32[8,128]{1,0:T(8,128)} %bitcast.42, f32[8,128]{1,0:T(8,128)} %bitcast.43), custom_call_target="tpu_custom_call" | custom-call | tf_op jit(solution)/shard_map/pallas_call | solution.py:98
  1.6 3.1 %collective-permute-start = (bf16[1,136,512]{2,1,0:T(8,128)(2,1)S(1)}, bf16[1,136,512]{2,1,0:T(8,128)(2,1)S(1)}, u32[]{:S(2)}, u32[]{:S(2)}) collective-permute-start(bf16[1,136,512]{2,1,0:T(8,128)(2,1)S(1)} %shard_map.104.after_ref.refs_4_), channel_id=1, source_target_pairs={{0,4},{4,8},{8,12},{12,0},{1,5},{5,9},{9,13},{13,1},{2,6},{6,10},{... | collective-permute-start | bytes 417800 | tf_op jit(solution)/shard_map/ppermute | solution.py:57
  4.7 2.1 %collective-permute-start.1 = (bf16[1,136,512]{2,1,0:T(8,128)(2,1)S(1)}, bf16[1,136,512]{2,1,0:T(8,128)(2,1)S(1)}, u32[]{:S(2)}, u32[]{:S(2)}) collective-permute-start(bf16[1,136,512]{2,1,0:T(8,128)(2,1)S(1)} %shard_map.104.after_ref.refs_4_), channel_id=1, source_target_pairs={{0,12},{4,0},{8,4},{12,8},{1,13},{5,1},{9,5},{13,9},{2,14},{6,2},{... | collective-permute-start | bytes 417800 | tf_op jit(solution)/shard_map/ppermute | solution.py:57
  6.8 1.6 %collective-permute-start.2 = (bf16[1,136,512]{2,1,0:T(8,128)(2,1)S(1)}, bf16[1,136,512]{2,1,0:T(8,128)(2,1)S(1)}, u32[]{:S(2)}, u32[]{:S(2)}) collective-permute-start(bf16[1,136,512]{2,1,0:T(8,128)(2,1)S(1)} %shard_map.104.after_ref.refs_4_), channel_id=1, source_target_pairs={{0,2},{1,3},{2,0},{3,1},{4,6},{5,7},{6,4},{7,5},{8,10},{9,11},{10,... | collective-permute-start | bytes 417800 | tf_op jit(solution)/shard_map/ppermute | solution.py:62
  8.4 3.8 %shard_map.105 = (bf16[2,768,2048]{2,1,0:T(8,128)(2,1)S(1)}, bf16[768,2048]{1,0:T(8,128)(2,1)S(1)}, bf16[4,24,512]{2,1,0:T(8,128)(2,1)S(1)}) custom-call(bf16[2,6144,2048]{2,1,0:T(8,128)(2,1)} %gate_up_ref.5, bf16[6144,2048]{1,0:T(8,128)(2,1)} %down_ref.5, bf16[1,136,512]{2,1,0:T(8,128)(2,1)S(1)} %shard_map.104.after_ref.refs_4_, bf16[128,256]{1,0:T(8,128)(2,1)} %kv_ref.1, ...), custom_call_target="tpu_custom_call" | custom-call | bytes 9437184 | tf_op jit(solution)/shard_map/pallas_call | solution.py:200
  12.3 0.5 collective-permute-done.1.after_ref.refs_16_
  12.8 1.1 %collective-permute-start.4 = (bf16[1,136,512]{2,1,0:T(8,128)(2,1)S(1)}, bf16[1,136,512]{2,1,0:T(8,128)(2,1)S(1)}, u32[]{:S(2)}, u32[]{:S(2)}) collective-permute-start(bf16[1,136,512]{2,1,0:T(8,128)(2,1)S(1)} %collective-permute-done.refs_8_), channel_id=1, source_target_pairs={{0,4},{4,8},{8,12},{12,0},{1,5},{5,9},{9,13},{13,1},{2,6},{6,10},{... | collective-permute-start | bytes 417800 | tf_op jit(solution)/shard_map/ppermute | solution.py:57
  13.9 1.5 %collective-permute-start.5 = (bf16[1,136,512]{2,1,0:T(8,128)(2,1)S(1)}, bf16[1,136,512]{2,1,0:T(8,128)(2,1)S(1)}, u32[]{:S(2)}, u32[]{:S(2)}) collective-permute-start(bf16[1,136,512]{2,1,0:T(8,128)(2,1)S(1)} %collective-permute-done.refs_8_), channel_id=1, source_target_pairs={{0,2},{1,3},{2,0},{3,1},{4,6},{5,7},{6,4},{7,5},{8,10},{9,11},{10,... | collective-permute-start | bytes 417800 | tf_op jit(solution)/shard_map/ppermute | solution.py:62
  15.4 0.5 collective-permute-start.6
  16.0 3.8 %shard_map.106 = (bf16[2,768,2048]{2,1,0:T(8,128)(2,1)S(1)}, bf16[768,2048]{1,0:T(8,128)(2,1)S(1)}) custom-call(bf16[2,6144,2048]{2,1,0:T(8,128)(2,1)} %gate_up_ref.5, bf16[6144,2048]{1,0:T(8,128)(2,1)} %down_ref.5, bf16[1,136,512]{2,1,0:T(8,128)(2,1)S(1)} %collective-permute-done.1.after_ref.refs_16_), custom_call_target="tpu_custom_call" | custom-call | bytes 9437184 | tf_op jit(solution)/shard_map/pallas_call | solution.py:200
  19.8 0.4 collective-permute-done.4.refs_12_
  20.5 1.7 %collective-permute-done.6.refs_18_ = bf16[1,136,512]{2,1,0:T(8,128)(2,1)S(1)} collective-permute-done((bf16[1,136,512]{2,1,0:T(8,128)(2,1)S(1)}, bf16[1,136,512]{2,1,0:T(8,128)(2,1)S(1)}, u32[]{:S(2)}, u32[]{:S(2)}) %collective-permute-start.6) | collective-permute-done | bytes 139296 | tf_op jit(solution)/shard_map/ppermute | solution.py:62
  22.2 1.5 %collective-permute-start.11 = (bf16[1,136,512]{2,1,0:T(8,128)(2,1)S(1)}, bf16[1,136,512]{2,1,0:T(8,128)(2,1)S(1)}, u32[]{:S(2)}, u32[]{:S(2)}) collective-permute-start(bf16[1,136,512]{2,1,0:T(8,128)(2,1)S(1)} %collective-permute-done.4.refs_12_), channel_id=1, source_target_pairs={{0,2},{1,3},{2,0},{3,1},{4,6},{5,7},{6,4},{7,5},{8,10},{9,11},{10,... | collective-permute-start | bytes 417800 | tf_op jit(solution)/shard_map/ppermute | solution.py:62
  23.7 0.5 collective-permute-start.13
  24.2 0.5 collective-permute-start.8
  24.7 2.5 %collective-permute-done.11.refs_14_ = bf16[1,136,512]{2,1,0:T(8,128)(2,1)S(1)} collective-permute-done((bf16[1,136,512]{2,1,0:T(8,128)(2,1)S(1)}, bf16[1,136,512]{2,1,0:T(8,128)(2,1)S(1)}, u32[]{:S(2)}, u32[]{:S(2)}) %collective-permute-start.11) | collective-permute-done | bytes 139296 | tf_op jit(solution)/shard_map/ppermute | solution.py:62
  27.3 0.5 collective-permute-start.12
  27.8 0.8 collective-permute-done.9.refs_11_
  28.8 31.5 %shard_map.107 = (bf16[2,1,128,512]{3,2,1,0:T(8,128)(2,1)S(1)}, bf16[2,1,128,512]{3,2,1,0:T(8,128)(2,1)S(1)}, bf16[2,2,128,512]{3,2,1,0:T(8,128)(2,1)S(1)}, bf16...) custom-call(f32[1,2048]{1,0:T(1,128)} %bitcast.41, ...), custom_call_target="tpu_custom_call" | custom-call | flops 4831838208 | bytes 75497472 | tf_op jit(solution)/shard_map/pallas_call | solution.py:418
  60.4 0.4 collective-permute-start.19
  61.0 0.3 collective-permute-start.15
  61.3 0.7 collective-permute-done.19
  62.1 1.6 %collective-permute-start.20 = (bf16[1,128,512]{2,1,0:T(8,128)(2,1)S(1)}, bf16[1,128,512]{2,1,0:T(8,128)(2,1)S(1)}, u32[]{:S(2)}, u32[]{:S(2)}) collective-permute-start(bf16[1,128,512]{2,1,0:T(8,128)(2,1)S(1)} %slice_bitcast_fusion.3), channel_id=1, source_target_pairs={{0,2},{1,3},{2,0},{3,1},{4,6},{5,7},{6,4},{7,5},{8,10},{9,11},{10,... | collective-permute-start | bytes 393224 | tf_op jit(solution)/shard_map/ppermute | solution.py:62
  63.9 1.0 %collective-permute-start.17 = (bf16[2,128,512]{2,1,0:T(8,128)(2,1)S(1)}, bf16[2,128,512]{2,1,0:T(8,128)(2,1)S(1)}, u32[]{:S(2)}, u32[]{:S(2)}) collective-permute-start(bf16[2,128,512]{2,1,0:T(8,128)(2,1)S(1)} %slice_bitcast_fusion.1), channel_id=1, source_target_pairs={{0,2},{1,3},{2,0},{3,1},{4,6},{5,7},{6,4},{7,5},{8,10},{9,11},{10,... | collective-permute-start | bytes 786440 | tf_op jit(solution)/shard_map/ppermute | solution.py:62
  65.0 3.5 %collective-permute-done.20 = bf16[1,128,512]{2,1,0:T(8,128)(2,1)S(1)} collective-permute-done((bf16[1,128,512]{2,1,0:T(8,128)(2,1)S(1)}, bf16[1,128,512]{2,1,0:T(8,128)(2,1)S(1)}, u32[]{:S(2)}, u32[]{:S(2)}) %collective-permute-start.20) | collective-permute-done | bytes 131104 | tf_op jit(solution)/shard_map/ppermute | solution.py:62
  68.6 2.8 %collective-permute-start.21 = (bf16[152,512]{1,0:T(8,128)(2,1)S(1)}, bf16[152,512]{1,0:T(8,128)(2,1)S(1)}, u32[]{:S(2)}, u32[]{:S(2)}) collective-permute-start(bf16[152,512]{1,0:T(8,128)(2,1)S(1)} %pad_maximum_fusion.1), channel_id=1, source_target_pairs={{0,12},{4,0},{8,4},{12,8},{1,13},{5,1},{9,5},{13,9},{2,14},{6,2},{... | collective-permute-start | bytes 466952 | tf_op jit(solution)/shard_map/ppermute | solution.py:57
  71.4 3.2 %collective-permute-done.21 = bf16[152,512]{1,0:T(8,128)(2,1)S(1)} collective-permute-done((bf16[152,512]{1,0:T(8,128)(2,1)S(1)}, bf16[152,512]{1,0:T(8,128)(2,1)S(1)}, u32[]{:S(2)}, u32[]{:S(2)}) %collective-permute-start.21) | collective-permute-done | bytes 155680 | tf_op jit(solution)/shard_map/ppermute | solution.py:57
  74.7 1.1 %collective-permute-start.18 = (bf16[1,128,512]{2,1,0:T(8,128)(2,1)S(1)}, bf16[1,128,512]{2,1,0:T(8,128)(2,1)S(1)}, u32[]{:S(2)}, u32[]{:S(2)}) collective-permute-start(bf16[1,128,512]{2,1,0:T(8,128)(2,1)S(1)} %slice_bitcast_fusion.6), channel_id=1, source_target_pairs={{0,2},{1,3},{2,0},{3,1},{4,6},{5,7},{6,4},{7,5},{8,10},{9,11},{10,... | collective-permute-start | bytes 393224 | tf_op jit(solution)/shard_map/ppermute | solution.py:62
  75.9 3.7 %collective-permute-start.22 = (bf16[176,512]{1,0:T(8,128)(2,1)S(1)}, bf16[176,512]{1,0:T(8,128)(2,1)S(1)}, u32[]{:S(2)}, u32[]{:S(2)}) collective-permute-start(bf16[176,512]{1,0:T(8,128)(2,1)S(1)} %pad_maximum_fusion), channel_id=1, source_target_pairs={{0,12},{4,0},{8,4},{12,8},{1,13},{5,1},{9,5},{13,9},{2,14},{6,2},{... | collective-permute-start | bytes 540680 | tf_op jit(solution)/shard_map/ppermute | solution.py:57
  79.8 3.2 %collective-permute-done.23.up_ref = bf16[152,512]{1,0:T(8,128)(2,1)S(1)} collective-permute-done((bf16[152,512]{1,0:T(8,128)(2,1)S(1)}, bf16[152,512]{1,0:T(8,128)(2,1)S(1)}, u32[]{:S(2)}, u32[]{:S(2)}) %collective-permute-start.23) | collective-permute-done | bytes 155680 | tf_op jit(solution)/shard_map/ppermute | solution.py:57
  83.0 1.3 %collective-permute-done.22.down_ref = bf16[176,512]{1,0:T(8,128)(2,1)S(1)} collective-permute-done((bf16[176,512]{1,0:T(8,128)(2,1)S(1)}, bf16[176,512]{1,0:T(8,128)(2,1)S(1)}, u32[]{:S(2)}, u32[]{:S(2)}) %collective-permute-start.22) | collective-permute-done | bytes 180256 | tf_op jit(solution)/shard_map/ppermute | solution.py:57
  84.4 0.8 shard_map.108
  (39 shorter events, 1.6 us)
Async XLA Ops:
  1.6 10.7 %collective-permute-start = (bf16[1,136,512]{2,1,0:T(8,128)(2,1)S(1)}, bf16[1,136,512]{2,1,0:T(8,128)(2,1)S(1)}, u32[]{:S(2)}, u32[]{:S(2)}) collective-permute-start(bf16[1,136,512]{2,1,0:T(8,128)(2,1)S(1)} %shard_map.104.after_ref.refs_4_), channel_id=1, source_target_pairs={{0,4},{4,8},{8,12},{12,0},{1,5},{5,9},{9,13},{13,1},{2,6},{6,10},{... | collective-permute-start | bytes 417800 | tf_op jit(solution)/shard_map/ppermute | solution.py:57
  4.7 8.1 %collective-permute-start.1 = (bf16[1,136,512]{2,1,0:T(8,128)(2,1)S(1)}, bf16[1,136,512]{2,1,0:T(8,128)(2,1)S(1)}, u32[]{:S(2)}, u32[]{:S(2)}) collective-permute-start(bf16[1,136,512]{2,1,0:T(8,128)(2,1)S(1)} %shard_map.104.after_ref.refs_4_), channel_id=1, source_target_pairs={{0,12},{4,0},{8,4},{12,8},{1,13},{5,1},{9,5},{13,9},{2,14},{6,2},{... | collective-permute-start | bytes 417800 | tf_op jit(solution)/shard_map/ppermute | solution.py:57
  6.8 6.0 %collective-permute-start.2 = (bf16[1,136,512]{2,1,0:T(8,128)(2,1)S(1)}, bf16[1,136,512]{2,1,0:T(8,128)(2,1)S(1)}, u32[]{:S(2)}, u32[]{:S(2)}) collective-permute-start(bf16[1,136,512]{2,1,0:T(8,128)(2,1)S(1)} %shard_map.104.after_ref.refs_4_), channel_id=1, source_target_pairs={{0,2},{1,3},{2,0},{3,1},{4,6},{5,7},{6,4},{7,5},{8,10},{9,11},{10,... | collective-permute-start | bytes 417800 | tf_op jit(solution)/shard_map/ppermute | solution.py:62
  8.4 4.4 %collective-permute-start.3 = (bf16[1,136,512]{2,1,0:T(8,128)(2,1)S(1)}, bf16[1,136,512]{2,1,0:T(8,128)(2,1)S(1)}, u32[]{:S(2)}, u32[]{:S(2)}) collective-permute-start(bf16[1,136,512]{2,1,0:T(8,128)(2,1)S(1)} %shard_map.104.after_ref.refs_4_), channel_id=1, source_target_pairs={{0,1},{1,0},{2,3},{3,2},{4,5},{5,4},{6,7},{7,6},{8,9},{9,8},{10,11... | collective-permute-start | bytes 417800 | tf_op jit(solution)/shard_map/ppermute | solution.py:67
  12.8 7.4 %collective-permute-start.4 = (bf16[1,136,512]{2,1,0:T(8,128)(2,1)S(1)}, bf16[1,136,512]{2,1,0:T(8,128)(2,1)S(1)}, u32[]{:S(2)}, u32[]{:S(2)}) collective-permute-start(bf16[1,136,512]{2,1,0:T(8,128)(2,1)S(1)} %collective-permute-done.refs_8_), channel_id=1, source_target_pairs={{0,4},{4,8},{8,12},{12,0},{1,5},{5,9},{9,13},{13,1},{2,6},{6,10},{... | collective-permute-start | bytes 417800 | tf_op jit(solution)/shard_map/ppermute | solution.py:57
  13.9 6.6 %collective-permute-start.5 = (bf16[1,136,512]{2,1,0:T(8,128)(2,1)S(1)}, bf16[1,136,512]{2,1,0:T(8,128)(2,1)S(1)}, u32[]{:S(2)}, u32[]{:S(2)}) collective-permute-start(bf16[1,136,512]{2,1,0:T(8,128)(2,1)S(1)} %collective-permute-done.refs_8_), channel_id=1, source_target_pairs={{0,2},{1,3},{2,0},{3,1},{4,6},{5,7},{6,4},{7,5},{8,10},{9,11},{10,... | collective-permute-start | bytes 417800 | tf_op jit(solution)/shard_map/ppermute | solution.py:62
  15.4 6.8 %collective-permute-start.6 = (bf16[1,136,512]{2,1,0:T(8,128)(2,1)S(1)}, bf16[1,136,512]{2,1,0:T(8,128)(2,1)S(1)}, u32[]{:S(2)}, u32[]{:S(2)}) collective-permute-start(bf16[1,136,512]{2,1,0:T(8,128)(2,1)S(1)} %collective-permute-done.1.after_ref.refs_16_), channel_id=1, source_target_pairs={{0,2},{1,3},{2,0},{3,1},{4,6},{5,7},{6,4},{7,5},{8,10},{9,11},{10,... | collective-permute-start | bytes 417800 | tf_op jit(solution)/shard_map/ppermute | solution.py:62
  19.7 4.5 %collective-permute-start.7 = (bf16[1,136,512]{2,1,0:T(8,128)(2,1)S(1)}, bf16[1,136,512]{2,1,0:T(8,128)(2,1)S(1)}, u32[]{:S(2)}, u32[]{:S(2)}) collective-permute-start(bf16[1,136,512]{2,1,0:T(8,128)(2,1)S(1)} %collective-permute-done.2.refs_6_), channel_id=1, source_target_pairs={{0,1},{1,0},{2,3},{3,2},{4,5},{5,4},{6,7},{7,6},{8,9},{9,8},{10,11... | collective-permute-start | bytes 417800 | tf_op jit(solution)/shard_map/ppermute | solution.py:67
  22.2 5.1 %collective-permute-start.11 = (bf16[1,136,512]{2,1,0:T(8,128)(2,1)S(1)}, bf16[1,136,512]{2,1,0:T(8,128)(2,1)S(1)}, u32[]{:S(2)}, u32[]{:S(2)}) collective-permute-start(bf16[1,136,512]{2,1,0:T(8,128)(2,1)S(1)} %collective-permute-done.4.refs_12_), channel_id=1, source_target_pairs={{0,2},{1,3},{2,0},{3,1},{4,6},{5,7},{6,4},{7,5},{8,10},{9,11},{10,... | collective-permute-start | bytes 417800 | tf_op jit(solution)/shard_map/ppermute | solution.py:62
  23.7 3.6 %collective-permute-start.10 = (bf16[1,136,512]{2,1,0:T(8,128)(2,1)S(1)}, bf16[1,136,512]{2,1,0:T(8,128)(2,1)S(1)}, u32[]{:S(2)}, u32[]{:S(2)}) collective-permute-start(bf16[1,136,512]{2,1,0:T(8,128)(2,1)S(1)} %collective-permute-done.4.refs_12_), channel_id=1, source_target_pairs={{0,1},{1,0},{2,3},{3,2},{4,5},{5,4},{6,7},{7,6},{8,9},{9,8},{10,11... | collective-permute-start | bytes 417800 | tf_op jit(solution)/shard_map/ppermute | solution.py:67
  23.7 4.1 %collective-permute-start.13 = (bf16[1,136,512]{2,1,0:T(8,128)(2,1)S(1)}, bf16[1,136,512]{2,1,0:T(8,128)(2,1)S(1)}, u32[]{:S(2)}, u32[]{:S(2)}) collective-permute-start(bf16[1,136,512]{2,1,0:T(8,128)(2,1)S(1)} %collective-permute-done.1.after_ref.refs_16_), channel_id=1, source_target_pairs={{0,1},{1,0},{2,3},{3,2},{4,5},{5,4},{6,7},{7,6},{8,9},{9,8},{10,11... | collective-permute-start | bytes 417800 | tf_op jit(solution)/shard_map/ppermute | solution.py:67
  24.2 3.6 %collective-permute-start.14 = (bf16[1,136,512]{2,1,0:T(8,128)(2,1)S(1)}, bf16[1,136,512]{2,1,0:T(8,128)(2,1)S(1)}, u32[]{:S(2)}, u32[]{:S(2)}) collective-permute-start(bf16[1,136,512]{2,1,0:T(8,128)(2,1)S(1)} %collective-permute-done.6.refs_18_), channel_id=1, source_target_pairs={{0,1},{1,0},{2,3},{3,2},{4,5},{5,4},{6,7},{7,6},{8,9},{9,8},{10,11... | collective-permute-start | bytes 417800 | tf_op jit(solution)/shard_map/ppermute | solution.py:67
  24.2 3.6 %collective-permute-start.8 = (bf16[1,136,512]{2,1,0:T(8,128)(2,1)S(1)}, bf16[1,136,512]{2,1,0:T(8,128)(2,1)S(1)}, u32[]{:S(2)}, u32[]{:S(2)}) collective-permute-start(bf16[1,136,512]{2,1,0:T(8,128)(2,1)S(1)} %collective-permute-done.refs_8_), channel_id=1, source_target_pairs={{0,1},{1,0},{2,3},{3,2},{4,5},{5,4},{6,7},{7,6},{8,9},{9,8},{10,11... | collective-permute-start | bytes 417800 | tf_op jit(solution)/shard_map/ppermute | solution.py:67
  27.3 1.4 %collective-permute-start.9 = (bf16[1,136,512]{2,1,0:T(8,128)(2,1)S(1)}, bf16[1,136,512]{2,1,0:T(8,128)(2,1)S(1)}, u32[]{:S(2)}, u32[]{:S(2)}) collective-permute-start(bf16[1,136,512]{2,1,0:T(8,128)(2,1)S(1)} %collective-permute-done.5.refs_10_), channel_id=1, source_target_pairs={{0,1},{1,0},{2,3},{3,2},{4,5},{5,4},{6,7},{7,6},{8,9},{9,8},{10,11... | collective-permute-start | bytes 417800 | tf_op jit(solution)/shard_map/ppermute | solution.py:67
  27.3 1.6 %collective-permute-start.12 = (bf16[1,136,512]{2,1,0:T(8,128)(2,1)S(1)}, bf16[1,136,512]{2,1,0:T(8,128)(2,1)S(1)}, u32[]{:S(2)}, u32[]{:S(2)}) collective-permute-start(bf16[1,136,512]{2,1,0:T(8,128)(2,1)S(1)} %collective-permute-done.11.refs_14_), channel_id=1, source_target_pairs={{0,1},{1,0},{2,3},{3,2},{4,5},{5,4},{6,7},{7,6},{8,9},{9,8},{10,11... | collective-permute-start | bytes 417800 | tf_op jit(solution)/shard_map/ppermute | solution.py:67
  60.4 24.0 %copy-start = (bf16[128,512]{1,0:T(8,128)(2,1)S(1)}, bf16[128,512]{1,0:T(8,128)(2,1)}, u32[]{:S(2)}) copy-start(bf16[128,512]{1,0:T(8,128)(2,1)} %hidden_ref.3) | copy-start | bytes 393220
  60.4 1.6 %collective-permute-start.19 = (bf16[2,1,128,512]{3,2,1,0:T(8,128)(2,1)S(1)}, bf16[2,1,128,512]{3,2,1,0:T(8,128)(2,1)S(1)}, u32[]{:S(2)}, u32[]{:S(2)}) collective-permute-start(bf16[2,1,128,512]{3,2,1,0:T(8,128)(2,1)S(1)} %get-tuple-element.51), channel_id=1, source_target_pairs={{0,1},{1,0},{2,3},{3,2},{4,5},{5,4},{6,7},{7,6},{8,9},{9,8},{10,11... | collective-permute-start | bytes 786440 | tf_op jit(solution)/shard_map/ppermute | solution.py:67
  60.8 3.0 %collective-permute-start.16 = (bf16[2,2,128,512]{3,2,1,0:T(8,128)(2,1)}, bf16[2,2,128,512]{3,2,1,0:T(8,128)(2,1)S(1)}, u32[]{:S(2)}, u32[]{:S(2)}) collective-permute-start(bf16[2,2,128,512]{3,2,1,0:T(8,128)(2,1)} %get-tuple-element.48), channel_id=1, source_target_pairs={{0,1},{1,0},{2,3},{3,2},{4,5},{5,4},{6,7},{7,6},{8,9},{9,8},{10,11... | collective-permute-start | bytes 1572872 | tf_op jit(solution)/shard_map/ppermute | solution.py:67
  61.0 2.7 %collective-permute-start.15 = (bf16[2,1,128,512]{3,2,1,0:T(8,128)(2,1)S(1)}, bf16[2,1,128,512]{3,2,1,0:T(8,128)(2,1)S(1)}, u32[]{:S(2)}, u32[]{:S(2)}) collective-permute-start(bf16[2,1,128,512]{3,2,1,0:T(8,128)(2,1)S(1)} %get-tuple-element.46), channel_id=1, source_target_pairs={{0,1},{1,0},{2,3},{3,2},{4,5},{5,4},{6,7},{7,6},{8,9},{9,8},{10,11... | collective-permute-start | bytes 786440 | tf_op jit(solution)/shard_map/ppermute | solution.py:67
  62.1 6.4 %collective-permute-start.20 = (bf16[1,128,512]{2,1,0:T(8,128)(2,1)S(1)}, bf16[1,128,512]{2,1,0:T(8,128)(2,1)S(1)}, u32[]{:S(2)}, u32[]{:S(2)}) collective-permute-start(bf16[1,128,512]{2,1,0:T(8,128)(2,1)S(1)} %slice_bitcast_fusion.3), channel_id=1, source_target_pairs={{0,2},{1,3},{2,0},{3,1},{4,6},{5,7},{6,4},{7,5},{8,10},{9,11},{10,... | collective-permute-start | bytes 393224 | tf_op jit(solution)/shard_map/ppermute | solution.py:62
  63.9 10.6 %collective-permute-start.17 = (bf16[2,128,512]{2,1,0:T(8,128)(2,1)S(1)}, bf16[2,128,512]{2,1,0:T(8,128)(2,1)S(1)}, u32[]{:S(2)}, u32[]{:S(2)}) collective-permute-start(bf16[2,128,512]{2,1,0:T(8,128)(2,1)S(1)} %slice_bitcast_fusion.1), channel_id=1, source_target_pairs={{0,2},{1,3},{2,0},{3,1},{4,6},{5,7},{6,4},{7,5},{8,10},{9,11},{10,... | collective-permute-start | bytes 786440 | tf_op jit(solution)/shard_map/ppermute | solution.py:62
  68.6 6.0 %collective-permute-start.21 = (bf16[152,512]{1,0:T(8,128)(2,1)S(1)}, bf16[152,512]{1,0:T(8,128)(2,1)S(1)}, u32[]{:S(2)}, u32[]{:S(2)}) collective-permute-start(bf16[152,512]{1,0:T(8,128)(2,1)S(1)} %pad_maximum_fusion.1), channel_id=1, source_target_pairs={{0,12},{4,0},{8,4},{12,8},{1,13},{5,1},{9,5},{13,9},{2,14},{6,2},{... | collective-permute-start | bytes 466952 | tf_op jit(solution)/shard_map/ppermute | solution.py:57
  74.7 8.4 %collective-permute-start.23 = (bf16[152,512]{1,0:T(8,128)(2,1)S(1)}, bf16[152,512]{1,0:T(8,128)(2,1)S(1)}, u32[]{:S(2)}, u32[]{:S(2)}) collective-permute-start(bf16[152,512]{1,0:T(8,128)(2,1)S(1)} %pad_maximum_fusion.2), channel_id=1, source_target_pairs={{0,4},{4,8},{8,12},{12,0},{1,5},{5,9},{9,13},{13,1},{2,6},{6,10},{... | collective-permute-start | bytes 466952 | tf_op jit(solution)/shard_map/ppermute | solution.py:57
  74.7 5.0 %collective-permute-start.18 = (bf16[1,128,512]{2,1,0:T(8,128)(2,1)S(1)}, bf16[1,128,512]{2,1,0:T(8,128)(2,1)S(1)}, u32[]{:S(2)}, u32[]{:S(2)}) collective-permute-start(bf16[1,128,512]{2,1,0:T(8,128)(2,1)S(1)} %slice_bitcast_fusion.6), channel_id=1, source_target_pairs={{0,2},{1,3},{2,0},{3,1},{4,6},{5,7},{6,4},{7,5},{8,10},{9,11},{10,... | collective-permute-start | bytes 393224 | tf_op jit(solution)/shard_map/ppermute | solution.py:62
  75.9 8.5 %collective-permute-start.22 = (bf16[176,512]{1,0:T(8,128)(2,1)S(1)}, bf16[176,512]{1,0:T(8,128)(2,1)S(1)}, u32[]{:S(2)}, u32[]{:S(2)}) collective-permute-start(bf16[176,512]{1,0:T(8,128)(2,1)S(1)} %pad_maximum_fusion), channel_id=1, source_target_pairs={{0,12},{4,0},{8,4},{12,8},{1,13},{5,1},{9,5},{13,9},{2,14},{6,2},{... | collective-permute-start | bytes 540680 | tf_op jit(solution)/shard_map/ppermute | solution.py:57

commit v8 on v6

--- a/solution.py
+++ b/solution.py
@@ -19,7 +19,10 @@
 PAGE_FOLD = 24
 SMALL_VMEM = 4 * 1024 * 1024
 WEIGHT_SLOTS = 2
-EXPERT_VMEM = 32 * 1024 * 1024
+NORM_ROWS = 16
+UNITS = 256
+FILL_COST = 18 * 1024 * 1024
+EXPERT_VMEM = 30 * 1024 * 1024
 
 epsilon = 1e-06
 
@@ -90,6 +93,10 @@
 
 def in_hbm(*arrays):
     return [pltpu.with_memory_space_constraint(array, pltpu.HBM) for array in arrays]
+
+
+def in_vmem(*arrays):
+    return [pltpu.with_memory_space_constraint(array, pltpu.VMEM) for array in arrays]
 
 
 def packed(hidden_states, routes, gates):
@@ -153,14 +160,14 @@
 def page_fill_kernel(
     gate_up_ref, down_ref, after_ref, kv_ref, lengths_ref, owners_ref,
     gate_up_out, down_out, pages_ref,
-    sems, kv_buf, lengths_buf, owners_buf, page_sems, *, expert,
+    sems, kv_buf, lengths_buf, owners_buf, page_sems,
 ):
     small = (
         pltpu.make_async_copy(kv_ref, kv_buf, page_sems.at[0]),
         pltpu.make_async_copy(lengths_ref, lengths_buf, page_sems.at[1]),
         pltpu.make_async_copy(owners_ref, owners_buf, page_sems.at[2]),
     )
-    copies = expert_copies(gate_up_ref, down_ref, expert, gate_up_out, down_out, sems)
+    copies = expert_copies(gate_up_ref, down_ref, 0, gate_up_out, down_out, sems)
     for copy in small + copies:
         copy.start()
     for copy in small:
@@ -170,44 +177,51 @@
         copy.wait()
 
 
-def filled(gate_up_weight, down_weight, expert, after, paged=None):
+def held_shapes(down_weight):
     width = down_weight.shape[1]
     ff_part = min(FF, down_weight.shape[0])
-    hbm = pl.BlockSpec(memory_space=pltpu.HBM)
-    vmem = pl.BlockSpec(memory_space=pltpu.VMEM)
-    out_shape = [
+    return [
         pltpu.VMEM((2, ff_part, width), down_weight.dtype),
         pltpu.VMEM((ff_part, width), down_weight.dtype),
     ]
-    scratch = [pltpu.SemaphoreType.DMA((3,))]
-    operands = [gate_up_weight, down_weight, after]
-    kernel = fill_kernel
-    if paged is not None:
-        kv_rows, lengths, owners = paged
-        kernel = page_fill_kernel
-        operands += in_hbm(kv_rows, lengths, owners)
-        out_shape.append(
+
+
+def first_fill(gate_up_weight, down_weight, after, kv_rows, lengths, owners):
+    hbm = pl.BlockSpec(memory_space=pltpu.HBM)
+    vmem = pl.BlockSpec(memory_space=pltpu.VMEM)
+    return pl.pallas_call(
+        page_fill_kernel,
+        out_shape=held_shapes(down_weight)
+        + [
             jax.ShapeDtypeStruct(
                 (lengths.shape[0], PAGE_FOLD, 2 * kv_rows.shape[1]), jnp.bfloat16
             )
-        )
-        scratch += [
+        ],
+        in_specs=[hbm, hbm, pl.BlockSpec(memory_space=pl.ANY), hbm, hbm, hbm],
+        out_specs=[vmem] * 3,
+        scratch_shapes=[
+            pltpu.SemaphoreType.DMA((3,)),
             pltpu.VMEM(kv_rows.shape, kv_rows.dtype),
             pltpu.SMEM(lengths.shape, jnp.int32),
             pltpu.SMEM(owners.shape, jnp.int32),
             pltpu.SemaphoreType.DMA((3,)),
-        ]
+        ],
+        compiler_params=pltpu.CompilerParams(vmem_limit_bytes=SMALL_VMEM),
+        cost_estimate=pl.CostEstimate(flops=0, bytes_accessed=FILL_COST, transcendentals=0),
+    )(gate_up_weight, down_weight, after, *in_hbm(kv_rows, lengths, owners))
+
+
+def next_fill(gate_up_weight, down_weight, expert, after):
+    hbm = pl.BlockSpec(memory_space=pltpu.HBM)
     return pl.pallas_call(
-        functools.partial(kernel, expert=expert),
-        out_shape=out_shape,
-        in_specs=[hbm, hbm, pl.BlockSpec(memory_space=pl.ANY)] + [hbm] * (len(operands) - 3),
-        out_specs=[vmem] * len(out_shape),
-        scratch_shapes=scratch,
+        functools.partial(fill_kernel, expert=expert),
+        out_shape=held_shapes(down_weight),
+        in_specs=[hbm, hbm, pl.BlockSpec(memory_space=pl.ANY)],
+        out_specs=[pl.BlockSpec(memory_space=pltpu.VMEM)] * 2,
+        scratch_shapes=[pltpu.SemaphoreType.DMA((3,))],
         compiler_params=pltpu.CompilerParams(vmem_limit_bytes=SMALL_VMEM),
-        cost_estimate=pl.CostEstimate(
-            flops=0, bytes_accessed=6 * ff_part * width, transcendentals=0
-        ),
-    )(*operands)
+        cost_estimate=pl.CostEstimate(flops=0, bytes_accessed=FILL_COST, transcendentals=0),
+    )(gate_up_weight, down_weight, after)
 
 
 def final_kernel(hidden_ref, own_ref, down_ref, up_ref, pages_ref, mixed_ref, cache_ref):
@@ -251,16 +265,16 @@
     gain_ref, gate_up_ref, down_ref, *refs, held, capacity, parts, chips, fills,
 ):
     held_refs, refs = refs[: 2 * fills], refs[2 * fills :]
-    block_refs, out_refs = refs[: parts * chips * CORES], refs[parts * chips * CORES :]
-    out_refs, scratch = out_refs[: len(RETURNS) * CORES], out_refs[len(RETURNS) * CORES :]
+    block_refs, refs = refs[: parts * chips * CORES], refs[parts * chips * CORES :]
+    out_refs, scratch = refs[: len(RETURNS) * CORES], refs[len(RETURNS) * CORES :]
     (
-        normed_ref, pick_ref, picked_ref, slot_gate_ref, served_ref, gain_buf, gu_buf, down_buf,
-        sems, gain_sem,
+        normed_ref, pick_ref, back_ref, picked_ref, slot_gate_ref, served_ref, active_ref,
+        rank_ref, gate_ref, gain_buf, gu_buf, down_buf, sems, gain_sem,
     ) = scratch
     _, block_rows, width = block_refs[0].shape
     tok_node = block_rows - TOPK
     tokens, model_width = normed_ref.shape
-    slots = down_buf.shape[0]
+    slots, ff_part, _ = down_buf.shape
 
     def fetch(h, slot):
         return expert_copies(
@@ -280,37 +294,14 @@
         [[block_refs[(z * chips + x) * CORES + c] for c in range(CORES)] for x in range(chips)]
         for z in range(parts)
     ]
-    features = [
-        [
-            pl.ds(
-                pl.multiple_of(
-                    (lax.rem(my_x + chips - x, chips) * CORES + (my_core ^ c)) * width,
-                    width,
-                ),
-                width,
-            )
-            for c in range(CORES)
-        ]
-        for x in range(chips)
-    ]
-
-    gain_copy.wait()
+
+    def features(x, c):
+        place = lax.rem(my_x + chips - x, chips) * CORES + (my_core ^ c)
+        return pl.ds(pl.multiple_of(place * width, width), width)
+
     expert = first_expert + lax.broadcasted_iota(jnp.int32, (held, 1), 0)
     named, gate = [], []
     for z in range(parts):
-        total = jnp.zeros((tok_node, 1), jnp.float32)
-        for x in range(chips):
-            for c in range(CORES):
-                wide = blocks[z][x][c][0, :tok_node, :].astype(jnp.float32)
-                total = total + jnp.sum(wide * wide, axis=1, keepdims=True)
-        inv_scale = lax.rsqrt(total / model_width + epsilon)
-        at = pl.ds(z * tok_node, tok_node)
-        for x in range(chips):
-            for c in range(CORES):
-                wide = blocks[z][x][c][0, :tok_node, :].astype(jnp.float32)
-                normed_ref[at, features[x][c]] = (
-                    wide * inv_scale * gain_buf[:, features[x][c]]
-                ).astype(jnp.bfloat16)
         choices = blocks[z][0][0][0, tok_node:, :].astype(jnp.float32)
         number = choices[:, :tok_node].astype(jnp.int32)
         value = (
@@ -326,9 +317,8 @@
             node_gate = node_gate + jnp.where(match, value[choice : choice + 1, :], 0.0)
         named.append(node_named)
         gate.append(node_gate)
-
     named = jnp.concatenate(named, axis=1)
-    gate = jnp.concatenate(gate, axis=1)
+    gate_ref[...] = jnp.concatenate(gate, axis=1)
     earlier = (
         lax.broadcasted_iota(jnp.int32, (tokens, tokens), 0)
         < lax.broadcasted_iota(jnp.int32, (tokens, tokens), 1)
@@ -338,33 +328,79 @@
         jnp.where(earlier, 1.0, 0.0).astype(jnp.bfloat16),
         preferred_element_type=jnp.float32,
     )
-    rank = jnp.where(named > 0.0, rank, -1.0).astype(jnp.int32)
-    slot_number = lax.broadcasted_iota(jnp.int32, (capacity, tokens), 0)
-    for h in range(held):
-        here = rank[h : h + 1, :] == slot_number
-        at = pl.ds(h * capacity, capacity)
+    rank_ref[...] = jnp.where(named > 0.0, rank, -1.0).astype(jnp.int32)
+
+    def slots_of(h, carry):
+        slot_number = lax.broadcasted_iota(jnp.int32, (capacity, tokens), 0)
+        here = rank_ref[pl.ds(h, 1), :] == slot_number
+        at = pl.ds(pl.multiple_of(h * capacity, capacity), capacity)
         pick_ref[at, :] = jnp.where(here, 1.0, 0.0).astype(jnp.bfloat16)
         slot_gate_ref[at, :] = jnp.sum(
-            jnp.where(here, gate[h : h + 1, :], 0.0), axis=1, keepdims=True
+            jnp.where(here, gate_ref[pl.ds(h, 1), :], 0.0), axis=1, keepdims=True
         )
-    for first in range(0, model_width, width):
-        part = slice(first, first + width)
+        return carry
+
+    lax.fori_loop(0, held, slots_of, 0)
+    back_ref[...] = pick_ref[...].T
+
+    gain_copy.wait()
+    for z in range(parts):
+
+        def some_rows(i, carry):
+            at = pl.ds(pl.multiple_of(i * NORM_ROWS, NORM_ROWS), NORM_ROWS)
+            wide = [
+                [blocks[z][x][c][0, at, :].astype(jnp.float32) for c in range(CORES)]
+                for x in range(chips)
+            ]
+            total = sum(
+                jnp.sum(part * part, axis=1, keepdims=True) for row in wide for part in row
+            )
+            inv_scale = lax.rsqrt(total / model_width + epsilon)
+            into = pl.ds(pl.multiple_of(z * tok_node + i * NORM_ROWS, NORM_ROWS), NORM_ROWS)
+            for x in range(chips):
+                for c in range(CORES):
+                    normed_ref[into, features(x, c)] = (
+                        wide[x][c] * inv_scale * gain_buf[:, features(x, c)]
+                    ).astype(jnp.bfloat16)
+            return carry
+
+        lax.fori_loop(0, tok_node // NORM_ROWS, some_rows, 0)
+
+    def gathered(i, carry):
+        part = pl.ds(pl.multiple_of(i * width, width), width)
         picked_ref[:, part] = jnp.dot(
             pick_ref[...], normed_ref[:, part], preferred_element_type=jnp.float32
         ).astype(jnp.bfloat16)
+        return carry
+
+    lax.fori_loop(0, model_width // width, gathered, 0)
 
     def one_expert(at, gate_up, down):
-        picked = picked_ref[at, :]
-        along = (((1,), (1,)), ((), ()))
-        gate_part = lax.dot_general(
-            picked, gate_up[0], along, preferred_element_type=jnp.float32
-        )
-        up_part = lax.dot_general(
-            picked, gate_up[1], along, preferred_element_type=jnp.float32
-        )
-        activated = (jax.nn.silu(gate_part) * up_part).astype(jnp.bfloat16)
-        served = jnp.dot(activated, down[...], preferred_element_type=jnp.float32)
-        served_ref[at, :] = (served * slot_gate_ref[at, :]).astype(jnp.bfloat16)
+        def some_units(i, carry):
+            units = pl.ds(pl.multiple_of(i * UNITS, UNITS), UNITS)
+            along = (((1,), (1,)), ((), ()))
+            picked = picked_ref[at, :]
+            gate_part = lax.dot_general(
+                gate_up[0, units, :], picked, along, preferred_element_type=jnp.float32
+            )
+            up_part = lax.dot_general(
+                gate_up[1, units, :], picked, along, preferred_element_type=jnp.float32
+            )
+            active_ref[units, :] = (jax.nn.silu(gate_part) * up_part).astype(jnp.bfloat16)
+            return carry
+
+        lax.fori_loop(0, ff_part // UNITS, some_units, 0)
+
+        def some_columns(i, carry):
+            part = pl.ds(pl.multiple_of(i * width, width), width)
+            served = lax.dot_general(
+                active_ref[...], down[:, part], (((0,), (0,)), ((), ())),
+                preferred_element_type=jnp.float32,
+            )
+            served_ref[at, part] = (served * slot_gate_ref[at, :]).astype(jnp.bfloat16)
+            return carry
+
+        lax.fori_loop(0, model_width // width, some_columns, 0)
 
     for h in range(fills):
         one_expert(pl.ds(h * capacity, capacity), held_refs[2 * h], held_refs[2 * h + 1])
@@ -385,17 +421,20 @@
 
     lax.fori_loop(fills, held, streamed, 0)
 
-    back = pick_ref[...].T
-    for x in range(chips):
-        for c in range(CORES):
+    for c in range(CORES):
+
+        def scattered(x, carry):
             summed = jnp.dot(
-                back, served_ref[:, features[x][c]], preferred_element_type=jnp.float32
+                back_ref[...], served_ref[:, features(x, c)], preferred_element_type=jnp.float32
             ).astype(jnp.bfloat16)
             for group, members in enumerate(RETURNS):
                 for i, z in enumerate(members):
                     out_refs[group * CORES + c][x, i] = summed[
                         z * tok_node : (z + 1) * tok_node, :
                     ]
+            return carry
+
+        lax.fori_loop(0, chips, scattered, 0)
 
 
 def expert_sums(gain, gate_up_weight, down_weight, held_weights, blocks):
@@ -406,13 +445,13 @@
     model_width = chips * CORES * width
     ff_dev = down_weight.shape[0]
     held = max(1, ff_dev // FF)
+    ff_part = ff_dev // held
     capacity = CAP * parts
-    ff_part = ff_dev // held
     all_slots = held * capacity
     vmem = pl.BlockSpec(memory_space=pltpu.VMEM)
     hbm = pl.BlockSpec(memory_space=pltpu.HBM)
-    held_weights = [pltpu.with_memory_space_constraint(w, pltpu.VMEM) for w in held_weights]
     flat = [blocks[z][x][c] for z in range(parts) for x in range(chips) for c in range(CORES)]
+    outs = len(RETURNS) * CORES
     sums = pl.pallas_call(
         functools.partial(
             expert_kernel, held=held, capacity=capacity, parts=parts, chips=chips,
@@ -424,13 +463,17 @@
             for _ in range(CORES)
         ],
         in_specs=[hbm] * 3 + [vmem] * (len(held_weights) + len(flat)),
-        out_specs=[vmem] * (len(RETURNS) * CORES),
+        out_specs=[vmem] * outs,
         scratch_shapes=[
             pltpu.VMEM((tokens, model_width), jnp.bfloat16),
             pltpu.VMEM((all_slots, tokens), jnp.bfloat16),
+            pltpu.VMEM((tokens, all_slots), jnp.bfloat16),
             pltpu.VMEM((all_slots, model_width), jnp.bfloat16),
             pltpu.VMEM((all_slots, 1), jnp.float32),
             pltpu.VMEM((all_slots, model_width), jnp.bfloat16),
+            pltpu.VMEM((ff_part, capacity), jnp.bfloat16),
+            pltpu.VMEM((held, tokens), jnp.int32),
+            pltpu.VMEM((held, tokens), jnp.float32),
             pltpu.VMEM((1, model_width), jnp.float32),
             pltpu.VMEM((WEIGHT_SLOTS, 2, ff_part, model_width), jnp.bfloat16),
             pltpu.VMEM((WEIGHT_SLOTS, ff_part, model_width), jnp.bfloat16),
@@ -439,11 +482,11 @@
         ],
         compiler_params=pltpu.CompilerParams(vmem_limit_bytes=EXPERT_VMEM),
         cost_estimate=pl.CostEstimate(
-            flops=6 * all_slots * (ff_dev // held) * model_width,
+            flops=6 * all_slots * ff_part * model_width,
             bytes_accessed=6 * ff_dev * model_width,
             transcendentals=0,
         ),
-    )(*in_hbm(gain), gate_up_weight, down_weight, *held_weights, *flat)
+    )(*in_hbm(gain), gate_up_weight, down_weight, *in_vmem(*held_weights), *flat)
     return [sums[g * CORES : (g + 1) * CORES] for g in range(len(RETURNS))]
 
 
@@ -533,13 +576,13 @@
 
     by_z = {0: block, 1: shift_dp(block, 1), 3: shift_dp(block, -1)}
     own_x = [shift_x(block, s) for s in range(1, chips)]
-    *held_a, pages = filled(gate_up_weight, down_weight, 0, block, (kv_rows, lengths, owners))
+    *weights, pages = first_fill(gate_up_weight, down_weight, block, kv_rows, lengths, owners)
     own_core = [other_core(block)]
-    by_z, own_x, own_core, held_a = lax.optimization_barrier((by_z, own_x, own_core, held_a))
+    by_z, own_x, own_core, weights = lax.optimization_barrier((by_z, own_x, own_core, weights))
     by_z[2] = shift_dp(by_z[1], 1)
     chip_rows = {z: [by_z[z]] + [shift_x(by_z[z], s) for s in range(1, chips)] for z in (1, 3)}
-    held_b = filled(gate_up_weight, down_weight, 1, by_z[3])
-    by_z[2], chip_rows, held_b = lax.optimization_barrier((by_z[2], chip_rows, held_b))
+    weights += next_fill(gate_up_weight, down_weight, 1, by_z[3])
+    by_z[2], chip_rows, weights = lax.optimization_barrier((by_z[2], chip_rows, weights))
     chip_rows[0] = [block] + own_x
     chip_rows[2] = [by_z[2]] + [shift_x(by_z[2], s) for s in range(1, chips)]
     own_core += [other_core(value) for value in own_x]
@@ -547,9 +590,7 @@
     blocks += [
         [(value, other_core(value)) for value in chip_rows[z]] for z in range(1, node_count)
     ]
-    sums = expert_sums(
-        norm_gain[None, :], gate_up_weight, down_weight, [*held_a, *held_b], blocks
-    )
+    sums = expert_sums(norm_gain[None, :], gate_up_weight, down_weight, weights, blocks)
 
     over = [other_core(send) for _, send in sums]
     chip_sums = [added(keep, came) for (keep, _), came in zip(sums, over)]

time: 86.4 us -> 93.2 us (1.079)
  Pallas kernels: 41.9 us -> 48.7 us
    pallas_call x1, Pallas kernels: 32.6 us -> 39.4 us  [expert_sums(): pl.pallas_call(functools.partial(expert_kernel, held=held, capacity=capac...]
  transfers between devices with their start and end apart: 24 -> 24, of which waited for: 13 -> 13; matrix products, arithmetic and copies ran while one was open for 1% -> 1% of each run, Pallas kernels for 9% -> 8%
where the time goes in v8:
time: 93.2 us; the launch traced here: 93 us
  Pallas kernels  48.7 us (52%)
  starting transfers between devices  24.2 us (26%)
  waiting for transfers between devices  18.7 us (20%)
    pallas_call x1, Pallas kernels, expert_sums(): pl.pallas_call(functools.partial(expert_kernel, held=held, capacity=capac...  39.4 us
    ppermute x6, starting transfers between devices, shift_dp(): lax.ppermute(value, 'dp', [(i, (i + shift) % count) for i in range(count)])  12.8 us
    ppermute x7, starting transfers between devices, shift_x(): lax.ppermute(value, 'mp', [(i, (i + CORES * shift) % count) for i in rang...  8.9 us
    ppermute x6, waiting for transfers between devices, shift_dp(): lax.ppermute(value, 'dp', [(i, (i + shift) % count) for i in range(count)])  8.69 us
    ppermute x7, waiting for transfers between devices, shift_x(): lax.ppermute(value, 'mp', [(i, (i + CORES * shift) % count) for i in rang...  8.22 us
    pallas_call x1, Pallas kernels, first_fill(): pl.pallas_call(page_fill_kernel, out_shape=held_shapes(down_weight) + [ja...  3.84 us
    pallas_call x1, Pallas kernels, next_fill(): pl.pallas_call(functools.partial(fill_kernel, expert=expert), out_shape=h...  3.78 us
    ppermute x11, starting transfers between devices, other_core(): return lax.ppermute(value, 'mp', [(i, i ^ 1) for i in range(count)])  2.5 us
  transfers between devices with their start and end apart: 24, of which 13 were waited for; matrix products, arithmetic and copies ran while one was open for 1% of the time, Pallas kernels for 8%

profile of v8, /device:TPU:0, one launch (start us, length us, event | category | flops | bytes accessed | tf_op | source)
XLA Modules:
  0.0 93.0 jit_solution(13189242727903602010)
XLA Ops:
  0.6 1.0 %shard_map.104.after_ref.refs_4_ = bf16[1,136,512]{2,1,0:T(8,128)(2,1)S(1)} custom-call(bf16[128,512]{1,0:T(8,128)(2,1)} %hidden_ref.3, s32[8,128]{1,0:T(8,128)} %bitcast.42, f32[8,128]{1,0:T(8,128)} %bitcast.43), custom_call_target="tpu_custom_call" | custom-call | tf_op jit(solution)/shard_map/pallas_call | solution.py:105
  1.6 3.1 %collective-permute-start = (bf16[1,136,512]{2,1,0:T(8,128)(2,1)S(1)}, bf16[1,136,512]{2,1,0:T(8,128)(2,1)S(1)}, u32[]{:S(2)}, u32[]{:S(2)}) collective-permute-start(bf16[1,136,512]{2,1,0:T(8,128)(2,1)S(1)} %shard_map.104.after_ref.refs_4_), channel_id=1, source_target_pairs={{0,4},{4,8},{8,12},{12,0},{1,5},{5,9},{9,13},{13,1},{2,6},{6,10},{... | collective-permute-start | bytes 417800 | tf_op jit(solution)/shard_map/ppermute | solution.py:60
  4.7 2.1 %collective-permute-start.1 = (bf16[1,136,512]{2,1,0:T(8,128)(2,1)S(1)}, bf16[1,136,512]{2,1,0:T(8,128)(2,1)S(1)}, u32[]{:S(2)}, u32[]{:S(2)}) collective-permute-start(bf16[1,136,512]{2,1,0:T(8,128)(2,1)S(1)} %shard_map.104.after_ref.refs_4_), channel_id=1, source_target_pairs={{0,12},{4,0},{8,4},{12,8},{1,13},{5,1},{9,5},{13,9},{2,14},{6,2},{... | collective-permute-start | bytes 417800 | tf_op jit(solution)/shard_map/ppermute | solution.py:60
  6.8 1.6 %collective-permute-start.2 = (bf16[1,136,512]{2,1,0:T(8,128)(2,1)S(1)}, bf16[1,136,512]{2,1,0:T(8,128)(2,1)S(1)}, u32[]{:S(2)}, u32[]{:S(2)}) collective-permute-start(bf16[1,136,512]{2,1,0:T(8,128)(2,1)S(1)} %shard_map.104.after_ref.refs_4_), channel_id=1, source_target_pairs={{0,2},{1,3},{2,0},{3,1},{4,6},{5,7},{6,4},{7,5},{8,10},{9,11},{10,... | collective-permute-start | bytes 417800 | tf_op jit(solution)/shard_map/ppermute | solution.py:65
  8.4 3.8 %shard_map.105 = (bf16[2,768,2048]{2,1,0:T(8,128)(2,1)S(1)}, bf16[768,2048]{1,0:T(8,128)(2,1)S(1)}, bf16[4,24,512]{2,1,0:T(8,128)(2,1)S(1)}) custom-call(bf16[2,6144,2048]{2,1,0:T(8,128)(2,1)} %gate_up_ref.5, bf16[6144,2048]{1,0:T(8,128)(2,1)} %down_ref.5, bf16[1,136,512]{2,1,0:T(8,128)(2,1)S(1)} %shard_map.104.after_ref.refs_4_, bf16[128,256]{1,0:T(8,128)(2,1)} %kv_ref.1, ...), custom_call_target="tpu_custom_call" | custom-call | bytes 18874368 | tf_op jit(solution)/shard_map/pallas_call | solution.py:192
  12.3 0.5 collective-permute-done.1.after_ref.refs_16_
  12.8 1.1 %collective-permute-start.4 = (bf16[1,136,512]{2,1,0:T(8,128)(2,1)S(1)}, bf16[1,136,512]{2,1,0:T(8,128)(2,1)S(1)}, u32[]{:S(2)}, u32[]{:S(2)}) collective-permute-start(bf16[1,136,512]{2,1,0:T(8,128)(2,1)S(1)} %collective-permute-done.refs_8_), channel_id=1, source_target_pairs={{0,4},{4,8},{8,12},{12,0},{1,5},{5,9},{9,13},{13,1},{2,6},{6,10},{... | collective-permute-start | bytes 417800 | tf_op jit(solution)/shard_map/ppermute | solution.py:60
  13.9 1.5 %collective-permute-start.5 = (bf16[1,136,512]{2,1,0:T(8,128)(2,1)S(1)}, bf16[1,136,512]{2,1,0:T(8,128)(2,1)S(1)}, u32[]{:S(2)}, u32[]{:S(2)}) collective-permute-start(bf16[1,136,512]{2,1,0:T(8,128)(2,1)S(1)} %collective-permute-done.refs_8_), channel_id=1, source_target_pairs={{0,2},{1,3},{2,0},{3,1},{4,6},{5,7},{6,4},{7,5},{8,10},{9,11},{10,... | collective-permute-start | bytes 417800 | tf_op jit(solution)/shard_map/ppermute | solution.py:65
  15.4 0.5 collective-permute-start.6
  16.0 3.8 %shard_map.106 = (bf16[2,768,2048]{2,1,0:T(8,128)(2,1)S(1)}, bf16[768,2048]{1,0:T(8,128)(2,1)S(1)}) custom-call(bf16[2,6144,2048]{2,1,0:T(8,128)(2,1)} %gate_up_ref.5, bf16[6144,2048]{1,0:T(8,128)(2,1)} %down_ref.5, bf16[1,136,512]{2,1,0:T(8,128)(2,1)S(1)} %collective-permute-done.1.after_ref.refs_16_), custom_call_target="tpu_custom_call" | custom-call | bytes 18874368 | tf_op jit(solution)/shard_map/pallas_call | solution.py:216
  19.8 0.4 collective-permute-done.4.refs_12_
  20.5 1.7 %collective-permute-done.6.refs_18_ = bf16[1,136,512]{2,1,0:T(8,128)(2,1)S(1)} collective-permute-done((bf16[1,136,512]{2,1,0:T(8,128)(2,1)S(1)}, bf16[1,136,512]{2,1,0:T(8,128)(2,1)S(1)}, u32[]{:S(2)}, u32[]{:S(2)}) %collective-permute-start.6) | collective-permute-done | bytes 139296 | tf_op jit(solution)/shard_map/ppermute | solution.py:65
  22.2 1.5 %collective-permute-start.11 = (bf16[1,136,512]{2,1,0:T(8,128)(2,1)S(1)}, bf16[1,136,512]{2,1,0:T(8,128)(2,1)S(1)}, u32[]{:S(2)}, u32[]{:S(2)}) collective-permute-start(bf16[1,136,512]{2,1,0:T(8,128)(2,1)S(1)} %collective-permute-done.4.refs_12_), channel_id=1, source_target_pairs={{0,2},{1,3},{2,0},{3,1},{4,6},{5,7},{6,4},{7,5},{8,10},{9,11},{10,... | collective-permute-start | bytes 417800 | tf_op jit(solution)/shard_map/ppermute | solution.py:65
  23.7 0.5 collective-permute-start.13
  24.2 0.5 collective-permute-start.8
  24.7 2.5 %collective-permute-done.11.refs_14_ = bf16[1,136,512]{2,1,0:T(8,128)(2,1)S(1)} collective-permute-done((bf16[1,136,512]{2,1,0:T(8,128)(2,1)S(1)}, bf16[1,136,512]{2,1,0:T(8,128)(2,1)S(1)}, u32[]{:S(2)}, u32[]{:S(2)}) %collective-permute-start.11) | collective-permute-done | bytes 139296 | tf_op jit(solution)/shard_map/ppermute | solution.py:65
  27.3 0.5 collective-permute-start.12
  27.8 0.8 collective-permute-done.9.refs_11_
  28.8 39.4 %shard_map.107 = (bf16[2,1,128,512]{3,2,1,0:T(8,128)(2,1)S(1)}, bf16[2,1,128,512]{3,2,1,0:T(8,128)(2,1)S(1)}, bf16[2,2,128,512]{3,2,1,0:T(8,128)(2,1)S(1)}, bf16...) custom-call(f32[1,2048]{1,0:T(1,128)} %bitcast.41, ...), custom_call_target="tpu_custom_call" | custom-call | flops 4831838208 | bytes 75497472 | tf_op jit(solution)/shard_map/pallas_call | solution.py:455
  68.3 0.4 collective-permute-start.19
  68.9 0.3 collective-permute-start.15
  69.2 0.7 collective-permute-done.19
  70.0 1.6 %collective-permute-start.20 = (bf16[1,128,512]{2,1,0:T(8,128)(2,1)S(1)}, bf16[1,128,512]{2,1,0:T(8,128)(2,1)S(1)}, u32[]{:S(2)}, u32[]{:S(2)}) collective-permute-start(bf16[1,128,512]{2,1,0:T(8,128)(2,1)S(1)} %slice_bitcast_fusion.3), channel_id=1, source_target_pairs={{0,2},{1,3},{2,0},{3,1},{4,6},{5,7},{6,4},{7,5},{8,10},{9,11},{10,... | collective-permute-start | bytes 393224 | tf_op jit(solution)/shard_map/ppermute | solution.py:65
  71.8 1.0 %collective-permute-start.17 = (bf16[2,128,512]{2,1,0:T(8,128)(2,1)S(1)}, bf16[2,128,512]{2,1,0:T(8,128)(2,1)S(1)}, u32[]{:S(2)}, u32[]{:S(2)}) collective-permute-start(bf16[2,128,512]{2,1,0:T(8,128)(2,1)S(1)} %slice_bitcast_fusion.1), channel_id=1, source_target_pairs={{0,2},{1,3},{2,0},{3,1},{4,6},{5,7},{6,4},{7,5},{8,10},{9,11},{10,... | collective-permute-start | bytes 786440 | tf_op jit(solution)/shard_map/ppermute | solution.py:65
  72.8 3.5 %collective-permute-done.20 = bf16[1,128,512]{2,1,0:T(8,128)(2,1)S(1)} collective-permute-done((bf16[1,128,512]{2,1,0:T(8,128)(2,1)S(1)}, bf16[1,128,512]{2,1,0:T(8,128)(2,1)S(1)}, u32[]{:S(2)}, u32[]{:S(2)}) %collective-permute-start.20) | collective-permute-done | bytes 131104 | tf_op jit(solution)/shard_map/ppermute | solution.py:65
  76.4 2.8 %collective-permute-start.21 = (bf16[152,512]{1,0:T(8,128)(2,1)S(1)}, bf16[152,512]{1,0:T(8,128)(2,1)S(1)}, u32[]{:S(2)}, u32[]{:S(2)}) collective-permute-start(bf16[152,512]{1,0:T(8,128)(2,1)S(1)} %pad_maximum_fusion.1), channel_id=1, source_target_pairs={{0,12},{4,0},{8,4},{12,8},{1,13},{5,1},{9,5},{13,9},{2,14},{6,2},{... | collective-permute-start | bytes 466952 | tf_op jit(solution)/shard_map/ppermute | solution.py:60
  79.2 3.2 %collective-permute-done.21 = bf16[152,512]{1,0:T(8,128)(2,1)S(1)} collective-permute-done((bf16[152,512]{1,0:T(8,128)(2,1)S(1)}, bf16[152,512]{1,0:T(8,128)(2,1)S(1)}, u32[]{:S(2)}, u32[]{:S(2)}) %collective-permute-start.21) | collective-permute-done | bytes 155680 | tf_op jit(solution)/shard_map/ppermute | solution.py:60
  82.6 1.2 %collective-permute-start.18 = (bf16[1,128,512]{2,1,0:T(8,128)(2,1)S(1)}, bf16[1,128,512]{2,1,0:T(8,128)(2,1)S(1)}, u32[]{:S(2)}, u32[]{:S(2)}) collective-permute-start(bf16[1,128,512]{2,1,0:T(8,128)(2,1)S(1)} %slice_bitcast_fusion.6), channel_id=1, source_target_pairs={{0,2},{1,3},{2,0},{3,1},{4,6},{5,7},{6,4},{7,5},{8,10},{9,11},{10,... | collective-permute-start | bytes 393224 | tf_op jit(solution)/shard_map/ppermute | solution.py:65
  83.8 3.7 %collective-permute-start.22 = (bf16[176,512]{1,0:T(8,128)(2,1)S(1)}, bf16[176,512]{1,0:T(8,128)(2,1)S(1)}, u32[]{:S(2)}, u32[]{:S(2)}) collective-permute-start(bf16[176,512]{1,0:T(8,128)(2,1)S(1)} %pad_maximum_fusion), channel_id=1, source_target_pairs={{0,12},{4,0},{8,4},{12,8},{1,13},{5,1},{9,5},{13,9},{2,14},{6,2},{... | collective-permute-start | bytes 540680 | tf_op jit(solution)/shard_map/ppermute | solution.py:60
  87.7 3.2 %collective-permute-done.23.up_ref = bf16[152,512]{1,0:T(8,128)(2,1)S(1)} collective-permute-done((bf16[152,512]{1,0:T(8,128)(2,1)S(1)}, bf16[152,512]{1,0:T(8,128)(2,1)S(1)}, u32[]{:S(2)}, u32[]{:S(2)}) %collective-permute-start.23) | collective-permute-done | bytes 155680 | tf_op jit(solution)/shard_map/ppermute | solution.py:60
  90.9 1.3 %collective-permute-done.22.down_ref = bf16[176,512]{1,0:T(8,128)(2,1)S(1)} collective-permute-done((bf16[176,512]{1,0:T(8,128)(2,1)S(1)}, bf16[176,512]{1,0:T(8,128)(2,1)S(1)}, u32[]{:S(2)}, u32[]{:S(2)}) %collective-permute-start.22) | collective-permute-done | bytes 180256 | tf_op jit(solution)/shard_map/ppermute | solution.py:60
  92.3 0.8 shard_map.108
  (39 shorter events, 1.5 us)
Async XLA Ops:
  1.6 10.7 %collective-permute-start = (bf16[1,136,512]{2,1,0:T(8,128)(2,1)S(1)}, bf16[1,136,512]{2,1,0:T(8,128)(2,1)S(1)}, u32[]{:S(2)}, u32[]{:S(2)}) collective-permute-start(bf16[1,136,512]{2,1,0:T(8,128)(2,1)S(1)} %shard_map.104.after_ref.refs_4_), channel_id=1, source_target_pairs={{0,4},{4,8},{8,12},{12,0},{1,5},{5,9},{9,13},{13,1},{2,6},{6,10},{... | collective-permute-start | bytes 417800 | tf_op jit(solution)/shard_map/ppermute | solution.py:60
  4.7 8.1 %collective-permute-start.1 = (bf16[1,136,512]{2,1,0:T(8,128)(2,1)S(1)}, bf16[1,136,512]{2,1,0:T(8,128)(2,1)S(1)}, u32[]{:S(2)}, u32[]{:S(2)}) collective-permute-start(bf16[1,136,512]{2,1,0:T(8,128)(2,1)S(1)} %shard_map.104.after_ref.refs_4_), channel_id=1, source_target_pairs={{0,12},{4,0},{8,4},{12,8},{1,13},{5,1},{9,5},{13,9},{2,14},{6,2},{... | collective-permute-start | bytes 417800 | tf_op jit(solution)/shard_map/ppermute | solution.py:60
  6.8 6.0 %collective-permute-start.2 = (bf16[1,136,512]{2,1,0:T(8,128)(2,1)S(1)}, bf16[1,136,512]{2,1,0:T(8,128)(2,1)S(1)}, u32[]{:S(2)}, u32[]{:S(2)}) collective-permute-start(bf16[1,136,512]{2,1,0:T(8,128)(2,1)S(1)} %shard_map.104.after_ref.refs_4_), channel_id=1, source_target_pairs={{0,2},{1,3},{2,0},{3,1},{4,6},{5,7},{6,4},{7,5},{8,10},{9,11},{10,... | collective-permute-start | bytes 417800 | tf_op jit(solution)/shard_map/ppermute | solution.py:65
  8.4 4.4 %collective-permute-start.3 = (bf16[1,136,512]{2,1,0:T(8,128)(2,1)S(1)}, bf16[1,136,512]{2,1,0:T(8,128)(2,1)S(1)}, u32[]{:S(2)}, u32[]{:S(2)}) collective-permute-start(bf16[1,136,512]{2,1,0:T(8,128)(2,1)S(1)} %shard_map.104.after_ref.refs_4_), channel_id=1, source_target_pairs={{0,1},{1,0},{2,3},{3,2},{4,5},{5,4},{6,7},{7,6},{8,9},{9,8},{10,11... | collective-permute-start | bytes 417800 | tf_op jit(solution)/shard_map/ppermute | solution.py:70
  12.8 7.4 %collective-permute-start.4 = (bf16[1,136,512]{2,1,0:T(8,128)(2,1)S(1)}, bf16[1,136,512]{2,1,0:T(8,128)(2,1)S(1)}, u32[]{:S(2)}, u32[]{:S(2)}) collective-permute-start(bf16[1,136,512]{2,1,0:T(8,128)(2,1)S(1)} %collective-permute-done.refs_8_), channel_id=1, source_target_pairs={{0,4},{4,8},{8,12},{12,0},{1,5},{5,9},{9,13},{13,1},{2,6},{6,10},{... | collective-permute-start | bytes 417800 | tf_op jit(solution)/shard_map/ppermute | solution.py:60
  13.9 6.6 %collective-permute-start.5 = (bf16[1,136,512]{2,1,0:T(8,128)(2,1)S(1)}, bf16[1,136,512]{2,1,0:T(8,128)(2,1)S(1)}, u32[]{:S(2)}, u32[]{:S(2)}) collective-permute-start(bf16[1,136,512]{2,1,0:T(8,128)(2,1)S(1)} %collective-permute-done.refs_8_), channel_id=1, source_target_pairs={{0,2},{1,3},{2,0},{3,1},{4,6},{5,7},{6,4},{7,5},{8,10},{9,11},{10,... | collective-permute-start | bytes 417800 | tf_op jit(solution)/shard_map/ppermute | solution.py:65
  15.4 6.8 %collective-permute-start.6 = (bf16[1,136,512]{2,1,0:T(8,128)(2,1)S(1)}, bf16[1,136,512]{2,1,0:T(8,128)(2,1)S(1)}, u32[]{:S(2)}, u32[]{:S(2)}) collective-permute-start(bf16[1,136,512]{2,1,0:T(8,128)(2,1)S(1)} %collective-permute-done.1.after_ref.refs_16_), channel_id=1, source_target_pairs={{0,2},{1,3},{2,0},{3,1},{4,6},{5,7},{6,4},{7,5},{8,10},{9,11},{10,... | collective-permute-start | bytes 417800 | tf_op jit(solution)/shard_map/ppermute | solution.py:65
  19.7 4.5 %collective-permute-start.7 = (bf16[1,136,512]{2,1,0:T(8,128)(2,1)S(1)}, bf16[1,136,512]{2,1,0:T(8,128)(2,1)S(1)}, u32[]{:S(2)}, u32[]{:S(2)}) collective-permute-start(bf16[1,136,512]{2,1,0:T(8,128)(2,1)S(1)} %collective-permute-done.2.refs_6_), channel_id=1, source_target_pairs={{0,1},{1,0},{2,3},{3,2},{4,5},{5,4},{6,7},{7,6},{8,9},{9,8},{10,11... | collective-permute-start | bytes 417800 | tf_op jit(solution)/shard_map/ppermute | solution.py:70
  22.2 5.1 %collective-permute-start.11 = (bf16[1,136,512]{2,1,0:T(8,128)(2,1)S(1)}, bf16[1,136,512]{2,1,0:T(8,128)(2,1)S(1)}, u32[]{:S(2)}, u32[]{:S(2)}) collective-permute-start(bf16[1,136,512]{2,1,0:T(8,128)(2,1)S(1)} %collective-permute-done.4.refs_12_), channel_id=1, source_target_pairs={{0,2},{1,3},{2,0},{3,1},{4,6},{5,7},{6,4},{7,5},{8,10},{9,11},{10,... | collective-permute-start | bytes 417800 | tf_op jit(solution)/shard_map/ppermute | solution.py:65
  23.7 3.6 %collective-permute-start.10 = (bf16[1,136,512]{2,1,0:T(8,128)(2,1)S(1)}, bf16[1,136,512]{2,1,0:T(8,128)(2,1)S(1)}, u32[]{:S(2)}, u32[]{:S(2)}) collective-permute-start(bf16[1,136,512]{2,1,0:T(8,128)(2,1)S(1)} %collective-permute-done.4.refs_12_), channel_id=1, source_target_pairs={{0,1},{1,0},{2,3},{3,2},{4,5},{5,4},{6,7},{7,6},{8,9},{9,8},{10,11... | collective-permute-start | bytes 417800 | tf_op jit(solution)/shard_map/ppermute | solution.py:70
  23.7 4.1 %collective-permute-start.13 = (bf16[1,136,512]{2,1,0:T(8,128)(2,1)S(1)}, bf16[1,136,512]{2,1,0:T(8,128)(2,1)S(1)}, u32[]{:S(2)}, u32[]{:S(2)}) collective-permute-start(bf16[1,136,512]{2,1,0:T(8,128)(2,1)S(1)} %collective-permute-done.1.after_ref.refs_16_), channel_id=1, source_target_pairs={{0,1},{1,0},{2,3},{3,2},{4,5},{5,4},{6,7},{7,6},{8,9},{9,8},{10,11... | collective-permute-start | bytes 417800 | tf_op jit(solution)/shard_map/ppermute | solution.py:70
  24.2 3.6 %collective-permute-start.14 = (bf16[1,136,512]{2,1,0:T(8,128)(2,1)S(1)}, bf16[1,136,512]{2,1,0:T(8,128)(2,1)S(1)}, u32[]{:S(2)}, u32[]{:S(2)}) collective-permute-start(bf16[1,136,512]{2,1,0:T(8,128)(2,1)S(1)} %collective-permute-done.6.refs_18_), channel_id=1, source_target_pairs={{0,1},{1,0},{2,3},{3,2},{4,5},{5,4},{6,7},{7,6},{8,9},{9,8},{10,11... | collective-permute-start | bytes 417800 | tf_op jit(solution)/shard_map/ppermute | solution.py:70
  24.2 3.6 %collective-permute-start.8 = (bf16[1,136,512]{2,1,0:T(8,128)(2,1)S(1)}, bf16[1,136,512]{2,1,0:T(8,128)(2,1)S(1)}, u32[]{:S(2)}, u32[]{:S(2)}) collective-permute-start(bf16[1,136,512]{2,1,0:T(8,128)(2,1)S(1)} %collective-permute-done.refs_8_), channel_id=1, source_target_pairs={{0,1},{1,0},{2,3},{3,2},{4,5},{5,4},{6,7},{7,6},{8,9},{9,8},{10,11... | collective-permute-start | bytes 417800 | tf_op jit(solution)/shard_map/ppermute | solution.py:70
  27.3 1.4 %collective-permute-start.9 = (bf16[1,136,512]{2,1,0:T(8,128)(2,1)S(1)}, bf16[1,136,512]{2,1,0:T(8,128)(2,1)S(1)}, u32[]{:S(2)}, u32[]{:S(2)}) collective-permute-start(bf16[1,136,512]{2,1,0:T(8,128)(2,1)S(1)} %collective-permute-done.5.refs_10_), channel_id=1, source_target_pairs={{0,1},{1,0},{2,3},{3,2},{4,5},{5,4},{6,7},{7,6},{8,9},{9,8},{10,11... | collective-permute-start | bytes 417800 | tf_op jit(solution)/shard_map/ppermute | solution.py:70
  27.3 1.6 %collective-permute-start.12 = (bf16[1,136,512]{2,1,0:T(8,128)(2,1)S(1)}, bf16[1,136,512]{2,1,0:T(8,128)(2,1)S(1)}, u32[]{:S(2)}, u32[]{:S(2)}) collective-permute-start(bf16[1,136,512]{2,1,0:T(8,128)(2,1)S(1)} %collective-permute-done.11.refs_14_), channel_id=1, source_target_pairs={{0,1},{1,0},{2,3},{3,2},{4,5},{5,4},{6,7},{7,6},{8,9},{9,8},{10,11... | collective-permute-start | bytes 417800 | tf_op jit(solution)/shard_map/ppermute | solution.py:70
  68.3 24.0 %copy-start = (bf16[128,512]{1,0:T(8,128)(2,1)S(1)}, bf16[128,512]{1,0:T(8,128)(2,1)}, u32[]{:S(2)}) copy-start(bf16[128,512]{1,0:T(8,128)(2,1)} %hidden_ref.3) | copy-start | bytes 393220
  68.3 1.6 %collective-permute-start.19 = (bf16[2,1,128,512]{3,2,1,0:T(8,128)(2,1)S(1)}, bf16[2,1,128,512]{3,2,1,0:T(8,128)(2,1)S(1)}, u32[]{:S(2)}, u32[]{:S(2)}) collective-permute-start(bf16[2,1,128,512]{3,2,1,0:T(8,128)(2,1)S(1)} %get-tuple-element.55), channel_id=1, source_target_pairs={{0,1},{1,0},{2,3},{3,2},{4,5},{5,4},{6,7},{7,6},{8,9},{9,8},{10,11... | collective-permute-start | bytes 786440 | tf_op jit(solution)/shard_map/ppermute | solution.py:70
  68.7 3.0 %collective-permute-start.16 = (bf16[2,2,128,512]{3,2,1,0:T(8,128)(2,1)S(1)}, bf16[2,2,128,512]{3,2,1,0:T(8,128)(2,1)S(1)}, u32[]{:S(2)}, u32[]{:S(2)}) collective-permute-start(bf16[2,2,128,512]{3,2,1,0:T(8,128)(2,1)S(1)} %get-tuple-element.52), channel_id=1, source_target_pairs={{0,1},{1,0},{2,3},{3,2},{4,5},{5,4},{6,7},{7,6},{8,9},{9,8},{10,11... | collective-permute-start | bytes 1572872 | tf_op jit(solution)/shard_map/ppermute | solution.py:70
  68.9 2.7 %collective-permute-start.15 = (bf16[2,1,128,512]{3,2,1,0:T(8,128)(2,1)S(1)}, bf16[2,1,128,512]{3,2,1,0:T(8,128)(2,1)S(1)}, u32[]{:S(2)}, u32[]{:S(2)}) collective-permute-start(bf16[2,1,128,512]{3,2,1,0:T(8,128)(2,1)S(1)} %get-tuple-element.50), channel_id=1, source_target_pairs={{0,1},{1,0},{2,3},{3,2},{4,5},{5,4},{6,7},{7,6},{8,9},{9,8},{10,11... | collective-permute-start | bytes 786440 | tf_op jit(solution)/shard_map/ppermute | solution.py:70
  70.0 6.4 %collective-permute-start.20 = (bf16[1,128,512]{2,1,0:T(8,128)(2,1)S(1)}, bf16[1,128,512]{2,1,0:T(8,128)(2,1)S(1)}, u32[]{:S(2)}, u32[]{:S(2)}) collective-permute-start(bf16[1,128,512]{2,1,0:T(8,128)(2,1)S(1)} %slice_bitcast_fusion.3), channel_id=1, source_target_pairs={{0,2},{1,3},{2,0},{3,1},{4,6},{5,7},{6,4},{7,5},{8,10},{9,11},{10,... | collective-permute-start | bytes 393224 | tf_op jit(solution)/shard_map/ppermute | solution.py:65
  71.8 10.6 %collective-permute-start.17 = (bf16[2,128,512]{2,1,0:T(8,128)(2,1)S(1)}, bf16[2,128,512]{2,1,0:T(8,128)(2,1)S(1)}, u32[]{:S(2)}, u32[]{:S(2)}) collective-permute-start(bf16[2,128,512]{2,1,0:T(8,128)(2,1)S(1)} %slice_bitcast_fusion.1), channel_id=1, source_target_pairs={{0,2},{1,3},{2,0},{3,1},{4,6},{5,7},{6,4},{7,5},{8,10},{9,11},{10,... | collective-permute-start | bytes 786440 | tf_op jit(solution)/shard_map/ppermute | solution.py:65
  76.4 6.0 %collective-permute-start.21 = (bf16[152,512]{1,0:T(8,128)(2,1)S(1)}, bf16[152,512]{1,0:T(8,128)(2,1)S(1)}, u32[]{:S(2)}, u32[]{:S(2)}) collective-permute-start(bf16[152,512]{1,0:T(8,128)(2,1)S(1)} %pad_maximum_fusion.1), channel_id=1, source_target_pairs={{0,12},{4,0},{8,4},{12,8},{1,13},{5,1},{9,5},{13,9},{2,14},{6,2},{... | collective-permute-start | bytes 466952 | tf_op jit(solution)/shard_map/ppermute | solution.py:60
  82.5 8.4 %collective-permute-start.23 = (bf16[152,512]{1,0:T(8,128)(2,1)S(1)}, bf16[152,512]{1,0:T(8,128)(2,1)S(1)}, u32[]{:S(2)}, u32[]{:S(2)}) collective-permute-start(bf16[152,512]{1,0:T(8,128)(2,1)S(1)} %pad_maximum_fusion.2), channel_id=1, source_target_pairs={{0,4},{4,8},{8,12},{12,0},{1,5},{5,9},{9,13},{13,1},{2,6},{6,10},{... | collective-permute-start | bytes 466952 | tf_op jit(solution)/shard_map/ppermute | solution.py:60
  82.6 5.0 %collective-permute-start.18 = (bf16[1,128,512]{2,1,0:T(8,128)(2,1)S(1)}, bf16[1,128,512]{2,1,0:T(8,128)(2,1)S(1)}, u32[]{:S(2)}, u32[]{:S(2)}) collective-permute-start(bf16[1,128,512]{2,1,0:T(8,128)(2,1)S(1)} %slice_bitcast_fusion.6), channel_id=1, source_target_pairs={{0,2},{1,3},{2,0},{3,1},{4,6},{5,7},{6,4},{7,5},{8,10},{9,11},{10,... | collective-permute-start | bytes 393224 | tf_op jit(solution)/shard_map/ppermute | solution.py:65
  83.8 8.4 %collective-permute-start.22 = (bf16[176,512]{1,0:T(8,128)(2,1)S(1)}, bf16[176,512]{1,0:T(8,128)(2,1)S(1)}, u32[]{:S(2)}, u32[]{:S(2)}) collective-permute-start(bf16[176,512]{1,0:T(8,128)(2,1)S(1)} %pad_maximum_fusion), channel_id=1, source_target_pairs={{0,12},{4,0},{8,4},{12,8},{1,13},{5,1},{9,5},{13,9},{2,14},{6,2},{... | collective-permute-start | bytes 540680 | tf_op jit(solution)/shard_map/ppermute | solution.py:60

commit v9 on v7

--- a/solution.py
+++ b/solution.py
@@ -18,8 +18,8 @@
 HOP_CHIPS = 2
 PAGE_FOLD = 24
 SMALL_VMEM = 4 * 1024 * 1024
-WEIGHT_SLOTS = 2
-EXPERT_VMEM = 32 * 1024 * 1024
+WEIGHT_SLOTS = 3
+EXPERT_VMEM = 31 * 1024 * 1024
 
 epsilon = 1e-06
 
@@ -248,18 +248,18 @@
 
 
 def expert_kernel(
-    gain_ref, gate_up_ref, down_ref, *refs, held, capacity, parts, chips, fills,
+    gain_ref, gate_up_ref, down_ref, *refs, held, parts, chips, fills,
 ):
     held_refs, refs = refs[: 2 * fills], refs[2 * fills :]
     block_refs, out_refs = refs[: parts * chips * CORES], refs[parts * chips * CORES :]
     out_refs, scratch = out_refs[: len(RETURNS) * CORES], out_refs[len(RETURNS) * CORES :]
     (
-        normed_ref, pick_ref, picked_ref, slot_gate_ref, served_ref, gain_buf, gu_buf, down_buf,
-        sems, gain_sem,
+        pick_ref, picked_ref, slot_gate_ref, gain_buf, gu_buf, down_buf, sems, gain_sem,
     ) = scratch
     _, block_rows, width = block_refs[0].shape
     tok_node = block_rows - TOPK
-    tokens, model_width = normed_ref.shape
+    model_width = picked_ref.shape[1]
+    served_ref = picked_ref
     slots = down_buf.shape[0]
 
     def fetch(h, slot):
@@ -294,23 +294,15 @@
         for x in range(chips)
     ]
 
+    expert = first_expert + lax.broadcasted_iota(jnp.int32, (held, 1), 0)
+    earlier = jnp.where(
+        lax.broadcasted_iota(jnp.int32, (tok_node, tok_node), 0)
+        < lax.broadcasted_iota(jnp.int32, (tok_node, tok_node), 1),
+        1.0, 0.0,
+    ).astype(jnp.bfloat16)
+    slot_number = lax.broadcasted_iota(jnp.int32, (CAP, tok_node), 0)
     gain_copy.wait()
-    expert = first_expert + lax.broadcasted_iota(jnp.int32, (held, 1), 0)
-    named, gate = [], []
     for z in range(parts):
-        total = jnp.zeros((tok_node, 1), jnp.float32)
-        for x in range(chips):
-            for c in range(CORES):
-                wide = blocks[z][x][c][0, :tok_node, :].astype(jnp.float32)
-                total = total + jnp.sum(wide * wide, axis=1, keepdims=True)
-        inv_scale = lax.rsqrt(total / model_width + epsilon)
-        at = pl.ds(z * tok_node, tok_node)
-        for x in range(chips):
-            for c in range(CORES):
-                wide = blocks[z][x][c][0, :tok_node, :].astype(jnp.float32)
-                normed_ref[at, features[x][c]] = (
-                    wide * inv_scale * gain_buf[:, features[x][c]]
-                ).astype(jnp.bfloat16)
         choices = blocks[z][0][0][0, tok_node:, :].astype(jnp.float32)
         number = choices[:, :tok_node].astype(jnp.int32)
         value = (
@@ -318,43 +310,43 @@
             + choices[:, 2 * tok_node : 3 * tok_node]
             + choices[:, 3 * tok_node :]
         )
-        node_named = jnp.zeros((held, tok_node), jnp.float32)
-        node_gate = jnp.zeros((held, tok_node), jnp.float32)
+        named = jnp.zeros((held, tok_node), jnp.float32)
+        gate = jnp.zeros((held, tok_node), jnp.float32)
         for choice in range(TOPK):
             match = number[choice : choice + 1, :] == expert
-            node_named = node_named + jnp.where(match, 1.0, 0.0)
-            node_gate = node_gate + jnp.where(match, value[choice : choice + 1, :], 0.0)
-        named.append(node_named)
-        gate.append(node_gate)
-
-    named = jnp.concatenate(named, axis=1)
-    gate = jnp.concatenate(gate, axis=1)
-    earlier = (
-        lax.broadcasted_iota(jnp.int32, (tokens, tokens), 0)
-        < lax.broadcasted_iota(jnp.int32, (tokens, tokens), 1)
-    )
-    rank = jnp.dot(
-        named.astype(jnp.bfloat16),
-        jnp.where(earlier, 1.0, 0.0).astype(jnp.bfloat16),
-        preferred_element_type=jnp.float32,
-    )
-    rank = jnp.where(named > 0.0, rank, -1.0).astype(jnp.int32)
-    slot_number = lax.broadcasted_iota(jnp.int32, (capacity, tokens), 0)
-    for h in range(held):
-        here = rank[h : h + 1, :] == slot_number
-        at = pl.ds(h * capacity, capacity)
-        pick_ref[at, :] = jnp.where(here, 1.0, 0.0).astype(jnp.bfloat16)
-        slot_gate_ref[at, :] = jnp.sum(
-            jnp.where(here, gate[h : h + 1, :], 0.0), axis=1, keepdims=True
-        )
-    for first in range(0, model_width, width):
-        part = slice(first, first + width)
-        picked_ref[:, part] = jnp.dot(
-            pick_ref[...], normed_ref[:, part], preferred_element_type=jnp.float32
-        ).astype(jnp.bfloat16)
-
-    def one_expert(at, gate_up, down):
-        picked = picked_ref[at, :]
+            named = named + jnp.where(match, 1.0, 0.0)
+            gate = gate + jnp.where(match, value[choice : choice + 1, :], 0.0)
+        rank = jnp.dot(named.astype(jnp.bfloat16), earlier, preferred_element_type=jnp.float32)
+        rank = jnp.where(named > 0.0, rank, -1.0).astype(jnp.int32)
+        for h in range(held):
+            here = rank[h : h + 1, :] == slot_number
+            pick_ref[z, pl.ds(h * CAP, CAP), :] = jnp.where(here, 1.0, 0.0).astype(jnp.bfloat16)
+            slot_gate_ref[pl.ds((z * held + h) * CAP, CAP), :] = jnp.sum(
+                jnp.where(here, gate[h : h + 1, :], 0.0), axis=1, keepdims=True
+            )
+        total = jnp.zeros((tok_node, 1), jnp.float32)
+        for x in range(chips):
+            for c in range(CORES):
+                wide = blocks[z][x][c][0, :tok_node, :].astype(jnp.float32)
+                total = total + jnp.sum(wide * wide, axis=1, keepdims=True)
+        inv_scale = lax.rsqrt(total / model_width + epsilon)
+        at = pl.ds(z * held * CAP, held * CAP)
+        for x in range(chips):
+            for c in range(CORES):
+                wide = blocks[z][x][c][0, :tok_node, :].astype(jnp.float32)
+                normed = (wide * inv_scale * gain_buf[:, features[x][c]]).astype(jnp.bfloat16)
+                picked_ref[at, features[x][c]] = jnp.dot(
+                    pick_ref[z], normed, preferred_element_type=jnp.float32
+                ).astype(jnp.bfloat16)
+
+    def rows_of(h):
+        first = [(z * held + h) * CAP for z in range(parts)]
+        if not isinstance(h, int):
+            first = [pl.multiple_of(at, CAP) for at in first]
+        return [pl.ds(at, CAP) for at in first]
+
+    def one_expert(h, gate_up, down):
+        picked = jnp.concatenate([picked_ref[at, :] for at in rows_of(h)], axis=0)
         along = (((1,), (1,)), ((), ()))
         gate_part = lax.dot_general(
             gate_up[0], picked, along, preferred_element_type=jnp.float32
@@ -366,17 +358,19 @@
         served = lax.dot_general(
             activated, down[...], (((0,), (0,)), ((), ())), preferred_element_type=jnp.float32
         )
-        served_ref[at, :] = (served * slot_gate_ref[at, :]).astype(jnp.bfloat16)
+        for z, at in enumerate(rows_of(h)):
+            served_ref[at, :] = (
+                served[z * CAP : (z + 1) * CAP, :] * slot_gate_ref[at, :]
+            ).astype(jnp.bfloat16)
 
     for h in range(fills):
-        one_expert(pl.ds(h * capacity, capacity), held_refs[2 * h], held_refs[2 * h + 1])
+        one_expert(h, held_refs[2 * h], held_refs[2 * h + 1])
 
     def streamed(h, carry):
         slot = lax.rem(h - fills, slots)
         for copy in fetch(h, slot):
             copy.wait()
-        at = pl.ds(pl.multiple_of(h * capacity, capacity), capacity)
-        one_expert(at, gu_buf.at[slot], down_buf.at[slot])
+        one_expert(h, gu_buf.at[slot], down_buf.at[slot])
 
         @pl.when(h + slots < held)
         def _():
@@ -387,24 +381,21 @@
 
     lax.fori_loop(fills, held, streamed, 0)
 
-    back = pick_ref[...].T
-    for x in range(chips):
-        for c in range(CORES):
-            summed = jnp.dot(
-                back, served_ref[:, features[x][c]], preferred_element_type=jnp.float32
-            ).astype(jnp.bfloat16)
-            for group, members in enumerate(RETURNS):
-                for i, z in enumerate(members):
-                    out_refs[group * CORES + c][x, i] = summed[
-                        z * tok_node : (z + 1) * tok_node, :
-                    ]
+    for group, members in enumerate(RETURNS):
+        for i, z in enumerate(members):
+            back = pick_ref[z].T
+            at = pl.ds(z * held * CAP, held * CAP)
+            for x in range(chips):
+                for c in range(CORES):
+                    out_refs[group * CORES + c][x, i] = jnp.dot(
+                        back, served_ref[at, features[x][c]], preferred_element_type=jnp.float32
+                    ).astype(jnp.bfloat16)
 
 
 def expert_sums(gain, gate_up_weight, down_weight, held_weights, blocks):
     parts, chips = len(blocks), len(blocks[0])
     _, block_rows, width = blocks[0][0][0].shape
     tok_node = block_rows - TOPK
-    tokens = parts * tok_node
     model_width = chips * CORES * width
     ff_dev = down_weight.shape[0]
     held = max(1, ff_dev // FF)
@@ -417,8 +408,7 @@
     flat = [blocks[z][x][c] for z in range(parts) for x in range(chips) for c in range(CORES)]
     sums = pl.pallas_call(
         functools.partial(
-            expert_kernel, held=held, capacity=capacity, parts=parts, chips=chips,
-            fills=len(held_weights) // 2,
+            expert_kernel, held=held, parts=parts, chips=chips, fills=len(held_weights) // 2
         ),
         out_shape=[
             jax.ShapeDtypeStruct((chips, len(members), tok_node, width), jnp.bfloat16)
@@ -428,11 +418,9 @@
         in_specs=[hbm] * 3 + [vmem] * (len(held_weights) + len(flat)),
         out_specs=[vmem] * (len(RETURNS) * CORES),
         scratch_shapes=[
-            pltpu.VMEM((tokens, model_width), jnp.bfloat16),
-            pltpu.VMEM((all_slots, tokens), jnp.bfloat16),
+            pltpu.VMEM((parts, held * CAP, tok_node), jnp.bfloat16),
             pltpu.VMEM((all_slots, model_width), jnp.bfloat16),
             pltpu.VMEM((all_slots, 1), jnp.float32),
-            pltpu.VMEM((all_slots, model_width), jnp.bfloat16),
             pltpu.VMEM((1, model_width), jnp.float32),
             pltpu.VMEM((WEIGHT_SLOTS, 2, ff_part, model_width), jnp.bfloat16),
             pltpu.VMEM((WEIGHT_SLOTS, ff_part, model_width), jnp.bfloat16),

time: 85.4 us -> 83 us (0.972)
  Pallas kernels: 40.9 us -> 38.6 us
    pallas_call x1, Pallas kernels: 31.5 us -> 29.2 us  [expert_sums(): pl.pallas_call(functools.partial(expert_kernel, held=held, parts=parts, c...]
where the time goes in v9:
time: 83 us; the launch traced here: 82.8 us
  Pallas kernels  38.6 us (47%)
  starting transfers between devices  24.2 us (29%)
  waiting for transfers between devices  18.7 us (23%)
    pallas_call x1, Pallas kernels, expert_sums(): pl.pallas_call(functools.partial(expert_kernel, held=held, parts=parts, c...  29.2 us
    ppermute x6, starting transfers between devices, shift_dp(): lax.ppermute(value, 'dp', [(i, (i + shift) % count) for i in range(count)])  12.8 us
    ppermute x7, starting transfers between devices, shift_x(): lax.ppermute(value, 'mp', [(i, (i + CORES * shift) % count) for i in rang...  8.86 us
    ppermute x6, waiting for transfers between devices, shift_dp(): lax.ppermute(value, 'dp', [(i, (i + shift) % count) for i in range(count)])  8.68 us
    ppermute x7, waiting for transfers between devices, shift_x(): lax.ppermute(value, 'mp', [(i, (i + CORES * shift) % count) for i in rang...  8.24 us
    pallas_call x2, Pallas kernels, filled(): pl.pallas_call(functools.partial(kernel, expert=expert), out_shape=out_sh...  7.62 us
    ppermute x11, starting transfers between devices, other_core(): return lax.ppermute(value, 'mp', [(i, i ^ 1) for i in range(count)])  2.5 us
    ppermute x11, waiting for transfers between devices, other_core(): return lax.ppermute(value, 'mp', [(i, i ^ 1) for i in range(count)])  1.75 us
  transfers between devices with their start and end apart: 24, of which 13 were waited for; matrix products, arithmetic and copies ran while one was open for 1% of the time, Pallas kernels for 9%

profile of v9, /device:TPU:0, one launch (start us, length us, event | category | flops | bytes accessed | tf_op | source)
XLA Modules:
  0.0 82.8 jit_solution(17373132381143468682)
XLA Ops:
  0.6 1.0 %shard_map.104.after_ref.refs_4_ = bf16[1,136,512]{2,1,0:T(8,128)(2,1)S(1)} custom-call(bf16[128,512]{1,0:T(8,128)(2,1)} %hidden_ref.3, s32[8,128]{1,0:T(8,128)} %bitcast.42, f32[8,128]{1,0:T(8,128)} %bitcast.43), custom_call_target="tpu_custom_call" | custom-call | tf_op jit(solution)/shard_map/pallas_call | solution.py:98
  1.6 3.1 %collective-permute-start = (bf16[1,136,512]{2,1,0:T(8,128)(2,1)S(1)}, bf16[1,136,512]{2,1,0:T(8,128)(2,1)S(1)}, u32[]{:S(2)}, u32[]{:S(2)}) collective-permute-start(bf16[1,136,512]{2,1,0:T(8,128)(2,1)S(1)} %shard_map.104.after_ref.refs_4_), channel_id=1, source_target_pairs={{0,4},{4,8},{8,12},{12,0},{1,5},{5,9},{9,13},{13,1},{2,6},{6,10},{... | collective-permute-start | bytes 417800 | tf_op jit(solution)/shard_map/ppermute | solution.py:57
  4.7 2.1 %collective-permute-start.1 = (bf16[1,136,512]{2,1,0:T(8,128)(2,1)S(1)}, bf16[1,136,512]{2,1,0:T(8,128)(2,1)S(1)}, u32[]{:S(2)}, u32[]{:S(2)}) collective-permute-start(bf16[1,136,512]{2,1,0:T(8,128)(2,1)S(1)} %shard_map.104.after_ref.refs_4_), channel_id=1, source_target_pairs={{0,12},{4,0},{8,4},{12,8},{1,13},{5,1},{9,5},{13,9},{2,14},{6,2},{... | collective-permute-start | bytes 417800 | tf_op jit(solution)/shard_map/ppermute | solution.py:57
  6.8 1.6 %collective-permute-start.2 = (bf16[1,136,512]{2,1,0:T(8,128)(2,1)S(1)}, bf16[1,136,512]{2,1,0:T(8,128)(2,1)S(1)}, u32[]{:S(2)}, u32[]{:S(2)}) collective-permute-start(bf16[1,136,512]{2,1,0:T(8,128)(2,1)S(1)} %shard_map.104.after_ref.refs_4_), channel_id=1, source_target_pairs={{0,2},{1,3},{2,0},{3,1},{4,6},{5,7},{6,4},{7,5},{8,10},{9,11},{10,... | collective-permute-start | bytes 417800 | tf_op jit(solution)/shard_map/ppermute | solution.py:62
  8.4 3.8 %shard_map.105 = (bf16[2,768,2048]{2,1,0:T(8,128)(2,1)S(1)}, bf16[768,2048]{1,0:T(8,128)(2,1)S(1)}, bf16[4,24,512]{2,1,0:T(8,128)(2,1)S(1)}) custom-call(bf16[2,6144,2048]{2,1,0:T(8,128)(2,1)} %gate_up_ref.5, bf16[6144,2048]{1,0:T(8,128)(2,1)} %down_ref.5, bf16[1,136,512]{2,1,0:T(8,128)(2,1)S(1)} %shard_map.104.after_ref.refs_4_, bf16[128,256]{1,0:T(8,128)(2,1)} %kv_ref.1, ...), custom_call_target="tpu_custom_call" | custom-call | bytes 9437184 | tf_op jit(solution)/shard_map/pallas_call | solution.py:200
  12.3 0.5 collective-permute-done.1.after_ref.refs_16_
  12.8 1.1 %collective-permute-start.4 = (bf16[1,136,512]{2,1,0:T(8,128)(2,1)S(1)}, bf16[1,136,512]{2,1,0:T(8,128)(2,1)S(1)}, u32[]{:S(2)}, u32[]{:S(2)}) collective-permute-start(bf16[1,136,512]{2,1,0:T(8,128)(2,1)S(1)} %collective-permute-done.refs_8_), channel_id=1, source_target_pairs={{0,4},{4,8},{8,12},{12,0},{1,5},{5,9},{9,13},{13,1},{2,6},{6,10},{... | collective-permute-start | bytes 417800 | tf_op jit(solution)/shard_map/ppermute | solution.py:57
  13.9 1.5 %collective-permute-start.5 = (bf16[1,136,512]{2,1,0:T(8,128)(2,1)S(1)}, bf16[1,136,512]{2,1,0:T(8,128)(2,1)S(1)}, u32[]{:S(2)}, u32[]{:S(2)}) collective-permute-start(bf16[1,136,512]{2,1,0:T(8,128)(2,1)S(1)} %collective-permute-done.refs_8_), channel_id=1, source_target_pairs={{0,2},{1,3},{2,0},{3,1},{4,6},{5,7},{6,4},{7,5},{8,10},{9,11},{10,... | collective-permute-start | bytes 417800 | tf_op jit(solution)/shard_map/ppermute | solution.py:62
  15.4 0.5 collective-permute-start.6
  16.0 3.8 %shard_map.106 = (bf16[2,768,2048]{2,1,0:T(8,128)(2,1)S(1)}, bf16[768,2048]{1,0:T(8,128)(2,1)S(1)}) custom-call(bf16[2,6144,2048]{2,1,0:T(8,128)(2,1)} %gate_up_ref.5, bf16[6144,2048]{1,0:T(8,128)(2,1)} %down_ref.5, bf16[1,136,512]{2,1,0:T(8,128)(2,1)S(1)} %collective-permute-done.1.after_ref.refs_16_), custom_call_target="tpu_custom_call" | custom-call | bytes 9437184 | tf_op jit(solution)/shard_map/pallas_call | solution.py:200
  19.8 0.4 collective-permute-done.4.refs_12_
  20.5 1.7 %collective-permute-done.6.refs_18_ = bf16[1,136,512]{2,1,0:T(8,128)(2,1)S(1)} collective-permute-done((bf16[1,136,512]{2,1,0:T(8,128)(2,1)S(1)}, bf16[1,136,512]{2,1,0:T(8,128)(2,1)S(1)}, u32[]{:S(2)}, u32[]{:S(2)}) %collective-permute-start.6) | collective-permute-done | bytes 139296 | tf_op jit(solution)/shard_map/ppermute | solution.py:62
  22.2 1.5 %collective-permute-start.11 = (bf16[1,136,512]{2,1,0:T(8,128)(2,1)S(1)}, bf16[1,136,512]{2,1,0:T(8,128)(2,1)S(1)}, u32[]{:S(2)}, u32[]{:S(2)}) collective-permute-start(bf16[1,136,512]{2,1,0:T(8,128)(2,1)S(1)} %collective-permute-done.4.refs_12_), channel_id=1, source_target_pairs={{0,2},{1,3},{2,0},{3,1},{4,6},{5,7},{6,4},{7,5},{8,10},{9,11},{10,... | collective-permute-start | bytes 417800 | tf_op jit(solution)/shard_map/ppermute | solution.py:62
  23.7 0.5 collective-permute-start.13
  24.2 0.5 collective-permute-start.8
  24.7 2.5 %collective-permute-done.11.refs_14_ = bf16[1,136,512]{2,1,0:T(8,128)(2,1)S(1)} collective-permute-done((bf16[1,136,512]{2,1,0:T(8,128)(2,1)S(1)}, bf16[1,136,512]{2,1,0:T(8,128)(2,1)S(1)}, u32[]{:S(2)}, u32[]{:S(2)}) %collective-permute-start.11) | collective-permute-done | bytes 139296 | tf_op jit(solution)/shard_map/ppermute | solution.py:62
  27.3 0.5 collective-permute-start.12
  27.8 0.8 %collective-permute-done.9.refs_11_ = bf16[1,136,512]{2,1,0:T(8,128)(2,1)S(1)} collective-permute-done((bf16[1,136,512]{2,1,0:T(8,128)(2,1)S(1)}, bf16[1,136,512]{2,1,0:T(8,128)(2,1)S(1)}, u32[]{:S(2)}, u32[]{:S(2)}) %collective-permute-start.9) | collective-permute-done | bytes 139296 | tf_op jit(solution)/shard_map/ppermute | solution.py:67
  28.8 29.2 %shard_map.107 = (bf16[2,1,128,512]{3,2,1,0:T(8,128)(2,1)S(1)}, bf16[2,1,128,512]{3,2,1,0:T(8,128)(2,1)S(1)}, bf16[2,2,128,512]{3,2,1,0:T(8,128)(2,1)S(1)}, bf16...) custom-call(f32[1,2048]{1,0:T(1,128)} %bitcast.41, ...), custom_call_target="tpu_custom_call" | custom-call | flops 4831838208 | bytes 75497472 | tf_op jit(solution)/shard_map/pallas_call | solution.py:409
  58.1 0.4 collective-permute-start.19
  58.7 0.3 collective-permute-start.15
  59.0 0.7 collective-permute-done.19
  59.8 1.5 %collective-permute-start.20 = (bf16[1,128,512]{2,1,0:T(8,128)(2,1)S(1)}, bf16[1,128,512]{2,1,0:T(8,128)(2,1)S(1)}, u32[]{:S(2)}, u32[]{:S(2)}) collective-permute-start(bf16[1,128,512]{2,1,0:T(8,128)(2,1)S(1)} %slice_bitcast_fusion.3), channel_id=1, source_target_pairs={{0,2},{1,3},{2,0},{3,1},{4,6},{5,7},{6,4},{7,5},{8,10},{9,11},{10,... | collective-permute-start | bytes 393224 | tf_op jit(solution)/shard_map/ppermute | solution.py:62
  61.6 1.0 %collective-permute-start.17 = (bf16[2,128,512]{2,1,0:T(8,128)(2,1)S(1)}, bf16[2,128,512]{2,1,0:T(8,128)(2,1)S(1)}, u32[]{:S(2)}, u32[]{:S(2)}) collective-permute-start(bf16[2,128,512]{2,1,0:T(8,128)(2,1)S(1)} %slice_bitcast_fusion.1), channel_id=1, source_target_pairs={{0,2},{1,3},{2,0},{3,1},{4,6},{5,7},{6,4},{7,5},{8,10},{9,11},{10,... | collective-permute-start | bytes 786440 | tf_op jit(solution)/shard_map/ppermute | solution.py:62
  62.6 3.6 %collective-permute-done.20 = bf16[1,128,512]{2,1,0:T(8,128)(2,1)S(1)} collective-permute-done((bf16[1,128,512]{2,1,0:T(8,128)(2,1)S(1)}, bf16[1,128,512]{2,1,0:T(8,128)(2,1)S(1)}, u32[]{:S(2)}, u32[]{:S(2)}) %collective-permute-start.20) | collective-permute-done | bytes 131104 | tf_op jit(solution)/shard_map/ppermute | solution.py:62
  66.3 2.8 %collective-permute-start.21 = (bf16[152,512]{1,0:T(8,128)(2,1)S(1)}, bf16[152,512]{1,0:T(8,128)(2,1)S(1)}, u32[]{:S(2)}, u32[]{:S(2)}) collective-permute-start(bf16[152,512]{1,0:T(8,128)(2,1)S(1)} %pad_maximum_fusion.1), channel_id=1, source_target_pairs={{0,12},{4,0},{8,4},{12,8},{1,13},{5,1},{9,5},{13,9},{2,14},{6,2},{... | collective-permute-start | bytes 466952 | tf_op jit(solution)/shard_map/ppermute | solution.py:57
  69.1 3.2 %collective-permute-done.21 = bf16[152,512]{1,0:T(8,128)(2,1)S(1)} collective-permute-done((bf16[152,512]{1,0:T(8,128)(2,1)S(1)}, bf16[152,512]{1,0:T(8,128)(2,1)S(1)}, u32[]{:S(2)}, u32[]{:S(2)}) %collective-permute-start.21) | collective-permute-done | bytes 155680 | tf_op jit(solution)/shard_map/ppermute | solution.py:57
  72.4 1.1 %collective-permute-start.18 = (bf16[1,128,512]{2,1,0:T(8,128)(2,1)S(1)}, bf16[1,128,512]{2,1,0:T(8,128)(2,1)S(1)}, u32[]{:S(2)}, u32[]{:S(2)}) collective-permute-start(bf16[1,128,512]{2,1,0:T(8,128)(2,1)S(1)} %slice_bitcast_fusion.6), channel_id=1, source_target_pairs={{0,2},{1,3},{2,0},{3,1},{4,6},{5,7},{6,4},{7,5},{8,10},{9,11},{10,... | collective-permute-start | bytes 393224 | tf_op jit(solution)/shard_map/ppermute | solution.py:62
  73.6 3.7 %collective-permute-start.22 = (bf16[176,512]{1,0:T(8,128)(2,1)S(1)}, bf16[176,512]{1,0:T(8,128)(2,1)S(1)}, u32[]{:S(2)}, u32[]{:S(2)}) collective-permute-start(bf16[176,512]{1,0:T(8,128)(2,1)S(1)} %pad_maximum_fusion), channel_id=1, source_target_pairs={{0,12},{4,0},{8,4},{12,8},{1,13},{5,1},{9,5},{13,9},{2,14},{6,2},{... | collective-permute-start | bytes 540680 | tf_op jit(solution)/shard_map/ppermute | solution.py:57
  77.5 3.2 %collective-permute-done.23.up_ref = bf16[152,512]{1,0:T(8,128)(2,1)S(1)} collective-permute-done((bf16[152,512]{1,0:T(8,128)(2,1)S(1)}, bf16[152,512]{1,0:T(8,128)(2,1)S(1)}, u32[]{:S(2)}, u32[]{:S(2)}) %collective-permute-start.23) | collective-permute-done | bytes 155680 | tf_op jit(solution)/shard_map/ppermute | solution.py:57
  80.7 1.3 %collective-permute-done.22.down_ref = bf16[176,512]{1,0:T(8,128)(2,1)S(1)} collective-permute-done((bf16[176,512]{1,0:T(8,128)(2,1)S(1)}, bf16[176,512]{1,0:T(8,128)(2,1)S(1)}, u32[]{:S(2)}, u32[]{:S(2)}) %collective-permute-start.22) | collective-permute-done | bytes 180256 | tf_op jit(solution)/shard_map/ppermute | solution.py:57
  82.1 0.8 shard_map.108
  (39 shorter events, 1.6 us)
Async XLA Ops:
  1.6 10.7 %collective-permute-start = (bf16[1,136,512]{2,1,0:T(8,128)(2,1)S(1)}, bf16[1,136,512]{2,1,0:T(8,128)(2,1)S(1)}, u32[]{:S(2)}, u32[]{:S(2)}) collective-permute-start(bf16[1,136,512]{2,1,0:T(8,128)(2,1)S(1)} %shard_map.104.after_ref.refs_4_), channel_id=1, source_target_pairs={{0,4},{4,8},{8,12},{12,0},{1,5},{5,9},{9,13},{13,1},{2,6},{6,10},{... | collective-permute-start | bytes 417800 | tf_op jit(solution)/shard_map/ppermute | solution.py:57
  4.7 8.1 %collective-permute-start.1 = (bf16[1,136,512]{2,1,0:T(8,128)(2,1)S(1)}, bf16[1,136,512]{2,1,0:T(8,128)(2,1)S(1)}, u32[]{:S(2)}, u32[]{:S(2)}) collective-permute-start(bf16[1,136,512]{2,1,0:T(8,128)(2,1)S(1)} %shard_map.104.after_ref.refs_4_), channel_id=1, source_target_pairs={{0,12},{4,0},{8,4},{12,8},{1,13},{5,1},{9,5},{13,9},{2,14},{6,2},{... | collective-permute-start | bytes 417800 | tf_op jit(solution)/shard_map/ppermute | solution.py:57
  6.8 6.0 %collective-permute-start.2 = (bf16[1,136,512]{2,1,0:T(8,128)(2,1)S(1)}, bf16[1,136,512]{2,1,0:T(8,128)(2,1)S(1)}, u32[]{:S(2)}, u32[]{:S(2)}) collective-permute-start(bf16[1,136,512]{2,1,0:T(8,128)(2,1)S(1)} %shard_map.104.after_ref.refs_4_), channel_id=1, source_target_pairs={{0,2},{1,3},{2,0},{3,1},{4,6},{5,7},{6,4},{7,5},{8,10},{9,11},{10,... | collective-permute-start | bytes 417800 | tf_op jit(solution)/shard_map/ppermute | solution.py:62
  8.4 4.4 %collective-permute-start.3 = (bf16[1,136,512]{2,1,0:T(8,128)(2,1)S(1)}, bf16[1,136,512]{2,1,0:T(8,128)(2,1)S(1)}, u32[]{:S(2)}, u32[]{:S(2)}) collective-permute-start(bf16[1,136,512]{2,1,0:T(8,128)(2,1)S(1)} %shard_map.104.after_ref.refs_4_), channel_id=1, source_target_pairs={{0,1},{1,0},{2,3},{3,2},{4,5},{5,4},{6,7},{7,6},{8,9},{9,8},{10,11... | collective-permute-start | bytes 417800 | tf_op jit(solution)/shard_map/ppermute | solution.py:67
  12.8 7.4 %collective-permute-start.4 = (bf16[1,136,512]{2,1,0:T(8,128)(2,1)S(1)}, bf16[1,136,512]{2,1,0:T(8,128)(2,1)S(1)}, u32[]{:S(2)}, u32[]{:S(2)}) collective-permute-start(bf16[1,136,512]{2,1,0:T(8,128)(2,1)S(1)} %collective-permute-done.refs_8_), channel_id=1, source_target_pairs={{0,4},{4,8},{8,12},{12,0},{1,5},{5,9},{9,13},{13,1},{2,6},{6,10},{... | collective-permute-start | bytes 417800 | tf_op jit(solution)/shard_map/ppermute | solution.py:57
  13.9 6.6 %collective-permute-start.5 = (bf16[1,136,512]{2,1,0:T(8,128)(2,1)S(1)}, bf16[1,136,512]{2,1,0:T(8,128)(2,1)S(1)}, u32[]{:S(2)}, u32[]{:S(2)}) collective-permute-start(bf16[1,136,512]{2,1,0:T(8,128)(2,1)S(1)} %collective-permute-done.refs_8_), channel_id=1, source_target_pairs={{0,2},{1,3},{2,0},{3,1},{4,6},{5,7},{6,4},{7,5},{8,10},{9,11},{10,... | collective-permute-start | bytes 417800 | tf_op jit(solution)/shard_map/ppermute | solution.py:62
  15.4 6.8 %collective-permute-start.6 = (bf16[1,136,512]{2,1,0:T(8,128)(2,1)S(1)}, bf16[1,136,512]{2,1,0:T(8,128)(2,1)S(1)}, u32[]{:S(2)}, u32[]{:S(2)}) collective-permute-start(bf16[1,136,512]{2,1,0:T(8,128)(2,1)S(1)} %collective-permute-done.1.after_ref.refs_16_), channel_id=1, source_target_pairs={{0,2},{1,3},{2,0},{3,1},{4,6},{5,7},{6,4},{7,5},{8,10},{9,11},{10,... | collective-permute-start | bytes 417800 | tf_op jit(solution)/shard_map/ppermute | solution.py:62
  19.7 4.5 %collective-permute-start.7 = (bf16[1,136,512]{2,1,0:T(8,128)(2,1)S(1)}, bf16[1,136,512]{2,1,0:T(8,128)(2,1)S(1)}, u32[]{:S(2)}, u32[]{:S(2)}) collective-permute-start(bf16[1,136,512]{2,1,0:T(8,128)(2,1)S(1)} %collective-permute-done.2.refs_6_), channel_id=1, source_target_pairs={{0,1},{1,0},{2,3},{3,2},{4,5},{5,4},{6,7},{7,6},{8,9},{9,8},{10,11... | collective-permute-start | bytes 417800 | tf_op jit(solution)/shard_map/ppermute | solution.py:67
  22.2 5.1 %collective-permute-start.11 = (bf16[1,136,512]{2,1,0:T(8,128)(2,1)S(1)}, bf16[1,136,512]{2,1,0:T(8,128)(2,1)S(1)}, u32[]{:S(2)}, u32[]{:S(2)}) collective-permute-start(bf16[1,136,512]{2,1,0:T(8,128)(2,1)S(1)} %collective-permute-done.4.refs_12_), channel_id=1, source_target_pairs={{0,2},{1,3},{2,0},{3,1},{4,6},{5,7},{6,4},{7,5},{8,10},{9,11},{10,... | collective-permute-start | bytes 417800 | tf_op jit(solution)/shard_map/ppermute | solution.py:62
  23.7 3.6 %collective-permute-start.10 = (bf16[1,136,512]{2,1,0:T(8,128)(2,1)S(1)}, bf16[1,136,512]{2,1,0:T(8,128)(2,1)S(1)}, u32[]{:S(2)}, u32[]{:S(2)}) collective-permute-start(bf16[1,136,512]{2,1,0:T(8,128)(2,1)S(1)} %collective-permute-done.4.refs_12_), channel_id=1, source_target_pairs={{0,1},{1,0},{2,3},{3,2},{4,5},{5,4},{6,7},{7,6},{8,9},{9,8},{10,11... | collective-permute-start | bytes 417800 | tf_op jit(solution)/shard_map/ppermute | solution.py:67
  23.7 4.1 %collective-permute-start.13 = (bf16[1,136,512]{2,1,0:T(8,128)(2,1)S(1)}, bf16[1,136,512]{2,1,0:T(8,128)(2,1)S(1)}, u32[]{:S(2)}, u32[]{:S(2)}) collective-permute-start(bf16[1,136,512]{2,1,0:T(8,128)(2,1)S(1)} %collective-permute-done.1.after_ref.refs_16_), channel_id=1, source_target_pairs={{0,1},{1,0},{2,3},{3,2},{4,5},{5,4},{6,7},{7,6},{8,9},{9,8},{10,11... | collective-permute-start | bytes 417800 | tf_op jit(solution)/shard_map/ppermute | solution.py:67
  24.2 3.6 %collective-permute-start.14 = (bf16[1,136,512]{2,1,0:T(8,128)(2,1)S(1)}, bf16[1,136,512]{2,1,0:T(8,128)(2,1)S(1)}, u32[]{:S(2)}, u32[]{:S(2)}) collective-permute-start(bf16[1,136,512]{2,1,0:T(8,128)(2,1)S(1)} %collective-permute-done.6.refs_18_), channel_id=1, source_target_pairs={{0,1},{1,0},{2,3},{3,2},{4,5},{5,4},{6,7},{7,6},{8,9},{9,8},{10,11... | collective-permute-start | bytes 417800 | tf_op jit(solution)/shard_map/ppermute | solution.py:67
  24.2 3.6 %collective-permute-start.8 = (bf16[1,136,512]{2,1,0:T(8,128)(2,1)S(1)}, bf16[1,136,512]{2,1,0:T(8,128)(2,1)S(1)}, u32[]{:S(2)}, u32[]{:S(2)}) collective-permute-start(bf16[1,136,512]{2,1,0:T(8,128)(2,1)S(1)} %collective-permute-done.refs_8_), channel_id=1, source_target_pairs={{0,1},{1,0},{2,3},{3,2},{4,5},{5,4},{6,7},{7,6},{8,9},{9,8},{10,11... | collective-permute-start | bytes 417800 | tf_op jit(solution)/shard_map/ppermute | solution.py:67
  27.3 1.4 %collective-permute-start.9 = (bf16[1,136,512]{2,1,0:T(8,128)(2,1)S(1)}, bf16[1,136,512]{2,1,0:T(8,128)(2,1)S(1)}, u32[]{:S(2)}, u32[]{:S(2)}) collective-permute-start(bf16[1,136,512]{2,1,0:T(8,128)(2,1)S(1)} %collective-permute-done.5.refs_10_), channel_id=1, source_target_pairs={{0,1},{1,0},{2,3},{3,2},{4,5},{5,4},{6,7},{7,6},{8,9},{9,8},{10,11... | collective-permute-start | bytes 417800 | tf_op jit(solution)/shard_map/ppermute | solution.py:67
  27.3 1.6 %collective-permute-start.12 = (bf16[1,136,512]{2,1,0:T(8,128)(2,1)S(1)}, bf16[1,136,512]{2,1,0:T(8,128)(2,1)S(1)}, u32[]{:S(2)}, u32[]{:S(2)}) collective-permute-start(bf16[1,136,512]{2,1,0:T(8,128)(2,1)S(1)} %collective-permute-done.11.refs_14_), channel_id=1, source_target_pairs={{0,1},{1,0},{2,3},{3,2},{4,5},{5,4},{6,7},{7,6},{8,9},{9,8},{10,11... | collective-permute-start | bytes 417800 | tf_op jit(solution)/shard_map/ppermute | solution.py:67
  58.1 24.0 %copy-start = (bf16[128,512]{1,0:T(8,128)(2,1)S(1)}, bf16[128,512]{1,0:T(8,128)(2,1)}, u32[]{:S(2)}) copy-start(bf16[128,512]{1,0:T(8,128)(2,1)} %hidden_ref.3) | copy-start | bytes 393220
  58.1 1.6 %collective-permute-start.19 = (bf16[2,1,128,512]{3,2,1,0:T(8,128)(2,1)S(1)}, bf16[2,1,128,512]{3,2,1,0:T(8,128)(2,1)S(1)}, u32[]{:S(2)}, u32[]{:S(2)}) collective-permute-start(bf16[2,1,128,512]{3,2,1,0:T(8,128)(2,1)S(1)} %get-tuple-element.51), channel_id=1, source_target_pairs={{0,1},{1,0},{2,3},{3,2},{4,5},{5,4},{6,7},{7,6},{8,9},{9,8},{10,11... | collective-permute-start | bytes 786440 | tf_op jit(solution)/shard_map/ppermute | solution.py:67
  58.5 2.9 %collective-permute-start.16 = (bf16[2,2,128,512]{3,2,1,0:T(8,128)(2,1)S(1)}, bf16[2,2,128,512]{3,2,1,0:T(8,128)(2,1)S(1)}, u32[]{:S(2)}, u32[]{:S(2)}) collective-permute-start(bf16[2,2,128,512]{3,2,1,0:T(8,128)(2,1)S(1)} %get-tuple-element.48), channel_id=1, source_target_pairs={{0,1},{1,0},{2,3},{3,2},{4,5},{5,4},{6,7},{7,6},{8,9},{9,8},{10,11... | collective-permute-start | bytes 1572872 | tf_op jit(solution)/shard_map/ppermute | solution.py:67
  58.7 2.7 %collective-permute-start.15 = (bf16[2,1,128,512]{3,2,1,0:T(8,128)(2,1)S(1)}, bf16[2,1,128,512]{3,2,1,0:T(8,128)(2,1)S(1)}, u32[]{:S(2)}, u32[]{:S(2)}) collective-permute-start(bf16[2,1,128,512]{3,2,1,0:T(8,128)(2,1)S(1)} %get-tuple-element.46), channel_id=1, source_target_pairs={{0,1},{1,0},{2,3},{3,2},{4,5},{5,4},{6,7},{7,6},{8,9},{9,8},{10,11... | collective-permute-start | bytes 786440 | tf_op jit(solution)/shard_map/ppermute | solution.py:67
  59.8 6.4 %collective-permute-start.20 = (bf16[1,128,512]{2,1,0:T(8,128)(2,1)S(1)}, bf16[1,128,512]{2,1,0:T(8,128)(2,1)S(1)}, u32[]{:S(2)}, u32[]{:S(2)}) collective-permute-start(bf16[1,128,512]{2,1,0:T(8,128)(2,1)S(1)} %slice_bitcast_fusion.3), channel_id=1, source_target_pairs={{0,2},{1,3},{2,0},{3,1},{4,6},{5,7},{6,4},{7,5},{8,10},{9,11},{10,... | collective-permute-start | bytes 393224 | tf_op jit(solution)/shard_map/ppermute | solution.py:62
  61.6 10.6 %collective-permute-start.17 = (bf16[2,128,512]{2,1,0:T(8,128)(2,1)S(1)}, bf16[2,128,512]{2,1,0:T(8,128)(2,1)S(1)}, u32[]{:S(2)}, u32[]{:S(2)}) collective-permute-start(bf16[2,128,512]{2,1,0:T(8,128)(2,1)S(1)} %slice_bitcast_fusion.1), channel_id=1, source_target_pairs={{0,2},{1,3},{2,0},{3,1},{4,6},{5,7},{6,4},{7,5},{8,10},{9,11},{10,... | collective-permute-start | bytes 786440 | tf_op jit(solution)/shard_map/ppermute | solution.py:62
  66.3 6.0 %collective-permute-start.21 = (bf16[152,512]{1,0:T(8,128)(2,1)S(1)}, bf16[152,512]{1,0:T(8,128)(2,1)S(1)}, u32[]{:S(2)}, u32[]{:S(2)}) collective-permute-start(bf16[152,512]{1,0:T(8,128)(2,1)S(1)} %pad_maximum_fusion.1), channel_id=1, source_target_pairs={{0,12},{4,0},{8,4},{12,8},{1,13},{5,1},{9,5},{13,9},{2,14},{6,2},{... | collective-permute-start | bytes 466952 | tf_op jit(solution)/shard_map/ppermute | solution.py:57
  72.3 8.4 %collective-permute-start.23 = (bf16[152,512]{1,0:T(8,128)(2,1)S(1)}, bf16[152,512]{1,0:T(8,128)(2,1)S(1)}, u32[]{:S(2)}, u32[]{:S(2)}) collective-permute-start(bf16[152,512]{1,0:T(8,128)(2,1)S(1)} %pad_maximum_fusion.2), channel_id=1, source_target_pairs={{0,4},{4,8},{8,12},{12,0},{1,5},{5,9},{9,13},{13,1},{2,6},{6,10},{... | collective-permute-start | bytes 466952 | tf_op jit(solution)/shard_map/ppermute | solution.py:57
  72.4 5.0 %collective-permute-start.18 = (bf16[1,128,512]{2,1,0:T(8,128)(2,1)S(1)}, bf16[1,128,512]{2,1,0:T(8,128)(2,1)S(1)}, u32[]{:S(2)}, u32[]{:S(2)}) collective-permute-start(bf16[1,128,512]{2,1,0:T(8,128)(2,1)S(1)} %slice_bitcast_fusion.6), channel_id=1, source_target_pairs={{0,2},{1,3},{2,0},{3,1},{4,6},{5,7},{6,4},{7,5},{8,10},{9,11},{10,... | collective-permute-start | bytes 393224 | tf_op jit(solution)/shard_map/ppermute | solution.py:62
  73.6 8.5 %collective-permute-start.22 = (bf16[176,512]{1,0:T(8,128)(2,1)S(1)}, bf16[176,512]{1,0:T(8,128)(2,1)S(1)}, u32[]{:S(2)}, u32[]{:S(2)}) collective-permute-start(bf16[176,512]{1,0:T(8,128)(2,1)S(1)} %pad_maximum_fusion), channel_id=1, source_target_pairs={{0,12},{4,0},{8,4},{12,8},{1,13},{5,1},{9,5},{13,9},{2,14},{6,2},{... | collective-permute-start | bytes 540680 | tf_op jit(solution)/shard_map/ppermute | solution.py:57

commit v10 on v9

--- a/solution.py
+++ b/solution.py
@@ -18,8 +18,8 @@
 HOP_CHIPS = 2
 PAGE_FOLD = 24
 SMALL_VMEM = 4 * 1024 * 1024
-WEIGHT_SLOTS = 3
-EXPERT_VMEM = 31 * 1024 * 1024
+WEIGHT_SLOTS = 4
+EXPERT_VMEM = 42 * 1024 * 1024
 
 epsilon = 1e-06
 
@@ -142,72 +142,38 @@
     )
 
 
-def fill_kernel(gate_up_ref, down_ref, after_ref, gate_up_out, down_out, sems, *, expert):
-    copies = expert_copies(gate_up_ref, down_ref, expert, gate_up_out, down_out, sems)
+def page_kernel(
+    kv_ref, lengths_ref, owners_ref, after_ref, pages_ref, kv_buf, lengths_buf, owners_buf, sems
+):
+    copies = (
+        pltpu.make_async_copy(kv_ref, kv_buf, sems.at[0]),
+        pltpu.make_async_copy(lengths_ref, lengths_buf, sems.at[1]),
+        pltpu.make_async_copy(owners_ref, owners_buf, sems.at[2]),
+    )
     for copy in copies:
         copy.start()
     for copy in copies:
         copy.wait()
-
-
-def page_fill_kernel(
-    gate_up_ref, down_ref, after_ref, kv_ref, lengths_ref, owners_ref,
-    gate_up_out, down_out, pages_ref,
-    sems, kv_buf, lengths_buf, owners_buf, page_sems, *, expert,
-):
-    small = (
-        pltpu.make_async_copy(kv_ref, kv_buf, page_sems.at[0]),
-        pltpu.make_async_copy(lengths_ref, lengths_buf, page_sems.at[1]),
-        pltpu.make_async_copy(owners_ref, owners_buf, page_sems.at[2]),
-    )
-    copies = expert_copies(gate_up_ref, down_ref, expert, gate_up_out, down_out, sems)
-    for copy in small + copies:
-        copy.start()
-    for copy in small:
-        copy.wait()
     write_pages(lengths_buf, owners_buf, kv_buf, pages_ref)
-    for copy in copies:
-        copy.wait()
-
-
-def filled(gate_up_weight, down_weight, expert, after, paged=None):
-    width = down_weight.shape[1]
-    ff_part = min(FF, down_weight.shape[0])
+
+
+def kv_pages(kv_rows, lengths, owners, after):
     hbm = pl.BlockSpec(memory_space=pltpu.HBM)
-    vmem = pl.BlockSpec(memory_space=pltpu.VMEM)
-    out_shape = [
-        pltpu.VMEM((2, ff_part, width), down_weight.dtype),
-        pltpu.VMEM((ff_part, width), down_weight.dtype),
-    ]
-    scratch = [pltpu.SemaphoreType.DMA((3,))]
-    operands = [gate_up_weight, down_weight, after]
-    kernel = fill_kernel
-    if paged is not None:
-        kv_rows, lengths, owners = paged
-        kernel = page_fill_kernel
-        operands += in_hbm(kv_rows, lengths, owners)
-        out_shape.append(
-            jax.ShapeDtypeStruct(
-                (lengths.shape[0], PAGE_FOLD, 2 * kv_rows.shape[1]), jnp.bfloat16
-            )
-        )
-        scratch += [
+    return pl.pallas_call(
+        page_kernel,
+        out_shape=jax.ShapeDtypeStruct(
+            (lengths.shape[0], PAGE_FOLD, 2 * kv_rows.shape[1]), jnp.bfloat16
+        ),
+        in_specs=[hbm, hbm, hbm, pl.BlockSpec(memory_space=pl.ANY)],
+        out_specs=pl.BlockSpec(memory_space=pltpu.VMEM),
+        scratch_shapes=[
             pltpu.VMEM(kv_rows.shape, kv_rows.dtype),
             pltpu.SMEM(lengths.shape, jnp.int32),
             pltpu.SMEM(owners.shape, jnp.int32),
             pltpu.SemaphoreType.DMA((3,)),
-        ]
-    return pl.pallas_call(
-        functools.partial(kernel, expert=expert),
-        out_shape=out_shape,
-        in_specs=[hbm, hbm, pl.BlockSpec(memory_space=pl.ANY)] + [hbm] * (len(operands) - 3),
-        out_specs=[vmem] * len(out_shape),
-        scratch_shapes=scratch,
+        ],
         compiler_params=pltpu.CompilerParams(vmem_limit_bytes=SMALL_VMEM),
-        cost_estimate=pl.CostEstimate(
-            flops=0, bytes_accessed=6 * ff_part * width, transcendentals=0
-        ),
-    )(*operands)
+    )(*in_hbm(kv_rows, lengths, owners), after)
 
 
 def final_kernel(hidden_ref, own_ref, down_ref, up_ref, pages_ref, mixed_ref, cache_ref):
@@ -248,9 +214,8 @@
 
 
 def expert_kernel(
-    gain_ref, gate_up_ref, down_ref, *refs, held, parts, chips, fills,
+    gain_ref, gate_up_ref, down_ref, *refs, held, parts, chips,
 ):
-    held_refs, refs = refs[: 2 * fills], refs[2 * fills :]
     block_refs, out_refs = refs[: parts * chips * CORES], refs[parts * chips * CORES :]
     out_refs, scratch = out_refs[: len(RETURNS) * CORES], out_refs[len(RETURNS) * CORES :]
     (
@@ -269,8 +234,8 @@
 
     gain_copy = pltpu.make_async_copy(gain_ref, gain_buf, gain_sem)
     gain_copy.start()
-    for slot in range(min(slots, held - fills)):
-        for copy in fetch(fills + slot, slot):
+    for h in range(min(slots, held)):
+        for copy in fetch(h, h):
             copy.start()
 
     column = lax.axis_index("mp")
@@ -340,10 +305,7 @@
                 ).astype(jnp.bfloat16)
 
     def rows_of(h):
-        first = [(z * held + h) * CAP for z in range(parts)]
-        if not isinstance(h, int):
-            first = [pl.multiple_of(at, CAP) for at in first]
-        return [pl.ds(at, CAP) for at in first]
+        return [pl.ds(pl.multiple_of((z * held + h) * CAP, CAP), CAP) for z in range(parts)]
 
     def one_expert(h, gate_up, down):
         picked = jnp.concatenate([picked_ref[at, :] for at in rows_of(h)], axis=0)
@@ -363,11 +325,8 @@
                 served[z * CAP : (z + 1) * CAP, :] * slot_gate_ref[at, :]
             ).astype(jnp.bfloat16)
 
-    for h in range(fills):
-        one_expert(h, held_refs[2 * h], held_refs[2 * h + 1])
-
     def streamed(h, carry):
-        slot = lax.rem(h - fills, slots)
+        slot = lax.rem(h, slots)
         for copy in fetch(h, slot):
             copy.wait()
         one_expert(h, gu_buf.at[slot], down_buf.at[slot])
@@ -379,7 +338,7 @@
 
         return carry
 
-    lax.fori_loop(fills, held, streamed, 0)
+    lax.fori_loop(0, held, streamed, 0)
 
     for group, members in enumerate(RETURNS):
         for i, z in enumerate(members):
@@ -392,7 +351,7 @@
                     ).astype(jnp.bfloat16)
 
 
-def expert_sums(gain, gate_up_weight, down_weight, held_weights, blocks):
+def expert_sums(gain, gate_up_weight, down_weight, blocks):
     parts, chips = len(blocks), len(blocks[0])
     _, block_rows, width = blocks[0][0][0].shape
     tok_node = block_rows - TOPK
@@ -404,18 +363,17 @@
     all_slots = held * capacity
     vmem = pl.BlockSpec(memory_space=pltpu.VMEM)
     hbm = pl.BlockSpec(memory_space=pltpu.HBM)
-    held_weights = [pltpu.with_memory_space_constraint(w, pltpu.VMEM) for w in held_weights]
     flat = [blocks[z][x][c] for z in range(parts) for x in range(chips) for c in range(CORES)]
     sums = pl.pallas_call(
         functools.partial(
-            expert_kernel, held=held, parts=parts, chips=chips, fills=len(held_weights) // 2
+            expert_kernel, held=held, parts=parts, chips=chips
         ),
         out_shape=[
             jax.ShapeDtypeStruct((chips, len(members), tok_node, width), jnp.bfloat16)
             for members in RETURNS
             for _ in range(CORES)
         ],
-        in_specs=[hbm] * 3 + [vmem] * (len(held_weights) + len(flat)),
+        in_specs=[hbm] * 3 + [vmem] * len(flat),
         out_specs=[vmem] * (len(RETURNS) * CORES),
         scratch_shapes=[
             pltpu.VMEM((parts, held * CAP, tok_node), jnp.bfloat16),
@@ -433,7 +391,7 @@
             bytes_accessed=6 * ff_dev * model_width,
             transcendentals=0,
         ),
-    )(*in_hbm(gain), gate_up_weight, down_weight, *held_weights, *flat)
+    )(*in_hbm(gain), gate_up_weight, down_weight, *flat)
     return [sums[g * CORES : (g + 1) * CORES] for g in range(len(RETURNS))]
 
 
@@ -522,24 +480,14 @@
     block = packed(hidden_states, routes, gates)
 
     by_z = {0: block, 1: shift_dp(block, 1), 3: shift_dp(block, -1)}
-    own_x = [shift_x(block, s) for s in range(1, chips)]
-    *held_a, pages = filled(gate_up_weight, down_weight, 0, block, (kv_rows, lengths, owners))
-    own_core = [other_core(block)]
-    by_z, own_x, own_core, held_a = lax.optimization_barrier((by_z, own_x, own_core, held_a))
+    pages = kv_pages(kv_rows, lengths, owners, block)
     by_z[2] = shift_dp(by_z[1], 1)
-    chip_rows = {z: [by_z[z]] + [shift_x(by_z[z], s) for s in range(1, chips)] for z in (1, 3)}
-    held_b = filled(gate_up_weight, down_weight, 1, by_z[3])
-    by_z[2], chip_rows, held_b = lax.optimization_barrier((by_z[2], chip_rows, held_b))
-    chip_rows[0] = [block] + own_x
-    chip_rows[2] = [by_z[2]] + [shift_x(by_z[2], s) for s in range(1, chips)]
-    own_core += [other_core(value) for value in own_x]
-    blocks = [list(zip(chip_rows[0], own_core))]
-    blocks += [
-        [(value, other_core(value)) for value in chip_rows[z]] for z in range(1, node_count)
+    chip_rows = {z: [by_z[z]] + [shift_x(by_z[z], s) for s in range(1, chips)] for z in by_z}
+    chip_rows[1], pages = lax.optimization_barrier((chip_rows[1], pages))
+    blocks = [
+        [(value, other_core(value)) for value in chip_rows[z]] for z in range(node_count)
     ]
-    sums = expert_sums(
-        norm_gain[None, :], gate_up_weight, down_weight, [*held_a, *held_b], blocks
-    )
+    sums = expert_sums(norm_gain[None, :], gate_up_weight, down_weight, blocks)
 
     over = [other_core(send) for _, send in sums]
     chip_sums = [added(keep, came) for (keep, _), came in zip(sums, over)]

time: 83 us -> 84 us (1.012)
  waiting for transfers between devices: 18.7 us -> 23.8 us
  Pallas kernels: 38.6 us -> 35 us
    pallas_call x2 -> x1, Pallas kernels: 7.62 us -> 1.09 us  [kv_pages(): pl.pallas_call(page_kernel, out_shape=jax.ShapeDtypeStruct((lengths.shape...]
    ppermute x6, waiting for transfers between devices: 8.68 us -> 12.2 us  [shift_dp(): lax.ppermute(value, 'dp', [(i, (i + shift) % count) for i in range(count)])]
    pallas_call x1, Pallas kernels: 29.2 us -> 32.2 us  [expert_sums(): pl.pallas_call(functools.partial(expert_kernel, held=held, parts=parts, c...]
    ppermute x11, waiting for transfers between devices: 1.75 us -> 2.59 us  [other_core(): return lax.ppermute(value, 'mp', [(i, i ^ 1) for i in range(count)])]
  transfers between devices with their start and end apart: 24 -> 24, of which waited for: 13 -> 11; matrix products, arithmetic and copies ran while one was open for 1% -> 1% of each run, Pallas kernels for 9% -> 1%
where the time goes in v10:
time: 84 us; the launch traced here: 83.8 us
  Pallas kernels  35 us (42%)
  waiting for transfers between devices  23.8 us (28%)
  starting transfers between devices  23.6 us (28%)
    pallas_call x1, Pallas kernels, expert_sums(): pl.pallas_call(functools.partial(expert_kernel, held=held, parts=parts, c...  32.2 us
    ppermute x6, starting transfers between devices, shift_dp(): lax.ppermute(value, 'dp', [(i, (i + shift) % count) for i in range(count)])  12.3 us
    ppermute x6, waiting for transfers between devices, shift_dp(): lax.ppermute(value, 'dp', [(i, (i + shift) % count) for i in range(count)])  12.2 us
    ppermute x7, starting transfers between devices, shift_x(): lax.ppermute(value, 'mp', [(i, (i + CORES * shift) % count) for i in rang...  9.5 us
    ppermute x7, waiting for transfers between devices, shift_x(): lax.ppermute(value, 'mp', [(i, (i + CORES * shift) % count) for i in rang...  9.01 us
    ppermute x11, waiting for transfers between devices, other_core(): return lax.ppermute(value, 'mp', [(i, i ^ 1) for i in range(count)])  2.59 us
    ppermute x11, starting transfers between devices, other_core(): return lax.ppermute(value, 'mp', [(i, i ^ 1) for i in range(count)])  1.81 us
  transfers between devices with their start and end apart: 24, of which 11 were waited for; matrix products, arithmetic and copies ran while one was open for 1% of the time, Pallas kernels for 1%

profile of v10, /device:TPU:0, one launch (start us, length us, event | category | flops | bytes accessed | tf_op | source)
XLA Modules:
  0.0 83.8 jit_solution(12240624486312794433)
XLA Ops:
  0.6 1.0 %shard_map.104.after_ref.refs_0_ = bf16[1,136,512]{2,1,0:T(8,128)(2,1)S(1)} custom-call(bf16[128,512]{1,0:T(8,128)(2,1)} %hidden_ref.3, s32[8,128]{1,0:T(8,128)} %bitcast.42, f32[8,128]{1,0:T(8,128)} %bitcast.43), custom_call_target="tpu_custom_call" | custom-call | tf_op jit(solution)/shard_map/pallas_call | solution.py:98
  1.6 3.1 %collective-permute-start.3 = (bf16[1,136,512]{2,1,0:T(8,128)(2,1)S(1)}, bf16[1,136,512]{2,1,0:T(8,128)(2,1)S(1)}, u32[]{:S(2)}, u32[]{:S(2)}) collective-permute-start(bf16[1,136,512]{2,1,0:T(8,128)(2,1)S(1)} %shard_map.104.after_ref.refs_0_), channel_id=1, source_target_pairs={{0,4},{4,8},{8,12},{12,0},{1,5},{5,9},{9,13},{13,1},{2,6},{6,10},{... | collective-permute-start | bytes 417800 | tf_op jit(solution)/shard_map/ppermute | solution.py:57
  4.7 2.1 %collective-permute-start.11 = (bf16[1,136,512]{2,1,0:T(8,128)(2,1)S(1)}, bf16[1,136,512]{2,1,0:T(8,128)(2,1)S(1)}, u32[]{:S(2)}, u32[]{:S(2)}) collective-permute-start(bf16[1,136,512]{2,1,0:T(8,128)(2,1)S(1)} %shard_map.104.after_ref.refs_0_), channel_id=1, source_target_pairs={{0,12},{4,0},{8,4},{12,8},{1,13},{5,1},{9,5},{13,9},{2,14},{6,2},{... | collective-permute-start | bytes 417800 | tf_op jit(solution)/shard_map/ppermute | solution.py:57
  6.8 1.6 %collective-permute-start.1 = (bf16[1,136,512]{2,1,0:T(8,128)(2,1)S(1)}, bf16[1,136,512]{2,1,0:T(8,128)(2,1)S(1)}, u32[]{:S(2)}, u32[]{:S(2)}) collective-permute-start(bf16[1,136,512]{2,1,0:T(8,128)(2,1)S(1)} %shard_map.104.after_ref.refs_0_), channel_id=1, source_target_pairs={{0,2},{1,3},{2,0},{3,1},{4,6},{5,7},{6,4},{7,5},{8,10},{9,11},{10,... | collective-permute-start | bytes 417800 | tf_op jit(solution)/shard_map/ppermute | solution.py:62
  8.5 2.8 %collective-permute-done.3.refs_4_ = bf16[1,136,512]{2,1,0:T(8,128)(2,1)S(1)} collective-permute-done((bf16[1,136,512]{2,1,0:T(8,128)(2,1)S(1)}, bf16[1,136,512]{2,1,0:T(8,128)(2,1)S(1)}, u32[]{:S(2)}, u32[]{:S(2)}) %collective-permute-start.3) | collective-permute-done | bytes 139296 | tf_op jit(solution)/shard_map/ppermute | solution.py:57
  11.3 1.7 %collective-permute-start.4 = (bf16[1,136,512]{2,1,0:T(8,128)(2,1)S(1)}, bf16[1,136,512]{2,1,0:T(8,128)(2,1)S(1)}, u32[]{:S(2)}, u32[]{:S(2)}) collective-permute-start(bf16[1,136,512]{2,1,0:T(8,128)(2,1)S(1)} %collective-permute-done.3.refs_4_), channel_id=1, source_target_pairs={{0,2},{1,3},{2,0},{3,1},{4,6},{5,7},{6,4},{7,5},{8,10},{9,11},{10,... | collective-permute-start | bytes 417800 | tf_op jit(solution)/shard_map/ppermute | solution.py:62
  13.0 1.3 %collective-permute-start.13 = (bf16[1,136,512]{2,1,0:T(8,128)(2,1)S(1)}, bf16[1,136,512]{2,1,0:T(8,128)(2,1)S(1)}, u32[]{:S(2)}, u32[]{:S(2)}) collective-permute-start(bf16[1,136,512]{2,1,0:T(8,128)(2,1)S(1)} %collective-permute-done.11.refs_12_), channel_id=1, source_target_pairs={{0,2},{1,3},{2,0},{3,1},{4,6},{5,7},{6,4},{7,5},{8,10},{9,11},{10,... | collective-permute-start | bytes 417800 | tf_op jit(solution)/shard_map/ppermute | solution.py:62
  14.3 2.6 %collective-permute-done.4.refs_6_ = bf16[1,136,512]{2,1,0:T(8,128)(2,1)S(1)} collective-permute-done((bf16[1,136,512]{2,1,0:T(8,128)(2,1)S(1)}, bf16[1,136,512]{2,1,0:T(8,128)(2,1)S(1)}, u32[]{:S(2)}, u32[]{:S(2)}) %collective-permute-start.4) | collective-permute-done | bytes 139296 | tf_op jit(solution)/shard_map/ppermute | solution.py:62
  16.9 2.9 %collective-permute-done.7.refs_8_ = bf16[1,136,512]{2,1,0:T(8,128)(2,1)S(1)} collective-permute-done((bf16[1,136,512]{2,1,0:T(8,128)(2,1)S(1)}, bf16[1,136,512]{2,1,0:T(8,128)(2,1)S(1)}, u32[]{:S(2)}, u32[]{:S(2)}) %collective-permute-start.7) | collective-permute-done | bytes 139296 | tf_op jit(solution)/shard_map/ppermute | solution.py:57
  19.8 0.4 collective-permute-start.9
  20.3 1.1 %shard_map.105.pages_ref = bf16[4,24,512]{2,1,0:T(8,128)(2,1)S(1)} custom-call(bf16[128,256]{1,0:T(8,128)(2,1)} %kv_ref.1, s32[4,4]{1,0:T(4,128)} %lengths_ref.1, s32[4,4]{1,0:T(4,128)} %owners_ref.1, bf16[1,136,512]{2,1,0:T(8,128)(2,1)S(1)} %shard_map.104.after_ref.refs_0_), custom_call_target="tpu_custom_call" | custom-call | tf_op jit(solution)/shard_map/pallas_call | solution.py:162
  21.5 0.5 collective-permute-start.6
  22.0 0.4 collective-permute-start.14
  22.5 2.4 %collective-permute-done.9.refs_10_ = bf16[1,136,512]{2,1,0:T(8,128)(2,1)S(1)} collective-permute-done((bf16[1,136,512]{2,1,0:T(8,128)(2,1)S(1)}, bf16[1,136,512]{2,1,0:T(8,128)(2,1)S(1)}, u32[]{:S(2)}, u32[]{:S(2)}) %collective-permute-start.9) | collective-permute-done | bytes 139296 | tf_op jit(solution)/shard_map/ppermute | solution.py:62
  24.9 1.3 %collective-permute-done.10.refs_11_ = bf16[1,136,512]{2,1,0:T(8,128)(2,1)S(1)} collective-permute-done((bf16[1,136,512]{2,1,0:T(8,128)(2,1)S(1)}, bf16[1,136,512]{2,1,0:T(8,128)(2,1)S(1)}, u32[]{:S(2)}, u32[]{:S(2)}) %collective-permute-start.10) | collective-permute-done | bytes 139296 | tf_op jit(solution)/shard_map/ppermute | solution.py:67
  26.3 32.2 %shard_map.106 = (bf16[2,1,128,512]{3,2,1,0:T(8,128)(2,1)S(1)}, bf16[2,1,128,512]{3,2,1,0:T(8,128)(2,1)S(1)}, bf16[2,2,128,512]{3,2,1,0:T(8,128)(2,1)S(1)}, bf16...) custom-call(f32[1,2048]{1,0:T(1,128)} %bitcast.41, ...), custom_call_target="tpu_custom_call" | custom-call | flops 4831838208 | bytes 75497472 | tf_op jit(solution)/shard_map/pallas_call | solution.py:367
  58.5 0.2 collective-permute-start.19
  58.7 0.4 collective-permute-start.16
  59.1 0.1 collective-permute-start.15
  59.2 0.9 %collective-permute-done.19 = bf16[2,1,128,512]{3,2,1,0:T(8,128)(2,1)S(1)} collective-permute-done((bf16[2,1,128,512]{3,2,1,0:T(8,128)(2,1)S(1)}, bf16[2,1,128,512]{3,2,1,0:T(8,128)(2,1)S(1)}, u32[]{:S(2)}, u32[]{:S(2)}) %collective-permute-start.19) | collective-permute-done | bytes 262176 | tf_op jit(solution)/shard_map/ppermute | solution.py:67
  60.2 0.7 collective-permute-start.20
  60.8 0.4 collective-permute-done.15
  61.3 0.1 add_convert_fusion
  61.4 1.1 %collective-permute-start.17 = (bf16[2,128,512]{2,1,0:T(8,128)(2,1)S(1)}, bf16[2,128,512]{2,1,0:T(8,128)(2,1)S(1)}, u32[]{:S(2)}, u32[]{:S(2)}) collective-permute-start(bf16[2,128,512]{2,1,0:T(8,128)(2,1)S(1)} %slice_bitcast_fusion.1), channel_id=1, source_target_pairs={{0,2},{1,3},{2,0},{3,1},{4,6},{5,7},{6,4},{7,5},{8,10},{9,11},{10,... | collective-permute-start | bytes 786440 | tf_op jit(solution)/shard_map/ppermute | solution.py:62
  62.6 4.0 %collective-permute-done.20 = bf16[1,128,512]{2,1,0:T(8,128)(2,1)S(1)} collective-permute-done((bf16[1,128,512]{2,1,0:T(8,128)(2,1)S(1)}, bf16[1,128,512]{2,1,0:T(8,128)(2,1)S(1)}, u32[]{:S(2)}, u32[]{:S(2)}) %collective-permute-start.20) | collective-permute-done | bytes 131104 | tf_op jit(solution)/shard_map/ppermute | solution.py:62
  66.6 2.7 %collective-permute-start.21 = (bf16[152,512]{1,0:T(8,128)(2,1)S(1)}, bf16[152,512]{1,0:T(8,128)(2,1)S(1)}, u32[]{:S(2)}, u32[]{:S(2)}) collective-permute-start(bf16[152,512]{1,0:T(8,128)(2,1)S(1)} %pad_maximum_fusion.1), channel_id=1, source_target_pairs={{0,12},{4,0},{8,4},{12,8},{1,13},{5,1},{9,5},{13,9},{2,14},{6,2},{... | collective-permute-start | bytes 466952 | tf_op jit(solution)/shard_map/ppermute | solution.py:57
  69.3 3.5 %collective-permute-done.21 = bf16[152,512]{1,0:T(8,128)(2,1)S(1)} collective-permute-done((bf16[152,512]{1,0:T(8,128)(2,1)S(1)}, bf16[152,512]{1,0:T(8,128)(2,1)S(1)}, u32[]{:S(2)}, u32[]{:S(2)}) %collective-permute-start.21) | collective-permute-done | bytes 155680 | tf_op jit(solution)/shard_map/ppermute | solution.py:57
  73.0 2.6 %collective-permute-start.18 = (bf16[1,128,512]{2,1,0:T(8,128)(2,1)S(1)}, bf16[1,128,512]{2,1,0:T(8,128)(2,1)S(1)}, u32[]{:S(2)}, u32[]{:S(2)}) collective-permute-start(bf16[1,128,512]{2,1,0:T(8,128)(2,1)S(1)} %slice_bitcast_fusion.6), channel_id=1, source_target_pairs={{0,2},{1,3},{2,0},{3,1},{4,6},{5,7},{6,4},{7,5},{8,10},{9,11},{10,... | collective-permute-start | bytes 393224 | tf_op jit(solution)/shard_map/ppermute | solution.py:62
  75.6 4.4 %collective-permute-start.22 = (bf16[176,512]{1,0:T(8,128)(2,1)S(1)}, bf16[176,512]{1,0:T(8,128)(2,1)S(1)}, u32[]{:S(2)}, u32[]{:S(2)}) collective-permute-start(bf16[176,512]{1,0:T(8,128)(2,1)S(1)} %pad_maximum_fusion), channel_id=1, source_target_pairs={{0,12},{4,0},{8,4},{12,8},{1,13},{5,1},{9,5},{13,9},{2,14},{6,2},{... | collective-permute-start | bytes 540680 | tf_op jit(solution)/shard_map/ppermute | solution.py:57
  80.1 1.3 %collective-permute-done.23.up_ref = bf16[152,512]{1,0:T(8,128)(2,1)S(1)} collective-permute-done((bf16[152,512]{1,0:T(8,128)(2,1)S(1)}, bf16[152,512]{1,0:T(8,128)(2,1)S(1)}, u32[]{:S(2)}, u32[]{:S(2)}) %collective-permute-start.23) | collective-permute-done | bytes 155680 | tf_op jit(solution)/shard_map/ppermute | solution.py:57
  81.4 1.7 %collective-permute-done.22.down_ref = bf16[176,512]{1,0:T(8,128)(2,1)S(1)} collective-permute-done((bf16[176,512]{1,0:T(8,128)(2,1)S(1)}, bf16[176,512]{1,0:T(8,128)(2,1)S(1)}, u32[]{:S(2)}, u32[]{:S(2)}) %collective-permute-start.22) | collective-permute-done | bytes 180256 | tf_op jit(solution)/shard_map/ppermute | solution.py:57
  83.1 0.7 shard_map.107
  (38 shorter events, 0.7 us)
Async XLA Ops:
  0.6 82.5 %copy-start = (bf16[128,512]{1,0:T(8,128)(2,1)S(1)}, bf16[128,512]{1,0:T(8,128)(2,1)}, u32[]{:S(2)}) copy-start(bf16[128,512]{1,0:T(8,128)(2,1)} %hidden_ref.3) | copy-start | bytes 393220
  1.6 9.6 %collective-permute-start.3 = (bf16[1,136,512]{2,1,0:T(8,128)(2,1)S(1)}, bf16[1,136,512]{2,1,0:T(8,128)(2,1)S(1)}, u32[]{:S(2)}, u32[]{:S(2)}) collective-permute-start(bf16[1,136,512]{2,1,0:T(8,128)(2,1)S(1)} %shard_map.104.after_ref.refs_0_), channel_id=1, source_target_pairs={{0,4},{4,8},{8,12},{12,0},{1,5},{5,9},{9,13},{13,1},{2,6},{6,10},{... | collective-permute-start | bytes 417800 | tf_op jit(solution)/shard_map/ppermute | solution.py:57
  4.7 8.3 %collective-permute-start.11 = (bf16[1,136,512]{2,1,0:T(8,128)(2,1)S(1)}, bf16[1,136,512]{2,1,0:T(8,128)(2,1)S(1)}, u32[]{:S(2)}, u32[]{:S(2)}) collective-permute-start(bf16[1,136,512]{2,1,0:T(8,128)(2,1)S(1)} %shard_map.104.after_ref.refs_0_), channel_id=1, source_target_pairs={{0,12},{4,0},{8,4},{12,8},{1,13},{5,1},{9,5},{13,9},{2,14},{6,2},{... | collective-permute-start | bytes 417800 | tf_op jit(solution)/shard_map/ppermute | solution.py:57
  6.8 7.5 %collective-permute-start.1 = (bf16[1,136,512]{2,1,0:T(8,128)(2,1)S(1)}, bf16[1,136,512]{2,1,0:T(8,128)(2,1)S(1)}, u32[]{:S(2)}, u32[]{:S(2)}) collective-permute-start(bf16[1,136,512]{2,1,0:T(8,128)(2,1)S(1)} %shard_map.104.after_ref.refs_0_), channel_id=1, source_target_pairs={{0,2},{1,3},{2,0},{3,1},{4,6},{5,7},{6,4},{7,5},{8,10},{9,11},{10,... | collective-permute-start | bytes 417800 | tf_op jit(solution)/shard_map/ppermute | solution.py:62
  11.3 5.6 %collective-permute-start.4 = (bf16[1,136,512]{2,1,0:T(8,128)(2,1)S(1)}, bf16[1,136,512]{2,1,0:T(8,128)(2,1)S(1)}, u32[]{:S(2)}, u32[]{:S(2)}) collective-permute-start(bf16[1,136,512]{2,1,0:T(8,128)(2,1)S(1)} %collective-permute-done.3.refs_4_), channel_id=1, source_target_pairs={{0,2},{1,3},{2,0},{3,1},{4,6},{5,7},{6,4},{7,5},{8,10},{9,11},{10,... | collective-permute-start | bytes 417800 | tf_op jit(solution)/shard_map/ppermute | solution.py:62
  13.0 6.9 %collective-permute-start.7 = (bf16[1,136,512]{2,1,0:T(8,128)(2,1)S(1)}, bf16[1,136,512]{2,1,0:T(8,128)(2,1)S(1)}, u32[]{:S(2)}, u32[]{:S(2)}) collective-permute-start(bf16[1,136,512]{2,1,0:T(8,128)(2,1)S(1)} %collective-permute-done.3.refs_4_), channel_id=1, source_target_pairs={{0,4},{4,8},{8,12},{12,0},{1,5},{5,9},{9,13},{13,1},{2,6},{6,10},{... | collective-permute-start | bytes 417800 | tf_op jit(solution)/shard_map/ppermute | solution.py:57
  13.0 8.4 %collective-permute-start = (bf16[1,136,512]{2,1,0:T(8,128)(2,1)S(1)}, bf16[1,136,512]{2,1,0:T(8,128)(2,1)S(1)}, u32[]{:S(2)}, u32[]{:S(2)}) collective-permute-start(bf16[1,136,512]{2,1,0:T(8,128)(2,1)S(1)} %shard_map.104.after_ref.refs_0_), channel_id=1, source_target_pairs={{0,1},{1,0},{2,3},{3,2},{4,5},{5,4},{6,7},{7,6},{8,9},{9,8},{10,11... | collective-permute-start | bytes 417800 | tf_op jit(solution)/shard_map/ppermute | solution.py:67
  13.0 8.5 %collective-permute-start.13 = (bf16[1,136,512]{2,1,0:T(8,128)(2,1)S(1)}, bf16[1,136,512]{2,1,0:T(8,128)(2,1)S(1)}, u32[]{:S(2)}, u32[]{:S(2)}) collective-permute-start(bf16[1,136,512]{2,1,0:T(8,128)(2,1)S(1)} %collective-permute-done.11.refs_12_), channel_id=1, source_target_pairs={{0,2},{1,3},{2,0},{3,1},{4,6},{5,7},{6,4},{7,5},{8,10},{9,11},{10,... | collective-permute-start | bytes 417800 | tf_op jit(solution)/shard_map/ppermute | solution.py:62
  14.3 7.6 %collective-permute-start.12 = (bf16[1,136,512]{2,1,0:T(8,128)(2,1)S(1)}, bf16[1,136,512]{2,1,0:T(8,128)(2,1)S(1)}, u32[]{:S(2)}, u32[]{:S(2)}) collective-permute-start(bf16[1,136,512]{2,1,0:T(8,128)(2,1)S(1)} %collective-permute-done.11.refs_12_), channel_id=1, source_target_pairs={{0,1},{1,0},{2,3},{3,2},{4,5},{5,4},{6,7},{7,6},{8,9},{9,8},{10,11... | collective-permute-start | bytes 417800 | tf_op jit(solution)/shard_map/ppermute | solution.py:67
  16.9 5.1 %collective-permute-start.2 = (bf16[1,136,512]{2,1,0:T(8,128)(2,1)S(1)}, bf16[1,136,512]{2,1,0:T(8,128)(2,1)S(1)}, u32[]{:S(2)}, u32[]{:S(2)}) collective-permute-start(bf16[1,136,512]{2,1,0:T(8,128)(2,1)S(1)} %collective-permute-done.1.refs_2_), channel_id=1, source_target_pairs={{0,1},{1,0},{2,3},{3,2},{4,5},{5,4},{6,7},{7,6},{8,9},{9,8},{10,11... | collective-permute-start | bytes 417800 | tf_op jit(solution)/shard_map/ppermute | solution.py:67
  19.8 5.1 %collective-permute-start.9 = (bf16[1,136,512]{2,1,0:T(8,128)(2,1)S(1)}, bf16[1,136,512]{2,1,0:T(8,128)(2,1)S(1)}, u32[]{:S(2)}, u32[]{:S(2)}) collective-permute-start(bf16[1,136,512]{2,1,0:T(8,128)(2,1)S(1)} %collective-permute-done.7.refs_8_), channel_id=1, source_target_pairs={{0,2},{1,3},{2,0},{3,1},{4,6},{5,7},{6,4},{7,5},{8,10},{9,11},{10,... | collective-permute-start | bytes 417800 | tf_op jit(solution)/shard_map/ppermute | solution.py:62
  21.4 3.5 %collective-permute-start.5 = (bf16[1,136,512]{2,1,0:T(8,128)(2,1)S(1)}, bf16[1,136,512]{2,1,0:T(8,128)(2,1)S(1)}, u32[]{:S(2)}, u32[]{:S(2)}) collective-permute-start(bf16[1,136,512]{2,1,0:T(8,128)(2,1)S(1)} %collective-permute-done.3.refs_4_), channel_id=1, source_target_pairs={{0,1},{1,0},{2,3},{3,2},{4,5},{5,4},{6,7},{7,6},{8,9},{9,8},{10,11... | collective-permute-start | bytes 417800 | tf_op jit(solution)/shard_map/ppermute | solution.py:67
  21.5 3.4 %collective-permute-start.6 = (bf16[1,136,512]{2,1,0:T(8,128)(2,1)S(1)}, bf16[1,136,512]{2,1,0:T(8,128)(2,1)S(1)}, u32[]{:S(2)}, u32[]{:S(2)}) collective-permute-start(bf16[1,136,512]{2,1,0:T(8,128)(2,1)S(1)} %collective-permute-done.4.refs_6_), channel_id=1, source_target_pairs={{0,1},{1,0},{2,3},{3,2},{4,5},{5,4},{6,7},{7,6},{8,9},{9,8},{10,11... | collective-permute-start | bytes 417800 | tf_op jit(solution)/shard_map/ppermute | solution.py:67
  22.0 3.0 %collective-permute-start.8 = (bf16[1,136,512]{2,1,0:T(8,128)(2,1)S(1)}, bf16[1,136,512]{2,1,0:T(8,128)(2,1)S(1)}, u32[]{:S(2)}, u32[]{:S(2)}) collective-permute-start(bf16[1,136,512]{2,1,0:T(8,128)(2,1)S(1)} %collective-permute-done.7.refs_8_), channel_id=1, source_target_pairs={{0,1},{1,0},{2,3},{3,2},{4,5},{5,4},{6,7},{7,6},{8,9},{9,8},{10,11... | collective-permute-start | bytes 417800 | tf_op jit(solution)/shard_map/ppermute | solution.py:67
  22.0 2.9 %collective-permute-start.14 = (bf16[1,136,512]{2,1,0:T(8,128)(2,1)S(1)}, bf16[1,136,512]{2,1,0:T(8,128)(2,1)S(1)}, u32[]{:S(2)}, u32[]{:S(2)}) collective-permute-start(bf16[1,136,512]{2,1,0:T(8,128)(2,1)S(1)} %collective-permute-done.13.refs_14_), channel_id=1, source_target_pairs={{0,1},{1,0},{2,3},{3,2},{4,5},{5,4},{6,7},{7,6},{8,9},{9,8},{10,11... | collective-permute-start | bytes 417800 | tf_op jit(solution)/shard_map/ppermute | solution.py:67
  24.9 1.4 %collective-permute-start.10 = (bf16[1,136,512]{2,1,0:T(8,128)(2,1)S(1)}, bf16[1,136,512]{2,1,0:T(8,128)(2,1)S(1)}, u32[]{:S(2)}, u32[]{:S(2)}) collective-permute-start(bf16[1,136,512]{2,1,0:T(8,128)(2,1)S(1)} %collective-permute-done.9.refs_10_), channel_id=1, source_target_pairs={{0,1},{1,0},{2,3},{3,2},{4,5},{5,4},{6,7},{7,6},{8,9},{9,8},{10,11... | collective-permute-start | bytes 417800 | tf_op jit(solution)/shard_map/ppermute | solution.py:67
  58.5 1.6 %collective-permute-start.19 = (bf16[2,1,128,512]{3,2,1,0:T(8,128)(2,1)S(1)}, bf16[2,1,128,512]{3,2,1,0:T(8,128)(2,1)S(1)}, u32[]{:S(2)}, u32[]{:S(2)}) collective-permute-start(bf16[2,1,128,512]{3,2,1,0:T(8,128)(2,1)S(1)} %get-tuple-element.21), channel_id=1, source_target_pairs={{0,1},{1,0},{2,3},{3,2},{4,5},{5,4},{6,7},{7,6},{8,9},{9,8},{10,11... | collective-permute-start | bytes 786440 | tf_op jit(solution)/shard_map/ppermute | solution.py:67
  58.7 2.6 %collective-permute-start.16 = (bf16[2,2,128,512]{3,2,1,0:T(8,128)(2,1)S(1)}, bf16[2,2,128,512]{3,2,1,0:T(8,128)(2,1)S(1)}, u32[]{:S(2)}, u32[]{:S(2)}) collective-permute-start(bf16[2,2,128,512]{3,2,1,0:T(8,128)(2,1)S(1)} %get-tuple-element.18), channel_id=1, source_target_pairs={{0,1},{1,0},{2,3},{3,2},{4,5},{5,4},{6,7},{7,6},{8,9},{9,8},{10,11... | collective-permute-start | bytes 1572872 | tf_op jit(solution)/shard_map/ppermute | solution.py:67
  59.1 2.1 %collective-permute-start.15 = (bf16[2,1,128,512]{3,2,1,0:T(8,128)(2,1)S(1)}, bf16[2,1,128,512]{3,2,1,0:T(8,128)(2,1)S(1)}, u32[]{:S(2)}, u32[]{:S(2)}) collective-permute-start(bf16[2,1,128,512]{3,2,1,0:T(8,128)(2,1)S(1)} %get-tuple-element.16), channel_id=1, source_target_pairs={{0,1},{1,0},{2,3},{3,2},{4,5},{5,4},{6,7},{7,6},{8,9},{9,8},{10,11... | collective-permute-start | bytes 786440 | tf_op jit(solution)/shard_map/ppermute | solution.py:67
  60.2 6.4 %collective-permute-start.20 = (bf16[1,128,512]{2,1,0:T(8,128)(2,1)S(1)}, bf16[1,128,512]{2,1,0:T(8,128)(2,1)S(1)}, u32[]{:S(2)}, u32[]{:S(2)}) collective-permute-start(bf16[1,128,512]{2,1,0:T(8,128)(2,1)S(1)} %slice_bitcast_fusion.3), channel_id=1, source_target_pairs={{0,2},{1,3},{2,0},{3,1},{4,6},{5,7},{6,4},{7,5},{8,10},{9,11},{10,... | collective-permute-start | bytes 393224 | tf_op jit(solution)/shard_map/ppermute | solution.py:62
  61.4 11.4 %collective-permute-start.17 = (bf16[2,128,512]{2,1,0:T(8,128)(2,1)S(1)}, bf16[2,128,512]{2,1,0:T(8,128)(2,1)S(1)}, u32[]{:S(2)}, u32[]{:S(2)}) collective-permute-start(bf16[2,128,512]{2,1,0:T(8,128)(2,1)S(1)} %slice_bitcast_fusion.1), channel_id=1, source_target_pairs={{0,2},{1,3},{2,0},{3,1},{4,6},{5,7},{6,4},{7,5},{8,10},{9,11},{10,... | collective-permute-start | bytes 786440 | tf_op jit(solution)/shard_map/ppermute | solution.py:62
  66.6 6.2 %collective-permute-start.21 = (bf16[152,512]{1,0:T(8,128)(2,1)S(1)}, bf16[152,512]{1,0:T(8,128)(2,1)S(1)}, u32[]{:S(2)}, u32[]{:S(2)}) collective-permute-start(bf16[152,512]{1,0:T(8,128)(2,1)S(1)} %pad_maximum_fusion.1), channel_id=1, source_target_pairs={{0,12},{4,0},{8,4},{12,8},{1,13},{5,1},{9,5},{13,9},{2,14},{6,2},{... | collective-permute-start | bytes 466952 | tf_op jit(solution)/shard_map/ppermute | solution.py:57
  72.9 8.5 %collective-permute-start.23 = (bf16[152,512]{1,0:T(8,128)(2,1)S(1)}, bf16[152,512]{1,0:T(8,128)(2,1)S(1)}, u32[]{:S(2)}, u32[]{:S(2)}) collective-permute-start(bf16[152,512]{1,0:T(8,128)(2,1)S(1)} %pad_maximum_fusion.2), channel_id=1, source_target_pairs={{0,4},{4,8},{8,12},{12,0},{1,5},{5,9},{9,13},{13,1},{2,6},{6,10},{... | collective-permute-start | bytes 466952 | tf_op jit(solution)/shard_map/ppermute | solution.py:57
  73.0 7.1 %collective-permute-start.18 = (bf16[1,128,512]{2,1,0:T(8,128)(2,1)S(1)}, bf16[1,128,512]{2,1,0:T(8,128)(2,1)S(1)}, u32[]{:S(2)}, u32[]{:S(2)}) collective-permute-start(bf16[1,128,512]{2,1,0:T(8,128)(2,1)S(1)} %slice_bitcast_fusion.6), channel_id=1, source_target_pairs={{0,2},{1,3},{2,0},{3,1},{4,6},{5,7},{6,4},{7,5},{8,10},{9,11},{10,... | collective-permute-start | bytes 393224 | tf_op jit(solution)/shard_map/ppermute | solution.py:62
  75.6 7.5 %collective-permute-start.22 = (bf16[176,512]{1,0:T(8,128)(2,1)S(1)}, bf16[176,512]{1,0:T(8,128)(2,1)S(1)}, u32[]{:S(2)}, u32[]{:S(2)}) collective-permute-start(bf16[176,512]{1,0:T(8,128)(2,1)S(1)} %pad_maximum_fusion), channel_id=1, source_target_pairs={{0,12},{4,0},{8,4},{12,8},{1,13},{5,1},{9,5},{13,9},{2,14},{6,2},{... | collective-permute-start | bytes 540680 | tf_op jit(solution)/shard_map/ppermute | solution.py:57

commit v11 on v9

--- a/solution.py
+++ b/solution.py
@@ -19,7 +19,7 @@
 PAGE_FOLD = 24
 SMALL_VMEM = 4 * 1024 * 1024
 WEIGHT_SLOTS = 3
-EXPERT_VMEM = 31 * 1024 * 1024
+EXPERT_VMEM = 32 * 1024 * 1024
 
 epsilon = 1e-06
 
@@ -349,15 +349,13 @@
         picked = jnp.concatenate([picked_ref[at, :] for at in rows_of(h)], axis=0)
         along = (((1,), (1,)), ((), ()))
         gate_part = lax.dot_general(
-            gate_up[0], picked, along, preferred_element_type=jnp.float32
+            picked, gate_up[0], along, preferred_element_type=jnp.float32
         )
         up_part = lax.dot_general(
-            gate_up[1], picked, along, preferred_element_type=jnp.float32
+            picked, gate_up[1], along, preferred_element_type=jnp.float32
         )
         activated = (jax.nn.silu(gate_part) * up_part).astype(jnp.bfloat16)
-        served = lax.dot_general(
-            activated, down[...], (((0,), (0,)), ((), ())), preferred_element_type=jnp.float32
-        )
+        served = jnp.dot(activated, down[...], preferred_element_type=jnp.float32)
         for z, at in enumerate(rows_of(h)):
             served_ref[at, :] = (
                 served[z * CAP : (z + 1) * CAP, :] * slot_gate_ref[at, :]
@@ -529,7 +527,8 @@
     by_z[2] = shift_dp(by_z[1], 1)
     chip_rows = {z: [by_z[z]] + [shift_x(by_z[z], s) for s in range(1, chips)] for z in (1, 3)}
     held_b = filled(gate_up_weight, down_weight, 1, by_z[3])
-    by_z[2], chip_rows, held_b = lax.optimization_barrier((by_z[2], chip_rows, held_b))
+    by_z[2], *_ = lax.optimization_barrier((by_z[2], *held_b))
+    chip_rows, held_b = lax.optimization_barrier((chip_rows, held_b))
     chip_rows[0] = [block] + own_x
     chip_rows[2] = [by_z[2]] + [shift_x(by_z[2], s) for s in range(1, chips)]
     own_core += [other_core(value) for value in own_x]

time: 83 us -> 85.5 us (1.030)
  Pallas kernels: 38.6 us -> 42 us
  waiting for transfers between devices: 18.7 us -> 17.3 us
    pallas_call x1, Pallas kernels: 29.2 us -> 32.7 us  [expert_sums(): pl.pallas_call(functools.partial(expert_kernel, held=held, parts=parts, c...]
    ppermute x7, waiting for transfers between devices: 8.24 us -> 7.36 us  [shift_x(): lax.ppermute(value, 'mp', [(i, (i + CORES * shift) % count) for i in rang...]
  transfers between devices with their start and end apart: 24 -> 24, of which waited for: 13 -> 11; matrix products, arithmetic and copies ran while one was open for 1% -> 1% of each run, Pallas kernels for 9% -> 9%
where the time goes in v11:
time: 85.5 us; the launch traced here: 85.3 us
  Pallas kernels  42 us (49%)
  starting transfers between devices  24.6 us (29%)
  waiting for transfers between devices  17.3 us (20%)
    pallas_call x1, Pallas kernels, expert_sums(): pl.pallas_call(functools.partial(expert_kernel, held=held, parts=parts, c...  32.7 us
    ppermute x6, starting transfers between devices, shift_dp(): lax.ppermute(value, 'dp', [(i, (i + shift) % count) for i in range(count)])  13.5 us
    ppermute x7, starting transfers between devices, shift_x(): lax.ppermute(value, 'mp', [(i, (i + CORES * shift) % count) for i in rang...  8.94 us
    ppermute x6, waiting for transfers between devices, shift_dp(): lax.ppermute(value, 'dp', [(i, (i + shift) % count) for i in range(count)])  8.19 us
    pallas_call x2, Pallas kernels, filled(): pl.pallas_call(functools.partial(kernel, expert=expert), out_shape=out_sh...  7.62 us
    ppermute x7, waiting for transfers between devices, shift_x(): lax.ppermute(value, 'mp', [(i, (i + CORES * shift) % count) for i in rang...  7.36 us
    ppermute x11, starting transfers between devices, other_core(): return lax.ppermute(value, 'mp', [(i, i ^ 1) for i in range(count)])  2.15 us
    ppermute x11, waiting for transfers between devices, other_core(): return lax.ppermute(value, 'mp', [(i, i ^ 1) for i in range(count)])  1.75 us
  transfers between devices with their start and end apart: 24, of which 11 were waited for; matrix products, arithmetic and copies ran while one was open for 1% of the time, Pallas kernels for 9%

profile of v11, /device:TPU:0, one launch (start us, length us, event | category | flops | bytes accessed | tf_op | source)
XLA Modules:
  0.0 85.3 jit_solution(8793961643157706080)
XLA Ops:
  0.6 1.0 %shard_map.104.after_ref.refs_4_ = bf16[1,136,512]{2,1,0:T(8,128)(2,1)S(1)} custom-call(bf16[128,512]{1,0:T(8,128)(2,1)} %hidden_ref.3, s32[8,128]{1,0:T(8,128)} %bitcast.42, f32[8,128]{1,0:T(8,128)} %bitcast.43), custom_call_target="tpu_custom_call" | custom-call | tf_op jit(solution)/shard_map/pallas_call | solution.py:98
  1.6 3.1 %collective-permute-start = (bf16[1,136,512]{2,1,0:T(8,128)(2,1)S(1)}, bf16[1,136,512]{2,1,0:T(8,128)(2,1)S(1)}, u32[]{:S(2)}, u32[]{:S(2)}) collective-permute-start(bf16[1,136,512]{2,1,0:T(8,128)(2,1)S(1)} %shard_map.104.after_ref.refs_4_), channel_id=1, source_target_pairs={{0,4},{4,8},{8,12},{12,0},{1,5},{5,9},{9,13},{13,1},{2,6},{6,10},{... | collective-permute-start | bytes 417800 | tf_op jit(solution)/shard_map/ppermute | solution.py:57
  4.7 2.1 %collective-permute-start.1 = (bf16[1,136,512]{2,1,0:T(8,128)(2,1)S(1)}, bf16[1,136,512]{2,1,0:T(8,128)(2,1)S(1)}, u32[]{:S(2)}, u32[]{:S(2)}) collective-permute-start(bf16[1,136,512]{2,1,0:T(8,128)(2,1)S(1)} %shard_map.104.after_ref.refs_4_), channel_id=1, source_target_pairs={{0,12},{4,0},{8,4},{12,8},{1,13},{5,1},{9,5},{13,9},{2,14},{6,2},{... | collective-permute-start | bytes 417800 | tf_op jit(solution)/shard_map/ppermute | solution.py:57
  6.8 1.6 %collective-permute-start.2 = (bf16[1,136,512]{2,1,0:T(8,128)(2,1)S(1)}, bf16[1,136,512]{2,1,0:T(8,128)(2,1)S(1)}, u32[]{:S(2)}, u32[]{:S(2)}) collective-permute-start(bf16[1,136,512]{2,1,0:T(8,128)(2,1)S(1)} %shard_map.104.after_ref.refs_4_), channel_id=1, source_target_pairs={{0,2},{1,3},{2,0},{3,1},{4,6},{5,7},{6,4},{7,5},{8,10},{9,11},{10,... | collective-permute-start | bytes 417800 | tf_op jit(solution)/shard_map/ppermute | solution.py:62
  8.4 3.8 %shard_map.105 = (bf16[2,768,2048]{2,1,0:T(8,128)(2,1)S(1)}, bf16[768,2048]{1,0:T(8,128)(2,1)S(1)}, bf16[4,24,512]{2,1,0:T(8,128)(2,1)S(1)}) custom-call(bf16[2,6144,2048]{2,1,0:T(8,128)(2,1)} %gate_up_ref.5, bf16[6144,2048]{1,0:T(8,128)(2,1)} %down_ref.5, bf16[1,136,512]{2,1,0:T(8,128)(2,1)S(1)} %shard_map.104.after_ref.refs_4_, bf16[128,256]{1,0:T(8,128)(2,1)} %kv_ref.1, ...), custom_call_target="tpu_custom_call" | custom-call | bytes 9437184 | tf_op jit(solution)/shard_map/pallas_call | solution.py:200
  12.3 0.5 collective-permute-done.1.after_ref.refs_16_
  12.8 1.1 %collective-permute-start.9 = (bf16[1,136,512]{2,1,0:T(8,128)(2,1)S(1)}, bf16[1,136,512]{2,1,0:T(8,128)(2,1)S(1)}, u32[]{:S(2)}, u32[]{:S(2)}) collective-permute-start(bf16[1,136,512]{2,1,0:T(8,128)(2,1)S(1)} %collective-permute-done.refs_8_), channel_id=1, source_target_pairs={{0,4},{4,8},{8,12},{12,0},{1,5},{5,9},{9,13},{13,1},{2,6},{6,10},{... | collective-permute-start | bytes 417800 | tf_op jit(solution)/shard_map/ppermute | solution.py:57
  13.9 1.5 %collective-permute-start.4 = (bf16[1,136,512]{2,1,0:T(8,128)(2,1)S(1)}, bf16[1,136,512]{2,1,0:T(8,128)(2,1)S(1)}, u32[]{:S(2)}, u32[]{:S(2)}) collective-permute-start(bf16[1,136,512]{2,1,0:T(8,128)(2,1)S(1)} %collective-permute-done.refs_8_), channel_id=1, source_target_pairs={{0,2},{1,3},{2,0},{3,1},{4,6},{5,7},{6,4},{7,5},{8,10},{9,11},{10,... | collective-permute-start | bytes 417800 | tf_op jit(solution)/shard_map/ppermute | solution.py:62
  15.4 0.5 collective-permute-start.5
  16.0 3.8 %shard_map.106 = (bf16[2,768,2048]{2,1,0:T(8,128)(2,1)S(1)}, bf16[768,2048]{1,0:T(8,128)(2,1)S(1)}) custom-call(bf16[2,6144,2048]{2,1,0:T(8,128)(2,1)} %gate_up_ref.5, bf16[6144,2048]{1,0:T(8,128)(2,1)} %down_ref.5, bf16[1,136,512]{2,1,0:T(8,128)(2,1)S(1)} %collective-permute-done.1.after_ref.refs_16_), custom_call_target="tpu_custom_call" | custom-call | bytes 9437184 | tf_op jit(solution)/shard_map/pallas_call | solution.py:200
  19.8 0.4 collective-permute-done.9.refs_12_
  20.2 1.2 %collective-permute-start.11 = (bf16[1,136,512]{2,1,0:T(8,128)(2,1)S(1)}, bf16[1,136,512]{2,1,0:T(8,128)(2,1)S(1)}, u32[]{:S(2)}, u32[]{:S(2)}) collective-permute-start(bf16[1,136,512]{2,1,0:T(8,128)(2,1)S(1)} %collective-permute-done.9.refs_12_), channel_id=1, source_target_pairs={{0,2},{1,3},{2,0},{3,1},{4,6},{5,7},{6,4},{7,5},{8,10},{9,11},{10,... | collective-permute-start | bytes 417800 | tf_op jit(solution)/shard_map/ppermute | solution.py:62
  21.6 0.7 collective-permute-done.5.refs_18_
  22.2 0.5 collective-permute-start.14
  22.8 3.2 %collective-permute-done.11.refs_14_ = bf16[1,136,512]{2,1,0:T(8,128)(2,1)S(1)} collective-permute-done((bf16[1,136,512]{2,1,0:T(8,128)(2,1)S(1)}, bf16[1,136,512]{2,1,0:T(8,128)(2,1)S(1)}, u32[]{:S(2)}, u32[]{:S(2)}) %collective-permute-start.11) | collective-permute-done | bytes 139296 | tf_op jit(solution)/shard_map/ppermute | solution.py:62
  25.9 0.5 collective-permute-start.12
  26.4 0.8 collective-permute-done.8.refs_11_
  27.5 32.7 %shard_map.107 = (bf16[2,1,128,512]{3,2,1,0:T(8,128)(2,1)S(1)}, bf16[2,1,128,512]{3,2,1,0:T(8,128)(2,1)S(1)}, bf16[2,2,128,512]{3,2,1,0:T(8,128)(2,1)S(1)}, bf16...) custom-call(f32[1,2048]{1,0:T(1,128)} %bitcast.41, ...), custom_call_target="tpu_custom_call" | custom-call | flops 4831838208 | bytes 75497472 | tf_op jit(solution)/shard_map/pallas_call | solution.py:407
  60.1 0.4 collective-permute-start.19
  60.7 0.3 collective-permute-start.15
  61.0 0.7 collective-permute-done.19
  61.8 1.6 %collective-permute-start.20 = (bf16[1,128,512]{2,1,0:T(8,128)(2,1)S(1)}, bf16[1,128,512]{2,1,0:T(8,128)(2,1)S(1)}, u32[]{:S(2)}, u32[]{:S(2)}) collective-permute-start(bf16[1,128,512]{2,1,0:T(8,128)(2,1)S(1)} %slice_bitcast_fusion.3), channel_id=1, source_target_pairs={{0,2},{1,3},{2,0},{3,1},{4,6},{5,7},{6,4},{7,5},{8,10},{9,11},{10,... | collective-permute-start | bytes 393224 | tf_op jit(solution)/shard_map/ppermute | solution.py:62
  63.7 1.0 %collective-permute-start.17 = (bf16[2,128,512]{2,1,0:T(8,128)(2,1)S(1)}, bf16[2,128,512]{2,1,0:T(8,128)(2,1)S(1)}, u32[]{:S(2)}, u32[]{:S(2)}) collective-permute-start(bf16[2,128,512]{2,1,0:T(8,128)(2,1)S(1)} %slice_bitcast_fusion.1), channel_id=1, source_target_pairs={{0,2},{1,3},{2,0},{3,1},{4,6},{5,7},{6,4},{7,5},{8,10},{9,11},{10,... | collective-permute-start | bytes 786440 | tf_op jit(solution)/shard_map/ppermute | solution.py:62
  64.7 3.5 %collective-permute-done.20 = bf16[1,128,512]{2,1,0:T(8,128)(2,1)S(1)} collective-permute-done((bf16[1,128,512]{2,1,0:T(8,128)(2,1)S(1)}, bf16[1,128,512]{2,1,0:T(8,128)(2,1)S(1)}, u32[]{:S(2)}, u32[]{:S(2)}) %collective-permute-start.20) | collective-permute-done | bytes 131104 | tf_op jit(solution)/shard_map/ppermute | solution.py:62
  68.3 2.8 %collective-permute-start.21 = (bf16[152,512]{1,0:T(8,128)(2,1)S(1)}, bf16[152,512]{1,0:T(8,128)(2,1)S(1)}, u32[]{:S(2)}, u32[]{:S(2)}) collective-permute-start(bf16[152,512]{1,0:T(8,128)(2,1)S(1)} %pad_maximum_fusion.1), channel_id=1, source_target_pairs={{0,12},{4,0},{8,4},{12,8},{1,13},{5,1},{9,5},{13,9},{2,14},{6,2},{... | collective-permute-start | bytes 466952 | tf_op jit(solution)/shard_map/ppermute | solution.py:57
  71.1 2.7 %collective-permute-done.21 = bf16[152,512]{1,0:T(8,128)(2,1)S(1)} collective-permute-done((bf16[152,512]{1,0:T(8,128)(2,1)S(1)}, bf16[152,512]{1,0:T(8,128)(2,1)S(1)}, u32[]{:S(2)}, u32[]{:S(2)}) %collective-permute-start.21) | collective-permute-done | bytes 155680 | tf_op jit(solution)/shard_map/ppermute | solution.py:57
  73.9 0.6 collective-permute-start.23
  74.5 1.5 %collective-permute-start.18 = (bf16[1,128,512]{2,1,0:T(8,128)(2,1)S(1)}, bf16[1,128,512]{2,1,0:T(8,128)(2,1)S(1)}, u32[]{:S(2)}, u32[]{:S(2)}) collective-permute-start(bf16[1,128,512]{2,1,0:T(8,128)(2,1)S(1)} %slice_bitcast_fusion.6), channel_id=1, source_target_pairs={{0,2},{1,3},{2,0},{3,1},{4,6},{5,7},{6,4},{7,5},{8,10},{9,11},{10,... | collective-permute-start | bytes 393224 | tf_op jit(solution)/shard_map/ppermute | solution.py:62
  76.1 3.8 %collective-permute-start.22 = (bf16[176,512]{1,0:T(8,128)(2,1)S(1)}, bf16[176,512]{1,0:T(8,128)(2,1)S(1)}, u32[]{:S(2)}, u32[]{:S(2)}) collective-permute-start(bf16[176,512]{1,0:T(8,128)(2,1)S(1)} %pad_maximum_fusion), channel_id=1, source_target_pairs={{0,12},{4,0},{8,4},{12,8},{1,13},{5,1},{9,5},{13,9},{2,14},{6,2},{... | collective-permute-start | bytes 540680 | tf_op jit(solution)/shard_map/ppermute | solution.py:57
  80.0 3.1 %collective-permute-done.23.up_ref = bf16[152,512]{1,0:T(8,128)(2,1)S(1)} collective-permute-done((bf16[152,512]{1,0:T(8,128)(2,1)S(1)}, bf16[152,512]{1,0:T(8,128)(2,1)S(1)}, u32[]{:S(2)}, u32[]{:S(2)}) %collective-permute-start.23) | collective-permute-done | bytes 155680 | tf_op jit(solution)/shard_map/ppermute | solution.py:57
  83.1 1.4 %collective-permute-done.22.down_ref = bf16[176,512]{1,0:T(8,128)(2,1)S(1)} collective-permute-done((bf16[176,512]{1,0:T(8,128)(2,1)S(1)}, bf16[176,512]{1,0:T(8,128)(2,1)S(1)}, u32[]{:S(2)}, u32[]{:S(2)}) %collective-permute-start.22) | collective-permute-done | bytes 180256 | tf_op jit(solution)/shard_map/ppermute | solution.py:57
  84.5 0.8 shard_map.108
  (39 shorter events, 1.2 us)
Async XLA Ops:
  1.6 10.7 %collective-permute-start = (bf16[1,136,512]{2,1,0:T(8,128)(2,1)S(1)}, bf16[1,136,512]{2,1,0:T(8,128)(2,1)S(1)}, u32[]{:S(2)}, u32[]{:S(2)}) collective-permute-start(bf16[1,136,512]{2,1,0:T(8,128)(2,1)S(1)} %shard_map.104.after_ref.refs_4_), channel_id=1, source_target_pairs={{0,4},{4,8},{8,12},{12,0},{1,5},{5,9},{9,13},{13,1},{2,6},{6,10},{... | collective-permute-start | bytes 417800 | tf_op jit(solution)/shard_map/ppermute | solution.py:57
  4.7 8.1 %collective-permute-start.1 = (bf16[1,136,512]{2,1,0:T(8,128)(2,1)S(1)}, bf16[1,136,512]{2,1,0:T(8,128)(2,1)S(1)}, u32[]{:S(2)}, u32[]{:S(2)}) collective-permute-start(bf16[1,136,512]{2,1,0:T(8,128)(2,1)S(1)} %shard_map.104.after_ref.refs_4_), channel_id=1, source_target_pairs={{0,12},{4,0},{8,4},{12,8},{1,13},{5,1},{9,5},{13,9},{2,14},{6,2},{... | collective-permute-start | bytes 417800 | tf_op jit(solution)/shard_map/ppermute | solution.py:57
  6.8 6.0 %collective-permute-start.2 = (bf16[1,136,512]{2,1,0:T(8,128)(2,1)S(1)}, bf16[1,136,512]{2,1,0:T(8,128)(2,1)S(1)}, u32[]{:S(2)}, u32[]{:S(2)}) collective-permute-start(bf16[1,136,512]{2,1,0:T(8,128)(2,1)S(1)} %shard_map.104.after_ref.refs_4_), channel_id=1, source_target_pairs={{0,2},{1,3},{2,0},{3,1},{4,6},{5,7},{6,4},{7,5},{8,10},{9,11},{10,... | collective-permute-start | bytes 417800 | tf_op jit(solution)/shard_map/ppermute | solution.py:62
  8.4 4.4 %collective-permute-start.3 = (bf16[1,136,512]{2,1,0:T(8,128)(2,1)S(1)}, bf16[1,136,512]{2,1,0:T(8,128)(2,1)S(1)}, u32[]{:S(2)}, u32[]{:S(2)}) collective-permute-start(bf16[1,136,512]{2,1,0:T(8,128)(2,1)S(1)} %shard_map.104.after_ref.refs_4_), channel_id=1, source_target_pairs={{0,1},{1,0},{2,3},{3,2},{4,5},{5,4},{6,7},{7,6},{8,9},{9,8},{10,11... | collective-permute-start | bytes 417800 | tf_op jit(solution)/shard_map/ppermute | solution.py:67
  12.8 7.4 %collective-permute-start.9 = (bf16[1,136,512]{2,1,0:T(8,128)(2,1)S(1)}, bf16[1,136,512]{2,1,0:T(8,128)(2,1)S(1)}, u32[]{:S(2)}, u32[]{:S(2)}) collective-permute-start(bf16[1,136,512]{2,1,0:T(8,128)(2,1)S(1)} %collective-permute-done.refs_8_), channel_id=1, source_target_pairs={{0,4},{4,8},{8,12},{12,0},{1,5},{5,9},{9,13},{13,1},{2,6},{6,10},{... | collective-permute-start | bytes 417800 | tf_op jit(solution)/shard_map/ppermute | solution.py:57
  13.9 7.6 %collective-permute-start.4 = (bf16[1,136,512]{2,1,0:T(8,128)(2,1)S(1)}, bf16[1,136,512]{2,1,0:T(8,128)(2,1)S(1)}, u32[]{:S(2)}, u32[]{:S(2)}) collective-permute-start(bf16[1,136,512]{2,1,0:T(8,128)(2,1)S(1)} %collective-permute-done.refs_8_), channel_id=1, source_target_pairs={{0,2},{1,3},{2,0},{3,1},{4,6},{5,7},{6,4},{7,5},{8,10},{9,11},{10,... | collective-permute-start | bytes 417800 | tf_op jit(solution)/shard_map/ppermute | solution.py:62
  15.4 6.8 %collective-permute-start.5 = (bf16[1,136,512]{2,1,0:T(8,128)(2,1)S(1)}, bf16[1,136,512]{2,1,0:T(8,128)(2,1)S(1)}, u32[]{:S(2)}, u32[]{:S(2)}) collective-permute-start(bf16[1,136,512]{2,1,0:T(8,128)(2,1)S(1)} %collective-permute-done.1.after_ref.refs_16_), channel_id=1, source_target_pairs={{0,2},{1,3},{2,0},{3,1},{4,6},{5,7},{6,4},{7,5},{8,10},{9,11},{10,... | collective-permute-start | bytes 417800 | tf_op jit(solution)/shard_map/ppermute | solution.py:62
  19.7 3.0 %collective-permute-start.6 = (bf16[1,136,512]{2,1,0:T(8,128)(2,1)S(1)}, bf16[1,136,512]{2,1,0:T(8,128)(2,1)S(1)}, u32[]{:S(2)}, u32[]{:S(2)}) collective-permute-start(bf16[1,136,512]{2,1,0:T(8,128)(2,1)S(1)} %collective-permute-done.2.refs_6_), channel_id=1, source_target_pairs={{0,1},{1,0},{2,3},{3,2},{4,5},{5,4},{6,7},{7,6},{8,9},{9,8},{10,11... | collective-permute-start | bytes 417800 | tf_op jit(solution)/shard_map/ppermute | solution.py:67
  20.2 5.7 %collective-permute-start.11 = (bf16[1,136,512]{2,1,0:T(8,128)(2,1)S(1)}, bf16[1,136,512]{2,1,0:T(8,128)(2,1)S(1)}, u32[]{:S(2)}, u32[]{:S(2)}) collective-permute-start(bf16[1,136,512]{2,1,0:T(8,128)(2,1)S(1)} %collective-permute-done.9.refs_12_), channel_id=1, source_target_pairs={{0,2},{1,3},{2,0},{3,1},{4,6},{5,7},{6,4},{7,5},{8,10},{9,11},{10,... | collective-permute-start | bytes 417800 | tf_op jit(solution)/shard_map/ppermute | solution.py:62
  21.4 4.5 %collective-permute-start.10 = (bf16[1,136,512]{2,1,0:T(8,128)(2,1)S(1)}, bf16[1,136,512]{2,1,0:T(8,128)(2,1)S(1)}, u32[]{:S(2)}, u32[]{:S(2)}) collective-permute-start(bf16[1,136,512]{2,1,0:T(8,128)(2,1)S(1)} %collective-permute-done.9.refs_12_), channel_id=1, source_target_pairs={{0,1},{1,0},{2,3},{3,2},{4,5},{5,4},{6,7},{7,6},{8,9},{9,8},{10,11... | collective-permute-start | bytes 417800 | tf_op jit(solution)/shard_map/ppermute | solution.py:67
  22.2 4.2 %collective-permute-start.13 = (bf16[1,136,512]{2,1,0:T(8,128)(2,1)S(1)}, bf16[1,136,512]{2,1,0:T(8,128)(2,1)S(1)}, u32[]{:S(2)}, u32[]{:S(2)}) collective-permute-start(bf16[1,136,512]{2,1,0:T(8,128)(2,1)S(1)} %collective-permute-done.1.after_ref.refs_16_), channel_id=1, source_target_pairs={{0,1},{1,0},{2,3},{3,2},{4,5},{5,4},{6,7},{7,6},{8,9},{9,8},{10,11... | collective-permute-start | bytes 417800 | tf_op jit(solution)/shard_map/ppermute | solution.py:67
  22.2 4.2 %collective-permute-start.14 = (bf16[1,136,512]{2,1,0:T(8,128)(2,1)S(1)}, bf16[1,136,512]{2,1,0:T(8,128)(2,1)S(1)}, u32[]{:S(2)}, u32[]{:S(2)}) collective-permute-start(bf16[1,136,512]{2,1,0:T(8,128)(2,1)S(1)} %collective-permute-done.5.refs_18_), channel_id=1, source_target_pairs={{0,1},{1,0},{2,3},{3,2},{4,5},{5,4},{6,7},{7,6},{8,9},{9,8},{10,11... | collective-permute-start | bytes 417800 | tf_op jit(solution)/shard_map/ppermute | solution.py:67
  22.7 3.7 %collective-permute-start.7 = (bf16[1,136,512]{2,1,0:T(8,128)(2,1)S(1)}, bf16[1,136,512]{2,1,0:T(8,128)(2,1)S(1)}, u32[]{:S(2)}, u32[]{:S(2)}) collective-permute-start(bf16[1,136,512]{2,1,0:T(8,128)(2,1)S(1)} %collective-permute-done.refs_8_), channel_id=1, source_target_pairs={{0,1},{1,0},{2,3},{3,2},{4,5},{5,4},{6,7},{7,6},{8,9},{9,8},{10,11... | collective-permute-start | bytes 417800 | tf_op jit(solution)/shard_map/ppermute | solution.py:67
  25.9 1.4 %collective-permute-start.8 = (bf16[1,136,512]{2,1,0:T(8,128)(2,1)S(1)}, bf16[1,136,512]{2,1,0:T(8,128)(2,1)S(1)}, u32[]{:S(2)}, u32[]{:S(2)}) collective-permute-start(bf16[1,136,512]{2,1,0:T(8,128)(2,1)S(1)} %collective-permute-done.4.refs_10_), channel_id=1, source_target_pairs={{0,1},{1,0},{2,3},{3,2},{4,5},{5,4},{6,7},{7,6},{8,9},{9,8},{10,11... | collective-permute-start | bytes 417800 | tf_op jit(solution)/shard_map/ppermute | solution.py:67
  25.9 1.6 %collective-permute-start.12 = (bf16[1,136,512]{2,1,0:T(8,128)(2,1)S(1)}, bf16[1,136,512]{2,1,0:T(8,128)(2,1)S(1)}, u32[]{:S(2)}, u32[]{:S(2)}) collective-permute-start(bf16[1,136,512]{2,1,0:T(8,128)(2,1)S(1)} %collective-permute-done.11.refs_14_), channel_id=1, source_target_pairs={{0,1},{1,0},{2,3},{3,2},{4,5},{5,4},{6,7},{7,6},{8,9},{9,8},{10,11... | collective-permute-start | bytes 417800 | tf_op jit(solution)/shard_map/ppermute | solution.py:67
  60.1 24.4 %copy-start = (bf16[128,512]{1,0:T(8,128)(2,1)S(1)}, bf16[128,512]{1,0:T(8,128)(2,1)}, u32[]{:S(2)}) copy-start(bf16[128,512]{1,0:T(8,128)(2,1)} %hidden_ref.3) | copy-start | bytes 393220
  60.1 1.6 %collective-permute-start.19 = (bf16[2,1,128,512]{3,2,1,0:T(8,128)(2,1)S(1)}, bf16[2,1,128,512]{3,2,1,0:T(8,128)(2,1)S(1)}, u32[]{:S(2)}, u32[]{:S(2)}) collective-permute-start(bf16[2,1,128,512]{3,2,1,0:T(8,128)(2,1)S(1)} %get-tuple-element.51), channel_id=1, source_target_pairs={{0,1},{1,0},{2,3},{3,2},{4,5},{5,4},{6,7},{7,6},{8,9},{9,8},{10,11... | collective-permute-start | bytes 786440 | tf_op jit(solution)/shard_map/ppermute | solution.py:67
  60.5 3.0 %collective-permute-start.16 = (bf16[2,2,128,512]{3,2,1,0:T(8,128)(2,1)}, bf16[2,2,128,512]{3,2,1,0:T(8,128)(2,1)S(1)}, u32[]{:S(2)}, u32[]{:S(2)}) collective-permute-start(bf16[2,2,128,512]{3,2,1,0:T(8,128)(2,1)} %get-tuple-element.48), channel_id=1, source_target_pairs={{0,1},{1,0},{2,3},{3,2},{4,5},{5,4},{6,7},{7,6},{8,9},{9,8},{10,11... | collective-permute-start | bytes 1572872 | tf_op jit(solution)/shard_map/ppermute | solution.py:67
  60.7 2.7 %collective-permute-start.15 = (bf16[2,1,128,512]{3,2,1,0:T(8,128)(2,1)S(1)}, bf16[2,1,128,512]{3,2,1,0:T(8,128)(2,1)S(1)}, u32[]{:S(2)}, u32[]{:S(2)}) collective-permute-start(bf16[2,1,128,512]{3,2,1,0:T(8,128)(2,1)S(1)} %get-tuple-element.46), channel_id=1, source_target_pairs={{0,1},{1,0},{2,3},{3,2},{4,5},{5,4},{6,7},{7,6},{8,9},{9,8},{10,11... | collective-permute-start | bytes 786440 | tf_op jit(solution)/shard_map/ppermute | solution.py:67
  61.8 6.4 %collective-permute-start.20 = (bf16[1,128,512]{2,1,0:T(8,128)(2,1)S(1)}, bf16[1,128,512]{2,1,0:T(8,128)(2,1)S(1)}, u32[]{:S(2)}, u32[]{:S(2)}) collective-permute-start(bf16[1,128,512]{2,1,0:T(8,128)(2,1)S(1)} %slice_bitcast_fusion.3), channel_id=1, source_target_pairs={{0,2},{1,3},{2,0},{3,1},{4,6},{5,7},{6,4},{7,5},{8,10},{9,11},{10,... | collective-permute-start | bytes 393224 | tf_op jit(solution)/shard_map/ppermute | solution.py:62
  63.7 10.1 %collective-permute-start.17 = (bf16[2,128,512]{2,1,0:T(8,128)(2,1)S(1)}, bf16[2,128,512]{2,1,0:T(8,128)(2,1)S(1)}, u32[]{:S(2)}, u32[]{:S(2)}) collective-permute-start(bf16[2,128,512]{2,1,0:T(8,128)(2,1)S(1)} %slice_bitcast_fusion.1), channel_id=1, source_target_pairs={{0,2},{1,3},{2,0},{3,1},{4,6},{5,7},{6,4},{7,5},{8,10},{9,11},{10,... | collective-permute-start | bytes 786440 | tf_op jit(solution)/shard_map/ppermute | solution.py:62
  68.3 5.5 %collective-permute-start.21 = (bf16[152,512]{1,0:T(8,128)(2,1)S(1)}, bf16[152,512]{1,0:T(8,128)(2,1)S(1)}, u32[]{:S(2)}, u32[]{:S(2)}) collective-permute-start(bf16[152,512]{1,0:T(8,128)(2,1)S(1)} %pad_maximum_fusion.1), channel_id=1, source_target_pairs={{0,12},{4,0},{8,4},{12,8},{1,13},{5,1},{9,5},{13,9},{2,14},{6,2},{... | collective-permute-start | bytes 466952 | tf_op jit(solution)/shard_map/ppermute | solution.py:57
  73.9 9.2 %collective-permute-start.23 = (bf16[152,512]{1,0:T(8,128)(2,1)S(1)}, bf16[152,512]{1,0:T(8,128)(2,1)S(1)}, u32[]{:S(2)}, u32[]{:S(2)}) collective-permute-start(bf16[152,512]{1,0:T(8,128)(2,1)S(1)} %pad_maximum_fusion.2), channel_id=1, source_target_pairs={{0,4},{4,8},{8,12},{12,0},{1,5},{5,9},{9,13},{13,1},{2,6},{6,10},{... | collective-permute-start | bytes 466952 | tf_op jit(solution)/shard_map/ppermute | solution.py:57
  74.5 5.4 %collective-permute-start.18 = (bf16[1,128,512]{2,1,0:T(8,128)(2,1)S(1)}, bf16[1,128,512]{2,1,0:T(8,128)(2,1)S(1)}, u32[]{:S(2)}, u32[]{:S(2)}) collective-permute-start(bf16[1,128,512]{2,1,0:T(8,128)(2,1)S(1)} %slice_bitcast_fusion.6), channel_id=1, source_target_pairs={{0,2},{1,3},{2,0},{3,1},{4,6},{5,7},{6,4},{7,5},{8,10},{9,11},{10,... | collective-permute-start | bytes 393224 | tf_op jit(solution)/shard_map/ppermute | solution.py:62
  76.1 8.4 %collective-permute-start.22 = (bf16[176,512]{1,0:T(8,128)(2,1)S(1)}, bf16[176,512]{1,0:T(8,128)(2,1)S(1)}, u32[]{:S(2)}, u32[]{:S(2)}) collective-permute-start(bf16[176,512]{1,0:T(8,128)(2,1)S(1)} %pad_maximum_fusion), channel_id=1, source_target_pairs={{0,12},{4,0},{8,4},{12,8},{1,13},{5,1},{9,5},{13,9},{2,14},{6,2},{... | collective-permute-start | bytes 540680 | tf_op jit(solution)/shard_map/ppermute | solution.py:57

commit v12 on v10

--- a/solution.py
+++ b/solution.py
@@ -311,15 +311,13 @@
         picked = jnp.concatenate([picked_ref[at, :] for at in rows_of(h)], axis=0)
         along = (((1,), (1,)), ((), ()))
         gate_part = lax.dot_general(
-            gate_up[0], picked, along, preferred_element_type=jnp.float32
+            picked, gate_up[0], along, preferred_element_type=jnp.float32
         )
         up_part = lax.dot_general(
-            gate_up[1], picked, along, preferred_element_type=jnp.float32
+            picked, gate_up[1], along, preferred_element_type=jnp.float32
         )
         activated = (jax.nn.silu(gate_part) * up_part).astype(jnp.bfloat16)
-        served = lax.dot_general(
-            activated, down[...], (((0,), (0,)), ((), ())), preferred_element_type=jnp.float32
-        )
+        served = jnp.dot(activated, down[...], preferred_element_type=jnp.float32)
         for z, at in enumerate(rows_of(h)):
             served_ref[at, :] = (
                 served[z * CAP : (z + 1) * CAP, :] * slot_gate_ref[at, :]

time: 84 us -> 85.9 us (1.023)
  Pallas kernels: 35 us -> 36.9 us
    pallas_call x1, Pallas kernels: 32.2 us -> 34 us  [expert_sums(): pl.pallas_call(functools.partial(expert_kernel, held=held, parts=parts, c...]
where the time goes in v12:
time: 85.9 us; the launch traced here: 85.7 us
  Pallas kernels  36.9 us (43%)
  waiting for transfers between devices  23.8 us (28%)
  starting transfers between devices  23.6 us (27%)
    pallas_call x1, Pallas kernels, expert_sums(): pl.pallas_call(functools.partial(expert_kernel, held=held, parts=parts, c...  34 us
    ppermute x6, starting transfers between devices, shift_dp(): lax.ppermute(value, 'dp', [(i, (i + shift) % count) for i in range(count)])  12.3 us
    ppermute x6, waiting for transfers between devices, shift_dp(): lax.ppermute(value, 'dp', [(i, (i + shift) % count) for i in range(count)])  12.2 us
    ppermute x7, starting transfers between devices, shift_x(): lax.ppermute(value, 'mp', [(i, (i + CORES * shift) % count) for i in rang...  9.52 us
    ppermute x7, waiting for transfers between devices, shift_x(): lax.ppermute(value, 'mp', [(i, (i + CORES * shift) % count) for i in rang...  9.01 us
    ppermute x11, waiting for transfers between devices, other_core(): return lax.ppermute(value, 'mp', [(i, i ^ 1) for i in range(count)])  2.6 us
    ppermute x11, starting transfers between devices, other_core(): return lax.ppermute(value, 'mp', [(i, i ^ 1) for i in range(count)])  1.81 us
  transfers between devices with their start and end apart: 24, of which 11 were waited for; matrix products, arithmetic and copies ran while one was open for 1% of the time, Pallas kernels for 1%

profile of v12, /device:TPU:0, one launch (start us, length us, event | category | flops | bytes accessed | tf_op | source)
XLA Modules:
  0.0 85.7 jit_solution(2027652081421179089)
XLA Ops:
  0.6 1.0 %shard_map.104.after_ref.refs_0_ = bf16[1,136,512]{2,1,0:T(8,128)(2,1)S(1)} custom-call(bf16[128,512]{1,0:T(8,128)(2,1)} %hidden_ref.3, s32[8,128]{1,0:T(8,128)} %bitcast.42, f32[8,128]{1,0:T(8,128)} %bitcast.43), custom_call_target="tpu_custom_call" | custom-call | tf_op jit(solution)/shard_map/pallas_call | solution.py:98
  1.6 3.1 %collective-permute-start.3 = (bf16[1,136,512]{2,1,0:T(8,128)(2,1)S(1)}, bf16[1,136,512]{2,1,0:T(8,128)(2,1)S(1)}, u32[]{:S(2)}, u32[]{:S(2)}) collective-permute-start(bf16[1,136,512]{2,1,0:T(8,128)(2,1)S(1)} %shard_map.104.after_ref.refs_0_), channel_id=1, source_target_pairs={{0,4},{4,8},{8,12},{12,0},{1,5},{5,9},{9,13},{13,1},{2,6},{6,10},{... | collective-permute-start | bytes 417800 | tf_op jit(solution)/shard_map/ppermute | solution.py:57
  4.7 2.1 %collective-permute-start.11 = (bf16[1,136,512]{2,1,0:T(8,128)(2,1)S(1)}, bf16[1,136,512]{2,1,0:T(8,128)(2,1)S(1)}, u32[]{:S(2)}, u32[]{:S(2)}) collective-permute-start(bf16[1,136,512]{2,1,0:T(8,128)(2,1)S(1)} %shard_map.104.after_ref.refs_0_), channel_id=1, source_target_pairs={{0,12},{4,0},{8,4},{12,8},{1,13},{5,1},{9,5},{13,9},{2,14},{6,2},{... | collective-permute-start | bytes 417800 | tf_op jit(solution)/shard_map/ppermute | solution.py:57
  6.8 1.6 %collective-permute-start.1 = (bf16[1,136,512]{2,1,0:T(8,128)(2,1)S(1)}, bf16[1,136,512]{2,1,0:T(8,128)(2,1)S(1)}, u32[]{:S(2)}, u32[]{:S(2)}) collective-permute-start(bf16[1,136,512]{2,1,0:T(8,128)(2,1)S(1)} %shard_map.104.after_ref.refs_0_), channel_id=1, source_target_pairs={{0,2},{1,3},{2,0},{3,1},{4,6},{5,7},{6,4},{7,5},{8,10},{9,11},{10,... | collective-permute-start | bytes 417800 | tf_op jit(solution)/shard_map/ppermute | solution.py:62
  8.5 2.8 %collective-permute-done.3.refs_4_ = bf16[1,136,512]{2,1,0:T(8,128)(2,1)S(1)} collective-permute-done((bf16[1,136,512]{2,1,0:T(8,128)(2,1)S(1)}, bf16[1,136,512]{2,1,0:T(8,128)(2,1)S(1)}, u32[]{:S(2)}, u32[]{:S(2)}) %collective-permute-start.3) | collective-permute-done | bytes 139296 | tf_op jit(solution)/shard_map/ppermute | solution.py:57
  11.3 1.7 %collective-permute-start.4 = (bf16[1,136,512]{2,1,0:T(8,128)(2,1)S(1)}, bf16[1,136,512]{2,1,0:T(8,128)(2,1)S(1)}, u32[]{:S(2)}, u32[]{:S(2)}) collective-permute-start(bf16[1,136,512]{2,1,0:T(8,128)(2,1)S(1)} %collective-permute-done.3.refs_4_), channel_id=1, source_target_pairs={{0,2},{1,3},{2,0},{3,1},{4,6},{5,7},{6,4},{7,5},{8,10},{9,11},{10,... | collective-permute-start | bytes 417800 | tf_op jit(solution)/shard_map/ppermute | solution.py:62
  13.0 1.3 %collective-permute-start.13 = (bf16[1,136,512]{2,1,0:T(8,128)(2,1)S(1)}, bf16[1,136,512]{2,1,0:T(8,128)(2,1)S(1)}, u32[]{:S(2)}, u32[]{:S(2)}) collective-permute-start(bf16[1,136,512]{2,1,0:T(8,128)(2,1)S(1)} %collective-permute-done.11.refs_12_), channel_id=1, source_target_pairs={{0,2},{1,3},{2,0},{3,1},{4,6},{5,7},{6,4},{7,5},{8,10},{9,11},{10,... | collective-permute-start | bytes 417800 | tf_op jit(solution)/shard_map/ppermute | solution.py:62
  14.3 2.6 %collective-permute-done.4.refs_6_ = bf16[1,136,512]{2,1,0:T(8,128)(2,1)S(1)} collective-permute-done((bf16[1,136,512]{2,1,0:T(8,128)(2,1)S(1)}, bf16[1,136,512]{2,1,0:T(8,128)(2,1)S(1)}, u32[]{:S(2)}, u32[]{:S(2)}) %collective-permute-start.4) | collective-permute-done | bytes 139296 | tf_op jit(solution)/shard_map/ppermute | solution.py:62
  16.9 2.9 %collective-permute-done.7.refs_8_ = bf16[1,136,512]{2,1,0:T(8,128)(2,1)S(1)} collective-permute-done((bf16[1,136,512]{2,1,0:T(8,128)(2,1)S(1)}, bf16[1,136,512]{2,1,0:T(8,128)(2,1)S(1)}, u32[]{:S(2)}, u32[]{:S(2)}) %collective-permute-start.7) | collective-permute-done | bytes 139296 | tf_op jit(solution)/shard_map/ppermute | solution.py:57
  19.8 0.4 collective-permute-start.9
  20.3 1.1 %shard_map.105.pages_ref = bf16[4,24,512]{2,1,0:T(8,128)(2,1)S(1)} custom-call(bf16[128,256]{1,0:T(8,128)(2,1)} %kv_ref.1, s32[4,4]{1,0:T(4,128)} %lengths_ref.1, s32[4,4]{1,0:T(4,128)} %owners_ref.1, bf16[1,136,512]{2,1,0:T(8,128)(2,1)S(1)} %shard_map.104.after_ref.refs_0_), custom_call_target="tpu_custom_call" | custom-call | tf_op jit(solution)/shard_map/pallas_call | solution.py:162
  21.5 0.5 collective-permute-start.6
  22.0 0.4 collective-permute-start.14
  22.5 2.4 %collective-permute-done.9.refs_10_ = bf16[1,136,512]{2,1,0:T(8,128)(2,1)S(1)} collective-permute-done((bf16[1,136,512]{2,1,0:T(8,128)(2,1)S(1)}, bf16[1,136,512]{2,1,0:T(8,128)(2,1)S(1)}, u32[]{:S(2)}, u32[]{:S(2)}) %collective-permute-start.9) | collective-permute-done | bytes 139296 | tf_op jit(solution)/shard_map/ppermute | solution.py:62
  24.9 1.3 %collective-permute-done.10.refs_11_ = bf16[1,136,512]{2,1,0:T(8,128)(2,1)S(1)} collective-permute-done((bf16[1,136,512]{2,1,0:T(8,128)(2,1)S(1)}, bf16[1,136,512]{2,1,0:T(8,128)(2,1)S(1)}, u32[]{:S(2)}, u32[]{:S(2)}) %collective-permute-start.10) | collective-permute-done | bytes 139296 | tf_op jit(solution)/shard_map/ppermute | solution.py:67
  26.3 34.0 %shard_map.106 = (bf16[2,1,128,512]{3,2,1,0:T(8,128)(2,1)S(1)}, bf16[2,1,128,512]{3,2,1,0:T(8,128)(2,1)S(1)}, bf16[2,2,128,512]{3,2,1,0:T(8,128)(2,1)S(1)}, bf16...) custom-call(f32[1,2048]{1,0:T(1,128)} %bitcast.41, ...), custom_call_target="tpu_custom_call" | custom-call | flops 4831838208 | bytes 75497472 | tf_op jit(solution)/shard_map/pallas_call | solution.py:365
  60.3 0.2 collective-permute-start.19
  60.5 0.4 collective-permute-start.16
  60.9 0.1 collective-permute-start.15
  61.0 0.9 %collective-permute-done.19 = bf16[2,1,128,512]{3,2,1,0:T(8,128)(2,1)S(1)} collective-permute-done((bf16[2,1,128,512]{3,2,1,0:T(8,128)(2,1)S(1)}, bf16[2,1,128,512]{3,2,1,0:T(8,128)(2,1)S(1)}, u32[]{:S(2)}, u32[]{:S(2)}) %collective-permute-start.19) | collective-permute-done | bytes 262176 | tf_op jit(solution)/shard_map/ppermute | solution.py:67
  62.0 0.7 collective-permute-start.20
  62.6 0.4 collective-permute-done.15
  63.1 0.1 add_convert_fusion
  63.3 1.1 %collective-permute-start.17 = (bf16[2,128,512]{2,1,0:T(8,128)(2,1)S(1)}, bf16[2,128,512]{2,1,0:T(8,128)(2,1)S(1)}, u32[]{:S(2)}, u32[]{:S(2)}) collective-permute-start(bf16[2,128,512]{2,1,0:T(8,128)(2,1)S(1)} %slice_bitcast_fusion.1), channel_id=1, source_target_pairs={{0,2},{1,3},{2,0},{3,1},{4,6},{5,7},{6,4},{7,5},{8,10},{9,11},{10,... | collective-permute-start | bytes 786440 | tf_op jit(solution)/shard_map/ppermute | solution.py:62
  64.4 4.0 %collective-permute-done.20 = bf16[1,128,512]{2,1,0:T(8,128)(2,1)S(1)} collective-permute-done((bf16[1,128,512]{2,1,0:T(8,128)(2,1)S(1)}, bf16[1,128,512]{2,1,0:T(8,128)(2,1)S(1)}, u32[]{:S(2)}, u32[]{:S(2)}) %collective-permute-start.20) | collective-permute-done | bytes 131104 | tf_op jit(solution)/shard_map/ppermute | solution.py:62
  68.5 2.7 %collective-permute-start.21 = (bf16[152,512]{1,0:T(8,128)(2,1)S(1)}, bf16[152,512]{1,0:T(8,128)(2,1)S(1)}, u32[]{:S(2)}, u32[]{:S(2)}) collective-permute-start(bf16[152,512]{1,0:T(8,128)(2,1)S(1)} %pad_maximum_fusion.1), channel_id=1, source_target_pairs={{0,12},{4,0},{8,4},{12,8},{1,13},{5,1},{9,5},{13,9},{2,14},{6,2},{... | collective-permute-start | bytes 466952 | tf_op jit(solution)/shard_map/ppermute | solution.py:57
  71.1 3.5 %collective-permute-done.21 = bf16[152,512]{1,0:T(8,128)(2,1)S(1)} collective-permute-done((bf16[152,512]{1,0:T(8,128)(2,1)S(1)}, bf16[152,512]{1,0:T(8,128)(2,1)S(1)}, u32[]{:S(2)}, u32[]{:S(2)}) %collective-permute-start.21) | collective-permute-done | bytes 155680 | tf_op jit(solution)/shard_map/ppermute | solution.py:57
  74.8 2.6 %collective-permute-start.18 = (bf16[1,128,512]{2,1,0:T(8,128)(2,1)S(1)}, bf16[1,128,512]{2,1,0:T(8,128)(2,1)S(1)}, u32[]{:S(2)}, u32[]{:S(2)}) collective-permute-start(bf16[1,128,512]{2,1,0:T(8,128)(2,1)S(1)} %slice_bitcast_fusion.6), channel_id=1, source_target_pairs={{0,2},{1,3},{2,0},{3,1},{4,6},{5,7},{6,4},{7,5},{8,10},{9,11},{10,... | collective-permute-start | bytes 393224 | tf_op jit(solution)/shard_map/ppermute | solution.py:62
  77.5 4.4 %collective-permute-start.22 = (bf16[176,512]{1,0:T(8,128)(2,1)S(1)}, bf16[176,512]{1,0:T(8,128)(2,1)S(1)}, u32[]{:S(2)}, u32[]{:S(2)}) collective-permute-start(bf16[176,512]{1,0:T(8,128)(2,1)S(1)} %pad_maximum_fusion), channel_id=1, source_target_pairs={{0,12},{4,0},{8,4},{12,8},{1,13},{5,1},{9,5},{13,9},{2,14},{6,2},{... | collective-permute-start | bytes 540680 | tf_op jit(solution)/shard_map/ppermute | solution.py:57
  82.0 1.3 %collective-permute-done.23.up_ref = bf16[152,512]{1,0:T(8,128)(2,1)S(1)} collective-permute-done((bf16[152,512]{1,0:T(8,128)(2,1)S(1)}, bf16[152,512]{1,0:T(8,128)(2,1)S(1)}, u32[]{:S(2)}, u32[]{:S(2)}) %collective-permute-start.23) | collective-permute-done | bytes 155680 | tf_op jit(solution)/shard_map/ppermute | solution.py:57
  83.3 1.7 %collective-permute-done.22.down_ref = bf16[176,512]{1,0:T(8,128)(2,1)S(1)} collective-permute-done((bf16[176,512]{1,0:T(8,128)(2,1)S(1)}, bf16[176,512]{1,0:T(8,128)(2,1)S(1)}, u32[]{:S(2)}, u32[]{:S(2)}) %collective-permute-start.22) | collective-permute-done | bytes 180256 | tf_op jit(solution)/shard_map/ppermute | solution.py:57
  84.9 0.7 shard_map.107
  (38 shorter events, 0.7 us)
Async XLA Ops:
  0.6 84.3 %copy-start = (bf16[128,512]{1,0:T(8,128)(2,1)S(1)}, bf16[128,512]{1,0:T(8,128)(2,1)}, u32[]{:S(2)}) copy-start(bf16[128,512]{1,0:T(8,128)(2,1)} %hidden_ref.3) | copy-start | bytes 393220
  1.6 9.6 %collective-permute-start.3 = (bf16[1,136,512]{2,1,0:T(8,128)(2,1)S(1)}, bf16[1,136,512]{2,1,0:T(8,128)(2,1)S(1)}, u32[]{:S(2)}, u32[]{:S(2)}) collective-permute-start(bf16[1,136,512]{2,1,0:T(8,128)(2,1)S(1)} %shard_map.104.after_ref.refs_0_), channel_id=1, source_target_pairs={{0,4},{4,8},{8,12},{12,0},{1,5},{5,9},{9,13},{13,1},{2,6},{6,10},{... | collective-permute-start | bytes 417800 | tf_op jit(solution)/shard_map/ppermute | solution.py:57
  4.7 8.3 %collective-permute-start.11 = (bf16[1,136,512]{2,1,0:T(8,128)(2,1)S(1)}, bf16[1,136,512]{2,1,0:T(8,128)(2,1)S(1)}, u32[]{:S(2)}, u32[]{:S(2)}) collective-permute-start(bf16[1,136,512]{2,1,0:T(8,128)(2,1)S(1)} %shard_map.104.after_ref.refs_0_), channel_id=1, source_target_pairs={{0,12},{4,0},{8,4},{12,8},{1,13},{5,1},{9,5},{13,9},{2,14},{6,2},{... | collective-permute-start | bytes 417800 | tf_op jit(solution)/shard_map/ppermute | solution.py:57
  6.8 7.5 %collective-permute-start.1 = (bf16[1,136,512]{2,1,0:T(8,128)(2,1)S(1)}, bf16[1,136,512]{2,1,0:T(8,128)(2,1)S(1)}, u32[]{:S(2)}, u32[]{:S(2)}) collective-permute-start(bf16[1,136,512]{2,1,0:T(8,128)(2,1)S(1)} %shard_map.104.after_ref.refs_0_), channel_id=1, source_target_pairs={{0,2},{1,3},{2,0},{3,1},{4,6},{5,7},{6,4},{7,5},{8,10},{9,11},{10,... | collective-permute-start | bytes 417800 | tf_op jit(solution)/shard_map/ppermute | solution.py:62
  11.3 5.6 %collective-permute-start.4 = (bf16[1,136,512]{2,1,0:T(8,128)(2,1)S(1)}, bf16[1,136,512]{2,1,0:T(8,128)(2,1)S(1)}, u32[]{:S(2)}, u32[]{:S(2)}) collective-permute-start(bf16[1,136,512]{2,1,0:T(8,128)(2,1)S(1)} %collective-permute-done.3.refs_4_), channel_id=1, source_target_pairs={{0,2},{1,3},{2,0},{3,1},{4,6},{5,7},{6,4},{7,5},{8,10},{9,11},{10,... | collective-permute-start | bytes 417800 | tf_op jit(solution)/shard_map/ppermute | solution.py:62
  13.0 6.9 %collective-permute-start.7 = (bf16[1,136,512]{2,1,0:T(8,128)(2,1)S(1)}, bf16[1,136,512]{2,1,0:T(8,128)(2,1)S(1)}, u32[]{:S(2)}, u32[]{:S(2)}) collective-permute-start(bf16[1,136,512]{2,1,0:T(8,128)(2,1)S(1)} %collective-permute-done.3.refs_4_), channel_id=1, source_target_pairs={{0,4},{4,8},{8,12},{12,0},{1,5},{5,9},{9,13},{13,1},{2,6},{6,10},{... | collective-permute-start | bytes 417800 | tf_op jit(solution)/shard_map/ppermute | solution.py:57
  13.0 8.4 %collective-permute-start = (bf16[1,136,512]{2,1,0:T(8,128)(2,1)S(1)}, bf16[1,136,512]{2,1,0:T(8,128)(2,1)S(1)}, u32[]{:S(2)}, u32[]{:S(2)}) collective-permute-start(bf16[1,136,512]{2,1,0:T(8,128)(2,1)S(1)} %shard_map.104.after_ref.refs_0_), channel_id=1, source_target_pairs={{0,1},{1,0},{2,3},{3,2},{4,5},{5,4},{6,7},{7,6},{8,9},{9,8},{10,11... | collective-permute-start | bytes 417800 | tf_op jit(solution)/shard_map/ppermute | solution.py:67
  13.0 8.5 %collective-permute-start.13 = (bf16[1,136,512]{2,1,0:T(8,128)(2,1)S(1)}, bf16[1,136,512]{2,1,0:T(8,128)(2,1)S(1)}, u32[]{:S(2)}, u32[]{:S(2)}) collective-permute-start(bf16[1,136,512]{2,1,0:T(8,128)(2,1)S(1)} %collective-permute-done.11.refs_12_), channel_id=1, source_target_pairs={{0,2},{1,3},{2,0},{3,1},{4,6},{5,7},{6,4},{7,5},{8,10},{9,11},{10,... | collective-permute-start | bytes 417800 | tf_op jit(solution)/shard_map/ppermute | solution.py:62
  14.3 7.6 %collective-permute-start.12 = (bf16[1,136,512]{2,1,0:T(8,128)(2,1)S(1)}, bf16[1,136,512]{2,1,0:T(8,128)(2,1)S(1)}, u32[]{:S(2)}, u32[]{:S(2)}) collective-permute-start(bf16[1,136,512]{2,1,0:T(8,128)(2,1)S(1)} %collective-permute-done.11.refs_12_), channel_id=1, source_target_pairs={{0,1},{1,0},{2,3},{3,2},{4,5},{5,4},{6,7},{7,6},{8,9},{9,8},{10,11... | collective-permute-start | bytes 417800 | tf_op jit(solution)/shard_map/ppermute | solution.py:67
  16.9 5.1 %collective-permute-start.2 = (bf16[1,136,512]{2,1,0:T(8,128)(2,1)S(1)}, bf16[1,136,512]{2,1,0:T(8,128)(2,1)S(1)}, u32[]{:S(2)}, u32[]{:S(2)}) collective-permute-start(bf16[1,136,512]{2,1,0:T(8,128)(2,1)S(1)} %collective-permute-done.1.refs_2_), channel_id=1, source_target_pairs={{0,1},{1,0},{2,3},{3,2},{4,5},{5,4},{6,7},{7,6},{8,9},{9,8},{10,11... | collective-permute-start | bytes 417800 | tf_op jit(solution)/shard_map/ppermute | solution.py:67
  19.8 5.1 %collective-permute-start.9 = (bf16[1,136,512]{2,1,0:T(8,128)(2,1)S(1)}, bf16[1,136,512]{2,1,0:T(8,128)(2,1)S(1)}, u32[]{:S(2)}, u32[]{:S(2)}) collective-permute-start(bf16[1,136,512]{2,1,0:T(8,128)(2,1)S(1)} %collective-permute-done.7.refs_8_), channel_id=1, source_target_pairs={{0,2},{1,3},{2,0},{3,1},{4,6},{5,7},{6,4},{7,5},{8,10},{9,11},{10,... | collective-permute-start | bytes 417800 | tf_op jit(solution)/shard_map/ppermute | solution.py:62
  21.4 3.5 %collective-permute-start.5 = (bf16[1,136,512]{2,1,0:T(8,128)(2,1)S(1)}, bf16[1,136,512]{2,1,0:T(8,128)(2,1)S(1)}, u32[]{:S(2)}, u32[]{:S(2)}) collective-permute-start(bf16[1,136,512]{2,1,0:T(8,128)(2,1)S(1)} %collective-permute-done.3.refs_4_), channel_id=1, source_target_pairs={{0,1},{1,0},{2,3},{3,2},{4,5},{5,4},{6,7},{7,6},{8,9},{9,8},{10,11... | collective-permute-start | bytes 417800 | tf_op jit(solution)/shard_map/ppermute | solution.py:67
  21.5 3.4 %collective-permute-start.6 = (bf16[1,136,512]{2,1,0:T(8,128)(2,1)S(1)}, bf16[1,136,512]{2,1,0:T(8,128)(2,1)S(1)}, u32[]{:S(2)}, u32[]{:S(2)}) collective-permute-start(bf16[1,136,512]{2,1,0:T(8,128)(2,1)S(1)} %collective-permute-done.4.refs_6_), channel_id=1, source_target_pairs={{0,1},{1,0},{2,3},{3,2},{4,5},{5,4},{6,7},{7,6},{8,9},{9,8},{10,11... | collective-permute-start | bytes 417800 | tf_op jit(solution)/shard_map/ppermute | solution.py:67
  22.0 3.0 %collective-permute-start.8 = (bf16[1,136,512]{2,1,0:T(8,128)(2,1)S(1)}, bf16[1,136,512]{2,1,0:T(8,128)(2,1)S(1)}, u32[]{:S(2)}, u32[]{:S(2)}) collective-permute-start(bf16[1,136,512]{2,1,0:T(8,128)(2,1)S(1)} %collective-permute-done.7.refs_8_), channel_id=1, source_target_pairs={{0,1},{1,0},{2,3},{3,2},{4,5},{5,4},{6,7},{7,6},{8,9},{9,8},{10,11... | collective-permute-start | bytes 417800 | tf_op jit(solution)/shard_map/ppermute | solution.py:67
  22.0 2.9 %collective-permute-start.14 = (bf16[1,136,512]{2,1,0:T(8,128)(2,1)S(1)}, bf16[1,136,512]{2,1,0:T(8,128)(2,1)S(1)}, u32[]{:S(2)}, u32[]{:S(2)}) collective-permute-start(bf16[1,136,512]{2,1,0:T(8,128)(2,1)S(1)} %collective-permute-done.13.refs_14_), channel_id=1, source_target_pairs={{0,1},{1,0},{2,3},{3,2},{4,5},{5,4},{6,7},{7,6},{8,9},{9,8},{10,11... | collective-permute-start | bytes 417800 | tf_op jit(solution)/shard_map/ppermute | solution.py:67
  24.9 1.4 %collective-permute-start.10 = (bf16[1,136,512]{2,1,0:T(8,128)(2,1)S(1)}, bf16[1,136,512]{2,1,0:T(8,128)(2,1)S(1)}, u32[]{:S(2)}, u32[]{:S(2)}) collective-permute-start(bf16[1,136,512]{2,1,0:T(8,128)(2,1)S(1)} %collective-permute-done.9.refs_10_), channel_id=1, source_target_pairs={{0,1},{1,0},{2,3},{3,2},{4,5},{5,4},{6,7},{7,6},{8,9},{9,8},{10,11... | collective-permute-start | bytes 417800 | tf_op jit(solution)/shard_map/ppermute | solution.py:67
  60.3 1.6 %collective-permute-start.19 = (bf16[2,1,128,512]{3,2,1,0:T(8,128)(2,1)S(1)}, bf16[2,1,128,512]{3,2,1,0:T(8,128)(2,1)S(1)}, u32[]{:S(2)}, u32[]{:S(2)}) collective-permute-start(bf16[2,1,128,512]{3,2,1,0:T(8,128)(2,1)S(1)} %get-tuple-element.21), channel_id=1, source_target_pairs={{0,1},{1,0},{2,3},{3,2},{4,5},{5,4},{6,7},{7,6},{8,9},{9,8},{10,11... | collective-permute-start | bytes 786440 | tf_op jit(solution)/shard_map/ppermute | solution.py:67
  60.5 2.6 %collective-permute-start.16 = (bf16[2,2,128,512]{3,2,1,0:T(8,128)(2,1)S(1)}, bf16[2,2,128,512]{3,2,1,0:T(8,128)(2,1)S(1)}, u32[]{:S(2)}, u32[]{:S(2)}) collective-permute-start(bf16[2,2,128,512]{3,2,1,0:T(8,128)(2,1)S(1)} %get-tuple-element.18), channel_id=1, source_target_pairs={{0,1},{1,0},{2,3},{3,2},{4,5},{5,4},{6,7},{7,6},{8,9},{9,8},{10,11... | collective-permute-start | bytes 1572872 | tf_op jit(solution)/shard_map/ppermute | solution.py:67
  60.9 2.1 %collective-permute-start.15 = (bf16[2,1,128,512]{3,2,1,0:T(8,128)(2,1)S(1)}, bf16[2,1,128,512]{3,2,1,0:T(8,128)(2,1)S(1)}, u32[]{:S(2)}, u32[]{:S(2)}) collective-permute-start(bf16[2,1,128,512]{3,2,1,0:T(8,128)(2,1)S(1)} %get-tuple-element.16), channel_id=1, source_target_pairs={{0,1},{1,0},{2,3},{3,2},{4,5},{5,4},{6,7},{7,6},{8,9},{9,8},{10,11... | collective-permute-start | bytes 786440 | tf_op jit(solution)/shard_map/ppermute | solution.py:67
  62.0 6.4 %collective-permute-start.20 = (bf16[1,128,512]{2,1,0:T(8,128)(2,1)S(1)}, bf16[1,128,512]{2,1,0:T(8,128)(2,1)S(1)}, u32[]{:S(2)}, u32[]{:S(2)}) collective-permute-start(bf16[1,128,512]{2,1,0:T(8,128)(2,1)S(1)} %slice_bitcast_fusion.3), channel_id=1, source_target_pairs={{0,2},{1,3},{2,0},{3,1},{4,6},{5,7},{6,4},{7,5},{8,10},{9,11},{10,... | collective-permute-start | bytes 393224 | tf_op jit(solution)/shard_map/ppermute | solution.py:62
  63.3 11.4 %collective-permute-start.17 = (bf16[2,128,512]{2,1,0:T(8,128)(2,1)S(1)}, bf16[2,128,512]{2,1,0:T(8,128)(2,1)S(1)}, u32[]{:S(2)}, u32[]{:S(2)}) collective-permute-start(bf16[2,128,512]{2,1,0:T(8,128)(2,1)S(1)} %slice_bitcast_fusion.1), channel_id=1, source_target_pairs={{0,2},{1,3},{2,0},{3,1},{4,6},{5,7},{6,4},{7,5},{8,10},{9,11},{10,... | collective-permute-start | bytes 786440 | tf_op jit(solution)/shard_map/ppermute | solution.py:62
  68.5 6.2 %collective-permute-start.21 = (bf16[152,512]{1,0:T(8,128)(2,1)S(1)}, bf16[152,512]{1,0:T(8,128)(2,1)S(1)}, u32[]{:S(2)}, u32[]{:S(2)}) collective-permute-start(bf16[152,512]{1,0:T(8,128)(2,1)S(1)} %pad_maximum_fusion.1), channel_id=1, source_target_pairs={{0,12},{4,0},{8,4},{12,8},{1,13},{5,1},{9,5},{13,9},{2,14},{6,2},{... | collective-permute-start | bytes 466952 | tf_op jit(solution)/shard_map/ppermute | solution.py:57
  74.7 8.5 %collective-permute-start.23 = (bf16[152,512]{1,0:T(8,128)(2,1)S(1)}, bf16[152,512]{1,0:T(8,128)(2,1)S(1)}, u32[]{:S(2)}, u32[]{:S(2)}) collective-permute-start(bf16[152,512]{1,0:T(8,128)(2,1)S(1)} %pad_maximum_fusion.2), channel_id=1, source_target_pairs={{0,4},{4,8},{8,12},{12,0},{1,5},{5,9},{9,13},{13,1},{2,6},{6,10},{... | collective-permute-start | bytes 466952 | tf_op jit(solution)/shard_map/ppermute | solution.py:57
  74.8 7.1 %collective-permute-start.18 = (bf16[1,128,512]{2,1,0:T(8,128)(2,1)S(1)}, bf16[1,128,512]{2,1,0:T(8,128)(2,1)S(1)}, u32[]{:S(2)}, u32[]{:S(2)}) collective-permute-start(bf16[1,128,512]{2,1,0:T(8,128)(2,1)S(1)} %slice_bitcast_fusion.6), channel_id=1, source_target_pairs={{0,2},{1,3},{2,0},{3,1},{4,6},{5,7},{6,4},{7,5},{8,10},{9,11},{10,... | collective-permute-start | bytes 393224 | tf_op jit(solution)/shard_map/ppermute | solution.py:62
  77.5 7.4 %collective-permute-start.22 = (bf16[176,512]{1,0:T(8,128)(2,1)S(1)}, bf16[176,512]{1,0:T(8,128)(2,1)S(1)}, u32[]{:S(2)}, u32[]{:S(2)}) collective-permute-start(bf16[176,512]{1,0:T(8,128)(2,1)S(1)} %pad_maximum_fusion), channel_id=1, source_target_pairs={{0,12},{4,0},{8,4},{12,8},{1,13},{5,1},{9,5},{13,9},{2,14},{6,2},{... | collective-permute-start | bytes 540680 | tf_op jit(solution)/shard_map/ppermute | solution.py:57

commit v13 on v7

--- a/solution.py
+++ b/solution.py
@@ -18,8 +18,9 @@
 HOP_CHIPS = 2
 PAGE_FOLD = 24
 SMALL_VMEM = 4 * 1024 * 1024
-WEIGHT_SLOTS = 2
-EXPERT_VMEM = 32 * 1024 * 1024
+GATE_UP_SLOTS = 3
+DOWN_SLOTS = 2
+EXPERT_VMEM = 33 * 1024 * 1024
 
 epsilon = 1e-06
 
@@ -136,14 +137,16 @@
     ff_part = down_into.shape[0]
     at = pl.ds(pl.multiple_of(h * ff_part, ff_part), ff_part)
     return (
-        pltpu.make_async_copy(gate_up_ref.at[0, at, :], gate_up_into.at[0], sems.at[0]),
-        pltpu.make_async_copy(gate_up_ref.at[1, at, :], gate_up_into.at[1], sems.at[1]),
-        pltpu.make_async_copy(down_ref.at[at, :], down_into, sems.at[2]),
+        pltpu.make_async_copy(gate_up_ref.at[0, at, :], gate_up_into.at[0], sems[0]),
+        pltpu.make_async_copy(gate_up_ref.at[1, at, :], gate_up_into.at[1], sems[1]),
+        pltpu.make_async_copy(down_ref.at[at, :], down_into, sems[2]),
     )
 
 
 def fill_kernel(gate_up_ref, down_ref, after_ref, gate_up_out, down_out, sems, *, expert):
-    copies = expert_copies(gate_up_ref, down_ref, expert, gate_up_out, down_out, sems)
+    copies = expert_copies(
+        gate_up_ref, down_ref, expert, gate_up_out, down_out, [sems.at[i] for i in range(3)]
+    )
     for copy in copies:
         copy.start()
     for copy in copies:
@@ -160,7 +163,9 @@
         pltpu.make_async_copy(lengths_ref, lengths_buf, page_sems.at[1]),
         pltpu.make_async_copy(owners_ref, owners_buf, page_sems.at[2]),
     )
-    copies = expert_copies(gate_up_ref, down_ref, expert, gate_up_out, down_out, sems)
+    copies = expert_copies(
+        gate_up_ref, down_ref, expert, gate_up_out, down_out, [sems.at[i] for i in range(3)]
+    )
     for copy in small + copies:
         copy.start()
     for copy in small:
@@ -254,23 +259,29 @@
     block_refs, out_refs = refs[: parts * chips * CORES], refs[parts * chips * CORES :]
     out_refs, scratch = out_refs[: len(RETURNS) * CORES], out_refs[len(RETURNS) * CORES :]
     (
-        normed_ref, pick_ref, picked_ref, slot_gate_ref, served_ref, gain_buf, gu_buf, down_buf,
-        sems, gain_sem,
+        normed_ref, pick_ref, picked_ref, slot_gate_ref, gain_buf, gu_buf, down_buf,
+        gu_sems, down_sems, gain_sem,
     ) = scratch
     _, block_rows, width = block_refs[0].shape
     tok_node = block_rows - TOPK
     tokens, model_width = normed_ref.shape
-    slots = down_buf.shape[0]
-
-    def fetch(h, slot):
+    served_ref = picked_ref
+    gu_slots, down_slots = gu_buf.shape[0], down_buf.shape[0]
+
+    def slots_of(h):
+        return lax.rem(h - fills, gu_buf.shape[0]), lax.rem(h - fills, down_buf.shape[0])
+
+    def fetch(h):
+        gu_slot, down_slot = slots_of(h)
         return expert_copies(
-            gate_up_ref, down_ref, h, gu_buf.at[slot], down_buf.at[slot], sems.at[slot]
+            gate_up_ref, down_ref, h, gu_buf.at[gu_slot], down_buf.at[down_slot],
+            (gu_sems.at[gu_slot, 0], gu_sems.at[gu_slot, 1], down_sems.at[down_slot]),
         )
 
     gain_copy = pltpu.make_async_copy(gain_ref, gain_buf, gain_sem)
     gain_copy.start()
-    for slot in range(min(slots, held - fills)):
-        for copy in fetch(fills + slot, slot):
+    for i in range(gu_slots):
+        for copy in fetch(fills + i)[: 3 if i < down_slots else 2]:
             copy.start()
 
     column = lax.axis_index("mp")
@@ -372,15 +383,19 @@
         one_expert(pl.ds(h * capacity, capacity), held_refs[2 * h], held_refs[2 * h + 1])
 
     def streamed(h, carry):
-        slot = lax.rem(h - fills, slots)
-        for copy in fetch(h, slot):
+        gu_slot, down_slot = slots_of(h)
+        for copy in fetch(h):
             copy.wait()
         at = pl.ds(pl.multiple_of(h * capacity, capacity), capacity)
-        one_expert(at, gu_buf.at[slot], down_buf.at[slot])
-
-        @pl.when(h + slots < held)
+        one_expert(at, gu_buf.at[gu_slot], down_buf.at[down_slot])
+
+        @pl.when(h + down_slots < held)
         def _():
-            for copy in fetch(h + slots, slot):
+            fetch(h + down_slots)[2].start()
+
+        @pl.when(h + gu_slots < held)
+        def _():
+            for copy in fetch(h + gu_slots)[:2]:
                 copy.start()
 
         return carry
@@ -432,11 +447,11 @@
             pltpu.VMEM((all_slots, tokens), jnp.bfloat16),
             pltpu.VMEM((all_slots, model_width), jnp.bfloat16),
             pltpu.VMEM((all_slots, 1), jnp.float32),
-            pltpu.VMEM((all_slots, model_width), jnp.bfloat16),
             pltpu.VMEM((1, model_width), jnp.float32),
-            pltpu.VMEM((WEIGHT_SLOTS, 2, ff_part, model_width), jnp.bfloat16),
-            pltpu.VMEM((WEIGHT_SLOTS, ff_part, model_width), jnp.bfloat16),
-            pltpu.SemaphoreType.DMA((WEIGHT_SLOTS, 3)),
+            pltpu.VMEM((GATE_UP_SLOTS, 2, ff_part, model_width), jnp.bfloat16),
+            pltpu.VMEM((DOWN_SLOTS, ff_part, model_width), jnp.bfloat16),
+            pltpu.SemaphoreType.DMA((GATE_UP_SLOTS, 2)),
+            pltpu.SemaphoreType.DMA((DOWN_SLOTS,)),
             pltpu.SemaphoreType.DMA(()),
         ],
         compiler_params=pltpu.CompilerParams(vmem_limit_bytes=EXPERT_VMEM),
@@ -541,7 +556,8 @@
     by_z[2] = shift_dp(by_z[1], 1)
     chip_rows = {z: [by_z[z]] + [shift_x(by_z[z], s) for s in range(1, chips)] for z in (1, 3)}
     held_b = filled(gate_up_weight, down_weight, 1, by_z[3])
-    by_z[2], chip_rows, held_b = lax.optimization_barrier((by_z[2], chip_rows, held_b))
+    by_z[2], *_ = lax.optimization_barrier((by_z[2], *held_b))
+    chip_rows, held_b = lax.optimization_barrier((chip_rows, held_b))
     chip_rows[0] = [block] + own_x
     chip_rows[2] = [by_z[2]] + [shift_x(by_z[2], s) for s in range(1, chips)]
     own_core += [other_core(value) for value in own_x]

time: 85.4 us -> 83.6 us (0.979)
  waiting for transfers between devices: 18.7 us -> 16 us
  other arithmetic: 0.5 us -> 1.53 us
    ppermute x7, waiting for transfers between devices: 8.22 us -> 5.68 us  [shift_x(): lax.ppermute(value, 'mp', [(i, (i + CORES * shift) % count) for i in rang...]
    convert_element_type x5, other arithmetic: 0.39 us -> 1.42 us  [added(): sum((value.astype(jnp.float32) for value in values)).astype(jnp.bfloat16)]
  transfers between devices with their start and end apart: 24 -> 24, of which waited for: 13 -> 11; matrix products, arithmetic and copies ran while one was open for 1% -> 2% of each run, Pallas kernels for 9% -> 9%
where the time goes in v13:
time: 83.6 us; the launch traced here: 83.5 us
  Pallas kernels  40.3 us (48%)
  starting transfers between devices  24.8 us (30%)
  waiting for transfers between devices  16 us (19%)
  other arithmetic  1.53 us (2%)
    pallas_call x1, Pallas kernels, expert_sums(): pl.pallas_call(functools.partial(expert_kernel, held=held, capacity=capac...  31 us
    ppermute x6, starting transfers between devices, shift_dp(): lax.ppermute(value, 'dp', [(i, (i + shift) % count) for i in range(count)])  13.5 us
    ppermute x7, starting transfers between devices, shift_x(): lax.ppermute(value, 'mp', [(i, (i + CORES * shift) % count) for i in rang...  9.13 us
    ppermute x6, waiting for transfers between devices, shift_dp(): lax.ppermute(value, 'dp', [(i, (i + shift) % count) for i in range(count)])  8.53 us
    pallas_call x2, Pallas kernels, filled(): pl.pallas_call(functools.partial(kernel, expert=expert), out_shape=out_sh...  7.62 us
    ppermute x7, waiting for transfers between devices, shift_x(): lax.ppermute(value, 'mp', [(i, (i + CORES * shift) % count) for i in rang...  5.68 us
    ppermute x11, starting transfers between devices, other_core(): return lax.ppermute(value, 'mp', [(i, i ^ 1) for i in range(count)])  2.15 us
    ppermute x11, waiting for transfers between devices, other_core(): return lax.ppermute(value, 'mp', [(i, i ^ 1) for i in range(count)])  1.75 us
  transfers between devices with their start and end apart: 24, of which 11 were waited for; matrix products, arithmetic and copies ran while one was open for 2% of the time, Pallas kernels for 9%

profile of v13, /device:TPU:0, one launch (start us, length us, event | category | flops | bytes accessed | tf_op | source)
XLA Modules:
  0.0 83.5 jit_solution(8249849806501653167)
XLA Ops:
  0.6 1.0 %shard_map.104.after_ref.refs_4_ = bf16[1,136,512]{2,1,0:T(8,128)(2,1)S(1)} custom-call(bf16[128,512]{1,0:T(8,128)(2,1)} %hidden_ref.3, s32[8,128]{1,0:T(8,128)} %bitcast.42, f32[8,128]{1,0:T(8,128)} %bitcast.43), custom_call_target="tpu_custom_call" | custom-call | tf_op jit(solution)/shard_map/pallas_call | solution.py:99
  1.6 3.1 %collective-permute-start = (bf16[1,136,512]{2,1,0:T(8,128)(2,1)S(1)}, bf16[1,136,512]{2,1,0:T(8,128)(2,1)S(1)}, u32[]{:S(2)}, u32[]{:S(2)}) collective-permute-start(bf16[1,136,512]{2,1,0:T(8,128)(2,1)S(1)} %shard_map.104.after_ref.refs_4_), channel_id=1, source_target_pairs={{0,4},{4,8},{8,12},{12,0},{1,5},{5,9},{9,13},{13,1},{2,6},{6,10},{... | collective-permute-start | bytes 417800 | tf_op jit(solution)/shard_map/ppermute | solution.py:58
  4.7 2.1 %collective-permute-start.1 = (bf16[1,136,512]{2,1,0:T(8,128)(2,1)S(1)}, bf16[1,136,512]{2,1,0:T(8,128)(2,1)S(1)}, u32[]{:S(2)}, u32[]{:S(2)}) collective-permute-start(bf16[1,136,512]{2,1,0:T(8,128)(2,1)S(1)} %shard_map.104.after_ref.refs_4_), channel_id=1, source_target_pairs={{0,12},{4,0},{8,4},{12,8},{1,13},{5,1},{9,5},{13,9},{2,14},{6,2},{... | collective-permute-start | bytes 417800 | tf_op jit(solution)/shard_map/ppermute | solution.py:58
  6.8 1.6 %collective-permute-start.2 = (bf16[1,136,512]{2,1,0:T(8,128)(2,1)S(1)}, bf16[1,136,512]{2,1,0:T(8,128)(2,1)S(1)}, u32[]{:S(2)}, u32[]{:S(2)}) collective-permute-start(bf16[1,136,512]{2,1,0:T(8,128)(2,1)S(1)} %shard_map.104.after_ref.refs_4_), channel_id=1, source_target_pairs={{0,2},{1,3},{2,0},{3,1},{4,6},{5,7},{6,4},{7,5},{8,10},{9,11},{10,... | collective-permute-start | bytes 417800 | tf_op jit(solution)/shard_map/ppermute | solution.py:63
  8.4 3.8 %shard_map.105 = (bf16[2,768,2048]{2,1,0:T(8,128)(2,1)S(1)}, bf16[768,2048]{1,0:T(8,128)(2,1)S(1)}, bf16[4,24,512]{2,1,0:T(8,128)(2,1)S(1)}) custom-call(bf16[2,6144,2048]{2,1,0:T(8,128)(2,1)} %gate_up_ref.5, bf16[6144,2048]{1,0:T(8,128)(2,1)} %down_ref.5, bf16[1,136,512]{2,1,0:T(8,128)(2,1)S(1)} %shard_map.104.after_ref.refs_4_, bf16[128,256]{1,0:T(8,128)(2,1)} %kv_ref.1, ...), custom_call_target="tpu_custom_call" | custom-call | bytes 9437184 | tf_op jit(solution)/shard_map/pallas_call | solution.py:205
  12.3 0.5 collective-permute-done.1.after_ref.refs_16_
  12.8 1.1 %collective-permute-start.9 = (bf16[1,136,512]{2,1,0:T(8,128)(2,1)S(1)}, bf16[1,136,512]{2,1,0:T(8,128)(2,1)S(1)}, u32[]{:S(2)}, u32[]{:S(2)}) collective-permute-start(bf16[1,136,512]{2,1,0:T(8,128)(2,1)S(1)} %collective-permute-done.refs_8_), channel_id=1, source_target_pairs={{0,4},{4,8},{8,12},{12,0},{1,5},{5,9},{9,13},{13,1},{2,6},{6,10},{... | collective-permute-start | bytes 417800 | tf_op jit(solution)/shard_map/ppermute | solution.py:58
  13.9 1.5 %collective-permute-start.4 = (bf16[1,136,512]{2,1,0:T(8,128)(2,1)S(1)}, bf16[1,136,512]{2,1,0:T(8,128)(2,1)S(1)}, u32[]{:S(2)}, u32[]{:S(2)}) collective-permute-start(bf16[1,136,512]{2,1,0:T(8,128)(2,1)S(1)} %collective-permute-done.refs_8_), channel_id=1, source_target_pairs={{0,2},{1,3},{2,0},{3,1},{4,6},{5,7},{6,4},{7,5},{8,10},{9,11},{10,... | collective-permute-start | bytes 417800 | tf_op jit(solution)/shard_map/ppermute | solution.py:63
  15.4 0.5 collective-permute-start.5
  16.0 3.8 %shard_map.106 = (bf16[2,768,2048]{2,1,0:T(8,128)(2,1)S(1)}, bf16[768,2048]{1,0:T(8,128)(2,1)S(1)}) custom-call(bf16[2,6144,2048]{2,1,0:T(8,128)(2,1)} %gate_up_ref.5, bf16[6144,2048]{1,0:T(8,128)(2,1)} %down_ref.5, bf16[1,136,512]{2,1,0:T(8,128)(2,1)S(1)} %collective-permute-done.1.after_ref.refs_16_), custom_call_target="tpu_custom_call" | custom-call | bytes 9437184 | tf_op jit(solution)/shard_map/pallas_call | solution.py:205
  19.8 0.4 collective-permute-done.9.refs_12_
  20.2 1.2 %collective-permute-start.11 = (bf16[1,136,512]{2,1,0:T(8,128)(2,1)S(1)}, bf16[1,136,512]{2,1,0:T(8,128)(2,1)S(1)}, u32[]{:S(2)}, u32[]{:S(2)}) collective-permute-start(bf16[1,136,512]{2,1,0:T(8,128)(2,1)S(1)} %collective-permute-done.9.refs_12_), channel_id=1, source_target_pairs={{0,2},{1,3},{2,0},{3,1},{4,6},{5,7},{6,4},{7,5},{8,10},{9,11},{10,... | collective-permute-start | bytes 417800 | tf_op jit(solution)/shard_map/ppermute | solution.py:63
  21.6 0.7 collective-permute-done.5.refs_18_
  22.2 0.5 collective-permute-start.14
  22.8 3.2 %collective-permute-done.11.refs_14_ = bf16[1,136,512]{2,1,0:T(8,128)(2,1)S(1)} collective-permute-done((bf16[1,136,512]{2,1,0:T(8,128)(2,1)S(1)}, bf16[1,136,512]{2,1,0:T(8,128)(2,1)S(1)}, u32[]{:S(2)}, u32[]{:S(2)}) %collective-permute-start.11) | collective-permute-done | bytes 139296 | tf_op jit(solution)/shard_map/ppermute | solution.py:63
  25.9 0.5 collective-permute-start.12
  26.4 0.8 collective-permute-done.8.refs_11_
  27.5 31.0 %shard_map.107 = (bf16[2,1,128,512]{3,2,1,0:T(8,128)(2,1)S(1)}, bf16[2,1,128,512]{3,2,1,0:T(8,128)(2,1)S(1)}, bf16[2,2,128,512]{3,2,1,0:T(8,128)(2,1)}, bf16[2,2...) custom-call(f32[1,2048]{1,0:T(1,128)} %bitcast.41, ...), custom_call_target="tpu_custom_call" | custom-call | flops 4831838208 | bytes 75497472 | tf_op jit(solution)/shard_map/pallas_call | solution.py:433
  58.5 0.4 collective-permute-start.19
  59.4 0.7 collective-permute-done.19
  60.2 1.6 %collective-permute-start.20 = (bf16[1,128,512]{2,1,0:T(8,128)(2,1)S(1)}, bf16[1,128,512]{2,1,0:T(8,128)(2,1)S(1)}, u32[]{:S(2)}, u32[]{:S(2)}) collective-permute-start(bf16[1,128,512]{2,1,0:T(8,128)(2,1)S(1)} %slice_bitcast_fusion.3), channel_id=1, source_target_pairs={{0,2},{1,3},{2,0},{3,1},{4,6},{5,7},{6,4},{7,5},{8,10},{9,11},{10,... | collective-permute-start | bytes 393224 | tf_op jit(solution)/shard_map/ppermute | solution.py:63
  61.8 1.2 %add_convert_fusion = bf16[2,2,128,512]{3,2,1,0:T(8,128)(2,1)S(1)} fusion(bf16[2,2,128,512]{3,2,1,0:T(8,128)(2,1)S(1)} %collective-permute-done.16, bf16[2,2,128,512]{3,2,1,0:T(8,128)(2,1)} %get-tuple-element.47), kind=kLoop, calls=%fused_computation | loop fusion | flops 1048576 | bytes 1572864 | tf_op jit(solution)/shard_map/convert_element_type | solution.py:468
  63.0 1.2 %collective-permute-start.17 = (bf16[2,128,512]{2,1,0:T(8,128)(2,1)S(1)}, bf16[2,128,512]{2,1,0:T(8,128)(2,1)S(1)}, u32[]{:S(2)}, u32[]{:S(2)}) collective-permute-start(bf16[2,128,512]{2,1,0:T(8,128)(2,1)S(1)} %slice_bitcast_fusion.1), channel_id=1, source_target_pairs={{0,2},{1,3},{2,0},{3,1},{4,6},{5,7},{6,4},{7,5},{8,10},{9,11},{10,... | collective-permute-start | bytes 786440 | tf_op jit(solution)/shard_map/ppermute | solution.py:63
  64.3 1.8 %collective-permute-done.20 = bf16[1,128,512]{2,1,0:T(8,128)(2,1)S(1)} collective-permute-done((bf16[1,128,512]{2,1,0:T(8,128)(2,1)S(1)}, bf16[1,128,512]{2,1,0:T(8,128)(2,1)S(1)}, u32[]{:S(2)}, u32[]{:S(2)}) %collective-permute-start.20) | collective-permute-done | bytes 131104 | tf_op jit(solution)/shard_map/ppermute | solution.py:63
  66.2 2.8 %collective-permute-start.21 = (bf16[152,512]{1,0:T(8,128)(2,1)S(1)}, bf16[152,512]{1,0:T(8,128)(2,1)S(1)}, u32[]{:S(2)}, u32[]{:S(2)}) collective-permute-start(bf16[152,512]{1,0:T(8,128)(2,1)S(1)} %pad_maximum_fusion.1), channel_id=1, source_target_pairs={{0,12},{4,0},{8,4},{12,8},{1,13},{5,1},{9,5},{13,9},{2,14},{6,2},{... | collective-permute-start | bytes 466952 | tf_op jit(solution)/shard_map/ppermute | solution.py:58
  68.9 2.8 %collective-permute-done.21 = bf16[152,512]{1,0:T(8,128)(2,1)S(1)} collective-permute-done((bf16[152,512]{1,0:T(8,128)(2,1)S(1)}, bf16[152,512]{1,0:T(8,128)(2,1)S(1)}, u32[]{:S(2)}, u32[]{:S(2)}) %collective-permute-start.21) | collective-permute-done | bytes 155680 | tf_op jit(solution)/shard_map/ppermute | solution.py:58
  71.8 0.7 collective-permute-start.23
  72.5 1.5 %collective-permute-start.18 = (bf16[1,128,512]{2,1,0:T(8,128)(2,1)S(1)}, bf16[1,128,512]{2,1,0:T(8,128)(2,1)S(1)}, u32[]{:S(2)}, u32[]{:S(2)}) collective-permute-start(bf16[1,128,512]{2,1,0:T(8,128)(2,1)S(1)} %slice_bitcast_fusion.6), channel_id=1, source_target_pairs={{0,2},{1,3},{2,0},{3,1},{4,6},{5,7},{6,4},{7,5},{8,10},{9,11},{10,... | collective-permute-start | bytes 393224 | tf_op jit(solution)/shard_map/ppermute | solution.py:63
  74.1 3.8 %collective-permute-start.22 = (bf16[176,512]{1,0:T(8,128)(2,1)S(1)}, bf16[176,512]{1,0:T(8,128)(2,1)S(1)}, u32[]{:S(2)}, u32[]{:S(2)}) collective-permute-start(bf16[176,512]{1,0:T(8,128)(2,1)S(1)} %pad_maximum_fusion), channel_id=1, source_target_pairs={{0,12},{4,0},{8,4},{12,8},{1,13},{5,1},{9,5},{13,9},{2,14},{6,2},{... | collective-permute-start | bytes 540680 | tf_op jit(solution)/shard_map/ppermute | solution.py:58
  77.9 2.9 %collective-permute-done.23.up_ref = bf16[152,512]{1,0:T(8,128)(2,1)S(1)} collective-permute-done((bf16[152,512]{1,0:T(8,128)(2,1)S(1)}, bf16[152,512]{1,0:T(8,128)(2,1)S(1)}, u32[]{:S(2)}, u32[]{:S(2)}) %collective-permute-start.23) | collective-permute-done | bytes 155680 | tf_op jit(solution)/shard_map/ppermute | solution.py:58
  80.8 1.9 %collective-permute-done.22.down_ref = bf16[176,512]{1,0:T(8,128)(2,1)S(1)} collective-permute-done((bf16[176,512]{1,0:T(8,128)(2,1)S(1)}, bf16[176,512]{1,0:T(8,128)(2,1)S(1)}, u32[]{:S(2)}, u32[]{:S(2)}) %collective-permute-start.22) | collective-permute-done | bytes 180256 | tf_op jit(solution)/shard_map/ppermute | solution.py:58
  82.7 0.8 shard_map.108
  (39 shorter events, 1.4 us)
Async XLA Ops:
  1.6 10.7 %collective-permute-start = (bf16[1,136,512]{2,1,0:T(8,128)(2,1)S(1)}, bf16[1,136,512]{2,1,0:T(8,128)(2,1)S(1)}, u32[]{:S(2)}, u32[]{:S(2)}) collective-permute-start(bf16[1,136,512]{2,1,0:T(8,128)(2,1)S(1)} %shard_map.104.after_ref.refs_4_), channel_id=1, source_target_pairs={{0,4},{4,8},{8,12},{12,0},{1,5},{5,9},{9,13},{13,1},{2,6},{6,10},{... | collective-permute-start | bytes 417800 | tf_op jit(solution)/shard_map/ppermute | solution.py:58
  4.7 8.1 %collective-permute-start.1 = (bf16[1,136,512]{2,1,0:T(8,128)(2,1)S(1)}, bf16[1,136,512]{2,1,0:T(8,128)(2,1)S(1)}, u32[]{:S(2)}, u32[]{:S(2)}) collective-permute-start(bf16[1,136,512]{2,1,0:T(8,128)(2,1)S(1)} %shard_map.104.after_ref.refs_4_), channel_id=1, source_target_pairs={{0,12},{4,0},{8,4},{12,8},{1,13},{5,1},{9,5},{13,9},{2,14},{6,2},{... | collective-permute-start | bytes 417800 | tf_op jit(solution)/shard_map/ppermute | solution.py:58
  6.8 6.0 %collective-permute-start.2 = (bf16[1,136,512]{2,1,0:T(8,128)(2,1)S(1)}, bf16[1,136,512]{2,1,0:T(8,128)(2,1)S(1)}, u32[]{:S(2)}, u32[]{:S(2)}) collective-permute-start(bf16[1,136,512]{2,1,0:T(8,128)(2,1)S(1)} %shard_map.104.after_ref.refs_4_), channel_id=1, source_target_pairs={{0,2},{1,3},{2,0},{3,1},{4,6},{5,7},{6,4},{7,5},{8,10},{9,11},{10,... | collective-permute-start | bytes 417800 | tf_op jit(solution)/shard_map/ppermute | solution.py:63
  8.4 4.4 %collective-permute-start.3 = (bf16[1,136,512]{2,1,0:T(8,128)(2,1)S(1)}, bf16[1,136,512]{2,1,0:T(8,128)(2,1)S(1)}, u32[]{:S(2)}, u32[]{:S(2)}) collective-permute-start(bf16[1,136,512]{2,1,0:T(8,128)(2,1)S(1)} %shard_map.104.after_ref.refs_4_), channel_id=1, source_target_pairs={{0,1},{1,0},{2,3},{3,2},{4,5},{5,4},{6,7},{7,6},{8,9},{9,8},{10,11... | collective-permute-start | bytes 417800 | tf_op jit(solution)/shard_map/ppermute | solution.py:68
  12.8 7.4 %collective-permute-start.9 = (bf16[1,136,512]{2,1,0:T(8,128)(2,1)S(1)}, bf16[1,136,512]{2,1,0:T(8,128)(2,1)S(1)}, u32[]{:S(2)}, u32[]{:S(2)}) collective-permute-start(bf16[1,136,512]{2,1,0:T(8,128)(2,1)S(1)} %collective-permute-done.refs_8_), channel_id=1, source_target_pairs={{0,4},{4,8},{8,12},{12,0},{1,5},{5,9},{9,13},{13,1},{2,6},{6,10},{... | collective-permute-start | bytes 417800 | tf_op jit(solution)/shard_map/ppermute | solution.py:58
  13.9 7.6 %collective-permute-start.4 = (bf16[1,136,512]{2,1,0:T(8,128)(2,1)S(1)}, bf16[1,136,512]{2,1,0:T(8,128)(2,1)S(1)}, u32[]{:S(2)}, u32[]{:S(2)}) collective-permute-start(bf16[1,136,512]{2,1,0:T(8,128)(2,1)S(1)} %collective-permute-done.refs_8_), channel_id=1, source_target_pairs={{0,2},{1,3},{2,0},{3,1},{4,6},{5,7},{6,4},{7,5},{8,10},{9,11},{10,... | collective-permute-start | bytes 417800 | tf_op jit(solution)/shard_map/ppermute | solution.py:63
  15.4 6.8 %collective-permute-start.5 = (bf16[1,136,512]{2,1,0:T(8,128)(2,1)S(1)}, bf16[1,136,512]{2,1,0:T(8,128)(2,1)S(1)}, u32[]{:S(2)}, u32[]{:S(2)}) collective-permute-start(bf16[1,136,512]{2,1,0:T(8,128)(2,1)S(1)} %collective-permute-done.1.after_ref.refs_16_), channel_id=1, source_target_pairs={{0,2},{1,3},{2,0},{3,1},{4,6},{5,7},{6,4},{7,5},{8,10},{9,11},{10,... | collective-permute-start | bytes 417800 | tf_op jit(solution)/shard_map/ppermute | solution.py:63
  19.7 3.0 %collective-permute-start.6 = (bf16[1,136,512]{2,1,0:T(8,128)(2,1)S(1)}, bf16[1,136,512]{2,1,0:T(8,128)(2,1)S(1)}, u32[]{:S(2)}, u32[]{:S(2)}) collective-permute-start(bf16[1,136,512]{2,1,0:T(8,128)(2,1)S(1)} %collective-permute-done.2.refs_6_), channel_id=1, source_target_pairs={{0,1},{1,0},{2,3},{3,2},{4,5},{5,4},{6,7},{7,6},{8,9},{9,8},{10,11... | collective-permute-start | bytes 417800 | tf_op jit(solution)/shard_map/ppermute | solution.py:68
  20.2 5.7 %collective-permute-start.11 = (bf16[1,136,512]{2,1,0:T(8,128)(2,1)S(1)}, bf16[1,136,512]{2,1,0:T(8,128)(2,1)S(1)}, u32[]{:S(2)}, u32[]{:S(2)}) collective-permute-start(bf16[1,136,512]{2,1,0:T(8,128)(2,1)S(1)} %collective-permute-done.9.refs_12_), channel_id=1, source_target_pairs={{0,2},{1,3},{2,0},{3,1},{4,6},{5,7},{6,4},{7,5},{8,10},{9,11},{10,... | collective-permute-start | bytes 417800 | tf_op jit(solution)/shard_map/ppermute | solution.py:63
  21.4 4.5 %collective-permute-start.10 = (bf16[1,136,512]{2,1,0:T(8,128)(2,1)S(1)}, bf16[1,136,512]{2,1,0:T(8,128)(2,1)S(1)}, u32[]{:S(2)}, u32[]{:S(2)}) collective-permute-start(bf16[1,136,512]{2,1,0:T(8,128)(2,1)S(1)} %collective-permute-done.9.refs_12_), channel_id=1, source_target_pairs={{0,1},{1,0},{2,3},{3,2},{4,5},{5,4},{6,7},{7,6},{8,9},{9,8},{10,11... | collective-permute-start | bytes 417800 | tf_op jit(solution)/shard_map/ppermute | solution.py:68
  22.2 4.2 %collective-permute-start.13 = (bf16[1,136,512]{2,1,0:T(8,128)(2,1)S(1)}, bf16[1,136,512]{2,1,0:T(8,128)(2,1)S(1)}, u32[]{:S(2)}, u32[]{:S(2)}) collective-permute-start(bf16[1,136,512]{2,1,0:T(8,128)(2,1)S(1)} %collective-permute-done.1.after_ref.refs_16_), channel_id=1, source_target_pairs={{0,1},{1,0},{2,3},{3,2},{4,5},{5,4},{6,7},{7,6},{8,9},{9,8},{10,11... | collective-permute-start | bytes 417800 | tf_op jit(solution)/shard_map/ppermute | solution.py:68
  22.2 4.2 %collective-permute-start.14 = (bf16[1,136,512]{2,1,0:T(8,128)(2,1)S(1)}, bf16[1,136,512]{2,1,0:T(8,128)(2,1)S(1)}, u32[]{:S(2)}, u32[]{:S(2)}) collective-permute-start(bf16[1,136,512]{2,1,0:T(8,128)(2,1)S(1)} %collective-permute-done.5.refs_18_), channel_id=1, source_target_pairs={{0,1},{1,0},{2,3},{3,2},{4,5},{5,4},{6,7},{7,6},{8,9},{9,8},{10,11... | collective-permute-start | bytes 417800 | tf_op jit(solution)/shard_map/ppermute | solution.py:68
  22.7 3.7 %collective-permute-start.7 = (bf16[1,136,512]{2,1,0:T(8,128)(2,1)S(1)}, bf16[1,136,512]{2,1,0:T(8,128)(2,1)S(1)}, u32[]{:S(2)}, u32[]{:S(2)}) collective-permute-start(bf16[1,136,512]{2,1,0:T(8,128)(2,1)S(1)} %collective-permute-done.refs_8_), channel_id=1, source_target_pairs={{0,1},{1,0},{2,3},{3,2},{4,5},{5,4},{6,7},{7,6},{8,9},{9,8},{10,11... | collective-permute-start | bytes 417800 | tf_op jit(solution)/shard_map/ppermute | solution.py:68
  25.9 1.4 %collective-permute-start.8 = (bf16[1,136,512]{2,1,0:T(8,128)(2,1)S(1)}, bf16[1,136,512]{2,1,0:T(8,128)(2,1)S(1)}, u32[]{:S(2)}, u32[]{:S(2)}) collective-permute-start(bf16[1,136,512]{2,1,0:T(8,128)(2,1)S(1)} %collective-permute-done.4.refs_10_), channel_id=1, source_target_pairs={{0,1},{1,0},{2,3},{3,2},{4,5},{5,4},{6,7},{7,6},{8,9},{9,8},{10,11... | collective-permute-start | bytes 417800 | tf_op jit(solution)/shard_map/ppermute | solution.py:68
  25.9 1.6 %collective-permute-start.12 = (bf16[1,136,512]{2,1,0:T(8,128)(2,1)S(1)}, bf16[1,136,512]{2,1,0:T(8,128)(2,1)S(1)}, u32[]{:S(2)}, u32[]{:S(2)}) collective-permute-start(bf16[1,136,512]{2,1,0:T(8,128)(2,1)S(1)} %collective-permute-done.11.refs_14_), channel_id=1, source_target_pairs={{0,1},{1,0},{2,3},{3,2},{4,5},{5,4},{6,7},{7,6},{8,9},{9,8},{10,11... | collective-permute-start | bytes 417800 | tf_op jit(solution)/shard_map/ppermute | solution.py:68
  58.4 24.3 %copy-start = (bf16[128,512]{1,0:T(8,128)(2,1)S(1)}, bf16[128,512]{1,0:T(8,128)(2,1)}, u32[]{:S(2)}) copy-start(bf16[128,512]{1,0:T(8,128)(2,1)} %hidden_ref.3) | copy-start | bytes 393220
  58.5 1.6 %collective-permute-start.19 = (bf16[2,1,128,512]{3,2,1,0:T(8,128)(2,1)S(1)}, bf16[2,1,128,512]{3,2,1,0:T(8,128)(2,1)S(1)}, u32[]{:S(2)}, u32[]{:S(2)}) collective-permute-start(bf16[2,1,128,512]{3,2,1,0:T(8,128)(2,1)S(1)} %get-tuple-element.51), channel_id=1, source_target_pairs={{0,1},{1,0},{2,3},{3,2},{4,5},{5,4},{6,7},{7,6},{8,9},{9,8},{10,11... | collective-permute-start | bytes 786440 | tf_op jit(solution)/shard_map/ppermute | solution.py:68
  58.8 3.0 %collective-permute-start.16 = (bf16[2,2,128,512]{3,2,1,0:T(8,128)(2,1)}, bf16[2,2,128,512]{3,2,1,0:T(8,128)(2,1)S(1)}, u32[]{:S(2)}, u32[]{:S(2)}) collective-permute-start(bf16[2,2,128,512]{3,2,1,0:T(8,128)(2,1)} %get-tuple-element.48), channel_id=1, source_target_pairs={{0,1},{1,0},{2,3},{3,2},{4,5},{5,4},{6,7},{7,6},{8,9},{9,8},{10,11... | collective-permute-start | bytes 1572872 | tf_op jit(solution)/shard_map/ppermute | solution.py:68
  59.0 2.7 %collective-permute-start.15 = (bf16[2,1,128,512]{3,2,1,0:T(8,128)(2,1)}, bf16[2,1,128,512]{3,2,1,0:T(8,128)(2,1)S(1)}, u32[]{:S(2)}, u32[]{:S(2)}) collective-permute-start(bf16[2,1,128,512]{3,2,1,0:T(8,128)(2,1)} %get-tuple-element.46), channel_id=1, source_target_pairs={{0,1},{1,0},{2,3},{3,2},{4,5},{5,4},{6,7},{7,6},{8,9},{9,8},{10,11... | collective-permute-start | bytes 786440 | tf_op jit(solution)/shard_map/ppermute | solution.py:68
  60.2 5.9 %collective-permute-start.20 = (bf16[1,128,512]{2,1,0:T(8,128)(2,1)S(1)}, bf16[1,128,512]{2,1,0:T(8,128)(2,1)S(1)}, u32[]{:S(2)}, u32[]{:S(2)}) collective-permute-start(bf16[1,128,512]{2,1,0:T(8,128)(2,1)S(1)} %slice_bitcast_fusion.3), channel_id=1, source_target_pairs={{0,2},{1,3},{2,0},{3,1},{4,6},{5,7},{6,4},{7,5},{8,10},{9,11},{10,... | collective-permute-start | bytes 393224 | tf_op jit(solution)/shard_map/ppermute | solution.py:63
  63.0 8.7 %collective-permute-start.17 = (bf16[2,128,512]{2,1,0:T(8,128)(2,1)S(1)}, bf16[2,128,512]{2,1,0:T(8,128)(2,1)S(1)}, u32[]{:S(2)}, u32[]{:S(2)}) collective-permute-start(bf16[2,128,512]{2,1,0:T(8,128)(2,1)S(1)} %slice_bitcast_fusion.1), channel_id=1, source_target_pairs={{0,2},{1,3},{2,0},{3,1},{4,6},{5,7},{6,4},{7,5},{8,10},{9,11},{10,... | collective-permute-start | bytes 786440 | tf_op jit(solution)/shard_map/ppermute | solution.py:63
  66.2 5.5 %collective-permute-start.21 = (bf16[152,512]{1,0:T(8,128)(2,1)S(1)}, bf16[152,512]{1,0:T(8,128)(2,1)S(1)}, u32[]{:S(2)}, u32[]{:S(2)}) collective-permute-start(bf16[152,512]{1,0:T(8,128)(2,1)S(1)} %pad_maximum_fusion.1), channel_id=1, source_target_pairs={{0,12},{4,0},{8,4},{12,8},{1,13},{5,1},{9,5},{13,9},{2,14},{6,2},{... | collective-permute-start | bytes 466952 | tf_op jit(solution)/shard_map/ppermute | solution.py:58
  71.8 9.0 %collective-permute-start.23 = (bf16[152,512]{1,0:T(8,128)(2,1)S(1)}, bf16[152,512]{1,0:T(8,128)(2,1)S(1)}, u32[]{:S(2)}, u32[]{:S(2)}) collective-permute-start(bf16[152,512]{1,0:T(8,128)(2,1)S(1)} %pad_maximum_fusion.2), channel_id=1, source_target_pairs={{0,4},{4,8},{8,12},{12,0},{1,5},{5,9},{9,13},{13,1},{2,6},{6,10},{... | collective-permute-start | bytes 466952 | tf_op jit(solution)/shard_map/ppermute | solution.py:58
  72.5 5.4 %collective-permute-start.18 = (bf16[1,128,512]{2,1,0:T(8,128)(2,1)S(1)}, bf16[1,128,512]{2,1,0:T(8,128)(2,1)S(1)}, u32[]{:S(2)}, u32[]{:S(2)}) collective-permute-start(bf16[1,128,512]{2,1,0:T(8,128)(2,1)S(1)} %slice_bitcast_fusion.6), channel_id=1, source_target_pairs={{0,2},{1,3},{2,0},{3,1},{4,6},{5,7},{6,4},{7,5},{8,10},{9,11},{10,... | collective-permute-start | bytes 393224 | tf_op jit(solution)/shard_map/ppermute | solution.py:63
  74.1 8.7 %collective-permute-start.22 = (bf16[176,512]{1,0:T(8,128)(2,1)S(1)}, bf16[176,512]{1,0:T(8,128)(2,1)S(1)}, u32[]{:S(2)}, u32[]{:S(2)}) collective-permute-start(bf16[176,512]{1,0:T(8,128)(2,1)S(1)} %pad_maximum_fusion), channel_id=1, source_target_pairs={{0,12},{4,0},{8,4},{12,8},{1,13},{5,1},{9,5},{13,9},{2,14},{6,2},{... | collective-permute-start | bytes 540680 | tf_op jit(solution)/shard_map/ppermute | solution.py:58

commit v14 on v9

--- a/solution.py
+++ b/solution.py
@@ -14,12 +14,16 @@
 SEND_CAP = 40
 CORES = 2
 HOP_NODES = 4
+READY = (0, 1, 3)
+LAST = 2
 RETURNS = ((2,), (1, 3), (0,))
 HOP_CHIPS = 2
 PAGE_FOLD = 24
 SMALL_VMEM = 4 * 1024 * 1024
 WEIGHT_SLOTS = 3
-EXPERT_VMEM = 31 * 1024 * 1024
+ROWS_VMEM = 6 * 1024 * 1024
+FILL_COST = 18 * 1024 * 1024
+EXPERT_VMEM = 32 * 1024 * 1024
 
 epsilon = 1e-06
 
@@ -90,6 +94,10 @@
 
 def in_hbm(*arrays):
     return [pltpu.with_memory_space_constraint(array, pltpu.HBM) for array in arrays]
+
+
+def in_vmem(*arrays):
+    return [pltpu.with_memory_space_constraint(array, pltpu.VMEM) for array in arrays]
 
 
 def packed(hidden_states, routes, gates):
@@ -142,12 +150,152 @@
     )
 
 
-def fill_kernel(gate_up_ref, down_ref, after_ref, gate_up_out, down_out, sems, *, expert):
+def own_place(held, chips, width):
+    column = lax.axis_index("mp")
+    my_x, my_core = lax.div(column, CORES), lax.rem(column, CORES)
+    first_expert = (lax.axis_index("dp") * lax.axis_size("mp") + column) * held
+
+    def features(x, c):
+        place = lax.rem(my_x + chips - x, chips) * CORES + (my_core ^ c)
+        return pl.ds(pl.multiple_of(place * width, width), width)
+
+    return first_expert, features
+
+
+def write_rows(block_refs, gain_buf, gain_copy, rows_ref, pick_ref, gate_ref):
+    chips = len(block_refs) // CORES
+    _, block_rows, width = block_refs[0].shape
+    tok_node = block_rows - TOPK
+    all_slots, model_width = rows_ref.shape
+    held = all_slots // CAP
+    first_expert, features = own_place(held, chips, width)
+    expert = first_expert + lax.broadcasted_iota(jnp.int32, (held, 1), 0)
+    earlier = jnp.where(
+        lax.broadcasted_iota(jnp.int32, (tok_node, tok_node), 0)
+        < lax.broadcasted_iota(jnp.int32, (tok_node, tok_node), 1),
+        1.0, 0.0,
+    ).astype(jnp.bfloat16)
+    slot_number = lax.broadcasted_iota(jnp.int32, (CAP, tok_node), 0)
+    choices = block_refs[0][0, tok_node:, :].astype(jnp.float32)
+    number = choices[:, :tok_node].astype(jnp.int32)
+    value = (
+        choices[:, tok_node : 2 * tok_node]
+        + choices[:, 2 * tok_node : 3 * tok_node]
+        + choices[:, 3 * tok_node :]
+    )
+    named = jnp.zeros((held, tok_node), jnp.float32)
+    gate = jnp.zeros((held, tok_node), jnp.float32)
+    for choice in range(TOPK):
+        match = number[choice : choice + 1, :] == expert
+        named = named + jnp.where(match, 1.0, 0.0)
+        gate = gate + jnp.where(match, value[choice : choice + 1, :], 0.0)
+    rank = jnp.dot(named.astype(jnp.bfloat16), earlier, preferred_element_type=jnp.float32)
+    rank = jnp.where(named > 0.0, rank, -1.0).astype(jnp.int32)
+    for h in range(held):
+        here = rank[h : h + 1, :] == slot_number
+        at = pl.ds(h * CAP, CAP)
+        pick_ref[at, :] = jnp.where(here, 1.0, 0.0).astype(jnp.bfloat16)
+        gate_ref[at, :] = jnp.broadcast_to(
+            jnp.sum(jnp.where(here, gate[h : h + 1, :], 0.0), axis=1, keepdims=True),
+            (CAP, gate_ref.shape[1]),
+        )
+    total = jnp.zeros((tok_node, 1), jnp.float32)
+    for block in block_refs:
+        wide = block[0, :tok_node, :].astype(jnp.float32)
+        total = total + jnp.sum(wide * wide, axis=1, keepdims=True)
+    inv_scale = lax.rsqrt(total / model_width + epsilon)
+    gain_copy.wait()
+    for i, block in enumerate(block_refs):
+        part = features(i // CORES, i % CORES)
+        wide = block[0, :tok_node, :].astype(jnp.float32)
+        normed = (wide * inv_scale * gain_buf[:, part]).astype(jnp.bfloat16)
+        rows_ref[:, part] = jnp.dot(
+            pick_ref[...], normed, preferred_element_type=jnp.float32
+        ).astype(jnp.bfloat16)
+
+
+class ReadyCopy:
+    def wait(self):
+        pass
+
+
+def rows_kernel(gain_ref, *refs, nodes, blocks):
+    block_refs, refs = refs[: nodes * blocks], refs[nodes * blocks :]
+    out_refs, (gain_buf, gain_sem) = refs[: 3 * nodes], refs[3 * nodes :]
+    gain_copy = pltpu.make_async_copy(gain_ref, gain_buf, gain_sem)
+    gain_copy.start()
+    for i in range(nodes):
+        write_rows(
+            block_refs[i * blocks : (i + 1) * blocks], gain_buf, gain_copy if i == 0 else ReadyCopy(),
+            *out_refs[3 * i : 3 * i + 3],
+        )
+
+
+def fill_rows_kernel(gate_up_ref, down_ref, gain_ref, *refs, expert, blocks):
+    block_refs, refs = refs[:blocks], refs[blocks:]
+    gate_up_out, down_out, rows_ref, pick_ref, gate_ref, sems, gain_buf, gain_sem = refs
+    gain_copy = pltpu.make_async_copy(gain_ref, gain_buf, gain_sem)
+    gain_copy.start()
     copies = expert_copies(gate_up_ref, down_ref, expert, gate_up_out, down_out, sems)
     for copy in copies:
         copy.start()
+    write_rows(block_refs, gain_buf, gain_copy, rows_ref, pick_ref, gate_ref)
     for copy in copies:
         copy.wait()
+
+
+def row_shapes(held, tok_node, model_width):
+    return [
+        jax.ShapeDtypeStruct((held * CAP, model_width), jnp.bfloat16),
+        jax.ShapeDtypeStruct((held * CAP, tok_node), jnp.bfloat16),
+        jax.ShapeDtypeStruct((held * CAP, tok_node), jnp.float32),
+    ]
+
+
+def node_rows(gain, nodes, held):
+    flat = [block for blocks in nodes for block in blocks]
+    _, block_rows, width = flat[0].shape
+    blocks = len(nodes[0])
+    vmem = pl.BlockSpec(memory_space=pltpu.VMEM)
+    outs = pl.pallas_call(
+        functools.partial(rows_kernel, nodes=len(nodes), blocks=blocks),
+        out_shape=row_shapes(held, block_rows - TOPK, blocks * width) * len(nodes),
+        in_specs=[pl.BlockSpec(memory_space=pltpu.HBM)] + [vmem] * len(flat),
+        out_specs=[vmem] * (3 * len(nodes)),
+        scratch_shapes=[
+            pltpu.VMEM((1, blocks * width), jnp.float32),
+            pltpu.SemaphoreType.DMA(()),
+        ],
+        compiler_params=pltpu.CompilerParams(vmem_limit_bytes=ROWS_VMEM),
+        cost_estimate=pl.CostEstimate(flops=0, bytes_accessed=FILL_COST, transcendentals=0),
+    )(*in_hbm(gain), *flat)
+    return [outs[3 * i : 3 * i + 3] for i in range(len(nodes))]
+
+
+def filled_with_rows(gate_up_weight, down_weight, expert, gain, blocks):
+    width = down_weight.shape[1]
+    ff_part = min(FF, down_weight.shape[0])
+    held = max(1, down_weight.shape[0] // FF)
+    hbm = pl.BlockSpec(memory_space=pltpu.HBM)
+    vmem = pl.BlockSpec(memory_space=pltpu.VMEM)
+    *weights, rows, pick, gate = pl.pallas_call(
+        functools.partial(fill_rows_kernel, expert=expert, blocks=len(blocks)),
+        out_shape=[
+            pltpu.VMEM((2, ff_part, width), down_weight.dtype),
+            pltpu.VMEM((ff_part, width), down_weight.dtype),
+        ]
+        + row_shapes(held, blocks[0].shape[1] - TOPK, width),
+        in_specs=[hbm] * 3 + [vmem] * len(blocks),
+        out_specs=[vmem] * 5,
+        scratch_shapes=[
+            pltpu.SemaphoreType.DMA((3,)),
+            pltpu.VMEM((1, width), jnp.float32),
+            pltpu.SemaphoreType.DMA(()),
+        ],
+        compiler_params=pltpu.CompilerParams(vmem_limit_bytes=ROWS_VMEM),
+        cost_estimate=pl.CostEstimate(flops=0, bytes_accessed=FILL_COST, transcendentals=0),
+    )(gate_up_weight, down_weight, *in_hbm(gain), *blocks)
+    return weights, (rows, pick, gate)
 
 
 def page_fill_kernel(
@@ -170,7 +318,7 @@
         copy.wait()
 
 
-def filled(gate_up_weight, down_weight, expert, after, paged=None):
+def filled(gate_up_weight, down_weight, expert, after, paged):
     width = down_weight.shape[1]
     ff_part = min(FF, down_weight.shape[0])
     hbm = pl.BlockSpec(memory_space=pltpu.HBM)
@@ -181,24 +329,19 @@
     ]
     scratch = [pltpu.SemaphoreType.DMA((3,))]
     operands = [gate_up_weight, down_weight, after]
-    kernel = fill_kernel
-    if paged is not None:
-        kv_rows, lengths, owners = paged
-        kernel = page_fill_kernel
-        operands += in_hbm(kv_rows, lengths, owners)
-        out_shape.append(
-            jax.ShapeDtypeStruct(
-                (lengths.shape[0], PAGE_FOLD, 2 * kv_rows.shape[1]), jnp.bfloat16
-            )
-        )
-        scratch += [
-            pltpu.VMEM(kv_rows.shape, kv_rows.dtype),
-            pltpu.SMEM(lengths.shape, jnp.int32),
-            pltpu.SMEM(owners.shape, jnp.int32),
-            pltpu.SemaphoreType.DMA((3,)),
-        ]
+    kv_rows, lengths, owners = paged
+    operands += in_hbm(kv_rows, lengths, owners)
+    out_shape.append(
+        jax.ShapeDtypeStruct((lengths.shape[0], PAGE_FOLD, 2 * kv_rows.shape[1]), jnp.bfloat16)
+    )
+    scratch += [
+        pltpu.VMEM(kv_rows.shape, kv_rows.dtype),
+        pltpu.SMEM(lengths.shape, jnp.int32),
+        pltpu.SMEM(owners.shape, jnp.int32),
+        pltpu.SemaphoreType.DMA((3,)),
+    ]
     return pl.pallas_call(
-        functools.partial(kernel, expert=expert),
+        functools.partial(page_fill_kernel, expert=expert),
         out_shape=out_shape,
         in_specs=[hbm, hbm, pl.BlockSpec(memory_space=pl.ANY)] + [hbm] * (len(operands) - 3),
         out_specs=[vmem] * len(out_shape),
@@ -247,19 +390,16 @@
     )(hidden_states, own, down, up, pages)
 
 
-def expert_kernel(
-    gain_ref, gate_up_ref, down_ref, *refs, held, parts, chips, fills,
-):
+def expert_kernel(gain_ref, gate_up_ref, down_ref, *refs, held, parts, chips, fills):
     held_refs, refs = refs[: 2 * fills], refs[2 * fills :]
-    block_refs, out_refs = refs[: parts * chips * CORES], refs[parts * chips * CORES :]
-    out_refs, scratch = out_refs[: len(RETURNS) * CORES], out_refs[len(RETURNS) * CORES :]
+    block_refs, refs = refs[: chips * CORES], refs[chips * CORES :]
+    ready, refs = refs[: 3 * (parts - 1)], refs[3 * (parts - 1) :]
+    out_refs, scratch = refs[: len(RETURNS) * CORES], refs[len(RETURNS) * CORES :]
     (
-        pick_ref, picked_ref, slot_gate_ref, gain_buf, gu_buf, down_buf, sems, gain_sem,
+        last_rows, last_pick, last_gate, served_ref, gain_buf, gu_buf, down_buf, sems, gain_sem,
     ) = scratch
-    _, block_rows, width = block_refs[0].shape
-    tok_node = block_rows - TOPK
-    model_width = picked_ref.shape[1]
-    served_ref = picked_ref
+    width = block_refs[0].shape[2]
+    _, features = own_place(held, chips, width)
     slots = down_buf.shape[0]
 
     def fetch(h, slot):
@@ -273,80 +413,21 @@
         for copy in fetch(fills + slot, slot):
             copy.start()
 
-    column = lax.axis_index("mp")
-    my_x, my_core = lax.div(column, CORES), lax.rem(column, CORES)
-    first_expert = (lax.axis_index("dp") * lax.axis_size("mp") + column) * held
-    blocks = [
-        [[block_refs[(z * chips + x) * CORES + c] for c in range(CORES)] for x in range(chips)]
-        for z in range(parts)
-    ]
-    features = [
-        [
-            pl.ds(
-                pl.multiple_of(
-                    (lax.rem(my_x + chips - x, chips) * CORES + (my_core ^ c)) * width,
-                    width,
-                ),
-                width,
-            )
-            for c in range(CORES)
-        ]
-        for x in range(chips)
-    ]
-
-    expert = first_expert + lax.broadcasted_iota(jnp.int32, (held, 1), 0)
-    earlier = jnp.where(
-        lax.broadcasted_iota(jnp.int32, (tok_node, tok_node), 0)
-        < lax.broadcasted_iota(jnp.int32, (tok_node, tok_node), 1),
-        1.0, 0.0,
-    ).astype(jnp.bfloat16)
-    slot_number = lax.broadcasted_iota(jnp.int32, (CAP, tok_node), 0)
-    gain_copy.wait()
-    for z in range(parts):
-        choices = blocks[z][0][0][0, tok_node:, :].astype(jnp.float32)
-        number = choices[:, :tok_node].astype(jnp.int32)
-        value = (
-            choices[:, tok_node : 2 * tok_node]
-            + choices[:, 2 * tok_node : 3 * tok_node]
-            + choices[:, 3 * tok_node :]
-        )
-        named = jnp.zeros((held, tok_node), jnp.float32)
-        gate = jnp.zeros((held, tok_node), jnp.float32)
-        for choice in range(TOPK):
-            match = number[choice : choice + 1, :] == expert
-            named = named + jnp.where(match, 1.0, 0.0)
-            gate = gate + jnp.where(match, value[choice : choice + 1, :], 0.0)
-        rank = jnp.dot(named.astype(jnp.bfloat16), earlier, preferred_element_type=jnp.float32)
-        rank = jnp.where(named > 0.0, rank, -1.0).astype(jnp.int32)
-        for h in range(held):
-            here = rank[h : h + 1, :] == slot_number
-            pick_ref[z, pl.ds(h * CAP, CAP), :] = jnp.where(here, 1.0, 0.0).astype(jnp.bfloat16)
-            slot_gate_ref[pl.ds((z * held + h) * CAP, CAP), :] = jnp.sum(
-                jnp.where(here, gate[h : h + 1, :], 0.0), axis=1, keepdims=True
-            )
-        total = jnp.zeros((tok_node, 1), jnp.float32)
-        for x in range(chips):
-            for c in range(CORES):
-                wide = blocks[z][x][c][0, :tok_node, :].astype(jnp.float32)
-                total = total + jnp.sum(wide * wide, axis=1, keepdims=True)
-        inv_scale = lax.rsqrt(total / model_width + epsilon)
-        at = pl.ds(z * held * CAP, held * CAP)
-        for x in range(chips):
-            for c in range(CORES):
-                wide = blocks[z][x][c][0, :tok_node, :].astype(jnp.float32)
-                normed = (wide * inv_scale * gain_buf[:, features[x][c]]).astype(jnp.bfloat16)
-                picked_ref[at, features[x][c]] = jnp.dot(
-                    pick_ref[z], normed, preferred_element_type=jnp.float32
-                ).astype(jnp.bfloat16)
-
-    def rows_of(h):
-        first = [(z * held + h) * CAP for z in range(parts)]
-        if not isinstance(h, int):
-            first = [pl.multiple_of(at, CAP) for at in first]
-        return [pl.ds(at, CAP) for at in first]
+    write_rows(block_refs, gain_buf, gain_copy, last_rows, last_pick, last_gate)
+    ready = [ready[3 * i : 3 * i + 3] for i in range(parts - 1)]
+    by_node = {z: triple for z, triple in zip(READY, ready)}
+    by_node[LAST] = (last_rows, last_pick, last_gate)
+
+    def rows_at(h):
+        first = h * CAP
+        return pl.ds(first if isinstance(h, int) else pl.multiple_of(first, CAP), CAP)
+
+    def served_at(z, h):
+        first = (z * held + h) * CAP
+        return pl.ds(first if isinstance(h, int) else pl.multiple_of(first, CAP), CAP)
 
     def one_expert(h, gate_up, down):
-        picked = jnp.concatenate([picked_ref[at, :] for at in rows_of(h)], axis=0)
+        picked = jnp.concatenate([by_node[z][0][rows_at(h), :] for z in range(parts)], axis=0)
         along = (((1,), (1,)), ((), ()))
         gate_part = lax.dot_general(
             gate_up[0], picked, along, preferred_element_type=jnp.float32
@@ -358,9 +439,9 @@
         served = lax.dot_general(
             activated, down[...], (((0,), (0,)), ((), ())), preferred_element_type=jnp.float32
         )
-        for z, at in enumerate(rows_of(h)):
-            served_ref[at, :] = (
-                served[z * CAP : (z + 1) * CAP, :] * slot_gate_ref[at, :]
+        for z in range(parts):
+            served_ref[served_at(z, h), :] = (
+                served[z * CAP : (z + 1) * CAP, :] * by_node[z][2][rows_at(h), :1]
             ).astype(jnp.bfloat16)
 
     for h in range(fills):
@@ -383,29 +464,28 @@
 
     for group, members in enumerate(RETURNS):
         for i, z in enumerate(members):
-            back = pick_ref[z].T
+            back = by_node[z][1][...].T
             at = pl.ds(z * held * CAP, held * CAP)
             for x in range(chips):
                 for c in range(CORES):
                     out_refs[group * CORES + c][x, i] = jnp.dot(
-                        back, served_ref[at, features[x][c]], preferred_element_type=jnp.float32
+                        back, served_ref[at, features(x, c)], preferred_element_type=jnp.float32
                     ).astype(jnp.bfloat16)
 
 
-def expert_sums(gain, gate_up_weight, down_weight, held_weights, blocks):
-    parts, chips = len(blocks), len(blocks[0])
-    _, block_rows, width = blocks[0][0][0].shape
+def expert_sums(gain, gate_up_weight, down_weight, held_weights, blocks, ready):
+    parts, chips = len(ready) + 1, len(blocks) // CORES
+    _, block_rows, width = blocks[0].shape
     tok_node = block_rows - TOPK
     model_width = chips * CORES * width
     ff_dev = down_weight.shape[0]
     held = max(1, ff_dev // FF)
-    capacity = CAP * parts
     ff_part = ff_dev // held
-    all_slots = held * capacity
+    all_slots = held * CAP * parts
     vmem = pl.BlockSpec(memory_space=pltpu.VMEM)
     hbm = pl.BlockSpec(memory_space=pltpu.HBM)
-    held_weights = [pltpu.with_memory_space_constraint(w, pltpu.VMEM) for w in held_weights]
-    flat = [blocks[z][x][c] for z in range(parts) for x in range(chips) for c in range(CORES)]
+    flat = [array for triple in ready for array in triple]
+    outs = len(RETURNS) * CORES
     sums = pl.pallas_call(
         functools.partial(
             expert_kernel, held=held, parts=parts, chips=chips, fills=len(held_weights) // 2
@@ -415,12 +495,13 @@
             for members in RETURNS
             for _ in range(CORES)
         ],
-        in_specs=[hbm] * 3 + [vmem] * (len(held_weights) + len(flat)),
-        out_specs=[vmem] * (len(RETURNS) * CORES),
+        in_specs=[hbm] * 3 + [vmem] * (len(held_weights) + len(blocks) + len(flat)),
+        out_specs=[vmem] * outs,
         scratch_shapes=[
-            pltpu.VMEM((parts, held * CAP, tok_node), jnp.bfloat16),
+            pltpu.VMEM((held * CAP, model_width), jnp.bfloat16),
+            pltpu.VMEM((held * CAP, tok_node), jnp.bfloat16),
+            pltpu.VMEM((held * CAP, tok_node), jnp.float32),
             pltpu.VMEM((all_slots, model_width), jnp.bfloat16),
-            pltpu.VMEM((all_slots, 1), jnp.float32),
             pltpu.VMEM((1, model_width), jnp.float32),
             pltpu.VMEM((WEIGHT_SLOTS, 2, ff_part, model_width), jnp.bfloat16),
             pltpu.VMEM((WEIGHT_SLOTS, ff_part, model_width), jnp.bfloat16),
@@ -429,11 +510,11 @@
         ],
         compiler_params=pltpu.CompilerParams(vmem_limit_bytes=EXPERT_VMEM),
         cost_estimate=pl.CostEstimate(
-            flops=6 * all_slots * (ff_dev // held) * model_width,
+            flops=6 * all_slots * ff_part * model_width,
             bytes_accessed=6 * ff_dev * model_width,
             transcendentals=0,
         ),
-    )(*in_hbm(gain), gate_up_weight, down_weight, *held_weights, *flat)
+    )(*in_hbm(gain), gate_up_weight, down_weight, *in_vmem(*held_weights), *blocks, *flat)
     return [sums[g * CORES : (g + 1) * CORES] for g in range(len(RETURNS))]
 
 
@@ -527,18 +608,30 @@
     own_core = [other_core(block)]
     by_z, own_x, own_core, held_a = lax.optimization_barrier((by_z, own_x, own_core, held_a))
     by_z[2] = shift_dp(by_z[1], 1)
+    held_count = max(1, down_weight.shape[0] // FF)
+    gain = norm_gain[None, :]
+
+    def whole(rows, cores):
+        return [block for pair in zip(rows, cores) for block in pair]
+
     chip_rows = {z: [by_z[z]] + [shift_x(by_z[z], s) for s in range(1, chips)] for z in (1, 3)}
-    held_b = filled(gate_up_weight, down_weight, 1, by_z[3])
-    by_z[2], chip_rows, held_b = lax.optimization_barrier((by_z[2], chip_rows, held_b))
-    chip_rows[0] = [block] + own_x
+    own_core += [other_core(value) for value in own_x]
+    held_b, rows_0 = filled_with_rows(
+        gate_up_weight, down_weight, 1, gain, whole([block] + own_x, own_core)
+    )
+    by_z[2], *_ = lax.optimization_barrier((by_z[2], *held_b))
+    chip_rows, held_b = lax.optimization_barrier((chip_rows, held_b))
     chip_rows[2] = [by_z[2]] + [shift_x(by_z[2], s) for s in range(1, chips)]
-    own_core += [other_core(value) for value in own_x]
-    blocks = [list(zip(chip_rows[0], own_core))]
-    blocks += [
-        [(value, other_core(value)) for value in chip_rows[z]] for z in range(1, node_count)
-    ]
+    nodes = {
+        z: whole(chip_rows[z], [other_core(value) for value in chip_rows[z]]) for z in (1, 3)
+    }
+    rows_1, rows_3 = node_rows(gain, [nodes[1], nodes[3]], held_count)
+    core_2 = [other_core(by_z[2])]
+    chip_rows[2], rows_1, core_2 = lax.optimization_barrier((chip_rows[2], rows_1, core_2))
+    core_2 += [other_core(value) for value in chip_rows[2][1:]]
     sums = expert_sums(
-        norm_gain[None, :], gate_up_weight, down_weight, [*held_a, *held_b], blocks
+        gain, gate_up_weight, down_weight, [*held_a, *held_b], whole(chip_rows[2], core_2),
+        [rows_0, rows_1, rows_3],
     )
 
     over = [other_core(send) for _, send in sums]

time: 83 us -> 85.4 us (1.029)
  Pallas kernels: 38.6 us -> 40.8 us
    pallas_call x2 -> x3, Pallas kernels: 7.62 us -> 9.06 us  [the longest x1 3.84 us: filled(): pl.pallas_call(functools.partial(page_fill_kernel, expert=expert), out_sh...]
    ppermute x6, waiting for transfers between devices: 8.68 us -> 7.6 us  [shift_dp(): lax.ppermute(value, 'dp', [(i, (i + shift) % count) for i in range(count)])]
  transfers between devices with their start and end apart: 24 -> 24, of which waited for: 13 -> 11; matrix products, arithmetic and copies ran while one was open for 1% -> 1% of each run, Pallas kernels for 9% -> 11%
where the time goes in v14:
time: 85.4 us; the launch traced here: 85.1 us
  Pallas kernels  40.8 us (48%)
  starting transfers between devices  24.3 us (28%)
  waiting for transfers between devices  17.9 us (21%)
  local copies, waits for them, and re-layouts  0.88 us (1%)
    pallas_call x1, Pallas kernels, expert_sums(): pl.pallas_call(functools.partial(expert_kernel, held=held, parts=parts, c...  30 us
    ppermute x6, starting transfers between devices, shift_dp(): lax.ppermute(value, 'dp', [(i, (i + shift) % count) for i in range(count)])  13.2 us
    ppermute x7, starting transfers between devices, shift_x(): lax.ppermute(value, 'mp', [(i, (i + CORES * shift) % count) for i in rang...  9.26 us
    ppermute x7, waiting for transfers between devices, shift_x(): lax.ppermute(value, 'mp', [(i, (i + CORES * shift) % count) for i in rang...  7.76 us
    ppermute x6, waiting for transfers between devices, shift_dp(): lax.ppermute(value, 'dp', [(i, (i + shift) % count) for i in range(count)])  7.6 us
    pallas_call x1, Pallas kernels, filled(): pl.pallas_call(functools.partial(page_fill_kernel, expert=expert), out_sh...  3.84 us
    pallas_call x1, Pallas kernels, filled_with_rows(): pl.pallas_call(functools.partial(fill_rows_kernel, expert=expert, blocks=...  3.82 us
    ppermute x11, waiting for transfers between devices, other_core(): return lax.ppermute(value, 'mp', [(i, i ^ 1) for i in range(count)])  2.57 us
  transfers between devices with their start and end apart: 24, of which 11 were waited for; matrix products, arithmetic and copies ran while one was open for 1% of the time, Pallas kernels for 11%

profile of v14, /device:TPU:0, one launch (start us, length us, event | category | flops | bytes accessed | tf_op | source)
XLA Modules:
  0.0 85.1 jit_solution(14574602311531708893)
XLA Ops:
  0.6 1.0 %shard_map.104.after_ref.refs_0_ = bf16[1,136,512]{2,1,0:T(8,128)(2,1)S(1)} custom-call(bf16[128,512]{1,0:T(8,128)(2,1)} %hidden_ref.3, s32[8,128]{1,0:T(8,128)} %bitcast.44, f32[8,128]{1,0:T(8,128)} %bitcast.45), custom_call_target="tpu_custom_call" | custom-call | tf_op jit(solution)/shard_map/pallas_call | solution.py:106
  1.6 3.1 %collective-permute-start = (bf16[1,136,512]{2,1,0:T(8,128)(2,1)S(1)}, bf16[1,136,512]{2,1,0:T(8,128)(2,1)S(1)}, u32[]{:S(2)}, u32[]{:S(2)}) collective-permute-start(bf16[1,136,512]{2,1,0:T(8,128)(2,1)S(1)} %shard_map.104.after_ref.refs_0_), channel_id=1, source_target_pairs={{0,4},{4,8},{8,12},{12,0},{1,5},{5,9},{9,13},{13,1},{2,6},{6,10},{... | collective-permute-start | bytes 417800 | tf_op jit(solution)/shard_map/ppermute | solution.py:61
  4.7 2.1 %collective-permute-start.1 = (bf16[1,136,512]{2,1,0:T(8,128)(2,1)S(1)}, bf16[1,136,512]{2,1,0:T(8,128)(2,1)S(1)}, u32[]{:S(2)}, u32[]{:S(2)}) collective-permute-start(bf16[1,136,512]{2,1,0:T(8,128)(2,1)S(1)} %shard_map.104.after_ref.refs_0_), channel_id=1, source_target_pairs={{0,12},{4,0},{8,4},{12,8},{1,13},{5,1},{9,5},{13,9},{2,14},{6,2},{... | collective-permute-start | bytes 417800 | tf_op jit(solution)/shard_map/ppermute | solution.py:61
  6.8 1.6 %collective-permute-start.2 = (bf16[1,136,512]{2,1,0:T(8,128)(2,1)S(1)}, bf16[1,136,512]{2,1,0:T(8,128)(2,1)S(1)}, u32[]{:S(2)}, u32[]{:S(2)}) collective-permute-start(bf16[1,136,512]{2,1,0:T(8,128)(2,1)S(1)} %shard_map.104.after_ref.refs_0_), channel_id=1, source_target_pairs={{0,2},{1,3},{2,0},{3,1},{4,6},{5,7},{6,4},{7,5},{8,10},{9,11},{10,... | collective-permute-start | bytes 417800 | tf_op jit(solution)/shard_map/ppermute | solution.py:66
  8.4 3.8 %shard_map.105 = (bf16[2,768,2048]{2,1,0:T(8,128)(2,1)S(1)}, bf16[768,2048]{1,0:T(8,128)(2,1)S(1)}, bf16[4,24,512]{2,1,0:T(8,128)(2,1)S(1)}) custom-call(bf16[2,6144,2048]{2,1,0:T(8,128)(2,1)} %gate_up_ref.5, bf16[6144,2048]{1,0:T(8,128)(2,1)} %down_ref.5, bf16[1,136,512]{2,1,0:T(8,128)(2,1)S(1)} %shard_map.104.after_ref.refs_0_, bf16[128,256]{1,0:T(8,128)(2,1)} %kv_ref.1, ...), custom_call_target="tpu_custom_call" | custom-call | bytes 9437184 | tf_op jit(solution)/shard_map/pallas_call | solution.py:343
  12.3 0.5 collective-permute-done.1.refs_4_
  12.9 1.5 %collective-permute-start.4 = (bf16[1,136,512]{2,1,0:T(8,128)(2,1)S(1)}, bf16[1,136,512]{2,1,0:T(8,128)(2,1)S(1)}, u32[]{:S(2)}, u32[]{:S(2)}) collective-permute-start(bf16[1,136,512]{2,1,0:T(8,128)(2,1)S(1)} %collective-permute-done.refs_0_), channel_id=1, source_target_pairs={{0,2},{1,3},{2,0},{3,1},{4,6},{5,7},{6,4},{7,5},{8,10},{9,11},{10,... | collective-permute-start | bytes 417800 | tf_op jit(solution)/shard_map/ppermute | solution.py:66
  14.4 0.5 collective-permute-start.5
  14.9 1.1 %collective-permute-start.7 = (bf16[1,136,512]{2,1,0:T(8,128)(2,1)S(1)}, bf16[1,136,512]{2,1,0:T(8,128)(2,1)S(1)}, u32[]{:S(2)}, u32[]{:S(2)}) collective-permute-start(bf16[1,136,512]{2,1,0:T(8,128)(2,1)S(1)} %collective-permute-done.refs_0_), channel_id=1, source_target_pairs={{0,4},{4,8},{8,12},{12,0},{1,5},{5,9},{9,13},{13,1},{2,6},{6,10},{... | collective-permute-start | bytes 417800 | tf_op jit(solution)/shard_map/ppermute | solution.py:61
  16.0 3.8 %shard_map.106 = (bf16[2,768,2048]{2,1,0:T(8,128)(2,1)S(1)}, bf16[768,2048]{1,0:T(8,128)(2,1)S(1)}, bf16[128,2048]{1,0:T(8,128)(2,1)S(1)}, bf16[128,128]{1,0:T(8,128)(2,1)S(1)}, f32[128,128]{1,0:T(8,128)S(1)}) custom-call(bf16[2,6144,2048]{2,1,0:T(8,128)(2,1)} %gate_up_ref.5, bf16[6144,2048]{1,0:T(8,128)(2,1)} %down_ref.5, f32[1,2048]{1,0:T(1,128)} %bitcast.41, ...), custom_call_target="tpu_custom_call" | custom-call | bytes 18874368 | tf_op jit(solution)/shard_map/pallas_call | solution.py:281
  19.9 2.0 %collective-permute-done.5.refs_6_ = bf16[1,136,512]{2,1,0:T(8,128)(2,1)S(1)} collective-permute-done((bf16[1,136,512]{2,1,0:T(8,128)(2,1)S(1)}, bf16[1,136,512]{2,1,0:T(8,128)(2,1)S(1)}, u32[]{:S(2)}, u32[]{:S(2)}) %collective-permute-start.5) | collective-permute-done | bytes 139296 | tf_op jit(solution)/shard_map/ppermute | solution.py:66
  21.9 0.5 collective-permute-start.11
  22.4 0.5 collective-permute-start.9
  23.2 1.5 %collective-permute-start.8 = (bf16[1,136,512]{2,1,0:T(8,128)(2,1)S(1)}, bf16[1,136,512]{2,1,0:T(8,128)(2,1)S(1)}, u32[]{:S(2)}, u32[]{:S(2)}) collective-permute-start(bf16[1,136,512]{2,1,0:T(8,128)(2,1)S(1)} %collective-permute-done.7.refs_4_), channel_id=1, source_target_pairs={{0,2},{1,3},{2,0},{3,1},{4,6},{5,7},{6,4},{7,5},{8,10},{9,11},{10,... | collective-permute-start | bytes 417800 | tf_op jit(solution)/shard_map/ppermute | solution.py:66
  24.7 1.4 %shard_map.107 = (bf16[128,2048]{1,0:T(8,128)(2,1)S(1)}, bf16[128,128]{1,0:T(8,128)(2,1)S(1)}, f32[128,128]{1,0:T(8,128)S(1)}, bf16[128,2048]{1,0:T(8,128)(2,1)S...) custom-call(f32[1,2048]{1,0:T(1,128)} %bitcast.42, bf16[1,136,512]{2,1,0:T(8,128)(2,1)S(1)} %collective-permute-done.refs_0_, ...), custom_call_target="tpu_custom_call" | custom-call | bytes 18874368 | tf_op jit(solution)/shard_map/pallas_call | solution.py:260
  26.2 0.8 copy-done
  27.0 2.0 %collective-permute-done.8.refs_6_ = bf16[1,136,512]{2,1,0:T(8,128)(2,1)S(1)} collective-permute-done((bf16[1,136,512]{2,1,0:T(8,128)(2,1)S(1)}, bf16[1,136,512]{2,1,0:T(8,128)(2,1)S(1)}, u32[]{:S(2)}, u32[]{:S(2)}) %collective-permute-start.8) | collective-permute-done | bytes 139296 | tf_op jit(solution)/shard_map/ppermute | solution.py:66
  29.0 1.4 %collective-permute-done.14.refs_7_ = bf16[1,136,512]{2,1,0:T(8,128)(2,1)S(1)} collective-permute-done((bf16[1,136,512]{2,1,0:T(8,128)(2,1)S(1)}, bf16[1,136,512]{2,1,0:T(8,128)(2,1)S(1)}, u32[]{:S(2)}, u32[]{:S(2)}) %collective-permute-start.14) | collective-permute-done | bytes 139296 | tf_op jit(solution)/shard_map/ppermute | solution.py:71
  30.4 30.0 %shard_map.108 = (bf16[2,1,128,512]{3,2,1,0:T(8,128)(2,1)S(1)}, bf16[2,1,128,512]{3,2,1,0:T(8,128)(2,1)S(1)}, bf16[2,2,128,512]{3,2,1,0:T(8,128)(2,1)S(1)}, bf16...) custom-call(f32[1,2048]{1,0:T(1,128)} %bitcast.43, ...), custom_call_target="tpu_custom_call" | custom-call | flops 4831838208 | bytes 75497472 | tf_op jit(solution)/shard_map/pallas_call | solution.py:489
  60.6 0.4 collective-permute-start.16
  61.1 0.9 %collective-permute-done.19 = bf16[2,1,128,512]{3,2,1,0:T(8,128)(2,1)S(1)} collective-permute-done((bf16[2,1,128,512]{3,2,1,0:T(8,128)(2,1)S(1)}, bf16[2,1,128,512]{3,2,1,0:T(8,128)(2,1)S(1)}, u32[]{:S(2)}, u32[]{:S(2)}) %collective-permute-start.19) | collective-permute-done | bytes 262176 | tf_op jit(solution)/shard_map/ppermute | solution.py:71
  62.1 1.6 %collective-permute-start.20 = (bf16[1,128,512]{2,1,0:T(8,128)(2,1)S(1)}, bf16[1,128,512]{2,1,0:T(8,128)(2,1)S(1)}, u32[]{:S(2)}, u32[]{:S(2)}) collective-permute-start(bf16[1,128,512]{2,1,0:T(8,128)(2,1)S(1)} %slice_bitcast_fusion.3), channel_id=1, source_target_pairs={{0,2},{1,3},{2,0},{3,1},{4,6},{5,7},{6,4},{7,5},{8,10},{9,11},{10,... | collective-permute-start | bytes 393224 | tf_op jit(solution)/shard_map/ppermute | solution.py:66
  63.9 1.0 %collective-permute-start.17 = (bf16[2,128,512]{2,1,0:T(8,128)(2,1)S(1)}, bf16[2,128,512]{2,1,0:T(8,128)(2,1)S(1)}, u32[]{:S(2)}, u32[]{:S(2)}) collective-permute-start(bf16[2,128,512]{2,1,0:T(8,128)(2,1)S(1)} %slice_bitcast_fusion.1), channel_id=1, source_target_pairs={{0,2},{1,3},{2,0},{3,1},{4,6},{5,7},{6,4},{7,5},{8,10},{9,11},{10,... | collective-permute-start | bytes 786440 | tf_op jit(solution)/shard_map/ppermute | solution.py:66
  64.9 3.5 %collective-permute-done.20 = bf16[1,128,512]{2,1,0:T(8,128)(2,1)S(1)} collective-permute-done((bf16[1,128,512]{2,1,0:T(8,128)(2,1)S(1)}, bf16[1,128,512]{2,1,0:T(8,128)(2,1)S(1)}, u32[]{:S(2)}, u32[]{:S(2)}) %collective-permute-start.20) | collective-permute-done | bytes 131104 | tf_op jit(solution)/shard_map/ppermute | solution.py:66
  68.5 2.5 %collective-permute-start.21 = (bf16[152,512]{1,0:T(8,128)(2,1)S(1)}, bf16[152,512]{1,0:T(8,128)(2,1)S(1)}, u32[]{:S(2)}, u32[]{:S(2)}) collective-permute-start(bf16[152,512]{1,0:T(8,128)(2,1)S(1)} %pad_maximum_fusion.1), channel_id=1, source_target_pairs={{0,12},{4,0},{8,4},{12,8},{1,13},{5,1},{9,5},{13,9},{2,14},{6,2},{... | collective-permute-start | bytes 466952 | tf_op jit(solution)/shard_map/ppermute | solution.py:61
  71.0 2.8 %collective-permute-done.21 = bf16[152,512]{1,0:T(8,128)(2,1)S(1)} collective-permute-done((bf16[152,512]{1,0:T(8,128)(2,1)S(1)}, bf16[152,512]{1,0:T(8,128)(2,1)S(1)}, u32[]{:S(2)}, u32[]{:S(2)}) %collective-permute-start.21) | collective-permute-done | bytes 155680 | tf_op jit(solution)/shard_map/ppermute | solution.py:61
  73.9 1.2 %collective-permute-start.23 = (bf16[152,512]{1,0:T(8,128)(2,1)S(1)}, bf16[152,512]{1,0:T(8,128)(2,1)S(1)}, u32[]{:S(2)}, u32[]{:S(2)}) collective-permute-start(bf16[152,512]{1,0:T(8,128)(2,1)S(1)} %pad_maximum_fusion.2), channel_id=1, source_target_pairs={{0,4},{4,8},{8,12},{12,0},{1,5},{5,9},{9,13},{13,1},{2,6},{6,10},{... | collective-permute-start | bytes 466952 | tf_op jit(solution)/shard_map/ppermute | solution.py:61
  75.1 1.5 %collective-permute-start.18 = (bf16[1,128,512]{2,1,0:T(8,128)(2,1)S(1)}, bf16[1,128,512]{2,1,0:T(8,128)(2,1)S(1)}, u32[]{:S(2)}, u32[]{:S(2)}) collective-permute-start(bf16[1,128,512]{2,1,0:T(8,128)(2,1)S(1)} %slice_bitcast_fusion.6), channel_id=1, source_target_pairs={{0,2},{1,3},{2,0},{3,1},{4,6},{5,7},{6,4},{7,5},{8,10},{9,11},{10,... | collective-permute-start | bytes 393224 | tf_op jit(solution)/shard_map/ppermute | solution.py:66
  76.7 3.2 %collective-permute-start.22 = (bf16[176,512]{1,0:T(8,128)(2,1)S(1)}, bf16[176,512]{1,0:T(8,128)(2,1)S(1)}, u32[]{:S(2)}, u32[]{:S(2)}) collective-permute-start(bf16[176,512]{1,0:T(8,128)(2,1)S(1)} %pad_maximum_fusion), channel_id=1, source_target_pairs={{0,12},{4,0},{8,4},{12,8},{1,13},{5,1},{9,5},{13,9},{2,14},{6,2},{... | collective-permute-start | bytes 540680 | tf_op jit(solution)/shard_map/ppermute | solution.py:61
  80.1 2.7 %collective-permute-done.23.up_ref = bf16[152,512]{1,0:T(8,128)(2,1)S(1)} collective-permute-done((bf16[152,512]{1,0:T(8,128)(2,1)S(1)}, bf16[152,512]{1,0:T(8,128)(2,1)S(1)}, u32[]{:S(2)}, u32[]{:S(2)}) %collective-permute-start.23) | collective-permute-done | bytes 155680 | tf_op jit(solution)/shard_map/ppermute | solution.py:61
  82.8 1.6 %collective-permute-done.22.down_ref = bf16[176,512]{1,0:T(8,128)(2,1)S(1)} collective-permute-done((bf16[176,512]{1,0:T(8,128)(2,1)S(1)}, bf16[176,512]{1,0:T(8,128)(2,1)S(1)}, u32[]{:S(2)}, u32[]{:S(2)}) %collective-permute-start.22) | collective-permute-done | bytes 180256 | tf_op jit(solution)/shard_map/ppermute | solution.py:61
  84.4 0.8 shard_map.109
  (42 shorter events, 1.6 us)
Async XLA Ops:
  1.6 10.7 %collective-permute-start = (bf16[1,136,512]{2,1,0:T(8,128)(2,1)S(1)}, bf16[1,136,512]{2,1,0:T(8,128)(2,1)S(1)}, u32[]{:S(2)}, u32[]{:S(2)}) collective-permute-start(bf16[1,136,512]{2,1,0:T(8,128)(2,1)S(1)} %shard_map.104.after_ref.refs_0_), channel_id=1, source_target_pairs={{0,4},{4,8},{8,12},{12,0},{1,5},{5,9},{9,13},{13,1},{2,6},{6,10},{... | collective-permute-start | bytes 417800 | tf_op jit(solution)/shard_map/ppermute | solution.py:61
  4.7 8.1 %collective-permute-start.1 = (bf16[1,136,512]{2,1,0:T(8,128)(2,1)S(1)}, bf16[1,136,512]{2,1,0:T(8,128)(2,1)S(1)}, u32[]{:S(2)}, u32[]{:S(2)}) collective-permute-start(bf16[1,136,512]{2,1,0:T(8,128)(2,1)S(1)} %shard_map.104.after_ref.refs_0_), channel_id=1, source_target_pairs={{0,12},{4,0},{8,4},{12,8},{1,13},{5,1},{9,5},{13,9},{2,14},{6,2},{... | collective-permute-start | bytes 417800 | tf_op jit(solution)/shard_map/ppermute | solution.py:61
  6.8 6.0 %collective-permute-start.2 = (bf16[1,136,512]{2,1,0:T(8,128)(2,1)S(1)}, bf16[1,136,512]{2,1,0:T(8,128)(2,1)S(1)}, u32[]{:S(2)}, u32[]{:S(2)}) collective-permute-start(bf16[1,136,512]{2,1,0:T(8,128)(2,1)S(1)} %shard_map.104.after_ref.refs_0_), channel_id=1, source_target_pairs={{0,2},{1,3},{2,0},{3,1},{4,6},{5,7},{6,4},{7,5},{8,10},{9,11},{10,... | collective-permute-start | bytes 417800 | tf_op jit(solution)/shard_map/ppermute | solution.py:66
  8.4 4.4 %collective-permute-start.3 = (bf16[1,136,512]{2,1,0:T(8,128)(2,1)S(1)}, bf16[1,136,512]{2,1,0:T(8,128)(2,1)S(1)}, u32[]{:S(2)}, u32[]{:S(2)}) collective-permute-start(bf16[1,136,512]{2,1,0:T(8,128)(2,1)S(1)} %shard_map.104.after_ref.refs_0_), channel_id=1, source_target_pairs={{0,1},{1,0},{2,3},{3,2},{4,5},{5,4},{6,7},{7,6},{8,9},{9,8},{10,11... | collective-permute-start | bytes 417800 | tf_op jit(solution)/shard_map/ppermute | solution.py:71
  12.8 3.2 %collective-permute-start.6 = (bf16[1,136,512]{2,1,0:T(8,128)(2,1)S(1)}, bf16[1,136,512]{2,1,0:T(8,128)(2,1)S(1)}, u32[]{:S(2)}, u32[]{:S(2)}) collective-permute-start(bf16[1,136,512]{2,1,0:T(8,128)(2,1)S(1)} %collective-permute-done.2.refs_2_), channel_id=1, source_target_pairs={{0,1},{1,0},{2,3},{3,2},{4,5},{5,4},{6,7},{7,6},{8,9},{9,8},{10,11... | collective-permute-start | bytes 417800 | tf_op jit(solution)/shard_map/ppermute | solution.py:71
  12.9 7.0 %collective-permute-start.4 = (bf16[1,136,512]{2,1,0:T(8,128)(2,1)S(1)}, bf16[1,136,512]{2,1,0:T(8,128)(2,1)S(1)}, u32[]{:S(2)}, u32[]{:S(2)}) collective-permute-start(bf16[1,136,512]{2,1,0:T(8,128)(2,1)S(1)} %collective-permute-done.refs_0_), channel_id=1, source_target_pairs={{0,2},{1,3},{2,0},{3,1},{4,6},{5,7},{6,4},{7,5},{8,10},{9,11},{10,... | collective-permute-start | bytes 417800 | tf_op jit(solution)/shard_map/ppermute | solution.py:66
  14.4 7.5 %collective-permute-start.5 = (bf16[1,136,512]{2,1,0:T(8,128)(2,1)S(1)}, bf16[1,136,512]{2,1,0:T(8,128)(2,1)S(1)}, u32[]{:S(2)}, u32[]{:S(2)}) collective-permute-start(bf16[1,136,512]{2,1,0:T(8,128)(2,1)S(1)} %collective-permute-done.1.refs_4_), channel_id=1, source_target_pairs={{0,2},{1,3},{2,0},{3,1},{4,6},{5,7},{6,4},{7,5},{8,10},{9,11},{10,... | collective-permute-start | bytes 417800 | tf_op jit(solution)/shard_map/ppermute | solution.py:66
  14.9 8.0 %collective-permute-start.7 = (bf16[1,136,512]{2,1,0:T(8,128)(2,1)S(1)}, bf16[1,136,512]{2,1,0:T(8,128)(2,1)S(1)}, u32[]{:S(2)}, u32[]{:S(2)}) collective-permute-start(bf16[1,136,512]{2,1,0:T(8,128)(2,1)S(1)} %collective-permute-done.refs_0_), channel_id=1, source_target_pairs={{0,4},{4,8},{8,12},{12,0},{1,5},{5,9},{9,13},{13,1},{2,6},{6,10},{... | collective-permute-start | bytes 417800 | tf_op jit(solution)/shard_map/ppermute | solution.py:61
  21.9 1.4 %collective-permute-start.10 = (bf16[1,136,512]{2,1,0:T(8,128)(2,1)S(1)}, bf16[1,136,512]{2,1,0:T(8,128)(2,1)S(1)}, u32[]{:S(2)}, u32[]{:S(2)}) collective-permute-start(bf16[1,136,512]{2,1,0:T(8,128)(2,1)S(1)} %collective-permute-done.4.refs_2_), channel_id=1, source_target_pairs={{0,1},{1,0},{2,3},{3,2},{4,5},{5,4},{6,7},{7,6},{8,9},{9,8},{10,11... | collective-permute-start | bytes 417800 | tf_op jit(solution)/shard_map/ppermute | solution.py:71
  21.9 2.9 %collective-permute-start.11 = (bf16[1,136,512]{2,1,0:T(8,128)(2,1)S(1)}, bf16[1,136,512]{2,1,0:T(8,128)(2,1)S(1)}, u32[]{:S(2)}, u32[]{:S(2)}) collective-permute-start(bf16[1,136,512]{2,1,0:T(8,128)(2,1)S(1)} %collective-permute-done.1.refs_4_), channel_id=1, source_target_pairs={{0,1},{1,0},{2,3},{3,2},{4,5},{5,4},{6,7},{7,6},{8,9},{9,8},{10,11... | collective-permute-start | bytes 417800 | tf_op jit(solution)/shard_map/ppermute | solution.py:71
  22.4 2.3 %collective-permute-start.12 = (bf16[1,136,512]{2,1,0:T(8,128)(2,1)S(1)}, bf16[1,136,512]{2,1,0:T(8,128)(2,1)S(1)}, u32[]{:S(2)}, u32[]{:S(2)}) collective-permute-start(bf16[1,136,512]{2,1,0:T(8,128)(2,1)S(1)} %collective-permute-done.5.refs_6_), channel_id=1, source_target_pairs={{0,1},{1,0},{2,3},{3,2},{4,5},{5,4},{6,7},{7,6},{8,9},{9,8},{10,11... | collective-permute-start | bytes 417800 | tf_op jit(solution)/shard_map/ppermute | solution.py:71
  22.4 2.3 %collective-permute-start.9 = (bf16[1,136,512]{2,1,0:T(8,128)(2,1)S(1)}, bf16[1,136,512]{2,1,0:T(8,128)(2,1)S(1)}, u32[]{:S(2)}, u32[]{:S(2)}) collective-permute-start(bf16[1,136,512]{2,1,0:T(8,128)(2,1)S(1)} %collective-permute-done.refs_0_), channel_id=1, source_target_pairs={{0,1},{1,0},{2,3},{3,2},{4,5},{5,4},{6,7},{7,6},{8,9},{9,8},{10,11... | collective-permute-start | bytes 417800 | tf_op jit(solution)/shard_map/ppermute | solution.py:71
  22.9 4.1 %collective-permute-start.13 = (bf16[1,136,512]{2,1,0:T(8,128)(2,1)S(1)}, bf16[1,136,512]{2,1,0:T(8,128)(2,1)S(1)}, u32[]{:S(2)}, u32[]{:S(2)}) collective-permute-start(bf16[1,136,512]{2,1,0:T(8,128)(2,1)S(1)} %collective-permute-done.7.refs_4_), channel_id=1, source_target_pairs={{0,1},{1,0},{2,3},{3,2},{4,5},{5,4},{6,7},{7,6},{8,9},{9,8},{10,11... | collective-permute-start | bytes 417800 | tf_op jit(solution)/shard_map/ppermute | solution.py:71
  23.2 5.8 %collective-permute-start.8 = (bf16[1,136,512]{2,1,0:T(8,128)(2,1)S(1)}, bf16[1,136,512]{2,1,0:T(8,128)(2,1)S(1)}, u32[]{:S(2)}, u32[]{:S(2)}) collective-permute-start(bf16[1,136,512]{2,1,0:T(8,128)(2,1)S(1)} %collective-permute-done.7.refs_4_), channel_id=1, source_target_pairs={{0,2},{1,3},{2,0},{3,1},{4,6},{5,7},{6,4},{7,5},{8,10},{9,11},{10,... | collective-permute-start | bytes 417800 | tf_op jit(solution)/shard_map/ppermute | solution.py:66
  26.2 0.8 copy-start
  29.0 1.4 %collective-permute-start.14 = (bf16[1,136,512]{2,1,0:T(8,128)(2,1)S(1)}, bf16[1,136,512]{2,1,0:T(8,128)(2,1)S(1)}, u32[]{:S(2)}, u32[]{:S(2)}) collective-permute-start(bf16[1,136,512]{2,1,0:T(8,128)(2,1)S(1)} %collective-permute-done.8.refs_6_), channel_id=1, source_target_pairs={{0,1},{1,0},{2,3},{3,2},{4,5},{5,4},{6,7},{7,6},{8,9},{9,8},{10,11... | collective-permute-start | bytes 417800 | tf_op jit(solution)/shard_map/ppermute | solution.py:71
  60.4 24.0 %copy-start.1 = (bf16[128,512]{1,0:T(8,128)(2,1)S(1)}, bf16[128,512]{1,0:T(8,128)(2,1)}, u32[]{:S(2)}) copy-start(bf16[128,512]{1,0:T(8,128)(2,1)} %hidden_ref.3) | copy-start | bytes 393220
  60.4 1.6 %collective-permute-start.19 = (bf16[2,1,128,512]{3,2,1,0:T(8,128)(2,1)S(1)}, bf16[2,1,128,512]{3,2,1,0:T(8,128)(2,1)S(1)}, u32[]{:S(2)}, u32[]{:S(2)}) collective-permute-start(bf16[2,1,128,512]{3,2,1,0:T(8,128)(2,1)S(1)} %get-tuple-element.81), channel_id=1, source_target_pairs={{0,1},{1,0},{2,3},{3,2},{4,5},{5,4},{6,7},{7,6},{8,9},{9,8},{10,11... | collective-permute-start | bytes 786440 | tf_op jit(solution)/shard_map/ppermute | solution.py:71
  60.6 3.1 %collective-permute-start.16 = (bf16[2,2,128,512]{3,2,1,0:T(8,128)(2,1)S(1)}, bf16[2,2,128,512]{3,2,1,0:T(8,128)(2,1)S(1)}, u32[]{:S(2)}, u32[]{:S(2)}) collective-permute-start(bf16[2,2,128,512]{3,2,1,0:T(8,128)(2,1)S(1)} %get-tuple-element.78), channel_id=1, source_target_pairs={{0,1},{1,0},{2,3},{3,2},{4,5},{5,4},{6,7},{7,6},{8,9},{9,8},{10,11... | collective-permute-start | bytes 1572872 | tf_op jit(solution)/shard_map/ppermute | solution.py:71
  61.0 2.7 %collective-permute-start.15 = (bf16[2,1,128,512]{3,2,1,0:T(8,128)(2,1)S(1)}, bf16[2,1,128,512]{3,2,1,0:T(8,128)(2,1)S(1)}, u32[]{:S(2)}, u32[]{:S(2)}) collective-permute-start(bf16[2,1,128,512]{3,2,1,0:T(8,128)(2,1)S(1)} %get-tuple-element.76), channel_id=1, source_target_pairs={{0,1},{1,0},{2,3},{3,2},{4,5},{5,4},{6,7},{7,6},{8,9},{9,8},{10,11... | collective-permute-start | bytes 786440 | tf_op jit(solution)/shard_map/ppermute | solution.py:71
  62.1 6.4 %collective-permute-start.20 = (bf16[1,128,512]{2,1,0:T(8,128)(2,1)S(1)}, bf16[1,128,512]{2,1,0:T(8,128)(2,1)S(1)}, u32[]{:S(2)}, u32[]{:S(2)}) collective-permute-start(bf16[1,128,512]{2,1,0:T(8,128)(2,1)S(1)} %slice_bitcast_fusion.3), channel_id=1, source_target_pairs={{0,2},{1,3},{2,0},{3,1},{4,6},{5,7},{6,4},{7,5},{8,10},{9,11},{10,... | collective-permute-start | bytes 393224 | tf_op jit(solution)/shard_map/ppermute | solution.py:66
  63.9 9.9 %collective-permute-start.17 = (bf16[2,128,512]{2,1,0:T(8,128)(2,1)S(1)}, bf16[2,128,512]{2,1,0:T(8,128)(2,1)S(1)}, u32[]{:S(2)}, u32[]{:S(2)}) collective-permute-start(bf16[2,128,512]{2,1,0:T(8,128)(2,1)S(1)} %slice_bitcast_fusion.1), channel_id=1, source_target_pairs={{0,2},{1,3},{2,0},{3,1},{4,6},{5,7},{6,4},{7,5},{8,10},{9,11},{10,... | collective-permute-start | bytes 786440 | tf_op jit(solution)/shard_map/ppermute | solution.py:66
  68.5 5.3 %collective-permute-start.21 = (bf16[152,512]{1,0:T(8,128)(2,1)S(1)}, bf16[152,512]{1,0:T(8,128)(2,1)S(1)}, u32[]{:S(2)}, u32[]{:S(2)}) collective-permute-start(bf16[152,512]{1,0:T(8,128)(2,1)S(1)} %pad_maximum_fusion.1), channel_id=1, source_target_pairs={{0,12},{4,0},{8,4},{12,8},{1,13},{5,1},{9,5},{13,9},{2,14},{6,2},{... | collective-permute-start | bytes 466952 | tf_op jit(solution)/shard_map/ppermute | solution.py:61
  73.9 8.9 %collective-permute-start.23 = (bf16[152,512]{1,0:T(8,128)(2,1)S(1)}, bf16[152,512]{1,0:T(8,128)(2,1)S(1)}, u32[]{:S(2)}, u32[]{:S(2)}) collective-permute-start(bf16[152,512]{1,0:T(8,128)(2,1)S(1)} %pad_maximum_fusion.2), channel_id=1, source_target_pairs={{0,4},{4,8},{8,12},{12,0},{1,5},{5,9},{9,13},{13,1},{2,6},{6,10},{... | collective-permute-start | bytes 466952 | tf_op jit(solution)/shard_map/ppermute | solution.py:61
  75.1 5.0 %collective-permute-start.18 = (bf16[1,128,512]{2,1,0:T(8,128)(2,1)S(1)}, bf16[1,128,512]{2,1,0:T(8,128)(2,1)S(1)}, u32[]{:S(2)}, u32[]{:S(2)}) collective-permute-start(bf16[1,128,512]{2,1,0:T(8,128)(2,1)S(1)} %slice_bitcast_fusion.6), channel_id=1, source_target_pairs={{0,2},{1,3},{2,0},{3,1},{4,6},{5,7},{6,4},{7,5},{8,10},{9,11},{10,... | collective-permute-start | bytes 393224 | tf_op jit(solution)/shard_map/ppermute | solution.py:66
  76.7 7.7 %collective-permute-start.22 = (bf16[176,512]{1,0:T(8,128)(2,1)S(1)}, bf16[176,512]{1,0:T(8,128)(2,1)S(1)}, u32[]{:S(2)}, u32[]{:S(2)}) collective-permute-start(bf16[176,512]{1,0:T(8,128)(2,1)S(1)} %pad_maximum_fusion), channel_id=1, source_target_pairs={{0,12},{4,0},{8,4},{12,8},{1,13},{5,1},{9,5},{13,9},{2,14},{6,2},{... | collective-permute-start | bytes 540680 | tf_op jit(solution)/shard_map/ppermute | solution.py:61

commit v15 on v9

--- a/solution.py
+++ b/solution.py
@@ -19,7 +19,8 @@
 PAGE_FOLD = 24
 SMALL_VMEM = 4 * 1024 * 1024
 WEIGHT_SLOTS = 3
-EXPERT_VMEM = 31 * 1024 * 1024
+FILL_COST = 18 * 1024 * 1024
+EXPERT_VMEM = 8 * 1024 * 1024
 
 epsilon = 1e-06
 
@@ -90,6 +91,10 @@
 
 def in_hbm(*arrays):
     return [pltpu.with_memory_space_constraint(array, pltpu.HBM) for array in arrays]
+
+
+def in_vmem(*arrays):
+    return [pltpu.with_memory_space_constraint(array, pltpu.VMEM) for array in arrays]
 
 
 def packed(hidden_states, routes, gates):
@@ -132,18 +137,20 @@
             ).astype(jnp.bfloat16)
 
 
-def expert_copies(gate_up_ref, down_ref, h, gate_up_into, down_into, sems):
-    ff_part = down_into.shape[0]
+def expert_copies(gate_up_ref, down_ref, h, rings, slot, sems):
+    gate_ring, up_ring, down_ring = rings
+    ff_part = down_ring.shape[1]
     at = pl.ds(pl.multiple_of(h * ff_part, ff_part), ff_part)
     return (
-        pltpu.make_async_copy(gate_up_ref.at[0, at, :], gate_up_into.at[0], sems.at[0]),
-        pltpu.make_async_copy(gate_up_ref.at[1, at, :], gate_up_into.at[1], sems.at[1]),
-        pltpu.make_async_copy(down_ref.at[at, :], down_into, sems.at[2]),
-    )
-
-
-def fill_kernel(gate_up_ref, down_ref, after_ref, gate_up_out, down_out, sems, *, expert):
-    copies = expert_copies(gate_up_ref, down_ref, expert, gate_up_out, down_out, sems)
+        pltpu.make_async_copy(gate_up_ref.at[0, at, :], gate_ring.at[slot], sems.at[0]),
+        pltpu.make_async_copy(gate_up_ref.at[1, at, :], up_ring.at[slot], sems.at[1]),
+        pltpu.make_async_copy(down_ref.at[at, :], down_ring.at[slot], sems.at[2]),
+    )
+
+
+def fill_kernel(gate_up_ref, down_ref, after_ref, *refs, expert):
+    rings, sems = refs[3:6], refs[6]
+    copies = expert_copies(gate_up_ref, down_ref, expert, rings, expert, sems)
     for copy in copies:
         copy.start()
     for copy in copies:
@@ -152,15 +159,16 @@
 
 def page_fill_kernel(
     gate_up_ref, down_ref, after_ref, kv_ref, lengths_ref, owners_ref,
-    gate_up_out, down_out, pages_ref,
-    sems, kv_buf, lengths_buf, owners_buf, page_sems, *, expert,
+    gate_ring, up_ring, down_ring, pages_ref,
+    sems, kv_buf, lengths_buf, owners_buf, page_sems,
 ):
     small = (
         pltpu.make_async_copy(kv_ref, kv_buf, page_sems.at[0]),
         pltpu.make_async_copy(lengths_ref, lengths_buf, page_sems.at[1]),
         pltpu.make_async_copy(owners_ref, owners_buf, page_sems.at[2]),
     )
-    copies = expert_copies(gate_up_ref, down_ref, expert, gate_up_out, down_out, sems)
+    rings = (gate_ring, up_ring, down_ring)
+    copies = expert_copies(gate_up_ref, down_ref, 0, rings, 0, sems)
     for copy in small + copies:
         copy.start()
     for copy in small:
@@ -170,44 +178,49 @@
         copy.wait()
 
 
-def filled(gate_up_weight, down_weight, expert, after, paged=None):
-    width = down_weight.shape[1]
+def ring_shapes(down_weight):
     ff_part = min(FF, down_weight.shape[0])
+    return [pltpu.VMEM((WEIGHT_SLOTS, ff_part, down_weight.shape[1]), down_weight.dtype)] * 3
+
+
+def first_fill(gate_up_weight, down_weight, after, kv_rows, lengths, owners):
     hbm = pl.BlockSpec(memory_space=pltpu.HBM)
-    vmem = pl.BlockSpec(memory_space=pltpu.VMEM)
-    out_shape = [
-        pltpu.VMEM((2, ff_part, width), down_weight.dtype),
-        pltpu.VMEM((ff_part, width), down_weight.dtype),
-    ]
-    scratch = [pltpu.SemaphoreType.DMA((3,))]
-    operands = [gate_up_weight, down_weight, after]
-    kernel = fill_kernel
-    if paged is not None:
-        kv_rows, lengths, owners = paged
-        kernel = page_fill_kernel
-        operands += in_hbm(kv_rows, lengths, owners)
-        out_shape.append(
+    *rings, pages = pl.pallas_call(
+        page_fill_kernel,
+        out_shape=ring_shapes(down_weight)
+        + [
             jax.ShapeDtypeStruct(
                 (lengths.shape[0], PAGE_FOLD, 2 * kv_rows.shape[1]), jnp.bfloat16
             )
-        )
-        scratch += [
+        ],
+        in_specs=[hbm, hbm, pl.BlockSpec(memory_space=pl.ANY), hbm, hbm, hbm],
+        out_specs=[pl.BlockSpec(memory_space=pltpu.VMEM)] * 4,
+        scratch_shapes=[
+            pltpu.SemaphoreType.DMA((3,)),
             pltpu.VMEM(kv_rows.shape, kv_rows.dtype),
             pltpu.SMEM(lengths.shape, jnp.int32),
             pltpu.SMEM(owners.shape, jnp.int32),
             pltpu.SemaphoreType.DMA((3,)),
-        ]
+        ],
+        compiler_params=pltpu.CompilerParams(vmem_limit_bytes=SMALL_VMEM),
+        cost_estimate=pl.CostEstimate(flops=0, bytes_accessed=FILL_COST, transcendentals=0),
+    )(gate_up_weight, down_weight, after, *in_hbm(kv_rows, lengths, owners))
+    return rings, pages
+
+
+def next_fill(gate_up_weight, down_weight, expert, after, rings):
+    hbm = pl.BlockSpec(memory_space=pltpu.HBM)
+    vmem = pl.BlockSpec(memory_space=pltpu.VMEM)
     return pl.pallas_call(
-        functools.partial(kernel, expert=expert),
-        out_shape=out_shape,
-        in_specs=[hbm, hbm, pl.BlockSpec(memory_space=pl.ANY)] + [hbm] * (len(operands) - 3),
-        out_specs=[vmem] * len(out_shape),
-        scratch_shapes=scratch,
+        functools.partial(fill_kernel, expert=expert),
+        out_shape=ring_shapes(down_weight),
+        in_specs=[hbm, hbm, pl.BlockSpec(memory_space=pl.ANY)] + [vmem] * 3,
+        out_specs=[vmem] * 3,
+        input_output_aliases={3: 0, 4: 1, 5: 2},
+        scratch_shapes=[pltpu.SemaphoreType.DMA((3,))],
         compiler_params=pltpu.CompilerParams(vmem_limit_bytes=SMALL_VMEM),
-        cost_estimate=pl.CostEstimate(
-            flops=0, bytes_accessed=6 * ff_part * width, transcendentals=0
-        ),
-    )(*operands)
+        cost_estimate=pl.CostEstimate(flops=0, bytes_accessed=FILL_COST, transcendentals=0),
+    )(gate_up_weight, down_weight, after, *in_vmem(*rings))
 
 
 def final_kernel(hidden_ref, own_ref, down_ref, up_ref, pages_ref, mixed_ref, cache_ref):
@@ -250,27 +263,25 @@
 def expert_kernel(
     gain_ref, gate_up_ref, down_ref, *refs, held, parts, chips, fills,
 ):
-    held_refs, refs = refs[: 2 * fills], refs[2 * fills :]
-    block_refs, out_refs = refs[: parts * chips * CORES], refs[parts * chips * CORES :]
+    block_refs, out_refs = refs[3 : 3 + parts * chips * CORES], refs[3 + parts * chips * CORES :]
     out_refs, scratch = out_refs[: len(RETURNS) * CORES], out_refs[len(RETURNS) * CORES :]
+    rings, scratch = scratch[:3], scratch[3:]
     (
-        pick_ref, picked_ref, slot_gate_ref, gain_buf, gu_buf, down_buf, sems, gain_sem,
+        pick_ref, picked_ref, slot_gate_ref, gain_buf, sems, gain_sem,
     ) = scratch
     _, block_rows, width = block_refs[0].shape
     tok_node = block_rows - TOPK
     model_width = picked_ref.shape[1]
     served_ref = picked_ref
-    slots = down_buf.shape[0]
+    slots = rings[0].shape[0]
 
     def fetch(h, slot):
-        return expert_copies(
-            gate_up_ref, down_ref, h, gu_buf.at[slot], down_buf.at[slot], sems.at[slot]
-        )
+        return expert_copies(gate_up_ref, down_ref, h, rings, slot, sems.at[slot])
 
     gain_copy = pltpu.make_async_copy(gain_ref, gain_buf, gain_sem)
     gain_copy.start()
-    for slot in range(min(slots, held - fills)):
-        for copy in fetch(fills + slot, slot):
+    for h in range(fills, min(slots, held)):
+        for copy in fetch(h, h):
             copy.start()
 
     column = lax.axis_index("mp")
@@ -340,19 +351,16 @@
                 ).astype(jnp.bfloat16)
 
     def rows_of(h):
-        first = [(z * held + h) * CAP for z in range(parts)]
-        if not isinstance(h, int):
-            first = [pl.multiple_of(at, CAP) for at in first]
-        return [pl.ds(at, CAP) for at in first]
-
-    def one_expert(h, gate_up, down):
+        return [pl.ds(pl.multiple_of((z * held + h) * CAP, CAP), CAP) for z in range(parts)]
+
+    def one_expert(h, gate_rows, up_rows, down):
         picked = jnp.concatenate([picked_ref[at, :] for at in rows_of(h)], axis=0)
         along = (((1,), (1,)), ((), ()))
         gate_part = lax.dot_general(
-            gate_up[0], picked, along, preferred_element_type=jnp.float32
+            gate_rows[...], picked, along, preferred_element_type=jnp.float32
         )
         up_part = lax.dot_general(
-            gate_up[1], picked, along, preferred_element_type=jnp.float32
+            up_rows[...], picked, along, preferred_element_type=jnp.float32
         )
         activated = (jax.nn.silu(gate_part) * up_part).astype(jnp.bfloat16)
         served = lax.dot_general(
@@ -363,14 +371,15 @@
                 served[z * CAP : (z + 1) * CAP, :] * slot_gate_ref[at, :]
             ).astype(jnp.bfloat16)
 
-    for h in range(fills):
-        one_expert(h, held_refs[2 * h], held_refs[2 * h + 1])
-
-    def streamed(h, carry):
-        slot = lax.rem(h - fills, slots)
-        for copy in fetch(h, slot):
-            copy.wait()
-        one_expert(h, gu_buf.at[slot], down_buf.at[slot])
+    def each_expert(h, carry):
+        slot = lax.rem(h, slots)
+
+        @pl.when(h >= fills)
+        def _():
+            for copy in fetch(h, slot):
+                copy.wait()
+
+        one_expert(h, *[ring.at[slot] for ring in rings])
 
         @pl.when(h + slots < held)
         def _():
@@ -379,7 +388,7 @@
 
         return carry
 
-    lax.fori_loop(fills, held, streamed, 0)
+    lax.fori_loop(0, held, each_expert, 0)
 
     for group, members in enumerate(RETURNS):
         for i, z in enumerate(members):
@@ -392,7 +401,7 @@
                     ).astype(jnp.bfloat16)
 
 
-def expert_sums(gain, gate_up_weight, down_weight, held_weights, blocks):
+def expert_sums(gain, gate_up_weight, down_weight, rings, fills, blocks):
     parts, chips = len(blocks), len(blocks[0])
     _, block_rows, width = blocks[0][0][0].shape
     tok_node = block_rows - TOPK
@@ -404,26 +413,26 @@
     all_slots = held * capacity
     vmem = pl.BlockSpec(memory_space=pltpu.VMEM)
     hbm = pl.BlockSpec(memory_space=pltpu.HBM)
-    held_weights = [pltpu.with_memory_space_constraint(w, pltpu.VMEM) for w in held_weights]
+    outs = len(RETURNS) * CORES
     flat = [blocks[z][x][c] for z in range(parts) for x in range(chips) for c in range(CORES)]
     sums = pl.pallas_call(
         functools.partial(
-            expert_kernel, held=held, parts=parts, chips=chips, fills=len(held_weights) // 2
+            expert_kernel, held=held, parts=parts, chips=chips, fills=fills
         ),
         out_shape=[
             jax.ShapeDtypeStruct((chips, len(members), tok_node, width), jnp.bfloat16)
             for members in RETURNS
             for _ in range(CORES)
-        ],
-        in_specs=[hbm] * 3 + [vmem] * (len(held_weights) + len(flat)),
-        out_specs=[vmem] * (len(RETURNS) * CORES),
+        ]
+        + ring_shapes(down_weight),
+        in_specs=[hbm] * 3 + [vmem] * (3 + len(flat)),
+        out_specs=[vmem] * (outs + 3),
+        input_output_aliases={3: outs, 4: outs + 1, 5: outs + 2},
         scratch_shapes=[
             pltpu.VMEM((parts, held * CAP, tok_node), jnp.bfloat16),
             pltpu.VMEM((all_slots, model_width), jnp.bfloat16),
             pltpu.VMEM((all_slots, 1), jnp.float32),
             pltpu.VMEM((1, model_width), jnp.float32),
-            pltpu.VMEM((WEIGHT_SLOTS, 2, ff_part, model_width), jnp.bfloat16),
-            pltpu.VMEM((WEIGHT_SLOTS, ff_part, model_width), jnp.bfloat16),
             pltpu.SemaphoreType.DMA((WEIGHT_SLOTS, 3)),
             pltpu.SemaphoreType.DMA(()),
         ],
@@ -433,7 +442,7 @@
             bytes_accessed=6 * ff_dev * model_width,
             transcendentals=0,
         ),
-    )(*in_hbm(gain), gate_up_weight, down_weight, *held_weights, *flat)
+    )(*in_hbm(gain), gate_up_weight, down_weight, *in_vmem(*rings), *flat)
     return [sums[g * CORES : (g + 1) * CORES] for g in range(len(RETURNS))]
 
 
@@ -523,13 +532,14 @@
 
     by_z = {0: block, 1: shift_dp(block, 1), 3: shift_dp(block, -1)}
     own_x = [shift_x(block, s) for s in range(1, chips)]
-    *held_a, pages = filled(gate_up_weight, down_weight, 0, block, (kv_rows, lengths, owners))
+    rings, pages = first_fill(gate_up_weight, down_weight, block, kv_rows, lengths, owners)
     own_core = [other_core(block)]
-    by_z, own_x, own_core, held_a = lax.optimization_barrier((by_z, own_x, own_core, held_a))
+    by_z, own_x, own_core, rings = lax.optimization_barrier((by_z, own_x, own_core, rings))
     by_z[2] = shift_dp(by_z[1], 1)
     chip_rows = {z: [by_z[z]] + [shift_x(by_z[z], s) for s in range(1, chips)] for z in (1, 3)}
-    held_b = filled(gate_up_weight, down_weight, 1, by_z[3])
-    by_z[2], chip_rows, held_b = lax.optimization_barrier((by_z[2], chip_rows, held_b))
+    rings = next_fill(gate_up_weight, down_weight, 1, by_z[3], rings)
+    by_z[2], *_ = lax.optimization_barrier((by_z[2], *rings))
+    chip_rows, rings = lax.optimization_barrier((chip_rows, rings))
     chip_rows[0] = [block] + own_x
     chip_rows[2] = [by_z[2]] + [shift_x(by_z[2], s) for s in range(1, chips)]
     own_core += [other_core(value) for value in own_x]
@@ -538,7 +548,7 @@
         [(value, other_core(value)) for value in chip_rows[z]] for z in range(1, node_count)
     ]
     sums = expert_sums(
-        norm_gain[None, :], gate_up_weight, down_weight, [*held_a, *held_b], blocks
+        norm_gain[None, :], gate_up_weight, down_weight, rings, 2, blocks
     )
 
     over = [other_core(send) for _, send in sums]

time: 83 us -> 77 us (0.928)
  Pallas kernels: 38.6 us -> 33.6 us
  waiting for transfers between devices: 18.7 us -> 17.5 us
    pallas_call x1, Pallas kernels: 29.2 us -> 24.3 us  [expert_sums(): pl.pallas_call(functools.partial(expert_kernel, held=held, parts=parts, c...]
  transfers between devices with their start and end apart: 24 -> 24, of which waited for: 13 -> 11; matrix products, arithmetic and copies ran while one was open for 1% -> 1% of each run, Pallas kernels for 9% -> 10%
where the time goes in v15:
time: 77 us; the launch traced here: 76.8 us
  Pallas kernels  33.6 us (44%)
  starting transfers between devices  24.4 us (32%)
  waiting for transfers between devices  17.5 us (23%)
  between operations  0.79 us (1%)
    pallas_call x1, Pallas kernels, expert_sums(): pl.pallas_call(functools.partial(expert_kernel, held=held, parts=parts, c...  24.3 us
    ppermute x6, starting transfers between devices, shift_dp(): lax.ppermute(value, 'dp', [(i, (i + shift) % count) for i in range(count)])  13.5 us
    ppermute x7, starting transfers between devices, shift_x(): lax.ppermute(value, 'mp', [(i, (i + CORES * shift) % count) for i in rang...  8.78 us
    ppermute x6, waiting for transfers between devices, shift_dp(): lax.ppermute(value, 'dp', [(i, (i + shift) % count) for i in range(count)])  8.29 us
    ppermute x7, waiting for transfers between devices, shift_x(): lax.ppermute(value, 'mp', [(i, (i + CORES * shift) % count) for i in rang...  7.43 us
    pallas_call x1, Pallas kernels, first_fill(): pl.pallas_call(page_fill_kernel, out_shape=ring_shapes(down_weight) + [ja...  3.84 us
    pallas_call x1, Pallas kernels, next_fill(): pl.pallas_call(functools.partial(fill_kernel, expert=expert), out_shape=r...  3.78 us
    ppermute x11, starting transfers between devices, other_core(): return lax.ppermute(value, 'mp', [(i, i ^ 1) for i in range(count)])  2.12 us
  transfers between devices with their start and end apart: 24, of which 11 were waited for; matrix products, arithmetic and copies ran while one was open for 1% of the time, Pallas kernels for 10%

profile of v15, /device:TPU:0, one launch (start us, length us, event | category | flops | bytes accessed | tf_op | source)
XLA Modules:
  0.0 76.8 jit_solution(3431285623979117726)
XLA Ops:
  0.6 1.0 %shard_map.104.after_ref.refs_3_ = bf16[1,136,512]{2,1,0:T(8,128)(2,1)S(1)} custom-call(bf16[128,512]{1,0:T(8,128)(2,1)} %hidden_ref.3, s32[8,128]{1,0:T(8,128)} %bitcast.42, f32[8,128]{1,0:T(8,128)} %bitcast.43), custom_call_target="tpu_custom_call" | custom-call | tf_op jit(solution)/shard_map/pallas_call | solution.py:103
  1.6 3.1 %collective-permute-start = (bf16[1,136,512]{2,1,0:T(8,128)(2,1)S(1)}, bf16[1,136,512]{2,1,0:T(8,128)(2,1)S(1)}, u32[]{:S(2)}, u32[]{:S(2)}) collective-permute-start(bf16[1,136,512]{2,1,0:T(8,128)(2,1)S(1)} %shard_map.104.after_ref.refs_3_), channel_id=1, source_target_pairs={{0,4},{4,8},{8,12},{12,0},{1,5},{5,9},{9,13},{13,1},{2,6},{6,10},{... | collective-permute-start | bytes 417800 | tf_op jit(solution)/shard_map/ppermute | solution.py:58
  4.7 2.1 %collective-permute-start.1 = (bf16[1,136,512]{2,1,0:T(8,128)(2,1)S(1)}, bf16[1,136,512]{2,1,0:T(8,128)(2,1)S(1)}, u32[]{:S(2)}, u32[]{:S(2)}) collective-permute-start(bf16[1,136,512]{2,1,0:T(8,128)(2,1)S(1)} %shard_map.104.after_ref.refs_3_), channel_id=1, source_target_pairs={{0,12},{4,0},{8,4},{12,8},{1,13},{5,1},{9,5},{13,9},{2,14},{6,2},{... | collective-permute-start | bytes 417800 | tf_op jit(solution)/shard_map/ppermute | solution.py:58
  6.8 1.6 %collective-permute-start.2 = (bf16[1,136,512]{2,1,0:T(8,128)(2,1)S(1)}, bf16[1,136,512]{2,1,0:T(8,128)(2,1)S(1)}, u32[]{:S(2)}, u32[]{:S(2)}) collective-permute-start(bf16[1,136,512]{2,1,0:T(8,128)(2,1)S(1)} %shard_map.104.after_ref.refs_3_), channel_id=1, source_target_pairs={{0,2},{1,3},{2,0},{3,1},{4,6},{5,7},{6,4},{7,5},{8,10},{9,11},{10,... | collective-permute-start | bytes 417800 | tf_op jit(solution)/shard_map/ppermute | solution.py:63
  8.4 3.8 %shard_map.105 = (bf16[3,768,2048]{2,1,0:T(8,128)(2,1)S(1)}, bf16[3,768,2048]{2,1,0:T(8,128)(2,1)S(1)}, bf16[3,768,2048]{2,1,0:T(8,128)(2,1)S(1)}, bf16[4,24,512]{2,1,0:T(8,128)(2,1)S(1)}) custom-call(bf16[2,6144,2048]{2,1,0:T(8,128)(2,1)} %gate_up_ref.5, bf16[6144,2048]{1,0:T(8,128)(2,1)} %down_ref.5, ...), custom_call_target="tpu_custom_call" | custom-call | bytes 18874368 | tf_op jit(solution)/shard_map/pallas_call | solution.py:188
  12.3 0.5 collective-permute-done.1.after_ref.refs_15_
  12.8 1.1 %collective-permute-start.9 = (bf16[1,136,512]{2,1,0:T(8,128)(2,1)S(1)}, bf16[1,136,512]{2,1,0:T(8,128)(2,1)S(1)}, u32[]{:S(2)}, u32[]{:S(2)}) collective-permute-start(bf16[1,136,512]{2,1,0:T(8,128)(2,1)S(1)} %collective-permute-done.refs_7_), channel_id=1, source_target_pairs={{0,4},{4,8},{8,12},{12,0},{1,5},{5,9},{9,13},{13,1},{2,6},{6,10},{... | collective-permute-start | bytes 417800 | tf_op jit(solution)/shard_map/ppermute | solution.py:58
  13.9 1.5 %collective-permute-start.4 = (bf16[1,136,512]{2,1,0:T(8,128)(2,1)S(1)}, bf16[1,136,512]{2,1,0:T(8,128)(2,1)S(1)}, u32[]{:S(2)}, u32[]{:S(2)}) collective-permute-start(bf16[1,136,512]{2,1,0:T(8,128)(2,1)S(1)} %collective-permute-done.refs_7_), channel_id=1, source_target_pairs={{0,2},{1,3},{2,0},{3,1},{4,6},{5,7},{6,4},{7,5},{8,10},{9,11},{10,... | collective-permute-start | bytes 417800 | tf_op jit(solution)/shard_map/ppermute | solution.py:63
  15.4 0.5 collective-permute-start.5
  16.0 3.8 %shard_map.106 = (bf16[3,768,2048]{2,1,0:T(8,128)(2,1)S(1)}, bf16[3,768,2048]{2,1,0:T(8,128)(2,1)S(1)}, bf16[3,768,2048]{2,1,0:T(8,128)(2,1)S(1)}) custom-call(bf16[2,6144,2048]{2,1,0:T(8,128)(2,1)} %gate_up_ref.5, bf16[6144,2048]{1,0:T(8,128)(2,1)} %down_ref.5, ...), custom_call_target="tpu_custom_call", output_to_operand_aliasing={{0}: (3, {}), {1}: (4, {}), {2}: (5, {})} | custom-call | bytes 18874368 | tf_op jit(solution)/shard_map/pallas_call | solution.py:214
  19.8 0.5 collective-permute-done.9.refs_11_
  20.2 1.1 %collective-permute-start.11 = (bf16[1,136,512]{2,1,0:T(8,128)(2,1)S(1)}, bf16[1,136,512]{2,1,0:T(8,128)(2,1)S(1)}, u32[]{:S(2)}, u32[]{:S(2)}) collective-permute-start(bf16[1,136,512]{2,1,0:T(8,128)(2,1)S(1)} %collective-permute-done.9.refs_11_), channel_id=1, source_target_pairs={{0,2},{1,3},{2,0},{3,1},{4,6},{5,7},{6,4},{7,5},{8,10},{9,11},{10,... | collective-permute-start | bytes 417800 | tf_op jit(solution)/shard_map/ppermute | solution.py:63
  21.5 0.7 collective-permute-done.5.refs_17_
  22.2 0.5 collective-permute-start.14
  22.8 3.2 %collective-permute-done.11.refs_13_ = bf16[1,136,512]{2,1,0:T(8,128)(2,1)S(1)} collective-permute-done((bf16[1,136,512]{2,1,0:T(8,128)(2,1)S(1)}, bf16[1,136,512]{2,1,0:T(8,128)(2,1)S(1)}, u32[]{:S(2)}, u32[]{:S(2)}) %collective-permute-start.11) | collective-permute-done | bytes 139296 | tf_op jit(solution)/shard_map/ppermute | solution.py:63
  25.9 0.5 collective-permute-start.12
  26.4 0.8 %collective-permute-done.8.refs_10_ = bf16[1,136,512]{2,1,0:T(8,128)(2,1)S(1)} collective-permute-done((bf16[1,136,512]{2,1,0:T(8,128)(2,1)S(1)}, bf16[1,136,512]{2,1,0:T(8,128)(2,1)S(1)}, u32[]{:S(2)}, u32[]{:S(2)}) %collective-permute-start.8) | collective-permute-done | bytes 139296 | tf_op jit(solution)/shard_map/ppermute | solution.py:68
  27.5 24.3 %shard_map.107 = (bf16[2,1,128,512]{3,2,1,0:T(8,128)(2,1)S(1)}, bf16[2,1,128,512]{3,2,1,0:T(8,128)(2,1)S(1)}, bf16[2,2,128,512]{3,2,1,0:T(8,128)(2,1)S(1)}, bf16...) custom-call(f32[1,2048]{1,0:T(1,128)} %bitcast.41, ...), custom_call_target="tpu_custom_call", output_to_operand_aliasing={{6}: (3, {}), {7}: (4, {}), {8}: (5, {})} | custom-call | flops 4831838208 | bytes 75497472 | tf_op jit(solution)/shard_map/pallas_call | solution.py:418
  51.8 0.4 collective-permute-start.19
  52.4 0.3 collective-permute-start.15
  52.7 0.7 collective-permute-done.19
  53.5 1.5 %collective-permute-start.20 = (bf16[1,128,512]{2,1,0:T(8,128)(2,1)S(1)}, bf16[1,128,512]{2,1,0:T(8,128)(2,1)S(1)}, u32[]{:S(2)}, u32[]{:S(2)}) collective-permute-start(bf16[1,128,512]{2,1,0:T(8,128)(2,1)S(1)} %slice_bitcast_fusion.3), channel_id=1, source_target_pairs={{0,2},{1,3},{2,0},{3,1},{4,6},{5,7},{6,4},{7,5},{8,10},{9,11},{10,... | collective-permute-start | bytes 393224 | tf_op jit(solution)/shard_map/ppermute | solution.py:63
  55.3 1.0 %collective-permute-start.17 = (bf16[2,128,512]{2,1,0:T(8,128)(2,1)S(1)}, bf16[2,128,512]{2,1,0:T(8,128)(2,1)S(1)}, u32[]{:S(2)}, u32[]{:S(2)}) collective-permute-start(bf16[2,128,512]{2,1,0:T(8,128)(2,1)S(1)} %slice_bitcast_fusion.1), channel_id=1, source_target_pairs={{0,2},{1,3},{2,0},{3,1},{4,6},{5,7},{6,4},{7,5},{8,10},{9,11},{10,... | collective-permute-start | bytes 786440 | tf_op jit(solution)/shard_map/ppermute | solution.py:63
  56.3 3.6 %collective-permute-done.20 = bf16[1,128,512]{2,1,0:T(8,128)(2,1)S(1)} collective-permute-done((bf16[1,128,512]{2,1,0:T(8,128)(2,1)S(1)}, bf16[1,128,512]{2,1,0:T(8,128)(2,1)S(1)}, u32[]{:S(2)}, u32[]{:S(2)}) %collective-permute-start.20) | collective-permute-done | bytes 131104 | tf_op jit(solution)/shard_map/ppermute | solution.py:63
  59.9 2.7 %collective-permute-start.21 = (bf16[152,512]{1,0:T(8,128)(2,1)S(1)}, bf16[152,512]{1,0:T(8,128)(2,1)S(1)}, u32[]{:S(2)}, u32[]{:S(2)}) collective-permute-start(bf16[152,512]{1,0:T(8,128)(2,1)S(1)} %pad_maximum_fusion.1), channel_id=1, source_target_pairs={{0,12},{4,0},{8,4},{12,8},{1,13},{5,1},{9,5},{13,9},{2,14},{6,2},{... | collective-permute-start | bytes 466952 | tf_op jit(solution)/shard_map/ppermute | solution.py:58
  62.7 2.7 %collective-permute-done.21 = bf16[152,512]{1,0:T(8,128)(2,1)S(1)} collective-permute-done((bf16[152,512]{1,0:T(8,128)(2,1)S(1)}, bf16[152,512]{1,0:T(8,128)(2,1)S(1)}, u32[]{:S(2)}, u32[]{:S(2)}) %collective-permute-start.21) | collective-permute-done | bytes 155680 | tf_op jit(solution)/shard_map/ppermute | solution.py:58
  65.5 0.6 collective-permute-start.23
  66.1 1.5 %collective-permute-start.18 = (bf16[1,128,512]{2,1,0:T(8,128)(2,1)S(1)}, bf16[1,128,512]{2,1,0:T(8,128)(2,1)S(1)}, u32[]{:S(2)}, u32[]{:S(2)}) collective-permute-start(bf16[1,128,512]{2,1,0:T(8,128)(2,1)S(1)} %slice_bitcast_fusion.6), channel_id=1, source_target_pairs={{0,2},{1,3},{2,0},{3,1},{4,6},{5,7},{6,4},{7,5},{8,10},{9,11},{10,... | collective-permute-start | bytes 393224 | tf_op jit(solution)/shard_map/ppermute | solution.py:63
  67.7 3.8 %collective-permute-start.22 = (bf16[176,512]{1,0:T(8,128)(2,1)S(1)}, bf16[176,512]{1,0:T(8,128)(2,1)S(1)}, u32[]{:S(2)}, u32[]{:S(2)}) collective-permute-start(bf16[176,512]{1,0:T(8,128)(2,1)S(1)} %pad_maximum_fusion), channel_id=1, source_target_pairs={{0,12},{4,0},{8,4},{12,8},{1,13},{5,1},{9,5},{13,9},{2,14},{6,2},{... | collective-permute-start | bytes 540680 | tf_op jit(solution)/shard_map/ppermute | solution.py:58
  71.6 3.2 %collective-permute-done.23.up_ref = bf16[152,512]{1,0:T(8,128)(2,1)S(1)} collective-permute-done((bf16[152,512]{1,0:T(8,128)(2,1)S(1)}, bf16[152,512]{1,0:T(8,128)(2,1)S(1)}, u32[]{:S(2)}, u32[]{:S(2)}) %collective-permute-start.23) | collective-permute-done | bytes 155680 | tf_op jit(solution)/shard_map/ppermute | solution.py:58
  74.7 1.3 %collective-permute-done.22.down_ref = bf16[176,512]{1,0:T(8,128)(2,1)S(1)} collective-permute-done((bf16[176,512]{1,0:T(8,128)(2,1)S(1)}, bf16[176,512]{1,0:T(8,128)(2,1)S(1)}, u32[]{:S(2)}, u32[]{:S(2)}) %collective-permute-start.22) | collective-permute-done | bytes 180256 | tf_op jit(solution)/shard_map/ppermute | solution.py:58
  76.1 0.8 shard_map.108
  (39 shorter events, 1.2 us)
Async XLA Ops:
  1.6 10.7 %collective-permute-start = (bf16[1,136,512]{2,1,0:T(8,128)(2,1)S(1)}, bf16[1,136,512]{2,1,0:T(8,128)(2,1)S(1)}, u32[]{:S(2)}, u32[]{:S(2)}) collective-permute-start(bf16[1,136,512]{2,1,0:T(8,128)(2,1)S(1)} %shard_map.104.after_ref.refs_3_), channel_id=1, source_target_pairs={{0,4},{4,8},{8,12},{12,0},{1,5},{5,9},{9,13},{13,1},{2,6},{6,10},{... | collective-permute-start | bytes 417800 | tf_op jit(solution)/shard_map/ppermute | solution.py:58
  4.7 8.1 %collective-permute-start.1 = (bf16[1,136,512]{2,1,0:T(8,128)(2,1)S(1)}, bf16[1,136,512]{2,1,0:T(8,128)(2,1)S(1)}, u32[]{:S(2)}, u32[]{:S(2)}) collective-permute-start(bf16[1,136,512]{2,1,0:T(8,128)(2,1)S(1)} %shard_map.104.after_ref.refs_3_), channel_id=1, source_target_pairs={{0,12},{4,0},{8,4},{12,8},{1,13},{5,1},{9,5},{13,9},{2,14},{6,2},{... | collective-permute-start | bytes 417800 | tf_op jit(solution)/shard_map/ppermute | solution.py:58
  6.8 6.0 %collective-permute-start.2 = (bf16[1,136,512]{2,1,0:T(8,128)(2,1)S(1)}, bf16[1,136,512]{2,1,0:T(8,128)(2,1)S(1)}, u32[]{:S(2)}, u32[]{:S(2)}) collective-permute-start(bf16[1,136,512]{2,1,0:T(8,128)(2,1)S(1)} %shard_map.104.after_ref.refs_3_), channel_id=1, source_target_pairs={{0,2},{1,3},{2,0},{3,1},{4,6},{5,7},{6,4},{7,5},{8,10},{9,11},{10,... | collective-permute-start | bytes 417800 | tf_op jit(solution)/shard_map/ppermute | solution.py:63
  8.4 4.4 %collective-permute-start.3 = (bf16[1,136,512]{2,1,0:T(8,128)(2,1)S(1)}, bf16[1,136,512]{2,1,0:T(8,128)(2,1)S(1)}, u32[]{:S(2)}, u32[]{:S(2)}) collective-permute-start(bf16[1,136,512]{2,1,0:T(8,128)(2,1)S(1)} %shard_map.104.after_ref.refs_3_), channel_id=1, source_target_pairs={{0,1},{1,0},{2,3},{3,2},{4,5},{5,4},{6,7},{7,6},{8,9},{9,8},{10,11... | collective-permute-start | bytes 417800 | tf_op jit(solution)/shard_map/ppermute | solution.py:68
  12.8 7.4 %collective-permute-start.9 = (bf16[1,136,512]{2,1,0:T(8,128)(2,1)S(1)}, bf16[1,136,512]{2,1,0:T(8,128)(2,1)S(1)}, u32[]{:S(2)}, u32[]{:S(2)}) collective-permute-start(bf16[1,136,512]{2,1,0:T(8,128)(2,1)S(1)} %collective-permute-done.refs_7_), channel_id=1, source_target_pairs={{0,4},{4,8},{8,12},{12,0},{1,5},{5,9},{9,13},{13,1},{2,6},{6,10},{... | collective-permute-start | bytes 417800 | tf_op jit(solution)/shard_map/ppermute | solution.py:58
  13.9 7.6 %collective-permute-start.4 = (bf16[1,136,512]{2,1,0:T(8,128)(2,1)S(1)}, bf16[1,136,512]{2,1,0:T(8,128)(2,1)S(1)}, u32[]{:S(2)}, u32[]{:S(2)}) collective-permute-start(bf16[1,136,512]{2,1,0:T(8,128)(2,1)S(1)} %collective-permute-done.refs_7_), channel_id=1, source_target_pairs={{0,2},{1,3},{2,0},{3,1},{4,6},{5,7},{6,4},{7,5},{8,10},{9,11},{10,... | collective-permute-start | bytes 417800 | tf_op jit(solution)/shard_map/ppermute | solution.py:63
  15.4 6.8 %collective-permute-start.5 = (bf16[1,136,512]{2,1,0:T(8,128)(2,1)S(1)}, bf16[1,136,512]{2,1,0:T(8,128)(2,1)S(1)}, u32[]{:S(2)}, u32[]{:S(2)}) collective-permute-start(bf16[1,136,512]{2,1,0:T(8,128)(2,1)S(1)} %collective-permute-done.1.after_ref.refs_15_), channel_id=1, source_target_pairs={{0,2},{1,3},{2,0},{3,1},{4,6},{5,7},{6,4},{7,5},{8,10},{9,11},{10,... | collective-permute-start | bytes 417800 | tf_op jit(solution)/shard_map/ppermute | solution.py:63
  16.0 6.8 %collective-permute-start.6 = (bf16[1,136,512]{2,1,0:T(8,128)(2,1)S(1)}, bf16[1,136,512]{2,1,0:T(8,128)(2,1)S(1)}, u32[]{:S(2)}, u32[]{:S(2)}) collective-permute-start(bf16[1,136,512]{2,1,0:T(8,128)(2,1)S(1)} %collective-permute-done.2.refs_5_), channel_id=1, source_target_pairs={{0,1},{1,0},{2,3},{3,2},{4,5},{5,4},{6,7},{7,6},{8,9},{9,8},{10,11... | collective-permute-start | bytes 417800 | tf_op jit(solution)/shard_map/ppermute | solution.py:68
  20.2 5.7 %collective-permute-start.11 = (bf16[1,136,512]{2,1,0:T(8,128)(2,1)S(1)}, bf16[1,136,512]{2,1,0:T(8,128)(2,1)S(1)}, u32[]{:S(2)}, u32[]{:S(2)}) collective-permute-start(bf16[1,136,512]{2,1,0:T(8,128)(2,1)S(1)} %collective-permute-done.9.refs_11_), channel_id=1, source_target_pairs={{0,2},{1,3},{2,0},{3,1},{4,6},{5,7},{6,4},{7,5},{8,10},{9,11},{10,... | collective-permute-start | bytes 417800 | tf_op jit(solution)/shard_map/ppermute | solution.py:63
  21.3 4.6 %collective-permute-start.10 = (bf16[1,136,512]{2,1,0:T(8,128)(2,1)S(1)}, bf16[1,136,512]{2,1,0:T(8,128)(2,1)S(1)}, u32[]{:S(2)}, u32[]{:S(2)}) collective-permute-start(bf16[1,136,512]{2,1,0:T(8,128)(2,1)S(1)} %collective-permute-done.9.refs_11_), channel_id=1, source_target_pairs={{0,1},{1,0},{2,3},{3,2},{4,5},{5,4},{6,7},{7,6},{8,9},{9,8},{10,11... | collective-permute-start | bytes 417800 | tf_op jit(solution)/shard_map/ppermute | solution.py:68
  22.2 4.2 %collective-permute-start.13 = (bf16[1,136,512]{2,1,0:T(8,128)(2,1)S(1)}, bf16[1,136,512]{2,1,0:T(8,128)(2,1)S(1)}, u32[]{:S(2)}, u32[]{:S(2)}) collective-permute-start(bf16[1,136,512]{2,1,0:T(8,128)(2,1)S(1)} %collective-permute-done.1.after_ref.refs_15_), channel_id=1, source_target_pairs={{0,1},{1,0},{2,3},{3,2},{4,5},{5,4},{6,7},{7,6},{8,9},{9,8},{10,11... | collective-permute-start | bytes 417800 | tf_op jit(solution)/shard_map/ppermute | solution.py:68
  22.2 4.2 %collective-permute-start.14 = (bf16[1,136,512]{2,1,0:T(8,128)(2,1)S(1)}, bf16[1,136,512]{2,1,0:T(8,128)(2,1)S(1)}, u32[]{:S(2)}, u32[]{:S(2)}) collective-permute-start(bf16[1,136,512]{2,1,0:T(8,128)(2,1)S(1)} %collective-permute-done.5.refs_17_), channel_id=1, source_target_pairs={{0,1},{1,0},{2,3},{3,2},{4,5},{5,4},{6,7},{7,6},{8,9},{9,8},{10,11... | collective-permute-start | bytes 417800 | tf_op jit(solution)/shard_map/ppermute | solution.py:68
  22.7 3.7 %collective-permute-start.7 = (bf16[1,136,512]{2,1,0:T(8,128)(2,1)S(1)}, bf16[1,136,512]{2,1,0:T(8,128)(2,1)S(1)}, u32[]{:S(2)}, u32[]{:S(2)}) collective-permute-start(bf16[1,136,512]{2,1,0:T(8,128)(2,1)S(1)} %collective-permute-done.refs_7_), channel_id=1, source_target_pairs={{0,1},{1,0},{2,3},{3,2},{4,5},{5,4},{6,7},{7,6},{8,9},{9,8},{10,11... | collective-permute-start | bytes 417800 | tf_op jit(solution)/shard_map/ppermute | solution.py:68
  25.9 1.4 %collective-permute-start.8 = (bf16[1,136,512]{2,1,0:T(8,128)(2,1)S(1)}, bf16[1,136,512]{2,1,0:T(8,128)(2,1)S(1)}, u32[]{:S(2)}, u32[]{:S(2)}) collective-permute-start(bf16[1,136,512]{2,1,0:T(8,128)(2,1)S(1)} %collective-permute-done.4.refs_9_), channel_id=1, source_target_pairs={{0,1},{1,0},{2,3},{3,2},{4,5},{5,4},{6,7},{7,6},{8,9},{9,8},{10,11... | collective-permute-start | bytes 417800 | tf_op jit(solution)/shard_map/ppermute | solution.py:68
  25.9 1.6 %collective-permute-start.12 = (bf16[1,136,512]{2,1,0:T(8,128)(2,1)S(1)}, bf16[1,136,512]{2,1,0:T(8,128)(2,1)S(1)}, u32[]{:S(2)}, u32[]{:S(2)}) collective-permute-start(bf16[1,136,512]{2,1,0:T(8,128)(2,1)S(1)} %collective-permute-done.11.refs_13_), channel_id=1, source_target_pairs={{0,1},{1,0},{2,3},{3,2},{4,5},{5,4},{6,7},{7,6},{8,9},{9,8},{10,11... | collective-permute-start | bytes 417800 | tf_op jit(solution)/shard_map/ppermute | solution.py:68
  27.5 48.6 %copy-start = (bf16[128,512]{1,0:T(8,128)(2,1)S(1)}, bf16[128,512]{1,0:T(8,128)(2,1)}, u32[]{:S(2)}) copy-start(bf16[128,512]{1,0:T(8,128)(2,1)} %hidden_ref.3) | copy-start | bytes 393220
  51.8 1.6 %collective-permute-start.19 = (bf16[2,1,128,512]{3,2,1,0:T(8,128)(2,1)S(1)}, bf16[2,1,128,512]{3,2,1,0:T(8,128)(2,1)S(1)}, u32[]{:S(2)}, u32[]{:S(2)}) collective-permute-start(bf16[2,1,128,512]{3,2,1,0:T(8,128)(2,1)S(1)} %get-tuple-element.59), channel_id=1, source_target_pairs={{0,1},{1,0},{2,3},{3,2},{4,5},{5,4},{6,7},{7,6},{8,9},{9,8},{10,11... | collective-permute-start | bytes 786440 | tf_op jit(solution)/shard_map/ppermute | solution.py:68
  52.2 2.9 %collective-permute-start.16 = (bf16[2,2,128,512]{3,2,1,0:T(8,128)(2,1)S(1)}, bf16[2,2,128,512]{3,2,1,0:T(8,128)(2,1)S(1)}, u32[]{:S(2)}, u32[]{:S(2)}) collective-permute-start(bf16[2,2,128,512]{3,2,1,0:T(8,128)(2,1)S(1)} %get-tuple-element.56), channel_id=1, source_target_pairs={{0,1},{1,0},{2,3},{3,2},{4,5},{5,4},{6,7},{7,6},{8,9},{9,8},{10,11... | collective-permute-start | bytes 1572872 | tf_op jit(solution)/shard_map/ppermute | solution.py:68
  52.4 2.6 %collective-permute-start.15 = (bf16[2,1,128,512]{3,2,1,0:T(8,128)(2,1)S(1)}, bf16[2,1,128,512]{3,2,1,0:T(8,128)(2,1)S(1)}, u32[]{:S(2)}, u32[]{:S(2)}) collective-permute-start(bf16[2,1,128,512]{3,2,1,0:T(8,128)(2,1)S(1)} %get-tuple-element.54), channel_id=1, source_target_pairs={{0,1},{1,0},{2,3},{3,2},{4,5},{5,4},{6,7},{7,6},{8,9},{9,8},{10,11... | collective-permute-start | bytes 786440 | tf_op jit(solution)/shard_map/ppermute | solution.py:68
  53.5 6.4 %collective-permute-start.20 = (bf16[1,128,512]{2,1,0:T(8,128)(2,1)S(1)}, bf16[1,128,512]{2,1,0:T(8,128)(2,1)S(1)}, u32[]{:S(2)}, u32[]{:S(2)}) collective-permute-start(bf16[1,128,512]{2,1,0:T(8,128)(2,1)S(1)} %slice_bitcast_fusion.3), channel_id=1, source_target_pairs={{0,2},{1,3},{2,0},{3,1},{4,6},{5,7},{6,4},{7,5},{8,10},{9,11},{10,... | collective-permute-start | bytes 393224 | tf_op jit(solution)/shard_map/ppermute | solution.py:63
  55.3 10.2 %collective-permute-start.17 = (bf16[2,128,512]{2,1,0:T(8,128)(2,1)S(1)}, bf16[2,128,512]{2,1,0:T(8,128)(2,1)S(1)}, u32[]{:S(2)}, u32[]{:S(2)}) collective-permute-start(bf16[2,128,512]{2,1,0:T(8,128)(2,1)S(1)} %slice_bitcast_fusion.1), channel_id=1, source_target_pairs={{0,2},{1,3},{2,0},{3,1},{4,6},{5,7},{6,4},{7,5},{8,10},{9,11},{10,... | collective-permute-start | bytes 786440 | tf_op jit(solution)/shard_map/ppermute | solution.py:63
  59.9 5.5 %collective-permute-start.21 = (bf16[152,512]{1,0:T(8,128)(2,1)S(1)}, bf16[152,512]{1,0:T(8,128)(2,1)S(1)}, u32[]{:S(2)}, u32[]{:S(2)}) collective-permute-start(bf16[152,512]{1,0:T(8,128)(2,1)S(1)} %pad_maximum_fusion.1), channel_id=1, source_target_pairs={{0,12},{4,0},{8,4},{12,8},{1,13},{5,1},{9,5},{13,9},{2,14},{6,2},{... | collective-permute-start | bytes 466952 | tf_op jit(solution)/shard_map/ppermute | solution.py:58
  65.5 9.2 %collective-permute-start.23 = (bf16[152,512]{1,0:T(8,128)(2,1)S(1)}, bf16[152,512]{1,0:T(8,128)(2,1)S(1)}, u32[]{:S(2)}, u32[]{:S(2)}) collective-permute-start(bf16[152,512]{1,0:T(8,128)(2,1)S(1)} %pad_maximum_fusion.2), channel_id=1, source_target_pairs={{0,4},{4,8},{8,12},{12,0},{1,5},{5,9},{9,13},{13,1},{2,6},{6,10},{... | collective-permute-start | bytes 466952 | tf_op jit(solution)/shard_map/ppermute | solution.py:58
  66.1 5.4 %collective-permute-start.18 = (bf16[1,128,512]{2,1,0:T(8,128)(2,1)S(1)}, bf16[1,128,512]{2,1,0:T(8,128)(2,1)S(1)}, u32[]{:S(2)}, u32[]{:S(2)}) collective-permute-start(bf16[1,128,512]{2,1,0:T(8,128)(2,1)S(1)} %slice_bitcast_fusion.6), channel_id=1, source_target_pairs={{0,2},{1,3},{2,0},{3,1},{4,6},{5,7},{6,4},{7,5},{8,10},{9,11},{10,... | collective-permute-start | bytes 393224 | tf_op jit(solution)/shard_map/ppermute | solution.py:63
  67.7 8.4 %collective-permute-start.22 = (bf16[176,512]{1,0:T(8,128)(2,1)S(1)}, bf16[176,512]{1,0:T(8,128)(2,1)S(1)}, u32[]{:S(2)}, u32[]{:S(2)}) collective-permute-start(bf16[176,512]{1,0:T(8,128)(2,1)S(1)} %pad_maximum_fusion), channel_id=1, source_target_pairs={{0,12},{4,0},{8,4},{12,8},{1,13},{5,1},{9,5},{13,9},{2,14},{6,2},{... | collective-permute-start | bytes 540680 | tf_op jit(solution)/shard_map/ppermute | solution.py:58

commit v16 on v15

--- a/solution.py
+++ b/solution.py
@@ -18,7 +18,7 @@
 HOP_CHIPS = 2
 PAGE_FOLD = 24
 SMALL_VMEM = 4 * 1024 * 1024
-WEIGHT_SLOTS = 3
+WEIGHT_SLOTS = 4
 FILL_COST = 18 * 1024 * 1024
 EXPERT_VMEM = 8 * 1024 * 1024
 
@@ -149,8 +149,9 @@
 
 
 def fill_kernel(gate_up_ref, down_ref, after_ref, *refs, expert):
-    rings, sems = refs[3:6], refs[6]
-    copies = expert_copies(gate_up_ref, down_ref, expert, rings, expert, sems)
+    rings, sems, rest_sems = refs[3:6], refs[6], refs[7]
+    copies = expert_copies(gate_up_ref, down_ref, expert - 1, rings, expert - 1, rest_sems)[2:]
+    copies += expert_copies(gate_up_ref, down_ref, expert, rings, expert, sems)
     for copy in copies:
         copy.start()
     for copy in copies:
@@ -168,7 +169,7 @@
         pltpu.make_async_copy(owners_ref, owners_buf, page_sems.at[2]),
     )
     rings = (gate_ring, up_ring, down_ring)
-    copies = expert_copies(gate_up_ref, down_ref, 0, rings, 0, sems)
+    copies = expert_copies(gate_up_ref, down_ref, 0, rings, 0, sems)[:2]
     for copy in small + copies:
         copy.start()
     for copy in small:
@@ -217,7 +218,7 @@
         in_specs=[hbm, hbm, pl.BlockSpec(memory_space=pl.ANY)] + [vmem] * 3,
         out_specs=[vmem] * 3,
         input_output_aliases={3: 0, 4: 1, 5: 2},
-        scratch_shapes=[pltpu.SemaphoreType.DMA((3,))],
+        scratch_shapes=[pltpu.SemaphoreType.DMA((3,)), pltpu.SemaphoreType.DMA((3,))],
         compiler_params=pltpu.CompilerParams(vmem_limit_bytes=SMALL_VMEM),
         cost_estimate=pl.CostEstimate(flops=0, bytes_accessed=FILL_COST, transcendentals=0),
     )(gate_up_weight, down_weight, after, *in_vmem(*rings))
@@ -395,10 +396,16 @@
             back = pick_ref[z].T
             at = pl.ds(z * held * CAP, held * CAP)
             for x in range(chips):
-                for c in range(CORES):
-                    out_refs[group * CORES + c][x, i] = jnp.dot(
-                        back, served_ref[at, features[x][c]], preferred_element_type=jnp.float32
-                    ).astype(jnp.bfloat16)
+                chip = lax.rem(my_x + chips - x, chips) * (CORES * width)
+                both = jnp.dot(
+                    back, served_ref[at, pl.ds(pl.multiple_of(chip, width), CORES * width)],
+                    preferred_element_type=jnp.float32,
+                )
+                low, high = both[:, :width], both[:, width:]
+                keep = jnp.where(my_core == 0, low, high)
+                send = jnp.where(my_core == 0, high, low)
+                out_refs[group * CORES][x, i] = keep.astype(jnp.bfloat16)
+                out_refs[group * CORES + 1][x, i] = send.astype(jnp.bfloat16)
 
 
 def expert_sums(gain, gate_up_weight, down_weight, rings, fills, blocks):

time: 77 us -> 80.6 us (1.047)
  Pallas kernels: 33.6 us -> 36.2 us
    pallas_call x1, Pallas kernels: 24.3 us -> 26.9 us  [expert_sums(): pl.pallas_call(functools.partial(expert_kernel, held=held, parts=parts, c...]
    pallas_call x1, Pallas kernels: 3.78 us -> 4.7 us  [next_fill(): pl.pallas_call(functools.partial(fill_kernel, expert=expert), out_shape=r...]
    pallas_call x1, Pallas kernels: 3.84 us -> 2.93 us  [first_fill(): pl.pallas_call(page_fill_kernel, out_shape=ring_shapes(down_weight) + [ja...]
  transfers between devices with their start and end apart: 24 -> 24, of which waited for: 11 -> 9; matrix products, arithmetic and copies ran while one was open for 1% -> 1% of each run, Pallas kernels for 10% -> 9%
where the time goes in v16:
time: 80.6 us; the launch traced here: 80.4 us
  Pallas kernels  36.2 us (45%)
  starting transfers between devices  25.2 us (31%)
  waiting for transfers between devices  17.6 us (22%)
    pallas_call x1, Pallas kernels, expert_sums(): pl.pallas_call(functools.partial(expert_kernel, held=held, parts=parts, c...  26.9 us
    ppermute x6, starting transfers between devices, shift_dp(): lax.ppermute(value, 'dp', [(i, (i + shift) % count) for i in range(count)])  13.5 us
    ppermute x7, starting transfers between devices, shift_x(): lax.ppermute(value, 'mp', [(i, (i + CORES * shift) % count) for i in rang...  9.29 us
    ppermute x6, waiting for transfers between devices, shift_dp(): lax.ppermute(value, 'dp', [(i, (i + shift) % count) for i in range(count)])  8.72 us
    ppermute x7, waiting for transfers between devices, shift_x(): lax.ppermute(value, 'mp', [(i, (i + CORES * shift) % count) for i in rang...  7.12 us
    pallas_call x1, Pallas kernels, next_fill(): pl.pallas_call(functools.partial(fill_kernel, expert=expert), out_shape=r...  4.7 us
    pallas_call x1, Pallas kernels, first_fill(): pl.pallas_call(page_fill_kernel, out_shape=ring_shapes(down_weight) + [ja...  2.93 us
    ppermute x11, starting transfers between devices, other_core(): return lax.ppermute(value, 'mp', [(i, i ^ 1) for i in range(count)])  2.43 us
  transfers between devices with their start and end apart: 24, of which 9 were waited for; matrix products, arithmetic and copies ran while one was open for 1% of the time, Pallas kernels for 9%

profile of v16, /device:TPU:0, one launch (start us, length us, event | category | flops | bytes accessed | tf_op | source)
XLA Modules:
  0.0 80.4 jit_solution(1225980919754915647)
XLA Ops:
  0.6 1.0 %shard_map.104.after_ref.refs_3_ = bf16[1,136,512]{2,1,0:T(8,128)(2,1)S(1)} custom-call(bf16[128,512]{1,0:T(8,128)(2,1)} %hidden_ref.3, s32[8,128]{1,0:T(8,128)} %bitcast.42, f32[8,128]{1,0:T(8,128)} %bitcast.43), custom_call_target="tpu_custom_call" | custom-call | tf_op jit(solution)/shard_map/pallas_call | solution.py:103
  1.6 3.1 %collective-permute-start = (bf16[1,136,512]{2,1,0:T(8,128)(2,1)S(1)}, bf16[1,136,512]{2,1,0:T(8,128)(2,1)S(1)}, u32[]{:S(2)}, u32[]{:S(2)}) collective-permute-start(bf16[1,136,512]{2,1,0:T(8,128)(2,1)S(1)} %shard_map.104.after_ref.refs_3_), channel_id=1, source_target_pairs={{0,4},{4,8},{8,12},{12,0},{1,5},{5,9},{9,13},{13,1},{2,6},{6,10},{... | collective-permute-start | bytes 417800 | tf_op jit(solution)/shard_map/ppermute | solution.py:58
  4.7 2.1 %collective-permute-start.1 = (bf16[1,136,512]{2,1,0:T(8,128)(2,1)S(1)}, bf16[1,136,512]{2,1,0:T(8,128)(2,1)S(1)}, u32[]{:S(2)}, u32[]{:S(2)}) collective-permute-start(bf16[1,136,512]{2,1,0:T(8,128)(2,1)S(1)} %shard_map.104.after_ref.refs_3_), channel_id=1, source_target_pairs={{0,12},{4,0},{8,4},{12,8},{1,13},{5,1},{9,5},{13,9},{2,14},{6,2},{... | collective-permute-start | bytes 417800 | tf_op jit(solution)/shard_map/ppermute | solution.py:58
  6.8 1.6 %collective-permute-start.2 = (bf16[1,136,512]{2,1,0:T(8,128)(2,1)S(1)}, bf16[1,136,512]{2,1,0:T(8,128)(2,1)S(1)}, u32[]{:S(2)}, u32[]{:S(2)}) collective-permute-start(bf16[1,136,512]{2,1,0:T(8,128)(2,1)S(1)} %shard_map.104.after_ref.refs_3_), channel_id=1, source_target_pairs={{0,2},{1,3},{2,0},{3,1},{4,6},{5,7},{6,4},{7,5},{8,10},{9,11},{10,... | collective-permute-start | bytes 417800 | tf_op jit(solution)/shard_map/ppermute | solution.py:63
  8.4 2.9 %shard_map.105 = (bf16[4,768,2048]{2,1,0:T(8,128)(2,1)S(1)}, bf16[4,768,2048]{2,1,0:T(8,128)(2,1)S(1)}, bf16[4,768,2048]{2,1,0:T(8,128)(2,1)S(1)}, bf16[4,24,512]{2,1,0:T(8,128)(2,1)S(1)}) custom-call(bf16[2,6144,2048]{2,1,0:T(8,128)(2,1)} %gate_up_ref.5, bf16[6144,2048]{1,0:T(8,128)(2,1)} %down_ref.5, ...), custom_call_target="tpu_custom_call" | custom-call | bytes 18874368 | tf_op jit(solution)/shard_map/pallas_call | solution.py:189
  11.4 1.4 %collective-permute-done.1.after_ref.refs_15_ = bf16[1,136,512]{2,1,0:T(8,128)(2,1)S(1)} collective-permute-done((bf16[1,136,512]{2,1,0:T(8,128)(2,1)S(1)}, bf16[1,136,512]{2,1,0:T(8,128)(2,1)S(1)}, u32[]{:S(2)}, u32[]{:S(2)}) %collective-permute-start.1) | collective-permute-done | bytes 139296 | tf_op jit(solution)/shard_map/ppermute | solution.py:58
  12.8 1.1 %collective-permute-start.9 = (bf16[1,136,512]{2,1,0:T(8,128)(2,1)S(1)}, bf16[1,136,512]{2,1,0:T(8,128)(2,1)S(1)}, u32[]{:S(2)}, u32[]{:S(2)}) collective-permute-start(bf16[1,136,512]{2,1,0:T(8,128)(2,1)S(1)} %collective-permute-done.refs_7_), channel_id=1, source_target_pairs={{0,4},{4,8},{8,12},{12,0},{1,5},{5,9},{9,13},{13,1},{2,6},{6,10},{... | collective-permute-start | bytes 417800 | tf_op jit(solution)/shard_map/ppermute | solution.py:58
  13.9 1.5 %collective-permute-start.4 = (bf16[1,136,512]{2,1,0:T(8,128)(2,1)S(1)}, bf16[1,136,512]{2,1,0:T(8,128)(2,1)S(1)}, u32[]{:S(2)}, u32[]{:S(2)}) collective-permute-start(bf16[1,136,512]{2,1,0:T(8,128)(2,1)S(1)} %collective-permute-done.refs_7_), channel_id=1, source_target_pairs={{0,2},{1,3},{2,0},{3,1},{4,6},{5,7},{6,4},{7,5},{8,10},{9,11},{10,... | collective-permute-start | bytes 417800 | tf_op jit(solution)/shard_map/ppermute | solution.py:63
  15.4 0.5 collective-permute-start.5
  16.0 4.7 %shard_map.106 = (bf16[4,768,2048]{2,1,0:T(8,128)(2,1)S(1)}, bf16[4,768,2048]{2,1,0:T(8,128)(2,1)S(1)}, bf16[4,768,2048]{2,1,0:T(8,128)(2,1)S(1)}) custom-call(bf16[2,6144,2048]{2,1,0:T(8,128)(2,1)} %gate_up_ref.5, bf16[6144,2048]{1,0:T(8,128)(2,1)} %down_ref.5, ...), custom_call_target="tpu_custom_call", output_to_operand_aliasing={{0}: (3, {}), {1}: (4, {}), {2}: (5, {})} | custom-call | bytes 18874368 | tf_op jit(solution)/shard_map/pallas_call | solution.py:215
  20.7 1.6 %collective-permute-start.11 = (bf16[1,136,512]{2,1,0:T(8,128)(2,1)S(1)}, bf16[1,136,512]{2,1,0:T(8,128)(2,1)S(1)}, u32[]{:S(2)}, u32[]{:S(2)}) collective-permute-start(bf16[1,136,512]{2,1,0:T(8,128)(2,1)S(1)} %collective-permute-done.9.refs_11_), channel_id=1, source_target_pairs={{0,2},{1,3},{2,0},{3,1},{4,6},{5,7},{6,4},{7,5},{8,10},{9,11},{10,... | collective-permute-start | bytes 417800 | tf_op jit(solution)/shard_map/ppermute | solution.py:63
  22.2 0.2 collective-permute-start.10
  22.5 0.3 collective-permute-start.13
  23.0 0.3 collective-permute-start.7
  23.3 3.6 %collective-permute-done.11.refs_13_ = bf16[1,136,512]{2,1,0:T(8,128)(2,1)S(1)} collective-permute-done((bf16[1,136,512]{2,1,0:T(8,128)(2,1)S(1)}, bf16[1,136,512]{2,1,0:T(8,128)(2,1)S(1)}, u32[]{:S(2)}, u32[]{:S(2)}) %collective-permute-start.11) | collective-permute-done | bytes 139296 | tf_op jit(solution)/shard_map/ppermute | solution.py:63
  26.8 0.5 collective-permute-start.12
  27.4 0.8 %collective-permute-done.8.refs_10_ = bf16[1,136,512]{2,1,0:T(8,128)(2,1)S(1)} collective-permute-done((bf16[1,136,512]{2,1,0:T(8,128)(2,1)S(1)}, bf16[1,136,512]{2,1,0:T(8,128)(2,1)S(1)}, u32[]{:S(2)}, u32[]{:S(2)}) %collective-permute-start.8) | collective-permute-done | bytes 139296 | tf_op jit(solution)/shard_map/ppermute | solution.py:68
  28.4 26.9 %shard_map.107 = (bf16[2,1,128,512]{3,2,1,0:T(8,128)(2,1)S(1)}, bf16[2,1,128,512]{3,2,1,0:T(8,128)(2,1)S(1)}, bf16[2,2,128,512]{3,2,1,0:T(8,128)(2,1)S(1)}, bf16...) custom-call(f32[1,2048]{1,0:T(1,128)} %bitcast.41, ...), custom_call_target="tpu_custom_call", output_to_operand_aliasing={{6}: (3, {}), {7}: (4, {}), {8}: (5, {})} | custom-call | flops 4831838208 | bytes 75497472 | tf_op jit(solution)/shard_map/pallas_call | solution.py:425
  55.3 0.4 collective-permute-start.19
  55.9 0.3 collective-permute-start.15
  56.2 0.7 collective-permute-done.19
  57.0 1.6 %collective-permute-start.20 = (bf16[1,128,512]{2,1,0:T(8,128)(2,1)S(1)}, bf16[1,128,512]{2,1,0:T(8,128)(2,1)S(1)}, u32[]{:S(2)}, u32[]{:S(2)}) collective-permute-start(bf16[1,128,512]{2,1,0:T(8,128)(2,1)S(1)} %slice_bitcast_fusion.3), channel_id=1, source_target_pairs={{0,2},{1,3},{2,0},{3,1},{4,6},{5,7},{6,4},{7,5},{8,10},{9,11},{10,... | collective-permute-start | bytes 393224 | tf_op jit(solution)/shard_map/ppermute | solution.py:63
  58.8 1.0 %collective-permute-start.17 = (bf16[2,128,512]{2,1,0:T(8,128)(2,1)S(1)}, bf16[2,128,512]{2,1,0:T(8,128)(2,1)S(1)}, u32[]{:S(2)}, u32[]{:S(2)}) collective-permute-start(bf16[2,128,512]{2,1,0:T(8,128)(2,1)S(1)} %slice_bitcast_fusion.1), channel_id=1, source_target_pairs={{0,2},{1,3},{2,0},{3,1},{4,6},{5,7},{6,4},{7,5},{8,10},{9,11},{10,... | collective-permute-start | bytes 786440 | tf_op jit(solution)/shard_map/ppermute | solution.py:63
  59.8 3.5 %collective-permute-done.20 = bf16[1,128,512]{2,1,0:T(8,128)(2,1)S(1)} collective-permute-done((bf16[1,128,512]{2,1,0:T(8,128)(2,1)S(1)}, bf16[1,128,512]{2,1,0:T(8,128)(2,1)S(1)}, u32[]{:S(2)}, u32[]{:S(2)}) %collective-permute-start.20) | collective-permute-done | bytes 131104 | tf_op jit(solution)/shard_map/ppermute | solution.py:63
  63.4 2.7 %collective-permute-start.21 = (bf16[152,512]{1,0:T(8,128)(2,1)S(1)}, bf16[152,512]{1,0:T(8,128)(2,1)S(1)}, u32[]{:S(2)}, u32[]{:S(2)}) collective-permute-start(bf16[152,512]{1,0:T(8,128)(2,1)S(1)} %pad_maximum_fusion.1), channel_id=1, source_target_pairs={{0,12},{4,0},{8,4},{12,8},{1,13},{5,1},{9,5},{13,9},{2,14},{6,2},{... | collective-permute-start | bytes 466952 | tf_op jit(solution)/shard_map/ppermute | solution.py:58
  66.2 2.7 %collective-permute-done.21 = bf16[152,512]{1,0:T(8,128)(2,1)S(1)} collective-permute-done((bf16[152,512]{1,0:T(8,128)(2,1)S(1)}, bf16[152,512]{1,0:T(8,128)(2,1)S(1)}, u32[]{:S(2)}, u32[]{:S(2)}) %collective-permute-start.21) | collective-permute-done | bytes 155680 | tf_op jit(solution)/shard_map/ppermute | solution.py:58
  69.1 0.6 collective-permute-start.23
  69.7 1.5 %collective-permute-start.18 = (bf16[1,128,512]{2,1,0:T(8,128)(2,1)S(1)}, bf16[1,128,512]{2,1,0:T(8,128)(2,1)S(1)}, u32[]{:S(2)}, u32[]{:S(2)}) collective-permute-start(bf16[1,128,512]{2,1,0:T(8,128)(2,1)S(1)} %slice_bitcast_fusion.6), channel_id=1, source_target_pairs={{0,2},{1,3},{2,0},{3,1},{4,6},{5,7},{6,4},{7,5},{8,10},{9,11},{10,... | collective-permute-start | bytes 393224 | tf_op jit(solution)/shard_map/ppermute | solution.py:63
  71.2 3.9 %collective-permute-start.22 = (bf16[176,512]{1,0:T(8,128)(2,1)S(1)}, bf16[176,512]{1,0:T(8,128)(2,1)S(1)}, u32[]{:S(2)}, u32[]{:S(2)}) collective-permute-start(bf16[176,512]{1,0:T(8,128)(2,1)S(1)} %pad_maximum_fusion), channel_id=1, source_target_pairs={{0,12},{4,0},{8,4},{12,8},{1,13},{5,1},{9,5},{13,9},{2,14},{6,2},{... | collective-permute-start | bytes 540680 | tf_op jit(solution)/shard_map/ppermute | solution.py:58
  75.1 3.2 %collective-permute-done.23.up_ref = bf16[152,512]{1,0:T(8,128)(2,1)S(1)} collective-permute-done((bf16[152,512]{1,0:T(8,128)(2,1)S(1)}, bf16[152,512]{1,0:T(8,128)(2,1)S(1)}, u32[]{:S(2)}, u32[]{:S(2)}) %collective-permute-start.23) | collective-permute-done | bytes 155680 | tf_op jit(solution)/shard_map/ppermute | solution.py:58
  78.3 1.4 %collective-permute-done.22.down_ref = bf16[176,512]{1,0:T(8,128)(2,1)S(1)} collective-permute-done((bf16[176,512]{1,0:T(8,128)(2,1)S(1)}, bf16[176,512]{1,0:T(8,128)(2,1)S(1)}, u32[]{:S(2)}, u32[]{:S(2)}) %collective-permute-start.22) | collective-permute-done | bytes 180256 | tf_op jit(solution)/shard_map/ppermute | solution.py:58
  79.7 0.8 shard_map.108
  (39 shorter events, 1.2 us)
Async XLA Ops:
  1.6 9.8 %collective-permute-start = (bf16[1,136,512]{2,1,0:T(8,128)(2,1)S(1)}, bf16[1,136,512]{2,1,0:T(8,128)(2,1)S(1)}, u32[]{:S(2)}, u32[]{:S(2)}) collective-permute-start(bf16[1,136,512]{2,1,0:T(8,128)(2,1)S(1)} %shard_map.104.after_ref.refs_3_), channel_id=1, source_target_pairs={{0,4},{4,8},{8,12},{12,0},{1,5},{5,9},{9,13},{13,1},{2,6},{6,10},{... | collective-permute-start | bytes 417800 | tf_op jit(solution)/shard_map/ppermute | solution.py:58
  4.7 8.1 %collective-permute-start.1 = (bf16[1,136,512]{2,1,0:T(8,128)(2,1)S(1)}, bf16[1,136,512]{2,1,0:T(8,128)(2,1)S(1)}, u32[]{:S(2)}, u32[]{:S(2)}) collective-permute-start(bf16[1,136,512]{2,1,0:T(8,128)(2,1)S(1)} %shard_map.104.after_ref.refs_3_), channel_id=1, source_target_pairs={{0,12},{4,0},{8,4},{12,8},{1,13},{5,1},{9,5},{13,9},{2,14},{6,2},{... | collective-permute-start | bytes 417800 | tf_op jit(solution)/shard_map/ppermute | solution.py:58
  6.8 6.0 %collective-permute-start.2 = (bf16[1,136,512]{2,1,0:T(8,128)(2,1)S(1)}, bf16[1,136,512]{2,1,0:T(8,128)(2,1)S(1)}, u32[]{:S(2)}, u32[]{:S(2)}) collective-permute-start(bf16[1,136,512]{2,1,0:T(8,128)(2,1)S(1)} %shard_map.104.after_ref.refs_3_), channel_id=1, source_target_pairs={{0,2},{1,3},{2,0},{3,1},{4,6},{5,7},{6,4},{7,5},{8,10},{9,11},{10,... | collective-permute-start | bytes 417800 | tf_op jit(solution)/shard_map/ppermute | solution.py:63
  8.4 4.4 %collective-permute-start.3 = (bf16[1,136,512]{2,1,0:T(8,128)(2,1)S(1)}, bf16[1,136,512]{2,1,0:T(8,128)(2,1)S(1)}, u32[]{:S(2)}, u32[]{:S(2)}) collective-permute-start(bf16[1,136,512]{2,1,0:T(8,128)(2,1)S(1)} %shard_map.104.after_ref.refs_3_), channel_id=1, source_target_pairs={{0,1},{1,0},{2,3},{3,2},{4,5},{5,4},{6,7},{7,6},{8,9},{9,8},{10,11... | collective-permute-start | bytes 417800 | tf_op jit(solution)/shard_map/ppermute | solution.py:68
  12.8 7.9 %collective-permute-start.9 = (bf16[1,136,512]{2,1,0:T(8,128)(2,1)S(1)}, bf16[1,136,512]{2,1,0:T(8,128)(2,1)S(1)}, u32[]{:S(2)}, u32[]{:S(2)}) collective-permute-start(bf16[1,136,512]{2,1,0:T(8,128)(2,1)S(1)} %collective-permute-done.refs_7_), channel_id=1, source_target_pairs={{0,4},{4,8},{8,12},{12,0},{1,5},{5,9},{9,13},{13,1},{2,6},{6,10},{... | collective-permute-start | bytes 417800 | tf_op jit(solution)/shard_map/ppermute | solution.py:58
  13.9 8.5 %collective-permute-start.4 = (bf16[1,136,512]{2,1,0:T(8,128)(2,1)S(1)}, bf16[1,136,512]{2,1,0:T(8,128)(2,1)S(1)}, u32[]{:S(2)}, u32[]{:S(2)}) collective-permute-start(bf16[1,136,512]{2,1,0:T(8,128)(2,1)S(1)} %collective-permute-done.refs_7_), channel_id=1, source_target_pairs={{0,2},{1,3},{2,0},{3,1},{4,6},{5,7},{6,4},{7,5},{8,10},{9,11},{10,... | collective-permute-start | bytes 417800 | tf_op jit(solution)/shard_map/ppermute | solution.py:63
  15.4 7.0 %collective-permute-start.5 = (bf16[1,136,512]{2,1,0:T(8,128)(2,1)S(1)}, bf16[1,136,512]{2,1,0:T(8,128)(2,1)S(1)}, u32[]{:S(2)}, u32[]{:S(2)}) collective-permute-start(bf16[1,136,512]{2,1,0:T(8,128)(2,1)S(1)} %collective-permute-done.1.after_ref.refs_15_), channel_id=1, source_target_pairs={{0,2},{1,3},{2,0},{3,1},{4,6},{5,7},{6,4},{7,5},{8,10},{9,11},{10,... | collective-permute-start | bytes 417800 | tf_op jit(solution)/shard_map/ppermute | solution.py:63
  16.0 7.0 %collective-permute-start.6 = (bf16[1,136,512]{2,1,0:T(8,128)(2,1)S(1)}, bf16[1,136,512]{2,1,0:T(8,128)(2,1)S(1)}, u32[]{:S(2)}, u32[]{:S(2)}) collective-permute-start(bf16[1,136,512]{2,1,0:T(8,128)(2,1)S(1)} %collective-permute-done.2.refs_5_), channel_id=1, source_target_pairs={{0,1},{1,0},{2,3},{3,2},{4,5},{5,4},{6,7},{7,6},{8,9},{9,8},{10,11... | collective-permute-start | bytes 417800 | tf_op jit(solution)/shard_map/ppermute | solution.py:68
  20.7 6.2 %collective-permute-start.11 = (bf16[1,136,512]{2,1,0:T(8,128)(2,1)S(1)}, bf16[1,136,512]{2,1,0:T(8,128)(2,1)S(1)}, u32[]{:S(2)}, u32[]{:S(2)}) collective-permute-start(bf16[1,136,512]{2,1,0:T(8,128)(2,1)S(1)} %collective-permute-done.9.refs_11_), channel_id=1, source_target_pairs={{0,2},{1,3},{2,0},{3,1},{4,6},{5,7},{6,4},{7,5},{8,10},{9,11},{10,... | collective-permute-start | bytes 417800 | tf_op jit(solution)/shard_map/ppermute | solution.py:63
  22.2 4.6 %collective-permute-start.10 = (bf16[1,136,512]{2,1,0:T(8,128)(2,1)S(1)}, bf16[1,136,512]{2,1,0:T(8,128)(2,1)S(1)}, u32[]{:S(2)}, u32[]{:S(2)}) collective-permute-start(bf16[1,136,512]{2,1,0:T(8,128)(2,1)S(1)} %collective-permute-done.9.refs_11_), channel_id=1, source_target_pairs={{0,1},{1,0},{2,3},{3,2},{4,5},{5,4},{6,7},{7,6},{8,9},{9,8},{10,11... | collective-permute-start | bytes 417800 | tf_op jit(solution)/shard_map/ppermute | solution.py:68
  22.5 4.9 %collective-permute-start.13 = (bf16[1,136,512]{2,1,0:T(8,128)(2,1)S(1)}, bf16[1,136,512]{2,1,0:T(8,128)(2,1)S(1)}, u32[]{:S(2)}, u32[]{:S(2)}) collective-permute-start(bf16[1,136,512]{2,1,0:T(8,128)(2,1)S(1)} %collective-permute-done.1.after_ref.refs_15_), channel_id=1, source_target_pairs={{0,1},{1,0},{2,3},{3,2},{4,5},{5,4},{6,7},{7,6},{8,9},{9,8},{10,11... | collective-permute-start | bytes 417800 | tf_op jit(solution)/shard_map/ppermute | solution.py:68
  22.8 4.6 %collective-permute-start.14 = (bf16[1,136,512]{2,1,0:T(8,128)(2,1)S(1)}, bf16[1,136,512]{2,1,0:T(8,128)(2,1)S(1)}, u32[]{:S(2)}, u32[]{:S(2)}) collective-permute-start(bf16[1,136,512]{2,1,0:T(8,128)(2,1)S(1)} %collective-permute-done.5.refs_17_), channel_id=1, source_target_pairs={{0,1},{1,0},{2,3},{3,2},{4,5},{5,4},{6,7},{7,6},{8,9},{9,8},{10,11... | collective-permute-start | bytes 417800 | tf_op jit(solution)/shard_map/ppermute | solution.py:68
  23.0 4.4 %collective-permute-start.7 = (bf16[1,136,512]{2,1,0:T(8,128)(2,1)S(1)}, bf16[1,136,512]{2,1,0:T(8,128)(2,1)S(1)}, u32[]{:S(2)}, u32[]{:S(2)}) collective-permute-start(bf16[1,136,512]{2,1,0:T(8,128)(2,1)S(1)} %collective-permute-done.refs_7_), channel_id=1, source_target_pairs={{0,1},{1,0},{2,3},{3,2},{4,5},{5,4},{6,7},{7,6},{8,9},{9,8},{10,11... | collective-permute-start | bytes 417800 | tf_op jit(solution)/shard_map/ppermute | solution.py:68
  26.8 1.4 %collective-permute-start.8 = (bf16[1,136,512]{2,1,0:T(8,128)(2,1)S(1)}, bf16[1,136,512]{2,1,0:T(8,128)(2,1)S(1)}, u32[]{:S(2)}, u32[]{:S(2)}) collective-permute-start(bf16[1,136,512]{2,1,0:T(8,128)(2,1)S(1)} %collective-permute-done.4.refs_9_), channel_id=1, source_target_pairs={{0,1},{1,0},{2,3},{3,2},{4,5},{5,4},{6,7},{7,6},{8,9},{9,8},{10,11... | collective-permute-start | bytes 417800 | tf_op jit(solution)/shard_map/ppermute | solution.py:68
  26.8 1.6 %collective-permute-start.12 = (bf16[1,136,512]{2,1,0:T(8,128)(2,1)S(1)}, bf16[1,136,512]{2,1,0:T(8,128)(2,1)S(1)}, u32[]{:S(2)}, u32[]{:S(2)}) collective-permute-start(bf16[1,136,512]{2,1,0:T(8,128)(2,1)S(1)} %collective-permute-done.11.refs_13_), channel_id=1, source_target_pairs={{0,1},{1,0},{2,3},{3,2},{4,5},{5,4},{6,7},{7,6},{8,9},{9,8},{10,11... | collective-permute-start | bytes 417800 | tf_op jit(solution)/shard_map/ppermute | solution.py:68
  28.4 51.3 %copy-start = (bf16[128,512]{1,0:T(8,128)(2,1)S(1)}, bf16[128,512]{1,0:T(8,128)(2,1)}, u32[]{:S(2)}) copy-start(bf16[128,512]{1,0:T(8,128)(2,1)} %hidden_ref.3) | copy-start | bytes 393220
  55.3 1.6 %collective-permute-start.19 = (bf16[2,1,128,512]{3,2,1,0:T(8,128)(2,1)S(1)}, bf16[2,1,128,512]{3,2,1,0:T(8,128)(2,1)S(1)}, u32[]{:S(2)}, u32[]{:S(2)}) collective-permute-start(bf16[2,1,128,512]{3,2,1,0:T(8,128)(2,1)S(1)} %get-tuple-element.59), channel_id=1, source_target_pairs={{0,1},{1,0},{2,3},{3,2},{4,5},{5,4},{6,7},{7,6},{8,9},{9,8},{10,11... | collective-permute-start | bytes 786440 | tf_op jit(solution)/shard_map/ppermute | solution.py:68
  55.7 2.9 %collective-permute-start.16 = (bf16[2,2,128,512]{3,2,1,0:T(8,128)(2,1)S(1)}, bf16[2,2,128,512]{3,2,1,0:T(8,128)(2,1)S(1)}, u32[]{:S(2)}, u32[]{:S(2)}) collective-permute-start(bf16[2,2,128,512]{3,2,1,0:T(8,128)(2,1)S(1)} %get-tuple-element.56), channel_id=1, source_target_pairs={{0,1},{1,0},{2,3},{3,2},{4,5},{5,4},{6,7},{7,6},{8,9},{9,8},{10,11... | collective-permute-start | bytes 1572872 | tf_op jit(solution)/shard_map/ppermute | solution.py:68
  55.9 2.7 %collective-permute-start.15 = (bf16[2,1,128,512]{3,2,1,0:T(8,128)(2,1)S(1)}, bf16[2,1,128,512]{3,2,1,0:T(8,128)(2,1)S(1)}, u32[]{:S(2)}, u32[]{:S(2)}) collective-permute-start(bf16[2,1,128,512]{3,2,1,0:T(8,128)(2,1)S(1)} %get-tuple-element.54), channel_id=1, source_target_pairs={{0,1},{1,0},{2,3},{3,2},{4,5},{5,4},{6,7},{7,6},{8,9},{9,8},{10,11... | collective-permute-start | bytes 786440 | tf_op jit(solution)/shard_map/ppermute | solution.py:68
  57.0 6.4 %collective-permute-start.20 = (bf16[1,128,512]{2,1,0:T(8,128)(2,1)S(1)}, bf16[1,128,512]{2,1,0:T(8,128)(2,1)S(1)}, u32[]{:S(2)}, u32[]{:S(2)}) collective-permute-start(bf16[1,128,512]{2,1,0:T(8,128)(2,1)S(1)} %slice_bitcast_fusion.3), channel_id=1, source_target_pairs={{0,2},{1,3},{2,0},{3,1},{4,6},{5,7},{6,4},{7,5},{8,10},{9,11},{10,... | collective-permute-start | bytes 393224 | tf_op jit(solution)/shard_map/ppermute | solution.py:63
  58.8 10.1 %collective-permute-start.17 = (bf16[2,128,512]{2,1,0:T(8,128)(2,1)S(1)}, bf16[2,128,512]{2,1,0:T(8,128)(2,1)S(1)}, u32[]{:S(2)}, u32[]{:S(2)}) collective-permute-start(bf16[2,128,512]{2,1,0:T(8,128)(2,1)S(1)} %slice_bitcast_fusion.1), channel_id=1, source_target_pairs={{0,2},{1,3},{2,0},{3,1},{4,6},{5,7},{6,4},{7,5},{8,10},{9,11},{10,... | collective-permute-start | bytes 786440 | tf_op jit(solution)/shard_map/ppermute | solution.py:63
  63.4 5.5 %collective-permute-start.21 = (bf16[152,512]{1,0:T(8,128)(2,1)S(1)}, bf16[152,512]{1,0:T(8,128)(2,1)S(1)}, u32[]{:S(2)}, u32[]{:S(2)}) collective-permute-start(bf16[152,512]{1,0:T(8,128)(2,1)S(1)} %pad_maximum_fusion.1), channel_id=1, source_target_pairs={{0,12},{4,0},{8,4},{12,8},{1,13},{5,1},{9,5},{13,9},{2,14},{6,2},{... | collective-permute-start | bytes 466952 | tf_op jit(solution)/shard_map/ppermute | solution.py:58
  69.1 9.2 %collective-permute-start.23 = (bf16[152,512]{1,0:T(8,128)(2,1)S(1)}, bf16[152,512]{1,0:T(8,128)(2,1)S(1)}, u32[]{:S(2)}, u32[]{:S(2)}) collective-permute-start(bf16[152,512]{1,0:T(8,128)(2,1)S(1)} %pad_maximum_fusion.2), channel_id=1, source_target_pairs={{0,4},{4,8},{8,12},{12,0},{1,5},{5,9},{9,13},{13,1},{2,6},{6,10},{... | collective-permute-start | bytes 466952 | tf_op jit(solution)/shard_map/ppermute | solution.py:58
  69.7 5.4 %collective-permute-start.18 = (bf16[1,128,512]{2,1,0:T(8,128)(2,1)S(1)}, bf16[1,128,512]{2,1,0:T(8,128)(2,1)S(1)}, u32[]{:S(2)}, u32[]{:S(2)}) collective-permute-start(bf16[1,128,512]{2,1,0:T(8,128)(2,1)S(1)} %slice_bitcast_fusion.6), channel_id=1, source_target_pairs={{0,2},{1,3},{2,0},{3,1},{4,6},{5,7},{6,4},{7,5},{8,10},{9,11},{10,... | collective-permute-start | bytes 393224 | tf_op jit(solution)/shard_map/ppermute | solution.py:63
  71.2 8.4 %collective-permute-start.22 = (bf16[176,512]{1,0:T(8,128)(2,1)S(1)}, bf16[176,512]{1,0:T(8,128)(2,1)S(1)}, u32[]{:S(2)}, u32[]{:S(2)}) collective-permute-start(bf16[176,512]{1,0:T(8,128)(2,1)S(1)} %pad_maximum_fusion), channel_id=1, source_target_pairs={{0,12},{4,0},{8,4},{12,8},{1,13},{5,1},{9,5},{13,9},{2,14},{6,2},{... | collective-permute-start | bytes 540680 | tf_op jit(solution)/shard_map/ppermute | solution.py:58

commit v17 on v15

--- a/solution.py
+++ b/solution.py
@@ -14,7 +14,7 @@
 SEND_CAP = 40
 CORES = 2
 HOP_NODES = 4
-RETURNS = ((2,), (1, 3), (0,))
+RETURNS = ((2,), (3,), (1,), (0,))
 HOP_CHIPS = 2
 PAGE_FOLD = 24
 SMALL_VMEM = 4 * 1024 * 1024
@@ -223,7 +223,9 @@
     )(gate_up_weight, down_weight, after, *in_vmem(*rings))
 
 
-def final_kernel(hidden_ref, own_ref, down_ref, up_ref, pages_ref, mixed_ref, cache_ref):
+def final_kernel(
+    hidden_ref, own_ref, passed_ref, down_ref, up_ref, pages_ref, mixed_ref, cache_ref
+):
     tok_node = hidden_ref.shape[0]
     nodes = pages_ref.shape[0]
     kv_width = cache_ref.shape[1]
@@ -231,8 +233,8 @@
     for ref in (own_ref, down_ref, up_ref):
         total = total + ref[:tok_node, :].astype(jnp.float32)
     mixed_ref[...] = total.astype(jnp.bfloat16)
-    came = [pages_ref[0], down_ref[tok_node : tok_node + PAGE_FOLD, :]]
-    came += [down_ref[tok_node + PAGE_FOLD :, :], up_ref[tok_node:, :]]
+    came = [pages_ref[0], passed_ref[tok_node + PAGE_FOLD :, :]]
+    came += [down_ref[tok_node:, :], up_ref[tok_node:, :]]
     came = [page.astype(jnp.float32) for page in came]
     me = lax.axis_index("dp")
     rows = []
@@ -245,7 +247,7 @@
     cache_ref[...] = jnp.concatenate(rows, axis=0).astype(jnp.bfloat16)
 
 
-def finished(hidden_states, own, down, up, pages):
+def finished(hidden_states, own, passed, down, up, pages):
     vmem = pl.BlockSpec(memory_space=pltpu.VMEM)
     nodes, _, width = pages.shape
     return pl.pallas_call(
@@ -254,10 +256,10 @@
             jax.ShapeDtypeStruct(hidden_states.shape, jnp.bfloat16),
             jax.ShapeDtypeStruct((nodes * SEND_CAP, width // 2), jnp.bfloat16),
         ],
-        in_specs=[vmem] * 5,
+        in_specs=[vmem] * 6,
         out_specs=[vmem] * 2,
         compiler_params=pltpu.CompilerParams(vmem_limit_bytes=SMALL_VMEM),
-    )(hidden_states, own, down, up, pages)
+    )(hidden_states, own, passed, down, up, pages)
 
 
 def expert_kernel(
@@ -551,24 +553,27 @@
         norm_gain[None, :], gate_up_weight, down_weight, rings, 2, blocks
     )
 
-    over = [other_core(send) for _, send in sums]
-    chip_sums = [added(keep, came) for (keep, _), came in zip(sums, over)]
+    chip_sums = [added(sums[0][0], other_core(sums[0][1]))]
+    later, _ = lax.optimization_barrier(([send for _, send in sums[1:]], chip_sums[0]))
+    chip_sums += [
+        added(keep, other_core(send)) for (keep, _), send in zip(sums[1:], later)
+    ]
     came = [shift_x(chip_sum[1], -1) for chip_sum in chip_sums[:2]]
-    first, _ = lax.optimization_barrier((came[0], chip_sums[1]))
-    last, _ = lax.optimization_barrier((chip_sums[2][1], came[1]))
-    came = [first, came[1], shift_x(last, -1)]
+    came[0], _ = lax.optimization_barrier((came[0], chip_sums[1]))
+    for group in (2, 3):
+        send, _ = lax.optimization_barrier((chip_sums[group][1], came[group - 2]))
+        came.append(shift_x(send, -1))
     shares = {}
     for members, chip_sum, extra in zip(RETURNS, chip_sums, came):
         share = added(chip_sum[0], extra)
         shares |= {z: share[i] for i, z in enumerate(members)}
-    passed = shift_dp(jnp.concatenate([shares[2], pages[2]], axis=0), -1)
     tok_node = hidden_states.shape[0]
-    down = jnp.concatenate(
-        [added(shares[1], passed[:tok_node]), pages[1], passed[tok_node:]], axis=0
-    )
+    passed = shift_dp(jnp.concatenate([shares[2], pages[2], pages[1]], axis=0), -1)
+    page_2 = passed[tok_node : tok_node + PAGE_FOLD]
+    down = jnp.concatenate([added(shares[1], passed[:tok_node]), page_2], axis=0)
     up = jnp.concatenate([shares[3], pages[3]], axis=0)
     return finished(
-        hidden_states, shares[0], shift_dp(down, -1), shift_dp(up, 1), pages
+        hidden_states, shares[0], passed, shift_dp(down, -1), shift_dp(up, 1), pages
     )
 
 

time: 77 us -> 77.2 us (level)
  starting transfers between devices: 24.4 us -> 25.3 us
    ppermute x6, waiting for transfers between devices: 8.29 us -> 7.07 us  [shift_dp(): lax.ppermute(value, 'dp', [(i, (i + shift) % count) for i in range(count)])]
    ppermute x7 -> x8, starting transfers between devices: 8.78 us -> 9.45 us  [shift_x(): lax.ppermute(value, 'mp', [(i, (i + CORES * shift) % count) for i in rang...]
    ppermute x11 -> x12, waiting for transfers between devices: 1.78 us -> 2.27 us  [other_core(): return lax.ppermute(value, 'mp', [(i, i ^ 1) for i in range(count)])]
    ppermute x11 -> x12, starting transfers between devices: 2.12 us -> 2.22 us  [other_core(): return lax.ppermute(value, 'mp', [(i, i ^ 1) for i in range(count)])]
    ppermute x7 -> x8, waiting for transfers between devices: 7.43 us -> 7.5 us  [shift_x(): lax.ppermute(value, 'mp', [(i, (i + CORES * shift) % count) for i in rang...]
  transfers between devices with their start and end apart: 24 -> 26, of which waited for: 11 -> 10; matrix products, arithmetic and copies ran while one was open for 1% -> 1% of each run, Pallas kernels for 10% -> 10%
where the time goes in v17:
time: 77.2 us; the launch traced here: 77.1 us
  Pallas kernels  33.6 us (44%)
  starting transfers between devices  25.3 us (33%)
  waiting for transfers between devices  16.8 us (22%)
  between operations  0.81 us (1%)
    pallas_call x1, Pallas kernels, expert_sums(): pl.pallas_call(functools.partial(expert_kernel, held=held, parts=parts, c...  24.3 us
    ppermute x6, starting transfers between devices, shift_dp(): lax.ppermute(value, 'dp', [(i, (i + shift) % count) for i in range(count)])  13.6 us
    ppermute x8, starting transfers between devices, shift_x(): lax.ppermute(value, 'mp', [(i, (i + CORES * shift) % count) for i in rang...  9.45 us
    ppermute x8, waiting for transfers between devices, shift_x(): lax.ppermute(value, 'mp', [(i, (i + CORES * shift) % count) for i in rang...  7.5 us
    ppermute x6, waiting for transfers between devices, shift_dp(): lax.ppermute(value, 'dp', [(i, (i + shift) % count) for i in range(count)])  7.07 us
    pallas_call x1, Pallas kernels, first_fill(): pl.pallas_call(page_fill_kernel, out_shape=ring_shapes(down_weight) + [ja...  3.84 us
    pallas_call x1, Pallas kernels, next_fill(): pl.pallas_call(functools.partial(fill_kernel, expert=expert), out_shape=r...  3.78 us
    ppermute x12, waiting for transfers between devices, other_core(): return lax.ppermute(value, 'mp', [(i, i ^ 1) for i in range(count)])  2.27 us
  transfers between devices with their start and end apart: 26, of which 10 were waited for; matrix products, arithmetic and copies ran while one was open for 1% of the time, Pallas kernels for 10%

profile of v17, /device:TPU:0, one launch (start us, length us, event | category | flops | bytes accessed | tf_op | source)
XLA Modules:
  0.0 77.1 jit_solution(8695962451497720238)
XLA Ops:
  0.6 1.0 %shard_map.104.after_ref.refs_3_ = bf16[1,136,512]{2,1,0:T(8,128)(2,1)S(1)} custom-call(bf16[128,512]{1,0:T(8,128)(2,1)} %hidden_ref.3, s32[8,128]{1,0:T(8,128)} %bitcast.49, f32[8,128]{1,0:T(8,128)} %bitcast.50), custom_call_target="tpu_custom_call" | custom-call | tf_op jit(solution)/shard_map/pallas_call | solution.py:103
  1.6 3.1 %collective-permute-start = (bf16[1,136,512]{2,1,0:T(8,128)(2,1)S(1)}, bf16[1,136,512]{2,1,0:T(8,128)(2,1)S(1)}, u32[]{:S(2)}, u32[]{:S(2)}) collective-permute-start(bf16[1,136,512]{2,1,0:T(8,128)(2,1)S(1)} %shard_map.104.after_ref.refs_3_), channel_id=1, source_target_pairs={{0,4},{4,8},{8,12},{12,0},{1,5},{5,9},{9,13},{13,1},{2,6},{6,10},{... | collective-permute-start | bytes 417800 | tf_op jit(solution)/shard_map/ppermute | solution.py:58
  4.7 2.1 %collective-permute-start.1 = (bf16[1,136,512]{2,1,0:T(8,128)(2,1)S(1)}, bf16[1,136,512]{2,1,0:T(8,128)(2,1)S(1)}, u32[]{:S(2)}, u32[]{:S(2)}) collective-permute-start(bf16[1,136,512]{2,1,0:T(8,128)(2,1)S(1)} %shard_map.104.after_ref.refs_3_), channel_id=1, source_target_pairs={{0,12},{4,0},{8,4},{12,8},{1,13},{5,1},{9,5},{13,9},{2,14},{6,2},{... | collective-permute-start | bytes 417800 | tf_op jit(solution)/shard_map/ppermute | solution.py:58
  6.8 1.6 %collective-permute-start.2 = (bf16[1,136,512]{2,1,0:T(8,128)(2,1)S(1)}, bf16[1,136,512]{2,1,0:T(8,128)(2,1)S(1)}, u32[]{:S(2)}, u32[]{:S(2)}) collective-permute-start(bf16[1,136,512]{2,1,0:T(8,128)(2,1)S(1)} %shard_map.104.after_ref.refs_3_), channel_id=1, source_target_pairs={{0,2},{1,3},{2,0},{3,1},{4,6},{5,7},{6,4},{7,5},{8,10},{9,11},{10,... | collective-permute-start | bytes 417800 | tf_op jit(solution)/shard_map/ppermute | solution.py:63
  8.4 3.8 %shard_map.105 = (bf16[3,768,2048]{2,1,0:T(8,128)(2,1)S(1)}, bf16[3,768,2048]{2,1,0:T(8,128)(2,1)S(1)}, bf16[3,768,2048]{2,1,0:T(8,128)(2,1)S(1)}, bf16[4,24,512]{2,1,0:T(8,128)(2,1)S(1)}) custom-call(bf16[2,6144,2048]{2,1,0:T(8,128)(2,1)} %gate_up_ref.5, bf16[6144,2048]{1,0:T(8,128)(2,1)} %down_ref.5, ...), custom_call_target="tpu_custom_call" | custom-call | bytes 18874368 | tf_op jit(solution)/shard_map/pallas_call | solution.py:188
  12.3 0.5 collective-permute-done.1.after_ref.refs_15_
  12.8 1.1 %collective-permute-start.9 = (bf16[1,136,512]{2,1,0:T(8,128)(2,1)S(1)}, bf16[1,136,512]{2,1,0:T(8,128)(2,1)S(1)}, u32[]{:S(2)}, u32[]{:S(2)}) collective-permute-start(bf16[1,136,512]{2,1,0:T(8,128)(2,1)S(1)} %collective-permute-done.refs_7_), channel_id=1, source_target_pairs={{0,4},{4,8},{8,12},{12,0},{1,5},{5,9},{9,13},{13,1},{2,6},{6,10},{... | collective-permute-start | bytes 417800 | tf_op jit(solution)/shard_map/ppermute | solution.py:58
  13.9 1.5 %collective-permute-start.4 = (bf16[1,136,512]{2,1,0:T(8,128)(2,1)S(1)}, bf16[1,136,512]{2,1,0:T(8,128)(2,1)S(1)}, u32[]{:S(2)}, u32[]{:S(2)}) collective-permute-start(bf16[1,136,512]{2,1,0:T(8,128)(2,1)S(1)} %collective-permute-done.refs_7_), channel_id=1, source_target_pairs={{0,2},{1,3},{2,0},{3,1},{4,6},{5,7},{6,4},{7,5},{8,10},{9,11},{10,... | collective-permute-start | bytes 417800 | tf_op jit(solution)/shard_map/ppermute | solution.py:63
  15.4 0.5 collective-permute-start.5
  16.0 3.8 %shard_map.106 = (bf16[3,768,2048]{2,1,0:T(8,128)(2,1)S(1)}, bf16[3,768,2048]{2,1,0:T(8,128)(2,1)S(1)}, bf16[3,768,2048]{2,1,0:T(8,128)(2,1)S(1)}) custom-call(bf16[2,6144,2048]{2,1,0:T(8,128)(2,1)} %gate_up_ref.5, bf16[6144,2048]{1,0:T(8,128)(2,1)} %down_ref.5, ...), custom_call_target="tpu_custom_call", output_to_operand_aliasing={{0}: (3, {}), {1}: (4, {}), {2}: (5, {})} | custom-call | bytes 18874368 | tf_op jit(solution)/shard_map/pallas_call | solution.py:214
  19.8 0.5 collective-permute-done.9.refs_11_
  20.2 1.1 %collective-permute-start.11 = (bf16[1,136,512]{2,1,0:T(8,128)(2,1)S(1)}, bf16[1,136,512]{2,1,0:T(8,128)(2,1)S(1)}, u32[]{:S(2)}, u32[]{:S(2)}) collective-permute-start(bf16[1,136,512]{2,1,0:T(8,128)(2,1)S(1)} %collective-permute-done.9.refs_11_), channel_id=1, source_target_pairs={{0,2},{1,3},{2,0},{3,1},{4,6},{5,7},{6,4},{7,5},{8,10},{9,11},{10,... | collective-permute-start | bytes 417800 | tf_op jit(solution)/shard_map/ppermute | solution.py:63
  21.3 0.2 collective-permute-start.10
  21.5 0.7 collective-permute-done.5.refs_17_
  22.2 0.5 collective-permute-start.14
  22.8 3.2 %collective-permute-done.11.refs_13_ = bf16[1,136,512]{2,1,0:T(8,128)(2,1)S(1)} collective-permute-done((bf16[1,136,512]{2,1,0:T(8,128)(2,1)S(1)}, bf16[1,136,512]{2,1,0:T(8,128)(2,1)S(1)}, u32[]{:S(2)}, u32[]{:S(2)}) %collective-permute-start.11) | collective-permute-done | bytes 139296 | tf_op jit(solution)/shard_map/ppermute | solution.py:63
  25.9 0.5 collective-permute-start.12
  26.4 0.8 %collective-permute-done.8.refs_10_ = bf16[1,136,512]{2,1,0:T(8,128)(2,1)S(1)} collective-permute-done((bf16[1,136,512]{2,1,0:T(8,128)(2,1)S(1)}, bf16[1,136,512]{2,1,0:T(8,128)(2,1)S(1)}, u32[]{:S(2)}, u32[]{:S(2)}) %collective-permute-start.8) | collective-permute-done | bytes 139296 | tf_op jit(solution)/shard_map/ppermute | solution.py:68
  27.5 24.3 %shard_map.107 = (bf16[2,1,128,512]{3,2,1,0:T(8,128)(2,1)S(1)}, bf16[2,1,128,512]{3,2,1,0:T(8,128)(2,1)S(1)}, bf16[2,1,128,512]{3,2,1,0:T(8,128)(2,1)S(1)}, bf16...) custom-call(f32[1,2048]{1,0:T(1,128)} %bitcast.48, ...), custom_call_target="tpu_custom_call", output_to_operand_aliasing={{8}: (3, {}), {9}: (4, {}), {10}: (5, {})} | custom-call | flops 4831838208 | bytes 75497472 | tf_op jit(solution)/shard_map/pallas_call | solution.py:420
  51.8 0.4 collective-permute-start.15
  52.2 1.2 %collective-permute-done.15 = bf16[2,1,128,512]{3,2,1,0:T(8,128)(2,1)S(1)} collective-permute-done((bf16[2,1,128,512]{3,2,1,0:T(8,128)(2,1)S(1)}, bf16[2,1,128,512]{3,2,1,0:T(8,128)(2,1)S(1)}, u32[]{:S(2)}, u32[]{:S(2)}) %collective-permute-start.15) | collective-permute-done | bytes 262176 | tf_op jit(solution)/shard_map/ppermute | solution.py:68
  53.5 0.4 collective-permute-start.17
  54.1 1.6 %collective-permute-start.20 = (bf16[1,128,512]{2,1,0:T(8,128)(2,1)S(1)}, bf16[1,128,512]{2,1,0:T(8,128)(2,1)S(1)}, u32[]{:S(2)}, u32[]{:S(2)}) collective-permute-start(bf16[1,128,512]{2,1,0:T(8,128)(2,1)S(1)} %slice_bitcast_fusion.3), channel_id=1, source_target_pairs={{0,2},{1,3},{2,0},{3,1},{4,6},{5,7},{6,4},{7,5},{8,10},{9,11},{10,... | collective-permute-start | bytes 393224 | tf_op jit(solution)/shard_map/ppermute | solution.py:63
  55.7 1.0 %collective-permute-start.18 = (bf16[1,128,512]{2,1,0:T(8,128)(2,1)S(1)}, bf16[1,128,512]{2,1,0:T(8,128)(2,1)S(1)}, u32[]{:S(2)}, u32[]{:S(2)}) collective-permute-start(bf16[1,128,512]{2,1,0:T(8,128)(2,1)S(1)} %slice_bitcast_fusion.5), channel_id=1, source_target_pairs={{0,2},{1,3},{2,0},{3,1},{4,6},{5,7},{6,4},{7,5},{8,10},{9,11},{10,... | collective-permute-start | bytes 393224 | tf_op jit(solution)/shard_map/ppermute | solution.py:63
  56.8 3.6 %collective-permute-done.20 = bf16[1,128,512]{2,1,0:T(8,128)(2,1)S(1)} collective-permute-done((bf16[1,128,512]{2,1,0:T(8,128)(2,1)S(1)}, bf16[1,128,512]{2,1,0:T(8,128)(2,1)S(1)}, u32[]{:S(2)}, u32[]{:S(2)}) %collective-permute-start.20) | collective-permute-done | bytes 131104 | tf_op jit(solution)/shard_map/ppermute | solution.py:63
  60.4 1.5 %collective-permute-start.23 = (bf16[1,128,512]{2,1,0:T(8,128)(2,1)S(1)}, bf16[1,128,512]{2,1,0:T(8,128)(2,1)S(1)}, u32[]{:S(2)}, u32[]{:S(2)}) collective-permute-start(bf16[1,128,512]{2,1,0:T(8,128)(2,1)S(1)} %slice_bitcast_fusion.1), channel_id=1, source_target_pairs={{0,2},{1,3},{2,0},{3,1},{4,6},{5,7},{6,4},{7,5},{8,10},{9,11},{10,... | collective-permute-start | bytes 393224 | tf_op jit(solution)/shard_map/ppermute | solution.py:63
  62.0 2.7 %collective-permute-start.21 = (bf16[176,512]{1,0:T(8,128)(2,1)S(1)}, bf16[176,512]{1,0:T(8,128)(2,1)S(1)}, u32[]{:S(2)}, u32[]{:S(2)}) collective-permute-start(bf16[176,512]{1,0:T(8,128)(2,1)S(1)} %pad_maximum_fusion), channel_id=1, source_target_pairs={{0,12},{4,0},{8,4},{12,8},{1,13},{5,1},{9,5},{13,9},{2,14},{6,2},{... | collective-permute-start | bytes 540680 | tf_op jit(solution)/shard_map/ppermute | solution.py:58
  65.0 0.6 collective-permute-start.19
  65.6 3.4 %collective-permute-done.21.passed_ref = bf16[176,512]{1,0:T(8,128)(2,1)S(1)} collective-permute-done((bf16[176,512]{1,0:T(8,128)(2,1)S(1)}, bf16[176,512]{1,0:T(8,128)(2,1)S(1)}, u32[]{:S(2)}, u32[]{:S(2)}) %collective-permute-start.21) | collective-permute-done | bytes 180256 | tf_op jit(solution)/shard_map/ppermute | solution.py:58
  69.1 4.5 %collective-permute-start.24 = (bf16[152,512]{1,0:T(8,128)(2,1)S(1)}, bf16[152,512]{1,0:T(8,128)(2,1)S(1)}, u32[]{:S(2)}, u32[]{:S(2)}) collective-permute-start(bf16[152,512]{1,0:T(8,128)(2,1)S(1)} %pad_maximum_fusion.1), channel_id=1, source_target_pairs={{0,12},{4,0},{8,4},{12,8},{1,13},{5,1},{9,5},{13,9},{2,14},{6,2},{... | collective-permute-start | bytes 466952 | tf_op jit(solution)/shard_map/ppermute | solution.py:58
  73.6 2.7 %collective-permute-done.24.down_ref = bf16[152,512]{1,0:T(8,128)(2,1)S(1)} collective-permute-done((bf16[152,512]{1,0:T(8,128)(2,1)S(1)}, bf16[152,512]{1,0:T(8,128)(2,1)S(1)}, u32[]{:S(2)}, u32[]{:S(2)}) %collective-permute-start.24) | collective-permute-done | bytes 155680 | tf_op jit(solution)/shard_map/ppermute | solution.py:58
  76.3 0.8 shard_map.108
  (44 shorter events, 1.0 us)
Async XLA Ops:
  1.6 10.7 %collective-permute-start = (bf16[1,136,512]{2,1,0:T(8,128)(2,1)S(1)}, bf16[1,136,512]{2,1,0:T(8,128)(2,1)S(1)}, u32[]{:S(2)}, u32[]{:S(2)}) collective-permute-start(bf16[1,136,512]{2,1,0:T(8,128)(2,1)S(1)} %shard_map.104.after_ref.refs_3_), channel_id=1, source_target_pairs={{0,4},{4,8},{8,12},{12,0},{1,5},{5,9},{9,13},{13,1},{2,6},{6,10},{... | collective-permute-start | bytes 417800 | tf_op jit(solution)/shard_map/ppermute | solution.py:58
  4.7 8.1 %collective-permute-start.1 = (bf16[1,136,512]{2,1,0:T(8,128)(2,1)S(1)}, bf16[1,136,512]{2,1,0:T(8,128)(2,1)S(1)}, u32[]{:S(2)}, u32[]{:S(2)}) collective-permute-start(bf16[1,136,512]{2,1,0:T(8,128)(2,1)S(1)} %shard_map.104.after_ref.refs_3_), channel_id=1, source_target_pairs={{0,12},{4,0},{8,4},{12,8},{1,13},{5,1},{9,5},{13,9},{2,14},{6,2},{... | collective-permute-start | bytes 417800 | tf_op jit(solution)/shard_map/ppermute | solution.py:58
  6.8 6.0 %collective-permute-start.2 = (bf16[1,136,512]{2,1,0:T(8,128)(2,1)S(1)}, bf16[1,136,512]{2,1,0:T(8,128)(2,1)S(1)}, u32[]{:S(2)}, u32[]{:S(2)}) collective-permute-start(bf16[1,136,512]{2,1,0:T(8,128)(2,1)S(1)} %shard_map.104.after_ref.refs_3_), channel_id=1, source_target_pairs={{0,2},{1,3},{2,0},{3,1},{4,6},{5,7},{6,4},{7,5},{8,10},{9,11},{10,... | collective-permute-start | bytes 417800 | tf_op jit(solution)/shard_map/ppermute | solution.py:63
  8.4 4.4 %collective-permute-start.3 = (bf16[1,136,512]{2,1,0:T(8,128)(2,1)S(1)}, bf16[1,136,512]{2,1,0:T(8,128)(2,1)S(1)}, u32[]{:S(2)}, u32[]{:S(2)}) collective-permute-start(bf16[1,136,512]{2,1,0:T(8,128)(2,1)S(1)} %shard_map.104.after_ref.refs_3_), channel_id=1, source_target_pairs={{0,1},{1,0},{2,3},{3,2},{4,5},{5,4},{6,7},{7,6},{8,9},{9,8},{10,11... | collective-permute-start | bytes 417800 | tf_op jit(solution)/shard_map/ppermute | solution.py:68
  12.8 7.4 %collective-permute-start.9 = (bf16[1,136,512]{2,1,0:T(8,128)(2,1)S(1)}, bf16[1,136,512]{2,1,0:T(8,128)(2,1)S(1)}, u32[]{:S(2)}, u32[]{:S(2)}) collective-permute-start(bf16[1,136,512]{2,1,0:T(8,128)(2,1)S(1)} %collective-permute-done.refs_7_), channel_id=1, source_target_pairs={{0,4},{4,8},{8,12},{12,0},{1,5},{5,9},{9,13},{13,1},{2,6},{6,10},{... | collective-permute-start | bytes 417800 | tf_op jit(solution)/shard_map/ppermute | solution.py:58
  13.9 7.6 %collective-permute-start.4 = (bf16[1,136,512]{2,1,0:T(8,128)(2,1)S(1)}, bf16[1,136,512]{2,1,0:T(8,128)(2,1)S(1)}, u32[]{:S(2)}, u32[]{:S(2)}) collective-permute-start(bf16[1,136,512]{2,1,0:T(8,128)(2,1)S(1)} %collective-permute-done.refs_7_), channel_id=1, source_target_pairs={{0,2},{1,3},{2,0},{3,1},{4,6},{5,7},{6,4},{7,5},{8,10},{9,11},{10,... | collective-permute-start | bytes 417800 | tf_op jit(solution)/shard_map/ppermute | solution.py:63
  15.4 6.8 %collective-permute-start.5 = (bf16[1,136,512]{2,1,0:T(8,128)(2,1)S(1)}, bf16[1,136,512]{2,1,0:T(8,128)(2,1)S(1)}, u32[]{:S(2)}, u32[]{:S(2)}) collective-permute-start(bf16[1,136,512]{2,1,0:T(8,128)(2,1)S(1)} %collective-permute-done.1.after_ref.refs_15_), channel_id=1, source_target_pairs={{0,2},{1,3},{2,0},{3,1},{4,6},{5,7},{6,4},{7,5},{8,10},{9,11},{10,... | collective-permute-start | bytes 417800 | tf_op jit(solution)/shard_map/ppermute | solution.py:63
  16.0 6.8 %collective-permute-start.6 = (bf16[1,136,512]{2,1,0:T(8,128)(2,1)S(1)}, bf16[1,136,512]{2,1,0:T(8,128)(2,1)S(1)}, u32[]{:S(2)}, u32[]{:S(2)}) collective-permute-start(bf16[1,136,512]{2,1,0:T(8,128)(2,1)S(1)} %collective-permute-done.2.refs_5_), channel_id=1, source_target_pairs={{0,1},{1,0},{2,3},{3,2},{4,5},{5,4},{6,7},{7,6},{8,9},{9,8},{10,11... | collective-permute-start | bytes 417800 | tf_op jit(solution)/shard_map/ppermute | solution.py:68
  20.2 5.7 %collective-permute-start.11 = (bf16[1,136,512]{2,1,0:T(8,128)(2,1)S(1)}, bf16[1,136,512]{2,1,0:T(8,128)(2,1)S(1)}, u32[]{:S(2)}, u32[]{:S(2)}) collective-permute-start(bf16[1,136,512]{2,1,0:T(8,128)(2,1)S(1)} %collective-permute-done.9.refs_11_), channel_id=1, source_target_pairs={{0,2},{1,3},{2,0},{3,1},{4,6},{5,7},{6,4},{7,5},{8,10},{9,11},{10,... | collective-permute-start | bytes 417800 | tf_op jit(solution)/shard_map/ppermute | solution.py:63
  21.3 4.6 %collective-permute-start.10 = (bf16[1,136,512]{2,1,0:T(8,128)(2,1)S(1)}, bf16[1,136,512]{2,1,0:T(8,128)(2,1)S(1)}, u32[]{:S(2)}, u32[]{:S(2)}) collective-permute-start(bf16[1,136,512]{2,1,0:T(8,128)(2,1)S(1)} %collective-permute-done.9.refs_11_), channel_id=1, source_target_pairs={{0,1},{1,0},{2,3},{3,2},{4,5},{5,4},{6,7},{7,6},{8,9},{9,8},{10,11... | collective-permute-start | bytes 417800 | tf_op jit(solution)/shard_map/ppermute | solution.py:68
  22.2 4.2 %collective-permute-start.13 = (bf16[1,136,512]{2,1,0:T(8,128)(2,1)S(1)}, bf16[1,136,512]{2,1,0:T(8,128)(2,1)S(1)}, u32[]{:S(2)}, u32[]{:S(2)}) collective-permute-start(bf16[1,136,512]{2,1,0:T(8,128)(2,1)S(1)} %collective-permute-done.1.after_ref.refs_15_), channel_id=1, source_target_pairs={{0,1},{1,0},{2,3},{3,2},{4,5},{5,4},{6,7},{7,6},{8,9},{9,8},{10,11... | collective-permute-start | bytes 417800 | tf_op jit(solution)/shard_map/ppermute | solution.py:68
  22.2 4.2 %collective-permute-start.14 = (bf16[1,136,512]{2,1,0:T(8,128)(2,1)S(1)}, bf16[1,136,512]{2,1,0:T(8,128)(2,1)S(1)}, u32[]{:S(2)}, u32[]{:S(2)}) collective-permute-start(bf16[1,136,512]{2,1,0:T(8,128)(2,1)S(1)} %collective-permute-done.5.refs_17_), channel_id=1, source_target_pairs={{0,1},{1,0},{2,3},{3,2},{4,5},{5,4},{6,7},{7,6},{8,9},{9,8},{10,11... | collective-permute-start | bytes 417800 | tf_op jit(solution)/shard_map/ppermute | solution.py:68
  22.7 3.7 %collective-permute-start.7 = (bf16[1,136,512]{2,1,0:T(8,128)(2,1)S(1)}, bf16[1,136,512]{2,1,0:T(8,128)(2,1)S(1)}, u32[]{:S(2)}, u32[]{:S(2)}) collective-permute-start(bf16[1,136,512]{2,1,0:T(8,128)(2,1)S(1)} %collective-permute-done.refs_7_), channel_id=1, source_target_pairs={{0,1},{1,0},{2,3},{3,2},{4,5},{5,4},{6,7},{7,6},{8,9},{9,8},{10,11... | collective-permute-start | bytes 417800 | tf_op jit(solution)/shard_map/ppermute | solution.py:68
  25.9 1.4 %collective-permute-start.8 = (bf16[1,136,512]{2,1,0:T(8,128)(2,1)S(1)}, bf16[1,136,512]{2,1,0:T(8,128)(2,1)S(1)}, u32[]{:S(2)}, u32[]{:S(2)}) collective-permute-start(bf16[1,136,512]{2,1,0:T(8,128)(2,1)S(1)} %collective-permute-done.4.refs_9_), channel_id=1, source_target_pairs={{0,1},{1,0},{2,3},{3,2},{4,5},{5,4},{6,7},{7,6},{8,9},{9,8},{10,11... | collective-permute-start | bytes 417800 | tf_op jit(solution)/shard_map/ppermute | solution.py:68
  25.9 1.6 %collective-permute-start.12 = (bf16[1,136,512]{2,1,0:T(8,128)(2,1)S(1)}, bf16[1,136,512]{2,1,0:T(8,128)(2,1)S(1)}, u32[]{:S(2)}, u32[]{:S(2)}) collective-permute-start(bf16[1,136,512]{2,1,0:T(8,128)(2,1)S(1)} %collective-permute-done.11.refs_13_), channel_id=1, source_target_pairs={{0,1},{1,0},{2,3},{3,2},{4,5},{5,4},{6,7},{7,6},{8,9},{9,8},{10,11... | collective-permute-start | bytes 417800 | tf_op jit(solution)/shard_map/ppermute | solution.py:68
  27.5 48.8 %copy-start = (bf16[128,512]{1,0:T(8,128)(2,1)S(1)}, bf16[128,512]{1,0:T(8,128)(2,1)}, u32[]{:S(2)}) copy-start(bf16[128,512]{1,0:T(8,128)(2,1)} %hidden_ref.3) | copy-start | bytes 393220
  51.8 1.6 %collective-permute-start.15 = (bf16[2,1,128,512]{3,2,1,0:T(8,128)(2,1)S(1)}, bf16[2,1,128,512]{3,2,1,0:T(8,128)(2,1)S(1)}, u32[]{:S(2)}, u32[]{:S(2)}) collective-permute-start(bf16[2,1,128,512]{3,2,1,0:T(8,128)(2,1)S(1)} %get-tuple-element.64), channel_id=1, source_target_pairs={{0,1},{1,0},{2,3},{3,2},{4,5},{5,4},{6,7},{7,6},{8,9},{9,8},{10,11... | collective-permute-start | bytes 786440 | tf_op jit(solution)/shard_map/ppermute | solution.py:68
  53.5 2.2 %collective-permute-start.17 = (bf16[2,1,128,512]{3,2,1,0:T(8,128)(2,1)S(1)}, bf16[2,1,128,512]{3,2,1,0:T(8,128)(2,1)S(1)}, u32[]{:S(2)}, u32[]{:S(2)}) collective-permute-start(bf16[2,1,128,512]{3,2,1,0:T(8,128)(2,1)S(1)} %get-tuple-element.67), channel_id=1, source_target_pairs={{0,1},{1,0},{2,3},{3,2},{4,5},{5,4},{6,7},{7,6},{8,9},{9,8},{10,11... | collective-permute-start | bytes 786440 | tf_op jit(solution)/shard_map/ppermute | solution.py:68
  53.8 2.9 %collective-permute-start.22 = (bf16[2,1,128,512]{3,2,1,0:T(8,128)(2,1)S(1)}, bf16[2,1,128,512]{3,2,1,0:T(8,128)(2,1)S(1)}, u32[]{:S(2)}, u32[]{:S(2)}) collective-permute-start(bf16[2,1,128,512]{3,2,1,0:T(8,128)(2,1)S(1)} %get-tuple-element.72), channel_id=1, source_target_pairs={{0,1},{1,0},{2,3},{3,2},{4,5},{5,4},{6,7},{7,6},{8,9},{9,8},{10,11... | collective-permute-start | bytes 786440 | tf_op jit(solution)/shard_map/ppermute | solution.py:68
  54.1 6.4 %collective-permute-start.20 = (bf16[1,128,512]{2,1,0:T(8,128)(2,1)S(1)}, bf16[1,128,512]{2,1,0:T(8,128)(2,1)S(1)}, u32[]{:S(2)}, u32[]{:S(2)}) collective-permute-start(bf16[1,128,512]{2,1,0:T(8,128)(2,1)S(1)} %slice_bitcast_fusion.3), channel_id=1, source_target_pairs={{0,2},{1,3},{2,0},{3,1},{4,6},{5,7},{6,4},{7,5},{8,10},{9,11},{10,... | collective-permute-start | bytes 393224 | tf_op jit(solution)/shard_map/ppermute | solution.py:63
  55.6 9.1 %collective-permute-start.16 = (bf16[2,1,128,512]{3,2,1,0:T(8,128)(2,1)S(1)}, bf16[2,1,128,512]{3,2,1,0:T(8,128)(2,1)S(1)}, u32[]{:S(2)}, u32[]{:S(2)}) collective-permute-start(bf16[2,1,128,512]{3,2,1,0:T(8,128)(2,1)S(1)} %get-tuple-element.65), channel_id=1, source_target_pairs={{0,1},{1,0},{2,3},{3,2},{4,5},{5,4},{6,7},{7,6},{8,9},{9,8},{10,11... | collective-permute-start | bytes 786440 | tf_op jit(solution)/shard_map/ppermute | solution.py:68
  55.7 9.1 %collective-permute-start.18 = (bf16[1,128,512]{2,1,0:T(8,128)(2,1)S(1)}, bf16[1,128,512]{2,1,0:T(8,128)(2,1)S(1)}, u32[]{:S(2)}, u32[]{:S(2)}) collective-permute-start(bf16[1,128,512]{2,1,0:T(8,128)(2,1)S(1)} %slice_bitcast_fusion.5), channel_id=1, source_target_pairs={{0,2},{1,3},{2,0},{3,1},{4,6},{5,7},{6,4},{7,5},{8,10},{9,11},{10,... | collective-permute-start | bytes 393224 | tf_op jit(solution)/shard_map/ppermute | solution.py:63
  60.4 5.2 %collective-permute-start.23 = (bf16[1,128,512]{2,1,0:T(8,128)(2,1)S(1)}, bf16[1,128,512]{2,1,0:T(8,128)(2,1)S(1)}, u32[]{:S(2)}, u32[]{:S(2)}) collective-permute-start(bf16[1,128,512]{2,1,0:T(8,128)(2,1)S(1)} %slice_bitcast_fusion.1), channel_id=1, source_target_pairs={{0,2},{1,3},{2,0},{3,1},{4,6},{5,7},{6,4},{7,5},{8,10},{9,11},{10,... | collective-permute-start | bytes 393224 | tf_op jit(solution)/shard_map/ppermute | solution.py:63
  62.0 7.0 %collective-permute-start.21 = (bf16[176,512]{1,0:T(8,128)(2,1)S(1)}, bf16[176,512]{1,0:T(8,128)(2,1)S(1)}, u32[]{:S(2)}, u32[]{:S(2)}) collective-permute-start(bf16[176,512]{1,0:T(8,128)(2,1)S(1)} %pad_maximum_fusion), channel_id=1, source_target_pairs={{0,12},{4,0},{8,4},{12,8},{1,13},{5,1},{9,5},{13,9},{2,14},{6,2},{... | collective-permute-start | bytes 540680 | tf_op jit(solution)/shard_map/ppermute | solution.py:58
  64.9 8.7 %collective-permute-start.25 = (bf16[152,512]{1,0:T(8,128)(2,1)S(1)}, bf16[152,512]{1,0:T(8,128)(2,1)S(1)}, u32[]{:S(2)}, u32[]{:S(2)}) collective-permute-start(bf16[152,512]{1,0:T(8,128)(2,1)S(1)} %pad_maximum_fusion.2), channel_id=1, source_target_pairs={{0,4},{4,8},{8,12},{12,0},{1,5},{5,9},{9,13},{13,1},{2,6},{6,10},{... | collective-permute-start | bytes 466952 | tf_op jit(solution)/shard_map/ppermute | solution.py:58
  65.0 8.6 %collective-permute-start.19 = (bf16[1,128,512]{2,1,0:T(8,128)(2,1)S(1)}, bf16[1,128,512]{2,1,0:T(8,128)(2,1)S(1)}, u32[]{:S(2)}, u32[]{:S(2)}) collective-permute-start(bf16[1,128,512]{2,1,0:T(8,128)(2,1)S(1)} %slice_bitcast_fusion.6), channel_id=1, source_target_pairs={{0,2},{1,3},{2,0},{3,1},{4,6},{5,7},{6,4},{7,5},{8,10},{9,11},{10,... | collective-permute-start | bytes 393224 | tf_op jit(solution)/shard_map/ppermute | solution.py:63
  69.1 7.2 %collective-permute-start.24 = (bf16[152,512]{1,0:T(8,128)(2,1)S(1)}, bf16[152,512]{1,0:T(8,128)(2,1)S(1)}, u32[]{:S(2)}, u32[]{:S(2)}) collective-permute-start(bf16[152,512]{1,0:T(8,128)(2,1)S(1)} %pad_maximum_fusion.1), channel_id=1, source_target_pairs={{0,12},{4,0},{8,4},{12,8},{1,13},{5,1},{9,5},{13,9},{2,14},{6,2},{... | collective-permute-start | bytes 466952 | tf_op jit(solution)/shard_map/ppermute | solution.py:58

commit v18 on v17

--- a/solution.py
+++ b/solution.py
@@ -14,7 +14,7 @@
 SEND_CAP = 40
 CORES = 2
 HOP_NODES = 4
-RETURNS = ((2,), (3,), (1,), (0,))
+RETURNS = ((2,), (1, 3, 0))
 HOP_CHIPS = 2
 PAGE_FOLD = 24
 SMALL_VMEM = 4 * 1024 * 1024
@@ -553,16 +553,10 @@
         norm_gain[None, :], gate_up_weight, down_weight, rings, 2, blocks
     )
 
-    chip_sums = [added(sums[0][0], other_core(sums[0][1]))]
-    later, _ = lax.optimization_barrier(([send for _, send in sums[1:]], chip_sums[0]))
-    chip_sums += [
-        added(keep, other_core(send)) for (keep, _), send in zip(sums[1:], later)
-    ]
-    came = [shift_x(chip_sum[1], -1) for chip_sum in chip_sums[:2]]
+    over = [other_core(send) for _, send in sums]
+    chip_sums = [added(keep, came) for (keep, _), came in zip(sums, over)]
+    came = [shift_x(chip_sum[1], -1) for chip_sum in chip_sums]
     came[0], _ = lax.optimization_barrier((came[0], chip_sums[1]))
-    for group in (2, 3):
-        send, _ = lax.optimization_barrier((chip_sums[group][1], came[group - 2]))
-        came.append(shift_x(send, -1))
     shares = {}
     for members, chip_sum, extra in zip(RETURNS, chip_sums, came):
         share = added(chip_sum[0], extra)

time: 77.2 us -> 77.3 us (level)
  waiting for transfers between devices: 16.8 us -> 22.5 us
  starting transfers between devices: 25.3 us -> 21.7 us
  Pallas kernels: 33.6 us -> 31.6 us
    ppermute x8 -> x6, starting transfers between devices: 9.45 us -> 6.91 us  [shift_x(): lax.ppermute(value, 'mp', [(i, (i + CORES * shift) % count) for i in rang...]
    ppermute x6, waiting for transfers between devices: 7.07 us -> 9.46 us  [shift_dp(): lax.ppermute(value, 'dp', [(i, (i + shift) % count) for i in range(count)])]
    ppermute x8 -> x6, waiting for transfers between devices: 7.5 us -> 9.81 us  [shift_x(): lax.ppermute(value, 'mp', [(i, (i + CORES * shift) % count) for i in rang...]
    pallas_call x1, Pallas kernels: 24.3 us -> 22.3 us  [expert_sums(): pl.pallas_call(functools.partial(expert_kernel, held=held, parts=parts, c...]
    ppermute x12 -> x10, waiting for transfers between devices: 2.27 us -> 3.19 us  [other_core(): return lax.ppermute(value, 'mp', [(i, i ^ 1) for i in range(count)])]
    ppermute x12 -> x10, starting transfers between devices: 2.22 us -> 1.83 us  [other_core(): return lax.ppermute(value, 'mp', [(i, i ^ 1) for i in range(count)])]
  transfers between devices with their start and end apart: 26 -> 22, of which waited for: 10 -> 12; matrix products, arithmetic and copies ran while one was open for 1% -> 1% of each run, Pallas kernels for 10% -> 10%
where the time goes in v18:
time: 77.3 us; the launch traced here: 77.1 us
  Pallas kernels  31.6 us (41%)
  waiting for transfers between devices  22.5 us (29%)
  starting transfers between devices  21.7 us (28%)
    pallas_call x1, Pallas kernels, expert_sums(): pl.pallas_call(functools.partial(expert_kernel, held=held, parts=parts, c...  22.3 us
    ppermute x6, starting transfers between devices, shift_dp(): lax.ppermute(value, 'dp', [(i, (i + shift) % count) for i in range(count)])  13 us
    ppermute x6, waiting for transfers between devices, shift_x(): lax.ppermute(value, 'mp', [(i, (i + CORES * shift) % count) for i in rang...  9.81 us
    ppermute x6, waiting for transfers between devices, shift_dp(): lax.ppermute(value, 'dp', [(i, (i + shift) % count) for i in range(count)])  9.46 us
    ppermute x6, starting transfers between devices, shift_x(): lax.ppermute(value, 'mp', [(i, (i + CORES * shift) % count) for i in rang...  6.91 us
    pallas_call x1, Pallas kernels, first_fill(): pl.pallas_call(page_fill_kernel, out_shape=ring_shapes(down_weight) + [ja...  3.84 us
    pallas_call x1, Pallas kernels, next_fill(): pl.pallas_call(functools.partial(fill_kernel, expert=expert), out_shape=r...  3.78 us
    ppermute x10, waiting for transfers between devices, other_core(): return lax.ppermute(value, 'mp', [(i, i ^ 1) for i in range(count)])  3.19 us
  transfers between devices with their start and end apart: 22, of which 12 were waited for; matrix products, arithmetic and copies ran while one was open for 1% of the time, Pallas kernels for 10%

profile of v18, /device:TPU:0, one launch (start us, length us, event | category | flops | bytes accessed | tf_op | source)
XLA Modules:
  0.0 77.1 jit_solution(4894957280856625251)
XLA Ops:
  0.6 1.0 %shard_map.104.after_ref.refs_3_ = bf16[1,136,512]{2,1,0:T(8,128)(2,1)S(1)} custom-call(bf16[128,512]{1,0:T(8,128)(2,1)} %hidden_ref.3, s32[8,128]{1,0:T(8,128)} %bitcast.35, f32[8,128]{1,0:T(8,128)} %bitcast.36), custom_call_target="tpu_custom_call" | custom-call | tf_op jit(solution)/shard_map/pallas_call | solution.py:103
  1.6 3.1 %collective-permute-start = (bf16[1,136,512]{2,1,0:T(8,128)(2,1)S(1)}, bf16[1,136,512]{2,1,0:T(8,128)(2,1)S(1)}, u32[]{:S(2)}, u32[]{:S(2)}) collective-permute-start(bf16[1,136,512]{2,1,0:T(8,128)(2,1)S(1)} %shard_map.104.after_ref.refs_3_), channel_id=1, source_target_pairs={{0,4},{4,8},{8,12},{12,0},{1,5},{5,9},{9,13},{13,1},{2,6},{6,10},{... | collective-permute-start | bytes 417800 | tf_op jit(solution)/shard_map/ppermute | solution.py:58
  4.7 2.1 %collective-permute-start.1 = (bf16[1,136,512]{2,1,0:T(8,128)(2,1)S(1)}, bf16[1,136,512]{2,1,0:T(8,128)(2,1)S(1)}, u32[]{:S(2)}, u32[]{:S(2)}) collective-permute-start(bf16[1,136,512]{2,1,0:T(8,128)(2,1)S(1)} %shard_map.104.after_ref.refs_3_), channel_id=1, source_target_pairs={{0,12},{4,0},{8,4},{12,8},{1,13},{5,1},{9,5},{13,9},{2,14},{6,2},{... | collective-permute-start | bytes 417800 | tf_op jit(solution)/shard_map/ppermute | solution.py:58
  6.8 1.6 %collective-permute-start.2 = (bf16[1,136,512]{2,1,0:T(8,128)(2,1)S(1)}, bf16[1,136,512]{2,1,0:T(8,128)(2,1)S(1)}, u32[]{:S(2)}, u32[]{:S(2)}) collective-permute-start(bf16[1,136,512]{2,1,0:T(8,128)(2,1)S(1)} %shard_map.104.after_ref.refs_3_), channel_id=1, source_target_pairs={{0,2},{1,3},{2,0},{3,1},{4,6},{5,7},{6,4},{7,5},{8,10},{9,11},{10,... | collective-permute-start | bytes 417800 | tf_op jit(solution)/shard_map/ppermute | solution.py:63
  8.4 3.8 %shard_map.105 = (bf16[3,768,2048]{2,1,0:T(8,128)(2,1)S(1)}, bf16[3,768,2048]{2,1,0:T(8,128)(2,1)S(1)}, bf16[3,768,2048]{2,1,0:T(8,128)(2,1)S(1)}, bf16[4,24,512]{2,1,0:T(8,128)(2,1)S(1)}) custom-call(bf16[2,6144,2048]{2,1,0:T(8,128)(2,1)} %gate_up_ref.5, bf16[6144,2048]{1,0:T(8,128)(2,1)} %down_ref.5, ...), custom_call_target="tpu_custom_call" | custom-call | bytes 18874368 | tf_op jit(solution)/shard_map/pallas_call | solution.py:188
  12.3 0.5 collective-permute-done.1.after_ref.refs_15_
  12.8 1.1 %collective-permute-start.9 = (bf16[1,136,512]{2,1,0:T(8,128)(2,1)S(1)}, bf16[1,136,512]{2,1,0:T(8,128)(2,1)S(1)}, u32[]{:S(2)}, u32[]{:S(2)}) collective-permute-start(bf16[1,136,512]{2,1,0:T(8,128)(2,1)S(1)} %collective-permute-done.refs_7_), channel_id=1, source_target_pairs={{0,4},{4,8},{8,12},{12,0},{1,5},{5,9},{9,13},{13,1},{2,6},{6,10},{... | collective-permute-start | bytes 417800 | tf_op jit(solution)/shard_map/ppermute | solution.py:58
  13.9 1.5 %collective-permute-start.4 = (bf16[1,136,512]{2,1,0:T(8,128)(2,1)S(1)}, bf16[1,136,512]{2,1,0:T(8,128)(2,1)S(1)}, u32[]{:S(2)}, u32[]{:S(2)}) collective-permute-start(bf16[1,136,512]{2,1,0:T(8,128)(2,1)S(1)} %collective-permute-done.refs_7_), channel_id=1, source_target_pairs={{0,2},{1,3},{2,0},{3,1},{4,6},{5,7},{6,4},{7,5},{8,10},{9,11},{10,... | collective-permute-start | bytes 417800 | tf_op jit(solution)/shard_map/ppermute | solution.py:63
  15.4 0.5 collective-permute-start.5
  16.0 3.8 %shard_map.106 = (bf16[3,768,2048]{2,1,0:T(8,128)(2,1)S(1)}, bf16[3,768,2048]{2,1,0:T(8,128)(2,1)S(1)}, bf16[3,768,2048]{2,1,0:T(8,128)(2,1)S(1)}) custom-call(bf16[2,6144,2048]{2,1,0:T(8,128)(2,1)} %gate_up_ref.5, bf16[6144,2048]{1,0:T(8,128)(2,1)} %down_ref.5, ...), custom_call_target="tpu_custom_call", output_to_operand_aliasing={{0}: (3, {}), {1}: (4, {}), {2}: (5, {})} | custom-call | bytes 18874368 | tf_op jit(solution)/shard_map/pallas_call | solution.py:214
  19.8 0.5 collective-permute-done.9.refs_11_
  20.2 1.1 %collective-permute-start.11 = (bf16[1,136,512]{2,1,0:T(8,128)(2,1)S(1)}, bf16[1,136,512]{2,1,0:T(8,128)(2,1)S(1)}, u32[]{:S(2)}, u32[]{:S(2)}) collective-permute-start(bf16[1,136,512]{2,1,0:T(8,128)(2,1)S(1)} %collective-permute-done.9.refs_11_), channel_id=1, source_target_pairs={{0,2},{1,3},{2,0},{3,1},{4,6},{5,7},{6,4},{7,5},{8,10},{9,11},{10,... | collective-permute-start | bytes 417800 | tf_op jit(solution)/shard_map/ppermute | solution.py:63
  21.3 0.2 collective-permute-start.10
  21.5 0.7 collective-permute-done.5.refs_17_
  22.2 0.5 collective-permute-start.14
  22.8 3.2 %collective-permute-done.11.refs_13_ = bf16[1,136,512]{2,1,0:T(8,128)(2,1)S(1)} collective-permute-done((bf16[1,136,512]{2,1,0:T(8,128)(2,1)S(1)}, bf16[1,136,512]{2,1,0:T(8,128)(2,1)S(1)}, u32[]{:S(2)}, u32[]{:S(2)}) %collective-permute-start.11) | collective-permute-done | bytes 139296 | tf_op jit(solution)/shard_map/ppermute | solution.py:63
  25.9 0.5 collective-permute-start.12
  26.4 0.8 %collective-permute-done.8.refs_10_ = bf16[1,136,512]{2,1,0:T(8,128)(2,1)S(1)} collective-permute-done((bf16[1,136,512]{2,1,0:T(8,128)(2,1)S(1)}, bf16[1,136,512]{2,1,0:T(8,128)(2,1)S(1)}, u32[]{:S(2)}, u32[]{:S(2)}) %collective-permute-start.8) | collective-permute-done | bytes 139296 | tf_op jit(solution)/shard_map/ppermute | solution.py:68
  27.5 22.3 %shard_map.107 = (bf16[2,1,128,512]{3,2,1,0:T(8,128)(2,1)S(1)}, bf16[2,1,128,512]{3,2,1,0:T(8,128)(2,1)S(1)}, bf16[2,3,128,512]{3,2,1,0:T(8,128)(2,1)S(1)}, bf16...) custom-call(f32[1,2048]{1,0:T(1,128)} %bitcast.34, ...), custom_call_target="tpu_custom_call", output_to_operand_aliasing={{4}: (3, {}), {5}: (4, {}), {6}: (5, {})} | custom-call | flops 4831838208 | bytes 75497472 | tf_op jit(solution)/shard_map/pallas_call | solution.py:420
  49.8 0.4 collective-permute-start.15
  50.4 2.1 %collective-permute-done.17 = bf16[2,1,128,512]{3,2,1,0:T(8,128)(2,1)S(1)} collective-permute-done((bf16[2,1,128,512]{3,2,1,0:T(8,128)(2,1)S(1)}, bf16[2,1,128,512]{3,2,1,0:T(8,128)(2,1)S(1)}, u32[]{:S(2)}, u32[]{:S(2)}) %collective-permute-start.17) | collective-permute-done | bytes 262176 | tf_op jit(solution)/shard_map/ppermute | solution.py:68
  52.6 1.6 %collective-permute-start.18 = (bf16[1,128,512]{2,1,0:T(8,128)(2,1)S(1)}, bf16[1,128,512]{2,1,0:T(8,128)(2,1)S(1)}, u32[]{:S(2)}, u32[]{:S(2)}) collective-permute-start(bf16[1,128,512]{2,1,0:T(8,128)(2,1)S(1)} %slice_bitcast_fusion.4), channel_id=1, source_target_pairs={{0,2},{1,3},{2,0},{3,1},{4,6},{5,7},{6,4},{7,5},{8,10},{9,11},{10,... | collective-permute-start | bytes 393224 | tf_op jit(solution)/shard_map/ppermute | solution.py:63
  54.5 0.5 collective-permute-start.16
  55.0 4.0 %collective-permute-done.18 = bf16[1,128,512]{2,1,0:T(8,128)(2,1)S(1)} collective-permute-done((bf16[1,128,512]{2,1,0:T(8,128)(2,1)S(1)}, bf16[1,128,512]{2,1,0:T(8,128)(2,1)S(1)}, u32[]{:S(2)}, u32[]{:S(2)}) %collective-permute-start.18) | collective-permute-done | bytes 131104 | tf_op jit(solution)/shard_map/ppermute | solution.py:63
  59.1 2.7 %collective-permute-start.19 = (bf16[176,512]{1,0:T(8,128)(2,1)S(1)}, bf16[176,512]{1,0:T(8,128)(2,1)S(1)}, u32[]{:S(2)}, u32[]{:S(2)}) collective-permute-start(bf16[176,512]{1,0:T(8,128)(2,1)S(1)} %pad_maximum_fusion), channel_id=1, source_target_pairs={{0,12},{4,0},{8,4},{12,8},{1,13},{5,1},{9,5},{13,9},{2,14},{6,2},{... | collective-permute-start | bytes 540680 | tf_op jit(solution)/shard_map/ppermute | solution.py:58
  61.8 3.0 %collective-permute-done.19.passed_ref = bf16[176,512]{1,0:T(8,128)(2,1)S(1)} collective-permute-done((bf16[176,512]{1,0:T(8,128)(2,1)S(1)}, bf16[176,512]{1,0:T(8,128)(2,1)S(1)}, u32[]{:S(2)}, u32[]{:S(2)}) %collective-permute-start.19) | collective-permute-done | bytes 180256 | tf_op jit(solution)/shard_map/ppermute | solution.py:58
  64.8 2.0 %collective-permute-done.16 = bf16[3,128,512]{2,1,0:T(8,128)(2,1)S(1)} collective-permute-done((bf16[3,128,512]{2,1,0:T(8,128)(2,1)S(1)}, bf16[3,128,512]{2,1,0:T(8,128)(2,1)S(1)}, u32[]{:S(2)}, u32[]{:S(2)}) %collective-permute-start.16) | collective-permute-done | bytes 393248 | tf_op jit(solution)/shard_map/ppermute | solution.py:63
  67.0 0.8 %collective-permute-start.21 = (bf16[152,512]{1,0:T(8,128)(2,1)S(1)}, bf16[152,512]{1,0:T(8,128)(2,1)S(1)}, u32[]{:S(2)}, u32[]{:S(2)}) collective-permute-start(bf16[152,512]{1,0:T(8,128)(2,1)S(1)} %pad_maximum_fusion.2), channel_id=1, source_target_pairs={{0,4},{4,8},{8,12},{12,0},{1,5},{5,9},{9,13},{13,1},{2,6},{6,10},{... | collective-permute-start | bytes 466952 | tf_op jit(solution)/shard_map/ppermute | solution.py:58
  67.8 3.1 %collective-permute-start.20 = (bf16[152,512]{1,0:T(8,128)(2,1)S(1)}, bf16[152,512]{1,0:T(8,128)(2,1)S(1)}, u32[]{:S(2)}, u32[]{:S(2)}) collective-permute-start(bf16[152,512]{1,0:T(8,128)(2,1)S(1)} %pad_maximum_fusion.1), channel_id=1, source_target_pairs={{0,12},{4,0},{8,4},{12,8},{1,13},{5,1},{9,5},{13,9},{2,14},{6,2},{... | collective-permute-start | bytes 466952 | tf_op jit(solution)/shard_map/ppermute | solution.py:58
  70.9 4.8 %collective-permute-done.21.up_ref = bf16[152,512]{1,0:T(8,128)(2,1)S(1)} collective-permute-done((bf16[152,512]{1,0:T(8,128)(2,1)S(1)}, bf16[152,512]{1,0:T(8,128)(2,1)S(1)}, u32[]{:S(2)}, u32[]{:S(2)}) %collective-permute-start.21) | collective-permute-done | bytes 155680 | tf_op jit(solution)/shard_map/ppermute | solution.py:58
  75.8 0.6 collective-permute-done.20.down_ref
  76.4 0.8 shard_map.108
  (32 shorter events, 1.0 us)
Async XLA Ops:
  1.6 10.7 %collective-permute-start = (bf16[1,136,512]{2,1,0:T(8,128)(2,1)S(1)}, bf16[1,136,512]{2,1,0:T(8,128)(2,1)S(1)}, u32[]{:S(2)}, u32[]{:S(2)}) collective-permute-start(bf16[1,136,512]{2,1,0:T(8,128)(2,1)S(1)} %shard_map.104.after_ref.refs_3_), channel_id=1, source_target_pairs={{0,4},{4,8},{8,12},{12,0},{1,5},{5,9},{9,13},{13,1},{2,6},{6,10},{... | collective-permute-start | bytes 417800 | tf_op jit(solution)/shard_map/ppermute | solution.py:58
  4.7 8.1 %collective-permute-start.1 = (bf16[1,136,512]{2,1,0:T(8,128)(2,1)S(1)}, bf16[1,136,512]{2,1,0:T(8,128)(2,1)S(1)}, u32[]{:S(2)}, u32[]{:S(2)}) collective-permute-start(bf16[1,136,512]{2,1,0:T(8,128)(2,1)S(1)} %shard_map.104.after_ref.refs_3_), channel_id=1, source_target_pairs={{0,12},{4,0},{8,4},{12,8},{1,13},{5,1},{9,5},{13,9},{2,14},{6,2},{... | collective-permute-start | bytes 417800 | tf_op jit(solution)/shard_map/ppermute | solution.py:58
  6.8 6.0 %collective-permute-start.2 = (bf16[1,136,512]{2,1,0:T(8,128)(2,1)S(1)}, bf16[1,136,512]{2,1,0:T(8,128)(2,1)S(1)}, u32[]{:S(2)}, u32[]{:S(2)}) collective-permute-start(bf16[1,136,512]{2,1,0:T(8,128)(2,1)S(1)} %shard_map.104.after_ref.refs_3_), channel_id=1, source_target_pairs={{0,2},{1,3},{2,0},{3,1},{4,6},{5,7},{6,4},{7,5},{8,10},{9,11},{10,... | collective-permute-start | bytes 417800 | tf_op jit(solution)/shard_map/ppermute | solution.py:63
  8.4 4.4 %collective-permute-start.3 = (bf16[1,136,512]{2,1,0:T(8,128)(2,1)S(1)}, bf16[1,136,512]{2,1,0:T(8,128)(2,1)S(1)}, u32[]{:S(2)}, u32[]{:S(2)}) collective-permute-start(bf16[1,136,512]{2,1,0:T(8,128)(2,1)S(1)} %shard_map.104.after_ref.refs_3_), channel_id=1, source_target_pairs={{0,1},{1,0},{2,3},{3,2},{4,5},{5,4},{6,7},{7,6},{8,9},{9,8},{10,11... | collective-permute-start | bytes 417800 | tf_op jit(solution)/shard_map/ppermute | solution.py:68
  12.8 7.4 %collective-permute-start.9 = (bf16[1,136,512]{2,1,0:T(8,128)(2,1)S(1)}, bf16[1,136,512]{2,1,0:T(8,128)(2,1)S(1)}, u32[]{:S(2)}, u32[]{:S(2)}) collective-permute-start(bf16[1,136,512]{2,1,0:T(8,128)(2,1)S(1)} %collective-permute-done.refs_7_), channel_id=1, source_target_pairs={{0,4},{4,8},{8,12},{12,0},{1,5},{5,9},{9,13},{13,1},{2,6},{6,10},{... | collective-permute-start | bytes 417800 | tf_op jit(solution)/shard_map/ppermute | solution.py:58
  13.9 7.6 %collective-permute-start.4 = (bf16[1,136,512]{2,1,0:T(8,128)(2,1)S(1)}, bf16[1,136,512]{2,1,0:T(8,128)(2,1)S(1)}, u32[]{:S(2)}, u32[]{:S(2)}) collective-permute-start(bf16[1,136,512]{2,1,0:T(8,128)(2,1)S(1)} %collective-permute-done.refs_7_), channel_id=1, source_target_pairs={{0,2},{1,3},{2,0},{3,1},{4,6},{5,7},{6,4},{7,5},{8,10},{9,11},{10,... | collective-permute-start | bytes 417800 | tf_op jit(solution)/shard_map/ppermute | solution.py:63
  15.4 6.8 %collective-permute-start.5 = (bf16[1,136,512]{2,1,0:T(8,128)(2,1)S(1)}, bf16[1,136,512]{2,1,0:T(8,128)(2,1)S(1)}, u32[]{:S(2)}, u32[]{:S(2)}) collective-permute-start(bf16[1,136,512]{2,1,0:T(8,128)(2,1)S(1)} %collective-permute-done.1.after_ref.refs_15_), channel_id=1, source_target_pairs={{0,2},{1,3},{2,0},{3,1},{4,6},{5,7},{6,4},{7,5},{8,10},{9,11},{10,... | collective-permute-start | bytes 417800 | tf_op jit(solution)/shard_map/ppermute | solution.py:63
  16.0 6.8 %collective-permute-start.6 = (bf16[1,136,512]{2,1,0:T(8,128)(2,1)S(1)}, bf16[1,136,512]{2,1,0:T(8,128)(2,1)S(1)}, u32[]{:S(2)}, u32[]{:S(2)}) collective-permute-start(bf16[1,136,512]{2,1,0:T(8,128)(2,1)S(1)} %collective-permute-done.2.refs_5_), channel_id=1, source_target_pairs={{0,1},{1,0},{2,3},{3,2},{4,5},{5,4},{6,7},{7,6},{8,9},{9,8},{10,11... | collective-permute-start | bytes 417800 | tf_op jit(solution)/shard_map/ppermute | solution.py:68
  20.2 5.7 %collective-permute-start.11 = (bf16[1,136,512]{2,1,0:T(8,128)(2,1)S(1)}, bf16[1,136,512]{2,1,0:T(8,128)(2,1)S(1)}, u32[]{:S(2)}, u32[]{:S(2)}) collective-permute-start(bf16[1,136,512]{2,1,0:T(8,128)(2,1)S(1)} %collective-permute-done.9.refs_11_), channel_id=1, source_target_pairs={{0,2},{1,3},{2,0},{3,1},{4,6},{5,7},{6,4},{7,5},{8,10},{9,11},{10,... | collective-permute-start | bytes 417800 | tf_op jit(solution)/shard_map/ppermute | solution.py:63
  21.3 4.6 %collective-permute-start.10 = (bf16[1,136,512]{2,1,0:T(8,128)(2,1)S(1)}, bf16[1,136,512]{2,1,0:T(8,128)(2,1)S(1)}, u32[]{:S(2)}, u32[]{:S(2)}) collective-permute-start(bf16[1,136,512]{2,1,0:T(8,128)(2,1)S(1)} %collective-permute-done.9.refs_11_), channel_id=1, source_target_pairs={{0,1},{1,0},{2,3},{3,2},{4,5},{5,4},{6,7},{7,6},{8,9},{9,8},{10,11... | collective-permute-start | bytes 417800 | tf_op jit(solution)/shard_map/ppermute | solution.py:68
  22.2 4.2 %collective-permute-start.13 = (bf16[1,136,512]{2,1,0:T(8,128)(2,1)S(1)}, bf16[1,136,512]{2,1,0:T(8,128)(2,1)S(1)}, u32[]{:S(2)}, u32[]{:S(2)}) collective-permute-start(bf16[1,136,512]{2,1,0:T(8,128)(2,1)S(1)} %collective-permute-done.1.after_ref.refs_15_), channel_id=1, source_target_pairs={{0,1},{1,0},{2,3},{3,2},{4,5},{5,4},{6,7},{7,6},{8,9},{9,8},{10,11... | collective-permute-start | bytes 417800 | tf_op jit(solution)/shard_map/ppermute | solution.py:68
  22.2 4.2 %collective-permute-start.14 = (bf16[1,136,512]{2,1,0:T(8,128)(2,1)S(1)}, bf16[1,136,512]{2,1,0:T(8,128)(2,1)S(1)}, u32[]{:S(2)}, u32[]{:S(2)}) collective-permute-start(bf16[1,136,512]{2,1,0:T(8,128)(2,1)S(1)} %collective-permute-done.5.refs_17_), channel_id=1, source_target_pairs={{0,1},{1,0},{2,3},{3,2},{4,5},{5,4},{6,7},{7,6},{8,9},{9,8},{10,11... | collective-permute-start | bytes 417800 | tf_op jit(solution)/shard_map/ppermute | solution.py:68
  22.7 3.7 %collective-permute-start.7 = (bf16[1,136,512]{2,1,0:T(8,128)(2,1)S(1)}, bf16[1,136,512]{2,1,0:T(8,128)(2,1)S(1)}, u32[]{:S(2)}, u32[]{:S(2)}) collective-permute-start(bf16[1,136,512]{2,1,0:T(8,128)(2,1)S(1)} %collective-permute-done.refs_7_), channel_id=1, source_target_pairs={{0,1},{1,0},{2,3},{3,2},{4,5},{5,4},{6,7},{7,6},{8,9},{9,8},{10,11... | collective-permute-start | bytes 417800 | tf_op jit(solution)/shard_map/ppermute | solution.py:68
  25.9 1.4 %collective-permute-start.8 = (bf16[1,136,512]{2,1,0:T(8,128)(2,1)S(1)}, bf16[1,136,512]{2,1,0:T(8,128)(2,1)S(1)}, u32[]{:S(2)}, u32[]{:S(2)}) collective-permute-start(bf16[1,136,512]{2,1,0:T(8,128)(2,1)S(1)} %collective-permute-done.4.refs_9_), channel_id=1, source_target_pairs={{0,1},{1,0},{2,3},{3,2},{4,5},{5,4},{6,7},{7,6},{8,9},{9,8},{10,11... | collective-permute-start | bytes 417800 | tf_op jit(solution)/shard_map/ppermute | solution.py:68
  25.9 1.6 %collective-permute-start.12 = (bf16[1,136,512]{2,1,0:T(8,128)(2,1)S(1)}, bf16[1,136,512]{2,1,0:T(8,128)(2,1)S(1)}, u32[]{:S(2)}, u32[]{:S(2)}) collective-permute-start(bf16[1,136,512]{2,1,0:T(8,128)(2,1)S(1)} %collective-permute-done.11.refs_13_), channel_id=1, source_target_pairs={{0,1},{1,0},{2,3},{3,2},{4,5},{5,4},{6,7},{7,6},{8,9},{9,8},{10,11... | collective-permute-start | bytes 417800 | tf_op jit(solution)/shard_map/ppermute | solution.py:68
  27.5 48.9 %copy-start = (bf16[128,512]{1,0:T(8,128)(2,1)S(1)}, bf16[128,512]{1,0:T(8,128)(2,1)}, u32[]{:S(2)}) copy-start(bf16[128,512]{1,0:T(8,128)(2,1)} %hidden_ref.3) | copy-start | bytes 393220
  49.8 4.4 %collective-permute-start.15 = (bf16[2,3,128,512]{3,2,1,0:T(8,128)(2,1)S(1)}, bf16[2,3,128,512]{3,2,1,0:T(8,128)(2,1)S(1)}, u32[]{:S(2)}, u32[]{:S(2)}) collective-permute-start(bf16[2,3,128,512]{3,2,1,0:T(8,128)(2,1)S(1)} %get-tuple-element.51), channel_id=1, source_target_pairs={{0,1},{1,0},{2,3},{3,2},{4,5},{5,4},{6,7},{7,6},{8,9},{9,8},{10,11... | collective-permute-start | bytes 2359304 | tf_op jit(solution)/shard_map/ppermute | solution.py:68
  50.2 2.4 %collective-permute-start.17 = (bf16[2,1,128,512]{3,2,1,0:T(8,128)(2,1)S(1)}, bf16[2,1,128,512]{3,2,1,0:T(8,128)(2,1)S(1)}, u32[]{:S(2)}, u32[]{:S(2)}) collective-permute-start(bf16[2,1,128,512]{3,2,1,0:T(8,128)(2,1)S(1)} %get-tuple-element.53), channel_id=1, source_target_pairs={{0,1},{1,0},{2,3},{3,2},{4,5},{5,4},{6,7},{7,6},{8,9},{9,8},{10,11... | collective-permute-start | bytes 786440 | tf_op jit(solution)/shard_map/ppermute | solution.py:68
  52.6 6.4 %collective-permute-start.18 = (bf16[1,128,512]{2,1,0:T(8,128)(2,1)S(1)}, bf16[1,128,512]{2,1,0:T(8,128)(2,1)S(1)}, u32[]{:S(2)}, u32[]{:S(2)}) collective-permute-start(bf16[1,128,512]{2,1,0:T(8,128)(2,1)S(1)} %slice_bitcast_fusion.4), channel_id=1, source_target_pairs={{0,2},{1,3},{2,0},{3,1},{4,6},{5,7},{6,4},{7,5},{8,10},{9,11},{10,... | collective-permute-start | bytes 393224 | tf_op jit(solution)/shard_map/ppermute | solution.py:63
  54.5 12.3 %collective-permute-start.16 = (bf16[3,128,512]{2,1,0:T(8,128)(2,1)S(1)}, bf16[3,128,512]{2,1,0:T(8,128)(2,1)S(1)}, u32[]{:S(2)}, u32[]{:S(2)}) collective-permute-start(bf16[3,128,512]{2,1,0:T(8,128)(2,1)S(1)} %slice_bitcast_fusion), channel_id=1, source_target_pairs={{0,2},{1,3},{2,0},{3,1},{4,6},{5,7},{6,4},{7,5},{8,10},{9,11},{10,... | collective-permute-start | bytes 1179656 | tf_op jit(solution)/shard_map/ppermute | solution.py:63
  59.1 5.8 %collective-permute-start.19 = (bf16[176,512]{1,0:T(8,128)(2,1)S(1)}, bf16[176,512]{1,0:T(8,128)(2,1)S(1)}, u32[]{:S(2)}, u32[]{:S(2)}) collective-permute-start(bf16[176,512]{1,0:T(8,128)(2,1)S(1)} %pad_maximum_fusion), channel_id=1, source_target_pairs={{0,12},{4,0},{8,4},{12,8},{1,13},{5,1},{9,5},{13,9},{2,14},{6,2},{... | collective-permute-start | bytes 540680 | tf_op jit(solution)/shard_map/ppermute | solution.py:58
  67.0 8.8 %collective-permute-start.21 = (bf16[152,512]{1,0:T(8,128)(2,1)S(1)}, bf16[152,512]{1,0:T(8,128)(2,1)S(1)}, u32[]{:S(2)}, u32[]{:S(2)}) collective-permute-start(bf16[152,512]{1,0:T(8,128)(2,1)S(1)} %pad_maximum_fusion.2), channel_id=1, source_target_pairs={{0,4},{4,8},{8,12},{12,0},{1,5},{5,9},{9,13},{13,1},{2,6},{6,10},{... | collective-permute-start | bytes 466952 | tf_op jit(solution)/shard_map/ppermute | solution.py:58
  67.8 8.5 %collective-permute-start.20 = (bf16[152,512]{1,0:T(8,128)(2,1)S(1)}, bf16[152,512]{1,0:T(8,128)(2,1)S(1)}, u32[]{:S(2)}, u32[]{:S(2)}) collective-permute-start(bf16[152,512]{1,0:T(8,128)(2,1)S(1)} %pad_maximum_fusion.1), channel_id=1, source_target_pairs={{0,12},{4,0},{8,4},{12,8},{1,13},{5,1},{9,5},{13,9},{2,14},{6,2},{... | collective-permute-start | bytes 466952 | tf_op jit(solution)/shard_map/ppermute | solution.py:58

commit v19 on v18

--- a/solution.py
+++ b/solution.py
@@ -553,8 +553,9 @@
         norm_gain[None, :], gate_up_weight, down_weight, rings, 2, blocks
     )
 
-    over = [other_core(send) for _, send in sums]
-    chip_sums = [added(keep, came) for (keep, _), came in zip(sums, over)]
+    chip_sums = [added(sums[0][0], other_core(sums[0][1]))]
+    later, _ = lax.optimization_barrier((sums[1][1], chip_sums[0]))
+    chip_sums.append(added(sums[1][0], other_core(later)))
     came = [shift_x(chip_sum[1], -1) for chip_sum in chip_sums]
     came[0], _ = lax.optimization_barrier((came[0], chip_sums[1]))
     shares = {}

time: 77.3 us -> 76.6 us (level)
  waiting for transfers between devices: 22.5 us -> 20.6 us
  starting transfers between devices: 21.7 us -> 23 us
    ppermute x6, waiting for transfers between devices: 9.81 us -> 8.3 us  [shift_x(): lax.ppermute(value, 'mp', [(i, (i + CORES * shift) % count) for i in rang...]
    ppermute x6, starting transfers between devices: 6.91 us -> 7.99 us  [shift_x(): lax.ppermute(value, 'mp', [(i, (i + CORES * shift) % count) for i in rang...]
  transfers between devices with their start and end apart: 22 -> 22, of which waited for: 12 -> 13; matrix products, arithmetic and copies ran while one was open for 1% -> 0% of each run, Pallas kernels for 10% -> 10%
where the time goes in v19:
time: 76.6 us; the launch traced here: 76.5 us
  Pallas kernels  31.6 us (41%)
  starting transfers between devices  23 us (30%)
  waiting for transfers between devices  20.6 us (27%)
    pallas_call x1, Pallas kernels, expert_sums(): pl.pallas_call(functools.partial(expert_kernel, held=held, parts=parts, c...  22.3 us
    ppermute x6, starting transfers between devices, shift_dp(): lax.ppermute(value, 'dp', [(i, (i + shift) % count) for i in range(count)])  13 us
    ppermute x6, waiting for transfers between devices, shift_dp(): lax.ppermute(value, 'dp', [(i, (i + shift) % count) for i in range(count)])  9.65 us
    ppermute x6, waiting for transfers between devices, shift_x(): lax.ppermute(value, 'mp', [(i, (i + CORES * shift) % count) for i in rang...  8.3 us
    ppermute x6, starting transfers between devices, shift_x(): lax.ppermute(value, 'mp', [(i, (i + CORES * shift) % count) for i in rang...  7.99 us
    pallas_call x1, Pallas kernels, first_fill(): pl.pallas_call(page_fill_kernel, out_shape=ring_shapes(down_weight) + [ja...  3.84 us
    pallas_call x1, Pallas kernels, next_fill(): pl.pallas_call(functools.partial(fill_kernel, expert=expert), out_shape=r...  3.78 us
    ppermute x10, waiting for transfers between devices, other_core(): return lax.ppermute(value, 'mp', [(i, i ^ 1) for i in range(count)])  2.62 us
  transfers between devices with their start and end apart: 22, of which 13 were waited for; matrix products, arithmetic and copies ran while one was open for 0% of the time, Pallas kernels for 10%

profile of v19, /device:TPU:0, one launch (start us, length us, event | category | flops | bytes accessed | tf_op | source)
XLA Modules:
  0.0 76.5 jit_solution(5335459147386884714)
XLA Ops:
  0.6 1.0 %shard_map.104.after_ref.refs_3_ = bf16[1,136,512]{2,1,0:T(8,128)(2,1)S(1)} custom-call(bf16[128,512]{1,0:T(8,128)(2,1)} %hidden_ref.3, s32[8,128]{1,0:T(8,128)} %bitcast.35, f32[8,128]{1,0:T(8,128)} %bitcast.36), custom_call_target="tpu_custom_call" | custom-call | tf_op jit(solution)/shard_map/pallas_call | solution.py:103
  1.6 3.1 %collective-permute-start = (bf16[1,136,512]{2,1,0:T(8,128)(2,1)S(1)}, bf16[1,136,512]{2,1,0:T(8,128)(2,1)S(1)}, u32[]{:S(2)}, u32[]{:S(2)}) collective-permute-start(bf16[1,136,512]{2,1,0:T(8,128)(2,1)S(1)} %shard_map.104.after_ref.refs_3_), channel_id=1, source_target_pairs={{0,4},{4,8},{8,12},{12,0},{1,5},{5,9},{9,13},{13,1},{2,6},{6,10},{... | collective-permute-start | bytes 417800 | tf_op jit(solution)/shard_map/ppermute | solution.py:58
  4.7 2.1 %collective-permute-start.1 = (bf16[1,136,512]{2,1,0:T(8,128)(2,1)S(1)}, bf16[1,136,512]{2,1,0:T(8,128)(2,1)S(1)}, u32[]{:S(2)}, u32[]{:S(2)}) collective-permute-start(bf16[1,136,512]{2,1,0:T(8,128)(2,1)S(1)} %shard_map.104.after_ref.refs_3_), channel_id=1, source_target_pairs={{0,12},{4,0},{8,4},{12,8},{1,13},{5,1},{9,5},{13,9},{2,14},{6,2},{... | collective-permute-start | bytes 417800 | tf_op jit(solution)/shard_map/ppermute | solution.py:58
  6.8 1.6 %collective-permute-start.2 = (bf16[1,136,512]{2,1,0:T(8,128)(2,1)S(1)}, bf16[1,136,512]{2,1,0:T(8,128)(2,1)S(1)}, u32[]{:S(2)}, u32[]{:S(2)}) collective-permute-start(bf16[1,136,512]{2,1,0:T(8,128)(2,1)S(1)} %shard_map.104.after_ref.refs_3_), channel_id=1, source_target_pairs={{0,2},{1,3},{2,0},{3,1},{4,6},{5,7},{6,4},{7,5},{8,10},{9,11},{10,... | collective-permute-start | bytes 417800 | tf_op jit(solution)/shard_map/ppermute | solution.py:63
  8.4 3.8 %shard_map.105 = (bf16[3,768,2048]{2,1,0:T(8,128)(2,1)S(1)}, bf16[3,768,2048]{2,1,0:T(8,128)(2,1)S(1)}, bf16[3,768,2048]{2,1,0:T(8,128)(2,1)S(1)}, bf16[4,24,512]{2,1,0:T(8,128)(2,1)S(1)}) custom-call(bf16[2,6144,2048]{2,1,0:T(8,128)(2,1)} %gate_up_ref.5, bf16[6144,2048]{1,0:T(8,128)(2,1)} %down_ref.5, ...), custom_call_target="tpu_custom_call" | custom-call | bytes 18874368 | tf_op jit(solution)/shard_map/pallas_call | solution.py:188
  12.3 0.5 collective-permute-done.1.after_ref.refs_15_
  12.8 1.1 %collective-permute-start.9 = (bf16[1,136,512]{2,1,0:T(8,128)(2,1)S(1)}, bf16[1,136,512]{2,1,0:T(8,128)(2,1)S(1)}, u32[]{:S(2)}, u32[]{:S(2)}) collective-permute-start(bf16[1,136,512]{2,1,0:T(8,128)(2,1)S(1)} %collective-permute-done.refs_7_), channel_id=1, source_target_pairs={{0,4},{4,8},{8,12},{12,0},{1,5},{5,9},{9,13},{13,1},{2,6},{6,10},{... | collective-permute-start | bytes 417800 | tf_op jit(solution)/shard_map/ppermute | solution.py:58
  13.9 1.5 %collective-permute-start.4 = (bf16[1,136,512]{2,1,0:T(8,128)(2,1)S(1)}, bf16[1,136,512]{2,1,0:T(8,128)(2,1)S(1)}, u32[]{:S(2)}, u32[]{:S(2)}) collective-permute-start(bf16[1,136,512]{2,1,0:T(8,128)(2,1)S(1)} %collective-permute-done.refs_7_), channel_id=1, source_target_pairs={{0,2},{1,3},{2,0},{3,1},{4,6},{5,7},{6,4},{7,5},{8,10},{9,11},{10,... | collective-permute-start | bytes 417800 | tf_op jit(solution)/shard_map/ppermute | solution.py:63
  15.4 0.5 collective-permute-start.5
  16.0 3.8 %shard_map.106 = (bf16[3,768,2048]{2,1,0:T(8,128)(2,1)S(1)}, bf16[3,768,2048]{2,1,0:T(8,128)(2,1)S(1)}, bf16[3,768,2048]{2,1,0:T(8,128)(2,1)S(1)}) custom-call(bf16[2,6144,2048]{2,1,0:T(8,128)(2,1)} %gate_up_ref.5, bf16[6144,2048]{1,0:T(8,128)(2,1)} %down_ref.5, ...), custom_call_target="tpu_custom_call", output_to_operand_aliasing={{0}: (3, {}), {1}: (4, {}), {2}: (5, {})} | custom-call | bytes 18874368 | tf_op jit(solution)/shard_map/pallas_call | solution.py:214
  19.8 0.5 collective-permute-done.9.refs_11_
  20.2 1.1 %collective-permute-start.11 = (bf16[1,136,512]{2,1,0:T(8,128)(2,1)S(1)}, bf16[1,136,512]{2,1,0:T(8,128)(2,1)S(1)}, u32[]{:S(2)}, u32[]{:S(2)}) collective-permute-start(bf16[1,136,512]{2,1,0:T(8,128)(2,1)S(1)} %collective-permute-done.9.refs_11_), channel_id=1, source_target_pairs={{0,2},{1,3},{2,0},{3,1},{4,6},{5,7},{6,4},{7,5},{8,10},{9,11},{10,... | collective-permute-start | bytes 417800 | tf_op jit(solution)/shard_map/ppermute | solution.py:63
  21.5 0.7 collective-permute-done.5.refs_17_
  22.2 0.5 collective-permute-start.14
  22.8 3.2 %collective-permute-done.11.refs_13_ = bf16[1,136,512]{2,1,0:T(8,128)(2,1)S(1)} collective-permute-done((bf16[1,136,512]{2,1,0:T(8,128)(2,1)S(1)}, bf16[1,136,512]{2,1,0:T(8,128)(2,1)S(1)}, u32[]{:S(2)}, u32[]{:S(2)}) %collective-permute-start.11) | collective-permute-done | bytes 139296 | tf_op jit(solution)/shard_map/ppermute | solution.py:63
  25.9 0.5 collective-permute-start.12
  26.4 0.8 %collective-permute-done.8.refs_10_ = bf16[1,136,512]{2,1,0:T(8,128)(2,1)S(1)} collective-permute-done((bf16[1,136,512]{2,1,0:T(8,128)(2,1)S(1)}, bf16[1,136,512]{2,1,0:T(8,128)(2,1)S(1)}, u32[]{:S(2)}, u32[]{:S(2)}) %collective-permute-start.8) | collective-permute-done | bytes 139296 | tf_op jit(solution)/shard_map/ppermute | solution.py:68
  27.5 22.3 %shard_map.107 = (bf16[2,1,128,512]{3,2,1,0:T(8,128)(2,1)S(1)}, bf16[2,1,128,512]{3,2,1,0:T(8,128)(2,1)S(1)}, bf16[2,3,128,512]{3,2,1,0:T(8,128)(2,1)S(1)}, bf16...) custom-call(f32[1,2048]{1,0:T(1,128)} %bitcast.34, ...), custom_call_target="tpu_custom_call", output_to_operand_aliasing={{4}: (3, {}), {5}: (4, {}), {6}: (5, {})} | custom-call | flops 4831838208 | bytes 75497472 | tf_op jit(solution)/shard_map/pallas_call | solution.py:420
  49.8 0.4 collective-permute-start.15
  50.2 1.2 %collective-permute-done.15 = bf16[2,1,128,512]{3,2,1,0:T(8,128)(2,1)S(1)} collective-permute-done((bf16[2,1,128,512]{3,2,1,0:T(8,128)(2,1)S(1)}, bf16[2,1,128,512]{3,2,1,0:T(8,128)(2,1)S(1)}, u32[]{:S(2)}, u32[]{:S(2)}) %collective-permute-start.15) | collective-permute-done | bytes 262176 | tf_op jit(solution)/shard_map/ppermute | solution.py:68
  51.5 0.4 collective-permute-start.16
  51.8 1.6 %collective-permute-start.18 = (bf16[1,128,512]{2,1,0:T(8,128)(2,1)S(1)}, bf16[1,128,512]{2,1,0:T(8,128)(2,1)S(1)}, u32[]{:S(2)}, u32[]{:S(2)}) collective-permute-start(bf16[1,128,512]{2,1,0:T(8,128)(2,1)S(1)} %slice_bitcast_fusion.4), channel_id=1, source_target_pairs={{0,2},{1,3},{2,0},{3,1},{4,6},{5,7},{6,4},{7,5},{8,10},{9,11},{10,... | collective-permute-start | bytes 393224 | tf_op jit(solution)/shard_map/ppermute | solution.py:63
  54.1 1.6 %collective-permute-start.17 = (bf16[3,128,512]{2,1,0:T(8,128)(2,1)S(1)}, bf16[3,128,512]{2,1,0:T(8,128)(2,1)S(1)}, u32[]{:S(2)}, u32[]{:S(2)}) collective-permute-start(bf16[3,128,512]{2,1,0:T(8,128)(2,1)S(1)} %slice_bitcast_fusion), channel_id=1, source_target_pairs={{0,2},{1,3},{2,0},{3,1},{4,6},{5,7},{6,4},{7,5},{8,10},{9,11},{10,... | collective-permute-start | bytes 1179656 | tf_op jit(solution)/shard_map/ppermute | solution.py:63
  55.7 2.3 %collective-permute-done.18 = bf16[1,128,512]{2,1,0:T(8,128)(2,1)S(1)} collective-permute-done((bf16[1,128,512]{2,1,0:T(8,128)(2,1)S(1)}, bf16[1,128,512]{2,1,0:T(8,128)(2,1)S(1)}, u32[]{:S(2)}, u32[]{:S(2)}) %collective-permute-start.18) | collective-permute-done | bytes 131104 | tf_op jit(solution)/shard_map/ppermute | solution.py:63
  58.0 2.7 %collective-permute-start.19 = (bf16[176,512]{1,0:T(8,128)(2,1)S(1)}, bf16[176,512]{1,0:T(8,128)(2,1)S(1)}, u32[]{:S(2)}, u32[]{:S(2)}) collective-permute-start(bf16[176,512]{1,0:T(8,128)(2,1)S(1)} %pad_maximum_fusion), channel_id=1, source_target_pairs={{0,12},{4,0},{8,4},{12,8},{1,13},{5,1},{9,5},{13,9},{2,14},{6,2},{... | collective-permute-start | bytes 540680 | tf_op jit(solution)/shard_map/ppermute | solution.py:58
  60.8 3.0 %collective-permute-done.19.passed_ref = bf16[176,512]{1,0:T(8,128)(2,1)S(1)} collective-permute-done((bf16[176,512]{1,0:T(8,128)(2,1)S(1)}, bf16[176,512]{1,0:T(8,128)(2,1)S(1)}, u32[]{:S(2)}, u32[]{:S(2)}) %collective-permute-start.19) | collective-permute-done | bytes 180256 | tf_op jit(solution)/shard_map/ppermute | solution.py:58
  63.8 2.2 %collective-permute-done.17 = bf16[3,128,512]{2,1,0:T(8,128)(2,1)S(1)} collective-permute-done((bf16[3,128,512]{2,1,0:T(8,128)(2,1)S(1)}, bf16[3,128,512]{2,1,0:T(8,128)(2,1)S(1)}, u32[]{:S(2)}, u32[]{:S(2)}) %collective-permute-start.17) | collective-permute-done | bytes 393248 | tf_op jit(solution)/shard_map/ppermute | solution.py:63
  66.1 0.8 %collective-permute-start.21 = (bf16[152,512]{1,0:T(8,128)(2,1)S(1)}, bf16[152,512]{1,0:T(8,128)(2,1)S(1)}, u32[]{:S(2)}, u32[]{:S(2)}) collective-permute-start(bf16[152,512]{1,0:T(8,128)(2,1)S(1)} %pad_maximum_fusion.2), channel_id=1, source_target_pairs={{0,4},{4,8},{8,12},{12,0},{1,5},{5,9},{9,13},{13,1},{2,6},{6,10},{... | collective-permute-start | bytes 466952 | tf_op jit(solution)/shard_map/ppermute | solution.py:58
  67.0 3.1 %collective-permute-start.20 = (bf16[152,512]{1,0:T(8,128)(2,1)S(1)}, bf16[152,512]{1,0:T(8,128)(2,1)S(1)}, u32[]{:S(2)}, u32[]{:S(2)}) collective-permute-start(bf16[152,512]{1,0:T(8,128)(2,1)S(1)} %pad_maximum_fusion.1), channel_id=1, source_target_pairs={{0,12},{4,0},{8,4},{12,8},{1,13},{5,1},{9,5},{13,9},{2,14},{6,2},{... | collective-permute-start | bytes 466952 | tf_op jit(solution)/shard_map/ppermute | solution.py:58
  70.1 4.8 %collective-permute-done.21.up_ref = bf16[152,512]{1,0:T(8,128)(2,1)S(1)} collective-permute-done((bf16[152,512]{1,0:T(8,128)(2,1)S(1)}, bf16[152,512]{1,0:T(8,128)(2,1)S(1)}, u32[]{:S(2)}, u32[]{:S(2)}) %collective-permute-start.21) | collective-permute-done | bytes 155680 | tf_op jit(solution)/shard_map/ppermute | solution.py:58
  74.9 0.8 %collective-permute-done.20.down_ref = bf16[152,512]{1,0:T(8,128)(2,1)S(1)} collective-permute-done((bf16[152,512]{1,0:T(8,128)(2,1)S(1)}, bf16[152,512]{1,0:T(8,128)(2,1)S(1)}, u32[]{:S(2)}, u32[]{:S(2)}) %collective-permute-start.20) | collective-permute-done | bytes 155680 | tf_op jit(solution)/shard_map/ppermute | solution.py:58
  75.7 0.8 shard_map.108
  (32 shorter events, 1.3 us)
Async XLA Ops:
  1.6 10.7 %collective-permute-start = (bf16[1,136,512]{2,1,0:T(8,128)(2,1)S(1)}, bf16[1,136,512]{2,1,0:T(8,128)(2,1)S(1)}, u32[]{:S(2)}, u32[]{:S(2)}) collective-permute-start(bf16[1,136,512]{2,1,0:T(8,128)(2,1)S(1)} %shard_map.104.after_ref.refs_3_), channel_id=1, source_target_pairs={{0,4},{4,8},{8,12},{12,0},{1,5},{5,9},{9,13},{13,1},{2,6},{6,10},{... | collective-permute-start | bytes 417800 | tf_op jit(solution)/shard_map/ppermute | solution.py:58
  4.7 8.1 %collective-permute-start.1 = (bf16[1,136,512]{2,1,0:T(8,128)(2,1)S(1)}, bf16[1,136,512]{2,1,0:T(8,128)(2,1)S(1)}, u32[]{:S(2)}, u32[]{:S(2)}) collective-permute-start(bf16[1,136,512]{2,1,0:T(8,128)(2,1)S(1)} %shard_map.104.after_ref.refs_3_), channel_id=1, source_target_pairs={{0,12},{4,0},{8,4},{12,8},{1,13},{5,1},{9,5},{13,9},{2,14},{6,2},{... | collective-permute-start | bytes 417800 | tf_op jit(solution)/shard_map/ppermute | solution.py:58
  6.8 6.0 %collective-permute-start.2 = (bf16[1,136,512]{2,1,0:T(8,128)(2,1)S(1)}, bf16[1,136,512]{2,1,0:T(8,128)(2,1)S(1)}, u32[]{:S(2)}, u32[]{:S(2)}) collective-permute-start(bf16[1,136,512]{2,1,0:T(8,128)(2,1)S(1)} %shard_map.104.after_ref.refs_3_), channel_id=1, source_target_pairs={{0,2},{1,3},{2,0},{3,1},{4,6},{5,7},{6,4},{7,5},{8,10},{9,11},{10,... | collective-permute-start | bytes 417800 | tf_op jit(solution)/shard_map/ppermute | solution.py:63
  8.4 4.4 %collective-permute-start.3 = (bf16[1,136,512]{2,1,0:T(8,128)(2,1)S(1)}, bf16[1,136,512]{2,1,0:T(8,128)(2,1)S(1)}, u32[]{:S(2)}, u32[]{:S(2)}) collective-permute-start(bf16[1,136,512]{2,1,0:T(8,128)(2,1)S(1)} %shard_map.104.after_ref.refs_3_), channel_id=1, source_target_pairs={{0,1},{1,0},{2,3},{3,2},{4,5},{5,4},{6,7},{7,6},{8,9},{9,8},{10,11... | collective-permute-start | bytes 417800 | tf_op jit(solution)/shard_map/ppermute | solution.py:68
  12.8 7.4 %collective-permute-start.9 = (bf16[1,136,512]{2,1,0:T(8,128)(2,1)S(1)}, bf16[1,136,512]{2,1,0:T(8,128)(2,1)S(1)}, u32[]{:S(2)}, u32[]{:S(2)}) collective-permute-start(bf16[1,136,512]{2,1,0:T(8,128)(2,1)S(1)} %collective-permute-done.refs_7_), channel_id=1, source_target_pairs={{0,4},{4,8},{8,12},{12,0},{1,5},{5,9},{9,13},{13,1},{2,6},{6,10},{... | collective-permute-start | bytes 417800 | tf_op jit(solution)/shard_map/ppermute | solution.py:58
  13.9 7.6 %collective-permute-start.4 = (bf16[1,136,512]{2,1,0:T(8,128)(2,1)S(1)}, bf16[1,136,512]{2,1,0:T(8,128)(2,1)S(1)}, u32[]{:S(2)}, u32[]{:S(2)}) collective-permute-start(bf16[1,136,512]{2,1,0:T(8,128)(2,1)S(1)} %collective-permute-done.refs_7_), channel_id=1, source_target_pairs={{0,2},{1,3},{2,0},{3,1},{4,6},{5,7},{6,4},{7,5},{8,10},{9,11},{10,... | collective-permute-start | bytes 417800 | tf_op jit(solution)/shard_map/ppermute | solution.py:63
  15.4 6.8 %collective-permute-start.5 = (bf16[1,136,512]{2,1,0:T(8,128)(2,1)S(1)}, bf16[1,136,512]{2,1,0:T(8,128)(2,1)S(1)}, u32[]{:S(2)}, u32[]{:S(2)}) collective-permute-start(bf16[1,136,512]{2,1,0:T(8,128)(2,1)S(1)} %collective-permute-done.1.after_ref.refs_15_), channel_id=1, source_target_pairs={{0,2},{1,3},{2,0},{3,1},{4,6},{5,7},{6,4},{7,5},{8,10},{9,11},{10,... | collective-permute-start | bytes 417800 | tf_op jit(solution)/shard_map/ppermute | solution.py:63
  16.0 6.8 %collective-permute-start.6 = (bf16[1,136,512]{2,1,0:T(8,128)(2,1)S(1)}, bf16[1,136,512]{2,1,0:T(8,128)(2,1)S(1)}, u32[]{:S(2)}, u32[]{:S(2)}) collective-permute-start(bf16[1,136,512]{2,1,0:T(8,128)(2,1)S(1)} %collective-permute-done.2.refs_5_), channel_id=1, source_target_pairs={{0,1},{1,0},{2,3},{3,2},{4,5},{5,4},{6,7},{7,6},{8,9},{9,8},{10,11... | collective-permute-start | bytes 417800 | tf_op jit(solution)/shard_map/ppermute | solution.py:68
  20.2 5.7 %collective-permute-start.11 = (bf16[1,136,512]{2,1,0:T(8,128)(2,1)S(1)}, bf16[1,136,512]{2,1,0:T(8,128)(2,1)S(1)}, u32[]{:S(2)}, u32[]{:S(2)}) collective-permute-start(bf16[1,136,512]{2,1,0:T(8,128)(2,1)S(1)} %collective-permute-done.9.refs_11_), channel_id=1, source_target_pairs={{0,2},{1,3},{2,0},{3,1},{4,6},{5,7},{6,4},{7,5},{8,10},{9,11},{10,... | collective-permute-start | bytes 417800 | tf_op jit(solution)/shard_map/ppermute | solution.py:63
  21.3 4.6 %collective-permute-start.10 = (bf16[1,136,512]{2,1,0:T(8,128)(2,1)S(1)}, bf16[1,136,512]{2,1,0:T(8,128)(2,1)S(1)}, u32[]{:S(2)}, u32[]{:S(2)}) collective-permute-start(bf16[1,136,512]{2,1,0:T(8,128)(2,1)S(1)} %collective-permute-done.9.refs_11_), channel_id=1, source_target_pairs={{0,1},{1,0},{2,3},{3,2},{4,5},{5,4},{6,7},{7,6},{8,9},{9,8},{10,11... | collective-permute-start | bytes 417800 | tf_op jit(solution)/shard_map/ppermute | solution.py:68
  22.2 4.2 %collective-permute-start.13 = (bf16[1,136,512]{2,1,0:T(8,128)(2,1)S(1)}, bf16[1,136,512]{2,1,0:T(8,128)(2,1)S(1)}, u32[]{:S(2)}, u32[]{:S(2)}) collective-permute-start(bf16[1,136,512]{2,1,0:T(8,128)(2,1)S(1)} %collective-permute-done.1.after_ref.refs_15_), channel_id=1, source_target_pairs={{0,1},{1,0},{2,3},{3,2},{4,5},{5,4},{6,7},{7,6},{8,9},{9,8},{10,11... | collective-permute-start | bytes 417800 | tf_op jit(solution)/shard_map/ppermute | solution.py:68
  22.2 4.2 %collective-permute-start.14 = (bf16[1,136,512]{2,1,0:T(8,128)(2,1)S(1)}, bf16[1,136,512]{2,1,0:T(8,128)(2,1)S(1)}, u32[]{:S(2)}, u32[]{:S(2)}) collective-permute-start(bf16[1,136,512]{2,1,0:T(8,128)(2,1)S(1)} %collective-permute-done.5.refs_17_), channel_id=1, source_target_pairs={{0,1},{1,0},{2,3},{3,2},{4,5},{5,4},{6,7},{7,6},{8,9},{9,8},{10,11... | collective-permute-start | bytes 417800 | tf_op jit(solution)/shard_map/ppermute | solution.py:68
  22.7 3.7 %collective-permute-start.7 = (bf16[1,136,512]{2,1,0:T(8,128)(2,1)S(1)}, bf16[1,136,512]{2,1,0:T(8,128)(2,1)S(1)}, u32[]{:S(2)}, u32[]{:S(2)}) collective-permute-start(bf16[1,136,512]{2,1,0:T(8,128)(2,1)S(1)} %collective-permute-done.refs_7_), channel_id=1, source_target_pairs={{0,1},{1,0},{2,3},{3,2},{4,5},{5,4},{6,7},{7,6},{8,9},{9,8},{10,11... | collective-permute-start | bytes 417800 | tf_op jit(solution)/shard_map/ppermute | solution.py:68
  25.9 1.4 %collective-permute-start.8 = (bf16[1,136,512]{2,1,0:T(8,128)(2,1)S(1)}, bf16[1,136,512]{2,1,0:T(8,128)(2,1)S(1)}, u32[]{:S(2)}, u32[]{:S(2)}) collective-permute-start(bf16[1,136,512]{2,1,0:T(8,128)(2,1)S(1)} %collective-permute-done.4.refs_9_), channel_id=1, source_target_pairs={{0,1},{1,0},{2,3},{3,2},{4,5},{5,4},{6,7},{7,6},{8,9},{9,8},{10,11... | collective-permute-start | bytes 417800 | tf_op jit(solution)/shard_map/ppermute | solution.py:68
  25.9 1.6 %collective-permute-start.12 = (bf16[1,136,512]{2,1,0:T(8,128)(2,1)S(1)}, bf16[1,136,512]{2,1,0:T(8,128)(2,1)S(1)}, u32[]{:S(2)}, u32[]{:S(2)}) collective-permute-start(bf16[1,136,512]{2,1,0:T(8,128)(2,1)S(1)} %collective-permute-done.11.refs_13_), channel_id=1, source_target_pairs={{0,1},{1,0},{2,3},{3,2},{4,5},{5,4},{6,7},{7,6},{8,9},{9,8},{10,11... | collective-permute-start | bytes 417800 | tf_op jit(solution)/shard_map/ppermute | solution.py:68
  27.5 48.2 %copy-start = (bf16[128,512]{1,0:T(8,128)(2,1)S(1)}, bf16[128,512]{1,0:T(8,128)(2,1)}, u32[]{:S(2)}) copy-start(bf16[128,512]{1,0:T(8,128)(2,1)} %hidden_ref.3) | copy-start | bytes 393220
  49.8 1.6 %collective-permute-start.15 = (bf16[2,1,128,512]{3,2,1,0:T(8,128)(2,1)S(1)}, bf16[2,1,128,512]{3,2,1,0:T(8,128)(2,1)S(1)}, u32[]{:S(2)}, u32[]{:S(2)}) collective-permute-start(bf16[2,1,128,512]{3,2,1,0:T(8,128)(2,1)S(1)} %get-tuple-element.54), channel_id=1, source_target_pairs={{0,1},{1,0},{2,3},{3,2},{4,5},{5,4},{6,7},{7,6},{8,9},{9,8},{10,11... | collective-permute-start | bytes 786440 | tf_op jit(solution)/shard_map/ppermute | solution.py:68
  51.5 2.4 %collective-permute-start.16 = (bf16[2,3,128,512]{3,2,1,0:T(8,128)(2,1)S(1)}, bf16[2,3,128,512]{3,2,1,0:T(8,128)(2,1)S(1)}, u32[]{:S(2)}, u32[]{:S(2)}) collective-permute-start(bf16[2,3,128,512]{3,2,1,0:T(8,128)(2,1)S(1)} %get-tuple-element.55), channel_id=1, source_target_pairs={{0,1},{1,0},{2,3},{3,2},{4,5},{5,4},{6,7},{7,6},{8,9},{9,8},{10,11... | collective-permute-start | bytes 2359304 | tf_op jit(solution)/shard_map/ppermute | solution.py:68
  51.8 6.1 %collective-permute-start.18 = (bf16[1,128,512]{2,1,0:T(8,128)(2,1)S(1)}, bf16[1,128,512]{2,1,0:T(8,128)(2,1)S(1)}, u32[]{:S(2)}, u32[]{:S(2)}) collective-permute-start(bf16[1,128,512]{2,1,0:T(8,128)(2,1)S(1)} %slice_bitcast_fusion.4), channel_id=1, source_target_pairs={{0,2},{1,3},{2,0},{3,1},{4,6},{5,7},{6,4},{7,5},{8,10},{9,11},{10,... | collective-permute-start | bytes 393224 | tf_op jit(solution)/shard_map/ppermute | solution.py:63
  54.1 11.9 %collective-permute-start.17 = (bf16[3,128,512]{2,1,0:T(8,128)(2,1)S(1)}, bf16[3,128,512]{2,1,0:T(8,128)(2,1)S(1)}, u32[]{:S(2)}, u32[]{:S(2)}) collective-permute-start(bf16[3,128,512]{2,1,0:T(8,128)(2,1)S(1)} %slice_bitcast_fusion), channel_id=1, source_target_pairs={{0,2},{1,3},{2,0},{3,1},{4,6},{5,7},{6,4},{7,5},{8,10},{9,11},{10,... | collective-permute-start | bytes 1179656 | tf_op jit(solution)/shard_map/ppermute | solution.py:63
  58.0 5.8 %collective-permute-start.19 = (bf16[176,512]{1,0:T(8,128)(2,1)S(1)}, bf16[176,512]{1,0:T(8,128)(2,1)S(1)}, u32[]{:S(2)}, u32[]{:S(2)}) collective-permute-start(bf16[176,512]{1,0:T(8,128)(2,1)S(1)} %pad_maximum_fusion), channel_id=1, source_target_pairs={{0,12},{4,0},{8,4},{12,8},{1,13},{5,1},{9,5},{13,9},{2,14},{6,2},{... | collective-permute-start | bytes 540680 | tf_op jit(solution)/shard_map/ppermute | solution.py:58
  66.1 8.8 %collective-permute-start.21 = (bf16[152,512]{1,0:T(8,128)(2,1)S(1)}, bf16[152,512]{1,0:T(8,128)(2,1)S(1)}, u32[]{:S(2)}, u32[]{:S(2)}) collective-permute-start(bf16[152,512]{1,0:T(8,128)(2,1)S(1)} %pad_maximum_fusion.2), channel_id=1, source_target_pairs={{0,4},{4,8},{8,12},{12,0},{1,5},{5,9},{9,13},{13,1},{2,6},{6,10},{... | collective-permute-start | bytes 466952 | tf_op jit(solution)/shard_map/ppermute | solution.py:58
  67.0 8.7 %collective-permute-start.20 = (bf16[152,512]{1,0:T(8,128)(2,1)S(1)}, bf16[152,512]{1,0:T(8,128)(2,1)S(1)}, u32[]{:S(2)}, u32[]{:S(2)}) collective-permute-start(bf16[152,512]{1,0:T(8,128)(2,1)S(1)} %pad_maximum_fusion.1), channel_id=1, source_target_pairs={{0,12},{4,0},{8,4},{12,8},{1,13},{5,1},{9,5},{13,9},{2,14},{6,2},{... | collective-permute-start | bytes 466952 | tf_op jit(solution)/shard_map/ppermute | solution.py:58
